TPU v7x, 32 devices: a whole 2x2x4 slice. The times are simulated.
32 devices in a mesh: uv: 4 (over z), chan: 8 (over y, x, core).
Axes of the slice: x: 2, y: 2, z: 4, core: 2. Of those that a mesh axis runs over, the one named last changes fastest.
Arguments:
- visibility: bfloat16 [2, 512, 32, 4096], P(None, 'chan', 'uv'), may hold values from -6 to 6
- eigen_basis: bfloat16 [512, 512], P('chan'), may hold values from -0.25 to 0.25
- eigenvalues: float32 [512], replicated, may hold values from 0.01 to 100
- noise_power: float32 [32], P('uv'), may hold values from 0.1 to 10
Outputs:
- image_cube: bfloat16 [2, 512, 32, 4096], P(None, ('uv', 'chan'))
All inputs are finite; a program needn't handle non-finite values.
Results may differ from a plain program's by a relative error of at most 0.019.
Values may be sent and summed in bfloat16 or wider, within the bound.
No kernel may reach another device: no remote copies, remote signals or barrier semaphores. Data moves between devices by JAX's collectives and lax.ppermute only.
A program may use at most 128 MiB of HBM per device.

v0:
```python
import math

import jax
import jax.numpy as jnp
from jax import lax
from jax.sharding import PartitionSpec as P


def split_length(length):
    inner_size = math.gcd(length, 128)
    return (length // inner_size, inner_size)


def dft_table(length):
    positions = jnp.arange(length, dtype=jnp.int32)
    phase_radians = (jnp.outer(positions, positions) % length).astype(jnp.float32) * (
        2.0 * math.pi / length
    )
    cosine = jnp.cos(phase_radians)
    sine_part = jnp.sin(phase_radians)
    upper_half = jnp.stack([cosine, -sine_part], axis=1)
    lower_half = jnp.stack([sine_part, cosine], axis=1)
    return jnp.stack([upper_half, lower_half], axis=0)


def column_transform(field_data):
    length = field_data.shape[2]
    outer_size, inner_size = split_length(length)
    blocks = field_data.reshape(2, field_data.shape[1], outer_size, inner_size)
    section_one = jnp.einsum(
        "sjta,tmab->smjb",
        dft_table(outer_size),
        blocks,
        precision=lax.Precision.HIGH,
        preferred_element_type=jnp.float32,
    )
    outer_pos = jnp.arange(outer_size, dtype=jnp.int32)[:, None]
    inner_pos = jnp.arange(inner_size, dtype=jnp.int32)[None, :]
    phase_radians = (outer_pos * inner_pos % length).astype(jnp.float32) * (2.0 * math.pi / length)
    cosine = jnp.cos(phase_radians)
    sine_part = jnp.sin(phase_radians)
    turned = jnp.stack(
        [
            section_one[0] * cosine - section_one[1] * sine_part,
            section_one[0] * sine_part + section_one[1] * cosine,
        ]
    )
    return jnp.einsum(
        "sltb,tmjb->smjl",
        dft_table(inner_size),
        turned,
        precision=lax.Precision.HIGH,
        preferred_element_type=jnp.float32,
    )


def row_transform(planes):
    row_total = planes.shape[2]
    norm_scale = 1.0 / math.sqrt(row_total * planes.shape[3] * planes.shape[4])
    result = jnp.einsum(
        "sxtu,tkujl->skxlj",
        dft_table(row_total),
        planes,
        precision=lax.Precision.HIGH,
        preferred_element_type=jnp.float32,
    )
    return (result.reshape(2, planes.shape[1], row_total, -1) * norm_scale).astype(jnp.bfloat16)


def shards(visibility, eigen_basis, eigenvalues, noise_power):
    uv_count = lax.axis_size("uv")
    chan_count = lax.axis_size("chan")
    exchanged = lax.all_to_all(visibility, "chan", split_axis=3, concat_axis=1, tiled=True)
    total_chans = exchanged.shape[1]
    rows_dev = exchanged.shape[2]
    piece_width = exchanged.shape[3]
    full_length = piece_width * chan_count
    outer_size, inner_size = split_length(full_length)
    mode_filter_gain = eigenvalues[:, None] / (eigenvalues[:, None] + noise_power[None, :])
    basis_full = lax.all_gather(eigen_basis, "chan", axis=0, tiled=True)
    mode_amplitudes = jnp.einsum(
        "ck,scrw->skrw", basis_full, exchanged, preferred_element_type=jnp.float32
    ).astype(jnp.bfloat16)
    foreground_signal = (
        mode_filter_gain[None, :, :, None] * mode_amplitudes.astype(jnp.float32)
    ).astype(jnp.bfloat16)
    rearranged_slab = jnp.einsum(
        "ck,skrw->scrw", basis_full, foreground_signal, preferred_element_type=jnp.float32
    )
    cleaned = (exchanged - rearranged_slab).astype(jnp.bfloat16)
    plane_count = total_chans // (uv_count * chan_count)
    grouped = cleaned.reshape(2, uv_count, chan_count, plane_count, rows_dev, piece_width)
    returned = lax.all_to_all(grouped, "chan", split_axis=2, concat_axis=5, tiled=True)
    flattened = returned.reshape(2, -1, full_length)
    turned = column_transform(flattened).reshape(
        2, uv_count, 1, plane_count, rows_dev, outer_size, inner_size
    )
    received_rows = lax.all_to_all(
        turned.astype(jnp.bfloat16), "uv", split_axis=1, concat_axis=4, tiled=True
    ).astype(turned.dtype)
    planes = received_rows.reshape(2, plane_count, -1, outer_size, inner_size)
    return row_transform(planes)


def solution(mesh):
    in_specs = (P(None, "chan", "uv", None), P("chan", None), P(), P("uv"))
    out_specs = P(None, ("uv", "chan"), None, None)
    return jax.shard_map(shards, mesh=mesh, in_specs=in_specs, out_specs=out_specs, check_vma=False)
```

profile of v0, /device:TPU:2, one launch (start us, length us, event | category | flops | bytes accessed | tf_op | source)
XLA Modules:
  0.0 653.4 jit_solution(6573153917084781859)
XLA Ops:
  0.0 24.4 %copy.48 = bf16[2,64,8,4096]{1,2,0,3:T(8,128)(2,1)} copy(bf16[2,64,8,4096]{3,2,1,0:T(8,128)(2,1)} %param.4) | data formatting | bytes 16777216 | tf_op args[0]
  24.4 16.8 %reshape.267 = bf16[8,2,262144]{2,1,0:T(2,128)(2,1)} reshape(bf16[4096,2,8,64]{3,2,1,0:T(8,128)(2,1)} %bitcast.97) | data formatting | bytes 16777216
  41.3 0.0 copy-start
  41.3 0.0 copy-start.1
  41.3 0.0 copy-start.2
  41.3 5.0 all-to-all-start
  46.3 0.0 copy-done
  46.3 96.7 %all_gather.3 = bf16[512,512]{1,0:T(8,128)(2,1)S(1)} all-gather(bf16[64,512]{1,0:T(8,128)(2,1)S(1)} %copy-done), channel_id=1, replica_groups=mesh['uv'=4,'chan'=8] {'chan'}, dimensions={0}, use_global_device_ids=true | all-gather | bytes 589824 | tf_op jit(solution)/shard_map/all_gather | solution.py:80
  143.0 0.0 copy-done.1
  143.0 0.0 copy-done.2
  143.0 0.1 add_divide_fusion
  143.1 0.0 all-to-all-done
  143.1 16.5 %reshape.268 = bf16[4096,2,8,64]{3,2,1,0:T(8,128)(2,1)} reshape(bf16[8,2,262144]{2,1,0:T(2,128)(2,1)} %all-to-all-done) | data formatting | bytes 16777216
  159.6 18.3 %copy.72 = bf16[2,8,64,8,512]{4,2,1,3,0:T(8,128)(2,1)} copy(bf16[2,8,64,8,512]{2,3,0,4,1:T(8,128)(2,1)} %bitcast.96) | data formatting | bytes 16777216 | tf_op jit(solution)/shard_map/all_to_all | solution.py:73
  177.9 14.6 %fusion.3 = bf16[2,512,8,512]{3,1,2,0:T(8,128)(2,1)} fusion(bf16[2,512,8,512]{3,1,2,0:T(8,128)(2,1)} %bitcast.99, f32[512,8]{0,1:T(8,128)S(1)} %add_divide_fusion, bf16[512,512]{1,0:T(8,128)(2,1)S(1)} %all_gather.3), kind=kOutput, calls=%fused_computation.7 | convolution fusion | flops 8619294720 | bytes 17317888 | tf_op jit(solution)/shard_map/ck,skrw->scrw/dot_general | solution.py:87
  192.5 8.2 %copy.55 = bf16[2,4,8,16,8,512]{5,3,1,4,0,2:T(8,128)(2,1)} copy(bf16[2,4,8,16,8,512]{5,3,2,1,4,0:T(8,128)(2,1)} %bitcast.100) | data formatting | bytes 16777216 | tf_op jit(solution)/shard_map/reshape | solution.py:92
  200.7 6.5 all-to-all-start.1
  207.3 0.1 fusion.52
  207.4 0.1 fusion.50
  207.4 0.1 fusion.48
  207.5 0.3 fusion.35
  207.8 0.3 fusion.33
  208.1 91.8 %all-to-all-done.1 = bf16[2,4,8,16,8,512]{5,3,1,4,0,2:T(8,128)(2,1)} async-done(((bf16[2,4,8,16,8,512]{5,3,1,4,0,2:T(8,128)(2,1)}), bf16[2,4,8,16,8,512]{5,3,1,4,0,2:T(8,128)(2,1)}, u32[]{:S(2)}, u32[]{:S(2)}) %all-to-all-start.1) | async-done | bytes 8388640 | tf_op jit(solution)/shard_map/all_to_all | solution.py:93
  299.9 11.6 %copy.56 = bf16[2,4,1,16,8,8,512]{6,5,0,4,3,1,2:T(8,128)(2,1)} copy(bf16[2,4,1,16,8,8,512]{6,3,1,4,0,5,2:T(8,128)(2,1)} %bitcast.12) | data formatting | bytes 16777216 | tf_op jit(solution)/shard_map/all_to_all | solution.py:93
  311.5 14.0 %reshape.257 = bf16[2,512,32,128,1]{3,2,0,1,4:T(8,128)(2,1)} reshape(bf16[2,4,1,16,8,8,512]{6,5,0,4,3,1,2:T(8,128)(2,1)} %copy.56) | data formatting | bytes 16777216 | tf_op jit(solution)/shard_map/reshape;reshape | solution.py:29
  325.4 7.4 %convolution_bitcast_fusion = f32[2,512,32,128]{3,2,0,1:T(8,128)S(1)} fusion(bf16[2,512,32,128,1]{3,2,0,1,4:T(8,128)(2,1)} %reshape.257, f32[1,32,2,32]{3,1,2,0:T(8,128)S(1)} %get-tuple-element.10, f32[1,32,2,32]{3,1,2,0:T(8,128)S(1)} %get-tuple-element.9), kind=kOutput, calls=%fused_computation.10 | convolution fusion | flops 1610616832 | bytes 25182208 | tf_op jit(solution)/shard_map/sjta,tmab->smjb/dot_general | solution.py:30
  332.8 7.1 %multiply_subtract_fusion = (f32[1,512,32,128]{3,2,0,1:T(8,128)}, f32[1,512,32,128]{3,2,0,1:T(8,128)}) fusion(f32[2,512,32,128]{3,2,0,1:T(8,128)S(1)} %convolution_bitcast_fusion, f32[32,128]{1,0:T(8,128)S(1)} %get-tuple-element.13, f32[32,128]{1,0:T(8,128)S(1)} %get-tuple-element.14), kind=kLoop, calls=%fused_computation.16 | loop fusion | flops 12582912 | bytes 33587200 | tf_op jit(solution)/shard_map/sub | solution.py:44
  339.9 11.8 %maximum_bitcast_fusion = f32[2,512,32,128,1]{3,2,0,1,4:T(8,128)} fusion(f32[1,512,32,128]{3,2,0,1:T(8,128)} %get-tuple-element.6, f32[1,512,32,128]{3,2,0,1:T(8,128)} %get-tuple-element.5), kind=kLoop, calls=%fused_computation | loop fusion | flops 4194304 | bytes 33554432 | tf_op jit(solution)/shard_map/stack | solution.py:42
  351.8 23.6 %bitcast_convert_fusion = bf16[512,32,2,128]{3,0,2,1:T(8,128)(2,1)} fusion(f32[2,512,32,128,1]{3,2,0,1,4:T(8,128)} %maximum_bitcast_fusion, f32[1,128,2,128]{3,1,2,0:T(8,128)S(1)} %get-tuple-element.8, f32[1,128,2,128]{3,1,2,0:T(8,128)S(1)} %get-tuple-element.7), kind=kOutput, calls=%fused_computation.3 | convolution fusion | flops 6446710784 | bytes 25427968 | tf_op jit(solution)/shard_map/sltb,tmjb->smjl/dot_general | solution.py:48
  375.4 10.3 %copy.58 = bf16[2,4,1,16,8,32,128]{6,4,3,0,5,2,1:T(8,128)(2,1)} copy(bf16[2,4,1,16,8,32,128]{6,4,3,1,0,5,2:T(8,128)(2,1)} %bitcast.98) | data formatting | bytes 16777216 | tf_op jit(solution)/shard_map/convert_element_type | solution.py:99
  385.7 189.2 %all_to_all.48 = bf16[2,4,1,16,8,32,128]{6,4,3,0,5,2,1:T(8,128)(2,1)S(1)} all-to-all(bf16[2,4,1,16,8,32,128]{6,4,3,0,5,2,1:T(8,128)(2,1)} %copy.58), channel_id=1, replica_groups=mesh['uv'=4,'chan'=8] {'uv'}, dimensions={1} | all-to-all | bytes 16777216 | tf_op jit(solution)/shard_map/all_to_all | solution.py:98
  574.9 7.9 %fusion.14 = bf16[2,16,32,128,32]{3,2,0,4,1:T(8,128)(2,1)} fusion(f32[1,32,2,32]{3,1,2,0:T(8,128)S(1)} %get-tuple-element.10, f32[1,32,2,32]{3,1,2,0:T(8,128)S(1)} %get-tuple-element.9, bf16[2,4,1,16,8,32,128]{6,4,3,0,5,2,1:T(8,128)(2,1)S(1)} %all_to_all.48), kind=kOutput, calls=%fused_computation.19 | convolution fusion | flops 1619005440 | bytes 16793600 | tf_op jit(solution)/shard_map/sxtu,tkujl->skxlj/dot_general | solution.py:60
  582.8 28.6 %copy.60 = bf16[2,16,32,128,32]{4,3,2,1,0:T(8,128)(2,1)} copy(bf16[2,16,32,128,32]{3,2,0,4,1:T(8,128)(2,1)} %fusion.14) | data formatting | bytes 16777216 | tf_op jit(solution)/shard_map/convert_element_type | solution.py:67
  611.4 41.6 %convert_element_type.125 = bf16[2,16,32,4096]{3,2,1,0:T(8,128)(2,1)} reshape(bf16[2,16,32,128,32]{4,3,2,1,0:T(8,128)(2,1)} %copy.60) | data formatting | bytes 16777216 | tf_op jit(solution)/shard_map/convert_element_type | solution.py:67
  (2 shorter events, 0.0 us)
Async XLA Ops:
  41.3 5.1 copy-start
  41.3 101.7 %copy-start.1 = (f32[512]{0:T(512)S(1)}, f32[512]{0:T(512)}, u32[]{:S(2)}) copy-start(f32[512]{0:T(512)} %param.6) | copy-start | bytes 6148
  41.3 101.7 %copy-start.2 = (f32[8]{0:T(128)S(1)}, f32[8]{0:T(128)}, u32[]{:S(2)}) copy-start(f32[8]{0:T(128)} %param.7) | copy-start | bytes 100
  41.3 101.8 %all-to-all-start = ((bf16[8,2,262144]{2,1,0:T(2,128)(2,1)}), bf16[8,2,262144]{2,1,0:T(2,128)(2,1)}, u32[]{:S(2)}, u32[]{:S(2)}) async-start(bf16[8,2,262144]{2,1,0:T(2,128)(2,1)} %reshape.267), calls=%async_computation | async-start | bytes 16777216 | tf_op jit(solution)/shard_map/all_to_all | solution.py:73
  200.7 99.1 %all-to-all-start.1 = ((bf16[2,4,8,16,8,512]{5,3,1,4,0,2:T(8,128)(2,1)}), bf16[2,4,8,16,8,512]{5,3,1,4,0,2:T(8,128)(2,1)}, u32[]{:S(2)}, u32[]{:S(2)}) async-start(bf16[2,4,8,16,8,512]{5,3,1,4,0,2:T(8,128)(2,1)} %copy.55), calls=%async_computation.1 | async-start | bytes 16777216 | tf_op jit(solution)/shard_map/all_to_all | solution.py:93
where the time goes:
time: 665 us; the launch traced here: 653 us
  blocking collectives  286 us (43%)
  local copies, waits for them, and re-layouts  190 us (29%)
  waiting for transfers between devices  91.8 us (14%)
  matrix products  53.5 us (8%)
  other arithmetic  19.9 us (3%)
  starting transfers between devices  11.6 us (2%)
    all_to_all x1, blocking collectives, shards(): lax.all_to_all(turned.astype(jnp.bfloat16), 'uv', split_axis=1, concat_ax...  189 us
    all_gather x1, blocking collectives, shards(): basis_full = lax.all_gather(eigen_basis, 'chan', axis=0, tiled=True)  96.7 us
    all_to_all x1, waiting for transfers between devices, shards(): lax.all_to_all(grouped, 'chan', split_axis=2, concat_axis=5, tiled=True)  91.8 us
    convert_element_type x2, local copies, waits for them, and re-layouts, row_transform(): (result.reshape(2, planes.shape[1], row_total, -1) * norm_scale).astype(j...  70.2 us
    unnamed x9, local copies, waits for them, and re-layouts  57.7 us
    dot_general x1, matrix products, column_transform(): jnp.einsum('sltb,tmjb->smjl', dft_table(inner_size), turned, precision=la...  23.6 us
    all_to_all x1, local copies, waits for them, and re-layouts, shards(): lax.all_to_all(visibility, 'chan', split_axis=3, concat_axis=1, tiled=True)  18.3 us
    dot_general x1, matrix products, shards(): jnp.einsum('ck,skrw->scrw', basis_full, foreground_signal, preferred_elem...  14.6 us
  transfers between devices with their start and end apart: 2, of which 1 were waited for; matrix products, arithmetic and copies ran while one was open for 0% of the time, Pallas kernels for 0%

commit v1 on v0

v1 whole, which is shorter than its diff:
```python
import functools
import math

import jax
import jax.numpy as jnp
import numpy as np
from jax import lax
from jax.experimental import pallas as pl
from jax.experimental.pallas import tpu as pltpu
from jax.sharding import PartitionSpec as P

LANES = 128
RADIX = 8
VMEM_BYTES = 56 * 1024 * 1024


def params():
    return pltpu.CompilerParams(vmem_limit_bytes=VMEM_BYTES)


def inner_table(size):
    position = np.arange(size)
    phase = 2.0 * np.pi * (np.outer(position, position) % size) / size
    cosine, sine = np.cos(phase), np.sin(phase)
    return np.block([[cosine, sine], [-sine, cosine]]).astype(jnp.bfloat16)


def twiddle_table(length):
    inner = length // RADIX
    phase = 2.0 * np.pi * np.outer(np.arange(RADIX), np.arange(inner)) / length
    return np.stack([np.cos(phase), np.sin(phase)], axis=1).astype(np.float32)


def lane_tables(length):
    span = LANES // RADIX
    table = np.zeros((RADIX, LANES, LANES), np.float32)
    for t in range(RADIX):
        for group in range(RADIX):
            y_lo = (group - t) % RADIX
            for h in range(span):
                table[t, group * span + h, h * RADIX + y_lo] = 1.0
    return table.astype(jnp.bfloat16)


def swap_table(major, minor):
    table = np.zeros((major * minor, major * minor), np.float32)
    for a in range(major):
        for b in range(minor):
            table[b * major + a, a * minor + b] = 1.0
    return table.astype(jnp.bfloat16)


def row_table(rows_dev, uv_count, group):
    total = rows_dev * uv_count
    position = np.arange(total)
    phase = 2.0 * np.pi * (np.outer(position, position) % total) / total
    cosine, sine = np.cos(phase), np.sin(phase)
    parts = np.array([[cosine, -sine], [sine, cosine]])
    parts = parts.reshape(2, 2, total, uv_count, rows_dev)
    eye = np.eye(group)
    table = np.einsum("tsxzu,cd->tcxzsdu", parts, eye)
    return table.reshape(2 * group * total, 2 * group * total).astype(jnp.bfloat16)


def butterfly8(re, im):
    def dft2(ar, ai, br, bi):
        return ar + br, ai + bi, ar - br, ai - bi

    def dft4(r, i):
        s0r, s0i, d0r, d0i = dft2(r[0], i[0], r[2], i[2])
        s1r, s1i, d1r, d1i = dft2(r[1], i[1], r[3], i[3])
        return (
            [s0r + s1r, d0r - d1i, s0r - s1r, d0r + d1i],
            [s0i + s1i, d0i + d1r, s0i - s1i, d0i - d1r],
        )

    er, ei = dft4(re[0::2], im[0::2])
    orr, oi = dft4(re[1::2], im[1::2])
    half = math.sqrt(0.5)
    turned_r = [orr[0], (orr[1] - oi[1]) * half, -oi[2], (-orr[3] - oi[3]) * half]
    turned_i = [oi[0], (orr[1] + oi[1]) * half, orr[2], (orr[3] - oi[3]) * half]
    out_r = [er[k] + turned_r[k] for k in range(4)] + [er[k] - turned_r[k] for k in range(4)]
    out_i = [ei[k] + turned_i[k] for k in range(4)] + [ei[k] - turned_i[k] for k in range(4)]
    return out_r, out_i


def column_kernel(x_ref, twiddle_ref, table_ref, out_ref, mid, wide):
    rows, length = x_ref.shape[1:]
    inner = length // RADIX
    width = out_ref.shape[3]
    step = 16

    def first(i, carry):
        at = pl.ds(pl.multiple_of(i * step, step), step)
        for block in range(inner // LANES):
            re, im = [], []
            for a in range(RADIX):
                lanes = slice(a * inner + block * LANES, a * inner + (block + 1) * LANES)
                re.append(x_ref[0, at, lanes].astype(jnp.float32))
                im.append(x_ref[1, at, lanes].astype(jnp.float32))
            re, im = butterfly8(re, im)
            lanes = slice(block * LANES, (block + 1) * LANES)
            for y_lo in range(RADIX):
                if y_lo == 0:
                    tr, ti = re[0], im[0]
                else:
                    cosine = twiddle_ref[y_lo, 0:1, lanes]
                    sine = twiddle_ref[y_lo, 1:2, lanes]
                    tr = re[y_lo] * cosine - im[y_lo] * sine
                    ti = re[y_lo] * sine + im[y_lo] * cosine
                mid[y_lo, at, lanes] = tr.astype(jnp.bfloat16)
                mid[y_lo, at, slice(inner + block * LANES, inner + (block + 1) * LANES)] = ti.astype(
                    jnp.bfloat16
                )
        return carry

    lax.fori_loop(0, rows // step, first, 0)
    for y_lo in range(RADIX):
        wide[y_lo] = jnp.dot(mid[y_lo], table_ref[...], preferred_element_type=jnp.float32)

    span = LANES // RADIX
    group_of = lax.broadcasted_iota(jnp.int32, (step, LANES), 1) // span

    def last(i, carry):
        at = pl.ds(pl.multiple_of(i * step, step), step)
        for part in range(2):
            for block in range(inner // LANES):
                lanes = slice(part * inner + block * LANES, part * inner + (block + 1) * LANES)
                tiles = []
                for y_lo in range(RADIX):
                    tile = wide[y_lo, at, lanes]
                    tiles.append(pltpu.roll(tile, y_lo * span, 1) if y_lo else tile)
                for t in range(RADIX):
                    value = tiles[(0 - t) % RADIX]
                    for group in range(1, RADIX):
                        value = jnp.where(group_of == group, tiles[(group - t) % RADIX], value)
                    start = (block * RADIX + t) * LANES
                    piece, lane = divmod(start, width)
                    out_ref[piece, part, at, lane : lane + LANES] = value.astype(jnp.bfloat16)
        return carry

    lax.fori_loop(0, rows // step, last, 0)


def column_transform(x, pieces):
    _, rows, length = x.shape
    inner = length // RADIX
    width = length // pieces
    block = math.gcd(rows, 64)
    return pl.pallas_call(
        column_kernel,
        grid=(rows // block,),
        in_specs=[
            pl.BlockSpec((2, block, length), lambda i: (0, i, 0)),
            pl.BlockSpec((RADIX, 2, inner), lambda i: (0, 0, 0)),
            pl.BlockSpec((2 * inner, 2 * inner), lambda i: (0, 0)),
        ],
        out_specs=pl.BlockSpec((pieces, 2, block, width), lambda i: (0, 0, i, 0)),
        out_shape=jax.ShapeDtypeStruct((pieces, 2, rows, width), jnp.bfloat16),
        scratch_shapes=[
            pltpu.VMEM((RADIX, block, 2 * inner), jnp.bfloat16),
            pltpu.VMEM((RADIX, block, 2 * inner), jnp.float32),
        ],
        compiler_params=params(),
        name="column_transform",
    )(x, jnp.asarray(twiddle_table(length)), jnp.asarray(inner_table(inner)))


def clean_kernel(group, x_ref, basis_ref, basis_t_ref, gain_ref, swap_ref, back_ref, lane_ref, out_ref, slab):
    sources, _, rows, width = x_ref.shape
    rows_dev, chans, _ = slab.shape
    tall = group * rows_dev
    for b in range(chans // group):
        if rows % tall == 0:
            source, row = divmod(b * tall, rows)
            tile = x_ref[source, 0, row : row + tall, :]
        else:
            take = tall // rows
            tile = x_ref[b * take : (b + 1) * take, 0].reshape(tall, width)
        turned = jnp.dot(swap_ref[...], tile, preferred_element_type=jnp.float32)
        slab[:, b * group : (b + 1) * group, :] = turned.astype(jnp.bfloat16).reshape(
            rows_dev, group, width
        )
    for u in range(rows_dev):
        line = slab[u]
        amps = jnp.dot(basis_t_ref[...], line, preferred_element_type=jnp.float32)
        amps = amps.astype(jnp.bfloat16).astype(jnp.float32)
        front = (gain_ref[:, u : u + 1] * amps).astype(jnp.bfloat16)
        drop = jnp.dot(basis_ref[...], front, preferred_element_type=jnp.float32)
        slab[u] = (line.astype(jnp.float32) - drop).astype(jnp.bfloat16)
    out_rows = out_ref.shape[2]
    for b in range(chans // group):
        tile = slab[:, b * group : (b + 1) * group, :].reshape(tall, width)
        turned = jnp.dot(back_ref[...], tile, preferred_element_type=jnp.float32).astype(jnp.bfloat16)
        for k in range(width // LANES):
            lanes = slice(k * LANES, (k + 1) * LANES)
            value = jnp.dot(turned[:, lanes], lane_ref[k], preferred_element_type=jnp.float32)
            if out_rows % tall == 0:
                target, row = divmod(b * tall, out_rows)
                out_ref[target, 0, row : row + tall, lanes] = value.astype(jnp.bfloat16)
            else:
                take = tall // out_rows
                out_ref[b * take : (b + 1) * take, 0, :, lanes] = value.reshape(
                    take, out_rows, LANES
                ).astype(jnp.bfloat16)


def clean(x, basis, gain, lane_table, targets, rows_dev):
    sources, _, rows, width = x.shape
    chans = basis.shape[0]
    group = 256 // rows_dev
    tile = min(width, 256)
    out_rows = chans * rows_dev // targets
    swap = swap_table(group, rows_dev)
    per_tile = tile // LANES
    return pl.pallas_call(
        functools.partial(clean_kernel, group),
        grid=(2, width // tile),
        in_specs=[
            pl.BlockSpec((sources, 1, rows, tile), lambda s, i: (0, s, 0, i)),
            pl.BlockSpec(basis.shape, lambda s, i: (0, 0)),
            pl.BlockSpec(basis.shape, lambda s, i: (0, 0)),
            pl.BlockSpec(gain.shape, lambda s, i: (0, 0)),
            pl.BlockSpec(swap.shape, lambda s, i: (0, 0)),
            pl.BlockSpec(swap.shape, lambda s, i: (0, 0)),
            pl.BlockSpec((per_tile, LANES, LANES), lambda s, i: (i, 0, 0)),
        ],
        out_specs=pl.BlockSpec((targets, 1, out_rows, tile), lambda s, i: (0, s, 0, i)),
        out_shape=jax.ShapeDtypeStruct((targets, 2, out_rows, width), jnp.bfloat16),
        scratch_shapes=[pltpu.VMEM((rows_dev, chans, tile), jnp.bfloat16)],
        compiler_params=params(),
        name="clean",
    )(x, basis, basis.T, gain, jnp.asarray(swap), jnp.asarray(np.ascontiguousarray(swap.T)), lane_table)


def row_kernel(scale, x_ref, table_ref, out_ref):
    z, _, parts, rows, width = x_ref.shape
    tall = z * parts * rows
    if rows % 16 == 0:
        tile = x_ref[:, 0].reshape(tall, width)
    else:
        tile = x_ref[:, 0].astype(jnp.float32).reshape(tall, width).astype(jnp.bfloat16)
    value = jnp.dot(table_ref[...], tile, preferred_element_type=jnp.float32) * scale
    out_ref[...] = value.reshape(out_ref.shape).astype(jnp.bfloat16)


def row_transform(x, chans, rows_dev):
    z, pieces, parts, rows, width = x.shape
    total = z * rows_dev
    length = pieces * width
    group = min(chans, max(1, 256 // (2 * total)))
    table = row_table(rows_dev, z, group)
    scale = 1.0 / math.sqrt(total * length)
    return pl.pallas_call(
        functools.partial(row_kernel, scale),
        grid=(chans // group, pieces),
        in_specs=[
            pl.BlockSpec((z, 1, 2, group * rows_dev, width), lambda c, j: (0, j, 0, c, 0)),
            pl.BlockSpec(table.shape, lambda c, j: (0, 0)),
        ],
        out_specs=pl.BlockSpec((2, group, total, width), lambda c, j: (0, c, 0, j)),
        out_shape=jax.ShapeDtypeStruct((2, chans, total, length), jnp.bfloat16),
        compiler_params=params(),
        name="row_transform",
    )(x, jnp.asarray(table))


def shards(visibility, eigen_basis, eigenvalues, noise_power):
    uv_count = lax.axis_size("uv")
    chan_count = lax.axis_size("chan")
    _, chans, rows_dev, length = visibility.shape
    width = length // chan_count
    out_chans = chans // uv_count
    flat = visibility.reshape(2, chans * rows_dev, length)
    pieces = column_transform(flat, chan_count)
    cells = lax.all_to_all(pieces, "chan", split_axis=0, concat_axis=0, tiled=True)
    basis = lax.all_gather(eigen_basis, "chan", axis=0, tiled=True)
    gain = eigenvalues[:, None] / (eigenvalues[:, None] + noise_power[None, :])
    per_piece = width // LANES
    first_tile = lax.rem(lax.axis_index("chan") * per_piece, RADIX)
    lanes = jnp.concatenate([jnp.asarray(lane_tables(length))] * 2, axis=0)
    lane_table = lax.dynamic_slice_in_dim(lanes, first_tile, per_piece, axis=0)
    cleaned = clean(cells, basis, gain, lane_table, uv_count * chan_count, rows_dev)
    planes = lax.all_to_all(cleaned, ("uv", "chan"), split_axis=0, concat_axis=0, tiled=True)
    planes = planes.reshape(uv_count, chan_count, 2, out_chans * rows_dev, width)
    return row_transform(planes, out_chans, rows_dev)


def solution(mesh):
    in_specs = (P(None, "chan", "uv", None), P("chan", None), P(), P("uv"))
    out_specs = P(None, ("uv", "chan"), None, None)
    return jax.shard_map(shards, mesh=mesh, in_specs=in_specs, out_specs=out_specs, check_vma=False)
```

time: 665 us -> 380 us (0.57)
  the two profiles are of different devices: /device:TPU:2 before, /device:TPU:8 now
where the time goes in v1:
time: 380 us; the launch traced here: 377 us
  blocking collectives  286 us (75%)
  Pallas kernels  82.7 us (22%)
  starting transfers between devices  5.09 us (1%)
    all_to_all x1, blocking collectives, shards(): lax.all_to_all(cleaned, ('uv', 'chan'), split_axis=0, concat_axis=0, tile...  188 us
    all_gather x1, blocking collectives, shards(): basis = lax.all_gather(eigen_basis, 'chan', axis=0, tiled=True)  98.3 us
    pallas_call x1, Pallas kernels, column_transform(): pl.pallas_call(column_kernel, grid=(rows // block,), in_specs=[pl.BlockSp...  39.2 us
    pallas_call x1, Pallas kernels, row_transform(): pl.pallas_call(functools.partial(row_kernel, scale), grid=(chans // group...  22.1 us
    pallas_call x1, Pallas kernels, clean(): pl.pallas_call(functools.partial(clean_kernel, group), grid=(2, width //...  21.4 us
  transfers between devices with their start and end apart: 1, of which 0 were waited for; matrix products, arithmetic and copies ran while one was open for 1% of the time, Pallas kernels for 0%

profile of v1, /device:TPU:8, one launch (start us, length us, event | category | flops | bytes accessed | tf_op | source)
XLA Modules:
  0.0 377.3 jit_solution(14926680202838745631)
XLA Ops:
  0.0 39.2 %column_transform.1 = bf16[8,2,512,512]{3,2,1,0:T(8,128)(2,1)} custom-call(bf16[2,512,4096]{2,1,0:T(8,128)(2,1)} %bitcast.4, f32[8,2,512]{2,1,0:T(2,128)} %constant.26.clone.twiddle_ref, bf16[1024,1024]{1,0:T(8,128)(2,1)} %constant.27.clone.table_ref), custom_call_target="tpu_custom_call" | custom-call | tf_op jit(solution)/shard_map/column_transform/pallas_call | solution.py:150
  39.2 0.0 copy-start.1
  39.2 0.0 copy-start.2
  39.2 0.0 copy-start.3
  39.2 5.1 %all-to-all-start = ((bf16[8,2,512,512]{3,2,1,0:T(8,128)(2,1)}), bf16[8,2,512,512]{3,2,1,0:T(8,128)(2,1)}, u32[]{:S(2)}, u32[]{:S(2)}) async-start(bf16[8,2,512,512]{3,2,1,0:T(8,128)(2,1)} %column_transform.1), calls=%async_computation | async-start | bytes 16777216 | tf_op jit(solution)/shard_map/all_to_all | solution.py:276
  44.3 0.0 copy-done.1
  44.3 98.3 %all_gather.3.basis_ref = bf16[512,512]{1,0:T(8,128)(2,1)S(1)} all-gather(bf16[64,512]{1,0:T(8,128)(2,1)S(1)} %copy-done.1), channel_id=1, replica_groups=mesh['uv'=4,'chan'=8] {'chan'}, dimensions={0}, use_global_device_ids=true | all-gather | bytes 589824 | tf_op jit(solution)/shard_map/all_gather | solution.py:277
  142.6 0.0 copy-start
  142.6 1.0 copy.14
  143.7 1.6 constant_dynamic-slice_fusion.lane_ref
  145.2 0.0 copy-done.2
  145.3 0.0 copy-done.3
  145.3 0.8 add_divide_fusion.gain_ref
  146.1 0.0 all-to-all-done.x_ref
  146.1 0.0 copy-done
  146.1 21.4 %clean.1 = bf16[32,2,128,512]{3,2,1,0:T(8,128)(2,1)} custom-call(bf16[8,2,512,512]{3,2,1,0:T(8,128)(2,1)} %all-to-all-done.x_ref, bf16[512,512]{1,0:T(8,128)(2,1)} %copy-done, bf16[512,512]{1,0:T(8,128)(2,1)} %bitcast.5, f32[512,8]{1,0:T(8,128)} %add_divide_fusion.gain_ref, bf16[256,256]{1,0:T(8,128)(2,1)} %constant.29.clone.swap_ref, ...), custom_call_target="tpu_custom_call" | custom-call | tf_op jit(solution)/shard_map/clean/pallas_call | solution.py:216
  167.5 187.7 %all_to_all.10 = bf16[32,2,128,512]{3,2,1,0:T(8,128)(2,1)} all-to-all(bf16[32,2,128,512]{3,2,1,0:T(8,128)(2,1)} %clean.1), channel_id=1, replica_groups=mesh['uv'=4,'chan'=8] {'uv','chan'}, dimensions={0} | all-to-all | bytes 16777216 | tf_op jit(solution)/shard_map/all_to_all | solution.py:284
  355.2 22.1 %row_transform.1 = bf16[2,16,32,4096]{3,2,1,0:T(8,128)(2,1)} custom-call(bf16[4,8,2,128,512]{4,3,2,1,0:T(8,128)(2,1)} %bitcast.3, bf16[256,256]{1,0:T(8,128)(2,1)} %constant.31.clone.table_ref), custom_call_target="tpu_custom_call" | custom-call | tf_op jit(solution)/shard_map/row_transform/pallas_call | solution.py:254
Async XLA Ops:
  39.2 5.1 %copy-start.1 = (bf16[64,512]{1,0:T(8,128)(2,1)S(1)}, bf16[64,512]{1,0:T(8,128)(2,1)}, u32[]{:S(2)}) copy-start(bf16[64,512]{1,0:T(8,128)(2,1)} %param.11) | copy-start | bytes 196612
  39.2 106.1 %copy-start.2 = (f32[512]{0:T(512)S(1)}, f32[512]{0:T(512)}, u32[]{:S(2)}) copy-start(f32[512]{0:T(512)} %param.12) | copy-start | bytes 6148
  39.2 106.1 %copy-start.3 = (f32[8]{0:T(128)S(1)}, f32[8]{0:T(128)}, u32[]{:S(2)}) copy-start(f32[8]{0:T(128)} %param.13) | copy-start | bytes 100
  39.2 106.9 %all-to-all-start = ((bf16[8,2,512,512]{3,2,1,0:T(8,128)(2,1)}), bf16[8,2,512,512]{3,2,1,0:T(8,128)(2,1)}, u32[]{:S(2)}, u32[]{:S(2)}) async-start(bf16[8,2,512,512]{3,2,1,0:T(8,128)(2,1)} %column_transform.1), calls=%async_computation | async-start | bytes 16777216 | tf_op jit(solution)/shard_map/all_to_all | solution.py:276
  142.6 3.5 copy-start

commit v2 on v1

v2 whole, which is shorter than its diff:
```python
import functools
import math

import jax
import jax.numpy as jnp
import numpy as np
from jax import lax
from jax.experimental import pallas as pl
from jax.experimental.pallas import tpu as pltpu
from jax.sharding import PartitionSpec as P

LANES = 128
RADIX = 8
VMEM_BYTES = 56 * 1024 * 1024


def params():
    return pltpu.CompilerParams(vmem_limit_bytes=VMEM_BYTES)


def inner_table(size):
    position = np.arange(size)
    phase = 2.0 * np.pi * (np.outer(position, position) % size) / size
    cosine, sine = np.cos(phase), np.sin(phase)
    return np.block([[cosine, sine], [-sine, cosine]]).astype(jnp.bfloat16)


def twiddle_table(length):
    inner = length // RADIX
    phase = 2.0 * np.pi * np.outer(np.arange(RADIX), np.arange(inner)) / length
    return np.stack([np.cos(phase), np.sin(phase)], axis=1).astype(np.float32)


def lane_tables(length):
    span = LANES // RADIX
    table = np.zeros((RADIX, LANES, LANES), np.float32)
    for t in range(RADIX):
        for group in range(RADIX):
            y_lo = (group - t) % RADIX
            for h in range(span):
                table[t, group * span + h, h * RADIX + y_lo] = 1.0
    return table.astype(jnp.bfloat16)


def swap_table(major, minor):
    table = np.zeros((major * minor, major * minor), np.float32)
    for a in range(major):
        for b in range(minor):
            table[b * major + a, a * minor + b] = 1.0
    return table.astype(jnp.bfloat16)


def row_tables(rows_dev, uv_count, group):
    total = rows_dev * uv_count
    position = np.arange(total)
    phase = 2.0 * np.pi * (np.outer(position, position) % total) / total
    cosine, sine = np.cos(phase), np.sin(phase)
    parts = np.array([[cosine, -sine], [sine, cosine]])
    parts = parts.reshape(2, 2, total, uv_count, rows_dev)
    eye = np.eye(group)
    size = 2 * group * total
    tables = []
    for at in range(uv_count):
        order = (at - np.arange(uv_count)) % uv_count
        table = np.einsum("tsxzu,cd->tcxzsdu", parts[:, :, :, order], eye)
        tables.append(table.reshape(size, size).astype(jnp.bfloat16))
    return np.stack(tables)


def butterfly8(re, im):
    def dft2(ar, ai, br, bi):
        return ar + br, ai + bi, ar - br, ai - bi

    def dft4(r, i):
        s0r, s0i, d0r, d0i = dft2(r[0], i[0], r[2], i[2])
        s1r, s1i, d1r, d1i = dft2(r[1], i[1], r[3], i[3])
        return (
            [s0r + s1r, d0r - d1i, s0r - s1r, d0r + d1i],
            [s0i + s1i, d0i + d1r, s0i - s1i, d0i - d1r],
        )

    er, ei = dft4(re[0::2], im[0::2])
    orr, oi = dft4(re[1::2], im[1::2])
    half = math.sqrt(0.5)
    turned_r = [orr[0], (orr[1] - oi[1]) * half, -oi[2], (-orr[3] - oi[3]) * half]
    turned_i = [oi[0], (orr[1] + oi[1]) * half, orr[2], (orr[3] - oi[3]) * half]
    out_r = [er[k] + turned_r[k] for k in range(4)] + [er[k] - turned_r[k] for k in range(4)]
    out_i = [ei[k] + turned_i[k] for k in range(4)] + [ei[k] - turned_i[k] for k in range(4)]
    return out_r, out_i


def column_kernel(x_ref, twiddle_ref, table_ref, *refs):
    *out_refs, mid, wide = refs
    rows, length = x_ref.shape[1:]
    inner = length // RADIX
    per_piece = len(out_refs)
    step = 16

    def first(i, carry):
        at = pl.ds(pl.multiple_of(i * step, step), step)
        for block in range(inner // LANES):
            re, im = [], []
            for a in range(RADIX):
                lanes = slice(a * inner + block * LANES, a * inner + (block + 1) * LANES)
                re.append(x_ref[0, at, lanes].astype(jnp.float32))
                im.append(x_ref[1, at, lanes].astype(jnp.float32))
            re, im = butterfly8(re, im)
            lanes = slice(block * LANES, (block + 1) * LANES)
            other = slice(inner + block * LANES, inner + (block + 1) * LANES)
            for y_lo in range(RADIX):
                if y_lo == 0:
                    tr, ti = re[0], im[0]
                else:
                    cosine = twiddle_ref[y_lo, 0:1, lanes]
                    sine = twiddle_ref[y_lo, 1:2, lanes]
                    tr = re[y_lo] * cosine - im[y_lo] * sine
                    ti = re[y_lo] * sine + im[y_lo] * cosine
                mid[y_lo, at, lanes] = tr.astype(jnp.bfloat16)
                mid[y_lo, at, other] = ti.astype(jnp.bfloat16)
        return carry

    lax.fori_loop(0, rows // step, first, 0)
    wide[...] = jnp.dot(
        mid[...].reshape(RADIX * rows, 2 * inner), table_ref[...], preferred_element_type=jnp.float32
    ).reshape(wide.shape)

    span = LANES // RADIX
    group_of = lax.broadcasted_iota(jnp.int32, (step, LANES), 1) // span

    def last(i, carry):
        at = pl.ds(pl.multiple_of(i * step, step), step)
        for part in range(2):
            for block in range(inner // LANES):
                lanes = slice(part * inner + block * LANES, part * inner + (block + 1) * LANES)
                tiles = []
                for y_lo in range(RADIX):
                    tile = wide[y_lo, at, lanes]
                    tiles.append(pltpu.roll(tile, y_lo * span, 1) if y_lo else tile)
                for t in range(RADIX):
                    value = tiles[(0 - t) % RADIX]
                    for group in range(1, RADIX):
                        value = jnp.where(group_of == group, tiles[(group - t) % RADIX], value)
                    piece, chunk = divmod(block * RADIX + t, per_piece)
                    out_refs[chunk][piece, part, at, :] = value.astype(jnp.bfloat16)
        return carry

    lax.fori_loop(0, rows // step, last, 0)


def column_transform(x, pieces):
    _, rows, length = x.shape
    inner = length // RADIX
    per_piece = length // pieces // LANES
    block = math.gcd(rows, 64)
    return pl.pallas_call(
        column_kernel,
        grid=(rows // block,),
        in_specs=[
            pl.BlockSpec((2, block, length), lambda i: (0, i, 0)),
            pl.BlockSpec((RADIX, 2, inner), lambda i: (0, 0, 0)),
            pl.BlockSpec((2 * inner, 2 * inner), lambda i: (0, 0)),
        ],
        out_specs=[pl.BlockSpec((pieces, 2, block, LANES), lambda i: (0, 0, i, 0))] * per_piece,
        out_shape=[jax.ShapeDtypeStruct((pieces, 2, rows, LANES), jnp.bfloat16)] * per_piece,
        scratch_shapes=[
            pltpu.VMEM((RADIX, block, 2 * inner), jnp.bfloat16),
            pltpu.VMEM((RADIX, block, 2 * inner), jnp.float32),
        ],
        compiler_params=params(),
        cost_estimate=pl.CostEstimate(
            flops=16 * rows * length * inner, bytes_accessed=8 * rows * length, transcendentals=0
        ),
        name="column_transform",
    )(x, jnp.asarray(twiddle_table(length)), jnp.asarray(inner_table(inner)))


def clean_kernel(group, at_ref, x_ref, basis_ref, basis_t_ref, gain_ref, swap_ref, back_ref, lane_ref, *refs):
    *out_refs, slab = refs
    sources, _, rows, _ = x_ref.shape
    chans = slab.shape[0]
    rows_dev = slab.shape[1] // LANES
    tall = group * rows_dev
    for b in range(chans // group):
        if rows % tall == 0:
            source, row = divmod(b * tall, rows)
            tile = x_ref[source, 0, row : row + tall, :]
        else:
            take = tall // rows
            tile = x_ref[b * take : (b + 1) * take, 0].reshape(tall, LANES)
        tile = jnp.dot(tile, lane_ref[...], preferred_element_type=jnp.float32).astype(jnp.bfloat16)
        turned = jnp.dot(swap_ref[...], tile, preferred_element_type=jnp.float32).astype(jnp.bfloat16)
        for u in range(rows_dev):
            slab[b * group : (b + 1) * group, u * LANES : (u + 1) * LANES] = turned[
                u * group : (u + 1) * group
            ]
    pair = math.gcd(rows_dev, 2)
    for first in range(0, rows_dev, pair):
        lanes = slice(first * LANES, (first + pair) * LANES)
        line = slab[:, lanes]
        amps = jnp.dot(basis_t_ref[...], line, preferred_element_type=jnp.float32)
        amps = amps.astype(jnp.bfloat16).astype(jnp.float32)
        front = jnp.concatenate(
            [
                gain_ref[:, first + k : first + k + 1] * amps[:, k * LANES : (k + 1) * LANES]
                for k in range(pair)
            ],
            axis=1,
        ).astype(jnp.bfloat16)
        drop = jnp.dot(basis_ref[...], front, preferred_element_type=jnp.float32)
        slab[:, lanes] = (line.astype(jnp.float32) - drop).astype(jnp.bfloat16)
    steps = len(out_refs)
    share = chans // steps
    out_rows = out_refs[0].shape[2]
    for step, out_ref in enumerate(out_refs):
        start = lax.rem(at_ref[0] + step, steps) * share
        for b in range(share // group):
            channels = pl.ds(pl.multiple_of(start + b * group, group), group)
            tile = jnp.concatenate(
                [slab[channels, u * LANES : (u + 1) * LANES] for u in range(rows_dev)], axis=0
            )
            value = jnp.dot(back_ref[...], tile, preferred_element_type=jnp.float32)
            if out_rows % tall == 0:
                target, row = divmod(b * tall, out_rows)
                out_ref[target, 0, row : row + tall, :] = value.astype(jnp.bfloat16)
            else:
                take = tall // out_rows
                out_ref[b * take : (b + 1) * take, 0] = value.reshape(
                    take, out_rows, LANES
                ).astype(jnp.bfloat16)


def clean(at, x, basis, gain, lane_table, steps, targets, rows_dev):
    sources, _, rows, _ = x.shape
    chans = basis.shape[0]
    group = 256 // rows_dev
    out_rows = chans * rows_dev // (targets * steps)
    swap = swap_table(group, rows_dev)
    whole = lambda s, at: (0, 0)
    return pl.pallas_call(
        functools.partial(clean_kernel, group),
        grid_spec=pltpu.PrefetchScalarGridSpec(
            num_scalar_prefetch=1,
            grid=(2,),
            in_specs=[
                pl.BlockSpec((sources, 1, rows, LANES), lambda s, at: (0, s, 0, 0)),
                pl.BlockSpec(basis.shape, whole),
                pl.BlockSpec(basis.shape, whole),
                pl.BlockSpec(gain.shape, whole),
                pl.BlockSpec(swap.shape, whole),
                pl.BlockSpec(swap.shape, whole),
                pl.BlockSpec((LANES, LANES), whole),
            ],
            out_specs=[
                pl.BlockSpec((targets, 1, out_rows, LANES), lambda s, at: (0, s, 0, 0))
            ] * steps,
            scratch_shapes=[pltpu.VMEM((chans, rows_dev * LANES), jnp.bfloat16)],
        ),
        out_shape=[jax.ShapeDtypeStruct((targets, 2, out_rows, LANES), jnp.bfloat16)] * steps,
        compiler_params=params(),
        cost_estimate=pl.CostEstimate(
            flops=12 * chans * chans * rows_dev * LANES,
            bytes_accessed=8 * chans * rows_dev * LANES,
            transcendentals=0,
        ),
        name="clean",
    )(at, x, basis, basis.T, gain, jnp.asarray(swap), jnp.asarray(np.ascontiguousarray(swap.T)), lane_table)


def row_kernel(scale, group, *refs):
    *x_refs, table_ref, out_ref = refs
    targets, _, chans, total, _ = out_ref.shape
    rows_dev = x_refs[0].shape[2] // chans
    tall = group * rows_dev
    for target in range(targets):
        for c in range(chans // group):
            rows = slice(c * tall, (c + 1) * tall)
            parts = [x_ref[target, s, rows, :] for x_ref in x_refs for s in range(2)]
            if tall % 16:
                parts = [part.astype(jnp.float32) for part in parts]
            tile = jnp.concatenate(parts, axis=0).astype(jnp.bfloat16)
            value = jnp.dot(table_ref[...], tile, preferred_element_type=jnp.float32) * scale
            out_ref[target, :, c * group : (c + 1) * group] = value.reshape(
                2, group, total, LANES
            ).astype(jnp.bfloat16)


def row_transform(pieces, at, chans, rows_dev, length):
    steps = len(pieces)
    targets, _, rows, _ = pieces[0].shape
    total = steps * rows_dev
    group = min(chans, max(1, 256 // (2 * total)))
    tables = jnp.asarray(row_tables(rows_dev, steps, group))
    table = lax.dynamic_index_in_dim(tables, at[0], 0, keepdims=False)
    scale = 1.0 / math.sqrt(total * length)
    block = math.gcd(targets, 2)
    return pl.pallas_call(
        functools.partial(row_kernel, scale, group),
        grid=(targets // block,),
        in_specs=[pl.BlockSpec((block, 2, rows, LANES), lambda j: (j, 0, 0, 0))] * steps
        + [pl.BlockSpec(table.shape, lambda j: (0, 0))],
        out_specs=pl.BlockSpec((block, 2, chans, total, LANES), lambda j: (j, 0, 0, 0, 0)),
        out_shape=jax.ShapeDtypeStruct((targets, 2, chans, total, LANES), jnp.bfloat16),
        compiler_params=params(),
        cost_estimate=pl.CostEstimate(
            flops=1024 * targets * chans * total * LANES,
            bytes_accessed=8 * targets * chans * total * LANES,
            transcendentals=0,
        ),
        name="row_transform",
    )(*pieces, table)


def place_kernel(x_ref, *refs):
    refs[-1][...] = x_ref[0]


def place(x, chunk, per_piece, held):
    pieces, _, chans, total, _ = x.shape
    shape = jax.ShapeDtypeStruct((2, chans, total, pieces * per_piece * LANES), jnp.bfloat16)
    return pl.pallas_call(
        place_kernel,
        grid=(pieces,),
        in_specs=[pl.BlockSpec((1, 2, chans, total, LANES), lambda j: (j, 0, 0, 0, 0))]
        + [pl.BlockSpec(memory_space=pl.ANY)] * len(held),
        out_specs=pl.BlockSpec((2, chans, total, LANES), lambda j: (0, 0, 0, j * per_piece + chunk)),
        out_shape=shape,
        input_output_aliases={1: 0} if held else {},
        compiler_params=params(),
        cost_estimate=pl.CostEstimate(
            flops=0, bytes_accessed=8 * pieces * chans * total * LANES, transcendentals=0
        ),
        name="place",
    )(x, *held)


def shards(visibility, eigen_basis, eigenvalues, noise_power):
    uv_count = lax.axis_size("uv")
    chan_count = lax.axis_size("chan")
    _, chans, rows_dev, length = visibility.shape
    per_piece = length // chan_count // LANES
    out_chans = chans // uv_count
    at = lax.axis_index("uv").astype(jnp.int32).reshape(1)
    basis = lax.all_gather(eigen_basis, "chan", axis=0, tiled=True)
    gain = eigenvalues[:, None] / (eigenvalues[:, None] + noise_power[None, :])
    lane_table = jnp.asarray(lane_tables(length))
    chunks = column_transform(visibility.reshape(2, chans * rows_dev, length), chan_count)
    cells = [
        lax.all_to_all(chunk, "chan", split_axis=0, concat_axis=0, tiled=True) for chunk in chunks
    ]
    held = []
    for k in range(per_piece):
        tile = lax.rem(lax.axis_index("chan") * per_piece + k, RADIX)
        lanes = lax.dynamic_index_in_dim(lane_table, tile, 0, keepdims=False)
        cleaned = clean(at, cells[k], basis, gain, lanes, uv_count, chan_count, rows_dev)
        pieces = [cleaned[0]] + [
            lax.ppermute(
                cleaned[step], "uv", [(z, (z + step) % uv_count) for z in range(uv_count)]
            )
            for step in range(1, uv_count)
        ]
        lines = row_transform(pieces, at, out_chans, rows_dev, length)
        returned = lax.all_to_all(lines, "chan", split_axis=0, concat_axis=0, tiled=True)
        held = [place(returned, k, per_piece, held)]
    return held[0]


def solution(mesh):
    in_specs = (P(None, "chan", "uv", None), P("chan", None), P(), P("uv"))
    out_specs = P(None, ("uv", "chan"), None, None)
    return jax.shard_map(shards, mesh=mesh, in_specs=in_specs, out_specs=out_specs, check_vma=False)
```

time: 380 us -> 466 us (1.23)
  waiting for transfers between devices: 0.01 us -> 186 us
  blocking collectives: 286 us -> 122 us
  starting transfers between devices: 5.09 us -> 36.2 us
  Pallas kernels: 82.7 us -> 111 us
  local copies, waits for them, and re-layouts: 2.62 us -> 9.76 us
    ppermute x0 -> x12, waiting for transfers between devices: none -> 176 us  [shards(): lax.ppermute(cleaned[step], 'uv', [(z, (z + step) % uv_count) for z in ra...]
    all_to_all x1 -> x3, blocking collectives: 188 us -> 90.7 us  [shards(): lax.all_to_all(chunk, 'chan', split_axis=0, concat_axis=0, tiled=True)]
    all_gather x1, blocking collectives: 98.3 us -> 30.9 us  [shards(): basis = lax.all_gather(eigen_basis, 'chan', axis=0, tiled=True)]
    pallas_call x2 -> x12, Pallas kernels: 43.5 us -> 85.7 us  [the longest x4 44 us: clean(): pl.pallas_call(functools.partial(clean_kernel, group), grid_spec=pltpu.Pr...]
    ppermute x0 -> x12, starting transfers between devices: none -> 16.1 us  [shards(): lax.ppermute(cleaned[step], 'uv', [(z, (z + step) % uv_count) for z in ra...]
    all_to_all x1 -> x5, starting transfers between devices: 5.09 us -> 20.1 us  [the longest x4 16.4 us: shards(): lax.all_to_all(lines, 'chan', split_axis=0, concat_axis=0, tiled=True)]
    pallas_call x1, Pallas kernels: 39.2 us -> 25 us  [column_transform(): pl.pallas_call(column_kernel, grid=(rows // block,), in_specs=[pl.BlockSp...]
    all_to_all x1 -> x5, waiting for transfers between devices: 0.01 us -> 9.74 us  [the longest x4 9.74 us: shards(): lax.all_to_all(lines, 'chan', split_axis=0, concat_axis=0, tiled=True)]
  transfers between devices with their start and end apart: 1 -> 17, of which waited for: 0 -> 13; matrix products, arithmetic and copies ran while one was open for 1% -> 1% of each run, Pallas kernels for 0% -> 17%
where the time goes in v2:
time: 466 us; the launch traced here: 465 us
  waiting for transfers between devices  186 us (40%)
  blocking collectives  122 us (26%)
  Pallas kernels  111 us (24%)
  starting transfers between devices  36.2 us (8%)
  local copies, waits for them, and re-layouts  9.76 us (2%)
    ppermute x12, waiting for transfers between devices, shards(): lax.ppermute(cleaned[step], 'uv', [(z, (z + step) % uv_count) for z in ra...  176 us
    all_to_all x3, blocking collectives, shards(): lax.all_to_all(chunk, 'chan', split_axis=0, concat_axis=0, tiled=True)  90.7 us
    pallas_call x4, Pallas kernels, clean(): pl.pallas_call(functools.partial(clean_kernel, group), grid_spec=pltpu.Pr...  44 us
    all_gather x1, blocking collectives, shards(): basis = lax.all_gather(eigen_basis, 'chan', axis=0, tiled=True)  30.9 us
    pallas_call x1, Pallas kernels, column_transform(): pl.pallas_call(column_kernel, grid=(rows // block,), in_specs=[pl.BlockSp...  25 us
    pallas_call x4, Pallas kernels, place(): pl.pallas_call(place_kernel, grid=(pieces,), in_specs=[pl.BlockSpec((1, 2...  22.6 us
    pallas_call x4, Pallas kernels, row_transform(): pl.pallas_call(functools.partial(row_kernel, scale, group), grid=(targets...  19.1 us
    all_to_all x4, starting transfers between devices, shards(): lax.all_to_all(lines, 'chan', split_axis=0, concat_axis=0, tiled=True)  16.4 us
  transfers between devices with their start and end apart: 17, of which 13 were waited for; matrix products, arithmetic and copies ran while one was open for 1% of the time, Pallas kernels for 17%

profile of v2, /device:TPU:8, one launch (start us, length us, event | category | flops | bytes accessed | tf_op | source)
XLA Modules:
  0.0 465.0 jit_solution(10862695548036824057)
XLA Ops:
  0.0 25.0 %column_transform.1 = (bf16[8,2,512,128]{3,2,1,0:T(8,128)(2,1)}, bf16[8,2,512,128]{3,2,1,0:T(8,128)(2,1)}, bf16[8,2,512,128]{3,2,1,0:T(8,128)(2,1)}, bf16[8,2,512,128]{3,2,1,0:T(8,128)(2,1)}) custom-call(bf16[2,512,4096]{2,1,0:T(8,128)(2,1)} %bitcast.17, f32[8,2,512]{2,1,0:T(2,128)} %constant.61.clone.twiddle_ref, bf16[1024,1024]{1,0:T(8,128)(2,1)} %constant.62.clone.table_ref), custom_call_target="tpu_custom_call" | custom-call | flops 17179869184 | bytes 16777216 | tf_op jit(solution)/shard_map/column_transform/pallas_call | solution.py:155
  25.0 31.1 %all_to_all.40.x_ref = bf16[8,2,512,128]{3,2,1,0:T(8,128)(2,1)} all-to-all(bf16[8,2,512,128]{3,2,1,0:T(8,128)(2,1)} %get-tuple-element.25), channel_id=1, replica_groups=mesh['uv'=4,'chan'=8] {'chan'}, dimensions={0} | all-to-all | bytes 4194304 | tf_op jit(solution)/shard_map/all_to_all | solution.py:348
  56.1 29.9 %all_to_all.41.x_ref = bf16[8,2,512,128]{3,2,1,0:T(8,128)(2,1)} all-to-all(bf16[8,2,512,128]{3,2,1,0:T(8,128)(2,1)S(1)} %copy-done.4), channel_id=1, replica_groups=mesh['uv'=4,'chan'=8] {'chan'}, dimensions={0} | all-to-all | bytes 4194304 | tf_op jit(solution)/shard_map/all_to_all | solution.py:348
  86.0 29.8 %all_to_all.42.x_ref = bf16[8,2,512,128]{3,2,1,0:T(8,128)(2,1)} all-to-all(bf16[8,2,512,128]{3,2,1,0:T(8,128)(2,1)S(1)} %copy-done.3), channel_id=1, replica_groups=mesh['uv'=4,'chan'=8] {'chan'}, dimensions={0} | all-to-all | bytes 4194304 | tf_op jit(solution)/shard_map/all_to_all | solution.py:348
  115.8 3.7 all-to-all-start.4
  119.5 30.9 %all_gather.3.basis_ref = bf16[512,512]{1,0:T(8,128)(2,1)S(1)} all-gather(bf16[64,512]{1,0:T(8,128)(2,1)S(1)} %copy-done.17), channel_id=1, replica_groups=mesh['uv'=4,'chan'=8] {'chan'}, dimensions={0}, use_global_device_ids=true | all-gather | bytes 589824 | tf_op jit(solution)/shard_map/all_gather | solution.py:343
  150.5 1.0 copy.28
  153.0 11.0 %clean.7 = (bf16[8,2,128,128]{3,2,1,0:T(8,128)(2,1)}, bf16[8,2,128,128]{3,2,1,0:T(8,128)(2,1)}, bf16[8,2,128,128]{3,2,1,0:T(8,128)(2,1)}, bf16[8,2,128,128]{3,2,1,0:T(8,128)(2,1)}) custom-call(s32[1]{0:T(128)} %bitcast.at_ref, bf16[8,2,512,128]{3,2,1,0:T(8,128)(2,1)} %all_to_all.42.x_ref, bf16[512,512]{1,0:T(8,128)(2,1)} %copy-done.5, ...), custom_call_target="tpu_custom_call" | custom-call | flops 3221225472 | bytes 4194304 | tf_op jit(solution)/shard_map/clean/pallas_call | solution.py:239
  164.0 1.6 collective-permute-start.9
  165.6 1.1 collective-permute-start.10
  166.6 2.0 collective-permute-start.11
  168.6 1.6 dynamic-slice_bitcast_fusion.refs_4_
  170.2 30.3 %collective-permute-done.9.refs_1_ = bf16[8,2,128,128]{3,2,1,0:T(8,128)(2,1)S(1)} collective-permute-done((bf16[8,2,128,128]{3,2,1,0:T(8,128)(2,1)}, bf16[8,2,128,128]{3,2,1,0:T(8,128)(2,1)S(1)}, u32[]{:S(2)}, u32[]{:S(2)}) %collective-permute-start.9) | collective-permute-done | bytes 524320 | tf_op jit(solution)/shard_map/ppermute | solution.py:356
  200.5 10.8 %collective-permute-done.10.refs_2_ = bf16[8,2,128,128]{3,2,1,0:T(8,128)(2,1)S(1)} collective-permute-done((bf16[8,2,128,128]{3,2,1,0:T(8,128)(2,1)}, bf16[8,2,128,128]{3,2,1,0:T(8,128)(2,1)S(1)}, u32[]{:S(2)}, u32[]{:S(2)}) %collective-permute-start.10) | collective-permute-done | bytes 524320 | tf_op jit(solution)/shard_map/ppermute | solution.py:356
  211.3 1.8 collective-permute-done.11.refs_3_
  213.1 4.8 %row_transform.7 = bf16[8,2,16,32,128]{4,3,2,1,0:T(8,128)(2,1)} custom-call(bf16[8,2,128,128]{3,2,1,0:T(8,128)(2,1)} %get-tuple-element.41.refs_0_, bf16[8,2,128,128]{3,2,1,0:T(8,128)(2,1)} %copy-done.6, bf16[8,2,128,128]{3,2,1,0:T(8,128)(2,1)} %copy-done.7, bf16[8,2,128,128]{3,2,1,0:T(8,128)(2,1)} %collective-permute-done.11.refs_3_, ...), custom_call_target="tpu_custom_call" | custom-call | flops 536870912 | bytes 4194304 | tf_op jit(solution)/shard_map/row_transform/pallas_call | solution.py:296
  217.9 1.3 copy-done.2
  219.2 3.6 all-to-all-start.7
  222.8 11.0 %clean.6 = (bf16[8,2,128,128]{3,2,1,0:T(8,128)(2,1)}, bf16[8,2,128,128]{3,2,1,0:T(8,128)(2,1)}, bf16[8,2,128,128]{3,2,1,0:T(8,128)(2,1)}, bf16[8,2,128,128]{3,2,1,0:T(8,128)(2,1)}) custom-call(s32[1]{0:T(128)} %bitcast.at_ref, bf16[8,2,512,128]{3,2,1,0:T(8,128)(2,1)} %copy-done.2, bf16[512,512]{1,0:T(8,128)(2,1)} %copy-done.5, bf16[512,512]{1,0:T(8,128)(2,1)} %bitcast.14, ...), custom_call_target="tpu_custom_call" | custom-call | flops 3221225472 | bytes 4194304 | tf_op jit(solution)/shard_map/clean/pallas_call | solution.py:239
  233.8 2.4 collective-permute-start.7
  236.2 2.0 collective-permute-start.8
  238.2 10.7 %collective-permute-done.6.refs_1_ = bf16[8,2,128,128]{3,2,1,0:T(8,128)(2,1)S(1)} collective-permute-done((bf16[8,2,128,128]{3,2,1,0:T(8,128)(2,1)}, bf16[8,2,128,128]{3,2,1,0:T(8,128)(2,1)S(1)}, u32[]{:S(2)}, u32[]{:S(2)}) %collective-permute-start.6) | collective-permute-done | bytes 524320 | tf_op jit(solution)/shard_map/ppermute | solution.py:356
  248.8 31.1 %collective-permute-done.7.refs_2_ = bf16[8,2,128,128]{3,2,1,0:T(8,128)(2,1)S(1)} collective-permute-done((bf16[8,2,128,128]{3,2,1,0:T(8,128)(2,1)}, bf16[8,2,128,128]{3,2,1,0:T(8,128)(2,1)S(1)}, u32[]{:S(2)}, u32[]{:S(2)}) %collective-permute-start.7) | collective-permute-done | bytes 524320 | tf_op jit(solution)/shard_map/ppermute | solution.py:356
  279.9 2.7 collective-permute-done.8.refs_3_
  283.4 4.8 %row_transform.6 = bf16[8,2,16,32,128]{4,3,2,1,0:T(8,128)(2,1)} custom-call(bf16[8,2,128,128]{3,2,1,0:T(8,128)(2,1)} %get-tuple-element.36.refs_0_, bf16[8,2,128,128]{3,2,1,0:T(8,128)(2,1)} %copy-done.9, bf16[8,2,128,128]{3,2,1,0:T(8,128)(2,1)} %copy-done.12, bf16[8,2,128,128]{3,2,1,0:T(8,128)(2,1)} %copy-done.15, ...), custom_call_target="tpu_custom_call" | custom-call | flops 536870912 | bytes 4194304 | tf_op jit(solution)/shard_map/row_transform/pallas_call | solution.py:296
  288.2 1.4 copy-done
  289.6 4.5 all-to-all-start.5
  294.1 11.0 %clean.5 = (bf16[8,2,128,128]{3,2,1,0:T(8,128)(2,1)}, bf16[8,2,128,128]{3,2,1,0:T(8,128)(2,1)}, bf16[8,2,128,128]{3,2,1,0:T(8,128)(2,1)}, bf16[8,2,128,128]{3,2,1,0:T(8,128)(2,1)}) custom-call(s32[1]{0:T(128)} %bitcast.at_ref, bf16[8,2,512,128]{3,2,1,0:T(8,128)(2,1)} %all_to_all.41.x_ref, bf16[512,512]{1,0:T(8,128)(2,1)} %copy-done.5, ...), custom_call_target="tpu_custom_call" | custom-call | flops 3221225472 | bytes 4194304 | tf_op jit(solution)/shard_map/clean/pallas_call | solution.py:239
  306.0 2.0 collective-permute-start.5
  307.9 12.1 %collective-permute-done.3.refs_1_ = bf16[8,2,128,128]{3,2,1,0:T(8,128)(2,1)S(1)} collective-permute-done((bf16[8,2,128,128]{3,2,1,0:T(8,128)(2,1)}, bf16[8,2,128,128]{3,2,1,0:T(8,128)(2,1)S(1)}, u32[]{:S(2)}, u32[]{:S(2)}) %collective-permute-start.3) | collective-permute-done | bytes 524320 | tf_op jit(solution)/shard_map/ppermute | solution.py:356
  320.1 30.9 %collective-permute-done.4.refs_2_ = bf16[8,2,128,128]{3,2,1,0:T(8,128)(2,1)S(1)} collective-permute-done((bf16[8,2,128,128]{3,2,1,0:T(8,128)(2,1)}, bf16[8,2,128,128]{3,2,1,0:T(8,128)(2,1)S(1)}, u32[]{:S(2)}, u32[]{:S(2)}) %collective-permute-start.4) | collective-permute-done | bytes 524320 | tf_op jit(solution)/shard_map/ppermute | solution.py:356
  350.9 1.2 collective-permute-done.5.refs_3_
  352.9 4.8 %row_transform.5 = bf16[8,2,16,32,128]{4,3,2,1,0:T(8,128)(2,1)} custom-call(bf16[8,2,128,128]{3,2,1,0:T(8,128)(2,1)} %get-tuple-element.31.refs_0_, bf16[8,2,128,128]{3,2,1,0:T(8,128)(2,1)} %copy-done.10, bf16[8,2,128,128]{3,2,1,0:T(8,128)(2,1)} %copy-done.13, bf16[8,2,128,128]{3,2,1,0:T(8,128)(2,1)} %copy-done.16, ...), custom_call_target="tpu_custom_call" | custom-call | flops 536870912 | bytes 4194304 | tf_op jit(solution)/shard_map/row_transform/pallas_call | solution.py:296
  357.7 3.9 all-to-all-start.3
  361.6 11.0 %clean.4 = (bf16[8,2,128,128]{3,2,1,0:T(8,128)(2,1)}, bf16[8,2,128,128]{3,2,1,0:T(8,128)(2,1)}, bf16[8,2,128,128]{3,2,1,0:T(8,128)(2,1)}, bf16[8,2,128,128]{3,2,1,0:T(8,128)(2,1)}) custom-call(s32[1]{0:T(128)} %bitcast.at_ref, bf16[8,2,512,128]{3,2,1,0:T(8,128)(2,1)} %all_to_all.40.x_ref, bf16[512,512]{1,0:T(8,128)(2,1)} %copy-done.5, ...), custom_call_target="tpu_custom_call" | custom-call | flops 3221225472 | bytes 4194304 | tf_op jit(solution)/shard_map/clean/pallas_call | solution.py:239
  372.6 2.3 collective-permute-start.1
  375.0 2.0 collective-permute-start.2
  376.9 10.6 %collective-permute-done.refs_1_ = bf16[8,2,128,128]{3,2,1,0:T(8,128)(2,1)S(1)} collective-permute-done((bf16[8,2,128,128]{3,2,1,0:T(8,128)(2,1)}, bf16[8,2,128,128]{3,2,1,0:T(8,128)(2,1)S(1)}, u32[]{:S(2)}, u32[]{:S(2)}) %collective-permute-start) | collective-permute-done | bytes 524320 | tf_op jit(solution)/shard_map/ppermute | solution.py:356
  387.6 31.2 %collective-permute-done.1.refs_2_ = bf16[8,2,128,128]{3,2,1,0:T(8,128)(2,1)S(1)} collective-permute-done((bf16[8,2,128,128]{3,2,1,0:T(8,128)(2,1)}, bf16[8,2,128,128]{3,2,1,0:T(8,128)(2,1)S(1)}, u32[]{:S(2)}, u32[]{:S(2)}) %collective-permute-start.1) | collective-permute-done | bytes 524320 | tf_op jit(solution)/shard_map/ppermute | solution.py:356
  418.8 2.7 collective-permute-done.2.refs_3_
  422.2 4.8 %row_transform.4 = bf16[8,2,16,32,128]{4,3,2,1,0:T(8,128)(2,1)} custom-call(bf16[8,2,128,128]{3,2,1,0:T(8,128)(2,1)} %get-tuple-element.26.refs_0_, bf16[8,2,128,128]{3,2,1,0:T(8,128)(2,1)} %copy-done.8, bf16[8,2,128,128]{3,2,1,0:T(8,128)(2,1)} %copy-done.11, bf16[8,2,128,128]{3,2,1,0:T(8,128)(2,1)} %copy-done.14, ...), custom_call_target="tpu_custom_call" | custom-call | flops 536870912 | bytes 4194304 | tf_op jit(solution)/shard_map/row_transform/pallas_call | solution.py:296
  427.0 1.3 copy-done.1
  428.3 4.4 all-to-all-start.1
  432.7 5.6 %place.4.refs_0_ = bf16[2,16,32,4096]{3,2,1,0:T(8,128)(2,1)} custom-call(bf16[8,2,16,32,128]{4,3,2,1,0:T(8,128)(2,1)} %copy-done), custom_call_target="tpu_custom_call" | custom-call | bytes 4194304 | tf_op jit(solution)/shard_map/place/pallas_call | solution.py:320
  438.4 5.6 %place.5.refs_0_ = bf16[2,16,32,4096]{3,2,1,0:T(8,128)(2,1)} custom-call(bf16[8,2,16,32,128]{4,3,2,1,0:T(8,128)(2,1)} %all-to-all-done.5.x_ref, bf16[2,16,32,4096]{3,2,1,0:T(8,128)(2,1)} %place.4.refs_0_), custom_call_target="tpu_custom_call", output_to_operand_aliasing={{}: (1, {})} | custom-call | bytes 4194304 | tf_op jit(solution)/shard_map/place/pallas_call | solution.py:320
  444.0 5.6 %place.6.refs_0_ = bf16[2,16,32,4096]{3,2,1,0:T(8,128)(2,1)} custom-call(bf16[8,2,16,32,128]{4,3,2,1,0:T(8,128)(2,1)} %copy-done.1, bf16[2,16,32,4096]{3,2,1,0:T(8,128)(2,1)} %place.5.refs_0_), custom_call_target="tpu_custom_call", output_to_operand_aliasing={{}: (1, {})} | custom-call | bytes 4194304 | tf_op jit(solution)/shard_map/place/pallas_call | solution.py:320
  449.7 9.7 %all-to-all-done.1.x_ref = bf16[8,2,16,32,128]{4,3,2,1,0:T(8,128)(2,1)} async-done(((bf16[8,2,16,32,128]{4,3,2,1,0:T(8,128)(2,1)}), bf16[8,2,16,32,128]{4,3,2,1,0:T(8,128)(2,1)}, u32[]{:S(2)}, u32[]{:S(2)}) %all-to-all-start.1) | async-done | bytes 2097184 | tf_op jit(solution)/shard_map/all_to_all | solution.py:362
  459.4 5.6 %place.7 = bf16[2,16,32,4096]{3,2,1,0:T(8,128)(2,1)} custom-call(bf16[8,2,16,32,128]{4,3,2,1,0:T(8,128)(2,1)} %all-to-all-done.1.x_ref, bf16[2,16,32,4096]{3,2,1,0:T(8,128)(2,1)} %place.6.refs_0_), custom_call_target="tpu_custom_call", output_to_operand_aliasing={{}: (1, {})} | custom-call | bytes 4194304 | tf_op jit(solution)/shard_map/place/pallas_call | solution.py:320
  (49 shorter events, 4.9 us)
Async XLA Ops:
  25.0 31.1 %copy-start.4 = (bf16[8,2,512,128]{3,2,1,0:T(8,128)(2,1)S(1)}, bf16[8,2,512,128]{3,2,1,0:T(8,128)(2,1)}, u32[]{:S(2)}) copy-start(bf16[8,2,512,128]{3,2,1,0:T(8,128)(2,1)} %get-tuple-element.30) | copy-start | bytes 6291460
  56.1 29.9 %copy-start.3 = (bf16[8,2,512,128]{3,2,1,0:T(8,128)(2,1)S(1)}, bf16[8,2,512,128]{3,2,1,0:T(8,128)(2,1)}, u32[]{:S(2)}) copy-start(bf16[8,2,512,128]{3,2,1,0:T(8,128)(2,1)} %get-tuple-element.40) | copy-start | bytes 6291460
  115.7 3.8 copy-start.17
  115.7 35.8 %copy-start.18 = (bf16[8,128,128]{2,1,0:T(8,128)(2,1)S(1)}, bf16[8,128,128]{2,1,0:T(8,128)(2,1)}, u32[]{:S(2)}) copy-start(bf16[8,128,128]{2,1,0:T(8,128)(2,1)} %constant.60.clone) | copy-start | bytes 786436
  115.7 36.4 %copy-start.19 = (f32[512]{0:T(512)S(1)}, f32[512]{0:T(512)}, u32[]{:S(2)}) copy-start(f32[512]{0:T(512)} %param.21) | copy-start | bytes 6148
  115.7 36.4 %copy-start.20 = (f32[8]{0:T(128)S(1)}, f32[8]{0:T(128)}, u32[]{:S(2)}) copy-start(f32[8]{0:T(128)} %param.22) | copy-start | bytes 100
  115.8 102.1 %all-to-all-start.4 = ((bf16[8,2,512,128]{3,2,1,0:T(8,128)(2,1)}), bf16[8,2,512,128]{3,2,1,0:T(8,128)(2,1)S(1)}, u32[]{:S(2)}, u32[]{:S(2)}) async-start(bf16[8,2,512,128]{3,2,1,0:T(8,128)(2,1)} %get-tuple-element.35), calls=%async_computation.4 | async-start | bytes 4194304 | tf_op jit(solution)/shard_map/all_to_all | solution.py:348
  150.5 2.5 copy-start.5
  164.0 36.5 %collective-permute-start.9 = (bf16[8,2,128,128]{3,2,1,0:T(8,128)(2,1)}, bf16[8,2,128,128]{3,2,1,0:T(8,128)(2,1)S(1)}, u32[]{:S(2)}, u32[]{:S(2)}) collective-permute-start(bf16[8,2,128,128]{3,2,1,0:T(8,128)(2,1)} %get-tuple-element.42), channel_id=1, source_target_pairs={{0,8},{8,16},{16,24},{24,0},{1,9},{9,17},{17,25},{25,1},{2,10},{10... | collective-permute-start | bytes 1572872 | tf_op jit(solution)/shard_map/ppermute | solution.py:356
  165.6 45.7 %collective-permute-start.10 = (bf16[8,2,128,128]{3,2,1,0:T(8,128)(2,1)}, bf16[8,2,128,128]{3,2,1,0:T(8,128)(2,1)S(1)}, u32[]{:S(2)}, u32[]{:S(2)}) collective-permute-start(bf16[8,2,128,128]{3,2,1,0:T(8,128)(2,1)} %get-tuple-element.43), channel_id=1, source_target_pairs={{0,16},{8,24},{16,0},{24,8},{1,17},{9,25},{17,1},{25,9},{2,18},{10... | collective-permute-start | bytes 1572872 | tf_op jit(solution)/shard_map/ppermute | solution.py:356
  166.6 46.4 %collective-permute-start.11 = (bf16[8,2,128,128]{3,2,1,0:T(8,128)(2,1)}, bf16[8,2,128,128]{3,2,1,0:T(8,128)(2,1)}, u32[]{:S(2)}, u32[]{:S(2)}) collective-permute-start(bf16[8,2,128,128]{3,2,1,0:T(8,128)(2,1)} %get-tuple-element.44), channel_id=1, source_target_pairs={{0,24},{8,0},{16,8},{24,16},{1,25},{9,1},{17,9},{25,17},{2,26},{10... | collective-permute-start | bytes 1572872 | tf_op jit(solution)/shard_map/ppermute | solution.py:356
  200.5 12.6 %copy-start.6 = (bf16[8,2,128,128]{3,2,1,0:T(8,128)(2,1)}, bf16[8,2,128,128]{3,2,1,0:T(8,128)(2,1)S(1)}, u32[]{:S(2)}) copy-start(bf16[8,2,128,128]{3,2,1,0:T(8,128)(2,1)S(1)} %collective-permute-done.9.refs_1_) | copy-start | bytes 1572868
  211.3 1.8 copy-start.7
  217.9 1.3 copy-start.2
  219.2 69.0 %all-to-all-start.7 = ((bf16[8,2,16,32,128]{4,3,2,1,0:T(8,128)(2,1)}), bf16[8,2,16,32,128]{4,3,2,1,0:T(8,128)(2,1)S(1)}, u32[]{:S(2)}, u32[]{:S(2)}) async-start(bf16[8,2,16,32,128]{4,3,2,1,0:T(8,128)(2,1)} %row_transform.7), calls=%async_computation.7 | async-start | bytes 4194304 | tf_op jit(solution)/shard_map/all_to_all | solution.py:362
  233.8 15.0 %collective-permute-start.6 = (bf16[8,2,128,128]{3,2,1,0:T(8,128)(2,1)}, bf16[8,2,128,128]{3,2,1,0:T(8,128)(2,1)S(1)}, u32[]{:S(2)}, u32[]{:S(2)}) collective-permute-start(bf16[8,2,128,128]{3,2,1,0:T(8,128)(2,1)} %get-tuple-element.37), channel_id=1, source_target_pairs={{0,8},{8,16},{16,24},{24,0},{1,9},{9,17},{17,25},{25,1},{2,10},{10... | collective-permute-start | bytes 1572872 | tf_op jit(solution)/shard_map/ppermute | solution.py:356
  233.8 46.0 %collective-permute-start.7 = (bf16[8,2,128,128]{3,2,1,0:T(8,128)(2,1)}, bf16[8,2,128,128]{3,2,1,0:T(8,128)(2,1)S(1)}, u32[]{:S(2)}, u32[]{:S(2)}) collective-permute-start(bf16[8,2,128,128]{3,2,1,0:T(8,128)(2,1)} %get-tuple-element.38), channel_id=1, source_target_pairs={{0,16},{8,24},{16,0},{24,8},{1,17},{9,25},{17,1},{25,9},{2,18},{10... | collective-permute-start | bytes 1572872 | tf_op jit(solution)/shard_map/ppermute | solution.py:356
  236.2 46.3 %collective-permute-start.8 = (bf16[8,2,128,128]{3,2,1,0:T(8,128)(2,1)}, bf16[8,2,128,128]{3,2,1,0:T(8,128)(2,1)S(1)}, u32[]{:S(2)}, u32[]{:S(2)}) collective-permute-start(bf16[8,2,128,128]{3,2,1,0:T(8,128)(2,1)} %get-tuple-element.39), channel_id=1, source_target_pairs={{0,24},{8,0},{16,8},{24,16},{1,25},{9,1},{17,9},{25,17},{2,26},{10... | collective-permute-start | bytes 1572872 | tf_op jit(solution)/shard_map/ppermute | solution.py:356
  248.8 33.7 %copy-start.9 = (bf16[8,2,128,128]{3,2,1,0:T(8,128)(2,1)}, bf16[8,2,128,128]{3,2,1,0:T(8,128)(2,1)S(1)}, u32[]{:S(2)}) copy-start(bf16[8,2,128,128]{3,2,1,0:T(8,128)(2,1)S(1)} %collective-permute-done.6.refs_1_) | copy-start | bytes 1572868
  279.9 2.7 copy-start.12
  282.5 0.8 copy-start.15
  288.2 1.4 copy-start
  289.6 68.1 %all-to-all-start.5 = ((bf16[8,2,16,32,128]{4,3,2,1,0:T(8,128)(2,1)}), bf16[8,2,16,32,128]{4,3,2,1,0:T(8,128)(2,1)}, u32[]{:S(2)}, u32[]{:S(2)}) async-start(bf16[8,2,16,32,128]{4,3,2,1,0:T(8,128)(2,1)} %row_transform.6), calls=%async_computation.5 | async-start | bytes 4194304 | tf_op jit(solution)/shard_map/all_to_all | solution.py:362
  305.1 15.0 %collective-permute-start.3 = (bf16[8,2,128,128]{3,2,1,0:T(8,128)(2,1)}, bf16[8,2,128,128]{3,2,1,0:T(8,128)(2,1)S(1)}, u32[]{:S(2)}, u32[]{:S(2)}) collective-permute-start(bf16[8,2,128,128]{3,2,1,0:T(8,128)(2,1)} %get-tuple-element.32), channel_id=1, source_target_pairs={{0,8},{8,16},{16,24},{24,0},{1,9},{9,17},{17,25},{25,1},{2,10},{10... | collective-permute-start | bytes 1572872 | tf_op jit(solution)/shard_map/ppermute | solution.py:356
  305.1 45.8 %collective-permute-start.4 = (bf16[8,2,128,128]{3,2,1,0:T(8,128)(2,1)}, bf16[8,2,128,128]{3,2,1,0:T(8,128)(2,1)S(1)}, u32[]{:S(2)}, u32[]{:S(2)}) collective-permute-start(bf16[8,2,128,128]{3,2,1,0:T(8,128)(2,1)} %get-tuple-element.33), channel_id=1, source_target_pairs={{0,16},{8,24},{16,0},{24,8},{1,17},{9,25},{17,1},{25,9},{2,18},{10... | collective-permute-start | bytes 1572872 | tf_op jit(solution)/shard_map/ppermute | solution.py:356
  306.0 46.2 %collective-permute-start.5 = (bf16[8,2,128,128]{3,2,1,0:T(8,128)(2,1)}, bf16[8,2,128,128]{3,2,1,0:T(8,128)(2,1)S(1)}, u32[]{:S(2)}, u32[]{:S(2)}) collective-permute-start(bf16[8,2,128,128]{3,2,1,0:T(8,128)(2,1)} %get-tuple-element.34), channel_id=1, source_target_pairs={{0,24},{8,0},{16,8},{24,16},{1,25},{9,1},{17,9},{25,17},{2,26},{10... | collective-permute-start | bytes 1572872 | tf_op jit(solution)/shard_map/ppermute | solution.py:356
  320.1 32.1 %copy-start.10 = (bf16[8,2,128,128]{3,2,1,0:T(8,128)(2,1)}, bf16[8,2,128,128]{3,2,1,0:T(8,128)(2,1)S(1)}, u32[]{:S(2)}) copy-start(bf16[8,2,128,128]{3,2,1,0:T(8,128)(2,1)S(1)} %collective-permute-done.3.refs_1_) | copy-start | bytes 1572868
  350.9 1.2 copy-start.13
  352.1 0.8 copy-start.16
  357.7 69.3 %all-to-all-start.3 = ((bf16[8,2,16,32,128]{4,3,2,1,0:T(8,128)(2,1)}), bf16[8,2,16,32,128]{4,3,2,1,0:T(8,128)(2,1)S(1)}, u32[]{:S(2)}, u32[]{:S(2)}) async-start(bf16[8,2,16,32,128]{4,3,2,1,0:T(8,128)(2,1)} %row_transform.5), calls=%async_computation.3 | async-start | bytes 4194304 | tf_op jit(solution)/shard_map/all_to_all | solution.py:362
  372.6 14.9 %collective-permute-start = (bf16[8,2,128,128]{3,2,1,0:T(8,128)(2,1)}, bf16[8,2,128,128]{3,2,1,0:T(8,128)(2,1)S(1)}, u32[]{:S(2)}, u32[]{:S(2)}) collective-permute-start(bf16[8,2,128,128]{3,2,1,0:T(8,128)(2,1)} %get-tuple-element.27), channel_id=1, source_target_pairs={{0,8},{8,16},{16,24},{24,0},{1,9},{9,17},{17,25},{25,1},{2,10},{10... | collective-permute-start | bytes 1572872 | tf_op jit(solution)/shard_map/ppermute | solution.py:356
  372.6 46.1 %collective-permute-start.1 = (bf16[8,2,128,128]{3,2,1,0:T(8,128)(2,1)}, bf16[8,2,128,128]{3,2,1,0:T(8,128)(2,1)S(1)}, u32[]{:S(2)}, u32[]{:S(2)}) collective-permute-start(bf16[8,2,128,128]{3,2,1,0:T(8,128)(2,1)} %get-tuple-element.28), channel_id=1, source_target_pairs={{0,16},{8,24},{16,0},{24,8},{1,17},{9,25},{17,1},{25,9},{2,18},{10... | collective-permute-start | bytes 1572872 | tf_op jit(solution)/shard_map/ppermute | solution.py:356
  375.0 46.5 %collective-permute-start.2 = (bf16[8,2,128,128]{3,2,1,0:T(8,128)(2,1)}, bf16[8,2,128,128]{3,2,1,0:T(8,128)(2,1)S(1)}, u32[]{:S(2)}, u32[]{:S(2)}) collective-permute-start(bf16[8,2,128,128]{3,2,1,0:T(8,128)(2,1)} %get-tuple-element.29), channel_id=1, source_target_pairs={{0,24},{8,0},{16,8},{24,16},{1,25},{9,1},{17,9},{25,17},{2,26},{10... | collective-permute-start | bytes 1572872 | tf_op jit(solution)/shard_map/ppermute | solution.py:356
  387.6 33.9 %copy-start.8 = (bf16[8,2,128,128]{3,2,1,0:T(8,128)(2,1)}, bf16[8,2,128,128]{3,2,1,0:T(8,128)(2,1)S(1)}, u32[]{:S(2)}) copy-start(bf16[8,2,128,128]{3,2,1,0:T(8,128)(2,1)S(1)} %collective-permute-done.refs_1_) | copy-start | bytes 1572868
  418.8 2.7 copy-start.11
  421.4 0.8 copy-start.14
  427.0 1.3 copy-start.1
  428.3 31.0 %all-to-all-start.1 = ((bf16[8,2,16,32,128]{4,3,2,1,0:T(8,128)(2,1)}), bf16[8,2,16,32,128]{4,3,2,1,0:T(8,128)(2,1)}, u32[]{:S(2)}, u32[]{:S(2)}) async-start(bf16[8,2,16,32,128]{4,3,2,1,0:T(8,128)(2,1)} %row_transform.4), calls=%async_computation.1 | async-start | bytes 4194304 | tf_op jit(solution)/shard_map/all_to_all | solution.py:362

commit v3 on v2

--- a/solution.py
+++ b/solution.py
@@ -174,8 +174,11 @@
     )(x, jnp.asarray(twiddle_table(length)), jnp.asarray(inner_table(inner)))
 
 
-def clean_kernel(group, at_ref, x_ref, basis_ref, basis_t_ref, gain_ref, swap_ref, back_ref, lane_ref, *refs):
-    *out_refs, slab = refs
+def clean_kernel(
+    group, later, at_ref, x_ref, basis_ref, basis_t_ref, gain_ref, swap_ref, back_ref, lane_ref, *refs
+):
+    *out_refs, slab = refs[later:]
+    out_refs = out_refs[: len(out_refs) - later]
     sources, _, rows, _ = x_ref.shape
     chans = slab.shape[0]
     rows_dev = slab.shape[1] // LANES
@@ -229,7 +232,7 @@
                 ).astype(jnp.bfloat16)
 
 
-def clean(at, x, basis, gain, lane_table, steps, targets, rows_dev):
+def clean(at, x, basis, basis_t, gain, lane_table, steps, targets, rows_dev, later):
     sources, _, rows, _ = x.shape
     chans = basis.shape[0]
     group = 256 // rows_dev
@@ -237,7 +240,7 @@
     swap = swap_table(group, rows_dev)
     whole = lambda s, at: (0, 0)
     return pl.pallas_call(
-        functools.partial(clean_kernel, group),
+        functools.partial(clean_kernel, group, len(later)),
         grid_spec=pltpu.PrefetchScalarGridSpec(
             num_scalar_prefetch=1,
             grid=(2,),
@@ -249,13 +252,17 @@
                 pl.BlockSpec(swap.shape, whole),
                 pl.BlockSpec(swap.shape, whole),
                 pl.BlockSpec((LANES, LANES), whole),
-            ],
+            ]
+            + [pl.BlockSpec(memory_space=pl.ANY)] * len(later),
             out_specs=[
                 pl.BlockSpec((targets, 1, out_rows, LANES), lambda s, at: (0, s, 0, 0))
-            ] * steps,
+            ] * steps
+            + [pl.BlockSpec(memory_space=pl.ANY)] * len(later),
             scratch_shapes=[pltpu.VMEM((chans, rows_dev * LANES), jnp.bfloat16)],
         ),
-        out_shape=[jax.ShapeDtypeStruct((targets, 2, out_rows, LANES), jnp.bfloat16)] * steps,
+        out_shape=[jax.ShapeDtypeStruct((targets, 2, out_rows, LANES), jnp.bfloat16)] * steps
+        + [jax.ShapeDtypeStruct(a.shape, a.dtype) for a in later],
+        input_output_aliases={8 + i: steps + i for i in range(len(later))},
         compiler_params=params(),
         cost_estimate=pl.CostEstimate(
             flops=12 * chans * chans * rows_dev * LANES,
@@ -263,11 +270,21 @@
             transcendentals=0,
         ),
         name="clean",
-    )(at, x, basis, basis.T, gain, jnp.asarray(swap), jnp.asarray(np.ascontiguousarray(swap.T)), lane_table)
-
-
-def row_kernel(scale, group, *refs):
-    *x_refs, table_ref, out_ref = refs
+    )(
+        at,
+        x,
+        basis,
+        basis_t,
+        gain,
+        jnp.asarray(swap),
+        jnp.asarray(np.ascontiguousarray(swap.T)),
+        lane_table,
+        *later,
+    )
+
+
+def row_kernel(scale, group, steps, *refs):
+    x_refs, table_ref, out_ref = refs[:steps], refs[steps], refs[-1]
     targets, _, chans, total, _ = out_ref.shape
     rows_dev = x_refs[0].shape[2] // chans
     tall = group * rows_dev
@@ -284,7 +301,7 @@
             ).astype(jnp.bfloat16)
 
 
-def row_transform(pieces, at, chans, rows_dev, length):
+def row_transform(pieces, at, chans, rows_dev, length, after):
     steps = len(pieces)
     targets, _, rows, _ = pieces[0].shape
     total = steps * rows_dev
@@ -294,10 +311,11 @@
     scale = 1.0 / math.sqrt(total * length)
     block = math.gcd(targets, 2)
     return pl.pallas_call(
-        functools.partial(row_kernel, scale, group),
+        functools.partial(row_kernel, scale, group, steps),
         grid=(targets // block,),
         in_specs=[pl.BlockSpec((block, 2, rows, LANES), lambda j: (j, 0, 0, 0))] * steps
-        + [pl.BlockSpec(table.shape, lambda j: (0, 0))],
+        + [pl.BlockSpec(table.shape, lambda j: (0, 0))]
+        + [pl.BlockSpec(memory_space=pl.ANY)] * len(after),
         out_specs=pl.BlockSpec((block, 2, chans, total, LANES), lambda j: (j, 0, 0, 0, 0)),
         out_shape=jax.ShapeDtypeStruct((targets, 2, chans, total, LANES), jnp.bfloat16),
         compiler_params=params(),
@@ -307,7 +325,7 @@
             transcendentals=0,
         ),
         name="row_transform",
-    )(*pieces, table)
+    )(*pieces, table, *after)
 
 
 def place_kernel(x_ref, *refs):
@@ -333,34 +351,64 @@
     )(x, *held)
 
 
+def turn_kernel(basis_ref, _, out_ref, __):
+    out_ref[...] = basis_ref[...].T
+
+
+def turn(basis, later):
+    return pl.pallas_call(
+        turn_kernel,
+        in_specs=[pl.BlockSpec(memory_space=pltpu.VMEM), pl.BlockSpec(memory_space=pl.ANY)],
+        out_specs=[pl.BlockSpec(memory_space=pltpu.VMEM), pl.BlockSpec(memory_space=pl.ANY)],
+        out_shape=[
+            jax.ShapeDtypeStruct(basis.shape, basis.dtype),
+            jax.ShapeDtypeStruct(later.shape, later.dtype),
+        ],
+        input_output_aliases={1: 1},
+        compiler_params=params(),
+        name="turn",
+    )(basis, later)
+
+
+def exchange(x):
+    return lax.all_to_all(x, "chan", split_axis=0, concat_axis=0, tiled=True)
+
+
 def shards(visibility, eigen_basis, eigenvalues, noise_power):
     uv_count = lax.axis_size("uv")
     chan_count = lax.axis_size("chan")
     _, chans, rows_dev, length = visibility.shape
-    per_piece = length // chan_count // LANES
+    count = length // chan_count // LANES
     out_chans = chans // uv_count
     at = lax.axis_index("uv").astype(jnp.int32).reshape(1)
-    basis = lax.all_gather(eigen_basis, "chan", axis=0, tiled=True)
+    basis = exchange(jnp.broadcast_to(eigen_basis, (chan_count,) + eigen_basis.shape))
+    basis = basis.reshape(chan_count * chans, -1)
     gain = eigenvalues[:, None] / (eigenvalues[:, None] + noise_power[None, :])
     lane_table = jnp.asarray(lane_tables(length))
-    chunks = column_transform(visibility.reshape(2, chans * rows_dev, length), chan_count)
-    cells = [
-        lax.all_to_all(chunk, "chan", split_axis=0, concat_axis=0, tiled=True) for chunk in chunks
-    ]
-    held = []
-    for k in range(per_piece):
-        tile = lax.rem(lax.axis_index("chan") * per_piece + k, RADIX)
+    chunks = list(column_transform(visibility.reshape(2, chans * rows_dev, length), chan_count))
+    basis_t, chunks[0] = turn(basis, chunks[0])
+    cells, cleaned, held = [], [], []
+    for k in range(min(2, count)):
+        cells.append(exchange(chunks[k]))
+    for k in range(count):
+        tile = lax.rem(lax.axis_index("chan") * count + k, RADIX)
         lanes = lax.dynamic_index_in_dim(lane_table, tile, 0, keepdims=False)
-        cleaned = clean(at, cells[k], basis, gain, lanes, uv_count, chan_count, rows_dev)
-        pieces = [cleaned[0]] + [
+        result = clean(
+            at, cells[k], basis, basis_t, gain, lanes, uv_count, chan_count, rows_dev, chunks[k + 2 : k + 3]
+        )
+        cleaned.append(result[:uv_count])
+        if k + 2 < count:
+            cells.append(exchange(result[uv_count]))
+    for k in range(count):
+        pieces = [cleaned[k][0]] + [
             lax.ppermute(
-                cleaned[step], "uv", [(z, (z + step) % uv_count) for z in range(uv_count)]
+                cleaned[k][step], "uv", [(z, (z + step) % uv_count) for z in range(uv_count)]
             )
             for step in range(1, uv_count)
         ]
-        lines = row_transform(pieces, at, out_chans, rows_dev, length)
-        returned = lax.all_to_all(lines, "chan", split_axis=0, concat_axis=0, tiled=True)
-        held = [place(returned, k, per_piece, held)]
+        after = [parts[0] for parts in cleaned[k + 2 : k + 3]] + cells[k + 3 : k + 4]
+        lines = row_transform(pieces, at, out_chans, rows_dev, length, after)
+        held = [place(exchange(lines), k, count, held)]
     return held[0]
 
 

time: 466 us -> 401 us (0.86)
  blocking collectives: 122 us -> 0 us
  waiting for transfers between devices: 186 us -> 218 us
  starting transfers between devices: 36.2 us -> 52.5 us
  local copies, waits for them, and re-layouts: 9.76 us -> 14.7 us
    all_to_all x3 -> x0, blocking collectives: 90.7 us -> none  [shards(): lax.all_to_all(chunk, 'chan', split_axis=0, concat_axis=0, tiled=True)]
    all_to_all x5 -> x9, waiting for transfers between devices: 9.74 us -> 63.9 us  [exchange(): return lax.all_to_all(x, 'chan', split_axis=0, concat_axis=0, tiled=True)]
    all_gather x1 -> x0, blocking collectives: 30.9 us -> none  [shards(): basis = lax.all_gather(eigen_basis, 'chan', axis=0, tiled=True)]
    ppermute x12, waiting for transfers between devices: 176 us -> 154 us  [shards(): lax.ppermute(cleaned[k][step], 'uv', [(z, (z + step) % uv_count) for z in...]
    all_to_all x5 -> x9, starting transfers between devices: 20.1 us -> 36.2 us  [exchange(): return lax.all_to_all(x, 'chan', split_axis=0, concat_axis=0, tiled=True)]
    unnamed x42 -> x58, local copies, waits for them, and re-layouts: 6.5 us -> 10.8 us
    pallas_call x8 -> x9, Pallas kernels: 63.2 us -> 65.2 us  [the longest x4 44 us: clean(): pl.pallas_call(functools.partial(clean_kernel, group, len(later)), grid_s...]
  transfers between devices with their start and end apart: 17 -> 21, of which waited for: 13 -> 15; matrix products, arithmetic and copies ran while one was open for 1% -> 1% of each run, Pallas kernels for 17% -> 27%
where the time goes in v3:
time: 401 us; the launch traced here: 399 us
  waiting for transfers between devices  218 us (54%)
  Pallas kernels  113 us (28%)
  starting transfers between devices  52.5 us (13%)
  local copies, waits for them, and re-layouts  14.7 us (4%)
    ppermute x12, waiting for transfers between devices, shards(): lax.ppermute(cleaned[k][step], 'uv', [(z, (z + step) % uv_count) for z in...  154 us
    all_to_all x9, waiting for transfers between devices, exchange(): return lax.all_to_all(x, 'chan', split_axis=0, concat_axis=0, tiled=True)  63.9 us
    pallas_call x4, Pallas kernels, clean(): pl.pallas_call(functools.partial(clean_kernel, group, len(later)), grid_s...  44 us
    all_to_all x9, starting transfers between devices, exchange(): return lax.all_to_all(x, 'chan', split_axis=0, concat_axis=0, tiled=True)  36.2 us
    pallas_call x1, Pallas kernels, column_transform(): pl.pallas_call(column_kernel, grid=(rows // block,), in_specs=[pl.BlockSp...  24.9 us
    pallas_call x4, Pallas kernels, place(): pl.pallas_call(place_kernel, grid=(pieces,), in_specs=[pl.BlockSpec((1, 2...  22.6 us
    pallas_call x4, Pallas kernels, row_transform(): pl.pallas_call(functools.partial(row_kernel, scale, group, steps), grid=(...  19.1 us
    ppermute x12, starting transfers between devices, shards(): lax.ppermute(cleaned[k][step], 'uv', [(z, (z + step) % uv_count) for z in...  16.2 us
  transfers between devices with their start and end apart: 21, of which 15 were waited for; matrix products, arithmetic and copies ran while one was open for 1% of the time, Pallas kernels for 27%

profile of v3, /device:TPU:8, one launch (start us, length us, event | category | flops | bytes accessed | tf_op | source)
XLA Modules:
  0.0 398.9 jit_solution(17865861243638824427)
XLA Ops:
  0.0 1.7 broadcast_in_dim.2
  1.7 3.7 all-to-all-start.1
  5.4 24.9 %column_transform.1 = (bf16[8,2,512,128]{3,2,1,0:T(8,128)(2,1)}, bf16[8,2,512,128]{3,2,1,0:T(8,128)(2,1)}, bf16[8,2,512,128]{3,2,1,0:T(8,128)(2,1)}, bf16[8,2,512,128]{3,2,1,0:T(8,128)(2,1)}) custom-call(bf16[2,512,4096]{2,1,0:T(8,128)(2,1)} %bitcast.18, f32[8,2,512]{2,1,0:T(2,128)} %constant.61.clone.twiddle_ref, bf16[1024,1024]{1,0:T(8,128)(2,1)} %constant.62.clone.table_ref), custom_call_target="tpu_custom_call" | custom-call | flops 17179869184 | bytes 16777216 | tf_op jit(solution)/shard_map/column_transform/pallas_call | solution.py:155
  31.1 4.2 %all-to-all-start = ((bf16[8,2,512,128]{3,2,1,0:T(8,128)(2,1)}), bf16[8,2,512,128]{3,2,1,0:T(8,128)(2,1)S(1)}, u32[]{:S(2)}, u32[]{:S(2)}) async-start(bf16[8,2,512,128]{3,2,1,0:T(8,128)(2,1)} %get-tuple-element.29), calls=%async_computation | async-start | bytes 4194304 | tf_op jit(solution)/shard_map/all_to_all | solution.py:374
  35.3 2.1 turn.1
  37.4 24.6 %all-to-all-done.x_ref = bf16[8,2,512,128]{3,2,1,0:T(8,128)(2,1)S(1)} async-done(((bf16[8,2,512,128]{3,2,1,0:T(8,128)(2,1)}), bf16[8,2,512,128]{3,2,1,0:T(8,128)(2,1)S(1)}, u32[]{:S(2)}, u32[]{:S(2)}) %all-to-all-start) | async-done | bytes 2097184 | tf_op jit(solution)/shard_map/all_to_all | solution.py:374
  63.3 3.6 all-to-all-start.4
  68.5 11.0 %clean.4 = (bf16[8,2,128,128]{3,2,1,0:T(8,128)(2,1)}, bf16[8,2,128,128]{3,2,1,0:T(8,128)(2,1)}, bf16[8,2,128,128]{3,2,1,0:T(8,128)(2,1)}, bf16[8,2,128,128]{3,2,1,0:T(8,128)(2,1)}, bf16[8,2,512,128]{3,2,1,0:T(8,128)(2,1)}) custom-call(s32[1]{0:T(128)} %bitcast.at_ref, bf16[8,2,512,128]{3,2,1,0:T(8,128)(2,1)} %copy-done.5, ...), custom_call_target="tpu_custom_call", output_to_operand_aliasing={{4}: (8, {})} | custom-call | flops 3221225472 | bytes 4194304 | tf_op jit(solution)/shard_map/clean/pallas_call | solution.py:242
  79.5 14.0 %all-to-all-done.4.x_ref = bf16[8,2,512,128]{3,2,1,0:T(8,128)(2,1)S(1)} async-done(((bf16[8,2,512,128]{3,2,1,0:T(8,128)(2,1)}), bf16[8,2,512,128]{3,2,1,0:T(8,128)(2,1)S(1)}, u32[]{:S(2)}, u32[]{:S(2)}) %all-to-all-start.4) | async-done | bytes 2097184 | tf_op jit(solution)/shard_map/all_to_all | solution.py:374
  94.8 3.6 all-to-all-start.2
  98.5 11.0 %clean.6 = (bf16[8,2,128,128]{3,2,1,0:T(8,128)(2,1)}, bf16[8,2,128,128]{3,2,1,0:T(8,128)(2,1)}, bf16[8,2,128,128]{3,2,1,0:T(8,128)(2,1)}, bf16[8,2,128,128]{3,2,1,0:T(8,128)(2,1)}, bf16[8,2,512,128]{3,2,1,0:T(8,128)(2,1)}) custom-call(s32[1]{0:T(128)} %bitcast.at_ref, bf16[8,2,512,128]{3,2,1,0:T(8,128)(2,1)} %copy-done.4, ...), custom_call_target="tpu_custom_call", output_to_operand_aliasing={{4}: (8, {})} | custom-call | flops 3221225472 | bytes 4194304 | tf_op jit(solution)/shard_map/clean/pallas_call | solution.py:242
  109.4 15.6 %all-to-all-done.2.x_ref.refs_6_ = bf16[8,2,512,128]{3,2,1,0:T(8,128)(2,1)S(1)} async-done(((bf16[8,2,512,128]{3,2,1,0:T(8,128)(2,1)}), bf16[8,2,512,128]{3,2,1,0:T(8,128)(2,1)S(1)}, u32[]{:S(2)}, u32[]{:S(2)}) %all-to-all-start.2) | async-done | bytes 2097184 | tf_op jit(solution)/shard_map/all_to_all | solution.py:374
  126.3 4.4 %all-to-all-start.5 = ((bf16[8,2,512,128]{3,2,1,0:T(8,128)(2,1)}), bf16[8,2,512,128]{3,2,1,0:T(8,128)(2,1)}, u32[]{:S(2)}, u32[]{:S(2)}) async-start(bf16[8,2,512,128]{3,2,1,0:T(8,128)(2,1)} %get-tuple-element.40), calls=%async_computation.5 | async-start | bytes 4194304 | tf_op jit(solution)/shard_map/all_to_all | solution.py:374
  130.7 1.6 collective-permute-start.6
  133.6 1.8 collective-permute-start.8
  135.4 1.6 dynamic-slice_bitcast_fusion.refs_4_
  137.0 10.9 %clean.5 = (bf16[8,2,128,128]{3,2,1,0:T(8,128)(2,1)}, bf16[8,2,128,128]{3,2,1,0:T(8,128)(2,1)}, bf16[8,2,128,128]{3,2,1,0:T(8,128)(2,1)}, bf16[8,2,128,128]{3,2,1,0:T(8,128)(2,1)}) custom-call(s32[1]{0:T(128)} %bitcast.at_ref, bf16[8,2,512,128]{3,2,1,0:T(8,128)(2,1)} %copy-done.2, bf16[512,512]{1,0:T(8,128)(2,1)} %bitcast.16, ...), custom_call_target="tpu_custom_call" | custom-call | flops 3221225472 | bytes 4194304 | tf_op jit(solution)/shard_map/clean/pallas_call | solution.py:242
  147.9 19.4 %collective-permute-done.6.refs_1_ = bf16[8,2,128,128]{3,2,1,0:T(8,128)(2,1)S(1)} collective-permute-done((bf16[8,2,128,128]{3,2,1,0:T(8,128)(2,1)}, bf16[8,2,128,128]{3,2,1,0:T(8,128)(2,1)S(1)}, u32[]{:S(2)}, u32[]{:S(2)}) %collective-permute-start.6) | collective-permute-done | bytes 524320 | tf_op jit(solution)/shard_map/ppermute | solution.py:404
  167.3 10.7 %collective-permute-done.7.refs_2_ = bf16[8,2,128,128]{3,2,1,0:T(8,128)(2,1)S(1)} collective-permute-done((bf16[8,2,128,128]{3,2,1,0:T(8,128)(2,1)S(1)}, bf16[8,2,128,128]{3,2,1,0:T(8,128)(2,1)S(1)}, u32[]{:S(2)}, u32[]{:S(2)}) %collective-permute-start.7) | collective-permute-done | bytes 524320 | tf_op jit(solution)/shard_map/ppermute | solution.py:404
  177.9 1.8 collective-permute-done.8.refs_3_
  180.5 4.8 %row_transform.6 = bf16[8,2,16,32,128]{4,3,2,1,0:T(8,128)(2,1)} custom-call(bf16[8,2,128,128]{3,2,1,0:T(8,128)(2,1)} %get-tuple-element.45.refs_0_, bf16[8,2,128,128]{3,2,1,0:T(8,128)(2,1)} %copy-done.6, bf16[8,2,128,128]{3,2,1,0:T(8,128)(2,1)} %copy-done.7, bf16[8,2,128,128]{3,2,1,0:T(8,128)(2,1)} %copy-done.8, ...), custom_call_target="tpu_custom_call" | custom-call | flops 536870912 | bytes 4194304 | tf_op jit(solution)/shard_map/row_transform/pallas_call | solution.py:313
  185.3 4.0 %all-to-all-start.7 = ((bf16[8,2,16,32,128]{4,3,2,1,0:T(8,128)(2,1)}), bf16[8,2,16,32,128]{4,3,2,1,0:T(8,128)(2,1)S(1)}, u32[]{:S(2)}, u32[]{:S(2)}) async-start(bf16[8,2,16,32,128]{4,3,2,1,0:T(8,128)(2,1)} %row_transform.6), calls=%async_computation.7 | async-start | bytes 4194304 | tf_op jit(solution)/shard_map/all_to_all | solution.py:374
  189.3 1.8 collective-permute-start.10
  191.2 1.9 collective-permute-start.11
  193.1 11.1 %clean.7 = (bf16[8,2,128,128]{3,2,1,0:T(8,128)(2,1)}, bf16[8,2,128,128]{3,2,1,0:T(8,128)(2,1)}, bf16[8,2,128,128]{3,2,1,0:T(8,128)(2,1)}, bf16[8,2,128,128]{3,2,1,0:T(8,128)(2,1)}) custom-call(s32[1]{0:T(128)} %bitcast.at_ref, bf16[8,2,512,128]{3,2,1,0:T(8,128)(2,1)} %all-to-all-done.5.x_ref, bf16[512,512]{1,0:T(8,128)(2,1)} %bitcast.17, ...), custom_call_target="tpu_custom_call" | custom-call | flops 3221225472 | bytes 4194304 | tf_op jit(solution)/shard_map/clean/pallas_call | solution.py:242
  204.3 31.1 %collective-permute-done.10.refs_2_ = bf16[8,2,128,128]{3,2,1,0:T(8,128)(2,1)S(1)} collective-permute-done((bf16[8,2,128,128]{3,2,1,0:T(8,128)(2,1)S(1)}, bf16[8,2,128,128]{3,2,1,0:T(8,128)(2,1)S(1)}, u32[]{:S(2)}, u32[]{:S(2)}) %collective-permute-start.10) | collective-permute-done | bytes 524320 | tf_op jit(solution)/shard_map/ppermute | solution.py:404
  235.4 2.3 collective-permute-done.11.refs_3_
  238.5 4.8 %row_transform.7 = bf16[8,2,16,32,128]{4,3,2,1,0:T(8,128)(2,1)} custom-call(bf16[8,2,128,128]{3,2,1,0:T(8,128)(2,1)} %get-tuple-element.49.refs_0_, bf16[8,2,128,128]{3,2,1,0:T(8,128)(2,1)} %copy-done.15, bf16[8,2,128,128]{3,2,1,0:T(8,128)(2,1)} %copy-done.16, bf16[8,2,128,128]{3,2,1,0:T(8,128)(2,1)} %copy-done.17, ...), custom_call_target="tpu_custom_call" | custom-call | flops 536870912 | bytes 4194304 | tf_op jit(solution)/shard_map/row_transform/pallas_call | solution.py:313
  244.6 4.3 %all-to-all-start.8 = ((bf16[8,2,16,32,128]{4,3,2,1,0:T(8,128)(2,1)}), bf16[8,2,16,32,128]{4,3,2,1,0:T(8,128)(2,1)}, u32[]{:S(2)}, u32[]{:S(2)}) async-start(bf16[8,2,16,32,128]{4,3,2,1,0:T(8,128)(2,1)} %row_transform.7), calls=%async_computation.8 | async-start | bytes 4194304 | tf_op jit(solution)/shard_map/all_to_all | solution.py:374
  249.1 1.4 collective-permute-start.4
  250.5 1.9 collective-permute-start.5
  252.4 11.6 %collective-permute-done.3.refs_1_ = bf16[8,2,128,128]{3,2,1,0:T(8,128)(2,1)S(1)} collective-permute-done((bf16[8,2,128,128]{3,2,1,0:T(8,128)(2,1)}, bf16[8,2,128,128]{3,2,1,0:T(8,128)(2,1)S(1)}, u32[]{:S(2)}, u32[]{:S(2)}) %collective-permute-start.3) | collective-permute-done | bytes 524320 | tf_op jit(solution)/shard_map/ppermute | solution.py:404
  264.0 30.9 %collective-permute-done.4.refs_2_ = bf16[8,2,128,128]{3,2,1,0:T(8,128)(2,1)S(1)} collective-permute-done((bf16[8,2,128,128]{3,2,1,0:T(8,128)(2,1)S(1)}, bf16[8,2,128,128]{3,2,1,0:T(8,128)(2,1)S(1)}, u32[]{:S(2)}, u32[]{:S(2)}) %collective-permute-start.4) | collective-permute-done | bytes 524320 | tf_op jit(solution)/shard_map/ppermute | solution.py:404
  294.9 1.9 collective-permute-done.5.refs_3_
  297.6 4.8 %row_transform.5 = bf16[8,2,16,32,128]{4,3,2,1,0:T(8,128)(2,1)} custom-call(bf16[8,2,128,128]{3,2,1,0:T(8,128)(2,1)} %get-tuple-element.41.refs_0_.refs_5_, bf16[8,2,128,128]{3,2,1,0:T(8,128)(2,1)} %copy-done.10, bf16[8,2,128,128]{3,2,1,0:T(8,128)(2,1)} %copy-done.12, bf16[8,2,128,128]{3,2,1,0:T(8,128)(2,1)} %copy-done.14, ...), custom_call_target="tpu_custom_call" | custom-call | flops 536870912 | bytes 4194304 | tf_op jit(solution)/shard_map/row_transform/pallas_call | solution.py:313
  302.3 4.0 %all-to-all-start.6 = ((bf16[8,2,16,32,128]{4,3,2,1,0:T(8,128)(2,1)}), bf16[8,2,16,32,128]{4,3,2,1,0:T(8,128)(2,1)S(1)}, u32[]{:S(2)}, u32[]{:S(2)}) async-start(bf16[8,2,16,32,128]{4,3,2,1,0:T(8,128)(2,1)} %row_transform.5), calls=%async_computation.6 | async-start | bytes 4194304 | tf_op jit(solution)/shard_map/all_to_all | solution.py:374
  306.4 2.4 collective-permute-start.1
  308.8 1.9 collective-permute-start.2
  310.8 10.5 %collective-permute-done.refs_1_ = bf16[8,2,128,128]{3,2,1,0:T(8,128)(2,1)S(1)} collective-permute-done((bf16[8,2,128,128]{3,2,1,0:T(8,128)(2,1)}, bf16[8,2,128,128]{3,2,1,0:T(8,128)(2,1)S(1)}, u32[]{:S(2)}, u32[]{:S(2)}) %collective-permute-start) | collective-permute-done | bytes 524320 | tf_op jit(solution)/shard_map/ppermute | solution.py:404
  321.3 31.1 %collective-permute-done.1.refs_2_ = bf16[8,2,128,128]{3,2,1,0:T(8,128)(2,1)S(1)} collective-permute-done((bf16[8,2,128,128]{3,2,1,0:T(8,128)(2,1)S(1)}, bf16[8,2,128,128]{3,2,1,0:T(8,128)(2,1)S(1)}, u32[]{:S(2)}, u32[]{:S(2)}) %collective-permute-start.1) | collective-permute-done | bytes 524320 | tf_op jit(solution)/shard_map/ppermute | solution.py:404
  352.4 2.9 collective-permute-done.2.refs_3_
  356.1 4.8 %row_transform.4 = bf16[8,2,16,32,128]{4,3,2,1,0:T(8,128)(2,1)} custom-call(bf16[8,2,128,128]{3,2,1,0:T(8,128)(2,1)} %get-tuple-element.34.refs_0_.refs_5_, bf16[8,2,128,128]{3,2,1,0:T(8,128)(2,1)} %copy-done.9, bf16[8,2,128,128]{3,2,1,0:T(8,128)(2,1)} %copy-done.11, bf16[8,2,128,128]{3,2,1,0:T(8,128)(2,1)} %copy-done.13, ...), custom_call_target="tpu_custom_call" | custom-call | flops 536870912 | bytes 4194304 | tf_op jit(solution)/shard_map/row_transform/pallas_call | solution.py:313
  362.2 4.3 %all-to-all-start.3 = ((bf16[8,2,16,32,128]{4,3,2,1,0:T(8,128)(2,1)}), bf16[8,2,16,32,128]{4,3,2,1,0:T(8,128)(2,1)}, u32[]{:S(2)}, u32[]{:S(2)}) async-start(bf16[8,2,16,32,128]{4,3,2,1,0:T(8,128)(2,1)} %row_transform.4), calls=%async_computation.3 | async-start | bytes 4194304 | tf_op jit(solution)/shard_map/all_to_all | solution.py:374
  366.6 5.6 %place.4.refs_0_ = bf16[2,16,32,4096]{3,2,1,0:T(8,128)(2,1)} custom-call(bf16[8,2,16,32,128]{4,3,2,1,0:T(8,128)(2,1)} %all-to-all-done.8.x_ref), custom_call_target="tpu_custom_call" | custom-call | bytes 4194304 | tf_op jit(solution)/shard_map/place/pallas_call | solution.py:338
  372.2 5.6 %place.5.refs_0_ = bf16[2,16,32,4096]{3,2,1,0:T(8,128)(2,1)} custom-call(bf16[8,2,16,32,128]{4,3,2,1,0:T(8,128)(2,1)} %copy-done, bf16[2,16,32,4096]{3,2,1,0:T(8,128)(2,1)} %place.4.refs_0_), custom_call_target="tpu_custom_call", output_to_operand_aliasing={{}: (1, {})} | custom-call | bytes 4194304 | tf_op jit(solution)/shard_map/place/pallas_call | solution.py:338
  377.9 5.6 %place.6.refs_0_ = bf16[2,16,32,4096]{3,2,1,0:T(8,128)(2,1)} custom-call(bf16[8,2,16,32,128]{4,3,2,1,0:T(8,128)(2,1)} %copy-done.1, bf16[2,16,32,4096]{3,2,1,0:T(8,128)(2,1)} %place.5.refs_0_), custom_call_target="tpu_custom_call", output_to_operand_aliasing={{}: (1, {})} | custom-call | bytes 4194304 | tf_op jit(solution)/shard_map/place/pallas_call | solution.py:338
  383.5 9.7 %all-to-all-done.3.x_ref = bf16[8,2,16,32,128]{4,3,2,1,0:T(8,128)(2,1)} async-done(((bf16[8,2,16,32,128]{4,3,2,1,0:T(8,128)(2,1)}), bf16[8,2,16,32,128]{4,3,2,1,0:T(8,128)(2,1)}, u32[]{:S(2)}, u32[]{:S(2)}) %all-to-all-start.3) | async-done | bytes 2097184 | tf_op jit(solution)/shard_map/all_to_all | solution.py:374
  393.2 5.6 %place.7 = bf16[2,16,32,4096]{3,2,1,0:T(8,128)(2,1)} custom-call(bf16[8,2,16,32,128]{4,3,2,1,0:T(8,128)(2,1)} %all-to-all-done.3.x_ref, bf16[2,16,32,4096]{3,2,1,0:T(8,128)(2,1)} %place.6.refs_0_), custom_call_target="tpu_custom_call", output_to_operand_aliasing={{}: (1, {})} | custom-call | bytes 4194304 | tf_op jit(solution)/shard_map/place/pallas_call | solution.py:338
  (70 shorter events, 13.7 us)
Async XLA Ops:
  1.7 28.6 %all-to-all-start.1 = ((bf16[8,64,512]{2,1,0:T(8,128)(2,1)}), bf16[8,64,512]{2,1,0:T(8,128)(2,1)S(1)}, u32[]{:S(2)}, u32[]{:S(2)}) async-start(bf16[8,64,512]{2,1,0:T(8,128)(2,1)} %broadcast_in_dim.2), calls=%async_computation.1 | async-start | bytes 1048576 | tf_op jit(solution)/shard_map/all_to_all | solution.py:374
  30.3 0.8 copy-start.3
  31.1 30.8 %all-to-all-start = ((bf16[8,2,512,128]{3,2,1,0:T(8,128)(2,1)}), bf16[8,2,512,128]{3,2,1,0:T(8,128)(2,1)S(1)}, u32[]{:S(2)}, u32[]{:S(2)}) async-start(bf16[8,2,512,128]{3,2,1,0:T(8,128)(2,1)} %get-tuple-element.29), calls=%async_computation | async-start | bytes 4194304 | tf_op jit(solution)/shard_map/all_to_all | solution.py:374
  62.0 1.4 copy-start.5
  62.0 5.0 %copy-start.18 = (bf16[8,128,128]{2,1,0:T(8,128)(2,1)S(1)}, bf16[8,128,128]{2,1,0:T(8,128)(2,1)}, u32[]{:S(2)}) copy-start(bf16[8,128,128]{2,1,0:T(8,128)(2,1)} %constant.60.clone) | copy-start | bytes 786436
  62.0 5.7 %copy-start.19 = (f32[512]{0:T(512)S(1)}, f32[512]{0:T(512)}, u32[]{:S(2)}) copy-start(f32[512]{0:T(512)} %param.21) | copy-start | bytes 6148
  62.0 5.7 %copy-start.20 = (f32[8]{0:T(128)S(1)}, f32[8]{0:T(128)}, u32[]{:S(2)}) copy-start(f32[8]{0:T(128)} %param.22) | copy-start | bytes 100
  63.3 30.2 %all-to-all-start.4 = ((bf16[8,2,512,128]{3,2,1,0:T(8,128)(2,1)}), bf16[8,2,512,128]{3,2,1,0:T(8,128)(2,1)S(1)}, u32[]{:S(2)}, u32[]{:S(2)}) async-start(bf16[8,2,512,128]{3,2,1,0:T(8,128)(2,1)} %get-tuple-element.38), calls=%async_computation.4 | async-start | bytes 4194304 | tf_op jit(solution)/shard_map/all_to_all | solution.py:374
  93.5 1.3 copy-start.4
  94.8 30.2 %all-to-all-start.2 = ((bf16[8,2,512,128]{3,2,1,0:T(8,128)(2,1)}), bf16[8,2,512,128]{3,2,1,0:T(8,128)(2,1)S(1)}, u32[]{:S(2)}, u32[]{:S(2)}) async-start(bf16[8,2,512,128]{3,2,1,0:T(8,128)(2,1)} %get-tuple-element.33), calls=%async_computation.2 | async-start | bytes 4194304 | tf_op jit(solution)/shard_map/all_to_all | solution.py:374
  125.0 1.3 copy-start.2
  125.0 7.3 %copy-start.26 = (bf16[8,2,128,128]{3,2,1,0:T(8,128)(2,1)S(1)}, bf16[8,2,128,128]{3,2,1,0:T(8,128)(2,1)}, u32[]{:S(2)}) copy-start(bf16[8,2,128,128]{3,2,1,0:T(8,128)(2,1)} %get-tuple-element.47) | copy-start | bytes 1572868
  125.0 8.6 %copy-start.25 = (bf16[8,2,128,128]{3,2,1,0:T(8,128)(2,1)S(1)}, bf16[8,2,128,128]{3,2,1,0:T(8,128)(2,1)}, u32[]{:S(2)}) copy-start(bf16[8,2,128,128]{3,2,1,0:T(8,128)(2,1)} %get-tuple-element.48) | copy-start | bytes 1572868
  126.3 58.9 %all-to-all-start.5 = ((bf16[8,2,512,128]{3,2,1,0:T(8,128)(2,1)}), bf16[8,2,512,128]{3,2,1,0:T(8,128)(2,1)}, u32[]{:S(2)}, u32[]{:S(2)}) async-start(bf16[8,2,512,128]{3,2,1,0:T(8,128)(2,1)} %get-tuple-element.40), calls=%async_computation.5 | async-start | bytes 4194304 | tf_op jit(solution)/shard_map/all_to_all | solution.py:374
  130.7 36.5 %collective-permute-start.6 = (bf16[8,2,128,128]{3,2,1,0:T(8,128)(2,1)}, bf16[8,2,128,128]{3,2,1,0:T(8,128)(2,1)S(1)}, u32[]{:S(2)}, u32[]{:S(2)}) collective-permute-start(bf16[8,2,128,128]{3,2,1,0:T(8,128)(2,1)} %get-tuple-element.46), channel_id=1, source_target_pairs={{0,8},{8,16},{16,24},{24,0},{1,9},{9,17},{17,25},{25,1},{2,10},{10... | collective-permute-start | bytes 1572872 | tf_op jit(solution)/shard_map/ppermute | solution.py:404
  132.3 45.6 %collective-permute-start.7 = (bf16[8,2,128,128]{3,2,1,0:T(8,128)(2,1)S(1)}, bf16[8,2,128,128]{3,2,1,0:T(8,128)(2,1)S(1)}, u32[]{:S(2)}, u32[]{:S(2)}) collective-permute-start(bf16[8,2,128,128]{3,2,1,0:T(8,128)(2,1)S(1)} %copy-done.26), channel_id=1, source_target_pairs={{0,16},{8,24},{16,0},{24,8},{1,17},{9,25},{17,1},{25,9},{2,18},{10... | collective-permute-start | bytes 1572872 | tf_op jit(solution)/shard_map/ppermute | solution.py:404
  133.6 46.1 %collective-permute-start.8 = (bf16[8,2,128,128]{3,2,1,0:T(8,128)(2,1)S(1)}, bf16[8,2,128,128]{3,2,1,0:T(8,128)(2,1)S(1)}, u32[]{:S(2)}, u32[]{:S(2)}) collective-permute-start(bf16[8,2,128,128]{3,2,1,0:T(8,128)(2,1)S(1)} %copy-done.25), channel_id=1, source_target_pairs={{0,24},{8,0},{16,8},{24,16},{1,25},{9,1},{17,9},{25,17},{2,26},{10... | collective-permute-start | bytes 1572872 | tf_op jit(solution)/shard_map/ppermute | solution.py:404
  167.3 12.5 %copy-start.6 = (bf16[8,2,128,128]{3,2,1,0:T(8,128)(2,1)}, bf16[8,2,128,128]{3,2,1,0:T(8,128)(2,1)S(1)}, u32[]{:S(2)}) copy-start(bf16[8,2,128,128]{3,2,1,0:T(8,128)(2,1)S(1)} %collective-permute-done.6.refs_1_) | copy-start | bytes 1572868
  177.9 1.8 copy-start.7
  185.3 4.1 %copy-start.24 = (bf16[8,2,128,128]{3,2,1,0:T(8,128)(2,1)S(1)}, bf16[8,2,128,128]{3,2,1,0:T(8,128)(2,1)}, u32[]{:S(2)}) copy-start(bf16[8,2,128,128]{3,2,1,0:T(8,128)(2,1)} %get-tuple-element.51) | copy-start | bytes 1572868
  185.3 5.9 %copy-start.23 = (bf16[8,2,128,128]{3,2,1,0:T(8,128)(2,1)S(1)}, bf16[8,2,128,128]{3,2,1,0:T(8,128)(2,1)}, u32[]{:S(2)}) copy-start(bf16[8,2,128,128]{3,2,1,0:T(8,128)(2,1)} %get-tuple-element.52) | copy-start | bytes 1572868
  185.3 58.0 %all-to-all-start.7 = ((bf16[8,2,16,32,128]{4,3,2,1,0:T(8,128)(2,1)}), bf16[8,2,16,32,128]{4,3,2,1,0:T(8,128)(2,1)S(1)}, u32[]{:S(2)}, u32[]{:S(2)}) async-start(bf16[8,2,16,32,128]{4,3,2,1,0:T(8,128)(2,1)} %row_transform.6), calls=%async_computation.7 | async-start | bytes 4194304 | tf_op jit(solution)/shard_map/all_to_all | solution.py:374
  189.3 14.9 %collective-permute-start.9 = (bf16[8,2,128,128]{3,2,1,0:T(8,128)(2,1)}, bf16[8,2,128,128]{3,2,1,0:T(8,128)(2,1)S(1)}, u32[]{:S(2)}, u32[]{:S(2)}) collective-permute-start(bf16[8,2,128,128]{3,2,1,0:T(8,128)(2,1)} %get-tuple-element.50), channel_id=1, source_target_pairs={{0,8},{8,16},{16,24},{24,0},{1,9},{9,17},{17,25},{25,1},{2,10},{10... | collective-permute-start | bytes 1572872 | tf_op jit(solution)/shard_map/ppermute | solution.py:404
  189.3 46.0 %collective-permute-start.10 = (bf16[8,2,128,128]{3,2,1,0:T(8,128)(2,1)S(1)}, bf16[8,2,128,128]{3,2,1,0:T(8,128)(2,1)S(1)}, u32[]{:S(2)}, u32[]{:S(2)}) collective-permute-start(bf16[8,2,128,128]{3,2,1,0:T(8,128)(2,1)S(1)} %copy-done.24), channel_id=1, source_target_pairs={{0,16},{8,24},{16,0},{24,8},{1,17},{9,25},{17,1},{25,9},{2,18},{10... | collective-permute-start | bytes 1572872 | tf_op jit(solution)/shard_map/ppermute | solution.py:404
  191.2 46.5 %collective-permute-start.11 = (bf16[8,2,128,128]{3,2,1,0:T(8,128)(2,1)S(1)}, bf16[8,2,128,128]{3,2,1,0:T(8,128)(2,1)S(1)}, u32[]{:S(2)}, u32[]{:S(2)}) collective-permute-start(bf16[8,2,128,128]{3,2,1,0:T(8,128)(2,1)S(1)} %copy-done.23), channel_id=1, source_target_pairs={{0,24},{8,0},{16,8},{24,16},{1,25},{9,1},{17,9},{25,17},{2,26},{10... | collective-permute-start | bytes 1572872 | tf_op jit(solution)/shard_map/ppermute | solution.py:404
  204.2 33.4 %copy-start.15 = (bf16[8,2,128,128]{3,2,1,0:T(8,128)(2,1)}, bf16[8,2,128,128]{3,2,1,0:T(8,128)(2,1)S(1)}, u32[]{:S(2)}) copy-start(bf16[8,2,128,128]{3,2,1,0:T(8,128)(2,1)S(1)} %collective-permute-done.9.refs_1_) | copy-start | bytes 1572868
  235.4 2.3 copy-start.16
  237.6 0.9 copy-start.17
  243.3 5.8 %copy-start.28 = (bf16[8,2,128,128]{3,2,1,0:T(8,128)(2,1)S(1)}, bf16[8,2,128,128]{3,2,1,0:T(8,128)(2,1)}, u32[]{:S(2)}) copy-start(bf16[8,2,128,128]{3,2,1,0:T(8,128)(2,1)} %get-tuple-element.43) | copy-start | bytes 1572868
  243.3 7.2 %copy-start.27 = (bf16[8,2,128,128]{3,2,1,0:T(8,128)(2,1)S(1)}, bf16[8,2,128,128]{3,2,1,0:T(8,128)(2,1)}, u32[]{:S(2)}) copy-start(bf16[8,2,128,128]{3,2,1,0:T(8,128)(2,1)} %get-tuple-element.44) | copy-start | bytes 1572868
  243.3 1.3 copy-start
  244.6 57.7 %all-to-all-start.8 = ((bf16[8,2,16,32,128]{4,3,2,1,0:T(8,128)(2,1)}), bf16[8,2,16,32,128]{4,3,2,1,0:T(8,128)(2,1)}, u32[]{:S(2)}, u32[]{:S(2)}) async-start(bf16[8,2,16,32,128]{4,3,2,1,0:T(8,128)(2,1)} %row_transform.7), calls=%async_computation.8 | async-start | bytes 4194304 | tf_op jit(solution)/shard_map/all_to_all | solution.py:374
  249.0 15.0 %collective-permute-start.3 = (bf16[8,2,128,128]{3,2,1,0:T(8,128)(2,1)}, bf16[8,2,128,128]{3,2,1,0:T(8,128)(2,1)S(1)}, u32[]{:S(2)}, u32[]{:S(2)}) collective-permute-start(bf16[8,2,128,128]{3,2,1,0:T(8,128)(2,1)} %get-tuple-element.42), channel_id=1, source_target_pairs={{0,8},{8,16},{16,24},{24,0},{1,9},{9,17},{17,25},{25,1},{2,10},{10... | collective-permute-start | bytes 1572872 | tf_op jit(solution)/shard_map/ppermute | solution.py:404
  249.1 45.8 %collective-permute-start.4 = (bf16[8,2,128,128]{3,2,1,0:T(8,128)(2,1)S(1)}, bf16[8,2,128,128]{3,2,1,0:T(8,128)(2,1)S(1)}, u32[]{:S(2)}, u32[]{:S(2)}) collective-permute-start(bf16[8,2,128,128]{3,2,1,0:T(8,128)(2,1)S(1)} %copy-done.28), channel_id=1, source_target_pairs={{0,16},{8,24},{16,0},{24,8},{1,17},{9,25},{17,1},{25,9},{2,18},{10... | collective-permute-start | bytes 1572872 | tf_op jit(solution)/shard_map/ppermute | solution.py:404
  250.5 46.3 %collective-permute-start.5 = (bf16[8,2,128,128]{3,2,1,0:T(8,128)(2,1)S(1)}, bf16[8,2,128,128]{3,2,1,0:T(8,128)(2,1)S(1)}, u32[]{:S(2)}, u32[]{:S(2)}) collective-permute-start(bf16[8,2,128,128]{3,2,1,0:T(8,128)(2,1)S(1)} %copy-done.27), channel_id=1, source_target_pairs={{0,24},{8,0},{16,8},{24,16},{1,25},{9,1},{17,9},{25,17},{2,26},{10... | collective-permute-start | bytes 1572872 | tf_op jit(solution)/shard_map/ppermute | solution.py:404
  264.0 32.8 %copy-start.10 = (bf16[8,2,128,128]{3,2,1,0:T(8,128)(2,1)}, bf16[8,2,128,128]{3,2,1,0:T(8,128)(2,1)S(1)}, u32[]{:S(2)}) copy-start(bf16[8,2,128,128]{3,2,1,0:T(8,128)(2,1)S(1)} %collective-permute-done.3.refs_1_) | copy-start | bytes 1572868
  294.9 1.9 copy-start.12
  302.3 4.0 %copy-start.22 = (bf16[8,2,128,128]{3,2,1,0:T(8,128)(2,1)S(1)}, bf16[8,2,128,128]{3,2,1,0:T(8,128)(2,1)}, u32[]{:S(2)}) copy-start(bf16[8,2,128,128]{3,2,1,0:T(8,128)(2,1)} %get-tuple-element.36) | copy-start | bytes 1572868
  302.3 6.5 %copy-start.21 = (bf16[8,2,128,128]{3,2,1,0:T(8,128)(2,1)S(1)}, bf16[8,2,128,128]{3,2,1,0:T(8,128)(2,1)}, u32[]{:S(2)}) copy-start(bf16[8,2,128,128]{3,2,1,0:T(8,128)(2,1)} %get-tuple-element.37) | copy-start | bytes 1572868
  302.3 58.6 %all-to-all-start.6 = ((bf16[8,2,16,32,128]{4,3,2,1,0:T(8,128)(2,1)}), bf16[8,2,16,32,128]{4,3,2,1,0:T(8,128)(2,1)S(1)}, u32[]{:S(2)}, u32[]{:S(2)}) async-start(bf16[8,2,16,32,128]{4,3,2,1,0:T(8,128)(2,1)} %row_transform.5), calls=%async_computation.6 | async-start | bytes 4194304 | tf_op jit(solution)/shard_map/all_to_all | solution.py:374
  306.4 14.9 %collective-permute-start = (bf16[8,2,128,128]{3,2,1,0:T(8,128)(2,1)}, bf16[8,2,128,128]{3,2,1,0:T(8,128)(2,1)S(1)}, u32[]{:S(2)}, u32[]{:S(2)}) collective-permute-start(bf16[8,2,128,128]{3,2,1,0:T(8,128)(2,1)} %get-tuple-element.35), channel_id=1, source_target_pairs={{0,8},{8,16},{16,24},{24,0},{1,9},{9,17},{17,25},{25,1},{2,10},{10... | collective-permute-start | bytes 1572872 | tf_op jit(solution)/shard_map/ppermute | solution.py:404
  306.4 46.0 %collective-permute-start.1 = (bf16[8,2,128,128]{3,2,1,0:T(8,128)(2,1)S(1)}, bf16[8,2,128,128]{3,2,1,0:T(8,128)(2,1)S(1)}, u32[]{:S(2)}, u32[]{:S(2)}) collective-permute-start(bf16[8,2,128,128]{3,2,1,0:T(8,128)(2,1)S(1)} %copy-done.22), channel_id=1, source_target_pairs={{0,16},{8,24},{16,0},{24,8},{1,17},{9,25},{17,1},{25,9},{2,18},{10... | collective-permute-start | bytes 1572872 | tf_op jit(solution)/shard_map/ppermute | solution.py:404
  308.8 46.5 %collective-permute-start.2 = (bf16[8,2,128,128]{3,2,1,0:T(8,128)(2,1)S(1)}, bf16[8,2,128,128]{3,2,1,0:T(8,128)(2,1)S(1)}, u32[]{:S(2)}, u32[]{:S(2)}) collective-permute-start(bf16[8,2,128,128]{3,2,1,0:T(8,128)(2,1)S(1)} %copy-done.21), channel_id=1, source_target_pairs={{0,24},{8,0},{16,8},{24,16},{1,25},{9,1},{17,9},{25,17},{2,26},{10... | collective-permute-start | bytes 1572872 | tf_op jit(solution)/shard_map/ppermute | solution.py:404
  321.3 34.0 %copy-start.9 = (bf16[8,2,128,128]{3,2,1,0:T(8,128)(2,1)}, bf16[8,2,128,128]{3,2,1,0:T(8,128)(2,1)S(1)}, u32[]{:S(2)}) copy-start(bf16[8,2,128,128]{3,2,1,0:T(8,128)(2,1)S(1)} %collective-permute-done.refs_1_) | copy-start | bytes 1572868
  352.4 2.9 copy-start.11
  355.3 0.8 copy-start.13
  360.9 1.3 copy-start.1
  362.2 31.0 %all-to-all-start.3 = ((bf16[8,2,16,32,128]{4,3,2,1,0:T(8,128)(2,1)}), bf16[8,2,16,32,128]{4,3,2,1,0:T(8,128)(2,1)}, u32[]{:S(2)}, u32[]{:S(2)}) async-start(bf16[8,2,16,32,128]{4,3,2,1,0:T(8,128)(2,1)} %row_transform.4), calls=%async_computation.3 | async-start | bytes 4194304 | tf_op jit(solution)/shard_map/all_to_all | solution.py:374
  (2 other events, 1.6 us)

commit v4 on v3

--- a/solution.py
+++ b/solution.py
@@ -11,6 +11,7 @@
 
 LANES = 128
 RADIX = 8
+PARTS = 2
 VMEM_BYTES = 56 * 1024 * 1024
 
 
@@ -31,15 +32,12 @@
     return np.stack([np.cos(phase), np.sin(phase)], axis=1).astype(np.float32)
 
 
-def lane_tables(length):
-    span = LANES // RADIX
-    table = np.zeros((RADIX, LANES, LANES), np.float32)
-    for t in range(RADIX):
-        for group in range(RADIX):
-            y_lo = (group - t) % RADIX
-            for h in range(span):
-                table[t, group * span + h, h * RADIX + y_lo] = 1.0
-    return table.astype(jnp.bfloat16)
+def order_table():
+    table = np.zeros((RADIX, LANES, LANES, RADIX), np.float32)
+    for y_lo in range(RADIX):
+        for y_hi in range(LANES):
+            table[y_lo, y_hi, y_hi, y_lo] = 1.0
+    return table.reshape(RADIX * LANES, RADIX * LANES).astype(jnp.bfloat16)
 
 
 def swap_table(major, minor):
@@ -89,15 +87,13 @@
     return out_r, out_i
 
 
-def column_kernel(x_ref, twiddle_ref, table_ref, *refs):
-    *out_refs, mid, wide = refs
+def column_kernel(held, x_ref, twiddle_ref, table_ref, *refs):
+    *out_refs, mid = refs[held:]
     rows, length = x_ref.shape[1:]
     inner = length // RADIX
-    per_piece = len(out_refs)
     step = 16
-
-    def first(i, carry):
-        at = pl.ds(pl.multiple_of(i * step, step), step)
+    for i in range(rows // step):
+        at = slice(i * step, (i + 1) * step)
         for block in range(inner // LANES):
             re, im = [], []
             for a in range(RADIX):
@@ -117,85 +113,78 @@
                     ti = re[y_lo] * sine + im[y_lo] * cosine
                 mid[y_lo, at, lanes] = tr.astype(jnp.bfloat16)
                 mid[y_lo, at, other] = ti.astype(jnp.bfloat16)
-        return carry
-
-    lax.fori_loop(0, rows // step, first, 0)
-    wide[...] = jnp.dot(
-        mid[...].reshape(RADIX * rows, 2 * inner), table_ref[...], preferred_element_type=jnp.float32
-    ).reshape(wide.shape)
-
-    span = LANES // RADIX
-    group_of = lax.broadcasted_iota(jnp.int32, (step, LANES), 1) // span
-
-    def last(i, carry):
-        at = pl.ds(pl.multiple_of(i * step, step), step)
-        for part in range(2):
-            for block in range(inner // LANES):
-                lanes = slice(part * inner + block * LANES, part * inner + (block + 1) * LANES)
-                tiles = []
+    groups = out_refs[0].shape[0] // RADIX
+    for part in range(2):
+        for block in range(0, inner // LANES, 2):
+            start = part * inner + block * LANES
+            pair = min(2, inner // LANES - block)
+            wide = jnp.dot(
+                mid[...].reshape(RADIX * rows, 2 * inner),
+                table_ref[:, start : start + pair * LANES],
+                preferred_element_type=jnp.float32,
+            ).astype(jnp.bfloat16)
+            for k in range(pair):
+                chunk, group = divmod(block + k, groups)
                 for y_lo in range(RADIX):
-                    tile = wide[y_lo, at, lanes]
-                    tiles.append(pltpu.roll(tile, y_lo * span, 1) if y_lo else tile)
-                for t in range(RADIX):
-                    value = tiles[(0 - t) % RADIX]
-                    for group in range(1, RADIX):
-                        value = jnp.where(group_of == group, tiles[(group - t) % RADIX], value)
-                    piece, chunk = divmod(block * RADIX + t, per_piece)
-                    out_refs[chunk][piece, part, at, :] = value.astype(jnp.bfloat16)
-        return carry
-
-    lax.fori_loop(0, rows // step, last, 0)
-
-
-def column_transform(x, pieces):
+                    out_refs[chunk][group * RADIX + y_lo, part] = wide[
+                        y_lo * rows : (y_lo + 1) * rows, k * LANES : (k + 1) * LANES
+                    ]
+
+
+def column_transform(x, pieces, share, held):
     _, rows, length = x.shape
     inner = length // RADIX
-    per_piece = length // pieces // LANES
-    block = math.gcd(rows, 64)
+    count = length // pieces // LANES
+    own = rows // PARTS
+    block = math.gcd(own, 64)
+    first = share * (own // block)
+    kept = pl.BlockSpec((pieces, 2, block, LANES), lambda i: (0, 0, i + first, 0))
     return pl.pallas_call(
-        column_kernel,
-        grid=(rows // block,),
+        functools.partial(column_kernel, len(held)),
+        grid=(own // block,),
         in_specs=[
-            pl.BlockSpec((2, block, length), lambda i: (0, i, 0)),
+            pl.BlockSpec((2, block, length), lambda i: (0, i + first, 0)),
             pl.BlockSpec((RADIX, 2, inner), lambda i: (0, 0, 0)),
             pl.BlockSpec((2 * inner, 2 * inner), lambda i: (0, 0)),
-        ],
-        out_specs=[pl.BlockSpec((pieces, 2, block, LANES), lambda i: (0, 0, i, 0))] * per_piece,
-        out_shape=[jax.ShapeDtypeStruct((pieces, 2, rows, LANES), jnp.bfloat16)] * per_piece,
-        scratch_shapes=[
-            pltpu.VMEM((RADIX, block, 2 * inner), jnp.bfloat16),
-            pltpu.VMEM((RADIX, block, 2 * inner), jnp.float32),
-        ],
+        ]
+        + [pl.BlockSpec(memory_space=pl.ANY)] * len(held),
+        out_specs=[pl.BlockSpec((pieces, 2, block, LANES), lambda i: (0, 0, i, 0))]
+        + [kept] * (count - 1),
+        out_shape=[jax.ShapeDtypeStruct((pieces, 2, own, LANES), jnp.bfloat16)]
+        + [jax.ShapeDtypeStruct((pieces, 2, rows, LANES), jnp.bfloat16)] * (count - 1),
+        scratch_shapes=[pltpu.VMEM((RADIX, block, 2 * inner), jnp.bfloat16)],
+        input_output_aliases={3 + i: 1 + i for i in range(len(held))},
         compiler_params=params(),
         cost_estimate=pl.CostEstimate(
-            flops=16 * rows * length * inner, bytes_accessed=8 * rows * length, transcendentals=0
+            flops=16 * own * length * inner, bytes_accessed=8 * own * length, transcendentals=0
         ),
         name="column_transform",
-    )(x, jnp.asarray(twiddle_table(length)), jnp.asarray(inner_table(inner)))
-
-
-def clean_kernel(
-    group, later, at_ref, x_ref, basis_ref, basis_t_ref, gain_ref, swap_ref, back_ref, lane_ref, *refs
-):
-    *out_refs, slab = refs[later:]
+    )(x, jnp.asarray(twiddle_table(length)), jnp.asarray(inner_table(inner)), *held)
+
+
+def clean_kernel(count, after, later, at_ref, *refs):
+    x_refs, refs = refs[:count], refs[count:]
+    basis_ref, basis_t_ref, gain_ref, swap_ref, back_ref = refs[:5]
+    *out_refs, slab = refs[5 + after + later :]
     out_refs = out_refs[: len(out_refs) - later]
-    sources, _, rows, _ = x_ref.shape
     chans = slab.shape[0]
     rows_dev = slab.shape[1] // LANES
-    tall = group * rows_dev
-    for b in range(chans // group):
-        if rows % tall == 0:
-            source, row = divmod(b * tall, rows)
-            tile = x_ref[source, 0, row : row + tall, :]
-        else:
-            take = tall // rows
-            tile = x_ref[b * take : (b + 1) * take, 0].reshape(tall, LANES)
-        tile = jnp.dot(tile, lane_ref[...], preferred_element_type=jnp.float32).astype(jnp.bfloat16)
-        turned = jnp.dot(swap_ref[...], tile, preferred_element_type=jnp.float32).astype(jnp.bfloat16)
-        for u in range(rows_dev):
-            slab[b * group : (b + 1) * group, u * LANES : (u + 1) * LANES] = turned[
-                u * group : (u + 1) * group
-            ]
+    tall = swap_ref.shape[0]
+    group = tall // rows_dev
+    begin = 0
+    for source in range(x_refs[0].shape[0]):
+        for x_ref in x_refs:
+            for row in range(0, x_ref.shape[2], tall):
+                turned = jnp.dot(
+                    swap_ref[...],
+                    x_ref[source, 0, row : row + tall, :],
+                    preferred_element_type=jnp.float32,
+                ).astype(jnp.bfloat16)
+                for u in range(rows_dev):
+                    slab[begin : begin + group, u * LANES : (u + 1) * LANES] = turned[
+                        u * group : (u + 1) * group
+                    ]
+                begin += group
     pair = math.gcd(rows_dev, 2)
     for first in range(0, rows_dev, pair):
         lanes = slice(first * LANES, (first + pair) * LANES)
@@ -214,6 +203,8 @@
     steps = len(out_refs)
     share = chans // steps
     out_rows = out_refs[0].shape[2]
+    tall = back_ref.shape[0]
+    group = tall // rows_dev
     for step, out_ref in enumerate(out_refs):
         start = lax.rem(at_ref[0] + step, steps) * share
         for b in range(share // group):
@@ -232,28 +223,33 @@
                 ).astype(jnp.bfloat16)
 
 
-def clean(at, x, basis, basis_t, gain, lane_table, steps, targets, rows_dev, later):
-    sources, _, rows, _ = x.shape
+def clean(at, xs, basis, basis_t, gain, steps, targets, rows_dev, after, later):
+    sources = xs[0].shape[0]
     chans = basis.shape[0]
-    group = 256 // rows_dev
+    own = chans // sources // len(xs)
+    swap = swap_table(min(256 // rows_dev, own), rows_dev)
+    back = np.ascontiguousarray(swap_table(256 // rows_dev, rows_dev).T)
     out_rows = chans * rows_dev // (targets * steps)
-    swap = swap_table(group, rows_dev)
     whole = lambda s, at: (0, 0)
+    waits = [pl.BlockSpec(memory_space=pl.ANY)] * (len(after) + len(later))
+    first_later = 1 + len(xs) + 5 + len(after)
     return pl.pallas_call(
-        functools.partial(clean_kernel, group, len(later)),
+        functools.partial(clean_kernel, len(xs), len(after), len(later)),
         grid_spec=pltpu.PrefetchScalarGridSpec(
             num_scalar_prefetch=1,
             grid=(2,),
             in_specs=[
-                pl.BlockSpec((sources, 1, rows, LANES), lambda s, at: (0, s, 0, 0)),
+                pl.BlockSpec((sources, 1, own * rows_dev, LANES), lambda s, at: (0, s, 0, 0))
+                for x in xs
+            ]
+            + [
                 pl.BlockSpec(basis.shape, whole),
                 pl.BlockSpec(basis.shape, whole),
                 pl.BlockSpec(gain.shape, whole),
                 pl.BlockSpec(swap.shape, whole),
-                pl.BlockSpec(swap.shape, whole),
-                pl.BlockSpec((LANES, LANES), whole),
+                pl.BlockSpec(back.shape, whole),
             ]
-            + [pl.BlockSpec(memory_space=pl.ANY)] * len(later),
+            + waits,
             out_specs=[
                 pl.BlockSpec((targets, 1, out_rows, LANES), lambda s, at: (0, s, 0, 0))
             ] * steps
@@ -262,7 +258,7 @@
         ),
         out_shape=[jax.ShapeDtypeStruct((targets, 2, out_rows, LANES), jnp.bfloat16)] * steps
         + [jax.ShapeDtypeStruct(a.shape, a.dtype) for a in later],
-        input_output_aliases={8 + i: steps + i for i in range(len(later))},
+        input_output_aliases={first_later + i: steps + i for i in range(len(later))},
         compiler_params=params(),
         cost_estimate=pl.CostEstimate(
             flops=12 * chans * chans * rows_dev * LANES,
@@ -270,17 +266,7 @@
             transcendentals=0,
         ),
         name="clean",
-    )(
-        at,
-        x,
-        basis,
-        basis_t,
-        gain,
-        jnp.asarray(swap),
-        jnp.asarray(np.ascontiguousarray(swap.T)),
-        lane_table,
-        *later,
-    )
+    )(at, *xs, basis, basis_t, gain, jnp.asarray(swap), jnp.asarray(back), *after, *later)
 
 
 def row_kernel(scale, group, steps, *refs):
@@ -328,46 +314,62 @@
     )(*pieces, table, *after)
 
 
-def place_kernel(x_ref, *refs):
-    refs[-1][...] = x_ref[0]
-
-
-def place(x, chunk, per_piece, held):
+def place_kernel(x_ref, table_ref, *refs):
+    out_ref = refs[-1]
+    shape = out_ref.shape
+    rows = shape[0] * shape[1] * shape[2]
+    tile = jnp.concatenate(
+        [x_ref[y_lo].reshape(rows, LANES) for y_lo in range(RADIX)], axis=1
+    )
+    value = jnp.dot(tile, table_ref[...], preferred_element_type=jnp.float32)
+    out_ref[...] = value.astype(jnp.bfloat16).reshape(shape)
+
+
+def place(x, chunk, count, held):
     pieces, _, chans, total, _ = x.shape
-    shape = jax.ShapeDtypeStruct((2, chans, total, pieces * per_piece * LANES), jnp.bfloat16)
+    groups = pieces // RADIX
+    table = order_table()
+    wide = RADIX * LANES
+    block = math.gcd(chans, 4)
     return pl.pallas_call(
         place_kernel,
-        grid=(pieces,),
-        in_specs=[pl.BlockSpec((1, 2, chans, total, LANES), lambda j: (j, 0, 0, 0, 0))]
+        grid=(chans // block, groups),
+        in_specs=[
+            pl.BlockSpec((RADIX, 2, block, total, LANES), lambda c, g: (g, 0, c, 0, 0)),
+            pl.BlockSpec(table.shape, lambda c, g: (0, 0)),
+        ]
         + [pl.BlockSpec(memory_space=pl.ANY)] * len(held),
-        out_specs=pl.BlockSpec((2, chans, total, LANES), lambda j: (0, 0, 0, j * per_piece + chunk)),
-        out_shape=shape,
-        input_output_aliases={1: 0} if held else {},
+        out_specs=pl.BlockSpec(
+            (2, block, total, wide), lambda c, g: (0, c, 0, chunk * groups + g)
+        ),
+        out_shape=jax.ShapeDtypeStruct((2, chans, total, count * groups * wide), jnp.bfloat16),
+        input_output_aliases={2: 0} if held else {},
         compiler_params=params(),
         cost_estimate=pl.CostEstimate(
-            flops=0, bytes_accessed=8 * pieces * chans * total * LANES, transcendentals=0
+            flops=4 * pieces * chans * total * LANES * wide,
+            bytes_accessed=8 * pieces * chans * total * LANES,
+            transcendentals=0,
         ),
         name="place",
-    )(x, *held)
-
-
-def turn_kernel(basis_ref, _, out_ref, __):
+    )(x, jnp.asarray(table), *held)
+
+
+def turn_kernel(later, basis_ref, *refs):
+    out_ref = refs[-1 - later]
     out_ref[...] = basis_ref[...].T
 
 
-def turn(basis, later):
+def turn(basis, after, later):
+    untouched = pl.BlockSpec(memory_space=pl.ANY)
     return pl.pallas_call(
-        turn_kernel,
-        in_specs=[pl.BlockSpec(memory_space=pltpu.VMEM), pl.BlockSpec(memory_space=pl.ANY)],
-        out_specs=[pl.BlockSpec(memory_space=pltpu.VMEM), pl.BlockSpec(memory_space=pl.ANY)],
-        out_shape=[
-            jax.ShapeDtypeStruct(basis.shape, basis.dtype),
-            jax.ShapeDtypeStruct(later.shape, later.dtype),
-        ],
-        input_output_aliases={1: 1},
+        functools.partial(turn_kernel, len(later)),
+        in_specs=[pl.BlockSpec(memory_space=pltpu.VMEM)] + [untouched] * (len(after) + len(later)),
+        out_specs=[pl.BlockSpec(memory_space=pltpu.VMEM)] + [untouched] * len(later),
+        out_shape=[jax.ShapeDtypeStruct(a.shape, a.dtype) for a in (basis, *later)],
+        input_output_aliases={1 + len(after) + i: 1 + i for i in range(len(later))},
         compiler_params=params(),
         name="turn",
-    )(basis, later)
+    )(basis, *after, *later)
 
 
 def exchange(x):
@@ -384,30 +386,38 @@
     basis = exchange(jnp.broadcast_to(eigen_basis, (chan_count,) + eigen_basis.shape))
     basis = basis.reshape(chan_count * chans, -1)
     gain = eigenvalues[:, None] / (eigenvalues[:, None] + noise_power[None, :])
-    lane_table = jnp.asarray(lane_tables(length))
-    chunks = list(column_transform(visibility.reshape(2, chans * rows_dev, length), chan_count))
-    basis_t, chunks[0] = turn(basis, chunks[0])
-    cells, cleaned, held = [], [], []
-    for k in range(min(2, count)):
-        cells.append(exchange(chunks[k]))
+    flat = visibility.reshape(2, chans * rows_dev, length)
+    firsts, chunks = [], []
+    for share in range(PARTS):
+        first, *chunks = column_transform(flat, chan_count, share, chunks)
+        firsts.append(exchange(first))
+    basis_t, *chunks = turn(basis, firsts[:1], chunks)
+    cells = [firsts] + [[exchange(chunk)] for chunk in chunks[:1]]
+    chunks = chunks[1:]
+    pieces, lines, held = [], [], []
     for k in range(count):
-        tile = lax.rem(lax.axis_index("chan") * count + k, RADIX)
-        lanes = lax.dynamic_index_in_dim(lane_table, tile, 0, keepdims=False)
+        after = pieces[k - 2][1:] if k >= 2 else []
+        later = chunks[:1]
+        chunks = chunks[1:]
         result = clean(
-            at, cells[k], basis, basis_t, gain, lanes, uv_count, chan_count, rows_dev, chunks[k + 2 : k + 3]
+            at, cells[k], basis, basis_t, gain, uv_count, chan_count, rows_dev, after, later
         )
-        cleaned.append(result[:uv_count])
-        if k + 2 < count:
-            cells.append(exchange(result[uv_count]))
+        cells += [[exchange(chunk)] for chunk in result[uv_count:]]
+        pieces.append(
+            [result[0]]
+            + [
+                lax.ppermute(
+                    result[step], "uv", [(z, (z + step) % uv_count) for z in range(uv_count)]
+                )
+                for step in range(1, uv_count)
+            ]
+        )
     for k in range(count):
-        pieces = [cleaned[k][0]] + [
-            lax.ppermute(
-                cleaned[k][step], "uv", [(z, (z + step) % uv_count) for z in range(uv_count)]
-            )
-            for step in range(1, uv_count)
-        ]
-        after = [parts[0] for parts in cleaned[k + 2 : k + 3]] + cells[k + 3 : k + 4]
-        lines = row_transform(pieces, at, out_chans, rows_dev, length, after)
+        after = [parts[0] for parts in pieces[k + 2 : k + 3]]
+        after += [parts[1] for parts in pieces[k + 1 : k + 2]]
+        if k == 0:
+            after += cells[-1]
+        lines = row_transform(pieces[k], at, out_chans, rows_dev, length, after)
         held = [place(exchange(lines), k, count, held)]
     return held[0]
 

time: 401 us -> 406 us (1.012)
  waiting for transfers between devices: 218 us -> 238 us
  Pallas kernels: 113 us -> 98.5 us
    ppermute x12, waiting for transfers between devices: 154 us -> 175 us  [shards(): lax.ppermute(result[step], 'uv', [(z, (z + step) % uv_count) for z in ran...]
    pallas_call x10 -> x11, Pallas kernels: 93.6 us -> 79.3 us  [the longest x4 33.5 us: clean(): pl.pallas_call(functools.partial(clean_kernel, len(xs), len(after), len(l...]
    ppermute x12, starting transfers between devices: 16.2 us -> 12.2 us  [shards(): lax.ppermute(result[step], 'uv', [(z, (z + step) % uv_count) for z in ran...]
    unnamed x58 -> x48, local copies, waits for them, and re-layouts: 10.8 us -> 13.2 us
    all_to_all x9 -> x10, starting transfers between devices: 36.2 us -> 38.3 us  [exchange(): return lax.all_to_all(x, 'chan', split_axis=0, concat_axis=0, tiled=True)]
    all_to_all x9 -> x10, waiting for transfers between devices: 63.9 us -> 62.9 us  [exchange(): return lax.all_to_all(x, 'chan', split_axis=0, concat_axis=0, tiled=True)]
  transfers between devices with their start and end apart: 21 -> 22, of which waited for: 15 -> 14; matrix products, arithmetic and copies ran while one was open for 1% -> 1% of each run, Pallas kernels for 27% -> 22%
where the time goes in v4:
time: 406 us; the launch traced here: 405 us
  waiting for transfers between devices  238 us (59%)
  Pallas kernels  98.5 us (24%)
  starting transfers between devices  50.4 us (12%)
  local copies, waits for them, and re-layouts  16.5 us (4%)
    ppermute x12, waiting for transfers between devices, shards(): lax.ppermute(result[step], 'uv', [(z, (z + step) % uv_count) for z in ran...  175 us
    all_to_all x10, waiting for transfers between devices, exchange(): return lax.all_to_all(x, 'chan', split_axis=0, concat_axis=0, tiled=True)  62.9 us
    all_to_all x10, starting transfers between devices, exchange(): return lax.all_to_all(x, 'chan', split_axis=0, concat_axis=0, tiled=True)  38.3 us
    pallas_call x4, Pallas kernels, clean(): pl.pallas_call(functools.partial(clean_kernel, len(xs), len(after), len(l...  33.5 us
    pallas_call x4, Pallas kernels, place(): pl.pallas_call(place_kernel, grid=(chans // block, groups), in_specs=[pl....  24.1 us
    pallas_call x2, Pallas kernels, column_transform(): pl.pallas_call(functools.partial(column_kernel, len(held)), grid=(own //...  19.7 us
    pallas_call x4, Pallas kernels, row_transform(): pl.pallas_call(functools.partial(row_kernel, scale, group, steps), grid=(...  19.2 us
    unnamed x48, local copies, waits for them, and re-layouts  13.2 us
  transfers between devices with their start and end apart: 22, of which 14 were waited for; matrix products, arithmetic and copies ran while one was open for 1% of the time, Pallas kernels for 22%

profile of v4, /device:TPU:8, one launch (start us, length us, event | category | flops | bytes accessed | tf_op | source)
XLA Modules:
  0.0 404.8 jit_solution(12242088203568677305)
XLA Ops:
  0.0 1.7 broadcast_in_dim.2
  1.7 3.7 all-to-all-start
  5.4 9.8 %column_transform.2 = (bf16[8,2,256,128]{3,2,1,0:T(8,128)(2,1)}, bf16[8,2,512,128]{3,2,1,0:T(8,128)(2,1)}, bf16[8,2,512,128]{3,2,1,0:T(8,128)(2,1)}, bf16[8,2,512,128]{3,2,1,0:T(8,128)(2,1)}) custom-call(bf16[2,512,4096]{2,1,0:T(8,128)(2,1)} %bitcast.10, f32[8,2,512]{2,1,0:T(2,128)} %constant.29.clone.twiddle_ref, bf16[1024,1024]{1,0:T(8,128)(2,1)} %constant.30.clone.table_ref), custom_call_target="tpu_custom_call" | custom-call | flops 8589934592 | bytes 8388608 | tf_op jit(solution)/shard_map/column_transform/pallas_call | solution.py:142
  15.3 4.2 %all-to-all-start.1 = ((bf16[8,2,256,128]{3,2,1,0:T(8,128)(2,1)}), bf16[8,2,256,128]{3,2,1,0:T(8,128)(2,1)S(1)}, u32[]{:S(2)}, u32[]{:S(2)}) async-start(bf16[8,2,256,128]{3,2,1,0:T(8,128)(2,1)} %get-tuple-element.35), calls=%async_computation.1 | async-start | bytes 2097152 | tf_op jit(solution)/shard_map/all_to_all | solution.py:376
  19.5 9.9 %column_transform.3 = (bf16[8,2,256,128]{3,2,1,0:T(8,128)(2,1)}, bf16[8,2,512,128]{3,2,1,0:T(8,128)(2,1)}, bf16[8,2,512,128]{3,2,1,0:T(8,128)(2,1)}, bf16[8,2,512,128]{3,2,1,0:T(8,128)(2,1)}) custom-call(bf16[2,512,4096]{2,1,0:T(8,128)(2,1)} %bitcast.11, ...), custom_call_target="tpu_custom_call", output_to_operand_aliasing={{1}: (3, {}), {2}: (4, {}), {3}: (5, {})} | custom-call | flops 8589934592 | bytes 8388608 | tf_op jit(solution)/shard_map/column_transform/pallas_call | solution.py:142
  29.4 5.5 %all-to-all-done.1.refs_0_ = bf16[8,2,256,128]{3,2,1,0:T(8,128)(2,1)S(1)} async-done(((bf16[8,2,256,128]{3,2,1,0:T(8,128)(2,1)}), bf16[8,2,256,128]{3,2,1,0:T(8,128)(2,1)S(1)}, u32[]{:S(2)}, u32[]{:S(2)}) %all-to-all-start.1) | async-done | bytes 1048608 | tf_op jit(solution)/shard_map/all_to_all | solution.py:376
  34.9 3.6 all-to-all-start.5
  38.5 2.1 turn.1
  40.5 13.3 %all-to-all-done.5.refs_1_ = bf16[8,2,256,128]{3,2,1,0:T(8,128)(2,1)S(1)} async-done(((bf16[8,2,256,128]{3,2,1,0:T(8,128)(2,1)}), bf16[8,2,256,128]{3,2,1,0:T(8,128)(2,1)S(1)}, u32[]{:S(2)}, u32[]{:S(2)}) %all-to-all-start.5) | async-done | bytes 1048608 | tf_op jit(solution)/shard_map/all_to_all | solution.py:376
  54.8 3.6 all-to-all-start.2
  59.3 8.4 %clean.6 = (bf16[8,2,128,128]{3,2,1,0:T(8,128)(2,1)}, bf16[8,2,128,128]{3,2,1,0:T(8,128)(2,1)}, bf16[8,2,128,128]{3,2,1,0:T(8,128)(2,1)}, bf16[8,2,128,128]{3,2,1,0:T(8,128)(2,1)}, bf16[8,2,512,128]{3,2,1,0:T(8,128)(2,1)}) custom-call(s32[1]{0:T(128)} %bitcast.at_ref, bf16[8,2,256,128]{3,2,1,0:T(8,128)(2,1)} %copy-done.4, ...), custom_call_target="tpu_custom_call", output_to_operand_aliasing={{4}: (8, {})} | custom-call | flops 3221225472 | bytes 4194304 | tf_op jit(solution)/shard_map/clean/pallas_call | solution.py:236
  67.7 17.3 %all-to-all-done.2.refs_0_ = bf16[8,2,512,128]{3,2,1,0:T(8,128)(2,1)S(1)} async-done(((bf16[8,2,512,128]{3,2,1,0:T(8,128)(2,1)}), bf16[8,2,512,128]{3,2,1,0:T(8,128)(2,1)S(1)}, u32[]{:S(2)}, u32[]{:S(2)}) %all-to-all-start.2) | async-done | bytes 2097184 | tf_op jit(solution)/shard_map/all_to_all | solution.py:376
  85.0 1.3 copy-done.8
  86.3 3.6 all-to-all-start.6
  89.9 8.4 %clean.4 = (bf16[8,2,128,128]{3,2,1,0:T(8,128)(2,1)}, bf16[8,2,128,128]{3,2,1,0:T(8,128)(2,1)}, bf16[8,2,128,128]{3,2,1,0:T(8,128)(2,1)}, bf16[8,2,128,128]{3,2,1,0:T(8,128)(2,1)}, bf16[8,2,512,128]{3,2,1,0:T(8,128)(2,1)}) custom-call(s32[1]{0:T(128)} %bitcast.at_ref, bf16[8,2,512,128]{3,2,1,0:T(8,128)(2,1)} %copy-done.8, ...), custom_call_target="tpu_custom_call", output_to_operand_aliasing={{4}: (7, {})} | custom-call | flops 3221225472 | bytes 4194304 | tf_op jit(solution)/shard_map/clean/pallas_call | solution.py:236
  98.3 18.2 %all-to-all-done.6.refs_0_ = bf16[8,2,512,128]{3,2,1,0:T(8,128)(2,1)S(1)} async-done(((bf16[8,2,512,128]{3,2,1,0:T(8,128)(2,1)}), bf16[8,2,512,128]{3,2,1,0:T(8,128)(2,1)S(1)}, u32[]{:S(2)}, u32[]{:S(2)}) %all-to-all-start.6) | async-done | bytes 2097184 | tf_op jit(solution)/shard_map/all_to_all | solution.py:376
  117.8 3.6 all-to-all-start.3
  121.4 1.6 collective-permute-start.6
  124.3 1.8 collective-permute-start.8
  126.3 1.6 dynamic-slice_bitcast_fusion.refs_4_
  127.9 29.8 %collective-permute-done.6.refs_6_.refs_1_ = bf16[8,2,128,128]{3,2,1,0:T(8,128)(2,1)S(1)} collective-permute-done((bf16[8,2,128,128]{3,2,1,0:T(8,128)(2,1)}, bf16[8,2,128,128]{3,2,1,0:T(8,128)(2,1)S(1)}, u32[]{:S(2)}, u32[]{:S(2)}) %collective-permute-start.6) | collective-permute-done | bytes 524320 | tf_op jit(solution)/shard_map/ppermute | solution.py:409
  157.7 11.7 %collective-permute-done.7.refs_7_.refs_2_ = bf16[8,2,128,128]{3,2,1,0:T(8,128)(2,1)} collective-permute-done((bf16[8,2,128,128]{3,2,1,0:T(8,128)(2,1)}, bf16[8,2,128,128]{3,2,1,0:T(8,128)(2,1)}, u32[]{:S(2)}, u32[]{:S(2)}) %collective-permute-start.7) | collective-permute-done | bytes 524320 | tf_op jit(solution)/shard_map/ppermute | solution.py:409
  169.4 12.4 %collective-permute-done.8.refs_8_.refs_3_ = bf16[8,2,128,128]{3,2,1,0:T(8,128)(2,1)} collective-permute-done((bf16[8,2,128,128]{3,2,1,0:T(8,128)(2,1)}, bf16[8,2,128,128]{3,2,1,0:T(8,128)(2,1)}, u32[]{:S(2)}, u32[]{:S(2)}) %collective-permute-start.8) | collective-permute-done | bytes 524320 | tf_op jit(solution)/shard_map/ppermute | solution.py:409
  181.8 8.3 %clean.7 = (bf16[8,2,128,128]{3,2,1,0:T(8,128)(2,1)}, bf16[8,2,128,128]{3,2,1,0:T(8,128)(2,1)}, bf16[8,2,128,128]{3,2,1,0:T(8,128)(2,1)}, bf16[8,2,128,128]{3,2,1,0:T(8,128)(2,1)}) custom-call(s32[1]{0:T(128)} %bitcast.at_ref, bf16[8,2,512,128]{3,2,1,0:T(8,128)(2,1)} %copy-done.7, bf16[512,512]{1,0:T(8,128)(2,1)} %bitcast.8, ...), custom_call_target="tpu_custom_call" | custom-call | flops 3221225472 | bytes 4194304 | tf_op jit(solution)/shard_map/clean/pallas_call | solution.py:236
  191.6 4.8 %row_transform.7 = bf16[8,2,16,32,128]{4,3,2,1,0:T(8,128)(2,1)} custom-call(bf16[8,2,128,128]{3,2,1,0:T(8,128)(2,1)} %get-tuple-element.64.refs_0_, bf16[8,2,128,128]{3,2,1,0:T(8,128)(2,1)} %copy-done.12, bf16[8,2,128,128]{3,2,1,0:T(8,128)(2,1)} %collective-permute-done.7.refs_7_.refs_2_, bf16[8,2,128,128]{3,2,1,0:T(8,128)(2,1)} %collective-permute-done.8.refs_8_.refs_3_, ...), custom_call_target="tpu_custom_call" | custom-call | flops 536870912 | bytes 4194304 | tf_op jit(solution)/shard_map/row_transform/pallas_call | solution.py:299
  196.4 3.9 all-to-all-start.9
  202.4 33.0 %collective-permute-done.1.refs_7_.refs_2_ = bf16[8,2,128,128]{3,2,1,0:T(8,128)(2,1)S(1)} collective-permute-done((bf16[8,2,128,128]{3,2,1,0:T(8,128)(2,1)}, bf16[8,2,128,128]{3,2,1,0:T(8,128)(2,1)S(1)}, u32[]{:S(2)}, u32[]{:S(2)}) %collective-permute-start.1) | collective-permute-done | bytes 524320 | tf_op jit(solution)/shard_map/ppermute | solution.py:409
  235.4 10.9 %collective-permute-done.2.refs_8_.refs_3_ = bf16[8,2,128,128]{3,2,1,0:T(8,128)(2,1)S(1)} collective-permute-done((bf16[8,2,128,128]{3,2,1,0:T(8,128)(2,1)}, bf16[8,2,128,128]{3,2,1,0:T(8,128)(2,1)S(1)}, u32[]{:S(2)}, u32[]{:S(2)}) %collective-permute-start.2) | collective-permute-done | bytes 524320 | tf_op jit(solution)/shard_map/ppermute | solution.py:409
  247.2 8.4 %clean.5 = (bf16[8,2,128,128]{3,2,1,0:T(8,128)(2,1)}, bf16[8,2,128,128]{3,2,1,0:T(8,128)(2,1)}, bf16[8,2,128,128]{3,2,1,0:T(8,128)(2,1)}, bf16[8,2,128,128]{3,2,1,0:T(8,128)(2,1)}) custom-call(s32[1]{0:T(128)} %bitcast.at_ref, bf16[8,2,512,128]{3,2,1,0:T(8,128)(2,1)} %copy-done, bf16[512,512]{1,0:T(8,128)(2,1)} %bitcast.9, ...), custom_call_target="tpu_custom_call" | custom-call | flops 3221225472 | bytes 4194304 | tf_op jit(solution)/shard_map/clean/pallas_call | solution.py:236
  256.4 4.8 %row_transform.6 = bf16[8,2,16,32,128]{4,3,2,1,0:T(8,128)(2,1)} custom-call(bf16[8,2,128,128]{3,2,1,0:T(8,128)(2,1)} %get-tuple-element.63.refs_0_, bf16[8,2,128,128]{3,2,1,0:T(8,128)(2,1)} %copy-done.5, bf16[8,2,128,128]{3,2,1,0:T(8,128)(2,1)} %copy-done.17, bf16[8,2,128,128]{3,2,1,0:T(8,128)(2,1)} %copy-done.18, ...), custom_call_target="tpu_custom_call" | custom-call | flops 536870912 | bytes 4194304 | tf_op jit(solution)/shard_map/row_transform/pallas_call | solution.py:299
  261.2 1.3 copy-done.3
  262.5 3.8 all-to-all-start.8
  268.5 33.1 %collective-permute-done.10.refs_2_ = bf16[8,2,128,128]{3,2,1,0:T(8,128)(2,1)S(1)} collective-permute-done((bf16[8,2,128,128]{3,2,1,0:T(8,128)(2,1)}, bf16[8,2,128,128]{3,2,1,0:T(8,128)(2,1)S(1)}, u32[]{:S(2)}, u32[]{:S(2)}) %collective-permute-start.10) | collective-permute-done | bytes 524320 | tf_op jit(solution)/shard_map/ppermute | solution.py:409
  301.5 11.0 %collective-permute-done.11.refs_3_ = bf16[8,2,128,128]{3,2,1,0:T(8,128)(2,1)S(1)} collective-permute-done((bf16[8,2,128,128]{3,2,1,0:T(8,128)(2,1)S(1)}, bf16[8,2,128,128]{3,2,1,0:T(8,128)(2,1)S(1)}, u32[]{:S(2)}, u32[]{:S(2)}) %collective-permute-start.11) | collective-permute-done | bytes 524320 | tf_op jit(solution)/shard_map/ppermute | solution.py:409
  314.2 4.7 %row_transform.5 = bf16[8,2,16,32,128]{4,3,2,1,0:T(8,128)(2,1)} custom-call(bf16[8,2,128,128]{3,2,1,0:T(8,128)(2,1)} %get-tuple-element.59.refs_0_.refs_5_, bf16[8,2,128,128]{3,2,1,0:T(8,128)(2,1)} %copy-done.9, bf16[8,2,128,128]{3,2,1,0:T(8,128)(2,1)} %copy-done.13, bf16[8,2,128,128]{3,2,1,0:T(8,128)(2,1)} %copy-done.14, ...), custom_call_target="tpu_custom_call" | custom-call | flops 536870912 | bytes 4194304 | tf_op jit(solution)/shard_map/row_transform/pallas_call | solution.py:299
  318.9 1.4 copy-done.1
  320.3 4.4 %all-to-all-start.7 = ((bf16[8,2,16,32,128]{4,3,2,1,0:T(8,128)(2,1)}), bf16[8,2,16,32,128]{4,3,2,1,0:T(8,128)(2,1)}, u32[]{:S(2)}, u32[]{:S(2)}) async-start(bf16[8,2,16,32,128]{4,3,2,1,0:T(8,128)(2,1)} %row_transform.5), calls=%async_computation.7 | async-start | bytes 4194304 | tf_op jit(solution)/shard_map/all_to_all | solution.py:376
  324.8 3.0 collective-permute-start.5
  327.8 31.3 %collective-permute-done.4.refs_2_ = bf16[8,2,128,128]{3,2,1,0:T(8,128)(2,1)S(1)} collective-permute-done((bf16[8,2,128,128]{3,2,1,0:T(8,128)(2,1)S(1)}, bf16[8,2,128,128]{3,2,1,0:T(8,128)(2,1)S(1)}, u32[]{:S(2)}, u32[]{:S(2)}) %collective-permute-start.4) | collective-permute-done | bytes 524320 | tf_op jit(solution)/shard_map/ppermute | solution.py:409
  359.1 2.1 collective-permute-done.5.refs_3_
  362.1 4.8 %row_transform.4 = bf16[8,2,16,32,128]{4,3,2,1,0:T(8,128)(2,1)} custom-call(bf16[8,2,128,128]{3,2,1,0:T(8,128)(2,1)} %get-tuple-element.49.refs_0_.refs_5_, bf16[8,2,128,128]{3,2,1,0:T(8,128)(2,1)} %copy-done.6, bf16[8,2,128,128]{3,2,1,0:T(8,128)(2,1)} %copy-done.15, bf16[8,2,128,128]{3,2,1,0:T(8,128)(2,1)} %copy-done.16, ...), custom_call_target="tpu_custom_call" | custom-call | flops 536870912 | bytes 4194304 | tf_op jit(solution)/shard_map/row_transform/pallas_call | solution.py:299
  366.9 3.9 all-to-all-start.4
  370.8 6.0 %place.4.refs_0_ = bf16[2,16,32,4096]{3,2,1,0:T(8,128)(2,1)} custom-call(bf16[8,2,16,32,128]{4,3,2,1,0:T(8,128)(2,1)} %copy-done.3, bf16[1024,1024]{1,0:T(8,128)(2,1)} %constant.34.clone.table_ref), custom_call_target="tpu_custom_call" | custom-call | flops 2147483648 | bytes 4194304 | tf_op jit(solution)/shard_map/place/pallas_call | solution.py:334
  376.8 6.0 %place.5.refs_0_ = bf16[2,16,32,4096]{3,2,1,0:T(8,128)(2,1)} custom-call(bf16[8,2,16,32,128]{4,3,2,1,0:T(8,128)(2,1)} %copy-done.1, bf16[1024,1024]{1,0:T(8,128)(2,1)} %constant.34.clone.table_ref, bf16[2,16,32,4096]{3,2,1,0:T(8,128)(2,1)} %place.4.refs_0_), custom_call_target="tpu_custom_call", output_to_operand_aliasing={{}: (2, {})} | custom-call | flops 2147483648 | bytes 4194304 | tf_op jit(solution)/shard_map/place/pallas_call | solution.py:334
  382.8 6.0 %place.6.refs_0_ = bf16[2,16,32,4096]{3,2,1,0:T(8,128)(2,1)} custom-call(bf16[8,2,16,32,128]{4,3,2,1,0:T(8,128)(2,1)} %all-to-all-done.7.x_ref, bf16[1024,1024]{1,0:T(8,128)(2,1)} %constant.34.clone.table_ref, bf16[2,16,32,4096]{3,2,1,0:T(8,128)(2,1)} %place.5.refs_0_), custom_call_target="tpu_custom_call", output_to_operand_aliasing={{}: (2, {})} | custom-call | flops 2147483648 | bytes 4194304 | tf_op jit(solution)/shard_map/place/pallas_call | solution.py:334
  388.8 8.6 %all-to-all-done.4.x_ref = bf16[8,2,16,32,128]{4,3,2,1,0:T(8,128)(2,1)S(1)} async-done(((bf16[8,2,16,32,128]{4,3,2,1,0:T(8,128)(2,1)}), bf16[8,2,16,32,128]{4,3,2,1,0:T(8,128)(2,1)S(1)}, u32[]{:S(2)}, u32[]{:S(2)}) %all-to-all-start.4) | async-done | bytes 2097184 | tf_op jit(solution)/shard_map/all_to_all | solution.py:376
  397.4 1.4 copy-done.2
  398.8 6.0 %place.7 = bf16[2,16,32,4096]{3,2,1,0:T(8,128)(2,1)} custom-call(bf16[8,2,16,32,128]{4,3,2,1,0:T(8,128)(2,1)} %copy-done.2, bf16[1024,1024]{1,0:T(8,128)(2,1)} %constant.34.clone.table_ref, bf16[2,16,32,4096]{3,2,1,0:T(8,128)(2,1)} %place.6.refs_0_), custom_call_target="tpu_custom_call", output_to_operand_aliasing={{}: (2, {})} | custom-call | flops 2147483648 | bytes 4194304 | tf_op jit(solution)/shard_map/place/pallas_call | solution.py:334
  (62 shorter events, 14.4 us)
Async XLA Ops:
  1.7 13.6 %all-to-all-start = ((bf16[8,64,512]{2,1,0:T(8,128)(2,1)}), bf16[8,64,512]{2,1,0:T(8,128)(2,1)S(1)}, u32[]{:S(2)}, u32[]{:S(2)}) async-start(bf16[8,64,512]{2,1,0:T(8,128)(2,1)} %broadcast_in_dim.2), calls=%async_computation | async-start | bytes 1048576 | tf_op jit(solution)/shard_map/all_to_all | solution.py:376
  15.2 14.1 %copy-start.10 = (bf16[8,64,512]{2,1,0:T(8,128)(2,1)}, bf16[8,64,512]{2,1,0:T(8,128)(2,1)S(1)}, u32[]{:S(2)}) copy-start(bf16[8,64,512]{2,1,0:T(8,128)(2,1)S(1)} %all-to-all-done) | copy-start | bytes 1572868
  15.3 19.6 %all-to-all-start.1 = ((bf16[8,2,256,128]{3,2,1,0:T(8,128)(2,1)}), bf16[8,2,256,128]{3,2,1,0:T(8,128)(2,1)S(1)}, u32[]{:S(2)}, u32[]{:S(2)}) async-start(bf16[8,2,256,128]{3,2,1,0:T(8,128)(2,1)} %get-tuple-element.35), calls=%async_computation.1 | async-start | bytes 2097152 | tf_op jit(solution)/shard_map/all_to_all | solution.py:376
  34.9 3.6 copy-start.4
  34.9 18.9 %all-to-all-start.5 = ((bf16[8,2,256,128]{3,2,1,0:T(8,128)(2,1)}), bf16[8,2,256,128]{3,2,1,0:T(8,128)(2,1)S(1)}, u32[]{:S(2)}, u32[]{:S(2)}) async-start(bf16[8,2,256,128]{3,2,1,0:T(8,128)(2,1)} %get-tuple-element.53), calls=%async_computation.5 | async-start | bytes 2097152 | tf_op jit(solution)/shard_map/all_to_all | solution.py:376
  53.8 1.0 copy-start.11
  53.8 4.6 %copy-start.19 = (f32[512]{0:T(512)S(1)}, f32[512]{0:T(512)}, u32[]{:S(2)}) copy-start(f32[512]{0:T(512)} %param.26) | copy-start | bytes 6148
  53.8 4.6 %copy-start.20 = (f32[8]{0:T(128)S(1)}, f32[8]{0:T(128)}, u32[]{:S(2)}) copy-start(f32[8]{0:T(128)} %param.27) | copy-start | bytes 100
  54.8 30.2 %all-to-all-start.2 = ((bf16[8,2,512,128]{3,2,1,0:T(8,128)(2,1)}), bf16[8,2,512,128]{3,2,1,0:T(8,128)(2,1)S(1)}, u32[]{:S(2)}, u32[]{:S(2)}) async-start(bf16[8,2,512,128]{3,2,1,0:T(8,128)(2,1)} %get-tuple-element.42), calls=%async_computation.2 | async-start | bytes 4194304 | tf_op jit(solution)/shard_map/all_to_all | solution.py:376
  85.0 1.3 copy-start.8
  86.3 30.2 %all-to-all-start.6 = ((bf16[8,2,512,128]{3,2,1,0:T(8,128)(2,1)}), bf16[8,2,512,128]{3,2,1,0:T(8,128)(2,1)S(1)}, u32[]{:S(2)}, u32[]{:S(2)}) async-start(bf16[8,2,512,128]{3,2,1,0:T(8,128)(2,1)} %get-tuple-element.55), calls=%async_computation.6 | async-start | bytes 4194304 | tf_op jit(solution)/shard_map/all_to_all | solution.py:376
  116.5 1.3 copy-start.7
  117.8 72.4 %all-to-all-start.3 = ((bf16[8,2,512,128]{3,2,1,0:T(8,128)(2,1)}), bf16[8,2,512,128]{3,2,1,0:T(8,128)(2,1)S(1)}, u32[]{:S(2)}, u32[]{:S(2)}) async-start(bf16[8,2,512,128]{3,2,1,0:T(8,128)(2,1)} %get-tuple-element.45), calls=%async_computation.3 | async-start | bytes 4194304 | tf_op jit(solution)/shard_map/all_to_all | solution.py:376
  121.4 36.3 %collective-permute-start.6 = (bf16[8,2,128,128]{3,2,1,0:T(8,128)(2,1)}, bf16[8,2,128,128]{3,2,1,0:T(8,128)(2,1)S(1)}, u32[]{:S(2)}, u32[]{:S(2)}) collective-permute-start(bf16[8,2,128,128]{3,2,1,0:T(8,128)(2,1)} %get-tuple-element.56), channel_id=1, source_target_pairs={{0,8},{8,16},{16,24},{24,0},{1,9},{9,17},{17,25},{25,1},{2,10},{10... | collective-permute-start | bytes 1572872 | tf_op jit(solution)/shard_map/ppermute | solution.py:409
  123.0 46.3 %collective-permute-start.7 = (bf16[8,2,128,128]{3,2,1,0:T(8,128)(2,1)}, bf16[8,2,128,128]{3,2,1,0:T(8,128)(2,1)}, u32[]{:S(2)}, u32[]{:S(2)}) collective-permute-start(bf16[8,2,128,128]{3,2,1,0:T(8,128)(2,1)} %get-tuple-element.57), channel_id=1, source_target_pairs={{0,16},{8,24},{16,0},{24,8},{1,17},{9,25},{17,1},{25,9},{2,18},{10... | collective-permute-start | bytes 1572872 | tf_op jit(solution)/shard_map/ppermute | solution.py:409
  124.3 57.5 %collective-permute-start.8 = (bf16[8,2,128,128]{3,2,1,0:T(8,128)(2,1)}, bf16[8,2,128,128]{3,2,1,0:T(8,128)(2,1)}, u32[]{:S(2)}, u32[]{:S(2)}) collective-permute-start(bf16[8,2,128,128]{3,2,1,0:T(8,128)(2,1)} %get-tuple-element.58), channel_id=1, source_target_pairs={{0,24},{8,0},{16,8},{24,16},{1,25},{9,1},{17,9},{25,17},{2,26},{10... | collective-permute-start | bytes 1572872 | tf_op jit(solution)/shard_map/ppermute | solution.py:409
  126.1 64.1 %collective-permute-start = (bf16[8,2,128,128]{3,2,1,0:T(8,128)(2,1)}, bf16[8,2,128,128]{3,2,1,0:T(8,128)(2,1)S(1)}, u32[]{:S(2)}, u32[]{:S(2)}) collective-permute-start(bf16[8,2,128,128]{3,2,1,0:T(8,128)(2,1)} %get-tuple-element.46), channel_id=1, source_target_pairs={{0,8},{8,16},{16,24},{24,0},{1,9},{9,17},{17,25},{25,1},{2,10},{10... | collective-permute-start | bytes 1572872 | tf_op jit(solution)/shard_map/ppermute | solution.py:409
  157.7 24.1 %copy-start.12 = (bf16[8,2,128,128]{3,2,1,0:T(8,128)(2,1)}, bf16[8,2,128,128]{3,2,1,0:T(8,128)(2,1)S(1)}, u32[]{:S(2)}) copy-start(bf16[8,2,128,128]{3,2,1,0:T(8,128)(2,1)S(1)} %collective-permute-done.6.refs_6_.refs_1_) | copy-start | bytes 1572868
  190.1 0.8 copy-start.5
  190.2 1.5 copy-start
  196.4 64.7 %all-to-all-start.9 = ((bf16[8,2,16,32,128]{4,3,2,1,0:T(8,128)(2,1)}), bf16[8,2,16,32,128]{4,3,2,1,0:T(8,128)(2,1)S(1)}, u32[]{:S(2)}, u32[]{:S(2)}) async-start(bf16[8,2,16,32,128]{4,3,2,1,0:T(8,128)(2,1)} %row_transform.7), calls=%async_computation.9 | async-start | bytes 4194304 | tf_op jit(solution)/shard_map/all_to_all | solution.py:376
  200.3 35.1 %collective-permute-start.1 = (bf16[8,2,128,128]{3,2,1,0:T(8,128)(2,1)}, bf16[8,2,128,128]{3,2,1,0:T(8,128)(2,1)S(1)}, u32[]{:S(2)}, u32[]{:S(2)}) collective-permute-start(bf16[8,2,128,128]{3,2,1,0:T(8,128)(2,1)} %get-tuple-element.47), channel_id=1, source_target_pairs={{0,16},{8,24},{16,0},{24,8},{1,17},{9,25},{17,1},{25,9},{2,18},{10... | collective-permute-start | bytes 1572872 | tf_op jit(solution)/shard_map/ppermute | solution.py:409
  200.3 46.1 %collective-permute-start.2 = (bf16[8,2,128,128]{3,2,1,0:T(8,128)(2,1)}, bf16[8,2,128,128]{3,2,1,0:T(8,128)(2,1)S(1)}, u32[]{:S(2)}, u32[]{:S(2)}) collective-permute-start(bf16[8,2,128,128]{3,2,1,0:T(8,128)(2,1)} %get-tuple-element.48), channel_id=1, source_target_pairs={{0,24},{8,0},{16,8},{24,16},{1,25},{9,1},{17,9},{25,17},{2,26},{10... | collective-permute-start | bytes 1572872 | tf_op jit(solution)/shard_map/ppermute | solution.py:409
  201.3 54.3 %collective-permute-start.9 = (bf16[8,2,128,128]{3,2,1,0:T(8,128)(2,1)}, bf16[8,2,128,128]{3,2,1,0:T(8,128)(2,1)S(1)}, u32[]{:S(2)}, u32[]{:S(2)}) collective-permute-start(bf16[8,2,128,128]{3,2,1,0:T(8,128)(2,1)} %get-tuple-element.60), channel_id=1, source_target_pairs={{0,8},{8,16},{16,24},{24,0},{1,9},{9,17},{17,25},{25,1},{2,10},{10... | collective-permute-start | bytes 1572872 | tf_op jit(solution)/shard_map/ppermute | solution.py:409
  235.4 10.9 %copy-start.17 = (bf16[8,2,128,128]{3,2,1,0:T(8,128)(2,1)}, bf16[8,2,128,128]{3,2,1,0:T(8,128)(2,1)S(1)}, u32[]{:S(2)}) copy-start(bf16[8,2,128,128]{3,2,1,0:T(8,128)(2,1)S(1)} %collective-permute-done.1.refs_7_.refs_2_) | copy-start | bytes 1572868
  246.4 0.8 copy-start.18
  255.6 0.8 copy-start.9
  261.1 5.2 %copy-start.21 = (bf16[8,2,128,128]{3,2,1,0:T(8,128)(2,1)S(1)}, bf16[8,2,128,128]{3,2,1,0:T(8,128)(2,1)}, u32[]{:S(2)}) copy-start(bf16[8,2,128,128]{3,2,1,0:T(8,128)(2,1)} %get-tuple-element.62) | copy-start | bytes 1572868
  261.2 1.4 copy-start.3
  262.5 56.4 %all-to-all-start.8 = ((bf16[8,2,16,32,128]{4,3,2,1,0:T(8,128)(2,1)}), bf16[8,2,16,32,128]{4,3,2,1,0:T(8,128)(2,1)S(1)}, u32[]{:S(2)}, u32[]{:S(2)}) async-start(bf16[8,2,16,32,128]{4,3,2,1,0:T(8,128)(2,1)} %row_transform.6), calls=%async_computation.8 | async-start | bytes 4194304 | tf_op jit(solution)/shard_map/all_to_all | solution.py:376
  266.4 35.2 %collective-permute-start.10 = (bf16[8,2,128,128]{3,2,1,0:T(8,128)(2,1)}, bf16[8,2,128,128]{3,2,1,0:T(8,128)(2,1)S(1)}, u32[]{:S(2)}, u32[]{:S(2)}) collective-permute-start(bf16[8,2,128,128]{3,2,1,0:T(8,128)(2,1)} %get-tuple-element.61), channel_id=1, source_target_pairs={{0,16},{8,24},{16,0},{24,8},{1,17},{9,25},{17,1},{25,9},{2,18},{10... | collective-permute-start | bytes 1572872 | tf_op jit(solution)/shard_map/ppermute | solution.py:409
  266.4 46.2 %collective-permute-start.11 = (bf16[8,2,128,128]{3,2,1,0:T(8,128)(2,1)S(1)}, bf16[8,2,128,128]{3,2,1,0:T(8,128)(2,1)S(1)}, u32[]{:S(2)}, u32[]{:S(2)}) collective-permute-start(bf16[8,2,128,128]{3,2,1,0:T(8,128)(2,1)S(1)} %copy-done.21), channel_id=1, source_target_pairs={{0,24},{8,0},{16,8},{24,16},{1,25},{9,1},{17,9},{25,17},{2,26},{10... | collective-permute-start | bytes 1572872 | tf_op jit(solution)/shard_map/ppermute | solution.py:409
  267.5 45.1 %collective-permute-start.3 = (bf16[8,2,128,128]{3,2,1,0:T(8,128)(2,1)}, bf16[8,2,128,128]{3,2,1,0:T(8,128)(2,1)S(1)}, u32[]{:S(2)}, u32[]{:S(2)}) collective-permute-start(bf16[8,2,128,128]{3,2,1,0:T(8,128)(2,1)} %get-tuple-element.50), channel_id=1, source_target_pairs={{0,8},{8,16},{16,24},{24,0},{1,9},{9,17},{17,25},{25,1},{2,10},{10... | collective-permute-start | bytes 1572872 | tf_op jit(solution)/shard_map/ppermute | solution.py:409
  301.5 11.1 %copy-start.13 = (bf16[8,2,128,128]{3,2,1,0:T(8,128)(2,1)}, bf16[8,2,128,128]{3,2,1,0:T(8,128)(2,1)S(1)}, u32[]{:S(2)}) copy-start(bf16[8,2,128,128]{3,2,1,0:T(8,128)(2,1)S(1)} %collective-permute-done.10.refs_2_) | copy-start | bytes 1572868
  312.5 0.8 copy-start.14
  313.4 0.8 copy-start.6
  318.9 5.8 %copy-start.23 = (bf16[8,2,128,128]{3,2,1,0:T(8,128)(2,1)S(1)}, bf16[8,2,128,128]{3,2,1,0:T(8,128)(2,1)}, u32[]{:S(2)}) copy-start(bf16[8,2,128,128]{3,2,1,0:T(8,128)(2,1)} %get-tuple-element.51) | copy-start | bytes 1572868
  318.9 5.8 %copy-start.22 = (bf16[8,2,128,128]{3,2,1,0:T(8,128)(2,1)S(1)}, bf16[8,2,128,128]{3,2,1,0:T(8,128)(2,1)}, u32[]{:S(2)}) copy-start(bf16[8,2,128,128]{3,2,1,0:T(8,128)(2,1)} %get-tuple-element.52) | copy-start | bytes 1572868
  318.9 1.4 copy-start.1
  320.3 46.6 %all-to-all-start.7 = ((bf16[8,2,16,32,128]{4,3,2,1,0:T(8,128)(2,1)}), bf16[8,2,16,32,128]{4,3,2,1,0:T(8,128)(2,1)}, u32[]{:S(2)}, u32[]{:S(2)}) async-start(bf16[8,2,16,32,128]{4,3,2,1,0:T(8,128)(2,1)} %row_transform.5), calls=%async_computation.7 | async-start | bytes 4194304 | tf_op jit(solution)/shard_map/all_to_all | solution.py:376
  324.7 34.5 %collective-permute-start.4 = (bf16[8,2,128,128]{3,2,1,0:T(8,128)(2,1)S(1)}, bf16[8,2,128,128]{3,2,1,0:T(8,128)(2,1)S(1)}, u32[]{:S(2)}, u32[]{:S(2)}) collective-permute-start(bf16[8,2,128,128]{3,2,1,0:T(8,128)(2,1)S(1)} %copy-done.23), channel_id=1, source_target_pairs={{0,16},{8,24},{16,0},{24,8},{1,17},{9,25},{17,1},{25,9},{2,18},{10... | collective-permute-start | bytes 1572872 | tf_op jit(solution)/shard_map/ppermute | solution.py:409
  324.8 36.5 %collective-permute-start.5 = (bf16[8,2,128,128]{3,2,1,0:T(8,128)(2,1)S(1)}, bf16[8,2,128,128]{3,2,1,0:T(8,128)(2,1)S(1)}, u32[]{:S(2)}, u32[]{:S(2)}) collective-permute-start(bf16[8,2,128,128]{3,2,1,0:T(8,128)(2,1)S(1)} %copy-done.22), channel_id=1, source_target_pairs={{0,24},{8,0},{16,8},{24,16},{1,25},{9,1},{17,9},{25,17},{2,26},{10... | collective-permute-start | bytes 1572872 | tf_op jit(solution)/shard_map/ppermute | solution.py:409
  359.1 2.1 copy-start.15
  361.2 0.8 copy-start.16
  366.9 30.5 %all-to-all-start.4 = ((bf16[8,2,16,32,128]{4,3,2,1,0:T(8,128)(2,1)}), bf16[8,2,16,32,128]{4,3,2,1,0:T(8,128)(2,1)S(1)}, u32[]{:S(2)}, u32[]{:S(2)}) async-start(bf16[8,2,16,32,128]{4,3,2,1,0:T(8,128)(2,1)} %row_transform.4), calls=%async_computation.4 | async-start | bytes 4194304 | tf_op jit(solution)/shard_map/all_to_all | solution.py:376
  397.4 1.4 copy-start.2

commit v5 on v4

--- a/solution.py
+++ b/solution.py
@@ -11,7 +11,6 @@
 
 LANES = 128
 RADIX = 8
-PARTS = 2
 VMEM_BYTES = 56 * 1024 * 1024
 
 
@@ -87,8 +86,11 @@
     return out_r, out_i
 
 
-def column_kernel(held, x_ref, twiddle_ref, table_ref, *refs):
-    *out_refs, mid = refs[held:]
+def column_kernel(groups, x_ref, twiddle_ref, table_ref, *refs):
+    *out_refs, mid = refs
+    if len(out_refs) > len(groups):
+        basis_ref, *out_refs, copy_ref = out_refs
+        copy_ref[...] = basis_ref[...]
     rows, length = x_ref.shape[1:]
     inner = length // RADIX
     step = 16
@@ -113,78 +115,74 @@
                     ti = re[y_lo] * sine + im[y_lo] * cosine
                 mid[y_lo, at, lanes] = tr.astype(jnp.bfloat16)
                 mid[y_lo, at, other] = ti.astype(jnp.bfloat16)
-    groups = out_refs[0].shape[0] // RADIX
-    for part in range(2):
-        for block in range(0, inner // LANES, 2):
-            start = part * inner + block * LANES
-            pair = min(2, inner // LANES - block)
-            wide = jnp.dot(
-                mid[...].reshape(RADIX * rows, 2 * inner),
-                table_ref[:, start : start + pair * LANES],
-                preferred_element_type=jnp.float32,
-            ).astype(jnp.bfloat16)
-            for k in range(pair):
-                chunk, group = divmod(block + k, groups)
-                for y_lo in range(RADIX):
-                    out_refs[chunk][group * RADIX + y_lo, part] = wide[
-                        y_lo * rows : (y_lo + 1) * rows, k * LANES : (k + 1) * LANES
-                    ]
-
-
-def column_transform(x, pieces, share, held):
+    spread = out_refs[0].shape[0] // RADIX
+    wanted = []
+    for out_ref, chunks in zip(out_refs, groups):
+        for place_at, chunk in enumerate(chunks):
+            for group in range(spread):
+                for part in range(2):
+                    column = part * inner + (chunk * spread + group) * LANES
+                    wanted.append((column, out_ref, group * RADIX, part, place_at * LANES))
+    for first in range(0, len(wanted), 2):
+        pair = wanted[first : first + 2]
+        table = jnp.concatenate([table_ref[:, item[0] : item[0] + LANES] for item in pair], axis=1)
+        wide = jnp.dot(
+            mid[...].reshape(RADIX * rows, 2 * inner), table, preferred_element_type=jnp.float32
+        ).astype(jnp.bfloat16)
+        for k, (_, out_ref, piece, part, lane) in enumerate(pair):
+            for y_lo in range(RADIX):
+                out_ref[piece + y_lo, part, :, lane : lane + LANES] = wide[
+                    y_lo * rows : (y_lo + 1) * rows, k * LANES : (k + 1) * LANES
+                ]
+
+
+def column_transform(x, pieces, groups, passed):
     _, rows, length = x.shape
     inner = length // RADIX
-    count = length // pieces // LANES
-    own = rows // PARTS
-    block = math.gcd(own, 64)
-    first = share * (own // block)
-    kept = pl.BlockSpec((pieces, 2, block, LANES), lambda i: (0, 0, i + first, 0))
+    block = math.gcd(rows, 64)
+    lanes = [len(chunks) * LANES for chunks in groups]
+    kept = [pl.BlockSpec(a.shape, lambda i: (0, 0)) for a in passed]
     return pl.pallas_call(
-        functools.partial(column_kernel, len(held)),
-        grid=(own // block,),
+        functools.partial(column_kernel, groups),
+        grid=(rows // block,),
         in_specs=[
-            pl.BlockSpec((2, block, length), lambda i: (0, i + first, 0)),
+            pl.BlockSpec((2, block, length), lambda i: (0, i, 0)),
             pl.BlockSpec((RADIX, 2, inner), lambda i: (0, 0, 0)),
             pl.BlockSpec((2 * inner, 2 * inner), lambda i: (0, 0)),
         ]
-        + [pl.BlockSpec(memory_space=pl.ANY)] * len(held),
-        out_specs=[pl.BlockSpec((pieces, 2, block, LANES), lambda i: (0, 0, i, 0))]
-        + [kept] * (count - 1),
-        out_shape=[jax.ShapeDtypeStruct((pieces, 2, own, LANES), jnp.bfloat16)]
-        + [jax.ShapeDtypeStruct((pieces, 2, rows, LANES), jnp.bfloat16)] * (count - 1),
+        + kept,
+        out_specs=[pl.BlockSpec((pieces, 2, block, n), lambda i: (0, 0, i, 0)) for n in lanes] + kept,
+        out_shape=[jax.ShapeDtypeStruct((pieces, 2, rows, n), jnp.bfloat16) for n in lanes]
+        + [jax.ShapeDtypeStruct(a.shape, a.dtype) for a in passed],
         scratch_shapes=[pltpu.VMEM((RADIX, block, 2 * inner), jnp.bfloat16)],
-        input_output_aliases={3 + i: 1 + i for i in range(len(held))},
         compiler_params=params(),
         cost_estimate=pl.CostEstimate(
-            flops=16 * own * length * inner, bytes_accessed=8 * own * length, transcendentals=0
+            flops=4 * rows * length * sum(lanes), bytes_accessed=8 * rows * length, transcendentals=0
         ),
         name="column_transform",
-    )(x, jnp.asarray(twiddle_table(length)), jnp.asarray(inner_table(inner)), *held)
-
-
-def clean_kernel(count, after, later, at_ref, *refs):
-    x_refs, refs = refs[:count], refs[count:]
-    basis_ref, basis_t_ref, gain_ref, swap_ref, back_ref = refs[:5]
-    *out_refs, slab = refs[5 + after + later :]
+    )(x, jnp.asarray(twiddle_table(length)), jnp.asarray(inner_table(inner)), *passed)
+
+
+def clean_kernel(after, later, at_ref, x_ref, basis_ref, basis_t_ref, gain_ref, swap_ref, back_ref, *refs):
+    *out_refs, slab = refs[after + later :]
     out_refs = out_refs[: len(out_refs) - later]
     chans = slab.shape[0]
     rows_dev = slab.shape[1] // LANES
     tall = swap_ref.shape[0]
     group = tall // rows_dev
     begin = 0
-    for source in range(x_refs[0].shape[0]):
-        for x_ref in x_refs:
-            for row in range(0, x_ref.shape[2], tall):
-                turned = jnp.dot(
-                    swap_ref[...],
-                    x_ref[source, 0, row : row + tall, :],
-                    preferred_element_type=jnp.float32,
-                ).astype(jnp.bfloat16)
-                for u in range(rows_dev):
-                    slab[begin : begin + group, u * LANES : (u + 1) * LANES] = turned[
-                        u * group : (u + 1) * group
-                    ]
-                begin += group
+    for source in range(x_ref.shape[0]):
+        for row in range(0, x_ref.shape[2], tall):
+            turned = jnp.dot(
+                swap_ref[...],
+                x_ref[source, 0, row : row + tall, :],
+                preferred_element_type=jnp.float32,
+            ).astype(jnp.bfloat16)
+            for u in range(rows_dev):
+                slab[begin : begin + group, u * LANES : (u + 1) * LANES] = turned[
+                    u * group : (u + 1) * group
+                ]
+            begin += group
     pair = math.gcd(rows_dev, 2)
     for first in range(0, rows_dev, pair):
         lanes = slice(first * LANES, (first + pair) * LANES)
@@ -200,6 +198,9 @@
         ).astype(jnp.bfloat16)
         drop = jnp.dot(basis_ref[...], front, preferred_element_type=jnp.float32)
         slab[:, lanes] = (line.astype(jnp.float32) - drop).astype(jnp.bfloat16)
+    if len(out_refs) == 1 and len(out_refs[0].shape) == 5:
+        joined = out_refs[0]
+        out_refs = [joined.at[:, step] for step in range(joined.shape[1])]
     steps = len(out_refs)
     share = chans // steps
     out_rows = out_refs[0].shape[2]
@@ -223,42 +224,45 @@
                 ).astype(jnp.bfloat16)
 
 
-def clean(at, xs, basis, basis_t, gain, steps, targets, rows_dev, after, later):
-    sources = xs[0].shape[0]
+def clean(at, x, tile, basis, basis_t, gain, steps, targets, rows_dev, joined, after, later):
+    sources = x.shape[0]
     chans = basis.shape[0]
-    own = chans // sources // len(xs)
+    own = chans // sources
     swap = swap_table(min(256 // rows_dev, own), rows_dev)
     back = np.ascontiguousarray(swap_table(256 // rows_dev, rows_dev).T)
     out_rows = chans * rows_dev // (targets * steps)
     whole = lambda s, at: (0, 0)
-    waits = [pl.BlockSpec(memory_space=pl.ANY)] * (len(after) + len(later))
-    first_later = 1 + len(xs) + 5 + len(after)
-    return pl.pallas_call(
-        functools.partial(clean_kernel, len(xs), len(after), len(later)),
+    untouched = pl.BlockSpec(memory_space=pl.ANY)
+    if joined:
+        out_specs = [
+            pl.BlockSpec((targets, steps, 1, out_rows, LANES), lambda s, at: (0, 0, s, 0, 0))
+        ]
+        out_shape = [jax.ShapeDtypeStruct((targets, steps, 2, out_rows, LANES), jnp.bfloat16)]
+    else:
+        out_specs = [
+            pl.BlockSpec((targets, 1, out_rows, LANES), lambda s, at: (0, s, 0, 0))
+        ] * steps
+        out_shape = [jax.ShapeDtypeStruct((targets, 2, out_rows, LANES), jnp.bfloat16)] * steps
+    aliases = {7 + len(after) + i: len(out_shape) + i for i in range(len(later))}
+    result = pl.pallas_call(
+        functools.partial(clean_kernel, len(after), len(later)),
         grid_spec=pltpu.PrefetchScalarGridSpec(
             num_scalar_prefetch=1,
             grid=(2,),
             in_specs=[
-                pl.BlockSpec((sources, 1, own * rows_dev, LANES), lambda s, at: (0, s, 0, 0))
-                for x in xs
-            ]
-            + [
+                pl.BlockSpec((sources, 1, own * rows_dev, LANES), lambda s, at: (0, s, 0, tile)),
                 pl.BlockSpec(basis.shape, whole),
                 pl.BlockSpec(basis.shape, whole),
                 pl.BlockSpec(gain.shape, whole),
                 pl.BlockSpec(swap.shape, whole),
                 pl.BlockSpec(back.shape, whole),
             ]
-            + waits,
-            out_specs=[
-                pl.BlockSpec((targets, 1, out_rows, LANES), lambda s, at: (0, s, 0, 0))
-            ] * steps
-            + [pl.BlockSpec(memory_space=pl.ANY)] * len(later),
+            + [untouched] * (len(after) + len(later)),
+            out_specs=out_specs + [untouched] * len(later),
             scratch_shapes=[pltpu.VMEM((chans, rows_dev * LANES), jnp.bfloat16)],
         ),
-        out_shape=[jax.ShapeDtypeStruct((targets, 2, out_rows, LANES), jnp.bfloat16)] * steps
-        + [jax.ShapeDtypeStruct(a.shape, a.dtype) for a in later],
-        input_output_aliases={first_later + i: steps + i for i in range(len(later))},
+        out_shape=out_shape + [jax.ShapeDtypeStruct(a.shape, a.dtype) for a in later],
+        input_output_aliases=aliases,
         compiler_params=params(),
         cost_estimate=pl.CostEstimate(
             flops=12 * chans * chans * rows_dev * LANES,
@@ -266,7 +270,8 @@
             transcendentals=0,
         ),
         name="clean",
-    )(at, *xs, basis, basis_t, gain, jnp.asarray(swap), jnp.asarray(back), *after, *later)
+    )(at, x, basis, basis_t, gain, jnp.asarray(swap), jnp.asarray(back), *after, *later)
+    return result[: len(out_shape)], result[len(out_shape) :]
 
 
 def row_kernel(scale, group, steps, *refs):
@@ -354,26 +359,63 @@
     )(x, jnp.asarray(table), *held)
 
 
-def turn_kernel(later, basis_ref, *refs):
-    out_ref = refs[-1 - later]
-    out_ref[...] = basis_ref[...].T
-
-
-def turn(basis, after, later):
+def gather_kernel(at_ref, *refs):
+    *block_refs, basis_ref, turned_ref = refs
+    count = len(block_refs)
+    rows = block_refs[0].shape[0]
+    for step, block_ref in enumerate(block_refs):
+        owner = lax.rem(at_ref[0] - step + count, count)
+        basis_ref[pl.ds(pl.multiple_of(owner * rows, rows), rows), :] = block_ref[...]
+    turned_ref[...] = basis_ref[...].T
+
+
+def gather(block):
+    count = lax.axis_size("chan")
+    blocks = [block] + [
+        lax.ppermute(block, "chan", [(j, (j + step) % count) for j in range(count)])
+        for step in range(1, count)
+    ]
+    rows, modes = block.shape
+    vmem = pl.BlockSpec(memory_space=pltpu.VMEM)
+    return pl.pallas_call(
+        gather_kernel,
+        in_specs=[pl.BlockSpec(memory_space=pltpu.SMEM)] + [vmem] * count,
+        out_specs=[vmem] * 2,
+        out_shape=[
+            jax.ShapeDtypeStruct((count * rows, modes), block.dtype),
+            jax.ShapeDtypeStruct((modes, count * rows), block.dtype),
+        ],
+        compiler_params=params(),
+        name="gather",
+    )(lax.axis_index("chan").astype(jnp.int32).reshape(1), *blocks)
+
+
+def hold_kernel(*refs):
+    pass
+
+
+def hold(x, after):
     untouched = pl.BlockSpec(memory_space=pl.ANY)
     return pl.pallas_call(
-        functools.partial(turn_kernel, len(later)),
-        in_specs=[pl.BlockSpec(memory_space=pltpu.VMEM)] + [untouched] * (len(after) + len(later)),
-        out_specs=[pl.BlockSpec(memory_space=pltpu.VMEM)] + [untouched] * len(later),
-        out_shape=[jax.ShapeDtypeStruct(a.shape, a.dtype) for a in (basis, *later)],
-        input_output_aliases={1 + len(after) + i: 1 + i for i in range(len(later))},
-        compiler_params=params(),
-        name="turn",
-    )(basis, *after, *later)
+        hold_kernel,
+        in_specs=[untouched] * (1 + len(after)),
+        out_specs=untouched,
+        out_shape=jax.ShapeDtypeStruct(x.shape, x.dtype),
+        input_output_aliases={0: 0},
+        name="hold",
+    )(x, *after)
 
 
 def exchange(x):
     return lax.all_to_all(x, "chan", split_axis=0, concat_axis=0, tiled=True)
+
+
+def spread_rows(parts):
+    count = len(parts)
+    return [parts[0]] + [
+        lax.ppermute(parts[step], "uv", [(z, (z + step) % count) for z in range(count)])
+        for step in range(1, count)
+    ]
 
 
 def shards(visibility, eigen_basis, eigenvalues, noise_power):
@@ -383,42 +425,61 @@
     count = length // chan_count // LANES
     out_chans = chans // uv_count
     at = lax.axis_index("uv").astype(jnp.int32).reshape(1)
-    basis = exchange(jnp.broadcast_to(eigen_basis, (chan_count,) + eigen_basis.shape))
-    basis = basis.reshape(chan_count * chans, -1)
     gain = eigenvalues[:, None] / (eigenvalues[:, None] + noise_power[None, :])
     flat = visibility.reshape(2, chans * rows_dev, length)
-    firsts, chunks = [], []
-    for share in range(PARTS):
-        first, *chunks = column_transform(flat, chan_count, share, chunks)
-        firsts.append(exchange(first))
-    basis_t, *chunks = turn(basis, firsts[:1], chunks)
-    cells = [firsts] + [[exchange(chunk)] for chunk in chunks[:1]]
-    chunks = chunks[1:]
-    pieces, lines, held = [], [], []
+    groups = [g for g in ([1], list(range(2, count))) if g and g[-1] < count]
+    first, block = column_transform(flat, chan_count, [[0]], [eigen_basis])
+    cells = [exchange(first)]
+    basis, basis_t = gather(block)
+    sends = column_transform(flat, chan_count, groups, []) if groups else []
+    cells += [exchange(send) for send in sends[:1]]
+    sends = sends[1:]
+
+    pieces, returned = {}, {}
     for k in range(count):
-        after = pieces[k - 2][1:] if k >= 2 else []
-        later = chunks[:1]
-        chunks = chunks[1:]
-        result = clean(
-            at, cells[k], basis, basis_t, gain, uv_count, chan_count, rows_dev, after, later
+        last = k == count - 1 and count > 1
+        after = [pieces[k - 1][1]] if k else []
+        results, passed = clean(
+            at,
+            cells[min(k, 2)],
+            max(k - 2, 0),
+            basis,
+            basis_t,
+            gain,
+            uv_count,
+            chan_count,
+            rows_dev,
+            last,
+            after,
+            sends,
         )
-        cells += [[exchange(chunk)] for chunk in result[uv_count:]]
-        pieces.append(
-            [result[0]]
-            + [
-                lax.ppermute(
-                    result[step], "uv", [(z, (z + step) % uv_count) for z in range(uv_count)]
-                )
-                for step in range(1, uv_count)
-            ]
-        )
-    for k in range(count):
-        after = [parts[0] for parts in pieces[k + 2 : k + 3]]
-        after += [parts[1] for parts in pieces[k + 1 : k + 2]]
-        if k == 0:
-            after += cells[-1]
-        lines = row_transform(pieces[k], at, out_chans, rows_dev, length, after)
-        held = [place(exchange(lines), k, count, held)]
+        cells += [exchange(send) for send in passed]
+        sends = []
+        if not last:
+            pieces[k] = spread_rows(results)
+        else:
+            joined = results[0]
+    transform = lambda k, after: row_transform(pieces[k], at, out_chans, rows_dev, length, after)
+    following = lambda k: [pieces[k + 1][1]] if k + 1 in pieces else []
+    if count == 1:
+        returned[0] = exchange(transform(0, []))
+    else:
+        first_lines = transform(0, following(0))
+        returned[0] = exchange(hold(first_lines, cells[-1:]))
+        joined = exchange(hold(joined, [returned[0]]))
+        middle = {k: transform(k, following(k)) for k in range(1, count - 1)}
+        pieces[count - 1] = spread_rows([joined[:, step] for step in range(uv_count)])
+        before = joined
+        for k in range(1, count - 1):
+            returned[k] = exchange(hold(middle[k], [before]))
+            before = returned[k]
+        returned[count - 1] = transform(count - 1, [])
+    order = list(range(count))
+    if count > 2:
+        order = order[:-2] + [count - 1, count - 2]
+    held = []
+    for k in order:
+        held = [place(returned[k], k, count, held)]
     return held[0]
 
 

time: 406 us -> 375 us (0.924)
  waiting for transfers between devices: 238 us -> 196 us
  Pallas kernels: 98.5 us -> 106 us
    all_to_all x10 -> x7, waiting for transfers between devices: 62.9 us -> 11.1 us  [exchange(): return lax.all_to_all(x, 'chan', split_axis=0, concat_axis=0, tiled=True)]
    ppermute x12 -> x19, starting transfers between devices: 12.2 us -> 25.8 us  [the longest x12 18.5 us: spread_rows(): lax.ppermute(parts[step], 'uv', [(z, (z + step) % count) for z in range(c...]
    all_to_all x10 -> x7, starting transfers between devices: 38.3 us -> 28.2 us  [exchange(): return lax.all_to_all(x, 'chan', split_axis=0, concat_axis=0, tiled=True)]
    ppermute x12 -> x19, waiting for transfers between devices: 175 us -> 185 us  [the longest x12 160 us: spread_rows(): lax.ppermute(parts[step], 'uv', [(z, (z + step) % count) for z in range(c...]
    pallas_call x7 -> x11, Pallas kernels: 55.3 us -> 62.8 us  [the longest x4 33.3 us: clean(): pl.pallas_call(functools.partial(clean_kernel, len(after), len(later)), g...]
    unnamed x48 -> x68, local copies, waits for them, and re-layouts: 13.2 us -> 12.6 us
  transfers between devices with their start and end apart: 22 -> 26, of which waited for: 14 -> 14; matrix products, arithmetic and copies ran while one was open for 1% -> 1% of each run, Pallas kernels for 22% -> 24%
where the time goes in v5:
time: 375 us; the launch traced here: 372 us
  waiting for transfers between devices  196 us (52%)
  Pallas kernels  106 us (28%)
  starting transfers between devices  54 us (14%)
  local copies, waits for them, and re-layouts  15.1 us (4%)
    ppermute x12, waiting for transfers between devices, spread_rows(): lax.ppermute(parts[step], 'uv', [(z, (z + step) % count) for z in range(c...  160 us
    pallas_call x4, Pallas kernels, clean(): pl.pallas_call(functools.partial(clean_kernel, len(after), len(later)), g...  33.3 us
    all_to_all x7, starting transfers between devices, exchange(): return lax.all_to_all(x, 'chan', split_axis=0, concat_axis=0, tiled=True)  28.2 us
    pallas_call x2, Pallas kernels, column_transform(): pl.pallas_call(functools.partial(column_kernel, groups), grid=(rows // bl...  27.4 us
    ppermute x7, waiting for transfers between devices, gather(): lax.ppermute(block, 'chan', [(j, (j + step) % count) for j in range(count)])  24.9 us
    pallas_call x4, Pallas kernels, place(): pl.pallas_call(place_kernel, grid=(chans // block, groups), in_specs=[pl....  24.1 us
    pallas_call x4, Pallas kernels, row_transform(): pl.pallas_call(functools.partial(row_kernel, scale, group, steps), grid=(...  19.1 us
    ppermute x12, starting transfers between devices, spread_rows(): lax.ppermute(parts[step], 'uv', [(z, (z + step) % count) for z in range(c...  18.5 us
  transfers between devices with their start and end apart: 26, of which 14 were waited for; matrix products, arithmetic and copies ran while one was open for 1% of the time, Pallas kernels for 24%

profile of v5, /device:TPU:8, one launch (start us, length us, event | category | flops | bytes accessed | tf_op | source)
XLA Modules:
  0.0 371.7 jit_solution(12851823293790387337)
XLA Ops:
  0.0 11.9 %column_transform.2 = (bf16[8,2,512,128]{3,2,1,0:T(8,128)(2,1)}, bf16[64,512]{1,0:T(8,128)(2,1)}) custom-call(bf16[2,512,4096]{2,1,0:T(8,128)(2,1)} %bitcast.21, f32[8,2,512]{2,1,0:T(2,128)} %constant.32.clone.twiddle_ref, bf16[1024,1024]{1,0:T(8,128)(2,1)} %constant.33.clone.table_ref, bf16[64,512]{1,0:T(8,128)(2,1)} %refs_0_.1), custom_call_target="tpu_custom_call" | custom-call | flops 1073741824 | bytes 16777216 | tf_op jit(solution)/shard_map/column_transform/pallas_call | solution.py:145
  11.9 3.7 %all-to-all-start = ((bf16[8,2,512,128]{3,2,1,0:T(8,128)(2,1)}), bf16[8,2,512,128]{3,2,1,0:T(8,128)(2,1)S(1)}, u32[]{:S(2)}, u32[]{:S(2)}) async-start(bf16[8,2,512,128]{3,2,1,0:T(8,128)(2,1)} %get-tuple-element.24), calls=%async_computation | async-start | bytes 4194304 | tf_op jit(solution)/shard_map/all_to_all | solution.py:410
  15.6 15.5 %column_transform.3 = (bf16[8,2,512,128]{3,2,1,0:T(8,128)(2,1)}, bf16[8,2,512,256]{3,2,1,0:T(8,128)(2,1)}) custom-call(bf16[2,512,4096]{2,1,0:T(8,128)(2,1)} %bitcast.22, f32[8,2,512]{2,1,0:T(2,128)} %constant.32.clone.twiddle_ref, bf16[1024,1024]{1,0:T(8,128)(2,1)} %constant.33.clone.table_ref), custom_call_target="tpu_custom_call" | custom-call | flops 3221225472 | bytes 16777216 | tf_op jit(solution)/shard_map/column_transform/pallas_call | solution.py:145
  31.2 11.1 %all-to-all-done.x_ref = bf16[8,2,512,128]{3,2,1,0:T(8,128)(2,1)S(1)} async-done(((bf16[8,2,512,128]{3,2,1,0:T(8,128)(2,1)}), bf16[8,2,512,128]{3,2,1,0:T(8,128)(2,1)S(1)}, u32[]{:S(2)}, u32[]{:S(2)}) %all-to-all-start) | async-done | bytes 2097184 | tf_op jit(solution)/shard_map/all_to_all | solution.py:410
  42.3 1.3 copy-done.7
  43.6 3.6 all-to-all-start.2
  47.2 2.6 collective-permute-start.6
  50.5 1.5 collective-permute-start.3
  52.2 20.3 %collective-permute-done.6.refs_7_ = bf16[64,512]{1,0:T(8,128)(2,1)S(1)} collective-permute-done((bf16[64,512]{1,0:T(8,128)(2,1)S(1)}, bf16[64,512]{1,0:T(8,128)(2,1)S(1)}, u32[]{:S(2)}, u32[]{:S(2)}) %collective-permute-start.6) | collective-permute-done | bytes 65568 | tf_op jit(solution)/shard_map/ppermute | solution.py:375
  72.5 1.9 collective-permute-start.1
  74.4 1.4 collective-permute-done.5.refs_6_
  78.1 2.3 collective-permute-done.refs_1_
  81.0 2.1 gather.1
  83.0 8.3 %clean.4 = (bf16[8,2,128,128]{3,2,1,0:T(8,128)(2,1)}, bf16[8,2,128,128]{3,2,1,0:T(8,128)(2,1)}, bf16[8,2,128,128]{3,2,1,0:T(8,128)(2,1)}, bf16[8,2,128,128]{3,2,1,0:T(8,128)(2,1)}, bf16[8,2,512,256]{3,2,1,0:T(8,128)(2,1)}) custom-call(s32[1]{0:T(128)} %bitcast.at_ref, bf16[8,2,512,128]{3,2,1,0:T(8,128)(2,1)} %copy-done.7, ...), custom_call_target="tpu_custom_call", output_to_operand_aliasing={{4}: (7, {})} | custom-call | flops 3221225472 | bytes 4194304 | tf_op jit(solution)/shard_map/clean/pallas_call | solution.py:247
  92.7 4.6 %all-to-all-start.1 = ((bf16[8,2,512,256]{3,2,1,0:T(8,128)(2,1)}), bf16[8,2,512,256]{3,2,1,0:T(8,128)(2,1)}, u32[]{:S(2)}, u32[]{:S(2)}) async-start(bf16[8,2,512,256]{3,2,1,0:T(8,128)(2,1)} %get-tuple-element.29), calls=%async_computation.1 | async-start | bytes 8388608 | tf_op jit(solution)/shard_map/all_to_all | solution.py:410
  97.3 1.6 collective-permute-start.7
  100.2 1.8 collective-permute-start.15
  102.0 31.3 %collective-permute-done.7.refs_0_.refs_1_ = bf16[8,2,128,128]{3,2,1,0:T(8,128)(2,1)S(1)} collective-permute-done((bf16[8,2,128,128]{3,2,1,0:T(8,128)(2,1)S(1)}, bf16[8,2,128,128]{3,2,1,0:T(8,128)(2,1)S(1)}, u32[]{:S(2)}, u32[]{:S(2)}) %collective-permute-start.7) | collective-permute-done | bytes 524320 | tf_op jit(solution)/shard_map/ppermute | solution.py:416
  134.1 8.3 %clean.5 = (bf16[8,2,128,128]{3,2,1,0:T(8,128)(2,1)}, bf16[8,2,128,128]{3,2,1,0:T(8,128)(2,1)}, bf16[8,2,128,128]{3,2,1,0:T(8,128)(2,1)}, bf16[8,2,128,128]{3,2,1,0:T(8,128)(2,1)}) custom-call(s32[1]{0:T(128)} %bitcast.at_ref, bf16[8,2,512,128]{3,2,1,0:T(8,128)(2,1)} %copy-done.6, bf16[512,512]{1,0:T(8,128)(2,1)} %get-tuple-element.26.basis_ref, ...), custom_call_target="tpu_custom_call" | custom-call | flops 3221225472 | bytes 4194304 | tf_op jit(solution)/shard_map/clean/pallas_call | solution.py:247
  142.4 2.9 collective-permute-start.8
  145.4 1.6 dynamic-slice_bitcast_fusion.refs_4_
  146.9 10.4 %collective-permute-done.15.refs_3_ = bf16[8,2,128,128]{3,2,1,0:T(8,128)(2,1)S(1)} collective-permute-done((bf16[8,2,128,128]{3,2,1,0:T(8,128)(2,1)S(1)}, bf16[8,2,128,128]{3,2,1,0:T(8,128)(2,1)S(1)}, u32[]{:S(2)}, u32[]{:S(2)}) %collective-permute-start.15) | collective-permute-done | bytes 524320 | tf_op jit(solution)/shard_map/ppermute | solution.py:416
  158.3 4.8 %row_transform.6.refs_0_ = bf16[8,2,16,32,128]{4,3,2,1,0:T(8,128)(2,1)} custom-call(bf16[8,2,128,128]{3,2,1,0:T(8,128)(2,1)} %get-tuple-element.40.refs_0_, bf16[8,2,128,128]{3,2,1,0:T(8,128)(2,1)} %copy-done.8, bf16[8,2,128,128]{3,2,1,0:T(8,128)(2,1)} %copy-done.9, bf16[8,2,128,128]{3,2,1,0:T(8,128)(2,1)} %copy-done.10, ...), custom_call_target="tpu_custom_call" | custom-call | flops 536870912 | bytes 4194304 | tf_op jit(solution)/shard_map/row_transform/pallas_call | solution.py:304
  163.1 3.9 %all-to-all-start.3 = ((bf16[8,2,16,32,128]{4,3,2,1,0:T(8,128)(2,1)}), bf16[8,2,16,32,128]{4,3,2,1,0:T(8,128)(2,1)S(1)}, u32[]{:S(2)}, u32[]{:S(2)}) async-start(bf16[8,2,16,32,128]{4,3,2,1,0:T(8,128)(2,1)} %hold.4), calls=%async_computation.3 | async-start | bytes 4194304 | tf_op jit(solution)/shard_map/all_to_all | solution.py:410
  167.0 8.3 %clean.6 = (bf16[8,2,128,128]{3,2,1,0:T(8,128)(2,1)}, bf16[8,2,128,128]{3,2,1,0:T(8,128)(2,1)}, bf16[8,2,128,128]{3,2,1,0:T(8,128)(2,1)}, bf16[8,2,128,128]{3,2,1,0:T(8,128)(2,1)}) custom-call(s32[1]{0:T(128)} %bitcast.at_ref, bf16[8,2,512,256]{3,2,1,0:T(8,128)(2,1)} %all-to-all-done.1.x_ref.refs_1_, bf16[512,512]{1,0:T(8,128)(2,1)} %get-tuple-element.26.basis_ref, ...), custom_call_target="tpu_custom_call" | custom-call | flops 3221225472 | bytes 4194304 | tf_op jit(solution)/shard_map/clean/pallas_call | solution.py:247
  175.9 14.0 %collective-permute-done.9.refs_1_.refs_5_.refs_0_ = bf16[8,2,128,128]{3,2,1,0:T(8,128)(2,1)S(1)} collective-permute-done((bf16[8,2,128,128]{3,2,1,0:T(8,128)(2,1)}, bf16[8,2,128,128]{3,2,1,0:T(8,128)(2,1)S(1)}, u32[]{:S(2)}, u32[]{:S(2)}) %collective-permute-start.9) | collective-permute-done | bytes 524320 | tf_op jit(solution)/shard_map/ppermute | solution.py:416
  190.7 8.3 %clean.7.refs_0_ = bf16[8,4,2,128,128]{4,3,2,1,0:T(8,128)(2,1)} custom-call(s32[1]{0:T(128)} %bitcast.at_ref, bf16[8,2,512,256]{3,2,1,0:T(8,128)(2,1)} %all-to-all-done.1.x_ref.refs_1_, bf16[512,512]{1,0:T(8,128)(2,1)} %get-tuple-element.26.basis_ref, bf16[512,512]{1,0:T(8,128)(2,1)} %get-tuple-element.27.basis_t_ref, f32[512,8]{1,0:T(8,128)} %add_divide_fusion.gain_ref, ...), custom_call_target="tpu_custom_call" | custom-call | flops 3221225472 | bytes 4194304 | tf_op jit(solution)/shard_map/clean/pallas_call | solution.py:247
  200.3 4.0 %all-to-all-start.4 = ((bf16[8,4,2,128,128]{4,3,2,1,0:T(8,128)(2,1)}), bf16[8,4,2,128,128]{4,3,2,1,0:T(8,128)(2,1)S(1)}, u32[]{:S(2)}, u32[]{:S(2)}) async-start(bf16[8,4,2,128,128]{4,3,2,1,0:T(8,128)(2,1)} %hold.5), calls=%async_computation.4 | async-start | bytes 4194304 | tf_op jit(solution)/shard_map/all_to_all | solution.py:410
  206.4 33.0 %collective-permute-done.12.refs_2_ = bf16[8,2,128,128]{3,2,1,0:T(8,128)(2,1)S(1)} collective-permute-done((bf16[8,2,128,128]{3,2,1,0:T(8,128)(2,1)S(1)}, bf16[8,2,128,128]{3,2,1,0:T(8,128)(2,1)S(1)}, u32[]{:S(2)}, u32[]{:S(2)}) %collective-permute-start.12) | collective-permute-done | bytes 524320 | tf_op jit(solution)/shard_map/ppermute | solution.py:416
  239.4 1.6 collective-permute-done.13.refs_3_
  241.8 4.7 %row_transform.5.refs_0_ = bf16[8,2,16,32,128]{4,3,2,1,0:T(8,128)(2,1)} custom-call(bf16[8,2,128,128]{3,2,1,0:T(8,128)(2,1)} %get-tuple-element.37.refs_0_, bf16[8,2,128,128]{3,2,1,0:T(8,128)(2,1)} %copy-done.4, bf16[8,2,128,128]{3,2,1,0:T(8,128)(2,1)} %copy-done.14, bf16[8,2,128,128]{3,2,1,0:T(8,128)(2,1)} %copy-done.16, ...), custom_call_target="tpu_custom_call" | custom-call | flops 536870912 | bytes 4194304 | tf_op jit(solution)/shard_map/row_transform/pallas_call | solution.py:304
  246.5 1.4 copy-done.1
  247.9 4.0 %all-to-all-start.5 = ((bf16[8,2,16,32,128]{4,3,2,1,0:T(8,128)(2,1)}), bf16[8,2,16,32,128]{4,3,2,1,0:T(8,128)(2,1)S(1)}, u32[]{:S(2)}, u32[]{:S(2)}) async-start(bf16[8,2,16,32,128]{4,3,2,1,0:T(8,128)(2,1)} %hold.6), calls=%async_computation.5 | async-start | bytes 4194304 | tf_op jit(solution)/shard_map/all_to_all | solution.py:410
  251.9 2.0 collective-permute-start.10
  253.9 32.8 %collective-permute-done.10.refs_2_ = bf16[8,2,128,128]{3,2,1,0:T(8,128)(2,1)S(1)} collective-permute-done((bf16[8,2,128,128]{3,2,1,0:T(8,128)(2,1)S(1)}, bf16[8,2,128,128]{3,2,1,0:T(8,128)(2,1)S(1)}, u32[]{:S(2)}, u32[]{:S(2)}) %collective-permute-start.10) | collective-permute-done | bytes 524320 | tf_op jit(solution)/shard_map/ppermute | solution.py:416
  287.7 4.7 %row_transform.4.refs_0_ = bf16[8,2,16,32,128]{4,3,2,1,0:T(8,128)(2,1)} custom-call(bf16[8,2,128,128]{3,2,1,0:T(8,128)(2,1)} %get-tuple-element.33.refs_0_, bf16[8,2,128,128]{3,2,1,0:T(8,128)(2,1)} %copy-done.5, bf16[8,2,128,128]{3,2,1,0:T(8,128)(2,1)} %copy-done.15, bf16[8,2,128,128]{3,2,1,0:T(8,128)(2,1)} %copy-done.17, ...), custom_call_target="tpu_custom_call" | custom-call | flops 536870912 | bytes 4194304 | tf_op jit(solution)/shard_map/row_transform/pallas_call | solution.py:304
  292.5 1.3 copy-done
  293.8 4.5 %all-to-all-start.6 = ((bf16[8,2,16,32,128]{4,3,2,1,0:T(8,128)(2,1)}), bf16[8,2,16,32,128]{4,3,2,1,0:T(8,128)(2,1)}, u32[]{:S(2)}, u32[]{:S(2)}) async-start(bf16[8,2,16,32,128]{4,3,2,1,0:T(8,128)(2,1)} %hold.7), calls=%async_computation.6 | async-start | bytes 4194304 | tf_op jit(solution)/shard_map/all_to_all | solution.py:410
  299.2 3.4 collective-permute-start.17
  302.6 2.9 collective-permute-start.16
  305.5 6.0 %place.4.refs_0_ = bf16[2,16,32,4096]{3,2,1,0:T(8,128)(2,1)} custom-call(bf16[8,2,16,32,128]{4,3,2,1,0:T(8,128)(2,1)} %copy-done.3, bf16[1024,1024]{1,0:T(8,128)(2,1)} %constant.37.clone.table_ref), custom_call_target="tpu_custom_call" | custom-call | flops 2147483648 | bytes 4194304 | tf_op jit(solution)/shard_map/place/pallas_call | solution.py:339
  311.5 2.4 collective-permute-done.18.refs_3_
  314.0 23.4 %collective-permute-done.17.refs_2_ = bf16[8,2,128,128]{3,2,1,0:T(8,128)(2,1)S(1)} collective-permute-done((bf16[8,2,128,128]{3,2,1,0:T(8,128)(2,1)S(1)}, bf16[8,2,128,128]{3,2,1,0:T(8,128)(2,1)S(1)}, u32[]{:S(2)}, u32[]{:S(2)}) %collective-permute-start.17) | collective-permute-done | bytes 524320 | tf_op jit(solution)/shard_map/ppermute | solution.py:416
  337.4 10.7 %collective-permute-done.16.refs_1_ = bf16[8,2,128,128]{3,2,1,0:T(8,128)(2,1)S(1)} collective-permute-done((bf16[8,2,128,128]{3,2,1,0:T(8,128)(2,1)S(1)}, bf16[8,2,128,128]{3,2,1,0:T(8,128)(2,1)S(1)}, u32[]{:S(2)}, u32[]{:S(2)}) %collective-permute-start.16) | collective-permute-done | bytes 524320 | tf_op jit(solution)/shard_map/ppermute | solution.py:416
  348.9 4.8 %row_transform.7.x_ref = bf16[8,2,16,32,128]{4,3,2,1,0:T(8,128)(2,1)} custom-call(bf16[8,2,128,128]{3,2,1,0:T(8,128)(2,1)} %get-tuple-element.46.refs_0_, bf16[8,2,128,128]{3,2,1,0:T(8,128)(2,1)} %copy-done.13, bf16[8,2,128,128]{3,2,1,0:T(8,128)(2,1)} %copy-done.12, bf16[8,2,128,128]{3,2,1,0:T(8,128)(2,1)} %copy-done.11, ...), custom_call_target="tpu_custom_call" | custom-call | flops 536870912 | bytes 4194304 | tf_op jit(solution)/shard_map/row_transform/pallas_call | solution.py:304
  353.7 6.0 %place.5.refs_0_ = bf16[2,16,32,4096]{3,2,1,0:T(8,128)(2,1)} custom-call(bf16[8,2,16,32,128]{4,3,2,1,0:T(8,128)(2,1)} %copy-done, bf16[1024,1024]{1,0:T(8,128)(2,1)} %constant.37.clone.table_ref, bf16[2,16,32,4096]{3,2,1,0:T(8,128)(2,1)} %place.4.refs_0_), custom_call_target="tpu_custom_call", output_to_operand_aliasing={{}: (2, {})} | custom-call | flops 2147483648 | bytes 4194304 | tf_op jit(solution)/shard_map/place/pallas_call | solution.py:339
  359.7 6.0 %place.6.refs_0_ = bf16[2,16,32,4096]{3,2,1,0:T(8,128)(2,1)} custom-call(bf16[8,2,16,32,128]{4,3,2,1,0:T(8,128)(2,1)} %row_transform.7.x_ref, bf16[1024,1024]{1,0:T(8,128)(2,1)} %constant.37.clone.table_ref, bf16[2,16,32,4096]{3,2,1,0:T(8,128)(2,1)} %place.5.refs_0_), custom_call_target="tpu_custom_call", output_to_operand_aliasing={{}: (2, {})} | custom-call | flops 2147483648 | bytes 4194304 | tf_op jit(solution)/shard_map/place/pallas_call | solution.py:339
  365.7 6.0 %place.7 = bf16[2,16,32,4096]{3,2,1,0:T(8,128)(2,1)} custom-call(bf16[8,2,16,32,128]{4,3,2,1,0:T(8,128)(2,1)} %all-to-all-done.6.x_ref, bf16[1024,1024]{1,0:T(8,128)(2,1)} %constant.37.clone.table_ref, bf16[2,16,32,4096]{3,2,1,0:T(8,128)(2,1)} %place.6.refs_0_), custom_call_target="tpu_custom_call", output_to_operand_aliasing={{}: (2, {})} | custom-call | flops 2147483648 | bytes 4194304 | tf_op jit(solution)/shard_map/place/pallas_call | solution.py:339
  (94 shorter events, 16.5 us)
Async XLA Ops:
  11.9 30.4 %all-to-all-start = ((bf16[8,2,512,128]{3,2,1,0:T(8,128)(2,1)}), bf16[8,2,512,128]{3,2,1,0:T(8,128)(2,1)S(1)}, u32[]{:S(2)}, u32[]{:S(2)}) async-start(bf16[8,2,512,128]{3,2,1,0:T(8,128)(2,1)} %get-tuple-element.24), calls=%async_computation | async-start | bytes 4194304 | tf_op jit(solution)/shard_map/all_to_all | solution.py:410
  42.3 5.0 %copy-start.18 = (bf16[64,512]{1,0:T(8,128)(2,1)S(1)}, bf16[64,512]{1,0:T(8,128)(2,1)}, u32[]{:S(2)}) copy-start(bf16[64,512]{1,0:T(8,128)(2,1)} %get-tuple-element.25.refs_0_) | copy-start | bytes 196612
  42.3 33.9 %copy-start.26 = (f32[512]{0:T(512)S(1)}, f32[512]{0:T(512)}, u32[]{:S(2)}) copy-start(f32[512]{0:T(512)} %param.26) | copy-start | bytes 6148
  42.3 33.9 %copy-start.27 = (f32[8]{0:T(128)S(1)}, f32[8]{0:T(128)}, u32[]{:S(2)}) copy-start(f32[8]{0:T(128)} %param.27) | copy-start | bytes 100
  43.6 47.8 %all-to-all-start.2 = ((bf16[8,2,512,128]{3,2,1,0:T(8,128)(2,1)}), bf16[8,2,512,128]{3,2,1,0:T(8,128)(2,1)S(1)}, u32[]{:S(2)}, u32[]{:S(2)}) async-start(bf16[8,2,512,128]{3,2,1,0:T(8,128)(2,1)} %get-tuple-element.30), calls=%async_computation.2 | async-start | bytes 4194304 | tf_op jit(solution)/shard_map/all_to_all | solution.py:410
  47.2 25.2 %collective-permute-start.6 = (bf16[64,512]{1,0:T(8,128)(2,1)S(1)}, bf16[64,512]{1,0:T(8,128)(2,1)S(1)}, u32[]{:S(2)}, u32[]{:S(2)}) collective-permute-start(bf16[64,512]{1,0:T(8,128)(2,1)S(1)} %copy-done.18), channel_id=1, source_target_pairs={{0,7},{1,0},{2,1},{3,2},{4,3},{5,4},{6,5},{7,6},{8,15},{9,8},{10,9... | collective-permute-start | bytes 196616 | tf_op jit(solution)/shard_map/ppermute | solution.py:375
  49.8 25.9 %collective-permute-start.5 = (bf16[64,512]{1,0:T(8,128)(2,1)S(1)}, bf16[64,512]{1,0:T(8,128)(2,1)S(1)}, u32[]{:S(2)}, u32[]{:S(2)}) collective-permute-start(bf16[64,512]{1,0:T(8,128)(2,1)S(1)} %copy-done.18), channel_id=1, source_target_pairs={{0,6},{1,7},{2,0},{3,1},{4,2},{5,3},{6,4},{7,5},{8,14},{9,15},{10,... | collective-permute-start | bytes 196616 | tf_op jit(solution)/shard_map/ppermute | solution.py:375
  50.4 26.6 %collective-permute-start.4 = (bf16[64,512]{1,0:T(8,128)(2,1)S(1)}, bf16[64,512]{1,0:T(8,128)(2,1)S(1)}, u32[]{:S(2)}, u32[]{:S(2)}) collective-permute-start(bf16[64,512]{1,0:T(8,128)(2,1)S(1)} %copy-done.18), channel_id=1, source_target_pairs={{0,5},{1,6},{2,7},{3,0},{4,1},{5,2},{6,3},{7,4},{8,13},{9,14},{10,... | collective-permute-start | bytes 196616 | tf_op jit(solution)/shard_map/ppermute | solution.py:375
  50.5 26.5 %collective-permute-start.3 = (bf16[64,512]{1,0:T(8,128)(2,1)S(1)}, bf16[64,512]{1,0:T(8,128)(2,1)S(1)}, u32[]{:S(2)}, u32[]{:S(2)}) collective-permute-start(bf16[64,512]{1,0:T(8,128)(2,1)S(1)} %copy-done.18), channel_id=1, source_target_pairs={{0,4},{1,5},{2,6},{3,7},{4,0},{5,1},{6,2},{7,3},{8,12},{9,13},{10,... | collective-permute-start | bytes 196616 | tf_op jit(solution)/shard_map/ppermute | solution.py:375
  52.0 25.1 %collective-permute-start.2 = (bf16[64,512]{1,0:T(8,128)(2,1)S(1)}, bf16[64,512]{1,0:T(8,128)(2,1)S(1)}, u32[]{:S(2)}, u32[]{:S(2)}) collective-permute-start(bf16[64,512]{1,0:T(8,128)(2,1)S(1)} %copy-done.18), channel_id=1, source_target_pairs={{0,3},{1,4},{2,5},{3,6},{4,7},{5,0},{6,1},{7,2},{8,11},{9,12},{10,... | collective-permute-start | bytes 196616 | tf_op jit(solution)/shard_map/ppermute | solution.py:375
  72.5 7.9 %copy-start.19 = (bf16[64,512]{1,0:T(8,128)(2,1)}, bf16[64,512]{1,0:T(8,128)(2,1)S(1)}, u32[]{:S(2)}) copy-start(bf16[64,512]{1,0:T(8,128)(2,1)S(1)} %collective-permute-done.6.refs_7_) | copy-start | bytes 196612
  72.5 5.6 %collective-permute-start.1 = (bf16[64,512]{1,0:T(8,128)(2,1)S(1)}, bf16[64,512]{1,0:T(8,128)(2,1)S(1)}, u32[]{:S(2)}, u32[]{:S(2)}) collective-permute-start(bf16[64,512]{1,0:T(8,128)(2,1)S(1)} %copy-done.18), channel_id=1, source_target_pairs={{0,2},{1,3},{2,4},{3,5},{4,6},{5,7},{6,0},{7,1},{8,10},{9,11},{10,... | collective-permute-start | bytes 196616 | tf_op jit(solution)/shard_map/ppermute | solution.py:375
  75.7 4.6 %copy-start.20 = (bf16[64,512]{1,0:T(8,128)(2,1)}, bf16[64,512]{1,0:T(8,128)(2,1)S(1)}, u32[]{:S(2)}) copy-start(bf16[64,512]{1,0:T(8,128)(2,1)S(1)} %collective-permute-done.5.refs_6_) | copy-start | bytes 196612
  75.7 4.6 %collective-permute-start = (bf16[64,512]{1,0:T(8,128)(2,1)S(1)}, bf16[64,512]{1,0:T(8,128)(2,1)S(1)}, u32[]{:S(2)}, u32[]{:S(2)}) collective-permute-start(bf16[64,512]{1,0:T(8,128)(2,1)S(1)} %copy-done.18), channel_id=1, source_target_pairs={{0,1},{1,2},{2,3},{3,4},{4,5},{5,6},{6,7},{7,0},{8,9},{9,10},{10,1... | collective-permute-start | bytes 196616 | tf_op jit(solution)/shard_map/ppermute | solution.py:375
  77.0 3.3 copy-start.21
  77.0 3.3 copy-start.22
  77.1 3.3 copy-start.23
  78.1 2.3 copy-start.24
  91.4 1.3 copy-start.6
  91.4 5.9 %copy-start.33 = (bf16[8,2,128,128]{3,2,1,0:T(8,128)(2,1)S(1)}, bf16[8,2,128,128]{3,2,1,0:T(8,128)(2,1)}, u32[]{:S(2)}) copy-start(bf16[8,2,128,128]{3,2,1,0:T(8,128)(2,1)} %get-tuple-element.31) | copy-start | bytes 1572868
  91.4 8.8 %copy-start.32 = (bf16[8,2,128,128]{3,2,1,0:T(8,128)(2,1)S(1)}, bf16[8,2,128,128]{3,2,1,0:T(8,128)(2,1)}, u32[]{:S(2)}) copy-start(bf16[8,2,128,128]{3,2,1,0:T(8,128)(2,1)} %get-tuple-element.42) | copy-start | bytes 1572868
  92.7 70.4 %all-to-all-start.1 = ((bf16[8,2,512,256]{3,2,1,0:T(8,128)(2,1)}), bf16[8,2,512,256]{3,2,1,0:T(8,128)(2,1)}, u32[]{:S(2)}, u32[]{:S(2)}) async-start(bf16[8,2,512,256]{3,2,1,0:T(8,128)(2,1)} %get-tuple-element.29), calls=%async_computation.1 | async-start | bytes 8388608 | tf_op jit(solution)/shard_map/all_to_all | solution.py:410
  97.3 36.0 %collective-permute-start.7 = (bf16[8,2,128,128]{3,2,1,0:T(8,128)(2,1)S(1)}, bf16[8,2,128,128]{3,2,1,0:T(8,128)(2,1)S(1)}, u32[]{:S(2)}, u32[]{:S(2)}) collective-permute-start(bf16[8,2,128,128]{3,2,1,0:T(8,128)(2,1)S(1)} %copy-done.33), channel_id=1, source_target_pairs={{0,8},{8,16},{16,24},{24,0},{1,9},{9,17},{17,25},{25,1},{2,10},{10... | collective-permute-start | bytes 1572872 | tf_op jit(solution)/shard_map/ppermute | solution.py:416
  99.0 48.0 %collective-permute-start.14 = (bf16[8,2,128,128]{3,2,1,0:T(8,128)(2,1)}, bf16[8,2,128,128]{3,2,1,0:T(8,128)(2,1)S(1)}, u32[]{:S(2)}, u32[]{:S(2)}) collective-permute-start(bf16[8,2,128,128]{3,2,1,0:T(8,128)(2,1)} %get-tuple-element.41), channel_id=1, source_target_pairs={{0,16},{8,24},{16,0},{24,8},{1,17},{9,25},{17,1},{25,9},{2,18},{10... | collective-permute-start | bytes 1572872 | tf_op jit(solution)/shard_map/ppermute | solution.py:416
  100.2 57.2 %collective-permute-start.15 = (bf16[8,2,128,128]{3,2,1,0:T(8,128)(2,1)S(1)}, bf16[8,2,128,128]{3,2,1,0:T(8,128)(2,1)S(1)}, u32[]{:S(2)}, u32[]{:S(2)}) collective-permute-start(bf16[8,2,128,128]{3,2,1,0:T(8,128)(2,1)S(1)} %copy-done.32), channel_id=1, source_target_pairs={{0,24},{8,0},{16,8},{24,16},{1,25},{9,1},{17,9},{25,17},{2,26},{10... | collective-permute-start | bytes 1572872 | tf_op jit(solution)/shard_map/ppermute | solution.py:416
  142.4 14.9 %collective-permute-start.8 = (bf16[8,2,128,128]{3,2,1,0:T(8,128)(2,1)}, bf16[8,2,128,128]{3,2,1,0:T(8,128)(2,1)S(1)}, u32[]{:S(2)}, u32[]{:S(2)}) collective-permute-start(bf16[8,2,128,128]{3,2,1,0:T(8,128)(2,1)} %get-tuple-element.32), channel_id=1, source_target_pairs={{0,8},{8,16},{16,24},{24,0},{1,9},{9,17},{17,25},{25,1},{2,10},{10... | collective-permute-start | bytes 1572872 | tf_op jit(solution)/shard_map/ppermute | solution.py:416
  146.9 10.4 %copy-start.9 = (bf16[8,2,128,128]{3,2,1,0:T(8,128)(2,1)}, bf16[8,2,128,128]{3,2,1,0:T(8,128)(2,1)S(1)}, u32[]{:S(2)}) copy-start(bf16[8,2,128,128]{3,2,1,0:T(8,128)(2,1)S(1)} %collective-permute-done.14.refs_2_) | copy-start | bytes 1572868
  163.1 35.9 %all-to-all-start.3 = ((bf16[8,2,16,32,128]{4,3,2,1,0:T(8,128)(2,1)}), bf16[8,2,16,32,128]{4,3,2,1,0:T(8,128)(2,1)S(1)}, u32[]{:S(2)}, u32[]{:S(2)}) async-start(bf16[8,2,16,32,128]{4,3,2,1,0:T(8,128)(2,1)} %hold.4), calls=%async_computation.3 | async-start | bytes 4194304 | tf_op jit(solution)/shard_map/all_to_all | solution.py:410
  175.3 14.5 %collective-permute-start.9 = (bf16[8,2,128,128]{3,2,1,0:T(8,128)(2,1)}, bf16[8,2,128,128]{3,2,1,0:T(8,128)(2,1)S(1)}, u32[]{:S(2)}, u32[]{:S(2)}) collective-permute-start(bf16[8,2,128,128]{3,2,1,0:T(8,128)(2,1)} %get-tuple-element.34), channel_id=1, source_target_pairs={{0,8},{8,16},{16,24},{24,0},{1,9},{9,17},{17,25},{25,1},{2,10},{10... | collective-permute-start | bytes 1572872 | tf_op jit(solution)/shard_map/ppermute | solution.py:416
  200.3 4.0 %copy-start.29 = (bf16[8,2,128,128]{3,2,1,0:T(8,128)(2,1)S(1)}, bf16[8,2,128,128]{3,2,1,0:T(8,128)(2,1)}, u32[]{:S(2)}) copy-start(bf16[8,2,128,128]{3,2,1,0:T(8,128)(2,1)} %get-tuple-element.38) | copy-start | bytes 1572868
  200.3 4.8 %copy-start.28 = (bf16[8,2,128,128]{3,2,1,0:T(8,128)(2,1)S(1)}, bf16[8,2,128,128]{3,2,1,0:T(8,128)(2,1)}, u32[]{:S(2)}) copy-start(bf16[8,2,128,128]{3,2,1,0:T(8,128)(2,1)} %get-tuple-element.39) | copy-start | bytes 1572868
  200.3 46.2 %all-to-all-start.4 = ((bf16[8,4,2,128,128]{4,3,2,1,0:T(8,128)(2,1)}), bf16[8,4,2,128,128]{4,3,2,1,0:T(8,128)(2,1)S(1)}, u32[]{:S(2)}, u32[]{:S(2)}) async-start(bf16[8,4,2,128,128]{4,3,2,1,0:T(8,128)(2,1)} %hold.5), calls=%async_computation.4 | async-start | bytes 4194304 | tf_op jit(solution)/shard_map/all_to_all | solution.py:410
  204.3 35.0 %collective-permute-start.12 = (bf16[8,2,128,128]{3,2,1,0:T(8,128)(2,1)S(1)}, bf16[8,2,128,128]{3,2,1,0:T(8,128)(2,1)S(1)}, u32[]{:S(2)}, u32[]{:S(2)}) collective-permute-start(bf16[8,2,128,128]{3,2,1,0:T(8,128)(2,1)S(1)} %copy-done.29), channel_id=1, source_target_pairs={{0,16},{8,24},{16,0},{24,8},{1,17},{9,25},{17,1},{25,9},{2,18},{10... | collective-permute-start | bytes 1572872 | tf_op jit(solution)/shard_map/ppermute | solution.py:416
  205.1 35.9 %collective-permute-start.13 = (bf16[8,2,128,128]{3,2,1,0:T(8,128)(2,1)S(1)}, bf16[8,2,128,128]{3,2,1,0:T(8,128)(2,1)S(1)}, u32[]{:S(2)}, u32[]{:S(2)}) collective-permute-start(bf16[8,2,128,128]{3,2,1,0:T(8,128)(2,1)S(1)} %copy-done.28), channel_id=1, source_target_pairs={{0,24},{8,0},{16,8},{24,16},{1,25},{9,1},{17,9},{25,17},{2,26},{10... | collective-permute-start | bytes 1572872 | tf_op jit(solution)/shard_map/ppermute | solution.py:416
  239.4 1.6 copy-start.14
  246.5 1.4 copy-start.1
  247.9 4.0 %copy-start.31 = (bf16[8,2,128,128]{3,2,1,0:T(8,128)(2,1)S(1)}, bf16[8,2,128,128]{3,2,1,0:T(8,128)(2,1)}, u32[]{:S(2)}) copy-start(bf16[8,2,128,128]{3,2,1,0:T(8,128)(2,1)} %get-tuple-element.35) | copy-start | bytes 1572868
  247.9 6.0 %copy-start.30 = (bf16[8,2,128,128]{3,2,1,0:T(8,128)(2,1)S(1)}, bf16[8,2,128,128]{3,2,1,0:T(8,128)(2,1)}, u32[]{:S(2)}) copy-start(bf16[8,2,128,128]{3,2,1,0:T(8,128)(2,1)} %get-tuple-element.36) | copy-start | bytes 1572868
  247.9 44.5 %all-to-all-start.5 = ((bf16[8,2,16,32,128]{4,3,2,1,0:T(8,128)(2,1)}), bf16[8,2,16,32,128]{4,3,2,1,0:T(8,128)(2,1)S(1)}, u32[]{:S(2)}, u32[]{:S(2)}) async-start(bf16[8,2,16,32,128]{4,3,2,1,0:T(8,128)(2,1)} %hold.6), calls=%async_computation.5 | async-start | bytes 4194304 | tf_op jit(solution)/shard_map/all_to_all | solution.py:410
  251.9 34.8 %collective-permute-start.10 = (bf16[8,2,128,128]{3,2,1,0:T(8,128)(2,1)S(1)}, bf16[8,2,128,128]{3,2,1,0:T(8,128)(2,1)S(1)}, u32[]{:S(2)}, u32[]{:S(2)}) collective-permute-start(bf16[8,2,128,128]{3,2,1,0:T(8,128)(2,1)S(1)} %copy-done.31), channel_id=1, source_target_pairs={{0,16},{8,24},{16,0},{24,8},{1,17},{9,25},{17,1},{25,9},{2,18},{10... | collective-permute-start | bytes 1572872 | tf_op jit(solution)/shard_map/ppermute | solution.py:416
  253.9 32.8 %collective-permute-start.11 = (bf16[8,2,128,128]{3,2,1,0:T(8,128)(2,1)S(1)}, bf16[8,2,128,128]{3,2,1,0:T(8,128)(2,1)S(1)}, u32[]{:S(2)}, u32[]{:S(2)}) collective-permute-start(bf16[8,2,128,128]{3,2,1,0:T(8,128)(2,1)S(1)} %copy-done.30), channel_id=1, source_target_pairs={{0,24},{8,0},{16,8},{24,16},{1,25},{9,1},{17,9},{25,17},{2,26},{10... | collective-permute-start | bytes 1572872 | tf_op jit(solution)/shard_map/ppermute | solution.py:416
  293.8 4.5 %copy-start.2 = (bf16[8,4,2,128,128]{4,3,2,1,0:T(8,128)(2,1)S(1)}, bf16[8,4,2,128,128]{4,3,2,1,0:T(8,128)(2,1)}, u32[]{:S(2)}) copy-start(bf16[8,4,2,128,128]{4,3,2,1,0:T(8,128)(2,1)} %copy-done.1) | copy-start | bytes 6291460
  293.8 71.9 %all-to-all-start.6 = ((bf16[8,2,16,32,128]{4,3,2,1,0:T(8,128)(2,1)}), bf16[8,2,16,32,128]{4,3,2,1,0:T(8,128)(2,1)}, u32[]{:S(2)}, u32[]{:S(2)}) async-start(bf16[8,2,16,32,128]{4,3,2,1,0:T(8,128)(2,1)} %hold.7), calls=%async_computation.6 | async-start | bytes 4194304 | tf_op jit(solution)/shard_map/all_to_all | solution.py:410
  299.2 14.8 %collective-permute-start.18 = (bf16[8,2,128,128]{3,2,1,0:T(8,128)(2,1)S(1)}, bf16[8,2,128,128]{3,2,1,0:T(8,128)(2,1)S(1)}, u32[]{:S(2)}, u32[]{:S(2)}) collective-permute-start(bf16[8,2,128,128]{3,2,1,0:T(8,128)(2,1)S(1)} %get-tuple-element.43), channel_id=1, source_target_pairs={{0,24},{8,0},{16,8},{24,16},{1,25},{9,1},{17,9},{25,17},{2,26},{10... | collective-permute-start | bytes 1572872 | tf_op jit(solution)/shard_map/ppermute | solution.py:416
  299.2 38.2 %collective-permute-start.17 = (bf16[8,2,128,128]{3,2,1,0:T(8,128)(2,1)S(1)}, bf16[8,2,128,128]{3,2,1,0:T(8,128)(2,1)S(1)}, u32[]{:S(2)}, u32[]{:S(2)}) collective-permute-start(bf16[8,2,128,128]{3,2,1,0:T(8,128)(2,1)S(1)} %get-tuple-element.44), channel_id=1, source_target_pairs={{0,16},{8,24},{16,0},{24,8},{1,17},{9,25},{17,1},{25,9},{2,18},{10... | collective-permute-start | bytes 1572872 | tf_op jit(solution)/shard_map/ppermute | solution.py:416
  302.6 45.4 %collective-permute-start.16 = (bf16[8,2,128,128]{3,2,1,0:T(8,128)(2,1)S(1)}, bf16[8,2,128,128]{3,2,1,0:T(8,128)(2,1)S(1)}, u32[]{:S(2)}, u32[]{:S(2)}) collective-permute-start(bf16[8,2,128,128]{3,2,1,0:T(8,128)(2,1)S(1)} %get-tuple-element.45), channel_id=1, source_target_pairs={{0,8},{8,16},{16,24},{24,0},{1,9},{9,17},{17,25},{25,1},{2,10},{10... | collective-permute-start | bytes 1572872 | tf_op jit(solution)/shard_map/ppermute | solution.py:416
  314.0 34.1 %copy-start.11 = (bf16[8,2,128,128]{3,2,1,0:T(8,128)(2,1)}, bf16[8,2,128,128]{3,2,1,0:T(8,128)(2,1)S(1)}, u32[]{:S(2)}) copy-start(bf16[8,2,128,128]{3,2,1,0:T(8,128)(2,1)S(1)} %collective-permute-done.18.refs_3_) | copy-start | bytes 1572868
  337.4 10.7 %copy-start.12 = (bf16[8,2,128,128]{3,2,1,0:T(8,128)(2,1)}, bf16[8,2,128,128]{3,2,1,0:T(8,128)(2,1)S(1)}, u32[]{:S(2)}) copy-start(bf16[8,2,128,128]{3,2,1,0:T(8,128)(2,1)S(1)} %collective-permute-done.17.refs_2_) | copy-start | bytes 1572868
  (12 other events, 11.4 us)

commit v6 on v5

--- a/solution.py
+++ b/solution.py
@@ -88,9 +88,6 @@
 
 def column_kernel(groups, x_ref, twiddle_ref, table_ref, *refs):
     *out_refs, mid = refs
-    if len(out_refs) > len(groups):
-        basis_ref, *out_refs, copy_ref = out_refs
-        copy_ref[...] = basis_ref[...]
     rows, length = x_ref.shape[1:]
     inner = length // RADIX
     step = 16
@@ -136,12 +133,11 @@
                 ]
 
 
-def column_transform(x, pieces, groups, passed):
+def column_transform(x, pieces, groups):
     _, rows, length = x.shape
     inner = length // RADIX
     block = math.gcd(rows, 64)
     lanes = [len(chunks) * LANES for chunks in groups]
-    kept = [pl.BlockSpec(a.shape, lambda i: (0, 0)) for a in passed]
     return pl.pallas_call(
         functools.partial(column_kernel, groups),
         grid=(rows // block,),
@@ -149,18 +145,16 @@
             pl.BlockSpec((2, block, length), lambda i: (0, i, 0)),
             pl.BlockSpec((RADIX, 2, inner), lambda i: (0, 0, 0)),
             pl.BlockSpec((2 * inner, 2 * inner), lambda i: (0, 0)),
-        ]
-        + kept,
-        out_specs=[pl.BlockSpec((pieces, 2, block, n), lambda i: (0, 0, i, 0)) for n in lanes] + kept,
-        out_shape=[jax.ShapeDtypeStruct((pieces, 2, rows, n), jnp.bfloat16) for n in lanes]
-        + [jax.ShapeDtypeStruct(a.shape, a.dtype) for a in passed],
+        ],
+        out_specs=[pl.BlockSpec((pieces, 2, block, n), lambda i: (0, 0, i, 0)) for n in lanes],
+        out_shape=[jax.ShapeDtypeStruct((pieces, 2, rows, n), jnp.bfloat16) for n in lanes],
         scratch_shapes=[pltpu.VMEM((RADIX, block, 2 * inner), jnp.bfloat16)],
         compiler_params=params(),
         cost_estimate=pl.CostEstimate(
             flops=4 * rows * length * sum(lanes), bytes_accessed=8 * rows * length, transcendentals=0
         ),
         name="column_transform",
-    )(x, jnp.asarray(twiddle_table(length)), jnp.asarray(inner_table(inner)), *passed)
+    )(x, jnp.asarray(twiddle_table(length)), jnp.asarray(inner_table(inner)))
 
 
 def clean_kernel(after, later, at_ref, x_ref, basis_ref, basis_t_ref, gain_ref, swap_ref, back_ref, *refs):
@@ -359,62 +353,51 @@
     )(x, jnp.asarray(table), *held)
 
 
-def gather_kernel(at_ref, *refs):
-    *block_refs, basis_ref, turned_ref = refs
-    count = len(block_refs)
-    rows = block_refs[0].shape[0]
-    for step, block_ref in enumerate(block_refs):
-        owner = lax.rem(at_ref[0] - step + count, count)
-        basis_ref[pl.ds(pl.multiple_of(owner * rows, rows), rows), :] = block_ref[...]
-    turned_ref[...] = basis_ref[...].T
-
-
-def gather(block):
-    count = lax.axis_size("chan")
-    blocks = [block] + [
-        lax.ppermute(block, "chan", [(j, (j + step) % count) for j in range(count)])
-        for step in range(1, count)
-    ]
-    rows, modes = block.shape
+def turn_kernel(basis_ref, out_ref):
+    out_ref[...] = basis_ref[...].T
+
+
+def turn(basis):
     vmem = pl.BlockSpec(memory_space=pltpu.VMEM)
     return pl.pallas_call(
-        gather_kernel,
-        in_specs=[pl.BlockSpec(memory_space=pltpu.SMEM)] + [vmem] * count,
-        out_specs=[vmem] * 2,
-        out_shape=[
-            jax.ShapeDtypeStruct((count * rows, modes), block.dtype),
-            jax.ShapeDtypeStruct((modes, count * rows), block.dtype),
-        ],
+        turn_kernel,
+        in_specs=[vmem],
+        out_specs=vmem,
+        out_shape=jax.ShapeDtypeStruct(basis.shape[::-1], basis.dtype),
         compiler_params=params(),
-        name="gather",
-    )(lax.axis_index("chan").astype(jnp.int32).reshape(1), *blocks)
+        name="turn",
+    )(basis)
 
 
 def hold_kernel(*refs):
     pass
 
 
-def hold(x, after):
+def hold(arrays, after):
+    if not after:
+        return list(arrays)
     untouched = pl.BlockSpec(memory_space=pl.ANY)
     return pl.pallas_call(
         hold_kernel,
-        in_specs=[untouched] * (1 + len(after)),
-        out_specs=untouched,
-        out_shape=jax.ShapeDtypeStruct(x.shape, x.dtype),
-        input_output_aliases={0: 0},
+        in_specs=[untouched] * (len(arrays) + len(after)),
+        out_specs=[untouched] * len(arrays),
+        out_shape=[jax.ShapeDtypeStruct(a.shape, a.dtype) for a in arrays],
+        input_output_aliases={i: i for i in range(len(arrays))},
         name="hold",
-    )(x, *after)
+    )(*arrays, *after)
 
 
 def exchange(x):
     return lax.all_to_all(x, "chan", split_axis=0, concat_axis=0, tiled=True)
 
 
-def spread_rows(parts):
+def spread_rows(parts, before):
     count = len(parts)
-    return [parts[0]] + [
-        lax.ppermute(parts[step], "uv", [(z, (z + step) % count) for z in range(count)])
-        for step in range(1, count)
+    own, *sent = parts
+    sent = hold(sent, before[1:])
+    return [own] + [
+        lax.ppermute(part, "uv", [(z, (z + step) % count) for z in range(count)])
+        for step, part in enumerate(sent, 1)
     ]
 
 
@@ -425,20 +408,21 @@
     count = length // chan_count // LANES
     out_chans = chans // uv_count
     at = lax.axis_index("uv").astype(jnp.int32).reshape(1)
+    basis = exchange(jnp.broadcast_to(eigen_basis, (chan_count,) + eigen_basis.shape))
+    basis = basis.reshape(chan_count * chans, -1)
+    basis_t = turn(basis)
     gain = eigenvalues[:, None] / (eigenvalues[:, None] + noise_power[None, :])
     flat = visibility.reshape(2, chans * rows_dev, length)
     groups = [g for g in ([1], list(range(2, count))) if g and g[-1] < count]
-    first, block = column_transform(flat, chan_count, [[0]], [eigen_basis])
-    cells = [exchange(first)]
-    basis, basis_t = gather(block)
-    sends = column_transform(flat, chan_count, groups, []) if groups else []
+    first = column_transform(flat, chan_count, [[0]])
+    cells = [exchange(first[0])]
+    sends = column_transform(flat, chan_count, groups) if groups else []
     cells += [exchange(send) for send in sends[:1]]
     sends = sends[1:]
 
-    pieces, returned = {}, {}
+    pieces, joined = [], None
     for k in range(count):
         last = k == count - 1 and count > 1
-        after = [pieces[k - 1][1]] if k else []
         results, passed = clean(
             at,
             cells[min(k, 2)],
@@ -450,30 +434,34 @@
             chan_count,
             rows_dev,
             last,
-            after,
+            [pieces[1][1]] if k > 1 else [],
             sends,
         )
         cells += [exchange(send) for send in passed]
         sends = []
-        if not last:
-            pieces[k] = spread_rows(results)
+        if last:
+            joined = results[0]
         else:
-            joined = results[0]
-    transform = lambda k, after: row_transform(pieces[k], at, out_chans, rows_dev, length, after)
-    following = lambda k: [pieces[k + 1][1]] if k + 1 in pieces else []
+            pieces.append(spread_rows(results, pieces[-1] if pieces else []))
+
+    def transform(k):
+        after = [parts[1] for parts in pieces[k + 1 : k + 2]]
+        return row_transform(pieces[k], at, out_chans, rows_dev, length, after)
+
+    def exchange_after(x, before):
+        return exchange(hold([x], before)[0])
+
     if count == 1:
-        returned[0] = exchange(transform(0, []))
+        returned = [exchange(transform(0))]
     else:
-        first_lines = transform(0, following(0))
-        returned[0] = exchange(hold(first_lines, cells[-1:]))
-        joined = exchange(hold(joined, [returned[0]]))
-        middle = {k: transform(k, following(k)) for k in range(1, count - 1)}
-        pieces[count - 1] = spread_rows([joined[:, step] for step in range(uv_count)])
-        before = joined
+        returned = [exchange_after(transform(0), cells[-1:])]
+        joined = exchange_after(joined, returned)
+        pieces.append(
+            spread_rows([joined[:, step] for step in range(uv_count)], pieces[-1])
+        )
         for k in range(1, count - 1):
-            returned[k] = exchange(hold(middle[k], [before]))
-            before = returned[k]
-        returned[count - 1] = transform(count - 1, [])
+            returned.append(exchange_after(transform(k), [joined] if k == 1 else returned[-1:]))
+        returned.append(transform(count - 1))
     order = list(range(count))
     if count > 2:
         order = order[:-2] + [count - 1, count - 2]

time: 375 us -> 381 us (1.016)
  waiting for transfers between devices: 196 us -> 210 us
  starting transfers between devices: 54 us -> 42.1 us
  local copies, waits for them, and re-layouts: 15.1 us -> 20 us
    all_to_all x7 -> x8, waiting for transfers between devices: 11.1 us -> 44.7 us  [exchange(): return lax.all_to_all(x, 'chan', split_axis=0, concat_axis=0, tiled=True)]
    ppermute x19 -> x12, waiting for transfers between devices: 185 us -> 165 us  [spread_rows(): lax.ppermute(part, 'uv', [(z, (z + step) % count) for z in range(count)])]
    ppermute x19 -> x12, starting transfers between devices: 25.8 us -> 11 us  [spread_rows(): lax.ppermute(part, 'uv', [(z, (z + step) % count) for z in range(count)])]
    all_to_all x7 -> x8, starting transfers between devices: 28.2 us -> 31.1 us  [exchange(): return lax.all_to_all(x, 'chan', split_axis=0, concat_axis=0, tiled=True)]
    unnamed x68 -> x50, local copies, waits for them, and re-layouts: 12.6 us -> 13.9 us
  transfers between devices with their start and end apart: 26 -> 20, of which waited for: 14 -> 15; matrix products, arithmetic and copies ran while one was open for 1% -> 1% of each run, Pallas kernels for 24% -> 26%
where the time goes in v6:
time: 381 us; the launch traced here: 379 us
  waiting for transfers between devices  210 us (55%)
  Pallas kernels  106 us (28%)
  starting transfers between devices  42.1 us (11%)
  local copies, waits for them, and re-layouts  20 us (5%)
    ppermute x12, waiting for transfers between devices, spread_rows(): lax.ppermute(part, 'uv', [(z, (z + step) % count) for z in range(count)])  165 us
    all_to_all x8, waiting for transfers between devices, exchange(): return lax.all_to_all(x, 'chan', split_axis=0, concat_axis=0, tiled=True)  44.7 us
    pallas_call x4, Pallas kernels, clean(): pl.pallas_call(functools.partial(clean_kernel, len(after), len(later)), g...  33.4 us
    all_to_all x8, starting transfers between devices, exchange(): return lax.all_to_all(x, 'chan', split_axis=0, concat_axis=0, tiled=True)  31.1 us
    pallas_call x2, Pallas kernels, column_transform(): pl.pallas_call(functools.partial(column_kernel, groups), grid=(rows // bl...  27.4 us
    pallas_call x4, Pallas kernels, place(): pl.pallas_call(place_kernel, grid=(chans // block, groups), in_specs=[pl....  24.1 us
    pallas_call x4, Pallas kernels, row_transform(): pl.pallas_call(functools.partial(row_kernel, scale, group, steps), grid=(...  19.1 us
    unnamed x50, local copies, waits for them, and re-layouts  13.9 us
  transfers between devices with their start and end apart: 20, of which 15 were waited for; matrix products, arithmetic and copies ran while one was open for 1% of the time, Pallas kernels for 26%

profile of v6, /device:TPU:8, one launch (start us, length us, event | category | flops | bytes accessed | tf_op | source)
XLA Modules:
  0.0 379.2 jit_solution(17625047109480550130)
XLA Ops:
  0.0 1.7 broadcast_in_dim.2
  1.7 3.7 all-to-all-start.1
  5.4 11.9 %column_transform.2 = bf16[8,2,512,128]{3,2,1,0:T(8,128)(2,1)} custom-call(bf16[2,512,4096]{2,1,0:T(8,128)(2,1)} %bitcast.21, f32[8,2,512]{2,1,0:T(2,128)} %constant.29.clone.twiddle_ref, bf16[1024,1024]{1,0:T(8,128)(2,1)} %constant.30.clone.table_ref), custom_call_target="tpu_custom_call" | custom-call | flops 1073741824 | bytes 16777216 | tf_op jit(solution)/shard_map/column_transform/pallas_call | solution.py:141
  17.3 4.2 %all-to-all-start = ((bf16[8,2,512,128]{3,2,1,0:T(8,128)(2,1)}), bf16[8,2,512,128]{3,2,1,0:T(8,128)(2,1)S(1)}, u32[]{:S(2)}, u32[]{:S(2)}) async-start(bf16[8,2,512,128]{3,2,1,0:T(8,128)(2,1)} %column_transform.2), calls=%async_computation | async-start | bytes 4194304 | tf_op jit(solution)/shard_map/all_to_all | solution.py:391
  21.5 15.5 %column_transform.3 = (bf16[8,2,512,128]{3,2,1,0:T(8,128)(2,1)}, bf16[8,2,512,256]{3,2,1,0:T(8,128)(2,1)}) custom-call(bf16[2,512,4096]{2,1,0:T(8,128)(2,1)} %bitcast.22, f32[8,2,512]{2,1,0:T(2,128)} %constant.29.clone.twiddle_ref, bf16[1024,1024]{1,0:T(8,128)(2,1)} %constant.30.clone.table_ref), custom_call_target="tpu_custom_call" | custom-call | flops 3221225472 | bytes 16777216 | tf_op jit(solution)/shard_map/column_transform/pallas_call | solution.py:141
  37.0 11.1 %all-to-all-done.x_ref = bf16[8,2,512,128]{3,2,1,0:T(8,128)(2,1)S(1)} async-done(((bf16[8,2,512,128]{3,2,1,0:T(8,128)(2,1)}), bf16[8,2,512,128]{3,2,1,0:T(8,128)(2,1)S(1)}, u32[]{:S(2)}, u32[]{:S(2)}) %all-to-all-start) | async-done | bytes 2097184 | tf_op jit(solution)/shard_map/all_to_all | solution.py:391
  48.1 1.4 copy-done.8
  49.5 3.6 all-to-all-start.3
  54.0 2.1 turn.1.basis_t_ref
  56.1 8.3 %clean.4 = (bf16[8,2,128,128]{3,2,1,0:T(8,128)(2,1)}, bf16[8,2,128,128]{3,2,1,0:T(8,128)(2,1)}, bf16[8,2,128,128]{3,2,1,0:T(8,128)(2,1)}, bf16[8,2,128,128]{3,2,1,0:T(8,128)(2,1)}, bf16[8,2,512,256]{3,2,1,0:T(8,128)(2,1)}) custom-call(s32[1]{0:T(128)} %bitcast.at_ref, bf16[8,2,512,128]{3,2,1,0:T(8,128)(2,1)} %copy-done.8, ...), custom_call_target="tpu_custom_call", output_to_operand_aliasing={{4}: (7, {})} | custom-call | flops 3221225472 | bytes 4194304 | tf_op jit(solution)/shard_map/clean/pallas_call | solution.py:241
  64.4 15.3 %all-to-all-done.3.x_ref = bf16[8,2,512,128]{3,2,1,0:T(8,128)(2,1)S(1)} async-done(((bf16[8,2,512,128]{3,2,1,0:T(8,128)(2,1)}), bf16[8,2,512,128]{3,2,1,0:T(8,128)(2,1)S(1)}, u32[]{:S(2)}, u32[]{:S(2)}) %all-to-all-start.3) | async-done | bytes 2097184 | tf_op jit(solution)/shard_map/all_to_all | solution.py:391
  79.7 1.4 copy-done.7
  81.0 4.6 %all-to-all-start.2 = ((bf16[8,2,512,256]{3,2,1,0:T(8,128)(2,1)}), bf16[8,2,512,256]{3,2,1,0:T(8,128)(2,1)}, u32[]{:S(2)}, u32[]{:S(2)}) async-start(bf16[8,2,512,256]{3,2,1,0:T(8,128)(2,1)} %get-tuple-element.30), calls=%async_computation.2 | async-start | bytes 8388608 | tf_op jit(solution)/shard_map/all_to_all | solution.py:391
  85.6 1.6 collective-permute-start
  88.5 1.8 collective-permute-start.2
  90.3 8.4 %clean.5 = (bf16[8,2,128,128]{3,2,1,0:T(8,128)(2,1)}, bf16[8,2,128,128]{3,2,1,0:T(8,128)(2,1)}, bf16[8,2,128,128]{3,2,1,0:T(8,128)(2,1)}, bf16[8,2,128,128]{3,2,1,0:T(8,128)(2,1)}) custom-call(s32[1]{0:T(128)} %bitcast.at_ref, bf16[8,2,512,128]{3,2,1,0:T(8,128)(2,1)} %copy-done.7, bf16[512,512]{1,0:T(8,128)(2,1)} %bitcast.25, ...), custom_call_target="tpu_custom_call" | custom-call | flops 3221225472 | bytes 4194304 | tf_op jit(solution)/shard_map/clean/pallas_call | solution.py:241
  98.7 23.5 %collective-permute-done.refs_3_.refs_1_ = bf16[8,2,128,128]{3,2,1,0:T(8,128)(2,1)S(1)} collective-permute-done((bf16[8,2,128,128]{3,2,1,0:T(8,128)(2,1)}, bf16[8,2,128,128]{3,2,1,0:T(8,128)(2,1)S(1)}, u32[]{:S(2)}, u32[]{:S(2)}) %collective-permute-start) | collective-permute-done | bytes 524320 | tf_op jit(solution)/shard_map/ppermute | solution.py:399
  122.2 10.7 %collective-permute-done.1.refs_4_.refs_2_ = bf16[8,2,128,128]{3,2,1,0:T(8,128)(2,1)S(1)} collective-permute-done((bf16[8,2,128,128]{3,2,1,0:T(8,128)(2,1)S(1)}, bf16[8,2,128,128]{3,2,1,0:T(8,128)(2,1)S(1)}, u32[]{:S(2)}, u32[]{:S(2)}) %collective-permute-start.1) | collective-permute-done | bytes 524320 | tf_op jit(solution)/shard_map/ppermute | solution.py:399
  132.8 1.8 collective-permute-done.2.refs_5_.refs_3_
  135.4 1.6 dynamic-slice_bitcast_fusion.refs_4_
  137.0 12.6 %collective-permute-done.3.refs_0_.refs_3_.refs_5_.refs_1_ = bf16[8,2,128,128]{3,2,1,0:T(8,128)(2,1)S(1)} collective-permute-done((bf16[8,2,128,128]{3,2,1,0:T(8,128)(2,1)}, bf16[8,2,128,128]{3,2,1,0:T(8,128)(2,1)S(1)}, u32[]{:S(2)}, u32[]{:S(2)}) %collective-permute-start.3) | collective-permute-done | bytes 524320 | tf_op jit(solution)/shard_map/ppermute | solution.py:399
  150.4 4.8 %row_transform.4.refs_0_ = bf16[8,2,16,32,128]{4,3,2,1,0:T(8,128)(2,1)} custom-call(bf16[8,2,128,128]{3,2,1,0:T(8,128)(2,1)} %get-tuple-element.48.refs_0_, bf16[8,2,128,128]{3,2,1,0:T(8,128)(2,1)} %copy-done.10, bf16[8,2,128,128]{3,2,1,0:T(8,128)(2,1)} %copy-done.11, bf16[8,2,128,128]{3,2,1,0:T(8,128)(2,1)} %copy-done.12, ...), custom_call_target="tpu_custom_call" | custom-call | flops 536870912 | bytes 4194304 | tf_op jit(solution)/shard_map/row_transform/pallas_call | solution.py:298
  155.2 3.8 %all-to-all-start.4 = ((bf16[8,2,16,32,128]{4,3,2,1,0:T(8,128)(2,1)}), bf16[8,2,16,32,128]{4,3,2,1,0:T(8,128)(2,1)S(1)}, u32[]{:S(2)}, u32[]{:S(2)}) async-start(bf16[8,2,16,32,128]{4,3,2,1,0:T(8,128)(2,1)} %hold.9), calls=%async_computation.4 | async-start | bytes 4194304 | tf_op jit(solution)/shard_map/all_to_all | solution.py:391
  159.0 8.3 %clean.7.refs_0_ = bf16[8,4,2,128,128]{4,3,2,1,0:T(8,128)(2,1)} custom-call(s32[1]{0:T(128)} %bitcast.at_ref, bf16[8,2,512,256]{3,2,1,0:T(8,128)(2,1)} %all-to-all-done.2.x_ref.refs_1_, bf16[512,512]{1,0:T(8,128)(2,1)} %bitcast.26, bf16[512,512]{1,0:T(8,128)(2,1)} %turn.1.basis_t_ref, f32[512,8]{1,0:T(8,128)} %add_divide_fusion.gain_ref, ...), custom_call_target="tpu_custom_call" | custom-call | flops 3221225472 | bytes 4194304 | tf_op jit(solution)/shard_map/clean/pallas_call | solution.py:241
  167.3 18.3 %all-to-all-done.4.refs_1_.x_ref = bf16[8,2,16,32,128]{4,3,2,1,0:T(8,128)(2,1)S(1)} async-done(((bf16[8,2,16,32,128]{4,3,2,1,0:T(8,128)(2,1)}), bf16[8,2,16,32,128]{4,3,2,1,0:T(8,128)(2,1)S(1)}, u32[]{:S(2)}, u32[]{:S(2)}) %all-to-all-start.4) | async-done | bytes 2097184 | tf_op jit(solution)/shard_map/all_to_all | solution.py:391
  185.6 1.4 copy-done.2
  187.0 3.6 all-to-all-start.5
  192.4 8.4 %clean.6 = (bf16[8,2,128,128]{3,2,1,0:T(8,128)(2,1)}, bf16[8,2,128,128]{3,2,1,0:T(8,128)(2,1)}, bf16[8,2,128,128]{3,2,1,0:T(8,128)(2,1)}, bf16[8,2,128,128]{3,2,1,0:T(8,128)(2,1)}) custom-call(s32[1]{0:T(128)} %bitcast.at_ref, bf16[8,2,512,256]{3,2,1,0:T(8,128)(2,1)} %all-to-all-done.2.x_ref.refs_1_, bf16[512,512]{1,0:T(8,128)(2,1)} %bitcast.27, ...), custom_call_target="tpu_custom_call" | custom-call | flops 3221225472 | bytes 4194304 | tf_op jit(solution)/shard_map/clean/pallas_call | solution.py:241
  200.8 25.4 %collective-permute-done.4.refs_4_.refs_2_ = bf16[8,2,128,128]{3,2,1,0:T(8,128)(2,1)S(1)} collective-permute-done((bf16[8,2,128,128]{3,2,1,0:T(8,128)(2,1)}, bf16[8,2,128,128]{3,2,1,0:T(8,128)(2,1)S(1)}, u32[]{:S(2)}, u32[]{:S(2)}) %collective-permute-start.4) | collective-permute-done | bytes 524320 | tf_op jit(solution)/shard_map/ppermute | solution.py:399
  226.2 1.5 collective-permute-done.5.refs_5_.refs_3_
  228.5 13.6 %collective-permute-done.6.refs_3_.refs_1_.refs_5_ = bf16[8,2,128,128]{3,2,1,0:T(8,128)(2,1)S(1)} collective-permute-done((bf16[8,2,128,128]{3,2,1,0:T(8,128)(2,1)}, bf16[8,2,128,128]{3,2,1,0:T(8,128)(2,1)S(1)}, u32[]{:S(2)}, u32[]{:S(2)}) %collective-permute-start.6) | collective-permute-done | bytes 524320 | tf_op jit(solution)/shard_map/ppermute | solution.py:399
  243.0 4.8 %row_transform.6.refs_0_ = bf16[8,2,16,32,128]{4,3,2,1,0:T(8,128)(2,1)} custom-call(bf16[8,2,128,128]{3,2,1,0:T(8,128)(2,1)} %get-tuple-element.50.refs_0_, bf16[8,2,128,128]{3,2,1,0:T(8,128)(2,1)} %copy-done.4, bf16[8,2,128,128]{3,2,1,0:T(8,128)(2,1)} %copy-done.13, bf16[8,2,128,128]{3,2,1,0:T(8,128)(2,1)} %copy-done.14, ...), custom_call_target="tpu_custom_call" | custom-call | flops 536870912 | bytes 4194304 | tf_op jit(solution)/shard_map/row_transform/pallas_call | solution.py:298
  249.1 3.7 all-to-all-start.6
  252.8 2.4 collective-permute-start.7
  255.2 2.9 slice_bitcast_fusion
  258.1 31.2 %collective-permute-done.7.refs_4_.refs_2_ = bf16[8,2,128,128]{3,2,1,0:T(8,128)(2,1)S(1)} collective-permute-done((bf16[8,2,128,128]{3,2,1,0:T(8,128)(2,1)}, bf16[8,2,128,128]{3,2,1,0:T(8,128)(2,1)S(1)}, u32[]{:S(2)}, u32[]{:S(2)}) %collective-permute-start.7) | collective-permute-done | bytes 524320 | tf_op jit(solution)/shard_map/ppermute | solution.py:399
  289.3 1.4 collective-permute-done.8.refs_5_.refs_3_
  291.5 14.1 %collective-permute-done.9.refs_5_.refs_1_ = bf16[8,2,128,128]{3,2,1,0:T(8,128)(2,1)S(1)} collective-permute-done((bf16[8,2,128,128]{3,2,1,0:T(8,128)(2,1)}, bf16[8,2,128,128]{3,2,1,0:T(8,128)(2,1)S(1)}, u32[]{:S(2)}, u32[]{:S(2)}) %collective-permute-start.9) | collective-permute-done | bytes 524320 | tf_op jit(solution)/shard_map/ppermute | solution.py:399
  306.4 4.8 %row_transform.5.refs_0_ = bf16[8,2,16,32,128]{4,3,2,1,0:T(8,128)(2,1)} custom-call(bf16[8,2,128,128]{3,2,1,0:T(8,128)(2,1)} %get-tuple-element.39.refs_0_, bf16[8,2,128,128]{3,2,1,0:T(8,128)(2,1)} %copy-done.5, bf16[8,2,128,128]{3,2,1,0:T(8,128)(2,1)} %copy-done.15, bf16[8,2,128,128]{3,2,1,0:T(8,128)(2,1)} %copy-done.16, ...), custom_call_target="tpu_custom_call" | custom-call | flops 536870912 | bytes 4194304 | tf_op jit(solution)/shard_map/row_transform/pallas_call | solution.py:298
  312.6 3.9 %all-to-all-start.7 = ((bf16[8,2,16,32,128]{4,3,2,1,0:T(8,128)(2,1)}), bf16[8,2,16,32,128]{4,3,2,1,0:T(8,128)(2,1)S(1)}, u32[]{:S(2)}, u32[]{:S(2)}) async-start(bf16[8,2,16,32,128]{4,3,2,1,0:T(8,128)(2,1)} %hold.13), calls=%async_computation.7 | async-start | bytes 4194304 | tf_op jit(solution)/shard_map/all_to_all | solution.py:391
  316.5 2.1 collective-permute-start.10
  318.6 6.0 %place.4.refs_0_ = bf16[2,16,32,4096]{3,2,1,0:T(8,128)(2,1)} custom-call(bf16[8,2,16,32,128]{4,3,2,1,0:T(8,128)(2,1)} %copy-done.2, bf16[1024,1024]{1,0:T(8,128)(2,1)} %constant.34.clone.table_ref), custom_call_target="tpu_custom_call" | custom-call | flops 2147483648 | bytes 4194304 | tf_op jit(solution)/shard_map/place/pallas_call | solution.py:333
  324.6 27.7 %collective-permute-done.10.refs_2_ = bf16[8,2,128,128]{3,2,1,0:T(8,128)(2,1)S(1)} collective-permute-done((bf16[8,2,128,128]{3,2,1,0:T(8,128)(2,1)S(1)}, bf16[8,2,128,128]{3,2,1,0:T(8,128)(2,1)S(1)}, u32[]{:S(2)}, u32[]{:S(2)}) %collective-permute-start.10) | collective-permute-done | bytes 524320 | tf_op jit(solution)/shard_map/ppermute | solution.py:399
  352.3 1.9 collective-permute-done.11.refs_3_
  355.1 4.8 %row_transform.7.x_ref = bf16[8,2,16,32,128]{4,3,2,1,0:T(8,128)(2,1)} custom-call(bf16[8,2,128,128]{3,2,1,0:T(8,128)(2,1)} %get-tuple-element.53.refs_0_, bf16[8,2,128,128]{3,2,1,0:T(8,128)(2,1)} %copy-done.6, bf16[8,2,128,128]{3,2,1,0:T(8,128)(2,1)} %copy-done.19, bf16[8,2,128,128]{3,2,1,0:T(8,128)(2,1)} %copy-done.20, ...), custom_call_target="tpu_custom_call" | custom-call | flops 536870912 | bytes 4194304 | tf_op jit(solution)/shard_map/row_transform/pallas_call | solution.py:298
  359.9 6.0 %place.5.refs_0_ = bf16[2,16,32,4096]{3,2,1,0:T(8,128)(2,1)} custom-call(bf16[8,2,16,32,128]{4,3,2,1,0:T(8,128)(2,1)} %copy-done, bf16[1024,1024]{1,0:T(8,128)(2,1)} %constant.34.clone.table_ref, bf16[2,16,32,4096]{3,2,1,0:T(8,128)(2,1)} %place.4.refs_0_), custom_call_target="tpu_custom_call", output_to_operand_aliasing={{}: (2, {})} | custom-call | flops 2147483648 | bytes 4194304 | tf_op jit(solution)/shard_map/place/pallas_call | solution.py:333
  365.9 6.0 %place.6.refs_0_ = bf16[2,16,32,4096]{3,2,1,0:T(8,128)(2,1)} custom-call(bf16[8,2,16,32,128]{4,3,2,1,0:T(8,128)(2,1)} %row_transform.7.x_ref, bf16[1024,1024]{1,0:T(8,128)(2,1)} %constant.34.clone.table_ref, bf16[2,16,32,4096]{3,2,1,0:T(8,128)(2,1)} %place.5.refs_0_), custom_call_target="tpu_custom_call", output_to_operand_aliasing={{}: (2, {})} | custom-call | flops 2147483648 | bytes 4194304 | tf_op jit(solution)/shard_map/place/pallas_call | solution.py:333
  373.2 6.0 %place.7 = bf16[2,16,32,4096]{3,2,1,0:T(8,128)(2,1)} custom-call(bf16[8,2,16,32,128]{4,3,2,1,0:T(8,128)(2,1)} %copy-done.3, bf16[1024,1024]{1,0:T(8,128)(2,1)} %constant.34.clone.table_ref, bf16[2,16,32,4096]{3,2,1,0:T(8,128)(2,1)} %place.6.refs_0_), custom_call_target="tpu_custom_call", output_to_operand_aliasing={{}: (2, {})} | custom-call | flops 2147483648 | bytes 4194304 | tf_op jit(solution)/shard_map/place/pallas_call | solution.py:333
  (68 shorter events, 13.7 us)
Async XLA Ops:
  1.7 15.6 %all-to-all-start.1 = ((bf16[8,64,512]{2,1,0:T(8,128)(2,1)}), bf16[8,64,512]{2,1,0:T(8,128)(2,1)S(1)}, u32[]{:S(2)}, u32[]{:S(2)}) async-start(bf16[8,64,512]{2,1,0:T(8,128)(2,1)} %broadcast_in_dim.2), calls=%async_computation.1 | async-start | bytes 1048576 | tf_op jit(solution)/shard_map/all_to_all | solution.py:391
  17.3 19.7 %copy-start.9 = (bf16[8,64,512]{2,1,0:T(8,128)(2,1)}, bf16[8,64,512]{2,1,0:T(8,128)(2,1)S(1)}, u32[]{:S(2)}) copy-start(bf16[8,64,512]{2,1,0:T(8,128)(2,1)S(1)} %all-to-all-done.1) | copy-start | bytes 1572868
  17.3 30.8 %all-to-all-start = ((bf16[8,2,512,128]{3,2,1,0:T(8,128)(2,1)}), bf16[8,2,512,128]{3,2,1,0:T(8,128)(2,1)S(1)}, u32[]{:S(2)}, u32[]{:S(2)}) async-start(bf16[8,2,512,128]{3,2,1,0:T(8,128)(2,1)} %column_transform.2), calls=%async_computation | async-start | bytes 4194304 | tf_op jit(solution)/shard_map/all_to_all | solution.py:391
  48.1 1.4 copy-start.8
  48.1 5.0 %copy-start.21 = (f32[512]{0:T(512)S(1)}, f32[512]{0:T(512)}, u32[]{:S(2)}) copy-start(f32[512]{0:T(512)} %param.26) | copy-start | bytes 6148
  48.1 5.0 %copy-start.22 = (f32[8]{0:T(128)S(1)}, f32[8]{0:T(128)}, u32[]{:S(2)}) copy-start(f32[8]{0:T(128)} %param.27) | copy-start | bytes 100
  49.5 30.2 %all-to-all-start.3 = ((bf16[8,2,512,128]{3,2,1,0:T(8,128)(2,1)}), bf16[8,2,512,128]{3,2,1,0:T(8,128)(2,1)S(1)}, u32[]{:S(2)}, u32[]{:S(2)}) async-start(bf16[8,2,512,128]{3,2,1,0:T(8,128)(2,1)} %get-tuple-element.31), calls=%async_computation.3 | async-start | bytes 4194304 | tf_op jit(solution)/shard_map/all_to_all | solution.py:391
  79.7 1.4 copy-start.7
  79.7 7.6 %copy-start.24 = (bf16[8,2,128,128]{3,2,1,0:T(8,128)(2,1)S(1)}, bf16[8,2,128,128]{3,2,1,0:T(8,128)(2,1)}, u32[]{:S(2)}) copy-start(bf16[8,2,128,128]{3,2,1,0:T(8,128)(2,1)} %get-tuple-element.36) | copy-start | bytes 1572868
  79.7 8.8 %copy-start.23 = (bf16[8,2,128,128]{3,2,1,0:T(8,128)(2,1)S(1)}, bf16[8,2,128,128]{3,2,1,0:T(8,128)(2,1)}, u32[]{:S(2)}) copy-start(bf16[8,2,128,128]{3,2,1,0:T(8,128)(2,1)} %get-tuple-element.37) | copy-start | bytes 1572868
  81.0 74.2 %all-to-all-start.2 = ((bf16[8,2,512,256]{3,2,1,0:T(8,128)(2,1)}), bf16[8,2,512,256]{3,2,1,0:T(8,128)(2,1)}, u32[]{:S(2)}, u32[]{:S(2)}) async-start(bf16[8,2,512,256]{3,2,1,0:T(8,128)(2,1)} %get-tuple-element.30), calls=%async_computation.2 | async-start | bytes 8388608 | tf_op jit(solution)/shard_map/all_to_all | solution.py:391
  85.6 36.5 %collective-permute-start = (bf16[8,2,128,128]{3,2,1,0:T(8,128)(2,1)}, bf16[8,2,128,128]{3,2,1,0:T(8,128)(2,1)S(1)}, u32[]{:S(2)}, u32[]{:S(2)}) collective-permute-start(bf16[8,2,128,128]{3,2,1,0:T(8,128)(2,1)} %get-tuple-element.35), channel_id=1, source_target_pairs={{0,8},{8,16},{16,24},{24,0},{1,9},{9,17},{17,25},{25,1},{2,10},{10... | collective-permute-start | bytes 1572872 | tf_op jit(solution)/shard_map/ppermute | solution.py:399
  87.3 45.6 %collective-permute-start.1 = (bf16[8,2,128,128]{3,2,1,0:T(8,128)(2,1)S(1)}, bf16[8,2,128,128]{3,2,1,0:T(8,128)(2,1)S(1)}, u32[]{:S(2)}, u32[]{:S(2)}) collective-permute-start(bf16[8,2,128,128]{3,2,1,0:T(8,128)(2,1)S(1)} %copy-done.24), channel_id=1, source_target_pairs={{0,16},{8,24},{16,0},{24,8},{1,17},{9,25},{17,1},{25,9},{2,18},{10... | collective-permute-start | bytes 1572872 | tf_op jit(solution)/shard_map/ppermute | solution.py:399
  88.5 46.1 %collective-permute-start.2 = (bf16[8,2,128,128]{3,2,1,0:T(8,128)(2,1)S(1)}, bf16[8,2,128,128]{3,2,1,0:T(8,128)(2,1)S(1)}, u32[]{:S(2)}, u32[]{:S(2)}) collective-permute-start(bf16[8,2,128,128]{3,2,1,0:T(8,128)(2,1)S(1)} %copy-done.23), channel_id=1, source_target_pairs={{0,24},{8,0},{16,8},{24,16},{1,25},{9,1},{17,9},{25,17},{2,26},{10... | collective-permute-start | bytes 1572872 | tf_op jit(solution)/shard_map/ppermute | solution.py:399
  122.2 12.5 %copy-start.10 = (bf16[8,2,128,128]{3,2,1,0:T(8,128)(2,1)}, bf16[8,2,128,128]{3,2,1,0:T(8,128)(2,1)S(1)}, u32[]{:S(2)}) copy-start(bf16[8,2,128,128]{3,2,1,0:T(8,128)(2,1)S(1)} %collective-permute-done.refs_3_.refs_1_) | copy-start | bytes 1572868
  132.8 1.8 copy-start.11
  134.6 0.8 copy-start.12
  135.4 14.2 %collective-permute-start.3 = (bf16[8,2,128,128]{3,2,1,0:T(8,128)(2,1)}, bf16[8,2,128,128]{3,2,1,0:T(8,128)(2,1)S(1)}, u32[]{:S(2)}, u32[]{:S(2)}) collective-permute-start(bf16[8,2,128,128]{3,2,1,0:T(8,128)(2,1)} %get-tuple-element.38), channel_id=1, source_target_pairs={{0,8},{8,16},{16,24},{24,0},{1,9},{9,17},{17,25},{25,1},{2,10},{10... | collective-permute-start | bytes 1572872 | tf_op jit(solution)/shard_map/ppermute | solution.py:399
  149.6 0.8 copy-start.4
  155.2 30.4 %all-to-all-start.4 = ((bf16[8,2,16,32,128]{4,3,2,1,0:T(8,128)(2,1)}), bf16[8,2,16,32,128]{4,3,2,1,0:T(8,128)(2,1)S(1)}, u32[]{:S(2)}, u32[]{:S(2)}) async-start(bf16[8,2,16,32,128]{4,3,2,1,0:T(8,128)(2,1)} %hold.9), calls=%async_computation.4 | async-start | bytes 4194304 | tf_op jit(solution)/shard_map/all_to_all | solution.py:391
  185.6 1.4 copy-start.2
  187.0 60.8 %all-to-all-start.5 = ((bf16[8,4,2,128,128]{4,3,2,1,0:T(8,128)(2,1)}), bf16[8,4,2,128,128]{4,3,2,1,0:T(8,128)(2,1)S(1)}, u32[]{:S(2)}, u32[]{:S(2)}) async-start(bf16[8,4,2,128,128]{4,3,2,1,0:T(8,128)(2,1)} %hold.10), calls=%async_computation.5 | async-start | bytes 4194304 | tf_op jit(solution)/shard_map/all_to_all | solution.py:391
  190.6 35.6 %collective-permute-start.4 = (bf16[8,2,128,128]{3,2,1,0:T(8,128)(2,1)}, bf16[8,2,128,128]{3,2,1,0:T(8,128)(2,1)S(1)}, u32[]{:S(2)}, u32[]{:S(2)}) collective-permute-start(bf16[8,2,128,128]{3,2,1,0:T(8,128)(2,1)} %get-tuple-element.43), channel_id=1, source_target_pairs={{0,16},{8,24},{16,0},{24,8},{1,17},{9,25},{17,1},{25,9},{2,18},{10... | collective-permute-start | bytes 1572872 | tf_op jit(solution)/shard_map/ppermute | solution.py:399
  191.7 36.0 %collective-permute-start.5 = (bf16[8,2,128,128]{3,2,1,0:T(8,128)(2,1)}, bf16[8,2,128,128]{3,2,1,0:T(8,128)(2,1)S(1)}, u32[]{:S(2)}, u32[]{:S(2)}) collective-permute-start(bf16[8,2,128,128]{3,2,1,0:T(8,128)(2,1)} %get-tuple-element.44), channel_id=1, source_target_pairs={{0,24},{8,0},{16,8},{24,16},{1,25},{9,1},{17,9},{25,17},{2,26},{10... | collective-permute-start | bytes 1572872 | tf_op jit(solution)/shard_map/ppermute | solution.py:399
  226.2 1.5 copy-start.13
  227.7 0.8 copy-start.14
  228.5 13.6 %collective-permute-start.6 = (bf16[8,2,128,128]{3,2,1,0:T(8,128)(2,1)}, bf16[8,2,128,128]{3,2,1,0:T(8,128)(2,1)S(1)}, u32[]{:S(2)}, u32[]{:S(2)}) collective-permute-start(bf16[8,2,128,128]{3,2,1,0:T(8,128)(2,1)} %get-tuple-element.45), channel_id=1, source_target_pairs={{0,8},{8,16},{16,24},{24,0},{1,9},{9,17},{17,25},{25,1},{2,10},{10... | collective-permute-start | bytes 1572872 | tf_op jit(solution)/shard_map/ppermute | solution.py:399
  242.1 0.9 copy-start.5
  247.7 1.3 copy-start.1
  249.1 62.1 %all-to-all-start.6 = ((bf16[8,2,16,32,128]{4,3,2,1,0:T(8,128)(2,1)}), bf16[8,2,16,32,128]{4,3,2,1,0:T(8,128)(2,1)S(1)}, u32[]{:S(2)}, u32[]{:S(2)}) async-start(bf16[8,2,16,32,128]{4,3,2,1,0:T(8,128)(2,1)} %hold.12), calls=%async_computation.6 | async-start | bytes 4194304 | tf_op jit(solution)/shard_map/all_to_all | solution.py:391
  252.8 36.5 %collective-permute-start.7 = (bf16[8,2,128,128]{3,2,1,0:T(8,128)(2,1)}, bf16[8,2,128,128]{3,2,1,0:T(8,128)(2,1)S(1)}, u32[]{:S(2)}, u32[]{:S(2)}) collective-permute-start(bf16[8,2,128,128]{3,2,1,0:T(8,128)(2,1)} %get-tuple-element.46), channel_id=1, source_target_pairs={{0,16},{8,24},{16,0},{24,8},{1,17},{9,25},{17,1},{25,9},{2,18},{10... | collective-permute-start | bytes 1572872 | tf_op jit(solution)/shard_map/ppermute | solution.py:399
  255.2 35.5 %collective-permute-start.8 = (bf16[8,2,128,128]{3,2,1,0:T(8,128)(2,1)}, bf16[8,2,128,128]{3,2,1,0:T(8,128)(2,1)S(1)}, u32[]{:S(2)}, u32[]{:S(2)}) collective-permute-start(bf16[8,2,128,128]{3,2,1,0:T(8,128)(2,1)} %get-tuple-element.47), channel_id=1, source_target_pairs={{0,24},{8,0},{16,8},{24,16},{1,25},{9,1},{17,9},{25,17},{2,26},{10... | collective-permute-start | bytes 1572872 | tf_op jit(solution)/shard_map/ppermute | solution.py:399
  289.3 1.4 copy-start.15
  290.7 0.8 copy-start.16
  291.5 14.1 %collective-permute-start.9 = (bf16[8,2,128,128]{3,2,1,0:T(8,128)(2,1)}, bf16[8,2,128,128]{3,2,1,0:T(8,128)(2,1)S(1)}, u32[]{:S(2)}, u32[]{:S(2)}) collective-permute-start(bf16[8,2,128,128]{3,2,1,0:T(8,128)(2,1)} %get-tuple-element.49), channel_id=1, source_target_pairs={{0,8},{8,16},{16,24},{24,0},{1,9},{9,17},{17,25},{25,1},{2,10},{10... | collective-permute-start | bytes 1572872 | tf_op jit(solution)/shard_map/ppermute | solution.py:399
  305.6 0.8 copy-start.6
  311.2 1.4 copy-start
  312.6 3.9 %copy-start.18 = (bf16[8,2,128,128]{3,2,1,0:T(8,128)(2,1)S(1)}, bf16[8,2,128,128]{3,2,1,0:T(8,128)(2,1)}, u32[]{:S(2)}) copy-start(bf16[8,2,128,128]{3,2,1,0:T(8,128)(2,1)} %get-tuple-element.51) | copy-start | bytes 1572868
  312.6 6.0 %copy-start.17 = (bf16[8,2,128,128]{3,2,1,0:T(8,128)(2,1)S(1)}, bf16[8,2,128,128]{3,2,1,0:T(8,128)(2,1)}, u32[]{:S(2)}) copy-start(bf16[8,2,128,128]{3,2,1,0:T(8,128)(2,1)} %get-tuple-element.52) | copy-start | bytes 1572868
  312.6 59.3 %all-to-all-start.7 = ((bf16[8,2,16,32,128]{4,3,2,1,0:T(8,128)(2,1)}), bf16[8,2,16,32,128]{4,3,2,1,0:T(8,128)(2,1)S(1)}, u32[]{:S(2)}, u32[]{:S(2)}) async-start(bf16[8,2,16,32,128]{4,3,2,1,0:T(8,128)(2,1)} %hold.13), calls=%async_computation.7 | async-start | bytes 4194304 | tf_op jit(solution)/shard_map/all_to_all | solution.py:391
  316.5 35.8 %collective-permute-start.10 = (bf16[8,2,128,128]{3,2,1,0:T(8,128)(2,1)S(1)}, bf16[8,2,128,128]{3,2,1,0:T(8,128)(2,1)S(1)}, u32[]{:S(2)}, u32[]{:S(2)}) collective-permute-start(bf16[8,2,128,128]{3,2,1,0:T(8,128)(2,1)S(1)} %copy-done.18), channel_id=1, source_target_pairs={{0,16},{8,24},{16,0},{24,8},{1,17},{9,25},{17,1},{25,9},{2,18},{10... | collective-permute-start | bytes 1572872 | tf_op jit(solution)/shard_map/ppermute | solution.py:399
  318.6 35.6 %collective-permute-start.11 = (bf16[8,2,128,128]{3,2,1,0:T(8,128)(2,1)S(1)}, bf16[8,2,128,128]{3,2,1,0:T(8,128)(2,1)S(1)}, u32[]{:S(2)}, u32[]{:S(2)}) collective-permute-start(bf16[8,2,128,128]{3,2,1,0:T(8,128)(2,1)S(1)} %copy-done.17), channel_id=1, source_target_pairs={{0,24},{8,0},{16,8},{24,16},{1,25},{9,1},{17,9},{25,17},{2,26},{10... | collective-permute-start | bytes 1572872 | tf_op jit(solution)/shard_map/ppermute | solution.py:399
  352.3 1.9 copy-start.19
  354.2 0.9 copy-start.20
  371.9 1.4 copy-start.3

commit v7 on v6

--- a/solution.py
+++ b/solution.py
@@ -16,6 +16,10 @@
 
 def params():
     return pltpu.CompilerParams(vmem_limit_bytes=VMEM_BYTES)
+
+
+def small():
+    return pl.CostEstimate(flops=1, bytes_accessed=1, transcendentals=0)
 
 
 def inner_table(size):
@@ -150,9 +154,7 @@
         out_shape=[jax.ShapeDtypeStruct((pieces, 2, rows, n), jnp.bfloat16) for n in lanes],
         scratch_shapes=[pltpu.VMEM((RADIX, block, 2 * inner), jnp.bfloat16)],
         compiler_params=params(),
-        cost_estimate=pl.CostEstimate(
-            flops=4 * rows * length * sum(lanes), bytes_accessed=8 * rows * length, transcendentals=0
-        ),
+        cost_estimate=small(),
         name="column_transform",
     )(x, jnp.asarray(twiddle_table(length)), jnp.asarray(inner_table(inner)))
 
@@ -258,11 +260,7 @@
         out_shape=out_shape + [jax.ShapeDtypeStruct(a.shape, a.dtype) for a in later],
         input_output_aliases=aliases,
         compiler_params=params(),
-        cost_estimate=pl.CostEstimate(
-            flops=12 * chans * chans * rows_dev * LANES,
-            bytes_accessed=8 * chans * rows_dev * LANES,
-            transcendentals=0,
-        ),
+        cost_estimate=small(),
         name="clean",
     )(at, x, basis, basis_t, gain, jnp.asarray(swap), jnp.asarray(back), *after, *later)
     return result[: len(out_shape)], result[len(out_shape) :]
@@ -304,11 +302,7 @@
         out_specs=pl.BlockSpec((block, 2, chans, total, LANES), lambda j: (j, 0, 0, 0, 0)),
         out_shape=jax.ShapeDtypeStruct((targets, 2, chans, total, LANES), jnp.bfloat16),
         compiler_params=params(),
-        cost_estimate=pl.CostEstimate(
-            flops=1024 * targets * chans * total * LANES,
-            bytes_accessed=8 * targets * chans * total * LANES,
-            transcendentals=0,
-        ),
+        cost_estimate=small(),
         name="row_transform",
     )(*pieces, table, *after)
 
@@ -344,11 +338,7 @@
         out_shape=jax.ShapeDtypeStruct((2, chans, total, count * groups * wide), jnp.bfloat16),
         input_output_aliases={2: 0} if held else {},
         compiler_params=params(),
-        cost_estimate=pl.CostEstimate(
-            flops=4 * pieces * chans * total * LANES * wide,
-            bytes_accessed=8 * pieces * chans * total * LANES,
-            transcendentals=0,
-        ),
+        cost_estimate=small(),
         name="place",
     )(x, jnp.asarray(table), *held)
 

time: 381 us -> 381 us (level)
  no operation moved by 1% of the time
where the time goes in v7:
time: 381 us; the launch traced here: 379 us
  waiting for transfers between devices  210 us (55%)
  Pallas kernels  106 us (28%)
  starting transfers between devices  42.1 us (11%)
  local copies, waits for them, and re-layouts  20 us (5%)
    ppermute x12, waiting for transfers between devices, spread_rows(): lax.ppermute(part, 'uv', [(z, (z + step) % count) for z in range(count)])  165 us
    all_to_all x8, waiting for transfers between devices, exchange(): return lax.all_to_all(x, 'chan', split_axis=0, concat_axis=0, tiled=True)  44.7 us
    pallas_call x4, Pallas kernels, clean(): pl.pallas_call(functools.partial(clean_kernel, len(after), len(later)), g...  33.4 us
    all_to_all x8, starting transfers between devices, exchange(): return lax.all_to_all(x, 'chan', split_axis=0, concat_axis=0, tiled=True)  31.1 us
    pallas_call x2, Pallas kernels, column_transform(): pl.pallas_call(functools.partial(column_kernel, groups), grid=(rows // bl...  27.4 us
    pallas_call x4, Pallas kernels, place(): pl.pallas_call(place_kernel, grid=(chans // block, groups), in_specs=[pl....  24.1 us
    pallas_call x4, Pallas kernels, row_transform(): pl.pallas_call(functools.partial(row_kernel, scale, group, steps), grid=(...  19.1 us
    unnamed x50, local copies, waits for them, and re-layouts  13.9 us
  transfers between devices with their start and end apart: 20, of which 15 were waited for; matrix products, arithmetic and copies ran while one was open for 1% of the time, Pallas kernels for 26%

profile of v7, /device:TPU:8, one launch (start us, length us, event | category | flops | bytes accessed | tf_op | source)
XLA Modules:
  0.0 379.2 jit_solution(13403174127320317340)
XLA Ops:
  0.0 1.7 broadcast_in_dim.2
  1.7 3.7 all-to-all-start.1
  5.4 11.9 %column_transform.2 = bf16[8,2,512,128]{3,2,1,0:T(8,128)(2,1)} custom-call(bf16[2,512,4096]{2,1,0:T(8,128)(2,1)} %bitcast.21, f32[8,2,512]{2,1,0:T(2,128)} %constant.29.clone.twiddle_ref, bf16[1024,1024]{1,0:T(8,128)(2,1)} %constant.30.clone.table_ref), custom_call_target="tpu_custom_call" | custom-call | flops 1 | bytes 1 | tf_op jit(solution)/shard_map/column_transform/pallas_call | solution.py:145
  17.3 4.2 %all-to-all-start = ((bf16[8,2,512,128]{3,2,1,0:T(8,128)(2,1)}), bf16[8,2,512,128]{3,2,1,0:T(8,128)(2,1)S(1)}, u32[]{:S(2)}, u32[]{:S(2)}) async-start(bf16[8,2,512,128]{3,2,1,0:T(8,128)(2,1)} %column_transform.2), calls=%async_computation | async-start | bytes 4194304 | tf_op jit(solution)/shard_map/all_to_all | solution.py:381
  21.5 15.5 %column_transform.3 = (bf16[8,2,512,128]{3,2,1,0:T(8,128)(2,1)}, bf16[8,2,512,256]{3,2,1,0:T(8,128)(2,1)}) custom-call(bf16[2,512,4096]{2,1,0:T(8,128)(2,1)} %bitcast.22, f32[8,2,512]{2,1,0:T(2,128)} %constant.29.clone.twiddle_ref, bf16[1024,1024]{1,0:T(8,128)(2,1)} %constant.30.clone.table_ref), custom_call_target="tpu_custom_call" | custom-call | flops 1 | bytes 1 | tf_op jit(solution)/shard_map/column_transform/pallas_call | solution.py:145
  37.0 11.1 %all-to-all-done.x_ref = bf16[8,2,512,128]{3,2,1,0:T(8,128)(2,1)S(1)} async-done(((bf16[8,2,512,128]{3,2,1,0:T(8,128)(2,1)}), bf16[8,2,512,128]{3,2,1,0:T(8,128)(2,1)S(1)}, u32[]{:S(2)}, u32[]{:S(2)}) %all-to-all-start) | async-done | bytes 2097184 | tf_op jit(solution)/shard_map/all_to_all | solution.py:381
  48.1 1.4 copy-done.7
  49.5 3.6 all-to-all-start.3
  54.0 2.1 turn.1.basis_t_ref
  56.1 8.3 %clean.4 = (bf16[8,2,128,128]{3,2,1,0:T(8,128)(2,1)}, bf16[8,2,128,128]{3,2,1,0:T(8,128)(2,1)}, bf16[8,2,128,128]{3,2,1,0:T(8,128)(2,1)}, bf16[8,2,128,128]{3,2,1,0:T(8,128)(2,1)}, bf16[8,2,512,256]{3,2,1,0:T(8,128)(2,1)}) custom-call(s32[1]{0:T(128)} %bitcast.at_ref, bf16[8,2,512,128]{3,2,1,0:T(8,128)(2,1)} %copy-done.7, ...), custom_call_target="tpu_custom_call", output_to_operand_aliasing={{4}: (7, {})} | custom-call | flops 1 | bytes 1 | tf_op jit(solution)/shard_map/clean/pallas_call | solution.py:243
  64.4 15.3 %all-to-all-done.3.x_ref = bf16[8,2,512,128]{3,2,1,0:T(8,128)(2,1)S(1)} async-done(((bf16[8,2,512,128]{3,2,1,0:T(8,128)(2,1)}), bf16[8,2,512,128]{3,2,1,0:T(8,128)(2,1)S(1)}, u32[]{:S(2)}, u32[]{:S(2)}) %all-to-all-start.3) | async-done | bytes 2097184 | tf_op jit(solution)/shard_map/all_to_all | solution.py:381
  79.7 1.4 copy-done.6
  81.0 4.6 %all-to-all-start.2 = ((bf16[8,2,512,256]{3,2,1,0:T(8,128)(2,1)}), bf16[8,2,512,256]{3,2,1,0:T(8,128)(2,1)}, u32[]{:S(2)}, u32[]{:S(2)}) async-start(bf16[8,2,512,256]{3,2,1,0:T(8,128)(2,1)} %get-tuple-element.30), calls=%async_computation.2 | async-start | bytes 8388608 | tf_op jit(solution)/shard_map/all_to_all | solution.py:381
  85.6 1.6 collective-permute-start
  88.5 1.8 collective-permute-start.2
  90.3 8.4 %clean.5 = (bf16[8,2,128,128]{3,2,1,0:T(8,128)(2,1)}, bf16[8,2,128,128]{3,2,1,0:T(8,128)(2,1)}, bf16[8,2,128,128]{3,2,1,0:T(8,128)(2,1)}, bf16[8,2,128,128]{3,2,1,0:T(8,128)(2,1)}) custom-call(s32[1]{0:T(128)} %bitcast.at_ref, bf16[8,2,512,128]{3,2,1,0:T(8,128)(2,1)} %copy-done.6, bf16[512,512]{1,0:T(8,128)(2,1)} %bitcast.25, ...), custom_call_target="tpu_custom_call" | custom-call | flops 1 | bytes 1 | tf_op jit(solution)/shard_map/clean/pallas_call | solution.py:243
  98.7 23.5 %collective-permute-done.refs_3_.refs_1_ = bf16[8,2,128,128]{3,2,1,0:T(8,128)(2,1)S(1)} collective-permute-done((bf16[8,2,128,128]{3,2,1,0:T(8,128)(2,1)}, bf16[8,2,128,128]{3,2,1,0:T(8,128)(2,1)S(1)}, u32[]{:S(2)}, u32[]{:S(2)}) %collective-permute-start) | collective-permute-done | bytes 524320 | tf_op jit(solution)/shard_map/ppermute | solution.py:389
  122.2 10.7 %collective-permute-done.1.refs_4_.refs_2_ = bf16[8,2,128,128]{3,2,1,0:T(8,128)(2,1)S(1)} collective-permute-done((bf16[8,2,128,128]{3,2,1,0:T(8,128)(2,1)S(1)}, bf16[8,2,128,128]{3,2,1,0:T(8,128)(2,1)S(1)}, u32[]{:S(2)}, u32[]{:S(2)}) %collective-permute-start.1) | collective-permute-done | bytes 524320 | tf_op jit(solution)/shard_map/ppermute | solution.py:389
  132.8 1.8 collective-permute-done.2.refs_5_.refs_3_
  135.4 1.6 dynamic-slice_bitcast_fusion.refs_4_
  137.0 12.6 %collective-permute-done.3.refs_0_.refs_3_.refs_5_.refs_1_ = bf16[8,2,128,128]{3,2,1,0:T(8,128)(2,1)S(1)} collective-permute-done((bf16[8,2,128,128]{3,2,1,0:T(8,128)(2,1)}, bf16[8,2,128,128]{3,2,1,0:T(8,128)(2,1)S(1)}, u32[]{:S(2)}, u32[]{:S(2)}) %collective-permute-start.3) | collective-permute-done | bytes 524320 | tf_op jit(solution)/shard_map/ppermute | solution.py:389
  150.4 4.8 %row_transform.4.refs_0_ = bf16[8,2,16,32,128]{4,3,2,1,0:T(8,128)(2,1)} custom-call(bf16[8,2,128,128]{3,2,1,0:T(8,128)(2,1)} %get-tuple-element.48.refs_0_, bf16[8,2,128,128]{3,2,1,0:T(8,128)(2,1)} %copy-done.10, bf16[8,2,128,128]{3,2,1,0:T(8,128)(2,1)} %copy-done.11, bf16[8,2,128,128]{3,2,1,0:T(8,128)(2,1)} %copy-done.12, ...), custom_call_target="tpu_custom_call" | custom-call | flops 1 | bytes 1 | tf_op jit(solution)/shard_map/row_transform/pallas_call | solution.py:296
  155.2 3.8 %all-to-all-start.4 = ((bf16[8,2,16,32,128]{4,3,2,1,0:T(8,128)(2,1)}), bf16[8,2,16,32,128]{4,3,2,1,0:T(8,128)(2,1)S(1)}, u32[]{:S(2)}, u32[]{:S(2)}) async-start(bf16[8,2,16,32,128]{4,3,2,1,0:T(8,128)(2,1)} %hold.9), calls=%async_computation.4 | async-start | bytes 4194304 | tf_op jit(solution)/shard_map/all_to_all | solution.py:381
  159.0 8.3 %clean.7.refs_0_ = bf16[8,4,2,128,128]{4,3,2,1,0:T(8,128)(2,1)} custom-call(s32[1]{0:T(128)} %bitcast.at_ref, bf16[8,2,512,256]{3,2,1,0:T(8,128)(2,1)} %all-to-all-done.2.x_ref.refs_1_, bf16[512,512]{1,0:T(8,128)(2,1)} %bitcast.26, bf16[512,512]{1,0:T(8,128)(2,1)} %turn.1.basis_t_ref, f32[512,8]{1,0:T(8,128)} %add_divide_fusion.gain_ref, ...), custom_call_target="tpu_custom_call" | custom-call | flops 1 | bytes 1 | tf_op jit(solution)/shard_map/clean/pallas_call | solution.py:243
  167.3 18.3 %all-to-all-done.4.refs_1_.x_ref = bf16[8,2,16,32,128]{4,3,2,1,0:T(8,128)(2,1)S(1)} async-done(((bf16[8,2,16,32,128]{4,3,2,1,0:T(8,128)(2,1)}), bf16[8,2,16,32,128]{4,3,2,1,0:T(8,128)(2,1)S(1)}, u32[]{:S(2)}, u32[]{:S(2)}) %all-to-all-start.4) | async-done | bytes 2097184 | tf_op jit(solution)/shard_map/all_to_all | solution.py:381
  185.6 1.4 copy-done.3
  187.0 3.6 all-to-all-start.5
  192.4 8.4 %clean.6 = (bf16[8,2,128,128]{3,2,1,0:T(8,128)(2,1)}, bf16[8,2,128,128]{3,2,1,0:T(8,128)(2,1)}, bf16[8,2,128,128]{3,2,1,0:T(8,128)(2,1)}, bf16[8,2,128,128]{3,2,1,0:T(8,128)(2,1)}) custom-call(s32[1]{0:T(128)} %bitcast.at_ref, bf16[8,2,512,256]{3,2,1,0:T(8,128)(2,1)} %all-to-all-done.2.x_ref.refs_1_, bf16[512,512]{1,0:T(8,128)(2,1)} %bitcast.27, ...), custom_call_target="tpu_custom_call" | custom-call | flops 1 | bytes 1 | tf_op jit(solution)/shard_map/clean/pallas_call | solution.py:243
  200.8 25.4 %collective-permute-done.4.refs_4_.refs_2_ = bf16[8,2,128,128]{3,2,1,0:T(8,128)(2,1)S(1)} collective-permute-done((bf16[8,2,128,128]{3,2,1,0:T(8,128)(2,1)}, bf16[8,2,128,128]{3,2,1,0:T(8,128)(2,1)S(1)}, u32[]{:S(2)}, u32[]{:S(2)}) %collective-permute-start.4) | collective-permute-done | bytes 524320 | tf_op jit(solution)/shard_map/ppermute | solution.py:389
  226.2 1.5 collective-permute-done.5.refs_5_.refs_3_
  228.5 13.6 %collective-permute-done.6.refs_3_.refs_1_.refs_5_ = bf16[8,2,128,128]{3,2,1,0:T(8,128)(2,1)S(1)} collective-permute-done((bf16[8,2,128,128]{3,2,1,0:T(8,128)(2,1)}, bf16[8,2,128,128]{3,2,1,0:T(8,128)(2,1)S(1)}, u32[]{:S(2)}, u32[]{:S(2)}) %collective-permute-start.6) | collective-permute-done | bytes 524320 | tf_op jit(solution)/shard_map/ppermute | solution.py:389
  243.0 4.8 %row_transform.6.refs_0_ = bf16[8,2,16,32,128]{4,3,2,1,0:T(8,128)(2,1)} custom-call(bf16[8,2,128,128]{3,2,1,0:T(8,128)(2,1)} %get-tuple-element.50.refs_0_, bf16[8,2,128,128]{3,2,1,0:T(8,128)(2,1)} %copy-done.4, bf16[8,2,128,128]{3,2,1,0:T(8,128)(2,1)} %copy-done.13, bf16[8,2,128,128]{3,2,1,0:T(8,128)(2,1)} %copy-done.14, ...), custom_call_target="tpu_custom_call" | custom-call | flops 1 | bytes 1 | tf_op jit(solution)/shard_map/row_transform/pallas_call | solution.py:296
  249.1 3.7 all-to-all-start.6
  252.8 2.4 collective-permute-start.7
  255.2 2.9 slice_bitcast_fusion
  258.1 31.2 %collective-permute-done.7.refs_4_.refs_2_ = bf16[8,2,128,128]{3,2,1,0:T(8,128)(2,1)S(1)} collective-permute-done((bf16[8,2,128,128]{3,2,1,0:T(8,128)(2,1)}, bf16[8,2,128,128]{3,2,1,0:T(8,128)(2,1)S(1)}, u32[]{:S(2)}, u32[]{:S(2)}) %collective-permute-start.7) | collective-permute-done | bytes 524320 | tf_op jit(solution)/shard_map/ppermute | solution.py:389
  289.3 1.4 collective-permute-done.8.refs_5_.refs_3_
  291.5 14.1 %collective-permute-done.9.refs_5_.refs_1_ = bf16[8,2,128,128]{3,2,1,0:T(8,128)(2,1)S(1)} collective-permute-done((bf16[8,2,128,128]{3,2,1,0:T(8,128)(2,1)}, bf16[8,2,128,128]{3,2,1,0:T(8,128)(2,1)S(1)}, u32[]{:S(2)}, u32[]{:S(2)}) %collective-permute-start.9) | collective-permute-done | bytes 524320 | tf_op jit(solution)/shard_map/ppermute | solution.py:389
  306.4 4.8 %row_transform.5.refs_0_ = bf16[8,2,16,32,128]{4,3,2,1,0:T(8,128)(2,1)} custom-call(bf16[8,2,128,128]{3,2,1,0:T(8,128)(2,1)} %get-tuple-element.39.refs_0_, bf16[8,2,128,128]{3,2,1,0:T(8,128)(2,1)} %copy-done.8, bf16[8,2,128,128]{3,2,1,0:T(8,128)(2,1)} %copy-done.15, bf16[8,2,128,128]{3,2,1,0:T(8,128)(2,1)} %copy-done.16, ...), custom_call_target="tpu_custom_call" | custom-call | flops 1 | bytes 1 | tf_op jit(solution)/shard_map/row_transform/pallas_call | solution.py:296
  312.6 3.9 %all-to-all-start.7 = ((bf16[8,2,16,32,128]{4,3,2,1,0:T(8,128)(2,1)}), bf16[8,2,16,32,128]{4,3,2,1,0:T(8,128)(2,1)S(1)}, u32[]{:S(2)}, u32[]{:S(2)}) async-start(bf16[8,2,16,32,128]{4,3,2,1,0:T(8,128)(2,1)} %hold.13), calls=%async_computation.7 | async-start | bytes 4194304 | tf_op jit(solution)/shard_map/all_to_all | solution.py:381
  316.5 2.1 collective-permute-start.10
  318.6 6.0 %place.4.refs_0_ = bf16[2,16,32,4096]{3,2,1,0:T(8,128)(2,1)} custom-call(bf16[8,2,16,32,128]{4,3,2,1,0:T(8,128)(2,1)} %copy-done.3, bf16[1024,1024]{1,0:T(8,128)(2,1)} %constant.34.clone.table_ref), custom_call_target="tpu_custom_call" | custom-call | flops 1 | bytes 1 | tf_op jit(solution)/shard_map/place/pallas_call | solution.py:327
  324.6 27.7 %collective-permute-done.10.refs_2_ = bf16[8,2,128,128]{3,2,1,0:T(8,128)(2,1)S(1)} collective-permute-done((bf16[8,2,128,128]{3,2,1,0:T(8,128)(2,1)S(1)}, bf16[8,2,128,128]{3,2,1,0:T(8,128)(2,1)S(1)}, u32[]{:S(2)}, u32[]{:S(2)}) %collective-permute-start.10) | collective-permute-done | bytes 524320 | tf_op jit(solution)/shard_map/ppermute | solution.py:389
  352.3 1.9 collective-permute-done.11.refs_3_
  355.1 4.8 %row_transform.7.x_ref = bf16[8,2,16,32,128]{4,3,2,1,0:T(8,128)(2,1)} custom-call(bf16[8,2,128,128]{3,2,1,0:T(8,128)(2,1)} %get-tuple-element.53.refs_0_, bf16[8,2,128,128]{3,2,1,0:T(8,128)(2,1)} %copy-done.9, bf16[8,2,128,128]{3,2,1,0:T(8,128)(2,1)} %copy-done.19, bf16[8,2,128,128]{3,2,1,0:T(8,128)(2,1)} %copy-done.20, ...), custom_call_target="tpu_custom_call" | custom-call | flops 1 | bytes 1 | tf_op jit(solution)/shard_map/row_transform/pallas_call | solution.py:296
  359.9 6.0 %place.5.refs_0_ = bf16[2,16,32,4096]{3,2,1,0:T(8,128)(2,1)} custom-call(bf16[8,2,16,32,128]{4,3,2,1,0:T(8,128)(2,1)} %copy-done, bf16[1024,1024]{1,0:T(8,128)(2,1)} %constant.34.clone.table_ref, bf16[2,16,32,4096]{3,2,1,0:T(8,128)(2,1)} %place.4.refs_0_), custom_call_target="tpu_custom_call", output_to_operand_aliasing={{}: (2, {})} | custom-call | flops 1 | bytes 1 | tf_op jit(solution)/shard_map/place/pallas_call | solution.py:327
  365.9 6.0 %place.6.refs_0_ = bf16[2,16,32,4096]{3,2,1,0:T(8,128)(2,1)} custom-call(bf16[8,2,16,32,128]{4,3,2,1,0:T(8,128)(2,1)} %row_transform.7.x_ref, bf16[1024,1024]{1,0:T(8,128)(2,1)} %constant.34.clone.table_ref, bf16[2,16,32,4096]{3,2,1,0:T(8,128)(2,1)} %place.5.refs_0_), custom_call_target="tpu_custom_call", output_to_operand_aliasing={{}: (2, {})} | custom-call | flops 1 | bytes 1 | tf_op jit(solution)/shard_map/place/pallas_call | solution.py:327
  373.2 6.0 %place.7 = bf16[2,16,32,4096]{3,2,1,0:T(8,128)(2,1)} custom-call(bf16[8,2,16,32,128]{4,3,2,1,0:T(8,128)(2,1)} %copy-done.5, bf16[1024,1024]{1,0:T(8,128)(2,1)} %constant.34.clone.table_ref, bf16[2,16,32,4096]{3,2,1,0:T(8,128)(2,1)} %place.6.refs_0_), custom_call_target="tpu_custom_call", output_to_operand_aliasing={{}: (2, {})} | custom-call | flops 1 | bytes 1 | tf_op jit(solution)/shard_map/place/pallas_call | solution.py:327
  (68 shorter events, 13.7 us)
Async XLA Ops:
  1.7 15.6 %all-to-all-start.1 = ((bf16[8,64,512]{2,1,0:T(8,128)(2,1)}), bf16[8,64,512]{2,1,0:T(8,128)(2,1)S(1)}, u32[]{:S(2)}, u32[]{:S(2)}) async-start(bf16[8,64,512]{2,1,0:T(8,128)(2,1)} %broadcast_in_dim.2), calls=%async_computation.1 | async-start | bytes 1048576 | tf_op jit(solution)/shard_map/all_to_all | solution.py:381
  17.3 19.7 %copy-start.2 = (bf16[8,64,512]{2,1,0:T(8,128)(2,1)}, bf16[8,64,512]{2,1,0:T(8,128)(2,1)S(1)}, u32[]{:S(2)}) copy-start(bf16[8,64,512]{2,1,0:T(8,128)(2,1)S(1)} %all-to-all-done.1) | copy-start | bytes 1572868
  17.3 30.8 %all-to-all-start = ((bf16[8,2,512,128]{3,2,1,0:T(8,128)(2,1)}), bf16[8,2,512,128]{3,2,1,0:T(8,128)(2,1)S(1)}, u32[]{:S(2)}, u32[]{:S(2)}) async-start(bf16[8,2,512,128]{3,2,1,0:T(8,128)(2,1)} %column_transform.2), calls=%async_computation | async-start | bytes 4194304 | tf_op jit(solution)/shard_map/all_to_all | solution.py:381
  48.1 1.4 copy-start.7
  48.1 5.0 %copy-start.21 = (f32[512]{0:T(512)S(1)}, f32[512]{0:T(512)}, u32[]{:S(2)}) copy-start(f32[512]{0:T(512)} %param.26) | copy-start | bytes 6148
  48.1 5.0 %copy-start.22 = (f32[8]{0:T(128)S(1)}, f32[8]{0:T(128)}, u32[]{:S(2)}) copy-start(f32[8]{0:T(128)} %param.27) | copy-start | bytes 100
  49.5 30.2 %all-to-all-start.3 = ((bf16[8,2,512,128]{3,2,1,0:T(8,128)(2,1)}), bf16[8,2,512,128]{3,2,1,0:T(8,128)(2,1)S(1)}, u32[]{:S(2)}, u32[]{:S(2)}) async-start(bf16[8,2,512,128]{3,2,1,0:T(8,128)(2,1)} %get-tuple-element.31), calls=%async_computation.3 | async-start | bytes 4194304 | tf_op jit(solution)/shard_map/all_to_all | solution.py:381
  79.7 1.4 copy-start.6
  79.7 7.6 %copy-start.24 = (bf16[8,2,128,128]{3,2,1,0:T(8,128)(2,1)S(1)}, bf16[8,2,128,128]{3,2,1,0:T(8,128)(2,1)}, u32[]{:S(2)}) copy-start(bf16[8,2,128,128]{3,2,1,0:T(8,128)(2,1)} %get-tuple-element.36) | copy-start | bytes 1572868
  79.7 8.8 %copy-start.23 = (bf16[8,2,128,128]{3,2,1,0:T(8,128)(2,1)S(1)}, bf16[8,2,128,128]{3,2,1,0:T(8,128)(2,1)}, u32[]{:S(2)}) copy-start(bf16[8,2,128,128]{3,2,1,0:T(8,128)(2,1)} %get-tuple-element.37) | copy-start | bytes 1572868
  81.0 74.2 %all-to-all-start.2 = ((bf16[8,2,512,256]{3,2,1,0:T(8,128)(2,1)}), bf16[8,2,512,256]{3,2,1,0:T(8,128)(2,1)}, u32[]{:S(2)}, u32[]{:S(2)}) async-start(bf16[8,2,512,256]{3,2,1,0:T(8,128)(2,1)} %get-tuple-element.30), calls=%async_computation.2 | async-start | bytes 8388608 | tf_op jit(solution)/shard_map/all_to_all | solution.py:381
  85.6 36.5 %collective-permute-start = (bf16[8,2,128,128]{3,2,1,0:T(8,128)(2,1)}, bf16[8,2,128,128]{3,2,1,0:T(8,128)(2,1)S(1)}, u32[]{:S(2)}, u32[]{:S(2)}) collective-permute-start(bf16[8,2,128,128]{3,2,1,0:T(8,128)(2,1)} %get-tuple-element.35), channel_id=1, source_target_pairs={{0,8},{8,16},{16,24},{24,0},{1,9},{9,17},{17,25},{25,1},{2,10},{10... | collective-permute-start | bytes 1572872 | tf_op jit(solution)/shard_map/ppermute | solution.py:389
  87.3 45.6 %collective-permute-start.1 = (bf16[8,2,128,128]{3,2,1,0:T(8,128)(2,1)S(1)}, bf16[8,2,128,128]{3,2,1,0:T(8,128)(2,1)S(1)}, u32[]{:S(2)}, u32[]{:S(2)}) collective-permute-start(bf16[8,2,128,128]{3,2,1,0:T(8,128)(2,1)S(1)} %copy-done.24), channel_id=1, source_target_pairs={{0,16},{8,24},{16,0},{24,8},{1,17},{9,25},{17,1},{25,9},{2,18},{10... | collective-permute-start | bytes 1572872 | tf_op jit(solution)/shard_map/ppermute | solution.py:389
  88.5 46.1 %collective-permute-start.2 = (bf16[8,2,128,128]{3,2,1,0:T(8,128)(2,1)S(1)}, bf16[8,2,128,128]{3,2,1,0:T(8,128)(2,1)S(1)}, u32[]{:S(2)}, u32[]{:S(2)}) collective-permute-start(bf16[8,2,128,128]{3,2,1,0:T(8,128)(2,1)S(1)} %copy-done.23), channel_id=1, source_target_pairs={{0,24},{8,0},{16,8},{24,16},{1,25},{9,1},{17,9},{25,17},{2,26},{10... | collective-permute-start | bytes 1572872 | tf_op jit(solution)/shard_map/ppermute | solution.py:389
  122.2 12.5 %copy-start.10 = (bf16[8,2,128,128]{3,2,1,0:T(8,128)(2,1)}, bf16[8,2,128,128]{3,2,1,0:T(8,128)(2,1)S(1)}, u32[]{:S(2)}) copy-start(bf16[8,2,128,128]{3,2,1,0:T(8,128)(2,1)S(1)} %collective-permute-done.refs_3_.refs_1_) | copy-start | bytes 1572868
  132.8 1.8 copy-start.11
  134.6 0.8 copy-start.12
  135.4 14.2 %collective-permute-start.3 = (bf16[8,2,128,128]{3,2,1,0:T(8,128)(2,1)}, bf16[8,2,128,128]{3,2,1,0:T(8,128)(2,1)S(1)}, u32[]{:S(2)}, u32[]{:S(2)}) collective-permute-start(bf16[8,2,128,128]{3,2,1,0:T(8,128)(2,1)} %get-tuple-element.38), channel_id=1, source_target_pairs={{0,8},{8,16},{16,24},{24,0},{1,9},{9,17},{17,25},{25,1},{2,10},{10... | collective-permute-start | bytes 1572872 | tf_op jit(solution)/shard_map/ppermute | solution.py:389
  149.6 0.8 copy-start.4
  155.2 30.4 %all-to-all-start.4 = ((bf16[8,2,16,32,128]{4,3,2,1,0:T(8,128)(2,1)}), bf16[8,2,16,32,128]{4,3,2,1,0:T(8,128)(2,1)S(1)}, u32[]{:S(2)}, u32[]{:S(2)}) async-start(bf16[8,2,16,32,128]{4,3,2,1,0:T(8,128)(2,1)} %hold.9), calls=%async_computation.4 | async-start | bytes 4194304 | tf_op jit(solution)/shard_map/all_to_all | solution.py:381
  185.6 1.4 copy-start.3
  187.0 60.8 %all-to-all-start.5 = ((bf16[8,4,2,128,128]{4,3,2,1,0:T(8,128)(2,1)}), bf16[8,4,2,128,128]{4,3,2,1,0:T(8,128)(2,1)S(1)}, u32[]{:S(2)}, u32[]{:S(2)}) async-start(bf16[8,4,2,128,128]{4,3,2,1,0:T(8,128)(2,1)} %hold.10), calls=%async_computation.5 | async-start | bytes 4194304 | tf_op jit(solution)/shard_map/all_to_all | solution.py:381
  190.6 35.6 %collective-permute-start.4 = (bf16[8,2,128,128]{3,2,1,0:T(8,128)(2,1)}, bf16[8,2,128,128]{3,2,1,0:T(8,128)(2,1)S(1)}, u32[]{:S(2)}, u32[]{:S(2)}) collective-permute-start(bf16[8,2,128,128]{3,2,1,0:T(8,128)(2,1)} %get-tuple-element.43), channel_id=1, source_target_pairs={{0,16},{8,24},{16,0},{24,8},{1,17},{9,25},{17,1},{25,9},{2,18},{10... | collective-permute-start | bytes 1572872 | tf_op jit(solution)/shard_map/ppermute | solution.py:389
  191.7 36.0 %collective-permute-start.5 = (bf16[8,2,128,128]{3,2,1,0:T(8,128)(2,1)}, bf16[8,2,128,128]{3,2,1,0:T(8,128)(2,1)S(1)}, u32[]{:S(2)}, u32[]{:S(2)}) collective-permute-start(bf16[8,2,128,128]{3,2,1,0:T(8,128)(2,1)} %get-tuple-element.44), channel_id=1, source_target_pairs={{0,24},{8,0},{16,8},{24,16},{1,25},{9,1},{17,9},{25,17},{2,26},{10... | collective-permute-start | bytes 1572872 | tf_op jit(solution)/shard_map/ppermute | solution.py:389
  226.2 1.5 copy-start.13
  227.7 0.8 copy-start.14
  228.5 13.6 %collective-permute-start.6 = (bf16[8,2,128,128]{3,2,1,0:T(8,128)(2,1)}, bf16[8,2,128,128]{3,2,1,0:T(8,128)(2,1)S(1)}, u32[]{:S(2)}, u32[]{:S(2)}) collective-permute-start(bf16[8,2,128,128]{3,2,1,0:T(8,128)(2,1)} %get-tuple-element.45), channel_id=1, source_target_pairs={{0,8},{8,16},{16,24},{24,0},{1,9},{9,17},{17,25},{25,1},{2,10},{10... | collective-permute-start | bytes 1572872 | tf_op jit(solution)/shard_map/ppermute | solution.py:389
  242.1 0.9 copy-start.8
  247.7 1.3 copy-start.1
  249.1 62.1 %all-to-all-start.6 = ((bf16[8,2,16,32,128]{4,3,2,1,0:T(8,128)(2,1)}), bf16[8,2,16,32,128]{4,3,2,1,0:T(8,128)(2,1)S(1)}, u32[]{:S(2)}, u32[]{:S(2)}) async-start(bf16[8,2,16,32,128]{4,3,2,1,0:T(8,128)(2,1)} %hold.12), calls=%async_computation.6 | async-start | bytes 4194304 | tf_op jit(solution)/shard_map/all_to_all | solution.py:381
  252.8 36.5 %collective-permute-start.7 = (bf16[8,2,128,128]{3,2,1,0:T(8,128)(2,1)}, bf16[8,2,128,128]{3,2,1,0:T(8,128)(2,1)S(1)}, u32[]{:S(2)}, u32[]{:S(2)}) collective-permute-start(bf16[8,2,128,128]{3,2,1,0:T(8,128)(2,1)} %get-tuple-element.46), channel_id=1, source_target_pairs={{0,16},{8,24},{16,0},{24,8},{1,17},{9,25},{17,1},{25,9},{2,18},{10... | collective-permute-start | bytes 1572872 | tf_op jit(solution)/shard_map/ppermute | solution.py:389
  255.2 35.5 %collective-permute-start.8 = (bf16[8,2,128,128]{3,2,1,0:T(8,128)(2,1)}, bf16[8,2,128,128]{3,2,1,0:T(8,128)(2,1)S(1)}, u32[]{:S(2)}, u32[]{:S(2)}) collective-permute-start(bf16[8,2,128,128]{3,2,1,0:T(8,128)(2,1)} %get-tuple-element.47), channel_id=1, source_target_pairs={{0,24},{8,0},{16,8},{24,16},{1,25},{9,1},{17,9},{25,17},{2,26},{10... | collective-permute-start | bytes 1572872 | tf_op jit(solution)/shard_map/ppermute | solution.py:389
  289.3 1.4 copy-start.15
  290.7 0.8 copy-start.16
  291.5 14.1 %collective-permute-start.9 = (bf16[8,2,128,128]{3,2,1,0:T(8,128)(2,1)}, bf16[8,2,128,128]{3,2,1,0:T(8,128)(2,1)S(1)}, u32[]{:S(2)}, u32[]{:S(2)}) collective-permute-start(bf16[8,2,128,128]{3,2,1,0:T(8,128)(2,1)} %get-tuple-element.49), channel_id=1, source_target_pairs={{0,8},{8,16},{16,24},{24,0},{1,9},{9,17},{17,25},{25,1},{2,10},{10... | collective-permute-start | bytes 1572872 | tf_op jit(solution)/shard_map/ppermute | solution.py:389
  305.6 0.8 copy-start.9
  311.2 1.4 copy-start
  312.6 3.9 %copy-start.18 = (bf16[8,2,128,128]{3,2,1,0:T(8,128)(2,1)S(1)}, bf16[8,2,128,128]{3,2,1,0:T(8,128)(2,1)}, u32[]{:S(2)}) copy-start(bf16[8,2,128,128]{3,2,1,0:T(8,128)(2,1)} %get-tuple-element.51) | copy-start | bytes 1572868
  312.6 6.0 %copy-start.17 = (bf16[8,2,128,128]{3,2,1,0:T(8,128)(2,1)S(1)}, bf16[8,2,128,128]{3,2,1,0:T(8,128)(2,1)}, u32[]{:S(2)}) copy-start(bf16[8,2,128,128]{3,2,1,0:T(8,128)(2,1)} %get-tuple-element.52) | copy-start | bytes 1572868
  312.6 59.3 %all-to-all-start.7 = ((bf16[8,2,16,32,128]{4,3,2,1,0:T(8,128)(2,1)}), bf16[8,2,16,32,128]{4,3,2,1,0:T(8,128)(2,1)S(1)}, u32[]{:S(2)}, u32[]{:S(2)}) async-start(bf16[8,2,16,32,128]{4,3,2,1,0:T(8,128)(2,1)} %hold.13), calls=%async_computation.7 | async-start | bytes 4194304 | tf_op jit(solution)/shard_map/all_to_all | solution.py:381
  316.5 35.8 %collective-permute-start.10 = (bf16[8,2,128,128]{3,2,1,0:T(8,128)(2,1)S(1)}, bf16[8,2,128,128]{3,2,1,0:T(8,128)(2,1)S(1)}, u32[]{:S(2)}, u32[]{:S(2)}) collective-permute-start(bf16[8,2,128,128]{3,2,1,0:T(8,128)(2,1)S(1)} %copy-done.18), channel_id=1, source_target_pairs={{0,16},{8,24},{16,0},{24,8},{1,17},{9,25},{17,1},{25,9},{2,18},{10... | collective-permute-start | bytes 1572872 | tf_op jit(solution)/shard_map/ppermute | solution.py:389
  318.6 35.6 %collective-permute-start.11 = (bf16[8,2,128,128]{3,2,1,0:T(8,128)(2,1)S(1)}, bf16[8,2,128,128]{3,2,1,0:T(8,128)(2,1)S(1)}, u32[]{:S(2)}, u32[]{:S(2)}) collective-permute-start(bf16[8,2,128,128]{3,2,1,0:T(8,128)(2,1)S(1)} %copy-done.17), channel_id=1, source_target_pairs={{0,24},{8,0},{16,8},{24,16},{1,25},{9,1},{17,9},{25,17},{2,26},{10... | collective-permute-start | bytes 1572872 | tf_op jit(solution)/shard_map/ppermute | solution.py:389
  352.3 1.9 copy-start.19
  354.2 0.9 copy-start.20
  371.9 1.4 copy-start.5

commit v8 on v1

v8 whole, which is shorter than its diff:
```python
import functools
import math

import jax
import jax.numpy as jnp
import numpy as np
from jax import lax
from jax.experimental import pallas as pl
from jax.experimental.pallas import tpu as pltpu
from jax.sharding import PartitionSpec as P

LANES = 128
RADIX = 8
VMEM_BYTES = 56 * 1024 * 1024


def params():
    return pltpu.CompilerParams(vmem_limit_bytes=VMEM_BYTES)


def inner_table(size):
    position = np.arange(size)
    phase = 2.0 * np.pi * (np.outer(position, position) % size) / size
    cosine, sine = np.cos(phase), np.sin(phase)
    return np.block([[cosine, sine], [-sine, cosine]]).astype(jnp.bfloat16)


def twiddle_table(length):
    inner = length // RADIX
    phase = 2.0 * np.pi * np.outer(np.arange(RADIX), np.arange(inner)) / length
    return np.stack([np.cos(phase), np.sin(phase)], axis=1).astype(np.float32)


def order_table():
    table = np.zeros((RADIX, LANES, LANES, RADIX), np.float32)
    for y_lo in range(RADIX):
        for y_hi in range(LANES):
            table[y_lo, y_hi, y_hi, y_lo] = 1.0
    return table.reshape(RADIX * LANES, RADIX * LANES).astype(jnp.bfloat16)


def swap_table(major, minor):
    table = np.zeros((major * minor, major * minor), np.float32)
    for a in range(major):
        for b in range(minor):
            table[b * major + a, a * minor + b] = 1.0
    return table.astype(jnp.bfloat16)


def row_table(rows_dev, uv_count, group):
    total = rows_dev * uv_count
    position = np.arange(total)
    phase = 2.0 * np.pi * (np.outer(position, position) % total) / total
    cosine, sine = np.cos(phase), np.sin(phase)
    parts = np.array([[cosine, -sine], [sine, cosine]])
    parts = parts.reshape(2, 2, total, uv_count, rows_dev)
    size = 2 * group * total
    table = np.einsum("tsxzu,cd->tcxzsdu", parts, np.eye(group))
    return table.reshape(size, size).astype(jnp.bfloat16)


def butterfly8(re, im):
    def dft2(ar, ai, br, bi):
        return ar + br, ai + bi, ar - br, ai - bi

    def dft4(r, i):
        s0r, s0i, d0r, d0i = dft2(r[0], i[0], r[2], i[2])
        s1r, s1i, d1r, d1i = dft2(r[1], i[1], r[3], i[3])
        return (
            [s0r + s1r, d0r - d1i, s0r - s1r, d0r + d1i],
            [s0i + s1i, d0i + d1r, s0i - s1i, d0i - d1r],
        )

    er, ei = dft4(re[0::2], im[0::2])
    orr, oi = dft4(re[1::2], im[1::2])
    half = math.sqrt(0.5)
    turned_r = [orr[0], (orr[1] - oi[1]) * half, -oi[2], (-orr[3] - oi[3]) * half]
    turned_i = [oi[0], (orr[1] + oi[1]) * half, orr[2], (orr[3] - oi[3]) * half]
    out_r = [er[k] + turned_r[k] for k in range(4)] + [er[k] - turned_r[k] for k in range(4)]
    out_i = [ei[k] + turned_i[k] for k in range(4)] + [ei[k] - turned_i[k] for k in range(4)]
    return out_r, out_i


def column_kernel(chunks, spread, split, at_ref, x_ref, twiddle_ref, table_ref, *refs):
    if split:
        *out_refs, mid, stage = refs
    else:
        *out_refs, mid = refs
    rows, length = x_ref.shape[1:]
    inner = length // RADIX
    step = 16
    for i in range(rows // step):
        at = slice(i * step, (i + 1) * step)
        for block in range(inner // LANES):
            re, im = [], []
            for a in range(RADIX):
                lanes = slice(a * inner + block * LANES, a * inner + (block + 1) * LANES)
                re.append(x_ref[0, at, lanes].astype(jnp.float32))
                im.append(x_ref[1, at, lanes].astype(jnp.float32))
            re, im = butterfly8(re, im)
            lanes = slice(block * LANES, (block + 1) * LANES)
            other = slice(inner + block * LANES, inner + (block + 1) * LANES)
            for y_lo in range(RADIX):
                if y_lo == 0:
                    tr, ti = re[0], im[0]
                else:
                    cosine = twiddle_ref[y_lo, 0:1, lanes]
                    sine = twiddle_ref[y_lo, 1:2, lanes]
                    tr = re[y_lo] * cosine - im[y_lo] * sine
                    ti = re[y_lo] * sine + im[y_lo] * cosine
                mid[y_lo, at, lanes] = tr.astype(jnp.bfloat16)
                mid[y_lo, at, other] = ti.astype(jnp.bfloat16)
    for n, chunk in enumerate(chunks):
        for group in range(spread):
            column = (chunk * spread + group) * LANES
            table = jnp.concatenate(
                [table_ref[:, at : at + LANES] for at in (column, inner + column)], axis=1
            )
            wide = jnp.dot(
                mid[...].reshape(RADIX * rows, 2 * inner), table, preferred_element_type=jnp.float32
            ).astype(jnp.bfloat16)
            for y_lo in range(RADIX):
                for part in range(2):
                    value = wide[y_lo * rows : (y_lo + 1) * rows, part * LANES : (part + 1) * LANES]
                    if split:
                        stage[group * RADIX + y_lo, part] = value
                    else:
                        out_refs[n][group * RADIX + y_lo, part] = value
        if split:
            pieces = spread * RADIX
            for step in range(pieces):
                out_refs[n * pieces + step][...] = stage[partner(at_ref[0], step, pieces)]


def partner(at, step, count):
    if count & (count - 1):
        return (count - at + step) % count
    return at ^ step


def column_transform(x, at, pieces, chunks, split):
    _, rows, length = x.shape
    inner = length // RADIX
    block = math.gcd(rows, 64)
    if split:
        spec = pl.BlockSpec((2, block, LANES), lambda i, at: (0, i, 0))
        shape = jax.ShapeDtypeStruct((2, rows, LANES), jnp.bfloat16)
        stage = [pltpu.VMEM((pieces, 2, block, LANES), jnp.bfloat16)]
        outs = len(chunks) * pieces
    else:
        spec = pl.BlockSpec((pieces, 2, block, LANES), lambda i, at: (0, 0, i, 0))
        shape = jax.ShapeDtypeStruct((pieces, 2, rows, LANES), jnp.bfloat16)
        stage = []
        outs = len(chunks)
    return pl.pallas_call(
        functools.partial(column_kernel, chunks, pieces // RADIX, split),
        grid_spec=pltpu.PrefetchScalarGridSpec(
            num_scalar_prefetch=1,
            grid=(rows // block,),
            in_specs=[
                pl.BlockSpec((2, block, length), lambda i, at: (0, i, 0)),
                pl.BlockSpec((RADIX, 2, inner), lambda i, at: (0, 0, 0)),
                pl.BlockSpec((2 * inner, 2 * inner), lambda i, at: (0, 0)),
            ],
            out_specs=[spec] * outs,
            scratch_shapes=[pltpu.VMEM((RADIX, block, 2 * inner), jnp.bfloat16)] + stage,
        ),
        out_shape=[shape] * outs,
        compiler_params=params(),
        cost_estimate=pl.CostEstimate(
            flops=4 * rows * length * LANES * pieces * len(chunks),
            bytes_accessed=8 * rows * length,
            transcendentals=0,
        ),
        name="column_transform",
    )(at, x, jnp.asarray(twiddle_table(length)), jnp.asarray(inner_table(inner)))


def clean_kernel(split, at_ref, *refs):
    *x_refs, basis_ref, basis_t_ref, gain_ref, swap_ref, back_ref, out_ref, slab = refs
    chans = slab.shape[0]
    rows_dev = slab.shape[1] // LANES
    tall = swap_ref.shape[0]
    group = tall // rows_dev
    sources = len(x_refs) if split else x_refs[0].shape[0]
    own = chans // sources
    for source in range(sources):
        block = x_refs[source].at[0] if split else x_refs[0].at[source, 0]
        begin = partner(at_ref[0], source, sources) * own if split else source * own
        for k in range(own // group):
            turned = jnp.dot(
                swap_ref[...], block[k * tall : (k + 1) * tall, :], preferred_element_type=jnp.float32
            ).astype(jnp.bfloat16)
            channels = pl.ds(pl.multiple_of(begin + k * group, group), group)
            for u in range(rows_dev):
                slab[channels, u * LANES : (u + 1) * LANES] = turned[u * group : (u + 1) * group]
    pair = math.gcd(rows_dev, 2)
    for first in range(0, rows_dev, pair):
        lanes = slice(first * LANES, (first + pair) * LANES)
        line = slab[:, lanes]
        amps = jnp.dot(basis_t_ref[...], line, preferred_element_type=jnp.float32)
        amps = amps.astype(jnp.bfloat16).astype(jnp.float32)
        front = jnp.concatenate(
            [
                gain_ref[:, first + k : first + k + 1] * amps[:, k * LANES : (k + 1) * LANES]
                for k in range(pair)
            ],
            axis=1,
        ).astype(jnp.bfloat16)
        drop = jnp.dot(basis_ref[...], front, preferred_element_type=jnp.float32)
        slab[:, lanes] = (line.astype(jnp.float32) - drop).astype(jnp.bfloat16)
    out_rows = out_ref.shape[2]
    tall = back_ref.shape[0]
    group = tall // rows_dev
    for b in range(chans // group):
        channels = slice(b * group, (b + 1) * group)
        tile = jnp.concatenate(
            [slab[channels, u * LANES : (u + 1) * LANES] for u in range(rows_dev)], axis=0
        )
        value = jnp.dot(back_ref[...], tile, preferred_element_type=jnp.float32)
        if out_rows % tall == 0:
            target, row = divmod(b * tall, out_rows)
            out_ref[target, 0, row : row + tall, :] = value.astype(jnp.bfloat16)
        else:
            take = tall // out_rows
            out_ref[b * take : (b + 1) * take, 0] = value.reshape(take, out_rows, LANES).astype(
                jnp.bfloat16
            )


def clean(at, xs, basis, basis_t, gain, targets, rows_dev):
    split = len(xs) > 1
    chans = basis.shape[0]
    sources = len(xs) if split else xs[0].shape[0]
    own = chans // sources
    swap = swap_table(min(256 // rows_dev, own), rows_dev)
    back = np.ascontiguousarray(swap_table(256 // rows_dev, rows_dev).T)
    out_rows = chans * rows_dev // targets
    whole = lambda s, at: (0, 0)
    if split:
        spec = pl.BlockSpec((1, own * rows_dev, LANES), lambda s, at: (s, 0, 0))
    else:
        spec = pl.BlockSpec((sources, 1, own * rows_dev, LANES), lambda s, at: (0, s, 0, 0))
    return pl.pallas_call(
        functools.partial(clean_kernel, split),
        grid_spec=pltpu.PrefetchScalarGridSpec(
            num_scalar_prefetch=1,
            grid=(2,),
            in_specs=[spec] * len(xs)
            + [
                pl.BlockSpec(basis.shape, whole),
                pl.BlockSpec(basis.shape, whole),
                pl.BlockSpec(gain.shape, whole),
                pl.BlockSpec(swap.shape, whole),
                pl.BlockSpec(back.shape, whole),
            ],
            out_specs=pl.BlockSpec((targets, 1, out_rows, LANES), lambda s, at: (0, s, 0, 0)),
            scratch_shapes=[pltpu.VMEM((chans, rows_dev * LANES), jnp.bfloat16)],
        ),
        out_shape=jax.ShapeDtypeStruct((targets, 2, out_rows, LANES), jnp.bfloat16),
        compiler_params=params(),
        cost_estimate=pl.CostEstimate(
            flops=12 * chans * chans * rows_dev * LANES,
            bytes_accessed=8 * chans * rows_dev * LANES,
            transcendentals=0,
        ),
        name="clean",
    )(at, *xs, basis, basis_t, gain, jnp.asarray(swap), jnp.asarray(back))


def image_kernel(scale, x_ref, table_ref, order_ref, *refs):
    out_ref = refs[-1]
    z, _, parts, rows, _ = x_ref.shape
    tiles = []
    for y_lo in range(RADIX):
        tile = x_ref[:, y_lo]
        if rows % 16:
            tile = tile.astype(jnp.float32)
        tile = tile.reshape(z * parts * rows, LANES).astype(jnp.bfloat16)
        tiles.append(tile)
    value = jnp.dot(table_ref[...], jnp.concatenate(tiles, axis=1), preferred_element_type=jnp.float32)
    value = (value * scale).astype(jnp.bfloat16)
    value = jnp.dot(value, order_ref[...], preferred_element_type=jnp.float32)
    out_ref[...] = value.astype(jnp.bfloat16).reshape(out_ref.shape)


def image(x, chunk, count, rows_dev, held):
    z, pieces, _, rows, _ = x.shape
    chans = rows // rows_dev
    total = z * rows_dev
    spread = pieces // RADIX
    wide = RADIX * LANES
    group = min(chans, max(1, 256 // (2 * total)))
    table = row_table(rows_dev, z, group)
    order = order_table()
    scale = 1.0 / math.sqrt(total * count * spread * wide)
    return pl.pallas_call(
        functools.partial(image_kernel, scale),
        grid=(chans // group, spread),
        in_specs=[
            pl.BlockSpec((z, RADIX, 2, group * rows_dev, LANES), lambda c, g: (0, g, 0, c, 0)),
            pl.BlockSpec(table.shape, lambda c, g: (0, 0)),
            pl.BlockSpec(order.shape, lambda c, g: (0, 0)),
        ]
        + [pl.BlockSpec(memory_space=pl.ANY)] * len(held),
        out_specs=pl.BlockSpec(
            (2, group, total, wide), lambda c, g: (0, c, 0, chunk * spread + g)
        ),
        out_shape=jax.ShapeDtypeStruct((2, chans, total, count * spread * wide), jnp.bfloat16),
        input_output_aliases={3: 0} if held else {},
        compiler_params=params(),
        cost_estimate=pl.CostEstimate(
            flops=4 * pieces * chans * total * LANES * wide,
            bytes_accessed=8 * pieces * chans * total * LANES,
            transcendentals=0,
        ),
        name="image",
    )(x, jnp.asarray(table), jnp.asarray(order), *held)


def turn_kernel(basis_ref, out_ref):
    out_ref[...] = basis_ref[...].T


def turn(basis):
    vmem = pl.BlockSpec(memory_space=pltpu.VMEM)
    return pl.pallas_call(
        turn_kernel,
        in_specs=[vmem],
        out_specs=vmem,
        out_shape=jax.ShapeDtypeStruct(basis.shape[::-1], basis.dtype),
        compiler_params=params(),
        name="turn",
    )(basis)


def exchange(x, axes):
    return lax.all_to_all(x, axes, split_axis=0, concat_axis=0, tiled=True)


def scatter(pieces):
    count = len(pieces)
    return [pieces[0]] + [
        lax.ppermute(
            pieces[step], "chan", [(j, int(partner(np.int32(j), step, count))) for j in range(count)]
        )
        for step in range(1, count)
    ]


def shards(visibility, eigen_basis, eigenvalues, noise_power):
    uv_count = lax.axis_size("uv")
    chan_count = lax.axis_size("chan")
    _, chans, rows_dev, length = visibility.shape
    count = length // chan_count // LANES
    targets = uv_count * chan_count
    at = lax.axis_index("chan").astype(jnp.int32).reshape(1)
    basis = exchange(jnp.broadcast_to(eigen_basis, (chan_count,) + eigen_basis.shape), "chan")
    basis = basis.reshape(chan_count * chans, -1)
    basis_t = turn(basis)
    gain = eigenvalues[:, None] / (eigenvalues[:, None] + noise_power[None, :])
    flat = visibility.reshape(2, chans * rows_dev, length)
    first = column_transform(flat, at, chan_count, [0], False)
    cells = [[exchange(first[0], "chan")]]
    if count > 1:
        sends = column_transform(flat, at, chan_count, list(range(1, count)), True)
        cells += [
            scatter(sends[k * chan_count : (k + 1) * chan_count]) for k in range(count - 1)
        ]
    held = []
    for k in range(count):
        cleaned = clean(at, cells[k], basis, basis_t, gain, targets, rows_dev)
        planes = exchange(cleaned, ("uv", "chan"))
        planes = planes.reshape((uv_count, chan_count) + planes.shape[1:])
        held = [image(planes, k, count, rows_dev, held)]
    return held[0]


def solution(mesh):
    in_specs = (P(None, "chan", "uv", None), P("chan", None), P(), P("uv"))
    out_specs = P(None, ("uv", "chan"), None, None)
    return jax.shard_map(shards, mesh=mesh, in_specs=in_specs, out_specs=out_specs, check_vma=False)
```

time: 380 us -> 326 us (0.86)
  blocking collectives: 286 us -> 0 us
  waiting for transfers between devices: 0.01 us -> 174 us
  starting transfers between devices: 5.09 us -> 46.5 us
  Pallas kernels: 82.7 us -> 91.2 us
  local copies, waits for them, and re-layouts: 2.62 us -> 8.61 us
    all_to_all x1 -> x0, blocking collectives: 188 us -> none  [shards(): lax.all_to_all(cleaned, ('uv', 'chan'), split_axis=0, concat_axis=0, tile...]
    ppermute x0 -> x21, waiting for transfers between devices: none -> 108 us  [scatter(): lax.ppermute(pieces[step], 'chan', [(j, int(partner(np.int32(j), step, co...]
    all_gather x1 -> x0, blocking collectives: 98.3 us -> none  [shards(): basis = lax.all_gather(eigen_basis, 'chan', axis=0, tiled=True)]
    all_to_all x1 -> x6, waiting for transfers between devices: 0.01 us -> 66 us  [exchange(): return lax.all_to_all(x, axes, split_axis=0, concat_axis=0, tiled=True)]
    all_to_all x1 -> x6, starting transfers between devices: 5.09 us -> 27.3 us  [exchange(): return lax.all_to_all(x, axes, split_axis=0, concat_axis=0, tiled=True)]
    ppermute x0 -> x21, starting transfers between devices: none -> 19.2 us  [scatter(): lax.ppermute(pieces[step], 'chan', [(j, int(partner(np.int32(j), step, co...]
    pallas_call x3 -> x11, Pallas kernels: 82.7 us -> 91.2 us  [the longest x4 34.1 us: clean(): pl.pallas_call(functools.partial(clean_kernel, split), grid_spec=pltpu.Pr...]
    unnamed x8 -> x74, local copies, waits for them, and re-layouts: 0.01 us -> 6.94 us
  transfers between devices with their start and end apart: 1 -> 27, of which waited for: 0 -> 15; matrix products, arithmetic and copies ran while one was open for 1% -> 0% of each run, Pallas kernels for 0% -> 26%
where the time goes in v8:
time: 326 us; the launch traced here: 322 us
  waiting for transfers between devices  174 us (53%)
  Pallas kernels  91.2 us (28%)
  starting transfers between devices  46.5 us (14%)
  local copies, waits for them, and re-layouts  8.61 us (3%)
    ppermute x21, waiting for transfers between devices, scatter(): lax.ppermute(pieces[step], 'chan', [(j, int(partner(np.int32(j), step, co...  108 us
    all_to_all x6, waiting for transfers between devices, exchange(): return lax.all_to_all(x, axes, split_axis=0, concat_axis=0, tiled=True)  66 us
    pallas_call x4, Pallas kernels, clean(): pl.pallas_call(functools.partial(clean_kernel, split), grid_spec=pltpu.Pr...  34.1 us
    pallas_call x2, Pallas kernels, column_transform(): pl.pallas_call(functools.partial(column_kernel, chunks, pieces // RADIX,...  29.4 us
    all_to_all x6, starting transfers between devices, exchange(): return lax.all_to_all(x, axes, split_axis=0, concat_axis=0, tiled=True)  27.3 us
    pallas_call x4, Pallas kernels, image(): pl.pallas_call(functools.partial(image_kernel, scale), grid=(chans // gro...  25.8 us
    ppermute x21, starting transfers between devices, scatter(): lax.ppermute(pieces[step], 'chan', [(j, int(partner(np.int32(j), step, co...  19.2 us
    unnamed x74, local copies, waits for them, and re-layouts  6.94 us
  transfers between devices with their start and end apart: 27, of which 15 were waited for; matrix products, arithmetic and copies ran while one was open for 0% of the time, Pallas kernels for 26%

profile of v8, /device:TPU:8, one launch (start us, length us, event | category | flops | bytes accessed | tf_op | source)
XLA Modules:
  0.0 321.5 jit_solution(4232623626093286922)
XLA Ops:
  0.0 1.7 broadcast_in_dim.2
  1.7 3.7 %all-to-all-start = ((bf16[8,64,512]{2,1,0:T(8,128)(2,1)}), bf16[8,64,512]{2,1,0:T(8,128)(2,1)S(1)}, u32[]{:S(2)}, u32[]{:S(2)}) async-start(bf16[8,64,512]{2,1,0:T(8,128)(2,1)} %broadcast_in_dim.2), calls=%async_computation | async-start | bytes 1048576 | tf_op jit(solution)/shard_map/all_to_all | solution.py:338
  5.4 11.9 %column_transform.3 = bf16[8,2,512,128]{3,2,1,0:T(8,128)(2,1)} custom-call(s32[1]{0:T(128)} %bitcast.at_ref, bf16[2,512,4096]{2,1,0:T(8,128)(2,1)} %bitcast.14, f32[8,2,512]{2,1,0:T(2,128)} %constant.16.clone.twiddle_ref, bf16[1024,1024]{1,0:T(8,128)(2,1)} %constant.17.clone.table_ref), custom_call_target="tpu_custom_call" | custom-call | flops 8589934592 | bytes 16777216 | tf_op jit(solution)/shard_map/column_transform/pallas_call | solution.py:155
  17.3 0.8 copy-done.3
  18.1 4.2 %all-to-all-start.4 = ((bf16[8,2,512,128]{3,2,1,0:T(8,128)(2,1)}), bf16[8,2,512,128]{3,2,1,0:T(8,128)(2,1)S(1)}, u32[]{:S(2)}, u32[]{:S(2)}) async-start(bf16[8,2,512,128]{3,2,1,0:T(8,128)(2,1)} %column_transform.3), calls=%async_computation.4 | async-start | bytes 4194304 | tf_op jit(solution)/shard_map/all_to_all | solution.py:338
  22.3 17.5 %column_transform.2 = (bf16[2,512,128]{2,1,0:T(8,128)(2,1)}, bf16[2,512,128]{2,1,0:T(8,128)(2,1)}, bf16[2,512,128]{2,1,0:T(8,128)(2,1)}, bf16[2,512,128]{2,1,0:T...) custom-call(s32[1]{0:T(128)} %bitcast.at_ref, ...), custom_call_target="tpu_custom_call" | custom-call | flops 25769803776 | bytes 16777216 | tf_op jit(solution)/shard_map/column_transform/pallas_call | solution.py:155
  40.3 1.7 collective-permute-start.8
  42.0 1.7 collective-permute-start.10
  43.8 2.6 collective-permute-start.12
  46.4 7.7 %collective-permute-done.8.refs_2_ = bf16[2,512,128]{2,1,0:T(8,128)(2,1)S(1)} collective-permute-done((bf16[2,512,128]{2,1,0:T(8,128)(2,1)}, bf16[2,512,128]{2,1,0:T(8,128)(2,1)S(1)}, u32[]{:S(2)}, u32[]{:S(2)}) %collective-permute-start.8) | collective-permute-done | bytes 262176 | tf_op jit(solution)/shard_map/ppermute | solution.py:344
  54.4 0.9 add_divide_fusion.refs_10_.refs_3_
  55.2 2.0 turn.1.refs_9_.refs_2_
  57.3 1.6 collective-permute-done.9.refs_3_
  58.8 1.7 collective-permute-done.11.refs_5_
  60.5 5.8 %collective-permute-done.12.refs_6_ = bf16[2,512,128]{2,1,0:T(8,128)(2,1)S(1)} collective-permute-done((bf16[2,512,128]{2,1,0:T(8,128)(2,1)}, bf16[2,512,128]{2,1,0:T(8,128)(2,1)S(1)}, u32[]{:S(2)}, u32[]{:S(2)}) %collective-permute-start.12) | collective-permute-done | bytes 262176 | tf_op jit(solution)/shard_map/ppermute | solution.py:344
  66.3 4.7 %collective-permute-done.13.refs_7_ = bf16[2,512,128]{2,1,0:T(8,128)(2,1)S(1)} collective-permute-done((bf16[2,512,128]{2,1,0:T(8,128)(2,1)}, bf16[2,512,128]{2,1,0:T(8,128)(2,1)S(1)}, u32[]{:S(2)}, u32[]{:S(2)}) %collective-permute-start.13) | collective-permute-done | bytes 262176 | tf_op jit(solution)/shard_map/ppermute | solution.py:344
  71.7 8.6 %clean.5 = bf16[32,2,128,128]{3,2,1,0:T(8,128)(2,1)} custom-call(s32[1]{0:T(128)} %bitcast.at_ref, bf16[2,512,128]{2,1,0:T(8,128)(2,1)} %get-tuple-element.37.refs_0_, bf16[2,512,128]{2,1,0:T(8,128)(2,1)} %copy-done.18, bf16[2,512,128]{2,1,0:T(8,128)(2,1)} %copy-done.21, bf16[2,512,128]{2,1,0:T(8,128)(2,1)} %copy-done.24, bf16[2,512,128]{2,1,0:T(8,128)(2,1)} %copy-done.27, ...), custom_call_target="tpu_custom_call" | custom-call | flops 3221225472 | bytes 4194304 | tf_op jit(solution)/shard_map/clean/pallas_call | solution.py:244
  80.3 1.4 copy-done.2
  81.7 4.2 %all-to-all-start.2 = ((bf16[32,2,128,128]{3,2,1,0:T(8,128)(2,1)}), bf16[32,2,128,128]{3,2,1,0:T(8,128)(2,1)S(1)}, u32[]{:S(2)}, u32[]{:S(2)}) async-start(bf16[32,2,128,128]{3,2,1,0:T(8,128)(2,1)} %clean.5), calls=%async_computation.2 | async-start | bytes 4194304 | tf_op jit(solution)/shard_map/all_to_all | solution.py:338
  86.2 1.5 collective-permute-start.15
  87.9 1.5 collective-permute-start.17
  89.7 2.4 collective-permute-start.19
  92.1 15.7 %collective-permute-done.15.refs_2_ = bf16[2,512,128]{2,1,0:T(8,128)(2,1)S(1)} collective-permute-done((bf16[2,512,128]{2,1,0:T(8,128)(2,1)}, bf16[2,512,128]{2,1,0:T(8,128)(2,1)S(1)}, u32[]{:S(2)}, u32[]{:S(2)}) %collective-permute-start.15) | collective-permute-done | bytes 262176 | tf_op jit(solution)/shard_map/ppermute | solution.py:344
  107.8 11.1 %collective-permute-done.16.refs_3_ = bf16[2,512,128]{2,1,0:T(8,128)(2,1)S(1)} collective-permute-done((bf16[2,512,128]{2,1,0:T(8,128)(2,1)S(1)}, bf16[2,512,128]{2,1,0:T(8,128)(2,1)S(1)}, u32[]{:S(2)}, u32[]{:S(2)}) %collective-permute-start.16) | collective-permute-done | bytes 262176 | tf_op jit(solution)/shard_map/ppermute | solution.py:344
  118.9 9.1 %collective-permute-done.19.refs_6_ = bf16[2,512,128]{2,1,0:T(8,128)(2,1)S(1)} collective-permute-done((bf16[2,512,128]{2,1,0:T(8,128)(2,1)S(1)}, bf16[2,512,128]{2,1,0:T(8,128)(2,1)S(1)}, u32[]{:S(2)}, u32[]{:S(2)}) %collective-permute-start.19) | collective-permute-done | bytes 262176 | tf_op jit(solution)/shard_map/ppermute | solution.py:344
  128.0 7.4 %collective-permute-done.20.refs_7_ = bf16[2,512,128]{2,1,0:T(8,128)(2,1)S(1)} collective-permute-done((bf16[2,512,128]{2,1,0:T(8,128)(2,1)S(1)}, bf16[2,512,128]{2,1,0:T(8,128)(2,1)S(1)}, u32[]{:S(2)}, u32[]{:S(2)}) %collective-permute-start.20) | collective-permute-done | bytes 262176 | tf_op jit(solution)/shard_map/ppermute | solution.py:344
  136.2 8.7 %clean.6 = bf16[32,2,128,128]{3,2,1,0:T(8,128)(2,1)} custom-call(s32[1]{0:T(128)} %bitcast.at_ref, bf16[2,512,128]{2,1,0:T(8,128)(2,1)} %get-tuple-element.45.refs_0_, bf16[2,512,128]{2,1,0:T(8,128)(2,1)} %copy-done.20, bf16[2,512,128]{2,1,0:T(8,128)(2,1)} %copy-done.23, bf16[2,512,128]{2,1,0:T(8,128)(2,1)} %copy-done.26, bf16[2,512,128]{2,1,0:T(8,128)(2,1)} %copy-done.28, ...), custom_call_target="tpu_custom_call" | custom-call | flops 3221225472 | bytes 4194304 | tf_op jit(solution)/shard_map/clean/pallas_call | solution.py:244
  144.9 1.3 copy-done
  146.2 4.5 %all-to-all-start.3 = ((bf16[32,2,128,128]{3,2,1,0:T(8,128)(2,1)}), bf16[32,2,128,128]{3,2,1,0:T(8,128)(2,1)}, u32[]{:S(2)}, u32[]{:S(2)}) async-start(bf16[32,2,128,128]{3,2,1,0:T(8,128)(2,1)} %clean.6), calls=%async_computation.3 | async-start | bytes 4194304 | tf_op jit(solution)/shard_map/all_to_all | solution.py:338
  150.7 8.1 %clean.7 = bf16[32,2,128,128]{3,2,1,0:T(8,128)(2,1)} custom-call(s32[1]{0:T(128)} %bitcast.at_ref, bf16[8,2,512,128]{3,2,1,0:T(8,128)(2,1)} %copy-done.2, bf16[512,512]{1,0:T(8,128)(2,1)} %bitcast.12, bf16[512,512]{1,0:T(8,128)(2,1)} %turn.1.refs_9_.refs_2_, f32[512,8]{1,0:T(8,128)} %add_divide_fusion.refs_10_.refs_3_, ...), custom_call_target="tpu_custom_call" | custom-call | flops 3221225472 | bytes 4194304 | tf_op jit(solution)/shard_map/clean/pallas_call | solution.py:244
  158.8 38.6 %all-to-all-done.3 = bf16[32,2,128,128]{3,2,1,0:T(8,128)(2,1)} async-done(((bf16[32,2,128,128]{3,2,1,0:T(8,128)(2,1)}), bf16[32,2,128,128]{3,2,1,0:T(8,128)(2,1)}, u32[]{:S(2)}, u32[]{:S(2)}) %all-to-all-start.3) | async-done | bytes 2097184 | tf_op jit(solution)/shard_map/all_to_all | solution.py:338
  197.4 6.2 %all-to-all-start.5 = ((bf16[32,2,128,128]{3,2,1,0:T(8,128)(2,1)}), bf16[32,2,128,128]{3,2,1,0:T(8,128)(2,1)S(1)}, u32[]{:S(2)}, u32[]{:S(2)}) async-start(bf16[32,2,128,128]{3,2,1,0:T(8,128)(2,1)} %clean.7), calls=%async_computation.5 | async-start | bytes 4194304 | tf_op jit(solution)/shard_map/all_to_all | solution.py:338
  203.9 1.5 collective-permute-start.1
  205.6 1.5 collective-permute-start.3
  207.4 2.4 collective-permute-start.5
  209.8 15.7 %collective-permute-done.1.refs_2_ = bf16[2,512,128]{2,1,0:T(8,128)(2,1)S(1)} collective-permute-done((bf16[2,512,128]{2,1,0:T(8,128)(2,1)}, bf16[2,512,128]{2,1,0:T(8,128)(2,1)S(1)}, u32[]{:S(2)}, u32[]{:S(2)}) %collective-permute-start.1) | collective-permute-done | bytes 262176 | tf_op jit(solution)/shard_map/ppermute | solution.py:344
  225.5 11.1 %collective-permute-done.2.refs_3_ = bf16[2,512,128]{2,1,0:T(8,128)(2,1)S(1)} collective-permute-done((bf16[2,512,128]{2,1,0:T(8,128)(2,1)S(1)}, bf16[2,512,128]{2,1,0:T(8,128)(2,1)S(1)}, u32[]{:S(2)}, u32[]{:S(2)}) %collective-permute-start.2) | collective-permute-done | bytes 262176 | tf_op jit(solution)/shard_map/ppermute | solution.py:344
  236.7 9.1 %collective-permute-done.5.refs_6_ = bf16[2,512,128]{2,1,0:T(8,128)(2,1)S(1)} collective-permute-done((bf16[2,512,128]{2,1,0:T(8,128)(2,1)S(1)}, bf16[2,512,128]{2,1,0:T(8,128)(2,1)S(1)}, u32[]{:S(2)}, u32[]{:S(2)}) %collective-permute-start.5) | collective-permute-done | bytes 262176 | tf_op jit(solution)/shard_map/ppermute | solution.py:344
  245.8 7.4 %collective-permute-done.6.refs_7_ = bf16[2,512,128]{2,1,0:T(8,128)(2,1)S(1)} collective-permute-done((bf16[2,512,128]{2,1,0:T(8,128)(2,1)S(1)}, bf16[2,512,128]{2,1,0:T(8,128)(2,1)S(1)}, u32[]{:S(2)}, u32[]{:S(2)}) %collective-permute-start.6) | collective-permute-done | bytes 262176 | tf_op jit(solution)/shard_map/ppermute | solution.py:344
  253.2 0.7 copy-done.34
  253.9 8.7 %clean.4 = bf16[32,2,128,128]{3,2,1,0:T(8,128)(2,1)} custom-call(s32[1]{0:T(128)} %bitcast.at_ref, bf16[2,512,128]{2,1,0:T(8,128)(2,1)} %get-tuple-element.29.refs_0_, bf16[2,512,128]{2,1,0:T(8,128)(2,1)} %copy-done.16, bf16[2,512,128]{2,1,0:T(8,128)(2,1)} %copy-done.17, bf16[2,512,128]{2,1,0:T(8,128)(2,1)} %copy-done.19, bf16[2,512,128]{2,1,0:T(8,128)(2,1)} %copy-done.22, ...), custom_call_target="tpu_custom_call" | custom-call | flops 3221225472 | bytes 4194304 | tf_op jit(solution)/shard_map/clean/pallas_call | solution.py:244
  262.6 1.3 copy-done.1
  263.9 4.5 %all-to-all-start.1 = ((bf16[32,2,128,128]{3,2,1,0:T(8,128)(2,1)}), bf16[32,2,128,128]{3,2,1,0:T(8,128)(2,1)}, u32[]{:S(2)}, u32[]{:S(2)}) async-start(bf16[32,2,128,128]{3,2,1,0:T(8,128)(2,1)} %clean.4), calls=%async_computation.1 | async-start | bytes 4194304 | tf_op jit(solution)/shard_map/all_to_all | solution.py:338
  268.4 6.5 %image.4.refs_0_ = bf16[2,16,32,4096]{3,2,1,0:T(8,128)(2,1)} custom-call(bf16[4,8,2,128,128]{4,3,2,1,0:T(8,128)(2,1)} %bitcast.8, bf16[256,256]{1,0:T(8,128)(2,1)} %constant.20.clone.table_ref, bf16[1024,1024]{1,0:T(8,128)(2,1)} %constant.21.clone.order_ref), custom_call_target="tpu_custom_call" | custom-call | flops 2147483648 | bytes 4194304 | tf_op jit(solution)/shard_map/image/pallas_call | solution.py:297
  274.8 6.4 %image.5.refs_0_ = bf16[2,16,32,4096]{3,2,1,0:T(8,128)(2,1)} custom-call(bf16[4,8,2,128,128]{4,3,2,1,0:T(8,128)(2,1)} %bitcast.5.x_ref, bf16[256,256]{1,0:T(8,128)(2,1)} %constant.20.clone.table_ref, bf16[1024,1024]{1,0:T(8,128)(2,1)} %constant.21.clone.order_ref, bf16[2,16,32,4096]{3,2,1,0:T(8,128)(2,1)} %image.4.refs_0_), custom_call_target="tpu_custom_call", output_to_operand_aliasing={{}: (3, {})} | custom-call | flops 2147483648 | bytes 4194304 | tf_op jit(solution)/shard_map/image/pallas_call | solution.py:297
  281.3 6.4 %image.6.refs_0_ = bf16[2,16,32,4096]{3,2,1,0:T(8,128)(2,1)} custom-call(bf16[4,8,2,128,128]{4,3,2,1,0:T(8,128)(2,1)} %bitcast.7, bf16[256,256]{1,0:T(8,128)(2,1)} %constant.20.clone.table_ref, bf16[1024,1024]{1,0:T(8,128)(2,1)} %constant.21.clone.order_ref, bf16[2,16,32,4096]{3,2,1,0:T(8,128)(2,1)} %image.5.refs_0_), custom_call_target="tpu_custom_call", output_to_operand_aliasing={{}: (3, {})} | custom-call | flops 2147483648 | bytes 4194304 | tf_op jit(solution)/shard_map/image/pallas_call | solution.py:297
  287.7 27.4 %all-to-all-done.1 = bf16[32,2,128,128]{3,2,1,0:T(8,128)(2,1)} async-done(((bf16[32,2,128,128]{3,2,1,0:T(8,128)(2,1)}), bf16[32,2,128,128]{3,2,1,0:T(8,128)(2,1)}, u32[]{:S(2)}, u32[]{:S(2)}) %all-to-all-start.1) | async-done | bytes 2097184 | tf_op jit(solution)/shard_map/all_to_all | solution.py:338
  315.1 6.4 %image.7 = bf16[2,16,32,4096]{3,2,1,0:T(8,128)(2,1)} custom-call(bf16[4,8,2,128,128]{4,3,2,1,0:T(8,128)(2,1)} %bitcast.3.x_ref, bf16[256,256]{1,0:T(8,128)(2,1)} %constant.20.clone.table_ref, bf16[1024,1024]{1,0:T(8,128)(2,1)} %constant.21.clone.order_ref, bf16[2,16,32,4096]{3,2,1,0:T(8,128)(2,1)} %image.6.refs_0_), custom_call_target="tpu_custom_call", output_to_operand_aliasing={{}: (3, {})} | custom-call | flops 2147483648 | bytes 4194304 | tf_op jit(solution)/shard_map/image/pallas_call | solution.py:297
  (93 shorter events, 3.9 us)
Async XLA Ops:
  1.7 15.6 %all-to-all-start = ((bf16[8,64,512]{2,1,0:T(8,128)(2,1)}), bf16[8,64,512]{2,1,0:T(8,128)(2,1)S(1)}, u32[]{:S(2)}, u32[]{:S(2)}) async-start(bf16[8,64,512]{2,1,0:T(8,128)(2,1)} %broadcast_in_dim.2), calls=%async_computation | async-start | bytes 1048576 | tf_op jit(solution)/shard_map/all_to_all | solution.py:338
  18.1 62.2 %all-to-all-start.4 = ((bf16[8,2,512,128]{3,2,1,0:T(8,128)(2,1)}), bf16[8,2,512,128]{3,2,1,0:T(8,128)(2,1)S(1)}, u32[]{:S(2)}, u32[]{:S(2)}) async-start(bf16[8,2,512,128]{3,2,1,0:T(8,128)(2,1)} %column_transform.3), calls=%async_computation.4 | async-start | bytes 4194304 | tf_op jit(solution)/shard_map/all_to_all | solution.py:338
  22.3 32.1 %copy-start.4 = (f32[512]{0:T(512)S(1)}, f32[512]{0:T(512)}, u32[]{:S(2)}) copy-start(f32[512]{0:T(512)} %param.26) | copy-start | bytes 6148
  22.3 32.1 %copy-start.5 = (f32[8]{0:T(128)S(1)}, f32[8]{0:T(128)}, u32[]{:S(2)}) copy-start(f32[8]{0:T(128)} %param.27) | copy-start | bytes 100
  39.8 4.0 %collective-permute-start.7 = (bf16[2,512,128]{2,1,0:T(8,128)(2,1)}, bf16[2,512,128]{2,1,0:T(8,128)(2,1)S(1)}, u32[]{:S(2)}, u32[]{:S(2)}) collective-permute-start(bf16[2,512,128]{2,1,0:T(8,128)(2,1)} %get-tuple-element.38), channel_id=1, source_target_pairs={{0,1},{1,0},{2,3},{3,2},{4,5},{5,4},{6,7},{7,6},{8,9},{9,8},{10,11... | collective-permute-start | bytes 786440 | tf_op jit(solution)/shard_map/ppermute | solution.py:344
  40.3 13.8 %collective-permute-start.8 = (bf16[2,512,128]{2,1,0:T(8,128)(2,1)}, bf16[2,512,128]{2,1,0:T(8,128)(2,1)S(1)}, u32[]{:S(2)}, u32[]{:S(2)}) collective-permute-start(bf16[2,512,128]{2,1,0:T(8,128)(2,1)} %get-tuple-element.39), channel_id=1, source_target_pairs={{0,2},{1,3},{2,0},{3,1},{4,6},{5,7},{6,4},{7,5},{8,10},{9,11},{10,... | collective-permute-start | bytes 786440 | tf_op jit(solution)/shard_map/ppermute | solution.py:344
  42.0 16.8 %collective-permute-start.9 = (bf16[2,512,128]{2,1,0:T(8,128)(2,1)}, bf16[2,512,128]{2,1,0:T(8,128)(2,1)S(1)}, u32[]{:S(2)}, u32[]{:S(2)}) collective-permute-start(bf16[2,512,128]{2,1,0:T(8,128)(2,1)} %get-tuple-element.40), channel_id=1, source_target_pairs={{0,3},{1,2},{2,1},{3,0},{4,7},{5,6},{6,5},{7,4},{8,11},{9,10},{10,... | collective-permute-start | bytes 786440 | tf_op jit(solution)/shard_map/ppermute | solution.py:344
  42.0 16.8 %collective-permute-start.10 = (bf16[2,512,128]{2,1,0:T(8,128)(2,1)}, bf16[2,512,128]{2,1,0:T(8,128)(2,1)S(1)}, u32[]{:S(2)}, u32[]{:S(2)}) collective-permute-start(bf16[2,512,128]{2,1,0:T(8,128)(2,1)} %get-tuple-element.41), channel_id=1, source_target_pairs={{0,4},{1,5},{2,6},{3,7},{4,0},{5,1},{6,2},{7,3},{8,12},{9,13},{10,... | collective-permute-start | bytes 786440 | tf_op jit(solution)/shard_map/ppermute | solution.py:344
  43.7 16.8 %collective-permute-start.11 = (bf16[2,512,128]{2,1,0:T(8,128)(2,1)}, bf16[2,512,128]{2,1,0:T(8,128)(2,1)S(1)}, u32[]{:S(2)}, u32[]{:S(2)}) collective-permute-start(bf16[2,512,128]{2,1,0:T(8,128)(2,1)} %get-tuple-element.42), channel_id=1, source_target_pairs={{0,5},{1,4},{2,7},{3,6},{4,1},{5,0},{6,3},{7,2},{8,13},{9,12},{10,... | collective-permute-start | bytes 786440 | tf_op jit(solution)/shard_map/ppermute | solution.py:344
  43.8 27.1 %copy-start.18 = (bf16[2,512,128]{2,1,0:T(8,128)(2,1)}, bf16[2,512,128]{2,1,0:T(8,128)(2,1)S(1)}, u32[]{:S(2)}) copy-start(bf16[2,512,128]{2,1,0:T(8,128)(2,1)S(1)} %collective-permute-done.7.refs_1_) | copy-start | bytes 786436
  43.8 22.5 %collective-permute-start.12 = (bf16[2,512,128]{2,1,0:T(8,128)(2,1)}, bf16[2,512,128]{2,1,0:T(8,128)(2,1)S(1)}, u32[]{:S(2)}, u32[]{:S(2)}) collective-permute-start(bf16[2,512,128]{2,1,0:T(8,128)(2,1)} %get-tuple-element.43), channel_id=1, source_target_pairs={{0,6},{1,7},{2,4},{3,5},{4,2},{5,3},{6,0},{7,1},{8,14},{9,15},{10,... | collective-permute-start | bytes 786440 | tf_op jit(solution)/shard_map/ppermute | solution.py:344
  54.1 16.8 %copy-start.21 = (bf16[2,512,128]{2,1,0:T(8,128)(2,1)}, bf16[2,512,128]{2,1,0:T(8,128)(2,1)S(1)}, u32[]{:S(2)}) copy-start(bf16[2,512,128]{2,1,0:T(8,128)(2,1)S(1)} %collective-permute-done.8.refs_2_) | copy-start | bytes 786436
  54.1 16.8 %collective-permute-start.13 = (bf16[2,512,128]{2,1,0:T(8,128)(2,1)}, bf16[2,512,128]{2,1,0:T(8,128)(2,1)S(1)}, u32[]{:S(2)}, u32[]{:S(2)}) collective-permute-start(bf16[2,512,128]{2,1,0:T(8,128)(2,1)} %get-tuple-element.44), channel_id=1, source_target_pairs={{0,7},{1,6},{2,5},{3,4},{4,3},{5,2},{6,1},{7,0},{8,15},{9,14},{10,... | collective-permute-start | bytes 786440 | tf_op jit(solution)/shard_map/ppermute | solution.py:344
  58.8 12.2 %copy-start.27 = (bf16[2,512,128]{2,1,0:T(8,128)(2,1)}, bf16[2,512,128]{2,1,0:T(8,128)(2,1)S(1)}, u32[]{:S(2)}) copy-start(bf16[2,512,128]{2,1,0:T(8,128)(2,1)S(1)} %collective-permute-done.10.refs_4_) | copy-start | bytes 786436
  80.3 27.5 %copy-start.11 = (bf16[2,512,128]{2,1,0:T(8,128)(2,1)S(1)}, bf16[2,512,128]{2,1,0:T(8,128)(2,1)}, u32[]{:S(2)}) copy-start(bf16[2,512,128]{2,1,0:T(8,128)(2,1)} %get-tuple-element.52) | copy-start | bytes 786436
  81.7 63.2 %all-to-all-start.2 = ((bf16[32,2,128,128]{3,2,1,0:T(8,128)(2,1)}), bf16[32,2,128,128]{3,2,1,0:T(8,128)(2,1)S(1)}, u32[]{:S(2)}, u32[]{:S(2)}) async-start(bf16[32,2,128,128]{3,2,1,0:T(8,128)(2,1)} %clean.5), calls=%async_computation.2 | async-start | bytes 4194304 | tf_op jit(solution)/shard_map/all_to_all | solution.py:338
  85.9 3.7 %collective-permute-start.14 = (bf16[2,512,128]{2,1,0:T(8,128)(2,1)}, bf16[2,512,128]{2,1,0:T(8,128)(2,1)S(1)}, u32[]{:S(2)}, u32[]{:S(2)}) collective-permute-start(bf16[2,512,128]{2,1,0:T(8,128)(2,1)} %get-tuple-element.46), channel_id=1, source_target_pairs={{0,1},{1,0},{2,3},{3,2},{4,5},{5,4},{6,7},{7,6},{8,9},{9,8},{10,11... | collective-permute-start | bytes 786440 | tf_op jit(solution)/shard_map/ppermute | solution.py:344
  86.2 21.6 %collective-permute-start.15 = (bf16[2,512,128]{2,1,0:T(8,128)(2,1)}, bf16[2,512,128]{2,1,0:T(8,128)(2,1)S(1)}, u32[]{:S(2)}, u32[]{:S(2)}) collective-permute-start(bf16[2,512,128]{2,1,0:T(8,128)(2,1)} %get-tuple-element.47), channel_id=1, source_target_pairs={{0,2},{1,3},{2,0},{3,1},{4,6},{5,7},{6,4},{7,5},{8,10},{9,11},{10,... | collective-permute-start | bytes 786440 | tf_op jit(solution)/shard_map/ppermute | solution.py:344
  87.6 31.3 %collective-permute-start.16 = (bf16[2,512,128]{2,1,0:T(8,128)(2,1)S(1)}, bf16[2,512,128]{2,1,0:T(8,128)(2,1)S(1)}, u32[]{:S(2)}, u32[]{:S(2)}) collective-permute-start(bf16[2,512,128]{2,1,0:T(8,128)(2,1)S(1)} %copy-done.15), channel_id=1, source_target_pairs={{0,3},{1,2},{2,1},{3,0},{4,7},{5,6},{6,5},{7,4},{8,11},{9,10},{10,... | collective-permute-start | bytes 786440 | tf_op jit(solution)/shard_map/ppermute | solution.py:344
  87.9 31.0 %collective-permute-start.17 = (bf16[2,512,128]{2,1,0:T(8,128)(2,1)S(1)}, bf16[2,512,128]{2,1,0:T(8,128)(2,1)S(1)}, u32[]{:S(2)}, u32[]{:S(2)}) collective-permute-start(bf16[2,512,128]{2,1,0:T(8,128)(2,1)S(1)} %copy-done.14), channel_id=1, source_target_pairs={{0,4},{1,5},{2,6},{3,7},{4,0},{5,1},{6,2},{7,3},{8,12},{9,13},{10,... | collective-permute-start | bytes 786440 | tf_op jit(solution)/shard_map/ppermute | solution.py:344
  89.3 29.6 %collective-permute-start.18 = (bf16[2,512,128]{2,1,0:T(8,128)(2,1)S(1)}, bf16[2,512,128]{2,1,0:T(8,128)(2,1)S(1)}, u32[]{:S(2)}, u32[]{:S(2)}) collective-permute-start(bf16[2,512,128]{2,1,0:T(8,128)(2,1)S(1)} %copy-done.13), channel_id=1, source_target_pairs={{0,5},{1,4},{2,7},{3,6},{4,1},{5,0},{6,3},{7,2},{8,13},{9,12},{10,... | collective-permute-start | bytes 786440 | tf_op jit(solution)/shard_map/ppermute | solution.py:344
  89.7 45.8 %copy-start.20 = (bf16[2,512,128]{2,1,0:T(8,128)(2,1)}, bf16[2,512,128]{2,1,0:T(8,128)(2,1)S(1)}, u32[]{:S(2)}) copy-start(bf16[2,512,128]{2,1,0:T(8,128)(2,1)S(1)} %collective-permute-done.14.refs_1_) | copy-start | bytes 786436
  89.7 38.4 %collective-permute-start.19 = (bf16[2,512,128]{2,1,0:T(8,128)(2,1)S(1)}, bf16[2,512,128]{2,1,0:T(8,128)(2,1)S(1)}, u32[]{:S(2)}, u32[]{:S(2)}) collective-permute-start(bf16[2,512,128]{2,1,0:T(8,128)(2,1)S(1)} %copy-done.12), channel_id=1, source_target_pairs={{0,6},{1,7},{2,4},{3,5},{4,2},{5,3},{6,0},{7,1},{8,14},{9,15},{10,... | collective-permute-start | bytes 786440 | tf_op jit(solution)/shard_map/ppermute | solution.py:344
  107.8 27.7 %copy-start.23 = (bf16[2,512,128]{2,1,0:T(8,128)(2,1)}, bf16[2,512,128]{2,1,0:T(8,128)(2,1)S(1)}, u32[]{:S(2)}) copy-start(bf16[2,512,128]{2,1,0:T(8,128)(2,1)S(1)} %collective-permute-done.15.refs_2_) | copy-start | bytes 786436
  107.8 27.6 %collective-permute-start.20 = (bf16[2,512,128]{2,1,0:T(8,128)(2,1)S(1)}, bf16[2,512,128]{2,1,0:T(8,128)(2,1)S(1)}, u32[]{:S(2)}, u32[]{:S(2)}) collective-permute-start(bf16[2,512,128]{2,1,0:T(8,128)(2,1)S(1)} %copy-done.11), channel_id=1, source_target_pairs={{0,7},{1,6},{2,5},{3,4},{4,3},{5,2},{6,1},{7,0},{8,15},{9,14},{10,... | collective-permute-start | bytes 786440 | tf_op jit(solution)/shard_map/ppermute | solution.py:344
  118.9 16.6 %copy-start.26 = (bf16[2,512,128]{2,1,0:T(8,128)(2,1)}, bf16[2,512,128]{2,1,0:T(8,128)(2,1)S(1)}, u32[]{:S(2)}) copy-start(bf16[2,512,128]{2,1,0:T(8,128)(2,1)S(1)} %collective-permute-done.16.refs_3_) | copy-start | bytes 786436
  118.9 16.6 %copy-start.28 = (bf16[2,512,128]{2,1,0:T(8,128)(2,1)}, bf16[2,512,128]{2,1,0:T(8,128)(2,1)S(1)}, u32[]{:S(2)}) copy-start(bf16[2,512,128]{2,1,0:T(8,128)(2,1)S(1)} %collective-permute-done.17.refs_4_) | copy-start | bytes 786436
  118.9 16.6 %copy-start.30 = (bf16[2,512,128]{2,1,0:T(8,128)(2,1)}, bf16[2,512,128]{2,1,0:T(8,128)(2,1)S(1)}, u32[]{:S(2)}) copy-start(bf16[2,512,128]{2,1,0:T(8,128)(2,1)S(1)} %collective-permute-done.18.refs_5_) | copy-start | bytes 786436
  146.2 51.2 %all-to-all-start.3 = ((bf16[32,2,128,128]{3,2,1,0:T(8,128)(2,1)}), bf16[32,2,128,128]{3,2,1,0:T(8,128)(2,1)}, u32[]{:S(2)}, u32[]{:S(2)}) async-start(bf16[32,2,128,128]{3,2,1,0:T(8,128)(2,1)} %clean.6), calls=%async_computation.3 | async-start | bytes 4194304 | tf_op jit(solution)/shard_map/all_to_all | solution.py:338
  158.8 46.6 %copy-start.10 = (bf16[2,512,128]{2,1,0:T(8,128)(2,1)S(1)}, bf16[2,512,128]{2,1,0:T(8,128)(2,1)}, u32[]{:S(2)}) copy-start(bf16[2,512,128]{2,1,0:T(8,128)(2,1)} %get-tuple-element.32) | copy-start | bytes 786436
  158.8 46.8 %copy-start.9 = (bf16[2,512,128]{2,1,0:T(8,128)(2,1)S(1)}, bf16[2,512,128]{2,1,0:T(8,128)(2,1)}, u32[]{:S(2)}) copy-start(bf16[2,512,128]{2,1,0:T(8,128)(2,1)} %get-tuple-element.33) | copy-start | bytes 786436
  158.8 48.3 %copy-start.8 = (bf16[2,512,128]{2,1,0:T(8,128)(2,1)S(1)}, bf16[2,512,128]{2,1,0:T(8,128)(2,1)}, u32[]{:S(2)}) copy-start(bf16[2,512,128]{2,1,0:T(8,128)(2,1)} %get-tuple-element.34) | copy-start | bytes 786436
  158.8 48.6 %copy-start.7 = (bf16[2,512,128]{2,1,0:T(8,128)(2,1)S(1)}, bf16[2,512,128]{2,1,0:T(8,128)(2,1)}, u32[]{:S(2)}) copy-start(bf16[2,512,128]{2,1,0:T(8,128)(2,1)} %get-tuple-element.35) | copy-start | bytes 786436
  158.8 66.7 %copy-start.6 = (bf16[2,512,128]{2,1,0:T(8,128)(2,1)S(1)}, bf16[2,512,128]{2,1,0:T(8,128)(2,1)}, u32[]{:S(2)}) copy-start(bf16[2,512,128]{2,1,0:T(8,128)(2,1)} %get-tuple-element.36) | copy-start | bytes 786436
  197.4 65.2 %all-to-all-start.5 = ((bf16[32,2,128,128]{3,2,1,0:T(8,128)(2,1)}), bf16[32,2,128,128]{3,2,1,0:T(8,128)(2,1)S(1)}, u32[]{:S(2)}, u32[]{:S(2)}) async-start(bf16[32,2,128,128]{3,2,1,0:T(8,128)(2,1)} %clean.7), calls=%async_computation.5 | async-start | bytes 4194304 | tf_op jit(solution)/shard_map/all_to_all | solution.py:338
  203.7 3.7 %collective-permute-start = (bf16[2,512,128]{2,1,0:T(8,128)(2,1)}, bf16[2,512,128]{2,1,0:T(8,128)(2,1)S(1)}, u32[]{:S(2)}, u32[]{:S(2)}) collective-permute-start(bf16[2,512,128]{2,1,0:T(8,128)(2,1)} %get-tuple-element.30), channel_id=1, source_target_pairs={{0,1},{1,0},{2,3},{3,2},{4,5},{5,4},{6,7},{7,6},{8,9},{9,8},{10,11... | collective-permute-start | bytes 786440 | tf_op jit(solution)/shard_map/ppermute | solution.py:344
  203.9 21.6 %collective-permute-start.1 = (bf16[2,512,128]{2,1,0:T(8,128)(2,1)}, bf16[2,512,128]{2,1,0:T(8,128)(2,1)S(1)}, u32[]{:S(2)}, u32[]{:S(2)}) collective-permute-start(bf16[2,512,128]{2,1,0:T(8,128)(2,1)} %get-tuple-element.31), channel_id=1, source_target_pairs={{0,2},{1,3},{2,0},{3,1},{4,6},{5,7},{6,4},{7,5},{8,10},{9,11},{10,... | collective-permute-start | bytes 786440 | tf_op jit(solution)/shard_map/ppermute | solution.py:344
  205.4 31.3 %collective-permute-start.2 = (bf16[2,512,128]{2,1,0:T(8,128)(2,1)S(1)}, bf16[2,512,128]{2,1,0:T(8,128)(2,1)S(1)}, u32[]{:S(2)}, u32[]{:S(2)}) collective-permute-start(bf16[2,512,128]{2,1,0:T(8,128)(2,1)S(1)} %copy-done.10), channel_id=1, source_target_pairs={{0,3},{1,2},{2,1},{3,0},{4,7},{5,6},{6,5},{7,4},{8,11},{9,10},{10,... | collective-permute-start | bytes 786440 | tf_op jit(solution)/shard_map/ppermute | solution.py:344
  205.6 31.0 %collective-permute-start.3 = (bf16[2,512,128]{2,1,0:T(8,128)(2,1)S(1)}, bf16[2,512,128]{2,1,0:T(8,128)(2,1)S(1)}, u32[]{:S(2)}, u32[]{:S(2)}) collective-permute-start(bf16[2,512,128]{2,1,0:T(8,128)(2,1)S(1)} %copy-done.9), channel_id=1, source_target_pairs={{0,4},{1,5},{2,6},{3,7},{4,0},{5,1},{6,2},{7,3},{8,12},{9,13},{10,... | collective-permute-start | bytes 786440 | tf_op jit(solution)/shard_map/ppermute | solution.py:344
  207.1 29.6 %collective-permute-start.4 = (bf16[2,512,128]{2,1,0:T(8,128)(2,1)S(1)}, bf16[2,512,128]{2,1,0:T(8,128)(2,1)S(1)}, u32[]{:S(2)}, u32[]{:S(2)}) collective-permute-start(bf16[2,512,128]{2,1,0:T(8,128)(2,1)S(1)} %copy-done.8), channel_id=1, source_target_pairs={{0,5},{1,4},{2,7},{3,6},{4,1},{5,0},{6,3},{7,2},{8,13},{9,12},{10,... | collective-permute-start | bytes 786440 | tf_op jit(solution)/shard_map/ppermute | solution.py:344
  207.4 45.8 %copy-start.16 = (bf16[2,512,128]{2,1,0:T(8,128)(2,1)}, bf16[2,512,128]{2,1,0:T(8,128)(2,1)S(1)}, u32[]{:S(2)}) copy-start(bf16[2,512,128]{2,1,0:T(8,128)(2,1)S(1)} %collective-permute-done.refs_1_) | copy-start | bytes 786436
  207.4 38.4 %collective-permute-start.5 = (bf16[2,512,128]{2,1,0:T(8,128)(2,1)S(1)}, bf16[2,512,128]{2,1,0:T(8,128)(2,1)S(1)}, u32[]{:S(2)}, u32[]{:S(2)}) collective-permute-start(bf16[2,512,128]{2,1,0:T(8,128)(2,1)S(1)} %copy-done.7), channel_id=1, source_target_pairs={{0,6},{1,7},{2,4},{3,5},{4,2},{5,3},{6,0},{7,1},{8,14},{9,15},{10,... | collective-permute-start | bytes 786440 | tf_op jit(solution)/shard_map/ppermute | solution.py:344
  225.5 27.7 %copy-start.17 = (bf16[2,512,128]{2,1,0:T(8,128)(2,1)}, bf16[2,512,128]{2,1,0:T(8,128)(2,1)S(1)}, u32[]{:S(2)}) copy-start(bf16[2,512,128]{2,1,0:T(8,128)(2,1)S(1)} %collective-permute-done.1.refs_2_) | copy-start | bytes 786436
  225.5 27.6 %collective-permute-start.6 = (bf16[2,512,128]{2,1,0:T(8,128)(2,1)S(1)}, bf16[2,512,128]{2,1,0:T(8,128)(2,1)S(1)}, u32[]{:S(2)}, u32[]{:S(2)}) collective-permute-start(bf16[2,512,128]{2,1,0:T(8,128)(2,1)S(1)} %copy-done.6), channel_id=1, source_target_pairs={{0,7},{1,6},{2,5},{3,4},{4,3},{5,2},{6,1},{7,0},{8,15},{9,14},{10,... | collective-permute-start | bytes 786440 | tf_op jit(solution)/shard_map/ppermute | solution.py:344
  236.6 16.6 %copy-start.19 = (bf16[2,512,128]{2,1,0:T(8,128)(2,1)}, bf16[2,512,128]{2,1,0:T(8,128)(2,1)S(1)}, u32[]{:S(2)}) copy-start(bf16[2,512,128]{2,1,0:T(8,128)(2,1)S(1)} %collective-permute-done.2.refs_3_) | copy-start | bytes 786436
  236.6 16.6 %copy-start.22 = (bf16[2,512,128]{2,1,0:T(8,128)(2,1)}, bf16[2,512,128]{2,1,0:T(8,128)(2,1)S(1)}, u32[]{:S(2)}) copy-start(bf16[2,512,128]{2,1,0:T(8,128)(2,1)S(1)} %collective-permute-done.3.refs_4_) | copy-start | bytes 786436
  236.6 16.6 %copy-start.25 = (bf16[2,512,128]{2,1,0:T(8,128)(2,1)}, bf16[2,512,128]{2,1,0:T(8,128)(2,1)S(1)}, u32[]{:S(2)}) copy-start(bf16[2,512,128]{2,1,0:T(8,128)(2,1)S(1)} %collective-permute-done.4.refs_5_) | copy-start | bytes 786436
  263.9 51.2 %all-to-all-start.1 = ((bf16[32,2,128,128]{3,2,1,0:T(8,128)(2,1)}), bf16[32,2,128,128]{3,2,1,0:T(8,128)(2,1)}, u32[]{:S(2)}, u32[]{:S(2)}) async-start(bf16[32,2,128,128]{3,2,1,0:T(8,128)(2,1)} %clean.4), calls=%async_computation.1 | async-start | bytes 4194304 | tf_op jit(solution)/shard_map/all_to_all | solution.py:338
  (16 other events, 82.6 us)

commit v9 on v8

--- a/solution.py
+++ b/solution.py
@@ -135,6 +135,8 @@
 def partner(at, step, count):
     if count & (count - 1):
         return (count - at + step) % count
+    if step:
+        step = sorted(range(1, count), key=lambda n: (-bin(n // 2).count("1"), -n))[step - 1]
     return at ^ step
 
 
@@ -176,8 +178,9 @@
     )(at, x, jnp.asarray(twiddle_table(length)), jnp.asarray(inner_table(inner)))
 
 
-def clean_kernel(split, at_ref, *refs):
-    *x_refs, basis_ref, basis_t_ref, gain_ref, swap_ref, back_ref, out_ref, slab = refs
+def clean_kernel(split, waits, at_ref, *refs):
+    *refs, out_ref, slab = refs
+    *x_refs, basis_ref, basis_t_ref, gain_ref, swap_ref, back_ref = refs[: len(refs) - waits]
     chans = slab.shape[0]
     rows_dev = slab.shape[1] // LANES
     tall = swap_ref.shape[0]
@@ -209,7 +212,7 @@
         ).astype(jnp.bfloat16)
         drop = jnp.dot(basis_ref[...], front, preferred_element_type=jnp.float32)
         slab[:, lanes] = (line.astype(jnp.float32) - drop).astype(jnp.bfloat16)
-    out_rows = out_ref.shape[2]
+    out_rows = out_ref.shape[3]
     tall = back_ref.shape[0]
     group = tall // rows_dev
     for b in range(chans // group):
@@ -220,15 +223,15 @@
         value = jnp.dot(back_ref[...], tile, preferred_element_type=jnp.float32)
         if out_rows % tall == 0:
             target, row = divmod(b * tall, out_rows)
-            out_ref[target, 0, row : row + tall, :] = value.astype(jnp.bfloat16)
+            out_ref[target, 0, 0, row : row + tall, :] = value.astype(jnp.bfloat16)
         else:
             take = tall // out_rows
-            out_ref[b * take : (b + 1) * take, 0] = value.reshape(take, out_rows, LANES).astype(
-                jnp.bfloat16
-            )
-
-
-def clean(at, xs, basis, basis_t, gain, targets, rows_dev):
+            out_ref[b * take : (b + 1) * take, 0, 0] = value.reshape(
+                take, out_rows, LANES
+            ).astype(jnp.bfloat16)
+
+
+def clean(at, xs, basis, basis_t, gain, targets, rows_dev, slot, slots, before):
     split = len(xs) > 1
     chans = basis.shape[0]
     sources = len(xs) if split else xs[0].shape[0]
@@ -242,7 +245,7 @@
     else:
         spec = pl.BlockSpec((sources, 1, own * rows_dev, LANES), lambda s, at: (0, s, 0, 0))
     return pl.pallas_call(
-        functools.partial(clean_kernel, split),
+        functools.partial(clean_kernel, split, len(before)),
         grid_spec=pltpu.PrefetchScalarGridSpec(
             num_scalar_prefetch=1,
             grid=(2,),
@@ -253,11 +256,15 @@
                 pl.BlockSpec(gain.shape, whole),
                 pl.BlockSpec(swap.shape, whole),
                 pl.BlockSpec(back.shape, whole),
-            ],
-            out_specs=pl.BlockSpec((targets, 1, out_rows, LANES), lambda s, at: (0, s, 0, 0)),
+            ]
+            + [pl.BlockSpec(memory_space=pl.ANY)] * len(before),
+            out_specs=pl.BlockSpec(
+                (targets, 1, 1, out_rows, LANES), lambda s, at: (0, slot, s, 0, 0)
+            ),
             scratch_shapes=[pltpu.VMEM((chans, rows_dev * LANES), jnp.bfloat16)],
         ),
-        out_shape=jax.ShapeDtypeStruct((targets, 2, out_rows, LANES), jnp.bfloat16),
+        out_shape=jax.ShapeDtypeStruct((targets, slots, 2, out_rows, LANES), jnp.bfloat16),
+        input_output_aliases={6 + len(xs): 0} if slot else {},
         compiler_params=params(),
         cost_estimate=pl.CostEstimate(
             flops=12 * chans * chans * rows_dev * LANES,
@@ -265,15 +272,15 @@
             transcendentals=0,
         ),
         name="clean",
-    )(at, *xs, basis, basis_t, gain, jnp.asarray(swap), jnp.asarray(back))
+    )(at, *xs, basis, basis_t, gain, jnp.asarray(swap), jnp.asarray(back), *before)
 
 
 def image_kernel(scale, x_ref, table_ref, order_ref, *refs):
     out_ref = refs[-1]
-    z, _, parts, rows, _ = x_ref.shape
+    z, _, _, parts, rows, _ = x_ref.shape
     tiles = []
     for y_lo in range(RADIX):
-        tile = x_ref[:, y_lo]
+        tile = x_ref[:, y_lo, 0]
         if rows % 16:
             tile = tile.astype(jnp.float32)
         tile = tile.reshape(z * parts * rows, LANES).astype(jnp.bfloat16)
@@ -284,8 +291,8 @@
     out_ref[...] = value.astype(jnp.bfloat16).reshape(out_ref.shape)
 
 
-def image(x, chunk, count, rows_dev, held):
-    z, pieces, _, rows, _ = x.shape
+def image(x, slot, chunk, count, rows_dev, held):
+    z, pieces, _, _, rows, _ = x.shape
     chans = rows // rows_dev
     total = z * rows_dev
     spread = pieces // RADIX
@@ -298,7 +305,9 @@
         functools.partial(image_kernel, scale),
         grid=(chans // group, spread),
         in_specs=[
-            pl.BlockSpec((z, RADIX, 2, group * rows_dev, LANES), lambda c, g: (0, g, 0, c, 0)),
+            pl.BlockSpec(
+                (z, RADIX, 1, 2, group * rows_dev, LANES), lambda c, g: (0, g, slot, 0, c, 0)
+            ),
             pl.BlockSpec(table.shape, lambda c, g: (0, 0)),
             pl.BlockSpec(order.shape, lambda c, g: (0, 0)),
         ]
@@ -367,12 +376,19 @@
         cells += [
             scatter(sends[k * chan_count : (k + 1) * chan_count]) for k in range(count - 1)
         ]
-    held = []
-    for k in range(count):
-        cleaned = clean(at, cells[k], basis, basis_t, gain, targets, rows_dev)
-        planes = exchange(cleaned, ("uv", "chan"))
+    groups = [[0]] + [g for g in (list(range(1, count - 1)), [count - 1]) if g and count > 1]
+    held, cleaned = [], []
+    for chunks in groups:
+        for slot, k in enumerate(chunks):
+            cleaned = [
+                clean(
+                    at, cells[k], basis, basis_t, gain, targets, rows_dev, slot, len(chunks), cleaned
+                )
+            ]
+        planes = exchange(cleaned[0], ("uv", "chan"))
         planes = planes.reshape((uv_count, chan_count) + planes.shape[1:])
-        held = [image(planes, k, count, rows_dev, held)]
+        for slot, k in enumerate(chunks):
+            held = [image(planes, slot, k, count, rows_dev, held)]
     return held[0]
 
 

time: 326 us -> 315 us (0.966)
  starting transfers between devices: 46.5 us -> 40.9 us
  waiting for transfers between devices: 174 us -> 170 us
    all_to_all x6 -> x5, starting transfers between devices: 27.3 us -> 23.2 us  [exchange(): return lax.all_to_all(x, axes, split_axis=0, concat_axis=0, tiled=True)]
    all_to_all x6 -> x5, waiting for transfers between devices: 66 us -> 64.3 us  [exchange(): return lax.all_to_all(x, axes, split_axis=0, concat_axis=0, tiled=True)]
    unnamed x74 -> x64, local copies, waits for them, and re-layouts: 6.94 us -> 5.88 us
  transfers between devices with their start and end apart: 27 -> 26, of which waited for: 15 -> 16; matrix products, arithmetic and copies ran while one was open for 0% -> 0% of each run, Pallas kernels for 26% -> 25%
where the time goes in v9:
time: 315 us; the launch traced here: 311 us
  waiting for transfers between devices  170 us (54%)
  Pallas kernels  91.2 us (29%)
  starting transfers between devices  40.9 us (13%)
  local copies, waits for them, and re-layouts  7.58 us (2%)
    ppermute x21, waiting for transfers between devices, scatter(): lax.ppermute(pieces[step], 'chan', [(j, int(partner(np.int32(j), step, co...  105 us
    all_to_all x5, waiting for transfers between devices, exchange(): return lax.all_to_all(x, axes, split_axis=0, concat_axis=0, tiled=True)  64.3 us
    pallas_call x4, Pallas kernels, clean(): pl.pallas_call(functools.partial(clean_kernel, split, len(before)), grid_...  33.9 us
    pallas_call x2, Pallas kernels, column_transform(): pl.pallas_call(functools.partial(column_kernel, chunks, pieces // RADIX,...  29.4 us
    pallas_call x4, Pallas kernels, image(): pl.pallas_call(functools.partial(image_kernel, scale), grid=(chans // gro...  25.9 us
    all_to_all x5, starting transfers between devices, exchange(): return lax.all_to_all(x, axes, split_axis=0, concat_axis=0, tiled=True)  23.2 us
    ppermute x21, starting transfers between devices, scatter(): lax.ppermute(pieces[step], 'chan', [(j, int(partner(np.int32(j), step, co...  17.7 us
  transfers between devices with their start and end apart: 26, of which 16 were waited for; matrix products, arithmetic and copies ran while one was open for 0% of the time, Pallas kernels for 25%

profile of v9, /device:TPU:8, one launch (start us, length us, event | category | flops | bytes accessed | tf_op | source)
XLA Modules:
  0.0 310.6 jit_solution(16323539253185313369)
XLA Ops:
  0.0 1.7 broadcast_in_dim.2
  1.7 3.7 %all-to-all-start = ((bf16[8,64,512]{2,1,0:T(8,128)(2,1)}), bf16[8,64,512]{2,1,0:T(8,128)(2,1)S(1)}, u32[]{:S(2)}, u32[]{:S(2)}) async-start(bf16[8,64,512]{2,1,0:T(8,128)(2,1)} %broadcast_in_dim.2), calls=%async_computation | async-start | bytes 1048576 | tf_op jit(solution)/shard_map/all_to_all | solution.py:347
  5.4 11.9 %column_transform.3 = bf16[8,2,512,128]{3,2,1,0:T(8,128)(2,1)} custom-call(s32[1]{0:T(128)} %bitcast.at_ref, bf16[2,512,4096]{2,1,0:T(8,128)(2,1)} %bitcast.13, f32[8,2,512]{2,1,0:T(2,128)} %constant.16.clone.twiddle_ref, bf16[1024,1024]{1,0:T(8,128)(2,1)} %constant.17.clone.table_ref), custom_call_target="tpu_custom_call" | custom-call | flops 8589934592 | bytes 16777216 | tf_op jit(solution)/shard_map/column_transform/pallas_call | solution.py:157
  17.3 4.2 %all-to-all-start.1 = ((bf16[8,2,512,128]{3,2,1,0:T(8,128)(2,1)}), bf16[8,2,512,128]{3,2,1,0:T(8,128)(2,1)S(1)}, u32[]{:S(2)}, u32[]{:S(2)}) async-start(bf16[8,2,512,128]{3,2,1,0:T(8,128)(2,1)} %column_transform.3), calls=%async_computation.1 | async-start | bytes 4194304 | tf_op jit(solution)/shard_map/all_to_all | solution.py:347
  21.5 0.9 add_divide_fusion.refs_3_.refs_10_
  22.4 2.0 turn.1.refs_2_.refs_9_
  24.4 23.7 %all-to-all-done.1.refs_0_ = bf16[8,2,512,128]{3,2,1,0:T(8,128)(2,1)S(1)} async-done(((bf16[8,2,512,128]{3,2,1,0:T(8,128)(2,1)}), bf16[8,2,512,128]{3,2,1,0:T(8,128)(2,1)S(1)}, u32[]{:S(2)}, u32[]{:S(2)}) %all-to-all-start.1) | async-done | bytes 2097184 | tf_op jit(solution)/shard_map/all_to_all | solution.py:347
  48.2 1.3 copy-done.3
  49.5 8.1 %clean.4.refs_13_ = bf16[32,1,2,128,128]{4,3,2,1,0:T(8,128)(2,1)} custom-call(s32[1]{0:T(128)} %bitcast.at_ref, bf16[8,2,512,128]{3,2,1,0:T(8,128)(2,1)} %copy-done.3, bf16[512,512]{1,0:T(8,128)(2,1)} %bitcast.9, bf16[512,512]{1,0:T(8,128)(2,1)} %turn.1.refs_2_.refs_9_, f32[512,8]{1,0:T(8,128)} %add_divide_fusion.refs_3_.refs_10_, ...), custom_call_target="tpu_custom_call" | custom-call | flops 3221225472 | bytes 4194304 | tf_op jit(solution)/shard_map/clean/pallas_call | solution.py:247
  57.5 4.2 %all-to-all-start.4 = ((bf16[32,1,2,128,128]{4,3,2,1,0:T(8,128)(2,1)}), bf16[32,1,2,128,128]{4,3,2,1,0:T(8,128)(2,1)S(1)}, u32[]{:S(2)}, u32[]{:S(2)}) async-start(bf16[32,1,2,128,128]{4,3,2,1,0:T(8,128)(2,1)} %clean.4.refs_13_), calls=%async_computation.4 | async-start | bytes 4194304 | tf_op jit(solution)/shard_map/all_to_all | solution.py:347
  61.8 17.5 %column_transform.2 = (bf16[2,512,128]{2,1,0:T(8,128)(2,1)}, bf16[2,512,128]{2,1,0:T(8,128)(2,1)}, bf16[2,512,128]{2,1,0:T(8,128)(2,1)}, bf16[2,512,128]{2,1,0:T...) custom-call(s32[1]{0:T(128)} %bitcast.at_ref, ...), custom_call_target="tpu_custom_call" | custom-call | flops 25769803776 | bytes 16777216 | tf_op jit(solution)/shard_map/column_transform/pallas_call | solution.py:157
  79.3 2.2 collective-permute-start.7
  82.0 2.0 collective-permute-start.14
  84.1 0.6 collective-permute-start.15
  84.6 1.2 collective-permute-start.16
  85.8 9.9 %collective-permute-done.7.refs_1_ = bf16[2,512,128]{2,1,0:T(8,128)(2,1)S(1)} collective-permute-done((bf16[2,512,128]{2,1,0:T(8,128)(2,1)}, bf16[2,512,128]{2,1,0:T(8,128)(2,1)S(1)}, u32[]{:S(2)}, u32[]{:S(2)}) %collective-permute-start.7) | collective-permute-done | bytes 262176 | tf_op jit(solution)/shard_map/ppermute | solution.py:353
  95.7 2.3 collective-permute-start.17
  98.0 6.2 %collective-permute-done.8.refs_2_ = bf16[2,512,128]{2,1,0:T(8,128)(2,1)S(1)} collective-permute-done((bf16[2,512,128]{2,1,0:T(8,128)(2,1)}, bf16[2,512,128]{2,1,0:T(8,128)(2,1)S(1)}, u32[]{:S(2)}, u32[]{:S(2)}) %collective-permute-start.8) | collective-permute-done | bytes 262176 | tf_op jit(solution)/shard_map/ppermute | solution.py:353
  104.6 7.8 %collective-permute-done.14.refs_1_ = bf16[2,512,128]{2,1,0:T(8,128)(2,1)S(1)} collective-permute-done((bf16[2,512,128]{2,1,0:T(8,128)(2,1)}, bf16[2,512,128]{2,1,0:T(8,128)(2,1)S(1)}, u32[]{:S(2)}, u32[]{:S(2)}) %collective-permute-start.14) | collective-permute-done | bytes 262176 | tf_op jit(solution)/shard_map/ppermute | solution.py:353
  112.3 1.1 collective-permute-start.19
  113.4 4.9 %collective-permute-done.15.refs_2_ = bf16[2,512,128]{2,1,0:T(8,128)(2,1)S(1)} collective-permute-done((bf16[2,512,128]{2,1,0:T(8,128)(2,1)}, bf16[2,512,128]{2,1,0:T(8,128)(2,1)S(1)}, u32[]{:S(2)}, u32[]{:S(2)}) %collective-permute-start.15) | collective-permute-done | bytes 262176 | tf_op jit(solution)/shard_map/ppermute | solution.py:353
  118.3 4.0 %collective-permute-done.16.refs_3_ = bf16[2,512,128]{2,1,0:T(8,128)(2,1)S(1)} collective-permute-done((bf16[2,512,128]{2,1,0:T(8,128)(2,1)}, bf16[2,512,128]{2,1,0:T(8,128)(2,1)S(1)}, u32[]{:S(2)}, u32[]{:S(2)}) %collective-permute-start.16) | collective-permute-done | bytes 262176 | tf_op jit(solution)/shard_map/ppermute | solution.py:353
  122.7 5.5 %collective-permute-done.17.refs_4_ = bf16[2,512,128]{2,1,0:T(8,128)(2,1)S(1)} collective-permute-done((bf16[2,512,128]{2,1,0:T(8,128)(2,1)}, bf16[2,512,128]{2,1,0:T(8,128)(2,1)S(1)}, u32[]{:S(2)}, u32[]{:S(2)}) %collective-permute-start.17) | collective-permute-done | bytes 262176 | tf_op jit(solution)/shard_map/ppermute | solution.py:353
  128.6 1.0 collective-permute-done.19.refs_6_
  130.7 8.6 %clean.5.refs_13_ = bf16[32,2,2,128,128]{4,3,2,1,0:T(8,128)(2,1)} custom-call(s32[1]{0:T(128)} %bitcast.at_ref, bf16[2,512,128]{2,1,0:T(8,128)(2,1)} %get-tuple-element.45.refs_0_, bf16[2,512,128]{2,1,0:T(8,128)(2,1)} %copy-done.18, bf16[2,512,128]{2,1,0:T(8,128)(2,1)} %copy-done.19, bf16[2,512,128]{2,1,0:T(8,128)(2,1)} %copy-done.20, ...), custom_call_target="tpu_custom_call" | custom-call | flops 3221225472 | bytes 4194304 | tf_op jit(solution)/shard_map/clean/pallas_call | solution.py:247
  139.4 2.9 collective-permute-done.12.refs_6_
  142.4 0.7 copy-done.9
  143.1 8.6 %clean.6.refs_13_ = bf16[32,2,2,128,128]{4,3,2,1,0:T(8,128)(2,1)} custom-call(s32[1]{0:T(128)} %bitcast.at_ref, bf16[2,512,128]{2,1,0:T(8,128)(2,1)} %get-tuple-element.37.refs_0_, bf16[2,512,128]{2,1,0:T(8,128)(2,1)} %copy-done.4, bf16[2,512,128]{2,1,0:T(8,128)(2,1)} %copy-done.5, bf16[2,512,128]{2,1,0:T(8,128)(2,1)} %copy-done.6, ...), custom_call_target="tpu_custom_call", output_to_operand_aliasing={{}: (14, {})} | custom-call | flops 3221225472 | bytes 4194304 | tf_op jit(solution)/shard_map/clean/pallas_call | solution.py:247
  151.8 1.4 copy-done
  153.2 4.0 %all-to-all-start.3 = ((bf16[32,2,2,128,128]{4,3,2,1,0:T(8,128)(2,1)}), bf16[32,2,2,128,128]{4,3,2,1,0:T(8,128)(2,1)}, u32[]{:S(2)}, u32[]{:S(2)}) async-start(bf16[32,2,2,128,128]{4,3,2,1,0:T(8,128)(2,1)} %clean.6.refs_13_), calls=%async_computation.3 | async-start | bytes 8388608 | tf_op jit(solution)/shard_map/all_to_all | solution.py:347
  157.2 2.2 collective-permute-start
  159.9 1.2 collective-permute-start.2
  161.6 1.2 collective-permute-start.4
  162.9 31.2 %collective-permute-done.refs_1_ = bf16[2,512,128]{2,1,0:T(8,128)(2,1)S(1)} collective-permute-done((bf16[2,512,128]{2,1,0:T(8,128)(2,1)}, bf16[2,512,128]{2,1,0:T(8,128)(2,1)S(1)}, u32[]{:S(2)}, u32[]{:S(2)}) %collective-permute-start) | collective-permute-done | bytes 262176 | tf_op jit(solution)/shard_map/ppermute | solution.py:353
  194.0 19.9 %collective-permute-done.1.refs_2_ = bf16[2,512,128]{2,1,0:T(8,128)(2,1)S(1)} collective-permute-done((bf16[2,512,128]{2,1,0:T(8,128)(2,1)}, bf16[2,512,128]{2,1,0:T(8,128)(2,1)S(1)}, u32[]{:S(2)}, u32[]{:S(2)}) %collective-permute-start.1) | collective-permute-done | bytes 262176 | tf_op jit(solution)/shard_map/ppermute | solution.py:353
  214.0 4.2 %collective-permute-done.3.refs_4_ = bf16[2,512,128]{2,1,0:T(8,128)(2,1)S(1)} collective-permute-done((bf16[2,512,128]{2,1,0:T(8,128)(2,1)S(1)}, bf16[2,512,128]{2,1,0:T(8,128)(2,1)S(1)}, u32[]{:S(2)}, u32[]{:S(2)}) %collective-permute-start.3) | collective-permute-done | bytes 262176 | tf_op jit(solution)/shard_map/ppermute | solution.py:353
  218.1 2.0 collective-permute-done.4.refs_5_
  220.2 6.1 %collective-permute-done.5.refs_6_ = bf16[2,512,128]{2,1,0:T(8,128)(2,1)S(1)} collective-permute-done((bf16[2,512,128]{2,1,0:T(8,128)(2,1)S(1)}, bf16[2,512,128]{2,1,0:T(8,128)(2,1)S(1)}, u32[]{:S(2)}, u32[]{:S(2)}) %collective-permute-start.5) | collective-permute-done | bytes 262176 | tf_op jit(solution)/shard_map/ppermute | solution.py:353
  226.4 0.7 copy-done.30
  227.1 8.6 %clean.7 = bf16[32,1,2,128,128]{4,3,2,1,0:T(8,128)(2,1)} custom-call(s32[1]{0:T(128)} %bitcast.at_ref, bf16[2,512,128]{2,1,0:T(8,128)(2,1)} %get-tuple-element.29.refs_0_, bf16[2,512,128]{2,1,0:T(8,128)(2,1)} %copy-done.23, bf16[2,512,128]{2,1,0:T(8,128)(2,1)} %copy-done.24, bf16[2,512,128]{2,1,0:T(8,128)(2,1)} %copy-done.26, ...), custom_call_target="tpu_custom_call" | custom-call | flops 3221225472 | bytes 4194304 | tf_op jit(solution)/shard_map/clean/pallas_call | solution.py:247
  235.7 13.3 %all-to-all-done.3 = bf16[32,2,2,128,128]{4,3,2,1,0:T(8,128)(2,1)} async-done(((bf16[32,2,2,128,128]{4,3,2,1,0:T(8,128)(2,1)}), bf16[32,2,2,128,128]{4,3,2,1,0:T(8,128)(2,1)}, u32[]{:S(2)}, u32[]{:S(2)}) %all-to-all-start.3) | async-done | bytes 4194336 | tf_op jit(solution)/shard_map/all_to_all | solution.py:347
  249.0 7.1 %all-to-all-start.2 = ((bf16[32,1,2,128,128]{4,3,2,1,0:T(8,128)(2,1)}), bf16[32,1,2,128,128]{4,3,2,1,0:T(8,128)(2,1)S(1)}, u32[]{:S(2)}, u32[]{:S(2)}) async-start(bf16[32,1,2,128,128]{4,3,2,1,0:T(8,128)(2,1)} %clean.7), calls=%async_computation.2 | async-start | bytes 4194304 | tf_op jit(solution)/shard_map/all_to_all | solution.py:347
  256.1 6.5 %image.4.refs_0_ = bf16[2,16,32,4096]{3,2,1,0:T(8,128)(2,1)} custom-call(bf16[4,8,1,2,128,128]{5,4,3,2,1,0:T(8,128)(2,1)} %bitcast.6, bf16[256,256]{1,0:T(8,128)(2,1)} %constant.20.clone.table_ref, bf16[1024,1024]{1,0:T(8,128)(2,1)} %constant.21.clone.order_ref), custom_call_target="tpu_custom_call" | custom-call | flops 2147483648 | bytes 4194304 | tf_op jit(solution)/shard_map/image/pallas_call | solution.py:304
  262.6 6.5 %image.5.refs_0_ = bf16[2,16,32,4096]{3,2,1,0:T(8,128)(2,1)} custom-call(bf16[4,8,2,2,128,128]{5,4,3,2,1,0:T(8,128)(2,1)} %bitcast.4.x_ref, bf16[256,256]{1,0:T(8,128)(2,1)} %constant.20.clone.table_ref, bf16[1024,1024]{1,0:T(8,128)(2,1)} %constant.21.clone.order_ref, bf16[2,16,32,4096]{3,2,1,0:T(8,128)(2,1)} %image.4.refs_0_), custom_call_target="tpu_custom_call", output_to_operand_aliasing={{}: (3, {})} | custom-call | flops 2147483648 | bytes 4194304 | tf_op jit(solution)/shard_map/image/pallas_call | solution.py:304
  269.1 6.5 %image.6.refs_0_ = bf16[2,16,32,4096]{3,2,1,0:T(8,128)(2,1)} custom-call(bf16[4,8,2,2,128,128]{5,4,3,2,1,0:T(8,128)(2,1)} %bitcast.4.x_ref, bf16[256,256]{1,0:T(8,128)(2,1)} %constant.20.clone.table_ref, bf16[1024,1024]{1,0:T(8,128)(2,1)} %constant.21.clone.order_ref, bf16[2,16,32,4096]{3,2,1,0:T(8,128)(2,1)} %image.5.refs_0_), custom_call_target="tpu_custom_call", output_to_operand_aliasing={{}: (3, {})} | custom-call | flops 2147483648 | bytes 4194304 | tf_op jit(solution)/shard_map/image/pallas_call | solution.py:304
  275.6 27.2 %all-to-all-done.2 = bf16[32,1,2,128,128]{4,3,2,1,0:T(8,128)(2,1)S(1)} async-done(((bf16[32,1,2,128,128]{4,3,2,1,0:T(8,128)(2,1)}), bf16[32,1,2,128,128]{4,3,2,1,0:T(8,128)(2,1)S(1)}, u32[]{:S(2)}, u32[]{:S(2)}) %all-to-all-start.2) | async-done | bytes 2097184 | tf_op jit(solution)/shard_map/all_to_all | solution.py:347
  302.8 1.4 copy-done.1
  304.1 6.4 %image.7 = bf16[2,16,32,4096]{3,2,1,0:T(8,128)(2,1)} custom-call(bf16[4,8,1,2,128,128]{5,4,3,2,1,0:T(8,128)(2,1)} %bitcast.7, bf16[256,256]{1,0:T(8,128)(2,1)} %constant.20.clone.table_ref, bf16[1024,1024]{1,0:T(8,128)(2,1)} %constant.21.clone.order_ref, bf16[2,16,32,4096]{3,2,1,0:T(8,128)(2,1)} %image.6.refs_0_), custom_call_target="tpu_custom_call", output_to_operand_aliasing={{}: (3, {})} | custom-call | flops 2147483648 | bytes 4194304 | tf_op jit(solution)/shard_map/image/pallas_call | solution.py:304
  (81 shorter events, 4.1 us)
Async XLA Ops:
  1.7 15.6 %all-to-all-start = ((bf16[8,64,512]{2,1,0:T(8,128)(2,1)}), bf16[8,64,512]{2,1,0:T(8,128)(2,1)S(1)}, u32[]{:S(2)}, u32[]{:S(2)}) async-start(bf16[8,64,512]{2,1,0:T(8,128)(2,1)} %broadcast_in_dim.2), calls=%async_computation | async-start | bytes 1048576 | tf_op jit(solution)/shard_map/all_to_all | solution.py:347
  17.3 4.2 %copy-start.11 = (f32[512]{0:T(512)S(1)}, f32[512]{0:T(512)}, u32[]{:S(2)}) copy-start(f32[512]{0:T(512)} %param.26) | copy-start | bytes 6148
  17.3 4.2 %copy-start.12 = (f32[8]{0:T(128)S(1)}, f32[8]{0:T(128)}, u32[]{:S(2)}) copy-start(f32[8]{0:T(128)} %param.27) | copy-start | bytes 100
  17.3 5.1 %copy-start.2 = (bf16[8,64,512]{2,1,0:T(8,128)(2,1)}, bf16[8,64,512]{2,1,0:T(8,128)(2,1)S(1)}, u32[]{:S(2)}) copy-start(bf16[8,64,512]{2,1,0:T(8,128)(2,1)S(1)} %all-to-all-done) | copy-start | bytes 1572868
  17.3 30.8 %all-to-all-start.1 = ((bf16[8,2,512,128]{3,2,1,0:T(8,128)(2,1)}), bf16[8,2,512,128]{3,2,1,0:T(8,128)(2,1)S(1)}, u32[]{:S(2)}, u32[]{:S(2)}) async-start(bf16[8,2,512,128]{3,2,1,0:T(8,128)(2,1)} %column_transform.3), calls=%async_computation.1 | async-start | bytes 4194304 | tf_op jit(solution)/shard_map/all_to_all | solution.py:347
  57.5 94.3 %all-to-all-start.4 = ((bf16[32,1,2,128,128]{4,3,2,1,0:T(8,128)(2,1)}), bf16[32,1,2,128,128]{4,3,2,1,0:T(8,128)(2,1)S(1)}, u32[]{:S(2)}, u32[]{:S(2)}) async-start(bf16[32,1,2,128,128]{4,3,2,1,0:T(8,128)(2,1)} %clean.4.refs_13_), calls=%async_computation.4 | async-start | bytes 4194304 | tf_op jit(solution)/shard_map/all_to_all | solution.py:347
  79.3 16.4 %collective-permute-start.7 = (bf16[2,512,128]{2,1,0:T(8,128)(2,1)}, bf16[2,512,128]{2,1,0:T(8,128)(2,1)S(1)}, u32[]{:S(2)}, u32[]{:S(2)}) collective-permute-start(bf16[2,512,128]{2,1,0:T(8,128)(2,1)} %get-tuple-element.38), channel_id=1, source_target_pairs={{0,7},{1,6},{2,5},{3,4},{4,3},{5,2},{6,1},{7,0},{8,15},{9,14},{10,... | collective-permute-start | bytes 786440 | tf_op jit(solution)/shard_map/ppermute | solution.py:353
  81.5 22.8 %collective-permute-start.8 = (bf16[2,512,128]{2,1,0:T(8,128)(2,1)}, bf16[2,512,128]{2,1,0:T(8,128)(2,1)S(1)}, u32[]{:S(2)}, u32[]{:S(2)}) collective-permute-start(bf16[2,512,128]{2,1,0:T(8,128)(2,1)} %get-tuple-element.39), channel_id=1, source_target_pairs={{0,6},{1,7},{2,4},{3,5},{4,2},{5,3},{6,0},{7,1},{8,14},{9,15},{10,... | collective-permute-start | bytes 786440 | tf_op jit(solution)/shard_map/ppermute | solution.py:353
  82.0 30.3 %collective-permute-start.14 = (bf16[2,512,128]{2,1,0:T(8,128)(2,1)}, bf16[2,512,128]{2,1,0:T(8,128)(2,1)S(1)}, u32[]{:S(2)}, u32[]{:S(2)}) collective-permute-start(bf16[2,512,128]{2,1,0:T(8,128)(2,1)} %get-tuple-element.46), channel_id=1, source_target_pairs={{0,7},{1,6},{2,5},{3,4},{4,3},{5,2},{6,1},{7,0},{8,15},{9,14},{10,... | collective-permute-start | bytes 786440 | tf_op jit(solution)/shard_map/ppermute | solution.py:353
  84.1 34.2 %collective-permute-start.15 = (bf16[2,512,128]{2,1,0:T(8,128)(2,1)}, bf16[2,512,128]{2,1,0:T(8,128)(2,1)S(1)}, u32[]{:S(2)}, u32[]{:S(2)}) collective-permute-start(bf16[2,512,128]{2,1,0:T(8,128)(2,1)} %get-tuple-element.47), channel_id=1, source_target_pairs={{0,6},{1,7},{2,4},{3,5},{4,2},{5,3},{6,0},{7,1},{8,14},{9,15},{10,... | collective-permute-start | bytes 786440 | tf_op jit(solution)/shard_map/ppermute | solution.py:353
  84.6 37.6 %collective-permute-start.16 = (bf16[2,512,128]{2,1,0:T(8,128)(2,1)}, bf16[2,512,128]{2,1,0:T(8,128)(2,1)S(1)}, u32[]{:S(2)}, u32[]{:S(2)}) collective-permute-start(bf16[2,512,128]{2,1,0:T(8,128)(2,1)} %get-tuple-element.48), channel_id=1, source_target_pairs={{0,5},{1,4},{2,7},{3,6},{4,1},{5,0},{6,3},{7,2},{8,13},{9,12},{10,... | collective-permute-start | bytes 786440 | tf_op jit(solution)/shard_map/ppermute | solution.py:353
  95.7 43.6 %copy-start.4 = (bf16[2,512,128]{2,1,0:T(8,128)(2,1)}, bf16[2,512,128]{2,1,0:T(8,128)(2,1)S(1)}, u32[]{:S(2)}) copy-start(bf16[2,512,128]{2,1,0:T(8,128)(2,1)S(1)} %collective-permute-done.7.refs_1_) | copy-start | bytes 786436
  95.7 32.4 %collective-permute-start.17 = (bf16[2,512,128]{2,1,0:T(8,128)(2,1)}, bf16[2,512,128]{2,1,0:T(8,128)(2,1)S(1)}, u32[]{:S(2)}, u32[]{:S(2)}) collective-permute-start(bf16[2,512,128]{2,1,0:T(8,128)(2,1)} %get-tuple-element.49), channel_id=1, source_target_pairs={{0,4},{1,5},{2,6},{3,7},{4,0},{5,1},{6,2},{7,3},{8,12},{9,13},{10,... | collective-permute-start | bytes 786440 | tf_op jit(solution)/shard_map/ppermute | solution.py:353
  104.3 35.1 %copy-start.5 = (bf16[2,512,128]{2,1,0:T(8,128)(2,1)}, bf16[2,512,128]{2,1,0:T(8,128)(2,1)S(1)}, u32[]{:S(2)}) copy-start(bf16[2,512,128]{2,1,0:T(8,128)(2,1)S(1)} %collective-permute-done.8.refs_2_) | copy-start | bytes 786436
  104.3 24.3 %collective-permute-start.18 = (bf16[2,512,128]{2,1,0:T(8,128)(2,1)}, bf16[2,512,128]{2,1,0:T(8,128)(2,1)S(1)}, u32[]{:S(2)}, u32[]{:S(2)}) collective-permute-start(bf16[2,512,128]{2,1,0:T(8,128)(2,1)} %get-tuple-element.50), channel_id=1, source_target_pairs={{0,3},{1,2},{2,1},{3,0},{4,7},{5,6},{6,5},{7,4},{8,11},{9,10},{10,... | collective-permute-start | bytes 786440 | tf_op jit(solution)/shard_map/ppermute | solution.py:353
  112.3 18.1 %copy-start.18 = (bf16[2,512,128]{2,1,0:T(8,128)(2,1)}, bf16[2,512,128]{2,1,0:T(8,128)(2,1)S(1)}, u32[]{:S(2)}) copy-start(bf16[2,512,128]{2,1,0:T(8,128)(2,1)S(1)} %collective-permute-done.14.refs_1_) | copy-start | bytes 786436
  112.3 17.3 %collective-permute-start.19 = (bf16[2,512,128]{2,1,0:T(8,128)(2,1)}, bf16[2,512,128]{2,1,0:T(8,128)(2,1)S(1)}, u32[]{:S(2)}, u32[]{:S(2)}) collective-permute-start(bf16[2,512,128]{2,1,0:T(8,128)(2,1)} %get-tuple-element.51), channel_id=1, source_target_pairs={{0,2},{1,3},{2,0},{3,1},{4,6},{5,7},{6,4},{7,5},{8,10},{9,11},{10,... | collective-permute-start | bytes 786440 | tf_op jit(solution)/shard_map/ppermute | solution.py:353
  118.3 12.2 %copy-start.19 = (bf16[2,512,128]{2,1,0:T(8,128)(2,1)}, bf16[2,512,128]{2,1,0:T(8,128)(2,1)S(1)}, u32[]{:S(2)}) copy-start(bf16[2,512,128]{2,1,0:T(8,128)(2,1)S(1)} %collective-permute-done.15.refs_2_) | copy-start | bytes 786436
  118.3 11.7 %collective-permute-start.20 = (bf16[2,512,128]{2,1,0:T(8,128)(2,1)}, bf16[2,512,128]{2,1,0:T(8,128)(2,1)S(1)}, u32[]{:S(2)}, u32[]{:S(2)}) collective-permute-start(bf16[2,512,128]{2,1,0:T(8,128)(2,1)} %get-tuple-element.52), channel_id=1, source_target_pairs={{0,1},{1,0},{2,3},{3,2},{4,5},{5,4},{6,7},{7,6},{8,9},{9,8},{10,11... | collective-permute-start | bytes 786440 | tf_op jit(solution)/shard_map/ppermute | solution.py:353
  122.2 8.2 %copy-start.20 = (bf16[2,512,128]{2,1,0:T(8,128)(2,1)}, bf16[2,512,128]{2,1,0:T(8,128)(2,1)S(1)}, u32[]{:S(2)}) copy-start(bf16[2,512,128]{2,1,0:T(8,128)(2,1)S(1)} %collective-permute-done.16.refs_3_) | copy-start | bytes 786436
  122.2 17.1 %collective-permute-start.9 = (bf16[2,512,128]{2,1,0:T(8,128)(2,1)}, bf16[2,512,128]{2,1,0:T(8,128)(2,1)S(1)}, u32[]{:S(2)}, u32[]{:S(2)}) collective-permute-start(bf16[2,512,128]{2,1,0:T(8,128)(2,1)} %get-tuple-element.40), channel_id=1, source_target_pairs={{0,5},{1,4},{2,7},{3,6},{4,1},{5,0},{6,3},{7,2},{8,13},{9,12},{10,... | collective-permute-start | bytes 786440 | tf_op jit(solution)/shard_map/ppermute | solution.py:353
  128.2 2.3 copy-start.21
  128.2 11.2 %collective-permute-start.10 = (bf16[2,512,128]{2,1,0:T(8,128)(2,1)}, bf16[2,512,128]{2,1,0:T(8,128)(2,1)S(1)}, u32[]{:S(2)}, u32[]{:S(2)}) collective-permute-start(bf16[2,512,128]{2,1,0:T(8,128)(2,1)} %get-tuple-element.41), channel_id=1, source_target_pairs={{0,4},{1,5},{2,6},{3,7},{4,0},{5,1},{6,2},{7,3},{8,12},{9,13},{10,... | collective-permute-start | bytes 786440 | tf_op jit(solution)/shard_map/ppermute | solution.py:353
  128.6 10.8 %collective-permute-start.11 = (bf16[2,512,128]{2,1,0:T(8,128)(2,1)}, bf16[2,512,128]{2,1,0:T(8,128)(2,1)S(1)}, u32[]{:S(2)}, u32[]{:S(2)}) collective-permute-start(bf16[2,512,128]{2,1,0:T(8,128)(2,1)} %get-tuple-element.42), channel_id=1, source_target_pairs={{0,3},{1,2},{2,1},{3,0},{4,7},{5,6},{6,5},{7,4},{8,11},{9,10},{10,... | collective-permute-start | bytes 786440 | tf_op jit(solution)/shard_map/ppermute | solution.py:353
  129.6 12.7 %collective-permute-start.12 = (bf16[2,512,128]{2,1,0:T(8,128)(2,1)}, bf16[2,512,128]{2,1,0:T(8,128)(2,1)S(1)}, u32[]{:S(2)}, u32[]{:S(2)}) collective-permute-start(bf16[2,512,128]{2,1,0:T(8,128)(2,1)} %get-tuple-element.43), channel_id=1, source_target_pairs={{0,2},{1,3},{2,0},{3,1},{4,6},{5,7},{6,4},{7,5},{8,10},{9,11},{10,... | collective-permute-start | bytes 786440 | tf_op jit(solution)/shard_map/ppermute | solution.py:353
  130.0 12.3 %collective-permute-start.13 = (bf16[2,512,128]{2,1,0:T(8,128)(2,1)}, bf16[2,512,128]{2,1,0:T(8,128)(2,1)S(1)}, u32[]{:S(2)}, u32[]{:S(2)}) collective-permute-start(bf16[2,512,128]{2,1,0:T(8,128)(2,1)} %get-tuple-element.44), channel_id=1, source_target_pairs={{0,1},{1,0},{2,3},{3,2},{4,5},{5,4},{6,7},{7,6},{8,9},{9,8},{10,11... | collective-permute-start | bytes 786440 | tf_op jit(solution)/shard_map/ppermute | solution.py:353
  139.4 3.0 copy-start.6
  139.4 3.0 copy-start.7
  139.4 3.0 copy-start.8
  151.7 8.2 %copy-start.17 = (bf16[2,512,128]{2,1,0:T(8,128)(2,1)S(1)}, bf16[2,512,128]{2,1,0:T(8,128)(2,1)}, u32[]{:S(2)}) copy-start(bf16[2,512,128]{2,1,0:T(8,128)(2,1)} %get-tuple-element.32) | copy-start | bytes 786436
  151.8 9.3 %copy-start.16 = (bf16[2,512,128]{2,1,0:T(8,128)(2,1)S(1)}, bf16[2,512,128]{2,1,0:T(8,128)(2,1)}, u32[]{:S(2)}) copy-start(bf16[2,512,128]{2,1,0:T(8,128)(2,1)} %get-tuple-element.33) | copy-start | bytes 786436
  151.8 9.9 %copy-start.15 = (bf16[2,512,128]{2,1,0:T(8,128)(2,1)S(1)}, bf16[2,512,128]{2,1,0:T(8,128)(2,1)}, u32[]{:S(2)}) copy-start(bf16[2,512,128]{2,1,0:T(8,128)(2,1)} %get-tuple-element.34) | copy-start | bytes 786436
  151.8 42.3 %copy-start.14 = (bf16[2,512,128]{2,1,0:T(8,128)(2,1)S(1)}, bf16[2,512,128]{2,1,0:T(8,128)(2,1)}, u32[]{:S(2)}) copy-start(bf16[2,512,128]{2,1,0:T(8,128)(2,1)} %get-tuple-element.35) | copy-start | bytes 786436
  151.8 62.2 %copy-start.13 = (bf16[2,512,128]{2,1,0:T(8,128)(2,1)S(1)}, bf16[2,512,128]{2,1,0:T(8,128)(2,1)}, u32[]{:S(2)}) copy-start(bf16[2,512,128]{2,1,0:T(8,128)(2,1)} %get-tuple-element.36) | copy-start | bytes 786436
  153.2 95.8 %all-to-all-start.3 = ((bf16[32,2,2,128,128]{4,3,2,1,0:T(8,128)(2,1)}), bf16[32,2,2,128,128]{4,3,2,1,0:T(8,128)(2,1)}, u32[]{:S(2)}, u32[]{:S(2)}) async-start(bf16[32,2,2,128,128]{4,3,2,1,0:T(8,128)(2,1)} %clean.6.refs_13_), calls=%async_computation.3 | async-start | bytes 8388608 | tf_op jit(solution)/shard_map/all_to_all | solution.py:347
  157.2 36.9 %collective-permute-start = (bf16[2,512,128]{2,1,0:T(8,128)(2,1)}, bf16[2,512,128]{2,1,0:T(8,128)(2,1)S(1)}, u32[]{:S(2)}, u32[]{:S(2)}) collective-permute-start(bf16[2,512,128]{2,1,0:T(8,128)(2,1)} %get-tuple-element.30), channel_id=1, source_target_pairs={{0,7},{1,6},{2,5},{3,4},{4,3},{5,2},{6,1},{7,0},{8,15},{9,14},{10,... | collective-permute-start | bytes 786440 | tf_op jit(solution)/shard_map/ppermute | solution.py:353
  159.4 54.6 %collective-permute-start.1 = (bf16[2,512,128]{2,1,0:T(8,128)(2,1)}, bf16[2,512,128]{2,1,0:T(8,128)(2,1)S(1)}, u32[]{:S(2)}, u32[]{:S(2)}) collective-permute-start(bf16[2,512,128]{2,1,0:T(8,128)(2,1)} %get-tuple-element.31), channel_id=1, source_target_pairs={{0,6},{1,7},{2,4},{3,5},{4,2},{5,3},{6,0},{7,1},{8,14},{9,15},{10,... | collective-permute-start | bytes 786440 | tf_op jit(solution)/shard_map/ppermute | solution.py:353
  159.9 54.0 %collective-permute-start.2 = (bf16[2,512,128]{2,1,0:T(8,128)(2,1)S(1)}, bf16[2,512,128]{2,1,0:T(8,128)(2,1)S(1)}, u32[]{:S(2)}, u32[]{:S(2)}) collective-permute-start(bf16[2,512,128]{2,1,0:T(8,128)(2,1)S(1)} %copy-done.17), channel_id=1, source_target_pairs={{0,5},{1,4},{2,7},{3,6},{4,1},{5,0},{6,3},{7,2},{8,13},{9,12},{10,... | collective-permute-start | bytes 786440 | tf_op jit(solution)/shard_map/ppermute | solution.py:353
  161.1 57.0 %collective-permute-start.3 = (bf16[2,512,128]{2,1,0:T(8,128)(2,1)S(1)}, bf16[2,512,128]{2,1,0:T(8,128)(2,1)S(1)}, u32[]{:S(2)}, u32[]{:S(2)}) collective-permute-start(bf16[2,512,128]{2,1,0:T(8,128)(2,1)S(1)} %copy-done.16), channel_id=1, source_target_pairs={{0,4},{1,5},{2,6},{3,7},{4,0},{5,1},{6,2},{7,3},{8,12},{9,13},{10,... | collective-permute-start | bytes 786440 | tf_op jit(solution)/shard_map/ppermute | solution.py:353
  161.6 58.6 %collective-permute-start.4 = (bf16[2,512,128]{2,1,0:T(8,128)(2,1)S(1)}, bf16[2,512,128]{2,1,0:T(8,128)(2,1)S(1)}, u32[]{:S(2)}, u32[]{:S(2)}) collective-permute-start(bf16[2,512,128]{2,1,0:T(8,128)(2,1)S(1)} %copy-done.15), channel_id=1, source_target_pairs={{0,3},{1,2},{2,1},{3,0},{4,7},{5,6},{6,5},{7,4},{8,11},{9,10},{10,... | collective-permute-start | bytes 786440 | tf_op jit(solution)/shard_map/ppermute | solution.py:353
  194.0 32.3 %copy-start.23 = (bf16[2,512,128]{2,1,0:T(8,128)(2,1)}, bf16[2,512,128]{2,1,0:T(8,128)(2,1)S(1)}, u32[]{:S(2)}) copy-start(bf16[2,512,128]{2,1,0:T(8,128)(2,1)S(1)} %collective-permute-done.refs_1_) | copy-start | bytes 786436
  194.0 32.3 %collective-permute-start.5 = (bf16[2,512,128]{2,1,0:T(8,128)(2,1)S(1)}, bf16[2,512,128]{2,1,0:T(8,128)(2,1)S(1)}, u32[]{:S(2)}, u32[]{:S(2)}) collective-permute-start(bf16[2,512,128]{2,1,0:T(8,128)(2,1)S(1)} %copy-done.14), channel_id=1, source_target_pairs={{0,2},{1,3},{2,0},{3,1},{4,6},{5,7},{6,4},{7,5},{8,10},{9,11},{10,... | collective-permute-start | bytes 786440 | tf_op jit(solution)/shard_map/ppermute | solution.py:353
  214.0 12.3 %copy-start.24 = (bf16[2,512,128]{2,1,0:T(8,128)(2,1)}, bf16[2,512,128]{2,1,0:T(8,128)(2,1)S(1)}, u32[]{:S(2)}) copy-start(bf16[2,512,128]{2,1,0:T(8,128)(2,1)S(1)} %collective-permute-done.1.refs_2_) | copy-start | bytes 786436
  214.0 12.3 %collective-permute-start.6 = (bf16[2,512,128]{2,1,0:T(8,128)(2,1)S(1)}, bf16[2,512,128]{2,1,0:T(8,128)(2,1)S(1)}, u32[]{:S(2)}, u32[]{:S(2)}) collective-permute-start(bf16[2,512,128]{2,1,0:T(8,128)(2,1)S(1)} %copy-done.13), channel_id=1, source_target_pairs={{0,1},{1,0},{2,3},{3,2},{4,5},{5,4},{6,7},{7,6},{8,9},{9,8},{10,11... | collective-permute-start | bytes 786440 | tf_op jit(solution)/shard_map/ppermute | solution.py:353
  214.0 12.3 %copy-start.26 = (bf16[2,512,128]{2,1,0:T(8,128)(2,1)}, bf16[2,512,128]{2,1,0:T(8,128)(2,1)S(1)}, u32[]{:S(2)}) copy-start(bf16[2,512,128]{2,1,0:T(8,128)(2,1)S(1)} %collective-permute-done.2.refs_3_) | copy-start | bytes 786436
  218.1 8.2 %copy-start.27 = (bf16[2,512,128]{2,1,0:T(8,128)(2,1)}, bf16[2,512,128]{2,1,0:T(8,128)(2,1)S(1)}, u32[]{:S(2)}) copy-start(bf16[2,512,128]{2,1,0:T(8,128)(2,1)S(1)} %collective-permute-done.3.refs_4_) | copy-start | bytes 786436
  220.2 6.1 %copy-start.28 = (bf16[2,512,128]{2,1,0:T(8,128)(2,1)}, bf16[2,512,128]{2,1,0:T(8,128)(2,1)S(1)}, u32[]{:S(2)}) copy-start(bf16[2,512,128]{2,1,0:T(8,128)(2,1)S(1)} %collective-permute-done.4.refs_5_) | copy-start | bytes 786436
  249.0 53.8 %all-to-all-start.2 = ((bf16[32,1,2,128,128]{4,3,2,1,0:T(8,128)(2,1)}), bf16[32,1,2,128,128]{4,3,2,1,0:T(8,128)(2,1)S(1)}, u32[]{:S(2)}, u32[]{:S(2)}) async-start(bf16[32,1,2,128,128]{4,3,2,1,0:T(8,128)(2,1)} %clean.7), calls=%async_computation.2 | async-start | bytes 4194304 | tf_op jit(solution)/shard_map/all_to_all | solution.py:347
  (10 other events, 10.5 us)

commit v10 on v9

--- a/solution.py
+++ b/solution.py
@@ -377,7 +377,7 @@
             scatter(sends[k * chan_count : (k + 1) * chan_count]) for k in range(count - 1)
         ]
     groups = [[0]] + [g for g in (list(range(1, count - 1)), [count - 1]) if g and count > 1]
-    held, cleaned = [], []
+    held, cleaned = [], cells[1][:1] if count > 1 else []
     for chunks in groups:
         for slot, k in enumerate(chunks):
             cleaned = [

time: 315 us -> 311 us (0.987)
  waiting for transfers between devices: 170 us -> 164 us
    all_to_all x5, waiting for transfers between devices: 64.3 us -> 47.2 us  [exchange(): return lax.all_to_all(x, axes, split_axis=0, concat_axis=0, tiled=True)]
    ppermute x21, waiting for transfers between devices: 105 us -> 117 us  [scatter(): lax.ppermute(pieces[step], 'chan', [(j, int(partner(np.int32(j), step, co...]
where the time goes in v10:
time: 311 us; the launch traced here: 306 us
  waiting for transfers between devices  164 us (53%)
  Pallas kernels  91.3 us (29%)
  starting transfers between devices  42 us (14%)
  local copies, waits for them, and re-layouts  7.95 us (3%)
    ppermute x21, waiting for transfers between devices, scatter(): lax.ppermute(pieces[step], 'chan', [(j, int(partner(np.int32(j), step, co...  117 us
    all_to_all x5, waiting for transfers between devices, exchange(): return lax.all_to_all(x, axes, split_axis=0, concat_axis=0, tiled=True)  47.2 us
    pallas_call x4, Pallas kernels, clean(): pl.pallas_call(functools.partial(clean_kernel, split, len(before)), grid_...  34 us
    pallas_call x2, Pallas kernels, column_transform(): pl.pallas_call(functools.partial(column_kernel, chunks, pieces // RADIX,...  29.4 us
    pallas_call x4, Pallas kernels, image(): pl.pallas_call(functools.partial(image_kernel, scale), grid=(chans // gro...  25.9 us
    all_to_all x5, starting transfers between devices, exchange(): return lax.all_to_all(x, axes, split_axis=0, concat_axis=0, tiled=True)  25 us
    ppermute x21, starting transfers between devices, scatter(): lax.ppermute(pieces[step], 'chan', [(j, int(partner(np.int32(j), step, co...  17 us
    unnamed x74, local copies, waits for them, and re-layouts  6.26 us
  transfers between devices with their start and end apart: 26, of which 16 were waited for; matrix products, arithmetic and copies ran while one was open for 0% of the time, Pallas kernels for 25%

profile of v10, /device:TPU:8, one launch (start us, length us, event | category | flops | bytes accessed | tf_op | source)
XLA Modules:
  0.0 306.1 jit_solution(9431403529195442968)
XLA Ops:
  0.0 1.7 broadcast_in_dim.2
  1.7 3.7 %all-to-all-start = ((bf16[8,64,512]{2,1,0:T(8,128)(2,1)}), bf16[8,64,512]{2,1,0:T(8,128)(2,1)S(1)}, u32[]{:S(2)}, u32[]{:S(2)}) async-start(bf16[8,64,512]{2,1,0:T(8,128)(2,1)} %broadcast_in_dim.2), calls=%async_computation | async-start | bytes 1048576 | tf_op jit(solution)/shard_map/all_to_all | solution.py:347
  5.4 11.9 %column_transform.3 = bf16[8,2,512,128]{3,2,1,0:T(8,128)(2,1)} custom-call(s32[1]{0:T(128)} %bitcast.at_ref, bf16[2,512,4096]{2,1,0:T(8,128)(2,1)} %bitcast.13, f32[8,2,512]{2,1,0:T(2,128)} %constant.16.clone.twiddle_ref, bf16[1024,1024]{1,0:T(8,128)(2,1)} %constant.17.clone.table_ref), custom_call_target="tpu_custom_call" | custom-call | flops 8589934592 | bytes 16777216 | tf_op jit(solution)/shard_map/column_transform/pallas_call | solution.py:157
  17.3 0.8 add_divide_fusion.refs_3_.refs_10_
  18.2 4.2 %all-to-all-start.1 = ((bf16[8,2,512,128]{3,2,1,0:T(8,128)(2,1)}), bf16[8,2,512,128]{3,2,1,0:T(8,128)(2,1)S(1)}, u32[]{:S(2)}, u32[]{:S(2)}) async-start(bf16[8,2,512,128]{3,2,1,0:T(8,128)(2,1)} %column_transform.3), calls=%async_computation.1 | async-start | bytes 4194304 | tf_op jit(solution)/shard_map/all_to_all | solution.py:347
  22.4 17.6 %column_transform.2 = (bf16[2,512,128]{2,1,0:T(8,128)(2,1)}, bf16[2,512,128]{2,1,0:T(8,128)(2,1)}, bf16[2,512,128]{2,1,0:T(8,128)(2,1)}, bf16[2,512,128]{2,1,0:T...) custom-call(s32[1]{0:T(128)} %bitcast.at_ref, ...), custom_call_target="tpu_custom_call" | custom-call | flops 25769803776 | bytes 16777216 | tf_op jit(solution)/shard_map/column_transform/pallas_call | solution.py:157
  39.9 2.0 turn.1.refs_2_.refs_9_
  41.9 7.1 %all-to-all-done.1.refs_0_ = bf16[8,2,512,128]{3,2,1,0:T(8,128)(2,1)S(1)} async-done(((bf16[8,2,512,128]{3,2,1,0:T(8,128)(2,1)}), bf16[8,2,512,128]{3,2,1,0:T(8,128)(2,1)S(1)}, u32[]{:S(2)}, u32[]{:S(2)}) %all-to-all-start.1) | async-done | bytes 2097184 | tf_op jit(solution)/shard_map/all_to_all | solution.py:347
  49.0 1.3 copy-done.3
  50.3 8.1 %clean.4.refs_13_ = bf16[32,1,2,128,128]{4,3,2,1,0:T(8,128)(2,1)} custom-call(s32[1]{0:T(128)} %bitcast.at_ref, bf16[8,2,512,128]{3,2,1,0:T(8,128)(2,1)} %copy-done.3, bf16[512,512]{1,0:T(8,128)(2,1)} %bitcast.9, bf16[512,512]{1,0:T(8,128)(2,1)} %turn.1.refs_2_.refs_9_, f32[512,8]{1,0:T(8,128)} %add_divide_fusion.refs_3_.refs_10_, ...), custom_call_target="tpu_custom_call" | custom-call | flops 3221225472 | bytes 4194304 | tf_op jit(solution)/shard_map/clean/pallas_call | solution.py:247
  58.4 4.2 %all-to-all-start.4 = ((bf16[32,1,2,128,128]{4,3,2,1,0:T(8,128)(2,1)}), bf16[32,1,2,128,128]{4,3,2,1,0:T(8,128)(2,1)S(1)}, u32[]{:S(2)}, u32[]{:S(2)}) async-start(bf16[32,1,2,128,128]{4,3,2,1,0:T(8,128)(2,1)} %clean.4.refs_13_), calls=%async_computation.4 | async-start | bytes 4194304 | tf_op jit(solution)/shard_map/all_to_all | solution.py:347
  62.7 2.2 collective-permute-start.7
  65.4 2.0 collective-permute-start.14
  68.0 1.2 collective-permute-start.16
  69.2 18.2 %collective-permute-done.7.refs_1_ = bf16[2,512,128]{2,1,0:T(8,128)(2,1)S(1)} collective-permute-done((bf16[2,512,128]{2,1,0:T(8,128)(2,1)}, bf16[2,512,128]{2,1,0:T(8,128)(2,1)S(1)}, u32[]{:S(2)}, u32[]{:S(2)}) %collective-permute-start.7) | collective-permute-done | bytes 262176 | tf_op jit(solution)/shard_map/ppermute | solution.py:353
  87.4 1.7 collective-permute-start.17
  89.1 11.5 %collective-permute-done.8.refs_2_ = bf16[2,512,128]{2,1,0:T(8,128)(2,1)S(1)} collective-permute-done((bf16[2,512,128]{2,1,0:T(8,128)(2,1)}, bf16[2,512,128]{2,1,0:T(8,128)(2,1)S(1)}, u32[]{:S(2)}, u32[]{:S(2)}) %collective-permute-start.8) | collective-permute-done | bytes 262176 | tf_op jit(solution)/shard_map/ppermute | solution.py:353
  100.7 4.9 %collective-permute-done.14.refs_1_ = bf16[2,512,128]{2,1,0:T(8,128)(2,1)S(1)} collective-permute-done((bf16[2,512,128]{2,1,0:T(8,128)(2,1)}, bf16[2,512,128]{2,1,0:T(8,128)(2,1)S(1)}, u32[]{:S(2)}, u32[]{:S(2)}) %collective-permute-start.14) | collective-permute-done | bytes 262176 | tf_op jit(solution)/shard_map/ppermute | solution.py:353
  105.6 1.7 collective-permute-start.19
  107.3 7.6 %collective-permute-done.15.refs_2_ = bf16[2,512,128]{2,1,0:T(8,128)(2,1)S(1)} collective-permute-done((bf16[2,512,128]{2,1,0:T(8,128)(2,1)}, bf16[2,512,128]{2,1,0:T(8,128)(2,1)S(1)}, u32[]{:S(2)}, u32[]{:S(2)}) %collective-permute-start.15) | collective-permute-done | bytes 262176 | tf_op jit(solution)/shard_map/ppermute | solution.py:353
  114.9 1.4 collective-permute-done.16.refs_3_
  116.4 5.7 %collective-permute-done.17.refs_4_ = bf16[2,512,128]{2,1,0:T(8,128)(2,1)S(1)} collective-permute-done((bf16[2,512,128]{2,1,0:T(8,128)(2,1)}, bf16[2,512,128]{2,1,0:T(8,128)(2,1)S(1)}, u32[]{:S(2)}, u32[]{:S(2)}) %collective-permute-start.17) | collective-permute-done | bytes 262176 | tf_op jit(solution)/shard_map/ppermute | solution.py:353
  122.1 0.8 collective-permute-start.11
  122.9 2.7 collective-permute-done.19.refs_6_
  126.8 8.6 %clean.5.refs_13_ = bf16[32,2,2,128,128]{4,3,2,1,0:T(8,128)(2,1)} custom-call(s32[1]{0:T(128)} %bitcast.at_ref, bf16[2,512,128]{2,1,0:T(8,128)(2,1)} %get-tuple-element.45.refs_6_.refs_0_, bf16[2,512,128]{2,1,0:T(8,128)(2,1)} %copy-done.23, bf16[2,512,128]{2,1,0:T(8,128)(2,1)} %copy-done.24, bf16[2,512,128]{2,1,0:T(8,128)(2,1)} %copy-done.25, ...), custom_call_target="tpu_custom_call" | custom-call | flops 3221225472 | bytes 4194304 | tf_op jit(solution)/shard_map/clean/pallas_call | solution.py:247
  135.5 1.2 collective-permute-done.12.refs_6_
  136.7 0.7 copy-done.9
  137.4 8.6 %clean.6.refs_13_ = bf16[32,2,2,128,128]{4,3,2,1,0:T(8,128)(2,1)} custom-call(s32[1]{0:T(128)} %bitcast.at_ref, bf16[2,512,128]{2,1,0:T(8,128)(2,1)} %get-tuple-element.37.refs_0_, bf16[2,512,128]{2,1,0:T(8,128)(2,1)} %copy-done.4, bf16[2,512,128]{2,1,0:T(8,128)(2,1)} %copy-done.5, bf16[2,512,128]{2,1,0:T(8,128)(2,1)} %copy-done.6, ...), custom_call_target="tpu_custom_call", output_to_operand_aliasing={{}: (14, {})} | custom-call | flops 3221225472 | bytes 4194304 | tf_op jit(solution)/shard_map/clean/pallas_call | solution.py:247
  146.1 1.4 copy-done
  147.5 5.3 %all-to-all-start.3 = ((bf16[32,2,2,128,128]{4,3,2,1,0:T(8,128)(2,1)}), bf16[32,2,2,128,128]{4,3,2,1,0:T(8,128)(2,1)}, u32[]{:S(2)}, u32[]{:S(2)}) async-start(bf16[32,2,2,128,128]{4,3,2,1,0:T(8,128)(2,1)} %clean.6.refs_13_), calls=%async_computation.3 | async-start | bytes 8388608 | tf_op jit(solution)/shard_map/all_to_all | solution.py:347
  152.8 2.2 collective-permute-start
  155.5 1.1 collective-permute-start.2
  157.2 1.2 collective-permute-start.4
  158.5 31.2 %collective-permute-done.refs_1_ = bf16[2,512,128]{2,1,0:T(8,128)(2,1)S(1)} collective-permute-done((bf16[2,512,128]{2,1,0:T(8,128)(2,1)}, bf16[2,512,128]{2,1,0:T(8,128)(2,1)S(1)}, u32[]{:S(2)}, u32[]{:S(2)}) %collective-permute-start) | collective-permute-done | bytes 262176 | tf_op jit(solution)/shard_map/ppermute | solution.py:353
  189.7 20.0 %collective-permute-done.1.refs_2_ = bf16[2,512,128]{2,1,0:T(8,128)(2,1)S(1)} collective-permute-done((bf16[2,512,128]{2,1,0:T(8,128)(2,1)}, bf16[2,512,128]{2,1,0:T(8,128)(2,1)S(1)}, u32[]{:S(2)}, u32[]{:S(2)}) %collective-permute-start.1) | collective-permute-done | bytes 262176 | tf_op jit(solution)/shard_map/ppermute | solution.py:353
  209.8 4.0 %collective-permute-done.3.refs_4_ = bf16[2,512,128]{2,1,0:T(8,128)(2,1)S(1)} collective-permute-done((bf16[2,512,128]{2,1,0:T(8,128)(2,1)S(1)}, bf16[2,512,128]{2,1,0:T(8,128)(2,1)S(1)}, u32[]{:S(2)}, u32[]{:S(2)}) %collective-permute-start.3) | collective-permute-done | bytes 262176 | tf_op jit(solution)/shard_map/ppermute | solution.py:353
  213.8 1.9 collective-permute-done.4.refs_5_
  215.6 6.1 %collective-permute-done.5.refs_6_ = bf16[2,512,128]{2,1,0:T(8,128)(2,1)S(1)} collective-permute-done((bf16[2,512,128]{2,1,0:T(8,128)(2,1)S(1)}, bf16[2,512,128]{2,1,0:T(8,128)(2,1)S(1)}, u32[]{:S(2)}, u32[]{:S(2)}) %collective-permute-start.5) | collective-permute-done | bytes 262176 | tf_op jit(solution)/shard_map/ppermute | solution.py:353
  221.8 0.6 copy-done.35
  222.6 8.7 %clean.7 = bf16[32,1,2,128,128]{4,3,2,1,0:T(8,128)(2,1)} custom-call(s32[1]{0:T(128)} %bitcast.at_ref, bf16[2,512,128]{2,1,0:T(8,128)(2,1)} %get-tuple-element.29.refs_0_, bf16[2,512,128]{2,1,0:T(8,128)(2,1)} %copy-done.28, bf16[2,512,128]{2,1,0:T(8,128)(2,1)} %copy-done.29, bf16[2,512,128]{2,1,0:T(8,128)(2,1)} %copy-done.31, ...), custom_call_target="tpu_custom_call" | custom-call | flops 3221225472 | bytes 4194304 | tf_op jit(solution)/shard_map/clean/pallas_call | solution.py:247
  231.3 12.9 %all-to-all-done.3 = bf16[32,2,2,128,128]{4,3,2,1,0:T(8,128)(2,1)} async-done(((bf16[32,2,2,128,128]{4,3,2,1,0:T(8,128)(2,1)}), bf16[32,2,2,128,128]{4,3,2,1,0:T(8,128)(2,1)}, u32[]{:S(2)}, u32[]{:S(2)}) %all-to-all-start.3) | async-done | bytes 4194336 | tf_op jit(solution)/shard_map/all_to_all | solution.py:347
  244.2 7.6 %all-to-all-start.2 = ((bf16[32,1,2,128,128]{4,3,2,1,0:T(8,128)(2,1)}), bf16[32,1,2,128,128]{4,3,2,1,0:T(8,128)(2,1)S(1)}, u32[]{:S(2)}, u32[]{:S(2)}) async-start(bf16[32,1,2,128,128]{4,3,2,1,0:T(8,128)(2,1)} %clean.7), calls=%async_computation.2 | async-start | bytes 4194304 | tf_op jit(solution)/shard_map/all_to_all | solution.py:347
  251.7 6.5 %image.4.refs_0_ = bf16[2,16,32,4096]{3,2,1,0:T(8,128)(2,1)} custom-call(bf16[4,8,1,2,128,128]{5,4,3,2,1,0:T(8,128)(2,1)} %bitcast.6, bf16[256,256]{1,0:T(8,128)(2,1)} %constant.20.clone.table_ref, bf16[1024,1024]{1,0:T(8,128)(2,1)} %constant.21.clone.order_ref), custom_call_target="tpu_custom_call" | custom-call | flops 2147483648 | bytes 4194304 | tf_op jit(solution)/shard_map/image/pallas_call | solution.py:304
  258.2 6.5 %image.5.refs_0_ = bf16[2,16,32,4096]{3,2,1,0:T(8,128)(2,1)} custom-call(bf16[4,8,2,2,128,128]{5,4,3,2,1,0:T(8,128)(2,1)} %bitcast.4.x_ref, bf16[256,256]{1,0:T(8,128)(2,1)} %constant.20.clone.table_ref, bf16[1024,1024]{1,0:T(8,128)(2,1)} %constant.21.clone.order_ref, bf16[2,16,32,4096]{3,2,1,0:T(8,128)(2,1)} %image.4.refs_0_), custom_call_target="tpu_custom_call", output_to_operand_aliasing={{}: (3, {})} | custom-call | flops 2147483648 | bytes 4194304 | tf_op jit(solution)/shard_map/image/pallas_call | solution.py:304
  264.7 6.5 %image.6.refs_0_ = bf16[2,16,32,4096]{3,2,1,0:T(8,128)(2,1)} custom-call(bf16[4,8,2,2,128,128]{5,4,3,2,1,0:T(8,128)(2,1)} %bitcast.4.x_ref, bf16[256,256]{1,0:T(8,128)(2,1)} %constant.20.clone.table_ref, bf16[1024,1024]{1,0:T(8,128)(2,1)} %constant.21.clone.order_ref, bf16[2,16,32,4096]{3,2,1,0:T(8,128)(2,1)} %image.5.refs_0_), custom_call_target="tpu_custom_call", output_to_operand_aliasing={{}: (3, {})} | custom-call | flops 2147483648 | bytes 4194304 | tf_op jit(solution)/shard_map/image/pallas_call | solution.py:304
  271.1 27.2 %all-to-all-done.2 = bf16[32,1,2,128,128]{4,3,2,1,0:T(8,128)(2,1)S(1)} async-done(((bf16[32,1,2,128,128]{4,3,2,1,0:T(8,128)(2,1)}), bf16[32,1,2,128,128]{4,3,2,1,0:T(8,128)(2,1)S(1)}, u32[]{:S(2)}, u32[]{:S(2)}) %all-to-all-start.2) | async-done | bytes 2097184 | tf_op jit(solution)/shard_map/all_to_all | solution.py:347
  298.4 1.3 copy-done.1
  299.7 6.4 %image.7 = bf16[2,16,32,4096]{3,2,1,0:T(8,128)(2,1)} custom-call(bf16[4,8,1,2,128,128]{5,4,3,2,1,0:T(8,128)(2,1)} %bitcast.7, bf16[256,256]{1,0:T(8,128)(2,1)} %constant.20.clone.table_ref, bf16[1024,1024]{1,0:T(8,128)(2,1)} %constant.21.clone.order_ref, bf16[2,16,32,4096]{3,2,1,0:T(8,128)(2,1)} %image.6.refs_0_), custom_call_target="tpu_custom_call", output_to_operand_aliasing={{}: (3, {})} | custom-call | flops 2147483648 | bytes 4194304 | tf_op jit(solution)/shard_map/image/pallas_call | solution.py:304
  (91 shorter events, 3.8 us)
Async XLA Ops:
  1.7 16.5 %all-to-all-start = ((bf16[8,64,512]{2,1,0:T(8,128)(2,1)}), bf16[8,64,512]{2,1,0:T(8,128)(2,1)S(1)}, u32[]{:S(2)}, u32[]{:S(2)}) async-start(bf16[8,64,512]{2,1,0:T(8,128)(2,1)} %broadcast_in_dim.2), calls=%async_computation | async-start | bytes 1048576 | tf_op jit(solution)/shard_map/all_to_all | solution.py:347
  5.4 11.9 %copy-start.11 = (f32[512]{0:T(512)S(1)}, f32[512]{0:T(512)}, u32[]{:S(2)}) copy-start(f32[512]{0:T(512)} %param.26) | copy-start | bytes 6148
  5.4 11.9 %copy-start.12 = (f32[8]{0:T(128)S(1)}, f32[8]{0:T(128)}, u32[]{:S(2)}) copy-start(f32[8]{0:T(128)} %param.27) | copy-start | bytes 100
  18.2 21.8 %copy-start.2 = (bf16[8,64,512]{2,1,0:T(8,128)(2,1)}, bf16[8,64,512]{2,1,0:T(8,128)(2,1)S(1)}, u32[]{:S(2)}) copy-start(bf16[8,64,512]{2,1,0:T(8,128)(2,1)S(1)} %all-to-all-done) | copy-start | bytes 1572868
  18.2 30.8 %all-to-all-start.1 = ((bf16[8,2,512,128]{3,2,1,0:T(8,128)(2,1)}), bf16[8,2,512,128]{3,2,1,0:T(8,128)(2,1)S(1)}, u32[]{:S(2)}, u32[]{:S(2)}) async-start(bf16[8,2,512,128]{3,2,1,0:T(8,128)(2,1)} %column_transform.3), calls=%async_computation.1 | async-start | bytes 4194304 | tf_op jit(solution)/shard_map/all_to_all | solution.py:347
  58.4 58.0 %copy-start.22 = (bf16[2,512,128]{2,1,0:T(8,128)(2,1)S(1)}, bf16[2,512,128]{2,1,0:T(8,128)(2,1)}, u32[]{:S(2)}) copy-start(bf16[2,512,128]{2,1,0:T(8,128)(2,1)} %get-tuple-element.40) | copy-start | bytes 786436
  58.4 63.7 %copy-start.21 = (bf16[2,512,128]{2,1,0:T(8,128)(2,1)S(1)}, bf16[2,512,128]{2,1,0:T(8,128)(2,1)}, u32[]{:S(2)}) copy-start(bf16[2,512,128]{2,1,0:T(8,128)(2,1)} %get-tuple-element.41) | copy-start | bytes 786436
  58.4 63.7 %copy-start.20 = (bf16[2,512,128]{2,1,0:T(8,128)(2,1)S(1)}, bf16[2,512,128]{2,1,0:T(8,128)(2,1)}, u32[]{:S(2)}) copy-start(bf16[2,512,128]{2,1,0:T(8,128)(2,1)} %get-tuple-element.42) | copy-start | bytes 786436
  58.4 67.2 %copy-start.19 = (bf16[2,512,128]{2,1,0:T(8,128)(2,1)S(1)}, bf16[2,512,128]{2,1,0:T(8,128)(2,1)}, u32[]{:S(2)}) copy-start(bf16[2,512,128]{2,1,0:T(8,128)(2,1)} %get-tuple-element.43) | copy-start | bytes 786436
  58.4 67.6 %copy-start.18 = (bf16[2,512,128]{2,1,0:T(8,128)(2,1)S(1)}, bf16[2,512,128]{2,1,0:T(8,128)(2,1)}, u32[]{:S(2)}) copy-start(bf16[2,512,128]{2,1,0:T(8,128)(2,1)} %get-tuple-element.44) | copy-start | bytes 786436
  58.4 87.7 %all-to-all-start.4 = ((bf16[32,1,2,128,128]{4,3,2,1,0:T(8,128)(2,1)}), bf16[32,1,2,128,128]{4,3,2,1,0:T(8,128)(2,1)S(1)}, u32[]{:S(2)}, u32[]{:S(2)}) async-start(bf16[32,1,2,128,128]{4,3,2,1,0:T(8,128)(2,1)} %clean.4.refs_13_), calls=%async_computation.4 | async-start | bytes 4194304 | tf_op jit(solution)/shard_map/all_to_all | solution.py:347
  62.7 24.8 %collective-permute-start.7 = (bf16[2,512,128]{2,1,0:T(8,128)(2,1)}, bf16[2,512,128]{2,1,0:T(8,128)(2,1)S(1)}, u32[]{:S(2)}, u32[]{:S(2)}) collective-permute-start(bf16[2,512,128]{2,1,0:T(8,128)(2,1)} %get-tuple-element.38), channel_id=1, source_target_pairs={{0,7},{1,6},{2,5},{3,4},{4,3},{5,2},{6,1},{7,0},{8,15},{9,14},{10,... | collective-permute-start | bytes 786440 | tf_op jit(solution)/shard_map/ppermute | solution.py:353
  64.8 35.8 %collective-permute-start.8 = (bf16[2,512,128]{2,1,0:T(8,128)(2,1)}, bf16[2,512,128]{2,1,0:T(8,128)(2,1)S(1)}, u32[]{:S(2)}, u32[]{:S(2)}) collective-permute-start(bf16[2,512,128]{2,1,0:T(8,128)(2,1)} %get-tuple-element.39), channel_id=1, source_target_pairs={{0,6},{1,7},{2,4},{3,5},{4,2},{5,3},{6,0},{7,1},{8,14},{9,15},{10,... | collective-permute-start | bytes 786440 | tf_op jit(solution)/shard_map/ppermute | solution.py:353
  65.4 40.2 %collective-permute-start.14 = (bf16[2,512,128]{2,1,0:T(8,128)(2,1)}, bf16[2,512,128]{2,1,0:T(8,128)(2,1)S(1)}, u32[]{:S(2)}, u32[]{:S(2)}) collective-permute-start(bf16[2,512,128]{2,1,0:T(8,128)(2,1)} %get-tuple-element.46), channel_id=1, source_target_pairs={{0,7},{1,6},{2,5},{3,4},{4,3},{5,2},{6,1},{7,0},{8,15},{9,14},{10,... | collective-permute-start | bytes 786440 | tf_op jit(solution)/shard_map/ppermute | solution.py:353
  67.5 47.5 %collective-permute-start.15 = (bf16[2,512,128]{2,1,0:T(8,128)(2,1)}, bf16[2,512,128]{2,1,0:T(8,128)(2,1)S(1)}, u32[]{:S(2)}, u32[]{:S(2)}) collective-permute-start(bf16[2,512,128]{2,1,0:T(8,128)(2,1)} %get-tuple-element.47), channel_id=1, source_target_pairs={{0,6},{1,7},{2,4},{3,5},{4,2},{5,3},{6,0},{7,1},{8,14},{9,15},{10,... | collective-permute-start | bytes 786440 | tf_op jit(solution)/shard_map/ppermute | solution.py:353
  68.0 48.3 %collective-permute-start.16 = (bf16[2,512,128]{2,1,0:T(8,128)(2,1)}, bf16[2,512,128]{2,1,0:T(8,128)(2,1)S(1)}, u32[]{:S(2)}, u32[]{:S(2)}) collective-permute-start(bf16[2,512,128]{2,1,0:T(8,128)(2,1)} %get-tuple-element.48), channel_id=1, source_target_pairs={{0,5},{1,4},{2,7},{3,6},{4,1},{5,0},{6,3},{7,2},{8,13},{9,12},{10,... | collective-permute-start | bytes 786440 | tf_op jit(solution)/shard_map/ppermute | solution.py:353
  87.4 48.0 %copy-start.4 = (bf16[2,512,128]{2,1,0:T(8,128)(2,1)}, bf16[2,512,128]{2,1,0:T(8,128)(2,1)S(1)}, u32[]{:S(2)}) copy-start(bf16[2,512,128]{2,1,0:T(8,128)(2,1)S(1)} %collective-permute-done.7.refs_1_) | copy-start | bytes 786436
  87.4 34.6 %collective-permute-start.17 = (bf16[2,512,128]{2,1,0:T(8,128)(2,1)}, bf16[2,512,128]{2,1,0:T(8,128)(2,1)S(1)}, u32[]{:S(2)}, u32[]{:S(2)}) collective-permute-start(bf16[2,512,128]{2,1,0:T(8,128)(2,1)} %get-tuple-element.49), channel_id=1, source_target_pairs={{0,4},{1,5},{2,6},{3,7},{4,0},{5,1},{6,2},{7,3},{8,12},{9,13},{10,... | collective-permute-start | bytes 786440 | tf_op jit(solution)/shard_map/ppermute | solution.py:353
  100.7 34.8 %copy-start.5 = (bf16[2,512,128]{2,1,0:T(8,128)(2,1)}, bf16[2,512,128]{2,1,0:T(8,128)(2,1)S(1)}, u32[]{:S(2)}) copy-start(bf16[2,512,128]{2,1,0:T(8,128)(2,1)S(1)} %collective-permute-done.8.refs_2_) | copy-start | bytes 786436
  100.7 21.4 %collective-permute-start.18 = (bf16[2,512,128]{2,1,0:T(8,128)(2,1)}, bf16[2,512,128]{2,1,0:T(8,128)(2,1)S(1)}, u32[]{:S(2)}, u32[]{:S(2)}) collective-permute-start(bf16[2,512,128]{2,1,0:T(8,128)(2,1)} %get-tuple-element.50), channel_id=1, source_target_pairs={{0,3},{1,2},{2,1},{3,0},{4,7},{5,6},{6,5},{7,4},{8,11},{9,10},{10,... | collective-permute-start | bytes 786440 | tf_op jit(solution)/shard_map/ppermute | solution.py:353
  105.6 20.5 %copy-start.23 = (bf16[2,512,128]{2,1,0:T(8,128)(2,1)}, bf16[2,512,128]{2,1,0:T(8,128)(2,1)S(1)}, u32[]{:S(2)}) copy-start(bf16[2,512,128]{2,1,0:T(8,128)(2,1)S(1)} %collective-permute-done.14.refs_1_) | copy-start | bytes 786436
  105.6 20.0 %collective-permute-start.19 = (bf16[2,512,128]{2,1,0:T(8,128)(2,1)}, bf16[2,512,128]{2,1,0:T(8,128)(2,1)S(1)}, u32[]{:S(2)}, u32[]{:S(2)}) collective-permute-start(bf16[2,512,128]{2,1,0:T(8,128)(2,1)} %get-tuple-element.51), channel_id=1, source_target_pairs={{0,2},{1,3},{2,0},{3,1},{4,6},{5,7},{6,4},{7,5},{8,10},{9,11},{10,... | collective-permute-start | bytes 786440 | tf_op jit(solution)/shard_map/ppermute | solution.py:353
  114.9 11.2 %copy-start.24 = (bf16[2,512,128]{2,1,0:T(8,128)(2,1)}, bf16[2,512,128]{2,1,0:T(8,128)(2,1)S(1)}, u32[]{:S(2)}) copy-start(bf16[2,512,128]{2,1,0:T(8,128)(2,1)S(1)} %collective-permute-done.15.refs_2_) | copy-start | bytes 786436
  114.9 11.1 %collective-permute-start.20 = (bf16[2,512,128]{2,1,0:T(8,128)(2,1)}, bf16[2,512,128]{2,1,0:T(8,128)(2,1)S(1)}, u32[]{:S(2)}, u32[]{:S(2)}) collective-permute-start(bf16[2,512,128]{2,1,0:T(8,128)(2,1)} %get-tuple-element.52), channel_id=1, source_target_pairs={{0,1},{1,0},{2,3},{3,2},{4,5},{5,4},{6,7},{7,6},{8,9},{9,8},{10,11... | collective-permute-start | bytes 786440 | tf_op jit(solution)/shard_map/ppermute | solution.py:353
  116.4 9.8 %copy-start.25 = (bf16[2,512,128]{2,1,0:T(8,128)(2,1)}, bf16[2,512,128]{2,1,0:T(8,128)(2,1)S(1)}, u32[]{:S(2)}) copy-start(bf16[2,512,128]{2,1,0:T(8,128)(2,1)S(1)} %collective-permute-done.16.refs_3_) | copy-start | bytes 786436
  116.4 19.1 %collective-permute-start.9 = (bf16[2,512,128]{2,1,0:T(8,128)(2,1)S(1)}, bf16[2,512,128]{2,1,0:T(8,128)(2,1)S(1)}, u32[]{:S(2)}, u32[]{:S(2)}) collective-permute-start(bf16[2,512,128]{2,1,0:T(8,128)(2,1)S(1)} %copy-done.22), channel_id=1, source_target_pairs={{0,5},{1,4},{2,7},{3,6},{4,1},{5,0},{6,3},{7,2},{8,13},{9,12},{10,... | collective-permute-start | bytes 786440 | tf_op jit(solution)/shard_map/ppermute | solution.py:353
  122.1 13.4 %collective-permute-start.10 = (bf16[2,512,128]{2,1,0:T(8,128)(2,1)S(1)}, bf16[2,512,128]{2,1,0:T(8,128)(2,1)S(1)}, u32[]{:S(2)}, u32[]{:S(2)}) collective-permute-start(bf16[2,512,128]{2,1,0:T(8,128)(2,1)S(1)} %copy-done.21), channel_id=1, source_target_pairs={{0,4},{1,5},{2,6},{3,7},{4,0},{5,1},{6,2},{7,3},{8,12},{9,13},{10,... | collective-permute-start | bytes 786440 | tf_op jit(solution)/shard_map/ppermute | solution.py:353
  122.1 13.4 %collective-permute-start.11 = (bf16[2,512,128]{2,1,0:T(8,128)(2,1)S(1)}, bf16[2,512,128]{2,1,0:T(8,128)(2,1)S(1)}, u32[]{:S(2)}, u32[]{:S(2)}) collective-permute-start(bf16[2,512,128]{2,1,0:T(8,128)(2,1)S(1)} %copy-done.20), channel_id=1, source_target_pairs={{0,3},{1,2},{2,1},{3,0},{4,7},{5,6},{6,5},{7,4},{8,11},{9,10},{10,... | collective-permute-start | bytes 786440 | tf_op jit(solution)/shard_map/ppermute | solution.py:353
  125.6 11.0 %collective-permute-start.12 = (bf16[2,512,128]{2,1,0:T(8,128)(2,1)S(1)}, bf16[2,512,128]{2,1,0:T(8,128)(2,1)S(1)}, u32[]{:S(2)}, u32[]{:S(2)}) collective-permute-start(bf16[2,512,128]{2,1,0:T(8,128)(2,1)S(1)} %copy-done.19), channel_id=1, source_target_pairs={{0,2},{1,3},{2,0},{3,1},{4,6},{5,7},{6,4},{7,5},{8,10},{9,11},{10,... | collective-permute-start | bytes 786440 | tf_op jit(solution)/shard_map/ppermute | solution.py:353
  126.1 10.6 %collective-permute-start.13 = (bf16[2,512,128]{2,1,0:T(8,128)(2,1)S(1)}, bf16[2,512,128]{2,1,0:T(8,128)(2,1)S(1)}, u32[]{:S(2)}, u32[]{:S(2)}) collective-permute-start(bf16[2,512,128]{2,1,0:T(8,128)(2,1)S(1)} %copy-done.18), channel_id=1, source_target_pairs={{0,1},{1,0},{2,3},{3,2},{4,5},{5,4},{6,7},{7,6},{8,9},{9,8},{10,11... | collective-permute-start | bytes 786440 | tf_op jit(solution)/shard_map/ppermute | solution.py:353
  146.0 9.5 %copy-start.17 = (bf16[2,512,128]{2,1,0:T(8,128)(2,1)S(1)}, bf16[2,512,128]{2,1,0:T(8,128)(2,1)}, u32[]{:S(2)}) copy-start(bf16[2,512,128]{2,1,0:T(8,128)(2,1)} %get-tuple-element.32) | copy-start | bytes 786436
  146.1 10.6 %copy-start.16 = (bf16[2,512,128]{2,1,0:T(8,128)(2,1)S(1)}, bf16[2,512,128]{2,1,0:T(8,128)(2,1)}, u32[]{:S(2)}) copy-start(bf16[2,512,128]{2,1,0:T(8,128)(2,1)} %get-tuple-element.33) | copy-start | bytes 786436
  146.1 11.2 %copy-start.15 = (bf16[2,512,128]{2,1,0:T(8,128)(2,1)S(1)}, bf16[2,512,128]{2,1,0:T(8,128)(2,1)}, u32[]{:S(2)}) copy-start(bf16[2,512,128]{2,1,0:T(8,128)(2,1)} %get-tuple-element.34) | copy-start | bytes 786436
  146.1 43.6 %copy-start.14 = (bf16[2,512,128]{2,1,0:T(8,128)(2,1)S(1)}, bf16[2,512,128]{2,1,0:T(8,128)(2,1)}, u32[]{:S(2)}) copy-start(bf16[2,512,128]{2,1,0:T(8,128)(2,1)} %get-tuple-element.35) | copy-start | bytes 786436
  146.1 63.6 %copy-start.13 = (bf16[2,512,128]{2,1,0:T(8,128)(2,1)S(1)}, bf16[2,512,128]{2,1,0:T(8,128)(2,1)}, u32[]{:S(2)}) copy-start(bf16[2,512,128]{2,1,0:T(8,128)(2,1)} %get-tuple-element.36) | copy-start | bytes 786436
  147.5 96.7 %all-to-all-start.3 = ((bf16[32,2,2,128,128]{4,3,2,1,0:T(8,128)(2,1)}), bf16[32,2,2,128,128]{4,3,2,1,0:T(8,128)(2,1)}, u32[]{:S(2)}, u32[]{:S(2)}) async-start(bf16[32,2,2,128,128]{4,3,2,1,0:T(8,128)(2,1)} %clean.6.refs_13_), calls=%async_computation.3 | async-start | bytes 8388608 | tf_op jit(solution)/shard_map/all_to_all | solution.py:347
  152.8 36.9 %collective-permute-start = (bf16[2,512,128]{2,1,0:T(8,128)(2,1)}, bf16[2,512,128]{2,1,0:T(8,128)(2,1)S(1)}, u32[]{:S(2)}, u32[]{:S(2)}) collective-permute-start(bf16[2,512,128]{2,1,0:T(8,128)(2,1)} %get-tuple-element.30), channel_id=1, source_target_pairs={{0,7},{1,6},{2,5},{3,4},{4,3},{5,2},{6,1},{7,0},{8,15},{9,14},{10,... | collective-permute-start | bytes 786440 | tf_op jit(solution)/shard_map/ppermute | solution.py:353
  155.0 54.8 %collective-permute-start.1 = (bf16[2,512,128]{2,1,0:T(8,128)(2,1)}, bf16[2,512,128]{2,1,0:T(8,128)(2,1)S(1)}, u32[]{:S(2)}, u32[]{:S(2)}) collective-permute-start(bf16[2,512,128]{2,1,0:T(8,128)(2,1)} %get-tuple-element.31), channel_id=1, source_target_pairs={{0,6},{1,7},{2,4},{3,5},{4,2},{5,3},{6,0},{7,1},{8,14},{9,15},{10,... | collective-permute-start | bytes 786440 | tf_op jit(solution)/shard_map/ppermute | solution.py:353
  155.5 54.2 %collective-permute-start.2 = (bf16[2,512,128]{2,1,0:T(8,128)(2,1)S(1)}, bf16[2,512,128]{2,1,0:T(8,128)(2,1)S(1)}, u32[]{:S(2)}, u32[]{:S(2)}) collective-permute-start(bf16[2,512,128]{2,1,0:T(8,128)(2,1)S(1)} %copy-done.17), channel_id=1, source_target_pairs={{0,5},{1,4},{2,7},{3,6},{4,1},{5,0},{6,3},{7,2},{8,13},{9,12},{10,... | collective-permute-start | bytes 786440 | tf_op jit(solution)/shard_map/ppermute | solution.py:353
  156.7 57.1 %collective-permute-start.3 = (bf16[2,512,128]{2,1,0:T(8,128)(2,1)S(1)}, bf16[2,512,128]{2,1,0:T(8,128)(2,1)S(1)}, u32[]{:S(2)}, u32[]{:S(2)}) collective-permute-start(bf16[2,512,128]{2,1,0:T(8,128)(2,1)S(1)} %copy-done.16), channel_id=1, source_target_pairs={{0,4},{1,5},{2,6},{3,7},{4,0},{5,1},{6,2},{7,3},{8,12},{9,13},{10,... | collective-permute-start | bytes 786440 | tf_op jit(solution)/shard_map/ppermute | solution.py:353
  157.2 58.4 %collective-permute-start.4 = (bf16[2,512,128]{2,1,0:T(8,128)(2,1)S(1)}, bf16[2,512,128]{2,1,0:T(8,128)(2,1)S(1)}, u32[]{:S(2)}, u32[]{:S(2)}) collective-permute-start(bf16[2,512,128]{2,1,0:T(8,128)(2,1)S(1)} %copy-done.15), channel_id=1, source_target_pairs={{0,3},{1,2},{2,1},{3,0},{4,7},{5,6},{6,5},{7,4},{8,11},{9,10},{10,... | collective-permute-start | bytes 786440 | tf_op jit(solution)/shard_map/ppermute | solution.py:353
  189.7 32.0 %copy-start.28 = (bf16[2,512,128]{2,1,0:T(8,128)(2,1)}, bf16[2,512,128]{2,1,0:T(8,128)(2,1)S(1)}, u32[]{:S(2)}) copy-start(bf16[2,512,128]{2,1,0:T(8,128)(2,1)S(1)} %collective-permute-done.refs_1_) | copy-start | bytes 786436
  189.7 32.0 %collective-permute-start.5 = (bf16[2,512,128]{2,1,0:T(8,128)(2,1)S(1)}, bf16[2,512,128]{2,1,0:T(8,128)(2,1)S(1)}, u32[]{:S(2)}, u32[]{:S(2)}) collective-permute-start(bf16[2,512,128]{2,1,0:T(8,128)(2,1)S(1)} %copy-done.14), channel_id=1, source_target_pairs={{0,2},{1,3},{2,0},{3,1},{4,6},{5,7},{6,4},{7,5},{8,10},{9,11},{10,... | collective-permute-start | bytes 786440 | tf_op jit(solution)/shard_map/ppermute | solution.py:353
  209.7 12.0 %copy-start.29 = (bf16[2,512,128]{2,1,0:T(8,128)(2,1)}, bf16[2,512,128]{2,1,0:T(8,128)(2,1)S(1)}, u32[]{:S(2)}) copy-start(bf16[2,512,128]{2,1,0:T(8,128)(2,1)S(1)} %collective-permute-done.1.refs_2_) | copy-start | bytes 786436
  209.7 12.0 %collective-permute-start.6 = (bf16[2,512,128]{2,1,0:T(8,128)(2,1)S(1)}, bf16[2,512,128]{2,1,0:T(8,128)(2,1)S(1)}, u32[]{:S(2)}, u32[]{:S(2)}) collective-permute-start(bf16[2,512,128]{2,1,0:T(8,128)(2,1)S(1)} %copy-done.13), channel_id=1, source_target_pairs={{0,1},{1,0},{2,3},{3,2},{4,5},{5,4},{6,7},{7,6},{8,9},{9,8},{10,11... | collective-permute-start | bytes 786440 | tf_op jit(solution)/shard_map/ppermute | solution.py:353
  209.7 12.0 %copy-start.31 = (bf16[2,512,128]{2,1,0:T(8,128)(2,1)}, bf16[2,512,128]{2,1,0:T(8,128)(2,1)S(1)}, u32[]{:S(2)}) copy-start(bf16[2,512,128]{2,1,0:T(8,128)(2,1)S(1)} %collective-permute-done.2.refs_3_) | copy-start | bytes 786436
  213.8 8.0 %copy-start.32 = (bf16[2,512,128]{2,1,0:T(8,128)(2,1)}, bf16[2,512,128]{2,1,0:T(8,128)(2,1)S(1)}, u32[]{:S(2)}) copy-start(bf16[2,512,128]{2,1,0:T(8,128)(2,1)S(1)} %collective-permute-done.3.refs_4_) | copy-start | bytes 786436
  244.2 54.2 %all-to-all-start.2 = ((bf16[32,1,2,128,128]{4,3,2,1,0:T(8,128)(2,1)}), bf16[32,1,2,128,128]{4,3,2,1,0:T(8,128)(2,1)S(1)}, u32[]{:S(2)}, u32[]{:S(2)}) async-start(bf16[32,1,2,128,128]{4,3,2,1,0:T(8,128)(2,1)} %clean.7), calls=%async_computation.2 | async-start | bytes 4194304 | tf_op jit(solution)/shard_map/all_to_all | solution.py:347
  (15 other events, 26.5 us)

commit v11 on v8

--- a/solution.py
+++ b/solution.py
@@ -11,6 +11,7 @@
 
 LANES = 128
 RADIX = 8
+ROWS = 16
 VMEM_BYTES = 56 * 1024 * 1024
 
 
@@ -28,7 +29,8 @@
 def twiddle_table(length):
     inner = length // RADIX
     phase = 2.0 * np.pi * np.outer(np.arange(RADIX), np.arange(inner)) / length
-    return np.stack([np.cos(phase), np.sin(phase)], axis=1).astype(np.float32)
+    table = np.stack([np.cos(phase), np.sin(phase)], axis=1)
+    return np.repeat(table[:, :, None], ROWS, axis=2).astype(jnp.bfloat16)
 
 
 def order_table():
@@ -88,28 +90,24 @@
         *out_refs, mid = refs
     rows, length = x_ref.shape[1:]
     inner = length // RADIX
-    step = 16
-    for i in range(rows // step):
-        at = slice(i * step, (i + 1) * step)
-        for block in range(inner // LANES):
+    for block in range(inner // LANES):
+        lanes = slice(block * LANES, (block + 1) * LANES)
+        other = slice(inner + block * LANES, inner + (block + 1) * LANES)
+        for i in range(rows // ROWS):
+            at = slice(i * ROWS, (i + 1) * ROWS)
             re, im = [], []
             for a in range(RADIX):
-                lanes = slice(a * inner + block * LANES, a * inner + (block + 1) * LANES)
-                re.append(x_ref[0, at, lanes].astype(jnp.float32))
-                im.append(x_ref[1, at, lanes].astype(jnp.float32))
+                wide = slice(a * inner + block * LANES, a * inner + (block + 1) * LANES)
+                re.append(x_ref[0, at, wide])
+                im.append(x_ref[1, at, wide])
             re, im = butterfly8(re, im)
-            lanes = slice(block * LANES, (block + 1) * LANES)
-            other = slice(inner + block * LANES, inner + (block + 1) * LANES)
-            for y_lo in range(RADIX):
-                if y_lo == 0:
-                    tr, ti = re[0], im[0]
-                else:
-                    cosine = twiddle_ref[y_lo, 0:1, lanes]
-                    sine = twiddle_ref[y_lo, 1:2, lanes]
-                    tr = re[y_lo] * cosine - im[y_lo] * sine
-                    ti = re[y_lo] * sine + im[y_lo] * cosine
-                mid[y_lo, at, lanes] = tr.astype(jnp.bfloat16)
-                mid[y_lo, at, other] = ti.astype(jnp.bfloat16)
+            mid[0, at, lanes] = re[0]
+            mid[0, at, other] = im[0]
+            for y_lo in range(1, RADIX):
+                cosine = twiddle_ref[y_lo, 0, :, lanes]
+                sine = twiddle_ref[y_lo, 1, :, lanes]
+                mid[y_lo, at, lanes] = re[y_lo] * cosine - im[y_lo] * sine
+                mid[y_lo, at, other] = re[y_lo] * sine + im[y_lo] * cosine
     for n, chunk in enumerate(chunks):
         for group in range(spread):
             column = (chunk * spread + group) * LANES
@@ -135,6 +133,8 @@
 def partner(at, step, count):
     if count & (count - 1):
         return (count - at + step) % count
+    if step:
+        step = sorted(range(1, count), key=lambda n: (-bin(n // 2).count("1"), -n))[step - 1]
     return at ^ step
 
 
@@ -159,7 +159,7 @@
             grid=(rows // block,),
             in_specs=[
                 pl.BlockSpec((2, block, length), lambda i, at: (0, i, 0)),
-                pl.BlockSpec((RADIX, 2, inner), lambda i, at: (0, 0, 0)),
+                pl.BlockSpec((RADIX, 2, ROWS, inner), lambda i, at: (0, 0, 0, 0)),
                 pl.BlockSpec((2 * inner, 2 * inner), lambda i, at: (0, 0)),
             ],
             out_specs=[spec] * outs,
@@ -176,37 +176,35 @@
     )(at, x, jnp.asarray(twiddle_table(length)), jnp.asarray(inner_table(inner)))
 
 
-def clean_kernel(split, at_ref, *refs):
-    *x_refs, basis_ref, basis_t_ref, gain_ref, swap_ref, back_ref, out_ref, slab = refs
+def clean_kernel(split, waits, at_ref, *refs):
+    *refs, out_ref, slab = refs
+    *x_refs, basis_ref, basis_t_ref, gain_ref, swap_ref, back_ref = refs[: len(refs) - waits]
     chans = slab.shape[0]
-    rows_dev = slab.shape[1] // LANES
+    pair = 2 * LANES
+    rows_dev = slab.shape[1] // pair
     tall = swap_ref.shape[0]
     group = tall // rows_dev
     sources = len(x_refs) if split else x_refs[0].shape[0]
     own = chans // sources
     for source in range(sources):
-        block = x_refs[source].at[0] if split else x_refs[0].at[source, 0]
+        block = x_refs[source] if split else x_refs[0].at[source]
         begin = partner(at_ref[0], source, sources) * own if split else source * own
         for k in range(own // group):
+            rows = slice(k * tall, (k + 1) * tall)
             turned = jnp.dot(
-                swap_ref[...], block[k * tall : (k + 1) * tall, :], preferred_element_type=jnp.float32
+                swap_ref[...],
+                jnp.concatenate([block[0, rows, :], block[1, rows, :]], axis=1),
+                preferred_element_type=jnp.float32,
             ).astype(jnp.bfloat16)
             channels = pl.ds(pl.multiple_of(begin + k * group, group), group)
             for u in range(rows_dev):
-                slab[channels, u * LANES : (u + 1) * LANES] = turned[u * group : (u + 1) * group]
-    pair = math.gcd(rows_dev, 2)
-    for first in range(0, rows_dev, pair):
-        lanes = slice(first * LANES, (first + pair) * LANES)
+                slab[channels, u * pair : (u + 1) * pair] = turned[u * group : (u + 1) * group]
+    for u in range(rows_dev):
+        lanes = slice(u * pair, (u + 1) * pair)
         line = slab[:, lanes]
         amps = jnp.dot(basis_t_ref[...], line, preferred_element_type=jnp.float32)
         amps = amps.astype(jnp.bfloat16).astype(jnp.float32)
-        front = jnp.concatenate(
-            [
-                gain_ref[:, first + k : first + k + 1] * amps[:, k * LANES : (k + 1) * LANES]
-                for k in range(pair)
-            ],
-            axis=1,
-        ).astype(jnp.bfloat16)
+        front = (gain_ref[:, u : u + 1] * amps).astype(jnp.bfloat16)
         drop = jnp.dot(basis_ref[...], front, preferred_element_type=jnp.float32)
         slab[:, lanes] = (line.astype(jnp.float32) - drop).astype(jnp.bfloat16)
     out_rows = out_ref.shape[2]
@@ -215,49 +213,39 @@
     for b in range(chans // group):
         channels = slice(b * group, (b + 1) * group)
         tile = jnp.concatenate(
-            [slab[channels, u * LANES : (u + 1) * LANES] for u in range(rows_dev)], axis=0
+            [slab[channels, u * pair : (u + 1) * pair] for u in range(rows_dev)], axis=0
         )
         value = jnp.dot(back_ref[...], tile, preferred_element_type=jnp.float32)
-        if out_rows % tall == 0:
-            target, row = divmod(b * tall, out_rows)
-            out_ref[target, 0, row : row + tall, :] = value.astype(jnp.bfloat16)
-        else:
-            take = tall // out_rows
-            out_ref[b * take : (b + 1) * take, 0] = value.reshape(take, out_rows, LANES).astype(
-                jnp.bfloat16
-            )
-
-
-def clean(at, xs, basis, basis_t, gain, targets, rows_dev):
+        for part in range(2):
+            half = value[:, part * LANES : (part + 1) * LANES]
+            if out_rows % tall == 0:
+                target, row = divmod(b * tall, out_rows)
+                out_ref[target, part, row : row + tall, :] = half.astype(jnp.bfloat16)
+            else:
+                take = tall // out_rows
+                out_ref[b * take : (b + 1) * take, part] = half.reshape(
+                    take, out_rows, LANES
+                ).astype(jnp.bfloat16)
+
+
+def clean(at, xs, basis, basis_t, gain, targets, rows_dev, before):
     split = len(xs) > 1
     chans = basis.shape[0]
     sources = len(xs) if split else xs[0].shape[0]
     own = chans // sources
     swap = swap_table(min(256 // rows_dev, own), rows_dev)
     back = np.ascontiguousarray(swap_table(256 // rows_dev, rows_dev).T)
-    out_rows = chans * rows_dev // targets
-    whole = lambda s, at: (0, 0)
-    if split:
-        spec = pl.BlockSpec((1, own * rows_dev, LANES), lambda s, at: (s, 0, 0))
-    else:
-        spec = pl.BlockSpec((sources, 1, own * rows_dev, LANES), lambda s, at: (0, s, 0, 0))
+    vmem = pl.BlockSpec(memory_space=pltpu.VMEM)
     return pl.pallas_call(
-        functools.partial(clean_kernel, split),
-        grid_spec=pltpu.PrefetchScalarGridSpec(
-            num_scalar_prefetch=1,
-            grid=(2,),
-            in_specs=[spec] * len(xs)
-            + [
-                pl.BlockSpec(basis.shape, whole),
-                pl.BlockSpec(basis.shape, whole),
-                pl.BlockSpec(gain.shape, whole),
-                pl.BlockSpec(swap.shape, whole),
-                pl.BlockSpec(back.shape, whole),
-            ],
-            out_specs=pl.BlockSpec((targets, 1, out_rows, LANES), lambda s, at: (0, s, 0, 0)),
-            scratch_shapes=[pltpu.VMEM((chans, rows_dev * LANES), jnp.bfloat16)],
-        ),
-        out_shape=jax.ShapeDtypeStruct((targets, 2, out_rows, LANES), jnp.bfloat16),
+        functools.partial(clean_kernel, split, len(before)),
+        in_specs=[pl.BlockSpec(memory_space=pltpu.SMEM)]
+        + [vmem] * (len(xs) + 5)
+        + [pl.BlockSpec(memory_space=pl.ANY)] * len(before),
+        out_specs=vmem,
+        out_shape=jax.ShapeDtypeStruct(
+            (targets, 2, chans * rows_dev // targets, LANES), jnp.bfloat16
+        ),
+        scratch_shapes=[pltpu.VMEM((chans, rows_dev * 2 * LANES), jnp.bfloat16)],
         compiler_params=params(),
         cost_estimate=pl.CostEstimate(
             flops=12 * chans * chans * rows_dev * LANES,
@@ -265,7 +253,7 @@
             transcendentals=0,
         ),
         name="clean",
-    )(at, *xs, basis, basis_t, gain, jnp.asarray(swap), jnp.asarray(back))
+    )(at, *xs, basis, basis_t, gain, jnp.asarray(swap), jnp.asarray(back), *before)
 
 
 def image_kernel(scale, x_ref, table_ref, order_ref, *refs):
@@ -367,9 +355,10 @@
         cells += [
             scatter(sends[k * chan_count : (k + 1) * chan_count]) for k in range(count - 1)
         ]
-    held = []
+    held, before = [], cells[1][:1] if count > 1 else []
     for k in range(count):
-        cleaned = clean(at, cells[k], basis, basis_t, gain, targets, rows_dev)
+        cleaned = clean(at, cells[k], basis, basis_t, gain, targets, rows_dev, before)
+        before = [cleaned]
         planes = exchange(cleaned, ("uv", "chan"))
         planes = planes.reshape((uv_count, chan_count) + planes.shape[1:])
         held = [image(planes, k, count, rows_dev, held)]

time: 326 us -> 324 us (level)
  blocking collectives: 0 us -> 53.1 us
  waiting for transfers between devices: 174 us -> 133 us
  Pallas kernels: 91.2 us -> 84.7 us
  starting transfers between devices: 46.5 us -> 40.1 us
    all_to_all x0 -> x1, blocking collectives: none -> 53.1 us  [exchange(): return lax.all_to_all(x, axes, split_axis=0, concat_axis=0, tiled=True)]
    all_to_all x6 -> x5, waiting for transfers between devices: 66 us -> 35.3 us  [exchange(): return lax.all_to_all(x, axes, split_axis=0, concat_axis=0, tiled=True)]
    ppermute x21, waiting for transfers between devices: 108 us -> 98 us  [scatter(): lax.ppermute(pieces[step], 'chan', [(j, int(partner(np.int32(j), step, co...]
    pallas_call x4, Pallas kernels: 34.1 us -> 28.8 us  [clean(): pl.pallas_call(functools.partial(clean_kernel, split, len(before)), in_sp...]
    all_to_all x6 -> x5, starting transfers between devices: 27.3 us -> 22.5 us  [exchange(): return lax.all_to_all(x, axes, split_axis=0, concat_axis=0, tiled=True)]
  transfers between devices with their start and end apart: 27 -> 26, of which waited for: 15 -> 15; matrix products, arithmetic and copies ran while one was open for 0% -> 0% of each run, Pallas kernels for 26% -> 22%
where the time goes in v11:
time: 324 us; the launch traced here: 320 us
  waiting for transfers between devices  133 us (41%)
  Pallas kernels  84.7 us (26%)
  blocking collectives  53.1 us (16%)
  starting transfers between devices  40.1 us (12%)
  local copies, waits for them, and re-layouts  7.32 us (2%)
    ppermute x21, waiting for transfers between devices, scatter(): lax.ppermute(pieces[step], 'chan', [(j, int(partner(np.int32(j), step, co...  98 us
    all_to_all x1, blocking collectives, exchange(): return lax.all_to_all(x, axes, split_axis=0, concat_axis=0, tiled=True)  53.1 us
    all_to_all x5, waiting for transfers between devices, exchange(): return lax.all_to_all(x, axes, split_axis=0, concat_axis=0, tiled=True)  35.3 us
    pallas_call x4, Pallas kernels, clean(): pl.pallas_call(functools.partial(clean_kernel, split, len(before)), in_sp...  28.8 us
    pallas_call x2, Pallas kernels, column_transform(): pl.pallas_call(functools.partial(column_kernel, chunks, pieces // RADIX,...  28.1 us
    pallas_call x4, Pallas kernels, image(): pl.pallas_call(functools.partial(image_kernel, scale), grid=(chans // gro...  25.8 us
    all_to_all x5, starting transfers between devices, exchange(): return lax.all_to_all(x, axes, split_axis=0, concat_axis=0, tiled=True)  22.5 us
    ppermute x21, starting transfers between devices, scatter(): lax.ppermute(pieces[step], 'chan', [(j, int(partner(np.int32(j), step, co...  17.6 us
  transfers between devices with their start and end apart: 26, of which 15 were waited for; matrix products, arithmetic and copies ran while one was open for 0% of the time, Pallas kernels for 22%

profile of v11, /device:TPU:8, one launch (start us, length us, event | category | flops | bytes accessed | tf_op | source)
XLA Modules:
  0.0 319.7 jit_solution(17304155229204261971)
XLA Ops:
  0.0 1.7 broadcast_in_dim.2
  1.7 3.7 %all-to-all-start = ((bf16[8,64,512]{2,1,0:T(8,128)(2,1)}), bf16[8,64,512]{2,1,0:T(8,128)(2,1)S(1)}, u32[]{:S(2)}, u32[]{:S(2)}) async-start(bf16[8,64,512]{2,1,0:T(8,128)(2,1)} %broadcast_in_dim.2), calls=%async_computation | async-start | bytes 1048576 | tf_op jit(solution)/shard_map/all_to_all | solution.py:326
  5.4 11.4 %column_transform.3 = bf16[8,2,512,128]{3,2,1,0:T(8,128)(2,1)} custom-call(s32[1]{0:T(128)} %bitcast.at_ref, bf16[2,512,4096]{2,1,0:T(8,128)(2,1)} %bitcast.15, bf16[8,2,16,512]{3,2,1,0:T(8,128)(2,1)} %constant.16.clone.twiddle_ref, bf16[1024,1024]{1,0:T(8,128)(2,1)} %constant.17.clone.table_ref), custom_call_target="tpu_custom_call" | custom-call | flops 8589934592 | bytes 16777216 | tf_op jit(solution)/shard_map/column_transform/pallas_call | solution.py:155
  16.8 0.8 add_divide_fusion.refs_3_.refs_10_
  17.7 0.8 copy-done.3
  18.5 4.2 %all-to-all-start.1 = ((bf16[8,2,512,128]{3,2,1,0:T(8,128)(2,1)}), bf16[8,2,512,128]{3,2,1,0:T(8,128)(2,1)S(1)}, u32[]{:S(2)}, u32[]{:S(2)}) async-start(bf16[8,2,512,128]{3,2,1,0:T(8,128)(2,1)} %column_transform.3), calls=%async_computation.1 | async-start | bytes 4194304 | tf_op jit(solution)/shard_map/all_to_all | solution.py:326
  22.7 16.7 %column_transform.2 = (bf16[2,512,128]{2,1,0:T(8,128)(2,1)}, bf16[2,512,128]{2,1,0:T(8,128)(2,1)}, bf16[2,512,128]{2,1,0:T(8,128)(2,1)}, bf16[2,512,128]{2,1,0:T...) custom-call(s32[1]{0:T(128)} %bitcast.at_ref, ...), custom_call_target="tpu_custom_call" | custom-call | flops 25769803776 | bytes 16777216 | tf_op jit(solution)/shard_map/column_transform/pallas_call | solution.py:155
  39.3 2.0 turn.1.refs_2_.refs_9_
  41.4 7.9 %all-to-all-done.1.refs_0_ = bf16[8,2,512,128]{3,2,1,0:T(8,128)(2,1)S(1)} async-done(((bf16[8,2,512,128]{3,2,1,0:T(8,128)(2,1)}), bf16[8,2,512,128]{3,2,1,0:T(8,128)(2,1)S(1)}, u32[]{:S(2)}, u32[]{:S(2)}) %all-to-all-start.1) | async-done | bytes 2097184 | tf_op jit(solution)/shard_map/all_to_all | solution.py:326
  49.3 1.3 copy-done.2
  50.6 7.1 %clean.4.refs_13_ = bf16[32,2,128,128]{3,2,1,0:T(8,128)(2,1)} custom-call(s32[1]{0:T(128)} %bitcast.at_ref, bf16[8,2,512,128]{3,2,1,0:T(8,128)(2,1)} %copy-done.2, bf16[512,512]{1,0:T(8,128)(2,1)} %bitcast.11, bf16[512,512]{1,0:T(8,128)(2,1)} %turn.1.refs_2_.refs_9_, f32[512,8]{1,0:T(8,128)} %add_divide_fusion.refs_3_.refs_10_, ...), custom_call_target="tpu_custom_call" | custom-call | flops 3221225472 | bytes 4194304 | tf_op jit(solution)/shard_map/clean/pallas_call | solution.py:239
  57.7 4.2 %all-to-all-start.5 = ((bf16[32,2,128,128]{3,2,1,0:T(8,128)(2,1)}), bf16[32,2,128,128]{3,2,1,0:T(8,128)(2,1)S(1)}, u32[]{:S(2)}, u32[]{:S(2)}) async-start(bf16[32,2,128,128]{3,2,1,0:T(8,128)(2,1)} %clean.4.refs_13_), calls=%async_computation.5 | async-start | bytes 4194304 | tf_op jit(solution)/shard_map/all_to_all | solution.py:326
  61.9 2.2 collective-permute-start.7
  64.7 2.0 collective-permute-start.14
  67.3 1.2 collective-permute-start.16
  68.5 18.2 %collective-permute-done.7.refs_1_ = bf16[2,512,128]{2,1,0:T(8,128)(2,1)S(1)} collective-permute-done((bf16[2,512,128]{2,1,0:T(8,128)(2,1)}, bf16[2,512,128]{2,1,0:T(8,128)(2,1)S(1)}, u32[]{:S(2)}, u32[]{:S(2)}) %collective-permute-start.7) | collective-permute-done | bytes 262176 | tf_op jit(solution)/shard_map/ppermute | solution.py:332
  86.7 1.7 collective-permute-start.17
  88.4 11.5 %collective-permute-done.8.refs_2_ = bf16[2,512,128]{2,1,0:T(8,128)(2,1)S(1)} collective-permute-done((bf16[2,512,128]{2,1,0:T(8,128)(2,1)}, bf16[2,512,128]{2,1,0:T(8,128)(2,1)S(1)}, u32[]{:S(2)}, u32[]{:S(2)}) %collective-permute-start.8) | collective-permute-done | bytes 262176 | tf_op jit(solution)/shard_map/ppermute | solution.py:332
  100.0 4.9 %collective-permute-done.14.refs_1_ = bf16[2,512,128]{2,1,0:T(8,128)(2,1)S(1)} collective-permute-done((bf16[2,512,128]{2,1,0:T(8,128)(2,1)}, bf16[2,512,128]{2,1,0:T(8,128)(2,1)S(1)}, u32[]{:S(2)}, u32[]{:S(2)}) %collective-permute-start.14) | collective-permute-done | bytes 262176 | tf_op jit(solution)/shard_map/ppermute | solution.py:332
  104.9 1.7 collective-permute-start.19
  106.6 7.6 %collective-permute-done.15.refs_2_ = bf16[2,512,128]{2,1,0:T(8,128)(2,1)S(1)} collective-permute-done((bf16[2,512,128]{2,1,0:T(8,128)(2,1)}, bf16[2,512,128]{2,1,0:T(8,128)(2,1)S(1)}, u32[]{:S(2)}, u32[]{:S(2)}) %collective-permute-start.15) | collective-permute-done | bytes 262176 | tf_op jit(solution)/shard_map/ppermute | solution.py:332
  114.2 1.4 collective-permute-done.16.refs_3_
  115.7 5.7 %collective-permute-done.17.refs_4_ = bf16[2,512,128]{2,1,0:T(8,128)(2,1)S(1)} collective-permute-done((bf16[2,512,128]{2,1,0:T(8,128)(2,1)}, bf16[2,512,128]{2,1,0:T(8,128)(2,1)S(1)}, u32[]{:S(2)}, u32[]{:S(2)}) %collective-permute-start.17) | collective-permute-done | bytes 262176 | tf_op jit(solution)/shard_map/ppermute | solution.py:332
  121.4 0.8 collective-permute-start.11
  122.2 2.7 collective-permute-done.19.refs_6_
  126.1 7.2 %clean.5.refs_13_ = bf16[32,2,128,128]{3,2,1,0:T(8,128)(2,1)} custom-call(s32[1]{0:T(128)} %bitcast.at_ref, bf16[2,512,128]{2,1,0:T(8,128)(2,1)} %get-tuple-element.45.refs_6_.refs_0_, bf16[2,512,128]{2,1,0:T(8,128)(2,1)} %copy-done.18, bf16[2,512,128]{2,1,0:T(8,128)(2,1)} %copy-done.19, bf16[2,512,128]{2,1,0:T(8,128)(2,1)} %copy-done.20, ...), custom_call_target="tpu_custom_call" | custom-call | flops 3221225472 | bytes 4194304 | tf_op jit(solution)/shard_map/clean/pallas_call | solution.py:239
  133.4 2.6 collective-permute-done.12.refs_6_
  136.0 0.7 copy-done.33
  136.7 7.3 %clean.6.refs_13_ = bf16[32,2,128,128]{3,2,1,0:T(8,128)(2,1)} custom-call(s32[1]{0:T(128)} %bitcast.at_ref, bf16[2,512,128]{2,1,0:T(8,128)(2,1)} %get-tuple-element.37.refs_0_, bf16[2,512,128]{2,1,0:T(8,128)(2,1)} %copy-done.16, bf16[2,512,128]{2,1,0:T(8,128)(2,1)} %copy-done.17, bf16[2,512,128]{2,1,0:T(8,128)(2,1)} %copy-done.22, ...), custom_call_target="tpu_custom_call" | custom-call | flops 3221225472 | bytes 4194304 | tf_op jit(solution)/shard_map/clean/pallas_call | solution.py:239
  144.0 53.1 %all_to_all.30 = bf16[32,2,128,128]{3,2,1,0:T(8,128)(2,1)} all-to-all(bf16[32,2,128,128]{3,2,1,0:T(8,128)(2,1)} %clean.6.refs_13_), channel_id=1, replica_groups=mesh['uv'=4,'chan'=8] {'uv','chan'}, dimensions={0} | all-to-all | bytes 4194304 | tf_op jit(solution)/shard_map/all_to_all | solution.py:326
  197.1 4.7 %all-to-all-start.4 = ((bf16[32,2,128,128]{3,2,1,0:T(8,128)(2,1)}), bf16[32,2,128,128]{3,2,1,0:T(8,128)(2,1)S(1)}, u32[]{:S(2)}, u32[]{:S(2)}) async-start(bf16[32,2,128,128]{3,2,1,0:T(8,128)(2,1)} %clean.5.refs_13_), calls=%async_computation.4 | async-start | bytes 4194304 | tf_op jit(solution)/shard_map/all_to_all | solution.py:326
  201.8 2.2 collective-permute-start
  204.5 1.1 collective-permute-start.2
  206.2 1.2 collective-permute-start.4
  207.5 19.1 %collective-permute-done.refs_1_ = bf16[2,512,128]{2,1,0:T(8,128)(2,1)S(1)} collective-permute-done((bf16[2,512,128]{2,1,0:T(8,128)(2,1)}, bf16[2,512,128]{2,1,0:T(8,128)(2,1)S(1)}, u32[]{:S(2)}, u32[]{:S(2)}) %collective-permute-start) | collective-permute-done | bytes 262176 | tf_op jit(solution)/shard_map/ppermute | solution.py:332
  226.5 0.6 collective-permute-start.5
  227.2 11.9 %collective-permute-done.1.refs_2_ = bf16[2,512,128]{2,1,0:T(8,128)(2,1)S(1)} collective-permute-done((bf16[2,512,128]{2,1,0:T(8,128)(2,1)}, bf16[2,512,128]{2,1,0:T(8,128)(2,1)S(1)}, u32[]{:S(2)}, u32[]{:S(2)}) %collective-permute-start.1) | collective-permute-done | bytes 262176 | tf_op jit(solution)/shard_map/ppermute | solution.py:332
  239.1 1.9 collective-permute-done.2.refs_3_
  241.1 8.2 %collective-permute-done.3.refs_4_ = bf16[2,512,128]{2,1,0:T(8,128)(2,1)S(1)} collective-permute-done((bf16[2,512,128]{2,1,0:T(8,128)(2,1)S(1)}, bf16[2,512,128]{2,1,0:T(8,128)(2,1)S(1)}, u32[]{:S(2)}, u32[]{:S(2)}) %collective-permute-start.3) | collective-permute-done | bytes 262176 | tf_op jit(solution)/shard_map/ppermute | solution.py:332
  249.2 2.2 collective-permute-done.5.refs_6_
  252.3 7.3 %clean.7 = bf16[32,2,128,128]{3,2,1,0:T(8,128)(2,1)} custom-call(s32[1]{0:T(128)} %bitcast.at_ref, bf16[2,512,128]{2,1,0:T(8,128)(2,1)} %get-tuple-element.29.refs_0_, bf16[2,512,128]{2,1,0:T(8,128)(2,1)} %copy-done.24, bf16[2,512,128]{2,1,0:T(8,128)(2,1)} %copy-done.25, bf16[2,512,128]{2,1,0:T(8,128)(2,1)} %copy-done.27, bf16[2,512,128]{2,1,0:T(8,128)(2,1)} %copy-done.29, ...), custom_call_target="tpu_custom_call" | custom-call | flops 3221225472 | bytes 4194304 | tf_op jit(solution)/shard_map/clean/pallas_call | solution.py:239
  259.6 1.3 copy-done.1
  260.9 5.7 %all-to-all-start.2 = ((bf16[32,2,128,128]{3,2,1,0:T(8,128)(2,1)}), bf16[32,2,128,128]{3,2,1,0:T(8,128)(2,1)}, u32[]{:S(2)}, u32[]{:S(2)}) async-start(bf16[32,2,128,128]{3,2,1,0:T(8,128)(2,1)} %clean.7), calls=%async_computation.2 | async-start | bytes 4194304 | tf_op jit(solution)/shard_map/all_to_all | solution.py:326
  266.6 6.5 %image.4.refs_0_ = bf16[2,16,32,4096]{3,2,1,0:T(8,128)(2,1)} custom-call(bf16[4,8,2,128,128]{4,3,2,1,0:T(8,128)(2,1)} %bitcast.7, bf16[256,256]{1,0:T(8,128)(2,1)} %constant.20.clone.table_ref, bf16[1024,1024]{1,0:T(8,128)(2,1)} %constant.21.clone.order_ref), custom_call_target="tpu_custom_call" | custom-call | flops 2147483648 | bytes 4194304 | tf_op jit(solution)/shard_map/image/pallas_call | solution.py:285
  273.0 6.4 %image.5.refs_0_ = bf16[2,16,32,4096]{3,2,1,0:T(8,128)(2,1)} custom-call(bf16[4,8,2,128,128]{4,3,2,1,0:T(8,128)(2,1)} %bitcast.9, bf16[256,256]{1,0:T(8,128)(2,1)} %constant.20.clone.table_ref, bf16[1024,1024]{1,0:T(8,128)(2,1)} %constant.21.clone.order_ref, bf16[2,16,32,4096]{3,2,1,0:T(8,128)(2,1)} %image.4.refs_0_), custom_call_target="tpu_custom_call", output_to_operand_aliasing={{}: (3, {})} | custom-call | flops 2147483648 | bytes 4194304 | tf_op jit(solution)/shard_map/image/pallas_call | solution.py:285
  279.5 6.4 %image.6.refs_0_ = bf16[2,16,32,4096]{3,2,1,0:T(8,128)(2,1)} custom-call(bf16[4,8,2,128,128]{4,3,2,1,0:T(8,128)(2,1)} %bitcast.8, bf16[256,256]{1,0:T(8,128)(2,1)} %constant.20.clone.table_ref, bf16[1024,1024]{1,0:T(8,128)(2,1)} %constant.21.clone.order_ref, bf16[2,16,32,4096]{3,2,1,0:T(8,128)(2,1)} %image.5.refs_0_), custom_call_target="tpu_custom_call", output_to_operand_aliasing={{}: (3, {})} | custom-call | flops 2147483648 | bytes 4194304 | tf_op jit(solution)/shard_map/image/pallas_call | solution.py:285
  285.9 27.4 %all-to-all-done.2 = bf16[32,2,128,128]{3,2,1,0:T(8,128)(2,1)} async-done(((bf16[32,2,128,128]{3,2,1,0:T(8,128)(2,1)}), bf16[32,2,128,128]{3,2,1,0:T(8,128)(2,1)}, u32[]{:S(2)}, u32[]{:S(2)}) %all-to-all-start.2) | async-done | bytes 2097184 | tf_op jit(solution)/shard_map/all_to_all | solution.py:326
  313.3 6.4 %image.7 = bf16[2,16,32,4096]{3,2,1,0:T(8,128)(2,1)} custom-call(bf16[4,8,2,128,128]{4,3,2,1,0:T(8,128)(2,1)} %bitcast.3.x_ref, bf16[256,256]{1,0:T(8,128)(2,1)} %constant.20.clone.table_ref, bf16[1024,1024]{1,0:T(8,128)(2,1)} %constant.21.clone.order_ref, bf16[2,16,32,4096]{3,2,1,0:T(8,128)(2,1)} %image.6.refs_0_), custom_call_target="tpu_custom_call", output_to_operand_aliasing={{}: (3, {})} | custom-call | flops 2147483648 | bytes 4194304 | tf_op jit(solution)/shard_map/image/pallas_call | solution.py:285
  (92 shorter events, 4.4 us)
Async XLA Ops:
  1.7 16.0 %all-to-all-start = ((bf16[8,64,512]{2,1,0:T(8,128)(2,1)}), bf16[8,64,512]{2,1,0:T(8,128)(2,1)S(1)}, u32[]{:S(2)}, u32[]{:S(2)}) async-start(bf16[8,64,512]{2,1,0:T(8,128)(2,1)} %broadcast_in_dim.2), calls=%async_computation | async-start | bytes 1048576 | tf_op jit(solution)/shard_map/all_to_all | solution.py:326
  5.4 11.4 %copy-start.4 = (f32[512]{0:T(512)S(1)}, f32[512]{0:T(512)}, u32[]{:S(2)}) copy-start(f32[512]{0:T(512)} %param.26) | copy-start | bytes 6148
  5.4 11.4 %copy-start.5 = (f32[8]{0:T(128)S(1)}, f32[8]{0:T(128)}, u32[]{:S(2)}) copy-start(f32[8]{0:T(128)} %param.27) | copy-start | bytes 100
  18.5 30.8 %all-to-all-start.1 = ((bf16[8,2,512,128]{3,2,1,0:T(8,128)(2,1)}), bf16[8,2,512,128]{3,2,1,0:T(8,128)(2,1)S(1)}, u32[]{:S(2)}, u32[]{:S(2)}) async-start(bf16[8,2,512,128]{3,2,1,0:T(8,128)(2,1)} %column_transform.3), calls=%async_computation.1 | async-start | bytes 4194304 | tf_op jit(solution)/shard_map/all_to_all | solution.py:326
  57.7 58.0 %copy-start.15 = (bf16[2,512,128]{2,1,0:T(8,128)(2,1)S(1)}, bf16[2,512,128]{2,1,0:T(8,128)(2,1)}, u32[]{:S(2)}) copy-start(bf16[2,512,128]{2,1,0:T(8,128)(2,1)} %get-tuple-element.40) | copy-start | bytes 786436
  57.7 63.7 %copy-start.14 = (bf16[2,512,128]{2,1,0:T(8,128)(2,1)S(1)}, bf16[2,512,128]{2,1,0:T(8,128)(2,1)}, u32[]{:S(2)}) copy-start(bf16[2,512,128]{2,1,0:T(8,128)(2,1)} %get-tuple-element.41) | copy-start | bytes 786436
  57.7 63.7 %copy-start.13 = (bf16[2,512,128]{2,1,0:T(8,128)(2,1)S(1)}, bf16[2,512,128]{2,1,0:T(8,128)(2,1)}, u32[]{:S(2)}) copy-start(bf16[2,512,128]{2,1,0:T(8,128)(2,1)} %get-tuple-element.42) | copy-start | bytes 786436
  57.7 67.2 %copy-start.12 = (bf16[2,512,128]{2,1,0:T(8,128)(2,1)S(1)}, bf16[2,512,128]{2,1,0:T(8,128)(2,1)}, u32[]{:S(2)}) copy-start(bf16[2,512,128]{2,1,0:T(8,128)(2,1)} %get-tuple-element.43) | copy-start | bytes 786436
  57.7 67.6 %copy-start.11 = (bf16[2,512,128]{2,1,0:T(8,128)(2,1)S(1)}, bf16[2,512,128]{2,1,0:T(8,128)(2,1)}, u32[]{:S(2)}) copy-start(bf16[2,512,128]{2,1,0:T(8,128)(2,1)} %get-tuple-element.44) | copy-start | bytes 786436
  57.7 86.3 %all-to-all-start.5 = ((bf16[32,2,128,128]{3,2,1,0:T(8,128)(2,1)}), bf16[32,2,128,128]{3,2,1,0:T(8,128)(2,1)S(1)}, u32[]{:S(2)}, u32[]{:S(2)}) async-start(bf16[32,2,128,128]{3,2,1,0:T(8,128)(2,1)} %clean.4.refs_13_), calls=%async_computation.5 | async-start | bytes 4194304 | tf_op jit(solution)/shard_map/all_to_all | solution.py:326
  61.9 24.8 %collective-permute-start.7 = (bf16[2,512,128]{2,1,0:T(8,128)(2,1)}, bf16[2,512,128]{2,1,0:T(8,128)(2,1)S(1)}, u32[]{:S(2)}, u32[]{:S(2)}) collective-permute-start(bf16[2,512,128]{2,1,0:T(8,128)(2,1)} %get-tuple-element.38), channel_id=1, source_target_pairs={{0,7},{1,6},{2,5},{3,4},{4,3},{5,2},{6,1},{7,0},{8,15},{9,14},{10,... | collective-permute-start | bytes 786440 | tf_op jit(solution)/shard_map/ppermute | solution.py:332
  64.1 35.8 %collective-permute-start.8 = (bf16[2,512,128]{2,1,0:T(8,128)(2,1)}, bf16[2,512,128]{2,1,0:T(8,128)(2,1)S(1)}, u32[]{:S(2)}, u32[]{:S(2)}) collective-permute-start(bf16[2,512,128]{2,1,0:T(8,128)(2,1)} %get-tuple-element.39), channel_id=1, source_target_pairs={{0,6},{1,7},{2,4},{3,5},{4,2},{5,3},{6,0},{7,1},{8,14},{9,15},{10,... | collective-permute-start | bytes 786440 | tf_op jit(solution)/shard_map/ppermute | solution.py:332
  64.7 40.2 %collective-permute-start.14 = (bf16[2,512,128]{2,1,0:T(8,128)(2,1)}, bf16[2,512,128]{2,1,0:T(8,128)(2,1)S(1)}, u32[]{:S(2)}, u32[]{:S(2)}) collective-permute-start(bf16[2,512,128]{2,1,0:T(8,128)(2,1)} %get-tuple-element.46), channel_id=1, source_target_pairs={{0,7},{1,6},{2,5},{3,4},{4,3},{5,2},{6,1},{7,0},{8,15},{9,14},{10,... | collective-permute-start | bytes 786440 | tf_op jit(solution)/shard_map/ppermute | solution.py:332
  66.7 47.5 %collective-permute-start.15 = (bf16[2,512,128]{2,1,0:T(8,128)(2,1)}, bf16[2,512,128]{2,1,0:T(8,128)(2,1)S(1)}, u32[]{:S(2)}, u32[]{:S(2)}) collective-permute-start(bf16[2,512,128]{2,1,0:T(8,128)(2,1)} %get-tuple-element.47), channel_id=1, source_target_pairs={{0,6},{1,7},{2,4},{3,5},{4,2},{5,3},{6,0},{7,1},{8,14},{9,15},{10,... | collective-permute-start | bytes 786440 | tf_op jit(solution)/shard_map/ppermute | solution.py:332
  67.3 48.3 %collective-permute-start.16 = (bf16[2,512,128]{2,1,0:T(8,128)(2,1)}, bf16[2,512,128]{2,1,0:T(8,128)(2,1)S(1)}, u32[]{:S(2)}, u32[]{:S(2)}) collective-permute-start(bf16[2,512,128]{2,1,0:T(8,128)(2,1)} %get-tuple-element.48), channel_id=1, source_target_pairs={{0,5},{1,4},{2,7},{3,6},{4,1},{5,0},{6,3},{7,2},{8,13},{9,12},{10,... | collective-permute-start | bytes 786440 | tf_op jit(solution)/shard_map/ppermute | solution.py:332
  86.7 46.6 %copy-start.16 = (bf16[2,512,128]{2,1,0:T(8,128)(2,1)}, bf16[2,512,128]{2,1,0:T(8,128)(2,1)S(1)}, u32[]{:S(2)}) copy-start(bf16[2,512,128]{2,1,0:T(8,128)(2,1)S(1)} %collective-permute-done.7.refs_1_) | copy-start | bytes 786436
  86.7 34.6 %collective-permute-start.17 = (bf16[2,512,128]{2,1,0:T(8,128)(2,1)}, bf16[2,512,128]{2,1,0:T(8,128)(2,1)S(1)}, u32[]{:S(2)}, u32[]{:S(2)}) collective-permute-start(bf16[2,512,128]{2,1,0:T(8,128)(2,1)} %get-tuple-element.49), channel_id=1, source_target_pairs={{0,4},{1,5},{2,6},{3,7},{4,0},{5,1},{6,2},{7,3},{8,12},{9,13},{10,... | collective-permute-start | bytes 786440 | tf_op jit(solution)/shard_map/ppermute | solution.py:332
  99.9 33.4 %copy-start.17 = (bf16[2,512,128]{2,1,0:T(8,128)(2,1)}, bf16[2,512,128]{2,1,0:T(8,128)(2,1)S(1)}, u32[]{:S(2)}) copy-start(bf16[2,512,128]{2,1,0:T(8,128)(2,1)S(1)} %collective-permute-done.8.refs_2_) | copy-start | bytes 786436
  99.9 21.4 %collective-permute-start.18 = (bf16[2,512,128]{2,1,0:T(8,128)(2,1)}, bf16[2,512,128]{2,1,0:T(8,128)(2,1)S(1)}, u32[]{:S(2)}, u32[]{:S(2)}) collective-permute-start(bf16[2,512,128]{2,1,0:T(8,128)(2,1)} %get-tuple-element.50), channel_id=1, source_target_pairs={{0,3},{1,2},{2,1},{3,0},{4,7},{5,6},{6,5},{7,4},{8,11},{9,10},{10,... | collective-permute-start | bytes 786440 | tf_op jit(solution)/shard_map/ppermute | solution.py:332
  104.9 20.5 %copy-start.18 = (bf16[2,512,128]{2,1,0:T(8,128)(2,1)}, bf16[2,512,128]{2,1,0:T(8,128)(2,1)S(1)}, u32[]{:S(2)}) copy-start(bf16[2,512,128]{2,1,0:T(8,128)(2,1)S(1)} %collective-permute-done.14.refs_1_) | copy-start | bytes 786436
  104.9 20.0 %collective-permute-start.19 = (bf16[2,512,128]{2,1,0:T(8,128)(2,1)}, bf16[2,512,128]{2,1,0:T(8,128)(2,1)S(1)}, u32[]{:S(2)}, u32[]{:S(2)}) collective-permute-start(bf16[2,512,128]{2,1,0:T(8,128)(2,1)} %get-tuple-element.51), channel_id=1, source_target_pairs={{0,2},{1,3},{2,0},{3,1},{4,6},{5,7},{6,4},{7,5},{8,10},{9,11},{10,... | collective-permute-start | bytes 786440 | tf_op jit(solution)/shard_map/ppermute | solution.py:332
  114.2 11.2 %copy-start.19 = (bf16[2,512,128]{2,1,0:T(8,128)(2,1)}, bf16[2,512,128]{2,1,0:T(8,128)(2,1)S(1)}, u32[]{:S(2)}) copy-start(bf16[2,512,128]{2,1,0:T(8,128)(2,1)S(1)} %collective-permute-done.15.refs_2_) | copy-start | bytes 786436
  114.2 11.1 %collective-permute-start.20 = (bf16[2,512,128]{2,1,0:T(8,128)(2,1)}, bf16[2,512,128]{2,1,0:T(8,128)(2,1)S(1)}, u32[]{:S(2)}, u32[]{:S(2)}) collective-permute-start(bf16[2,512,128]{2,1,0:T(8,128)(2,1)} %get-tuple-element.52), channel_id=1, source_target_pairs={{0,1},{1,0},{2,3},{3,2},{4,5},{5,4},{6,7},{7,6},{8,9},{9,8},{10,11... | collective-permute-start | bytes 786440 | tf_op jit(solution)/shard_map/ppermute | solution.py:332
  115.7 9.8 %copy-start.20 = (bf16[2,512,128]{2,1,0:T(8,128)(2,1)}, bf16[2,512,128]{2,1,0:T(8,128)(2,1)S(1)}, u32[]{:S(2)}) copy-start(bf16[2,512,128]{2,1,0:T(8,128)(2,1)S(1)} %collective-permute-done.16.refs_3_) | copy-start | bytes 786436
  115.7 17.7 %collective-permute-start.9 = (bf16[2,512,128]{2,1,0:T(8,128)(2,1)S(1)}, bf16[2,512,128]{2,1,0:T(8,128)(2,1)S(1)}, u32[]{:S(2)}, u32[]{:S(2)}) collective-permute-start(bf16[2,512,128]{2,1,0:T(8,128)(2,1)S(1)} %copy-done.15), channel_id=1, source_target_pairs={{0,5},{1,4},{2,7},{3,6},{4,1},{5,0},{6,3},{7,2},{8,13},{9,12},{10,... | collective-permute-start | bytes 786440 | tf_op jit(solution)/shard_map/ppermute | solution.py:332
  121.4 4.1 %copy-start.21 = (bf16[2,512,128]{2,1,0:T(8,128)(2,1)}, bf16[2,512,128]{2,1,0:T(8,128)(2,1)S(1)}, u32[]{:S(2)}) copy-start(bf16[2,512,128]{2,1,0:T(8,128)(2,1)S(1)} %collective-permute-done.17.refs_4_) | copy-start | bytes 786436
  121.4 12.0 %collective-permute-start.10 = (bf16[2,512,128]{2,1,0:T(8,128)(2,1)S(1)}, bf16[2,512,128]{2,1,0:T(8,128)(2,1)S(1)}, u32[]{:S(2)}, u32[]{:S(2)}) collective-permute-start(bf16[2,512,128]{2,1,0:T(8,128)(2,1)S(1)} %copy-done.14), channel_id=1, source_target_pairs={{0,4},{1,5},{2,6},{3,7},{4,0},{5,1},{6,2},{7,3},{8,12},{9,13},{10,... | collective-permute-start | bytes 786440 | tf_op jit(solution)/shard_map/ppermute | solution.py:332
  121.4 12.0 %collective-permute-start.11 = (bf16[2,512,128]{2,1,0:T(8,128)(2,1)S(1)}, bf16[2,512,128]{2,1,0:T(8,128)(2,1)S(1)}, u32[]{:S(2)}, u32[]{:S(2)}) collective-permute-start(bf16[2,512,128]{2,1,0:T(8,128)(2,1)S(1)} %copy-done.13), channel_id=1, source_target_pairs={{0,3},{1,2},{2,1},{3,0},{4,7},{5,6},{6,5},{7,4},{8,11},{9,10},{10,... | collective-permute-start | bytes 786440 | tf_op jit(solution)/shard_map/ppermute | solution.py:332
  124.9 11.0 %collective-permute-start.12 = (bf16[2,512,128]{2,1,0:T(8,128)(2,1)S(1)}, bf16[2,512,128]{2,1,0:T(8,128)(2,1)S(1)}, u32[]{:S(2)}, u32[]{:S(2)}) collective-permute-start(bf16[2,512,128]{2,1,0:T(8,128)(2,1)S(1)} %copy-done.12), channel_id=1, source_target_pairs={{0,2},{1,3},{2,0},{3,1},{4,6},{5,7},{6,4},{7,5},{8,10},{9,11},{10,... | collective-permute-start | bytes 786440 | tf_op jit(solution)/shard_map/ppermute | solution.py:332
  125.4 10.6 %collective-permute-start.13 = (bf16[2,512,128]{2,1,0:T(8,128)(2,1)S(1)}, bf16[2,512,128]{2,1,0:T(8,128)(2,1)S(1)}, u32[]{:S(2)}, u32[]{:S(2)}) collective-permute-start(bf16[2,512,128]{2,1,0:T(8,128)(2,1)S(1)} %copy-done.11), channel_id=1, source_target_pairs={{0,1},{1,0},{2,3},{3,2},{4,5},{5,4},{6,7},{7,6},{8,9},{9,8},{10,11... | collective-permute-start | bytes 786440 | tf_op jit(solution)/shard_map/ppermute | solution.py:332
  144.0 53.1 %copy-start = (bf16[32,2,128,128]{3,2,1,0:T(8,128)(2,1)}, bf16[32,2,128,128]{3,2,1,0:T(8,128)(2,1)S(1)}, u32[]{:S(2)}) copy-start(bf16[32,2,128,128]{3,2,1,0:T(8,128)(2,1)S(1)} %all-to-all-done.5) | copy-start | bytes 6291460
  197.0 7.5 %copy-start.10 = (bf16[2,512,128]{2,1,0:T(8,128)(2,1)S(1)}, bf16[2,512,128]{2,1,0:T(8,128)(2,1)}, u32[]{:S(2)}) copy-start(bf16[2,512,128]{2,1,0:T(8,128)(2,1)} %get-tuple-element.32) | copy-start | bytes 786436
  197.0 8.6 %copy-start.9 = (bf16[2,512,128]{2,1,0:T(8,128)(2,1)S(1)}, bf16[2,512,128]{2,1,0:T(8,128)(2,1)}, u32[]{:S(2)}) copy-start(bf16[2,512,128]{2,1,0:T(8,128)(2,1)} %get-tuple-element.33) | copy-start | bytes 786436
  197.0 9.2 %copy-start.8 = (bf16[2,512,128]{2,1,0:T(8,128)(2,1)S(1)}, bf16[2,512,128]{2,1,0:T(8,128)(2,1)}, u32[]{:S(2)}) copy-start(bf16[2,512,128]{2,1,0:T(8,128)(2,1)} %get-tuple-element.34) | copy-start | bytes 786436
  197.1 29.5 %copy-start.7 = (bf16[2,512,128]{2,1,0:T(8,128)(2,1)S(1)}, bf16[2,512,128]{2,1,0:T(8,128)(2,1)}, u32[]{:S(2)}) copy-start(bf16[2,512,128]{2,1,0:T(8,128)(2,1)} %get-tuple-element.35) | copy-start | bytes 786436
  197.1 42.1 %copy-start.6 = (bf16[2,512,128]{2,1,0:T(8,128)(2,1)S(1)}, bf16[2,512,128]{2,1,0:T(8,128)(2,1)}, u32[]{:S(2)}) copy-start(bf16[2,512,128]{2,1,0:T(8,128)(2,1)} %get-tuple-element.36) | copy-start | bytes 786436
  197.1 62.5 %all-to-all-start.4 = ((bf16[32,2,128,128]{3,2,1,0:T(8,128)(2,1)}), bf16[32,2,128,128]{3,2,1,0:T(8,128)(2,1)S(1)}, u32[]{:S(2)}, u32[]{:S(2)}) async-start(bf16[32,2,128,128]{3,2,1,0:T(8,128)(2,1)} %clean.5.refs_13_), calls=%async_computation.4 | async-start | bytes 4194304 | tf_op jit(solution)/shard_map/all_to_all | solution.py:326
  201.8 24.8 %collective-permute-start = (bf16[2,512,128]{2,1,0:T(8,128)(2,1)}, bf16[2,512,128]{2,1,0:T(8,128)(2,1)S(1)}, u32[]{:S(2)}, u32[]{:S(2)}) collective-permute-start(bf16[2,512,128]{2,1,0:T(8,128)(2,1)} %get-tuple-element.30), channel_id=1, source_target_pairs={{0,7},{1,6},{2,5},{3,4},{4,3},{5,2},{6,1},{7,0},{8,15},{9,14},{10,... | collective-permute-start | bytes 786440 | tf_op jit(solution)/shard_map/ppermute | solution.py:332
  204.0 35.2 %collective-permute-start.1 = (bf16[2,512,128]{2,1,0:T(8,128)(2,1)}, bf16[2,512,128]{2,1,0:T(8,128)(2,1)S(1)}, u32[]{:S(2)}, u32[]{:S(2)}) collective-permute-start(bf16[2,512,128]{2,1,0:T(8,128)(2,1)} %get-tuple-element.31), channel_id=1, source_target_pairs={{0,6},{1,7},{2,4},{3,5},{4,2},{5,3},{6,0},{7,1},{8,14},{9,15},{10,... | collective-permute-start | bytes 786440 | tf_op jit(solution)/shard_map/ppermute | solution.py:332
  204.5 36.5 %collective-permute-start.2 = (bf16[2,512,128]{2,1,0:T(8,128)(2,1)S(1)}, bf16[2,512,128]{2,1,0:T(8,128)(2,1)S(1)}, u32[]{:S(2)}, u32[]{:S(2)}) collective-permute-start(bf16[2,512,128]{2,1,0:T(8,128)(2,1)S(1)} %copy-done.10), channel_id=1, source_target_pairs={{0,5},{1,4},{2,7},{3,6},{4,1},{5,0},{6,3},{7,2},{8,13},{9,12},{10,... | collective-permute-start | bytes 786440 | tf_op jit(solution)/shard_map/ppermute | solution.py:332
  205.7 43.6 %collective-permute-start.3 = (bf16[2,512,128]{2,1,0:T(8,128)(2,1)S(1)}, bf16[2,512,128]{2,1,0:T(8,128)(2,1)S(1)}, u32[]{:S(2)}, u32[]{:S(2)}) collective-permute-start(bf16[2,512,128]{2,1,0:T(8,128)(2,1)S(1)} %copy-done.9), channel_id=1, source_target_pairs={{0,4},{1,5},{2,6},{3,7},{4,0},{5,1},{6,2},{7,3},{8,12},{9,13},{10,... | collective-permute-start | bytes 786440 | tf_op jit(solution)/shard_map/ppermute | solution.py:332
  206.2 43.0 %collective-permute-start.4 = (bf16[2,512,128]{2,1,0:T(8,128)(2,1)S(1)}, bf16[2,512,128]{2,1,0:T(8,128)(2,1)S(1)}, u32[]{:S(2)}, u32[]{:S(2)}) collective-permute-start(bf16[2,512,128]{2,1,0:T(8,128)(2,1)S(1)} %copy-done.8), channel_id=1, source_target_pairs={{0,3},{1,2},{2,1},{3,0},{4,7},{5,6},{6,5},{7,4},{8,11},{9,10},{10,... | collective-permute-start | bytes 786440 | tf_op jit(solution)/shard_map/ppermute | solution.py:332
  226.5 25.0 %copy-start.24 = (bf16[2,512,128]{2,1,0:T(8,128)(2,1)}, bf16[2,512,128]{2,1,0:T(8,128)(2,1)S(1)}, u32[]{:S(2)}) copy-start(bf16[2,512,128]{2,1,0:T(8,128)(2,1)S(1)} %collective-permute-done.refs_1_) | copy-start | bytes 786436
  226.5 24.9 %collective-permute-start.5 = (bf16[2,512,128]{2,1,0:T(8,128)(2,1)S(1)}, bf16[2,512,128]{2,1,0:T(8,128)(2,1)S(1)}, u32[]{:S(2)}, u32[]{:S(2)}) collective-permute-start(bf16[2,512,128]{2,1,0:T(8,128)(2,1)S(1)} %copy-done.7), channel_id=1, source_target_pairs={{0,2},{1,3},{2,0},{3,1},{4,6},{5,7},{6,4},{7,5},{8,10},{9,11},{10,... | collective-permute-start | bytes 786440 | tf_op jit(solution)/shard_map/ppermute | solution.py:332
  239.1 12.4 %copy-start.25 = (bf16[2,512,128]{2,1,0:T(8,128)(2,1)}, bf16[2,512,128]{2,1,0:T(8,128)(2,1)S(1)}, u32[]{:S(2)}) copy-start(bf16[2,512,128]{2,1,0:T(8,128)(2,1)S(1)} %collective-permute-done.1.refs_2_) | copy-start | bytes 786436
  239.1 12.4 %collective-permute-start.6 = (bf16[2,512,128]{2,1,0:T(8,128)(2,1)S(1)}, bf16[2,512,128]{2,1,0:T(8,128)(2,1)S(1)}, u32[]{:S(2)}, u32[]{:S(2)}) collective-permute-start(bf16[2,512,128]{2,1,0:T(8,128)(2,1)S(1)} %copy-done.6), channel_id=1, source_target_pairs={{0,1},{1,0},{2,3},{3,2},{4,5},{5,4},{6,7},{7,6},{8,9},{9,8},{10,11... | collective-permute-start | bytes 786440 | tf_op jit(solution)/shard_map/ppermute | solution.py:332
  241.1 10.4 %copy-start.27 = (bf16[2,512,128]{2,1,0:T(8,128)(2,1)}, bf16[2,512,128]{2,1,0:T(8,128)(2,1)S(1)}, u32[]{:S(2)}) copy-start(bf16[2,512,128]{2,1,0:T(8,128)(2,1)S(1)} %collective-permute-done.2.refs_3_) | copy-start | bytes 786436
  260.9 52.4 %all-to-all-start.2 = ((bf16[32,2,128,128]{3,2,1,0:T(8,128)(2,1)}), bf16[32,2,128,128]{3,2,1,0:T(8,128)(2,1)}, u32[]{:S(2)}, u32[]{:S(2)}) async-start(bf16[32,2,128,128]{3,2,1,0:T(8,128)(2,1)} %clean.7), calls=%async_computation.2 | async-start | bytes 4194304 | tf_op jit(solution)/shard_map/all_to_all | solution.py:326
  (15 other events, 24.4 us)

commit v12 on v11

--- a/solution.py
+++ b/solution.py
@@ -11,7 +11,7 @@
 
 LANES = 128
 RADIX = 8
-ROWS = 16
+EARLY = 6
 VMEM_BYTES = 56 * 1024 * 1024
 
 
@@ -29,8 +29,7 @@
 def twiddle_table(length):
     inner = length // RADIX
     phase = 2.0 * np.pi * np.outer(np.arange(RADIX), np.arange(inner)) / length
-    table = np.stack([np.cos(phase), np.sin(phase)], axis=1)
-    return np.repeat(table[:, :, None], ROWS, axis=2).astype(jnp.bfloat16)
+    return np.stack([np.cos(phase), np.sin(phase)], axis=1).astype(np.float32)
 
 
 def order_table():
@@ -90,24 +89,28 @@
         *out_refs, mid = refs
     rows, length = x_ref.shape[1:]
     inner = length // RADIX
-    for block in range(inner // LANES):
-        lanes = slice(block * LANES, (block + 1) * LANES)
-        other = slice(inner + block * LANES, inner + (block + 1) * LANES)
-        for i in range(rows // ROWS):
-            at = slice(i * ROWS, (i + 1) * ROWS)
+    step = 16
+    for i in range(rows // step):
+        at = slice(i * step, (i + 1) * step)
+        for block in range(inner // LANES):
             re, im = [], []
             for a in range(RADIX):
-                wide = slice(a * inner + block * LANES, a * inner + (block + 1) * LANES)
-                re.append(x_ref[0, at, wide])
-                im.append(x_ref[1, at, wide])
+                lanes = slice(a * inner + block * LANES, a * inner + (block + 1) * LANES)
+                re.append(x_ref[0, at, lanes].astype(jnp.float32))
+                im.append(x_ref[1, at, lanes].astype(jnp.float32))
             re, im = butterfly8(re, im)
-            mid[0, at, lanes] = re[0]
-            mid[0, at, other] = im[0]
-            for y_lo in range(1, RADIX):
-                cosine = twiddle_ref[y_lo, 0, :, lanes]
-                sine = twiddle_ref[y_lo, 1, :, lanes]
-                mid[y_lo, at, lanes] = re[y_lo] * cosine - im[y_lo] * sine
-                mid[y_lo, at, other] = re[y_lo] * sine + im[y_lo] * cosine
+            lanes = slice(block * LANES, (block + 1) * LANES)
+            other = slice(inner + block * LANES, inner + (block + 1) * LANES)
+            for y_lo in range(RADIX):
+                if y_lo == 0:
+                    tr, ti = re[0], im[0]
+                else:
+                    cosine = twiddle_ref[y_lo, 0:1, lanes]
+                    sine = twiddle_ref[y_lo, 1:2, lanes]
+                    tr = re[y_lo] * cosine - im[y_lo] * sine
+                    ti = re[y_lo] * sine + im[y_lo] * cosine
+                mid[y_lo, at, lanes] = tr.astype(jnp.bfloat16)
+                mid[y_lo, at, other] = ti.astype(jnp.bfloat16)
     for n, chunk in enumerate(chunks):
         for group in range(spread):
             column = (chunk * spread + group) * LANES
@@ -159,7 +162,7 @@
             grid=(rows // block,),
             in_specs=[
                 pl.BlockSpec((2, block, length), lambda i, at: (0, i, 0)),
-                pl.BlockSpec((RADIX, 2, ROWS, inner), lambda i, at: (0, 0, 0, 0)),
+                pl.BlockSpec((RADIX, 2, inner), lambda i, at: (0, 0, 0)),
                 pl.BlockSpec((2 * inner, 2 * inner), lambda i, at: (0, 0)),
             ],
             out_specs=[spec] * outs,
@@ -207,7 +210,7 @@
         front = (gain_ref[:, u : u + 1] * amps).astype(jnp.bfloat16)
         drop = jnp.dot(basis_ref[...], front, preferred_element_type=jnp.float32)
         slab[:, lanes] = (line.astype(jnp.float32) - drop).astype(jnp.bfloat16)
-    out_rows = out_ref.shape[2]
+    out_rows = out_ref.shape[3]
     tall = back_ref.shape[0]
     group = tall // rows_dev
     for b in range(chans // group):
@@ -220,15 +223,15 @@
             half = value[:, part * LANES : (part + 1) * LANES]
             if out_rows % tall == 0:
                 target, row = divmod(b * tall, out_rows)
-                out_ref[target, part, row : row + tall, :] = half.astype(jnp.bfloat16)
+                out_ref[target, 0, part, row : row + tall, :] = half.astype(jnp.bfloat16)
             else:
                 take = tall // out_rows
-                out_ref[b * take : (b + 1) * take, part] = half.reshape(
+                out_ref[b * take : (b + 1) * take, 0, part] = half.reshape(
                     take, out_rows, LANES
                 ).astype(jnp.bfloat16)
 
 
-def clean(at, xs, basis, basis_t, gain, targets, rows_dev, before):
+def clean(at, xs, basis, basis_t, gain, targets, rows_dev, slot, slots, before):
     split = len(xs) > 1
     chans = basis.shape[0]
     sources = len(xs) if split else xs[0].shape[0]
@@ -236,15 +239,16 @@
     swap = swap_table(min(256 // rows_dev, own), rows_dev)
     back = np.ascontiguousarray(swap_table(256 // rows_dev, rows_dev).T)
     vmem = pl.BlockSpec(memory_space=pltpu.VMEM)
+    out_rows = chans * rows_dev // targets
     return pl.pallas_call(
         functools.partial(clean_kernel, split, len(before)),
+        grid=(1,),
         in_specs=[pl.BlockSpec(memory_space=pltpu.SMEM)]
         + [vmem] * (len(xs) + 5)
         + [pl.BlockSpec(memory_space=pl.ANY)] * len(before),
-        out_specs=vmem,
-        out_shape=jax.ShapeDtypeStruct(
-            (targets, 2, chans * rows_dev // targets, LANES), jnp.bfloat16
-        ),
+        out_specs=pl.BlockSpec((targets, 1, 2, out_rows, LANES), lambda i: (0, slot, 0, 0, 0)),
+        out_shape=jax.ShapeDtypeStruct((targets, slots, 2, out_rows, LANES), jnp.bfloat16),
+        input_output_aliases={6 + len(xs): 0} if slot else {},
         scratch_shapes=[pltpu.VMEM((chans, rows_dev * 2 * LANES), jnp.bfloat16)],
         compiler_params=params(),
         cost_estimate=pl.CostEstimate(
@@ -258,10 +262,10 @@
 
 def image_kernel(scale, x_ref, table_ref, order_ref, *refs):
     out_ref = refs[-1]
-    z, _, parts, rows, _ = x_ref.shape
+    z, _, _, parts, rows, _ = x_ref.shape
     tiles = []
     for y_lo in range(RADIX):
-        tile = x_ref[:, y_lo]
+        tile = x_ref[:, y_lo, 0]
         if rows % 16:
             tile = tile.astype(jnp.float32)
         tile = tile.reshape(z * parts * rows, LANES).astype(jnp.bfloat16)
@@ -272,8 +276,8 @@
     out_ref[...] = value.astype(jnp.bfloat16).reshape(out_ref.shape)
 
 
-def image(x, chunk, count, rows_dev, held):
-    z, pieces, _, rows, _ = x.shape
+def image(x, slot, chunk, count, rows_dev, held):
+    z, pieces, _, _, rows, _ = x.shape
     chans = rows // rows_dev
     total = z * rows_dev
     spread = pieces // RADIX
@@ -286,7 +290,9 @@
         functools.partial(image_kernel, scale),
         grid=(chans // group, spread),
         in_specs=[
-            pl.BlockSpec((z, RADIX, 2, group * rows_dev, LANES), lambda c, g: (0, g, 0, c, 0)),
+            pl.BlockSpec(
+                (z, RADIX, 1, 2, group * rows_dev, LANES), lambda c, g: (0, g, slot, 0, c, 0)
+            ),
             pl.BlockSpec(table.shape, lambda c, g: (0, 0)),
             pl.BlockSpec(order.shape, lambda c, g: (0, 0)),
         ]
@@ -355,13 +361,18 @@
         cells += [
             scatter(sends[k * chan_count : (k + 1) * chan_count]) for k in range(count - 1)
         ]
-    held, before = [], cells[1][:1] if count > 1 else []
-    for k in range(count):
-        cleaned = clean(at, cells[k], basis, basis_t, gain, targets, rows_dev, before)
-        before = [cleaned]
+    groups = [[0]] + [g for g in (list(range(1, count - 1)), [count - 1]) if g and count > 1]
+    held, before = [], cells[1][1:EARLY] if count > 1 else []
+    for chunks in groups:
+        for slot, k in enumerate(chunks):
+            cleaned = clean(
+                at, cells[k], basis, basis_t, gain, targets, rows_dev, slot, len(chunks), before
+            )
+            before = [cleaned]
         planes = exchange(cleaned, ("uv", "chan"))
         planes = planes.reshape((uv_count, chan_count) + planes.shape[1:])
-        held = [image(planes, k, count, rows_dev, held)]
+        for slot, k in enumerate(chunks):
+            held = [image(planes, slot, k, count, rows_dev, held)]
     return held[0]
 
 

time: 324 us -> 312 us (0.963)
  blocking collectives: 53.1 us -> 0 us
  waiting for transfers between devices: 133 us -> 167 us
  starting transfers between devices: 40.1 us -> 45 us
    all_to_all x1 -> x0, blocking collectives: 53.1 us -> none  [exchange(): return lax.all_to_all(x, axes, split_axis=0, concat_axis=0, tiled=True)]
    ppermute x21, waiting for transfers between devices: 98 us -> 125 us  [scatter(): lax.ppermute(pieces[step], 'chan', [(j, int(partner(np.int32(j), step, co...]
    all_to_all x5, waiting for transfers between devices: 35.3 us -> 42.1 us  [exchange(): return lax.all_to_all(x, axes, split_axis=0, concat_axis=0, tiled=True)]
  transfers between devices with their start and end apart: 26 -> 26, of which waited for: 15 -> 15; matrix products, arithmetic and copies ran while one was open for 0% -> 0% of each run, Pallas kernels for 22% -> 24%
where the time goes in v12:
time: 312 us; the launch traced here: 308 us
  waiting for transfers between devices  167 us (54%)
  Pallas kernels  86.1 us (28%)
  starting transfers between devices  45 us (14%)
  local copies, waits for them, and re-layouts  8.73 us (3%)
    ppermute x21, waiting for transfers between devices, scatter(): lax.ppermute(pieces[step], 'chan', [(j, int(partner(np.int32(j), step, co...  125 us
    all_to_all x5, waiting for transfers between devices, exchange(): return lax.all_to_all(x, axes, split_axis=0, concat_axis=0, tiled=True)  42.1 us
    pallas_call x2, Pallas kernels, column_transform(): pl.pallas_call(functools.partial(column_kernel, chunks, pieces // RADIX,...  29.5 us
    pallas_call x4, Pallas kernels, clean(): pl.pallas_call(functools.partial(clean_kernel, split, len(before)), grid=...  28.8 us
    pallas_call x4, Pallas kernels, image(): pl.pallas_call(functools.partial(image_kernel, scale), grid=(chans // gro...  25.9 us
    all_to_all x5, starting transfers between devices, exchange(): return lax.all_to_all(x, axes, split_axis=0, concat_axis=0, tiled=True)  24.6 us
    ppermute x21, starting transfers between devices, scatter(): lax.ppermute(pieces[step], 'chan', [(j, int(partner(np.int32(j), step, co...  20.5 us
    unnamed x74, local copies, waits for them, and re-layouts  7.04 us
  transfers between devices with their start and end apart: 26, of which 15 were waited for; matrix products, arithmetic and copies ran while one was open for 0% of the time, Pallas kernels for 24%

profile of v12, /device:TPU:8, one launch (start us, length us, event | category | flops | bytes accessed | tf_op | source)
XLA Modules:
  0.0 307.8 jit_solution(17198105602329984946)
XLA Ops:
  0.0 1.7 broadcast_in_dim.2
  1.7 3.7 %all-to-all-start = ((bf16[8,64,512]{2,1,0:T(8,128)(2,1)}), bf16[8,64,512]{2,1,0:T(8,128)(2,1)S(1)}, u32[]{:S(2)}, u32[]{:S(2)}) async-start(bf16[8,64,512]{2,1,0:T(8,128)(2,1)} %broadcast_in_dim.2), calls=%async_computation | async-start | bytes 1048576 | tf_op jit(solution)/shard_map/all_to_all | solution.py:332
  5.4 11.9 %column_transform.3 = bf16[8,2,512,128]{3,2,1,0:T(8,128)(2,1)} custom-call(s32[1]{0:T(128)} %bitcast.at_ref, bf16[2,512,4096]{2,1,0:T(8,128)(2,1)} %bitcast.13, f32[8,2,512]{2,1,0:T(2,128)} %constant.16.clone.twiddle_ref, bf16[1024,1024]{1,0:T(8,128)(2,1)} %constant.17.clone.table_ref), custom_call_target="tpu_custom_call" | custom-call | flops 8589934592 | bytes 16777216 | tf_op jit(solution)/shard_map/column_transform/pallas_call | solution.py:158
  17.3 4.2 %all-to-all-start.1 = ((bf16[8,2,512,128]{3,2,1,0:T(8,128)(2,1)}), bf16[8,2,512,128]{3,2,1,0:T(8,128)(2,1)S(1)}, u32[]{:S(2)}, u32[]{:S(2)}) async-start(bf16[8,2,512,128]{3,2,1,0:T(8,128)(2,1)} %column_transform.3), calls=%async_computation.1 | async-start | bytes 4194304 | tf_op jit(solution)/shard_map/all_to_all | solution.py:332
  21.5 17.6 %column_transform.2 = (bf16[2,512,128]{2,1,0:T(8,128)(2,1)}, bf16[2,512,128]{2,1,0:T(8,128)(2,1)}, bf16[2,512,128]{2,1,0:T(8,128)(2,1)}, bf16[2,512,128]{2,1,0:T...) custom-call(s32[1]{0:T(128)} %bitcast.at_ref, ...), custom_call_target="tpu_custom_call" | custom-call | flops 25769803776 | bytes 16777216 | tf_op jit(solution)/shard_map/column_transform/pallas_call | solution.py:158
  39.1 2.7 collective-permute-start.14
  42.1 1.3 collective-permute-start.16
  43.9 1.4 collective-permute-start.18
  45.3 0.8 add_divide_fusion.refs_3_.refs_10_
  46.1 2.0 turn.1.refs_2_.refs_9_
  48.1 5.2 %collective-permute-done.14.refs_6_.refs_1_ = bf16[2,512,128]{2,1,0:T(8,128)(2,1)S(1)} collective-permute-done((bf16[2,512,128]{2,1,0:T(8,128)(2,1)}, bf16[2,512,128]{2,1,0:T(8,128)(2,1)S(1)}, u32[]{:S(2)}, u32[]{:S(2)}) %collective-permute-start.14) | collective-permute-done | bytes 262176 | tf_op jit(solution)/shard_map/ppermute | solution.py:338
  53.4 6.5 %collective-permute-done.15.refs_7_.refs_2_ = bf16[2,512,128]{2,1,0:T(8,128)(2,1)S(1)} collective-permute-done((bf16[2,512,128]{2,1,0:T(8,128)(2,1)}, bf16[2,512,128]{2,1,0:T(8,128)(2,1)S(1)}, u32[]{:S(2)}, u32[]{:S(2)}) %collective-permute-start.15) | collective-permute-done | bytes 262176 | tf_op jit(solution)/shard_map/ppermute | solution.py:338
  59.9 5.1 %collective-permute-done.16.refs_8_.refs_3_ = bf16[2,512,128]{2,1,0:T(8,128)(2,1)S(1)} collective-permute-done((bf16[2,512,128]{2,1,0:T(8,128)(2,1)}, bf16[2,512,128]{2,1,0:T(8,128)(2,1)S(1)}, u32[]{:S(2)}, u32[]{:S(2)}) %collective-permute-start.16) | collective-permute-done | bytes 262176 | tf_op jit(solution)/shard_map/ppermute | solution.py:338
  65.0 5.6 %collective-permute-done.17.refs_9_.refs_4_ = bf16[2,512,128]{2,1,0:T(8,128)(2,1)S(1)} collective-permute-done((bf16[2,512,128]{2,1,0:T(8,128)(2,1)}, bf16[2,512,128]{2,1,0:T(8,128)(2,1)S(1)}, u32[]{:S(2)}, u32[]{:S(2)}) %collective-permute-start.17) | collective-permute-done | bytes 262176 | tf_op jit(solution)/shard_map/ppermute | solution.py:338
  71.4 1.3 copy-done.3
  72.7 7.1 %clean.4.refs_13_ = bf16[32,1,2,128,128]{4,3,2,1,0:T(8,128)(2,1)} custom-call(s32[1]{0:T(128)} %bitcast.at_ref, bf16[8,2,512,128]{3,2,1,0:T(8,128)(2,1)} %copy-done.3, bf16[512,512]{1,0:T(8,128)(2,1)} %bitcast.9, bf16[512,512]{1,0:T(8,128)(2,1)} %turn.1.refs_2_.refs_9_, f32[512,8]{1,0:T(8,128)} %add_divide_fusion.refs_3_.refs_10_, ...), custom_call_target="tpu_custom_call" | custom-call | flops 3221225472 | bytes 4194304 | tf_op jit(solution)/shard_map/clean/pallas_call | solution.py:243
  79.8 4.2 %all-to-all-start.4 = ((bf16[32,1,2,128,128]{4,3,2,1,0:T(8,128)(2,1)}), bf16[32,1,2,128,128]{4,3,2,1,0:T(8,128)(2,1)S(1)}, u32[]{:S(2)}, u32[]{:S(2)}) async-start(bf16[32,1,2,128,128]{4,3,2,1,0:T(8,128)(2,1)} %clean.4.refs_13_), calls=%async_computation.4 | async-start | bytes 4194304 | tf_op jit(solution)/shard_map/all_to_all | solution.py:332
  84.0 2.2 collective-permute-start.7
  86.8 1.5 collective-permute-start.19
  88.2 1.6 collective-permute-start.9
  89.8 19.0 %collective-permute-done.7.refs_1_ = bf16[2,512,128]{2,1,0:T(8,128)(2,1)S(1)} collective-permute-done((bf16[2,512,128]{2,1,0:T(8,128)(2,1)}, bf16[2,512,128]{2,1,0:T(8,128)(2,1)S(1)}, u32[]{:S(2)}, u32[]{:S(2)}) %collective-permute-start.7) | collective-permute-done | bytes 262176 | tf_op jit(solution)/shard_map/ppermute | solution.py:338
  108.8 1.7 collective-permute-start.10
  110.5 10.9 %collective-permute-done.8.refs_2_ = bf16[2,512,128]{2,1,0:T(8,128)(2,1)S(1)} collective-permute-done((bf16[2,512,128]{2,1,0:T(8,128)(2,1)}, bf16[2,512,128]{2,1,0:T(8,128)(2,1)S(1)}, u32[]{:S(2)}, u32[]{:S(2)}) %collective-permute-start.8) | collective-permute-done | bytes 262176 | tf_op jit(solution)/shard_map/ppermute | solution.py:338
  121.4 4.4 %collective-permute-done.19.refs_6_ = bf16[2,512,128]{2,1,0:T(8,128)(2,1)S(1)} collective-permute-done((bf16[2,512,128]{2,1,0:T(8,128)(2,1)}, bf16[2,512,128]{2,1,0:T(8,128)(2,1)S(1)}, u32[]{:S(2)}, u32[]{:S(2)}) %collective-permute-start.19) | collective-permute-done | bytes 262176 | tf_op jit(solution)/shard_map/ppermute | solution.py:338
  125.8 1.0 collective-permute-start.12
  127.5 7.2 %clean.5.refs_13_ = bf16[32,2,2,128,128]{4,3,2,1,0:T(8,128)(2,1)} custom-call(s32[1]{0:T(128)} %bitcast.at_ref, bf16[2,512,128]{2,1,0:T(8,128)(2,1)} %get-tuple-element.45.refs_0_, bf16[2,512,128]{2,1,0:T(8,128)(2,1)} %copy-done.23, bf16[2,512,128]{2,1,0:T(8,128)(2,1)} %copy-done.24, bf16[2,512,128]{2,1,0:T(8,128)(2,1)} %copy-done.25, ...), custom_call_target="tpu_custom_call" | custom-call | flops 3221225472 | bytes 4194304 | tf_op jit(solution)/shard_map/clean/pallas_call | solution.py:243
  134.8 4.6 %collective-permute-done.12.refs_6_ = bf16[2,512,128]{2,1,0:T(8,128)(2,1)S(1)} collective-permute-done((bf16[2,512,128]{2,1,0:T(8,128)(2,1)S(1)}, bf16[2,512,128]{2,1,0:T(8,128)(2,1)S(1)}, u32[]{:S(2)}, u32[]{:S(2)}) %collective-permute-start.12) | collective-permute-done | bytes 262176 | tf_op jit(solution)/shard_map/ppermute | solution.py:338
  139.4 0.7 copy-done.9
  140.1 7.2 %clean.6.refs_13_ = bf16[32,2,2,128,128]{4,3,2,1,0:T(8,128)(2,1)} custom-call(s32[1]{0:T(128)} %bitcast.at_ref, bf16[2,512,128]{2,1,0:T(8,128)(2,1)} %get-tuple-element.37.refs_0_, bf16[2,512,128]{2,1,0:T(8,128)(2,1)} %copy-done.4, bf16[2,512,128]{2,1,0:T(8,128)(2,1)} %copy-done.5, bf16[2,512,128]{2,1,0:T(8,128)(2,1)} %copy-done.6, ...), custom_call_target="tpu_custom_call", output_to_operand_aliasing={{}: (14, {})} | custom-call | flops 3221225472 | bytes 4194304 | tf_op jit(solution)/shard_map/clean/pallas_call | solution.py:243
  147.4 1.4 copy-done
  148.8 5.7 %all-to-all-start.3 = ((bf16[32,2,2,128,128]{4,3,2,1,0:T(8,128)(2,1)}), bf16[32,2,2,128,128]{4,3,2,1,0:T(8,128)(2,1)}, u32[]{:S(2)}, u32[]{:S(2)}) async-start(bf16[32,2,2,128,128]{4,3,2,1,0:T(8,128)(2,1)} %clean.6.refs_13_), calls=%async_computation.3 | async-start | bytes 8388608 | tf_op jit(solution)/shard_map/all_to_all | solution.py:332
  154.5 2.2 collective-permute-start
  157.2 1.1 collective-permute-start.2
  158.9 1.2 collective-permute-start.4
  160.2 31.2 %collective-permute-done.refs_1_ = bf16[2,512,128]{2,1,0:T(8,128)(2,1)S(1)} collective-permute-done((bf16[2,512,128]{2,1,0:T(8,128)(2,1)}, bf16[2,512,128]{2,1,0:T(8,128)(2,1)S(1)}, u32[]{:S(2)}, u32[]{:S(2)}) %collective-permute-start) | collective-permute-done | bytes 262176 | tf_op jit(solution)/shard_map/ppermute | solution.py:338
  191.4 20.0 %collective-permute-done.1.refs_2_ = bf16[2,512,128]{2,1,0:T(8,128)(2,1)S(1)} collective-permute-done((bf16[2,512,128]{2,1,0:T(8,128)(2,1)}, bf16[2,512,128]{2,1,0:T(8,128)(2,1)S(1)}, u32[]{:S(2)}, u32[]{:S(2)}) %collective-permute-start.1) | collective-permute-done | bytes 262176 | tf_op jit(solution)/shard_map/ppermute | solution.py:338
  211.4 4.0 %collective-permute-done.3.refs_4_ = bf16[2,512,128]{2,1,0:T(8,128)(2,1)S(1)} collective-permute-done((bf16[2,512,128]{2,1,0:T(8,128)(2,1)S(1)}, bf16[2,512,128]{2,1,0:T(8,128)(2,1)S(1)}, u32[]{:S(2)}, u32[]{:S(2)}) %collective-permute-start.3) | collective-permute-done | bytes 262176 | tf_op jit(solution)/shard_map/ppermute | solution.py:338
  215.4 2.1 collective-permute-done.4.refs_5_
  217.5 6.1 %collective-permute-done.5.refs_6_ = bf16[2,512,128]{2,1,0:T(8,128)(2,1)S(1)} collective-permute-done((bf16[2,512,128]{2,1,0:T(8,128)(2,1)S(1)}, bf16[2,512,128]{2,1,0:T(8,128)(2,1)S(1)}, u32[]{:S(2)}, u32[]{:S(2)}) %collective-permute-start.5) | collective-permute-done | bytes 262176 | tf_op jit(solution)/shard_map/ppermute | solution.py:338
  224.4 7.3 %clean.7 = bf16[32,1,2,128,128]{4,3,2,1,0:T(8,128)(2,1)} custom-call(s32[1]{0:T(128)} %bitcast.at_ref, bf16[2,512,128]{2,1,0:T(8,128)(2,1)} %get-tuple-element.29.refs_0_, bf16[2,512,128]{2,1,0:T(8,128)(2,1)} %copy-done.28, bf16[2,512,128]{2,1,0:T(8,128)(2,1)} %copy-done.29, bf16[2,512,128]{2,1,0:T(8,128)(2,1)} %copy-done.30, ...), custom_call_target="tpu_custom_call" | custom-call | flops 3221225472 | bytes 4194304 | tf_op jit(solution)/shard_map/clean/pallas_call | solution.py:243
  231.7 14.9 %all-to-all-done.3 = bf16[32,2,2,128,128]{4,3,2,1,0:T(8,128)(2,1)} async-done(((bf16[32,2,2,128,128]{4,3,2,1,0:T(8,128)(2,1)}), bf16[32,2,2,128,128]{4,3,2,1,0:T(8,128)(2,1)}, u32[]{:S(2)}, u32[]{:S(2)}) %all-to-all-start.3) | async-done | bytes 4194336 | tf_op jit(solution)/shard_map/all_to_all | solution.py:332
  246.6 6.8 %all-to-all-start.2 = ((bf16[32,1,2,128,128]{4,3,2,1,0:T(8,128)(2,1)}), bf16[32,1,2,128,128]{4,3,2,1,0:T(8,128)(2,1)S(1)}, u32[]{:S(2)}, u32[]{:S(2)}) async-start(bf16[32,1,2,128,128]{4,3,2,1,0:T(8,128)(2,1)} %clean.7), calls=%async_computation.2 | async-start | bytes 4194304 | tf_op jit(solution)/shard_map/all_to_all | solution.py:332
  253.4 6.5 %image.4.refs_0_ = bf16[2,16,32,4096]{3,2,1,0:T(8,128)(2,1)} custom-call(bf16[4,8,1,2,128,128]{5,4,3,2,1,0:T(8,128)(2,1)} %bitcast.6, bf16[256,256]{1,0:T(8,128)(2,1)} %constant.20.clone.table_ref, bf16[1024,1024]{1,0:T(8,128)(2,1)} %constant.21.clone.order_ref), custom_call_target="tpu_custom_call" | custom-call | flops 2147483648 | bytes 4194304 | tf_op jit(solution)/shard_map/image/pallas_call | solution.py:289
  259.9 6.5 %image.5.refs_0_ = bf16[2,16,32,4096]{3,2,1,0:T(8,128)(2,1)} custom-call(bf16[4,8,2,2,128,128]{5,4,3,2,1,0:T(8,128)(2,1)} %bitcast.4.x_ref, bf16[256,256]{1,0:T(8,128)(2,1)} %constant.20.clone.table_ref, bf16[1024,1024]{1,0:T(8,128)(2,1)} %constant.21.clone.order_ref, bf16[2,16,32,4096]{3,2,1,0:T(8,128)(2,1)} %image.4.refs_0_), custom_call_target="tpu_custom_call", output_to_operand_aliasing={{}: (3, {})} | custom-call | flops 2147483648 | bytes 4194304 | tf_op jit(solution)/shard_map/image/pallas_call | solution.py:289
  266.3 6.5 %image.6.refs_0_ = bf16[2,16,32,4096]{3,2,1,0:T(8,128)(2,1)} custom-call(bf16[4,8,2,2,128,128]{5,4,3,2,1,0:T(8,128)(2,1)} %bitcast.4.x_ref, bf16[256,256]{1,0:T(8,128)(2,1)} %constant.20.clone.table_ref, bf16[1024,1024]{1,0:T(8,128)(2,1)} %constant.21.clone.order_ref, bf16[2,16,32,4096]{3,2,1,0:T(8,128)(2,1)} %image.5.refs_0_), custom_call_target="tpu_custom_call", output_to_operand_aliasing={{}: (3, {})} | custom-call | flops 2147483648 | bytes 4194304 | tf_op jit(solution)/shard_map/image/pallas_call | solution.py:289
  272.8 27.2 %all-to-all-done.2 = bf16[32,1,2,128,128]{4,3,2,1,0:T(8,128)(2,1)S(1)} async-done(((bf16[32,1,2,128,128]{4,3,2,1,0:T(8,128)(2,1)}), bf16[32,1,2,128,128]{4,3,2,1,0:T(8,128)(2,1)S(1)}, u32[]{:S(2)}, u32[]{:S(2)}) %all-to-all-start.2) | async-done | bytes 2097184 | tf_op jit(solution)/shard_map/all_to_all | solution.py:332
  300.0 1.3 copy-done.1
  301.4 6.4 %image.7 = bf16[2,16,32,4096]{3,2,1,0:T(8,128)(2,1)} custom-call(bf16[4,8,1,2,128,128]{5,4,3,2,1,0:T(8,128)(2,1)} %bitcast.7, bf16[256,256]{1,0:T(8,128)(2,1)} %constant.20.clone.table_ref, bf16[1024,1024]{1,0:T(8,128)(2,1)} %constant.21.clone.order_ref, bf16[2,16,32,4096]{3,2,1,0:T(8,128)(2,1)} %image.6.refs_0_), custom_call_target="tpu_custom_call", output_to_operand_aliasing={{}: (3, {})} | custom-call | flops 2147483648 | bytes 4194304 | tf_op jit(solution)/shard_map/image/pallas_call | solution.py:289
  (91 shorter events, 4.8 us)
Async XLA Ops:
  1.7 15.6 %all-to-all-start = ((bf16[8,64,512]{2,1,0:T(8,128)(2,1)}), bf16[8,64,512]{2,1,0:T(8,128)(2,1)S(1)}, u32[]{:S(2)}, u32[]{:S(2)}) async-start(bf16[8,64,512]{2,1,0:T(8,128)(2,1)} %broadcast_in_dim.2), calls=%async_computation | async-start | bytes 1048576 | tf_op jit(solution)/shard_map/all_to_all | solution.py:332
  17.3 21.8 %copy-start.2 = (bf16[8,64,512]{2,1,0:T(8,128)(2,1)}, bf16[8,64,512]{2,1,0:T(8,128)(2,1)S(1)}, u32[]{:S(2)}) copy-start(bf16[8,64,512]{2,1,0:T(8,128)(2,1)S(1)} %all-to-all-done) | copy-start | bytes 1572868
  17.3 53.3 %all-to-all-start.1 = ((bf16[8,2,512,128]{3,2,1,0:T(8,128)(2,1)}), bf16[8,2,512,128]{3,2,1,0:T(8,128)(2,1)S(1)}, u32[]{:S(2)}, u32[]{:S(2)}) async-start(bf16[8,2,512,128]{3,2,1,0:T(8,128)(2,1)} %column_transform.3), calls=%async_computation.1 | async-start | bytes 4194304 | tf_op jit(solution)/shard_map/all_to_all | solution.py:332
  21.5 23.8 %copy-start.11 = (f32[512]{0:T(512)S(1)}, f32[512]{0:T(512)}, u32[]{:S(2)}) copy-start(f32[512]{0:T(512)} %param.26) | copy-start | bytes 6148
  21.5 23.8 %copy-start.12 = (f32[8]{0:T(128)S(1)}, f32[8]{0:T(128)}, u32[]{:S(2)}) copy-start(f32[8]{0:T(128)} %param.27) | copy-start | bytes 100
  39.1 14.3 %collective-permute-start.14 = (bf16[2,512,128]{2,1,0:T(8,128)(2,1)}, bf16[2,512,128]{2,1,0:T(8,128)(2,1)S(1)}, u32[]{:S(2)}, u32[]{:S(2)}) collective-permute-start(bf16[2,512,128]{2,1,0:T(8,128)(2,1)} %get-tuple-element.46), channel_id=1, source_target_pairs={{0,7},{1,6},{2,5},{3,4},{4,3},{5,2},{6,1},{7,0},{8,15},{9,14},{10,... | collective-permute-start | bytes 786440 | tf_op jit(solution)/shard_map/ppermute | solution.py:338
  41.8 18.0 %collective-permute-start.15 = (bf16[2,512,128]{2,1,0:T(8,128)(2,1)}, bf16[2,512,128]{2,1,0:T(8,128)(2,1)S(1)}, u32[]{:S(2)}, u32[]{:S(2)}) collective-permute-start(bf16[2,512,128]{2,1,0:T(8,128)(2,1)} %get-tuple-element.47), channel_id=1, source_target_pairs={{0,6},{1,7},{2,4},{3,5},{4,2},{5,3},{6,0},{7,1},{8,14},{9,15},{10,... | collective-permute-start | bytes 786440 | tf_op jit(solution)/shard_map/ppermute | solution.py:338
  42.1 22.8 %collective-permute-start.16 = (bf16[2,512,128]{2,1,0:T(8,128)(2,1)}, bf16[2,512,128]{2,1,0:T(8,128)(2,1)S(1)}, u32[]{:S(2)}, u32[]{:S(2)}) collective-permute-start(bf16[2,512,128]{2,1,0:T(8,128)(2,1)} %get-tuple-element.48), channel_id=1, source_target_pairs={{0,5},{1,4},{2,7},{3,6},{4,1},{5,0},{6,3},{7,2},{8,13},{9,12},{10,... | collective-permute-start | bytes 786440 | tf_op jit(solution)/shard_map/ppermute | solution.py:338
  43.5 27.1 %collective-permute-start.17 = (bf16[2,512,128]{2,1,0:T(8,128)(2,1)}, bf16[2,512,128]{2,1,0:T(8,128)(2,1)S(1)}, u32[]{:S(2)}, u32[]{:S(2)}) collective-permute-start(bf16[2,512,128]{2,1,0:T(8,128)(2,1)} %get-tuple-element.49), channel_id=1, source_target_pairs={{0,4},{1,5},{2,6},{3,7},{4,0},{5,1},{6,2},{7,3},{8,12},{9,13},{10,... | collective-permute-start | bytes 786440 | tf_op jit(solution)/shard_map/ppermute | solution.py:338
  43.9 26.7 %collective-permute-start.18 = (bf16[2,512,128]{2,1,0:T(8,128)(2,1)}, bf16[2,512,128]{2,1,0:T(8,128)(2,1)S(1)}, u32[]{:S(2)}, u32[]{:S(2)}) collective-permute-start(bf16[2,512,128]{2,1,0:T(8,128)(2,1)} %get-tuple-element.50), channel_id=1, source_target_pairs={{0,3},{1,2},{2,1},{3,0},{4,7},{5,6},{6,5},{7,4},{8,11},{9,10},{10,... | collective-permute-start | bytes 786440 | tf_op jit(solution)/shard_map/ppermute | solution.py:338
  53.4 17.2 %copy-start.23 = (bf16[2,512,128]{2,1,0:T(8,128)(2,1)}, bf16[2,512,128]{2,1,0:T(8,128)(2,1)S(1)}, u32[]{:S(2)}) copy-start(bf16[2,512,128]{2,1,0:T(8,128)(2,1)S(1)} %collective-permute-done.14.refs_6_.refs_1_) | copy-start | bytes 786436
  59.9 10.7 %copy-start.24 = (bf16[2,512,128]{2,1,0:T(8,128)(2,1)}, bf16[2,512,128]{2,1,0:T(8,128)(2,1)S(1)}, u32[]{:S(2)}) copy-start(bf16[2,512,128]{2,1,0:T(8,128)(2,1)S(1)} %collective-permute-done.15.refs_7_.refs_2_) | copy-start | bytes 786436
  79.8 8.4 %copy-start.22 = (bf16[2,512,128]{2,1,0:T(8,128)(2,1)S(1)}, bf16[2,512,128]{2,1,0:T(8,128)(2,1)}, u32[]{:S(2)}) copy-start(bf16[2,512,128]{2,1,0:T(8,128)(2,1)} %get-tuple-element.40) | copy-start | bytes 786436
  79.8 29.0 %copy-start.21 = (bf16[2,512,128]{2,1,0:T(8,128)(2,1)S(1)}, bf16[2,512,128]{2,1,0:T(8,128)(2,1)}, u32[]{:S(2)}) copy-start(bf16[2,512,128]{2,1,0:T(8,128)(2,1)} %get-tuple-element.41) | copy-start | bytes 786436
  79.8 41.6 %copy-start.20 = (bf16[2,512,128]{2,1,0:T(8,128)(2,1)S(1)}, bf16[2,512,128]{2,1,0:T(8,128)(2,1)}, u32[]{:S(2)}) copy-start(bf16[2,512,128]{2,1,0:T(8,128)(2,1)} %get-tuple-element.42) | copy-start | bytes 786436
  79.8 46.0 %copy-start.19 = (bf16[2,512,128]{2,1,0:T(8,128)(2,1)S(1)}, bf16[2,512,128]{2,1,0:T(8,128)(2,1)}, u32[]{:S(2)}) copy-start(bf16[2,512,128]{2,1,0:T(8,128)(2,1)} %get-tuple-element.43) | copy-start | bytes 786436
  79.8 47.0 %copy-start.18 = (bf16[2,512,128]{2,1,0:T(8,128)(2,1)S(1)}, bf16[2,512,128]{2,1,0:T(8,128)(2,1)}, u32[]{:S(2)}) copy-start(bf16[2,512,128]{2,1,0:T(8,128)(2,1)} %get-tuple-element.44) | copy-start | bytes 786436
  79.8 67.6 %all-to-all-start.4 = ((bf16[32,1,2,128,128]{4,3,2,1,0:T(8,128)(2,1)}), bf16[32,1,2,128,128]{4,3,2,1,0:T(8,128)(2,1)S(1)}, u32[]{:S(2)}, u32[]{:S(2)}) async-start(bf16[32,1,2,128,128]{4,3,2,1,0:T(8,128)(2,1)} %clean.4.refs_13_), calls=%async_computation.4 | async-start | bytes 4194304 | tf_op jit(solution)/shard_map/all_to_all | solution.py:332
  84.0 24.8 %collective-permute-start.7 = (bf16[2,512,128]{2,1,0:T(8,128)(2,1)}, bf16[2,512,128]{2,1,0:T(8,128)(2,1)S(1)}, u32[]{:S(2)}, u32[]{:S(2)}) collective-permute-start(bf16[2,512,128]{2,1,0:T(8,128)(2,1)} %get-tuple-element.38), channel_id=1, source_target_pairs={{0,7},{1,6},{2,5},{3,4},{4,3},{5,2},{6,1},{7,0},{8,15},{9,14},{10,... | collective-permute-start | bytes 786440 | tf_op jit(solution)/shard_map/ppermute | solution.py:338
  86.2 35.2 %collective-permute-start.8 = (bf16[2,512,128]{2,1,0:T(8,128)(2,1)}, bf16[2,512,128]{2,1,0:T(8,128)(2,1)S(1)}, u32[]{:S(2)}, u32[]{:S(2)}) collective-permute-start(bf16[2,512,128]{2,1,0:T(8,128)(2,1)} %get-tuple-element.39), channel_id=1, source_target_pairs={{0,6},{1,7},{2,4},{3,5},{4,2},{5,3},{6,0},{7,1},{8,14},{9,15},{10,... | collective-permute-start | bytes 786440 | tf_op jit(solution)/shard_map/ppermute | solution.py:338
  86.8 39.0 %collective-permute-start.19 = (bf16[2,512,128]{2,1,0:T(8,128)(2,1)}, bf16[2,512,128]{2,1,0:T(8,128)(2,1)S(1)}, u32[]{:S(2)}, u32[]{:S(2)}) collective-permute-start(bf16[2,512,128]{2,1,0:T(8,128)(2,1)} %get-tuple-element.51), channel_id=1, source_target_pairs={{0,2},{1,3},{2,0},{3,1},{4,6},{5,7},{6,4},{7,5},{8,10},{9,11},{10,... | collective-permute-start | bytes 786440 | tf_op jit(solution)/shard_map/ppermute | solution.py:338
  88.2 38.6 %collective-permute-start.20 = (bf16[2,512,128]{2,1,0:T(8,128)(2,1)}, bf16[2,512,128]{2,1,0:T(8,128)(2,1)S(1)}, u32[]{:S(2)}, u32[]{:S(2)}) collective-permute-start(bf16[2,512,128]{2,1,0:T(8,128)(2,1)} %get-tuple-element.52), channel_id=1, source_target_pairs={{0,1},{1,0},{2,3},{3,2},{4,5},{5,4},{6,7},{7,6},{8,9},{9,8},{10,11... | collective-permute-start | bytes 786440 | tf_op jit(solution)/shard_map/ppermute | solution.py:338
  88.2 46.5 %collective-permute-start.9 = (bf16[2,512,128]{2,1,0:T(8,128)(2,1)S(1)}, bf16[2,512,128]{2,1,0:T(8,128)(2,1)S(1)}, u32[]{:S(2)}, u32[]{:S(2)}) collective-permute-start(bf16[2,512,128]{2,1,0:T(8,128)(2,1)S(1)} %copy-done.22), channel_id=1, source_target_pairs={{0,5},{1,4},{2,7},{3,6},{4,1},{5,0},{6,3},{7,2},{8,13},{9,12},{10,... | collective-permute-start | bytes 786440 | tf_op jit(solution)/shard_map/ppermute | solution.py:338
  108.8 25.9 %copy-start.4 = (bf16[2,512,128]{2,1,0:T(8,128)(2,1)}, bf16[2,512,128]{2,1,0:T(8,128)(2,1)S(1)}, u32[]{:S(2)}) copy-start(bf16[2,512,128]{2,1,0:T(8,128)(2,1)S(1)} %collective-permute-done.7.refs_1_) | copy-start | bytes 786436
  108.8 26.0 %collective-permute-start.10 = (bf16[2,512,128]{2,1,0:T(8,128)(2,1)S(1)}, bf16[2,512,128]{2,1,0:T(8,128)(2,1)S(1)}, u32[]{:S(2)}, u32[]{:S(2)}) collective-permute-start(bf16[2,512,128]{2,1,0:T(8,128)(2,1)S(1)} %copy-done.21), channel_id=1, source_target_pairs={{0,4},{1,5},{2,6},{3,7},{4,0},{5,1},{6,2},{7,3},{8,12},{9,13},{10,... | collective-permute-start | bytes 786440 | tf_op jit(solution)/shard_map/ppermute | solution.py:338
  121.4 13.3 %copy-start.5 = (bf16[2,512,128]{2,1,0:T(8,128)(2,1)}, bf16[2,512,128]{2,1,0:T(8,128)(2,1)S(1)}, u32[]{:S(2)}) copy-start(bf16[2,512,128]{2,1,0:T(8,128)(2,1)S(1)} %collective-permute-done.8.refs_2_) | copy-start | bytes 786436
  121.4 13.4 %collective-permute-start.11 = (bf16[2,512,128]{2,1,0:T(8,128)(2,1)S(1)}, bf16[2,512,128]{2,1,0:T(8,128)(2,1)S(1)}, u32[]{:S(2)}, u32[]{:S(2)}) collective-permute-start(bf16[2,512,128]{2,1,0:T(8,128)(2,1)S(1)} %copy-done.20), channel_id=1, source_target_pairs={{0,3},{1,2},{2,1},{3,0},{4,7},{5,6},{6,5},{7,4},{8,11},{9,10},{10,... | collective-permute-start | bytes 786440 | tf_op jit(solution)/shard_map/ppermute | solution.py:338
  125.8 13.6 %collective-permute-start.12 = (bf16[2,512,128]{2,1,0:T(8,128)(2,1)S(1)}, bf16[2,512,128]{2,1,0:T(8,128)(2,1)S(1)}, u32[]{:S(2)}, u32[]{:S(2)}) collective-permute-start(bf16[2,512,128]{2,1,0:T(8,128)(2,1)S(1)} %copy-done.19), channel_id=1, source_target_pairs={{0,2},{1,3},{2,0},{3,1},{4,6},{5,7},{6,4},{7,5},{8,10},{9,11},{10,... | collective-permute-start | bytes 786440 | tf_op jit(solution)/shard_map/ppermute | solution.py:338
  126.8 12.6 %collective-permute-start.13 = (bf16[2,512,128]{2,1,0:T(8,128)(2,1)S(1)}, bf16[2,512,128]{2,1,0:T(8,128)(2,1)S(1)}, u32[]{:S(2)}, u32[]{:S(2)}) collective-permute-start(bf16[2,512,128]{2,1,0:T(8,128)(2,1)S(1)} %copy-done.18), channel_id=1, source_target_pairs={{0,1},{1,0},{2,3},{3,2},{4,5},{5,4},{6,7},{7,6},{8,9},{9,8},{10,11... | collective-permute-start | bytes 786440 | tf_op jit(solution)/shard_map/ppermute | solution.py:338
  147.4 9.9 %copy-start.17 = (bf16[2,512,128]{2,1,0:T(8,128)(2,1)S(1)}, bf16[2,512,128]{2,1,0:T(8,128)(2,1)}, u32[]{:S(2)}) copy-start(bf16[2,512,128]{2,1,0:T(8,128)(2,1)} %get-tuple-element.32) | copy-start | bytes 786436
  147.4 11.0 %copy-start.16 = (bf16[2,512,128]{2,1,0:T(8,128)(2,1)S(1)}, bf16[2,512,128]{2,1,0:T(8,128)(2,1)}, u32[]{:S(2)}) copy-start(bf16[2,512,128]{2,1,0:T(8,128)(2,1)} %get-tuple-element.33) | copy-start | bytes 786436
  147.4 11.6 %copy-start.15 = (bf16[2,512,128]{2,1,0:T(8,128)(2,1)S(1)}, bf16[2,512,128]{2,1,0:T(8,128)(2,1)}, u32[]{:S(2)}) copy-start(bf16[2,512,128]{2,1,0:T(8,128)(2,1)} %get-tuple-element.34) | copy-start | bytes 786436
  147.4 44.0 %copy-start.14 = (bf16[2,512,128]{2,1,0:T(8,128)(2,1)S(1)}, bf16[2,512,128]{2,1,0:T(8,128)(2,1)}, u32[]{:S(2)}) copy-start(bf16[2,512,128]{2,1,0:T(8,128)(2,1)} %get-tuple-element.35) | copy-start | bytes 786436
  147.4 64.0 %copy-start.13 = (bf16[2,512,128]{2,1,0:T(8,128)(2,1)S(1)}, bf16[2,512,128]{2,1,0:T(8,128)(2,1)}, u32[]{:S(2)}) copy-start(bf16[2,512,128]{2,1,0:T(8,128)(2,1)} %get-tuple-element.36) | copy-start | bytes 786436
  148.8 97.8 %all-to-all-start.3 = ((bf16[32,2,2,128,128]{4,3,2,1,0:T(8,128)(2,1)}), bf16[32,2,2,128,128]{4,3,2,1,0:T(8,128)(2,1)}, u32[]{:S(2)}, u32[]{:S(2)}) async-start(bf16[32,2,2,128,128]{4,3,2,1,0:T(8,128)(2,1)} %clean.6.refs_13_), calls=%async_computation.3 | async-start | bytes 8388608 | tf_op jit(solution)/shard_map/all_to_all | solution.py:332
  154.5 36.9 %collective-permute-start = (bf16[2,512,128]{2,1,0:T(8,128)(2,1)}, bf16[2,512,128]{2,1,0:T(8,128)(2,1)S(1)}, u32[]{:S(2)}, u32[]{:S(2)}) collective-permute-start(bf16[2,512,128]{2,1,0:T(8,128)(2,1)} %get-tuple-element.30), channel_id=1, source_target_pairs={{0,7},{1,6},{2,5},{3,4},{4,3},{5,2},{6,1},{7,0},{8,15},{9,14},{10,... | collective-permute-start | bytes 786440 | tf_op jit(solution)/shard_map/ppermute | solution.py:338
  156.7 54.7 %collective-permute-start.1 = (bf16[2,512,128]{2,1,0:T(8,128)(2,1)}, bf16[2,512,128]{2,1,0:T(8,128)(2,1)S(1)}, u32[]{:S(2)}, u32[]{:S(2)}) collective-permute-start(bf16[2,512,128]{2,1,0:T(8,128)(2,1)} %get-tuple-element.31), channel_id=1, source_target_pairs={{0,6},{1,7},{2,4},{3,5},{4,2},{5,3},{6,0},{7,1},{8,14},{9,15},{10,... | collective-permute-start | bytes 786440 | tf_op jit(solution)/shard_map/ppermute | solution.py:338
  157.2 54.2 %collective-permute-start.2 = (bf16[2,512,128]{2,1,0:T(8,128)(2,1)S(1)}, bf16[2,512,128]{2,1,0:T(8,128)(2,1)S(1)}, u32[]{:S(2)}, u32[]{:S(2)}) collective-permute-start(bf16[2,512,128]{2,1,0:T(8,128)(2,1)S(1)} %copy-done.17), channel_id=1, source_target_pairs={{0,5},{1,4},{2,7},{3,6},{4,1},{5,0},{6,3},{7,2},{8,13},{9,12},{10,... | collective-permute-start | bytes 786440 | tf_op jit(solution)/shard_map/ppermute | solution.py:338
  158.4 57.1 %collective-permute-start.3 = (bf16[2,512,128]{2,1,0:T(8,128)(2,1)S(1)}, bf16[2,512,128]{2,1,0:T(8,128)(2,1)S(1)}, u32[]{:S(2)}, u32[]{:S(2)}) collective-permute-start(bf16[2,512,128]{2,1,0:T(8,128)(2,1)S(1)} %copy-done.16), channel_id=1, source_target_pairs={{0,4},{1,5},{2,6},{3,7},{4,0},{5,1},{6,2},{7,3},{8,12},{9,13},{10,... | collective-permute-start | bytes 786440 | tf_op jit(solution)/shard_map/ppermute | solution.py:338
  158.9 58.6 %collective-permute-start.4 = (bf16[2,512,128]{2,1,0:T(8,128)(2,1)S(1)}, bf16[2,512,128]{2,1,0:T(8,128)(2,1)S(1)}, u32[]{:S(2)}, u32[]{:S(2)}) collective-permute-start(bf16[2,512,128]{2,1,0:T(8,128)(2,1)S(1)} %copy-done.15), channel_id=1, source_target_pairs={{0,3},{1,2},{2,1},{3,0},{4,7},{5,6},{6,5},{7,4},{8,11},{9,10},{10,... | collective-permute-start | bytes 786440 | tf_op jit(solution)/shard_map/ppermute | solution.py:338
  191.4 32.2 %copy-start.28 = (bf16[2,512,128]{2,1,0:T(8,128)(2,1)}, bf16[2,512,128]{2,1,0:T(8,128)(2,1)S(1)}, u32[]{:S(2)}) copy-start(bf16[2,512,128]{2,1,0:T(8,128)(2,1)S(1)} %collective-permute-done.refs_1_) | copy-start | bytes 786436
  191.4 32.2 %collective-permute-start.5 = (bf16[2,512,128]{2,1,0:T(8,128)(2,1)S(1)}, bf16[2,512,128]{2,1,0:T(8,128)(2,1)S(1)}, u32[]{:S(2)}, u32[]{:S(2)}) collective-permute-start(bf16[2,512,128]{2,1,0:T(8,128)(2,1)S(1)} %copy-done.14), channel_id=1, source_target_pairs={{0,2},{1,3},{2,0},{3,1},{4,6},{5,7},{6,4},{7,5},{8,10},{9,11},{10,... | collective-permute-start | bytes 786440 | tf_op jit(solution)/shard_map/ppermute | solution.py:338
  211.4 12.2 %copy-start.29 = (bf16[2,512,128]{2,1,0:T(8,128)(2,1)}, bf16[2,512,128]{2,1,0:T(8,128)(2,1)S(1)}, u32[]{:S(2)}) copy-start(bf16[2,512,128]{2,1,0:T(8,128)(2,1)S(1)} %collective-permute-done.1.refs_2_) | copy-start | bytes 786436
  211.4 12.2 %collective-permute-start.6 = (bf16[2,512,128]{2,1,0:T(8,128)(2,1)S(1)}, bf16[2,512,128]{2,1,0:T(8,128)(2,1)S(1)}, u32[]{:S(2)}, u32[]{:S(2)}) collective-permute-start(bf16[2,512,128]{2,1,0:T(8,128)(2,1)S(1)} %copy-done.13), channel_id=1, source_target_pairs={{0,1},{1,0},{2,3},{3,2},{4,5},{5,4},{6,7},{7,6},{8,9},{9,8},{10,11... | collective-permute-start | bytes 786440 | tf_op jit(solution)/shard_map/ppermute | solution.py:338
  211.4 12.2 %copy-start.30 = (bf16[2,512,128]{2,1,0:T(8,128)(2,1)}, bf16[2,512,128]{2,1,0:T(8,128)(2,1)S(1)}, u32[]{:S(2)}) copy-start(bf16[2,512,128]{2,1,0:T(8,128)(2,1)S(1)} %collective-permute-done.2.refs_3_) | copy-start | bytes 786436
  215.4 8.2 %copy-start.31 = (bf16[2,512,128]{2,1,0:T(8,128)(2,1)}, bf16[2,512,128]{2,1,0:T(8,128)(2,1)S(1)}, u32[]{:S(2)}) copy-start(bf16[2,512,128]{2,1,0:T(8,128)(2,1)S(1)} %collective-permute-done.3.refs_4_) | copy-start | bytes 786436
  217.5 6.1 %copy-start.32 = (bf16[2,512,128]{2,1,0:T(8,128)(2,1)}, bf16[2,512,128]{2,1,0:T(8,128)(2,1)S(1)}, u32[]{:S(2)}) copy-start(bf16[2,512,128]{2,1,0:T(8,128)(2,1)S(1)} %collective-permute-done.4.refs_5_) | copy-start | bytes 786436
  246.6 53.4 %all-to-all-start.2 = ((bf16[32,1,2,128,128]{4,3,2,1,0:T(8,128)(2,1)}), bf16[32,1,2,128,128]{4,3,2,1,0:T(8,128)(2,1)S(1)}, u32[]{:S(2)}, u32[]{:S(2)}) async-start(bf16[32,1,2,128,128]{4,3,2,1,0:T(8,128)(2,1)} %clean.7), calls=%async_computation.2 | async-start | bytes 4194304 | tf_op jit(solution)/shard_map/all_to_all | solution.py:332
  (15 other events, 29.8 us)

commit v13 on v12

--- a/solution.py
+++ b/solution.py
@@ -11,7 +11,6 @@
 
 LANES = 128
 RADIX = 8
-EARLY = 6
 VMEM_BYTES = 56 * 1024 * 1024
 
 
@@ -82,11 +81,9 @@
     return out_r, out_i
 
 
-def column_kernel(chunks, spread, split, at_ref, x_ref, twiddle_ref, table_ref, *refs):
-    if split:
-        *out_refs, mid, stage = refs
-    else:
-        *out_refs, mid = refs
+def column_kernel(chunks, spread, at_ref, x_ref, twiddle_ref, table_ref, *refs):
+    *out_refs, mid, stage = refs
+    pieces = spread * RADIX
     rows, length = x_ref.shape[1:]
     inner = length // RADIX
     step = 16
@@ -111,7 +108,9 @@
                     ti = re[y_lo] * sine + im[y_lo] * cosine
                 mid[y_lo, at, lanes] = tr.astype(jnp.bfloat16)
                 mid[y_lo, at, other] = ti.astype(jnp.bfloat16)
-    for n, chunk in enumerate(chunks):
+    for chunk, split in chunks:
+        outs = out_refs[: pieces if split else 1]
+        out_refs = out_refs[len(outs) :]
         for group in range(spread):
             column = (chunk * spread + group) * LANES
             table = jnp.concatenate(
@@ -126,11 +125,10 @@
                     if split:
                         stage[group * RADIX + y_lo, part] = value
                     else:
-                        out_refs[n][group * RADIX + y_lo, part] = value
+                        outs[0][group * RADIX + y_lo, part] = value
         if split:
-            pieces = spread * RADIX
-            for step in range(pieces):
-                out_refs[n * pieces + step][...] = stage[partner(at_ref[0], step, pieces)]
+            for step, out_ref in enumerate(outs):
+                out_ref[...] = stage[partner(at_ref[0], step, pieces)]
 
 
 def partner(at, step, count):
@@ -141,22 +139,20 @@
     return at ^ step
 
 
-def column_transform(x, at, pieces, chunks, split):
+def column_transform(x, at, pieces, chunks):
     _, rows, length = x.shape
     inner = length // RADIX
-    block = math.gcd(rows, 64)
-    if split:
-        spec = pl.BlockSpec((2, block, LANES), lambda i, at: (0, i, 0))
-        shape = jax.ShapeDtypeStruct((2, rows, LANES), jnp.bfloat16)
-        stage = [pltpu.VMEM((pieces, 2, block, LANES), jnp.bfloat16)]
-        outs = len(chunks) * pieces
-    else:
-        spec = pl.BlockSpec((pieces, 2, block, LANES), lambda i, at: (0, 0, i, 0))
-        shape = jax.ShapeDtypeStruct((pieces, 2, rows, LANES), jnp.bfloat16)
-        stage = []
-        outs = len(chunks)
+    block = math.gcd(rows, 128)
+    specs, shapes = [], []
+    for _, split in chunks:
+        if split:
+            specs += [pl.BlockSpec((2, block, LANES), lambda i, at: (0, i, 0))] * pieces
+            shapes += [jax.ShapeDtypeStruct((2, rows, LANES), jnp.bfloat16)] * pieces
+        else:
+            specs.append(pl.BlockSpec((pieces, 2, block, LANES), lambda i, at: (0, 0, i, 0)))
+            shapes.append(jax.ShapeDtypeStruct((pieces, 2, rows, LANES), jnp.bfloat16))
     return pl.pallas_call(
-        functools.partial(column_kernel, chunks, pieces // RADIX, split),
+        functools.partial(column_kernel, chunks, pieces // RADIX),
         grid_spec=pltpu.PrefetchScalarGridSpec(
             num_scalar_prefetch=1,
             grid=(rows // block,),
@@ -165,10 +161,13 @@
                 pl.BlockSpec((RADIX, 2, inner), lambda i, at: (0, 0, 0)),
                 pl.BlockSpec((2 * inner, 2 * inner), lambda i, at: (0, 0)),
             ],
-            out_specs=[spec] * outs,
-            scratch_shapes=[pltpu.VMEM((RADIX, block, 2 * inner), jnp.bfloat16)] + stage,
-        ),
-        out_shape=[shape] * outs,
+            out_specs=specs,
+            scratch_shapes=[
+                pltpu.VMEM((RADIX, block, 2 * inner), jnp.bfloat16),
+                pltpu.VMEM((pieces, 2, block, LANES), jnp.bfloat16),
+            ],
+        ),
+        out_shape=shapes,
         compiler_params=params(),
         cost_estimate=pl.CostEstimate(
             flops=4 * rows * length * LANES * pieces * len(chunks),
@@ -354,15 +353,18 @@
     basis_t = turn(basis)
     gain = eigenvalues[:, None] / (eigenvalues[:, None] + noise_power[None, :])
     flat = visibility.reshape(2, chans * rows_dev, length)
-    first = column_transform(flat, at, chan_count, [0], False)
+    first = column_transform(flat, at, chan_count, [(0, False)])
     cells = [[exchange(first[0], "chan")]]
     if count > 1:
-        sends = column_transform(flat, at, chan_count, list(range(1, count)), True)
+        second, *sends = column_transform(
+            flat, at, chan_count, [(k, k > 1) for k in range(1, count)]
+        )
+        cells.append([exchange(second, "chan")])
         cells += [
-            scatter(sends[k * chan_count : (k + 1) * chan_count]) for k in range(count - 1)
+            scatter(sends[k * chan_count : (k + 1) * chan_count]) for k in range(count - 2)
         ]
     groups = [[0]] + [g for g in (list(range(1, count - 1)), [count - 1]) if g and count > 1]
-    held, before = [], cells[1][1:EARLY] if count > 1 else []
+    held, before = [], [second] if count > 1 else []
     for chunks in groups:
         for slot, k in enumerate(chunks):
             cleaned = clean(

time: 312 us -> 307 us (0.984)
  starting transfers between devices: 45 us -> 41 us
    all_to_all x5 -> x6, waiting for transfers between devices: 42.1 us -> 68.4 us  [exchange(): return lax.all_to_all(x, axes, split_axis=0, concat_axis=0, tiled=True)]
    ppermute x21 -> x14, waiting for transfers between devices: 125 us -> 99.4 us  [scatter(): lax.ppermute(pieces[step], 'chan', [(j, int(partner(np.int32(j), step, co...]
    ppermute x21 -> x14, starting transfers between devices: 20.5 us -> 12 us  [scatter(): lax.ppermute(pieces[step], 'chan', [(j, int(partner(np.int32(j), step, co...]
    all_to_all x5 -> x6, starting transfers between devices: 24.6 us -> 28.9 us  [exchange(): return lax.all_to_all(x, axes, split_axis=0, concat_axis=0, tiled=True)]
    unnamed x74 -> x62, local copies, waits for them, and re-layouts: 7.04 us -> 7.83 us
  transfers between devices with their start and end apart: 26 -> 20, of which waited for: 15 -> 13; matrix products, arithmetic and copies ran while one was open for 0% -> 0% of each run, Pallas kernels for 24% -> 25%
where the time goes in v13:
time: 307 us; the launch traced here: 303 us
  waiting for transfers between devices  168 us (55%)
  Pallas kernels  83.6 us (27%)
  starting transfers between devices  41 us (13%)
  local copies, waits for them, and re-layouts  9.5 us (3%)
    ppermute x14, waiting for transfers between devices, scatter(): lax.ppermute(pieces[step], 'chan', [(j, int(partner(np.int32(j), step, co...  99.4 us
    all_to_all x6, waiting for transfers between devices, exchange(): return lax.all_to_all(x, axes, split_axis=0, concat_axis=0, tiled=True)  68.4 us
    all_to_all x6, starting transfers between devices, exchange(): return lax.all_to_all(x, axes, split_axis=0, concat_axis=0, tiled=True)  28.9 us
    pallas_call x4, Pallas kernels, clean(): pl.pallas_call(functools.partial(clean_kernel, split, len(before)), grid=...  28.8 us
    pallas_call x2, Pallas kernels, column_transform(): pl.pallas_call(functools.partial(column_kernel, chunks, pieces // RADIX),...  26.9 us
    pallas_call x4, Pallas kernels, image(): pl.pallas_call(functools.partial(image_kernel, scale), grid=(chans // gro...  25.9 us
    ppermute x14, starting transfers between devices, scatter(): lax.ppermute(pieces[step], 'chan', [(j, int(partner(np.int32(j), step, co...  12 us
    unnamed x62, local copies, waits for them, and re-layouts  7.83 us
  transfers between devices with their start and end apart: 20, of which 13 were waited for; matrix products, arithmetic and copies ran while one was open for 0% of the time, Pallas kernels for 25%

profile of v13, /device:TPU:8, one launch (start us, length us, event | category | flops | bytes accessed | tf_op | source)
XLA Modules:
  0.0 302.9 jit_solution(15130854508185808363)
XLA Ops:
  0.0 1.7 broadcast_in_dim.2
  1.7 3.7 %all-to-all-start = ((bf16[8,64,512]{2,1,0:T(8,128)(2,1)}), bf16[8,64,512]{2,1,0:T(8,128)(2,1)S(1)}, u32[]{:S(2)}, u32[]{:S(2)}) async-start(bf16[8,64,512]{2,1,0:T(8,128)(2,1)} %broadcast_in_dim.2), calls=%async_computation | async-start | bytes 1048576 | tf_op jit(solution)/shard_map/all_to_all | solution.py:331
  5.4 10.6 %column_transform.3 = bf16[8,2,512,128]{3,2,1,0:T(8,128)(2,1)} custom-call(s32[1]{0:T(128)} %bitcast.at_ref, bf16[2,512,4096]{2,1,0:T(8,128)(2,1)} %bitcast.13, f32[8,2,512]{2,1,0:T(2,128)} %constant.16.clone.twiddle_ref, bf16[1024,1024]{1,0:T(8,128)(2,1)} %constant.17.clone.table_ref), custom_call_target="tpu_custom_call" | custom-call | flops 8589934592 | bytes 16777216 | tf_op jit(solution)/shard_map/column_transform/pallas_call | solution.py:154
  16.0 0.8 copy-done.2
  16.8 4.2 %all-to-all-start.2 = ((bf16[8,2,512,128]{3,2,1,0:T(8,128)(2,1)}), bf16[8,2,512,128]{3,2,1,0:T(8,128)(2,1)S(1)}, u32[]{:S(2)}, u32[]{:S(2)}) async-start(bf16[8,2,512,128]{3,2,1,0:T(8,128)(2,1)} %column_transform.3), calls=%async_computation.2 | async-start | bytes 4194304 | tf_op jit(solution)/shard_map/all_to_all | solution.py:331
  21.0 16.3 %column_transform.2 = (bf16[8,2,512,128]{3,2,1,0:T(8,128)(2,1)}, bf16[2,512,128]{2,1,0:T(8,128)(2,1)}, bf16[2,512,128]{2,1,0:T(8,128)(2,1)}, bf16[2,512,128]{2,1...) custom-call(s32[1]{0:T(128)} %bitcast.at_ref, ...), custom_call_target="tpu_custom_call" | custom-call | flops 25769803776 | bytes 16777216 | tf_op jit(solution)/shard_map/column_transform/pallas_call | solution.py:154
  37.3 10.3 %all-to-all-done.2.refs_0_ = bf16[8,2,512,128]{3,2,1,0:T(8,128)(2,1)S(1)} async-done(((bf16[8,2,512,128]{3,2,1,0:T(8,128)(2,1)}), bf16[8,2,512,128]{3,2,1,0:T(8,128)(2,1)S(1)}, u32[]{:S(2)}, u32[]{:S(2)}) %all-to-all-start.2) | async-done | bytes 2097184 | tf_op jit(solution)/shard_map/all_to_all | solution.py:331
  47.7 1.4 copy-done.4
  49.0 3.6 %all-to-all-start.1 = ((bf16[8,2,512,128]{3,2,1,0:T(8,128)(2,1)}), bf16[8,2,512,128]{3,2,1,0:T(8,128)(2,1)S(1)}, u32[]{:S(2)}, u32[]{:S(2)}) async-start(bf16[8,2,512,128]{3,2,1,0:T(8,128)(2,1)} %get-tuple-element.38.refs_6_), calls=%async_computation.1 | async-start | bytes 4194304 | tf_op jit(solution)/shard_map/all_to_all | solution.py:331
  52.6 0.9 add_divide_fusion.refs_3_.refs_10_
  53.5 2.0 turn.1.refs_2_.refs_9_
  55.5 7.1 %clean.4.refs_6_ = bf16[32,1,2,128,128]{4,3,2,1,0:T(8,128)(2,1)} custom-call(s32[1]{0:T(128)} %bitcast.at_ref, bf16[8,2,512,128]{3,2,1,0:T(8,128)(2,1)} %copy-done.4, bf16[512,512]{1,0:T(8,128)(2,1)} %bitcast.9, bf16[512,512]{1,0:T(8,128)(2,1)} %turn.1.refs_2_.refs_9_, f32[512,8]{1,0:T(8,128)} %add_divide_fusion.refs_3_.refs_10_, ...), custom_call_target="tpu_custom_call" | custom-call | flops 3221225472 | bytes 4194304 | tf_op jit(solution)/shard_map/clean/pallas_call | solution.py:242
  62.6 16.6 %all-to-all-done.1.refs_0_ = bf16[8,2,512,128]{3,2,1,0:T(8,128)(2,1)S(1)} async-done(((bf16[8,2,512,128]{3,2,1,0:T(8,128)(2,1)}), bf16[8,2,512,128]{3,2,1,0:T(8,128)(2,1)S(1)}, u32[]{:S(2)}, u32[]{:S(2)}) %all-to-all-start.1) | async-done | bytes 2097184 | tf_op jit(solution)/shard_map/all_to_all | solution.py:331
  79.2 1.4 copy-done.3
  80.6 4.2 %all-to-all-start.5 = ((bf16[32,1,2,128,128]{4,3,2,1,0:T(8,128)(2,1)}), bf16[32,1,2,128,128]{4,3,2,1,0:T(8,128)(2,1)S(1)}, u32[]{:S(2)}, u32[]{:S(2)}) async-start(bf16[32,1,2,128,128]{4,3,2,1,0:T(8,128)(2,1)} %clean.4.refs_6_), calls=%async_computation.5 | async-start | bytes 4194304 | tf_op jit(solution)/shard_map/all_to_all | solution.py:331
  84.8 2.2 collective-permute-start.7
  87.0 0.6 collective-permute-start.8
  87.5 1.1 collective-permute-start.9
  89.2 1.2 collective-permute-start.11
  90.5 19.1 %collective-permute-done.7.refs_1_ = bf16[2,512,128]{2,1,0:T(8,128)(2,1)S(1)} collective-permute-done((bf16[2,512,128]{2,1,0:T(8,128)(2,1)}, bf16[2,512,128]{2,1,0:T(8,128)(2,1)S(1)}, u32[]{:S(2)}, u32[]{:S(2)}) %collective-permute-start.7) | collective-permute-done | bytes 262176 | tf_op jit(solution)/shard_map/ppermute | solution.py:337
  109.5 0.6 collective-permute-start.12
  110.2 11.9 %collective-permute-done.8.refs_2_ = bf16[2,512,128]{2,1,0:T(8,128)(2,1)S(1)} collective-permute-done((bf16[2,512,128]{2,1,0:T(8,128)(2,1)}, bf16[2,512,128]{2,1,0:T(8,128)(2,1)S(1)}, u32[]{:S(2)}, u32[]{:S(2)}) %collective-permute-start.8) | collective-permute-done | bytes 262176 | tf_op jit(solution)/shard_map/ppermute | solution.py:337
  122.1 7.2 %clean.5.refs_13_ = bf16[32,2,2,128,128]{4,3,2,1,0:T(8,128)(2,1)} custom-call(s32[1]{0:T(128)} %bitcast.at_ref, bf16[8,2,512,128]{3,2,1,0:T(8,128)(2,1)} %copy-done.3, bf16[512,512]{1,0:T(8,128)(2,1)} %bitcast.10, bf16[512,512]{1,0:T(8,128)(2,1)} %turn.1.refs_2_.refs_9_, f32[512,8]{1,0:T(8,128)} %add_divide_fusion.refs_3_.refs_10_, ...), custom_call_target="tpu_custom_call" | custom-call | flops 3221225472 | bytes 4194304 | tf_op jit(solution)/shard_map/clean/pallas_call | solution.py:242
  129.3 2.9 collective-permute-done.10.refs_4_
  132.2 2.2 collective-permute-done.12.refs_6_
  134.5 0.7 copy-done.10
  135.3 7.2 %clean.6.refs_13_ = bf16[32,2,2,128,128]{4,3,2,1,0:T(8,128)(2,1)} custom-call(s32[1]{0:T(128)} %bitcast.at_ref, bf16[2,512,128]{2,1,0:T(8,128)(2,1)} %get-tuple-element.30.refs_0_, bf16[2,512,128]{2,1,0:T(8,128)(2,1)} %copy-done.5, bf16[2,512,128]{2,1,0:T(8,128)(2,1)} %copy-done.6, bf16[2,512,128]{2,1,0:T(8,128)(2,1)} %copy-done.7, ...), custom_call_target="tpu_custom_call", output_to_operand_aliasing={{}: (14, {})} | custom-call | flops 3221225472 | bytes 4194304 | tf_op jit(solution)/shard_map/clean/pallas_call | solution.py:242
  142.6 1.3 copy-done
  143.9 5.7 %all-to-all-start.4 = ((bf16[32,2,2,128,128]{4,3,2,1,0:T(8,128)(2,1)}), bf16[32,2,2,128,128]{4,3,2,1,0:T(8,128)(2,1)}, u32[]{:S(2)}, u32[]{:S(2)}) async-start(bf16[32,2,2,128,128]{4,3,2,1,0:T(8,128)(2,1)} %clean.6.refs_13_), calls=%async_computation.4 | async-start | bytes 8388608 | tf_op jit(solution)/shard_map/all_to_all | solution.py:331
  149.6 2.2 collective-permute-start
  151.8 0.6 collective-permute-start.1
  152.4 1.1 collective-permute-start.2
  154.1 1.2 collective-permute-start.4
  155.3 31.2 %collective-permute-done.refs_1_ = bf16[2,512,128]{2,1,0:T(8,128)(2,1)S(1)} collective-permute-done((bf16[2,512,128]{2,1,0:T(8,128)(2,1)}, bf16[2,512,128]{2,1,0:T(8,128)(2,1)S(1)}, u32[]{:S(2)}, u32[]{:S(2)}) %collective-permute-start) | collective-permute-done | bytes 262176 | tf_op jit(solution)/shard_map/ppermute | solution.py:337
  186.5 20.0 %collective-permute-done.1.refs_2_ = bf16[2,512,128]{2,1,0:T(8,128)(2,1)S(1)} collective-permute-done((bf16[2,512,128]{2,1,0:T(8,128)(2,1)}, bf16[2,512,128]{2,1,0:T(8,128)(2,1)S(1)}, u32[]{:S(2)}, u32[]{:S(2)}) %collective-permute-start.1) | collective-permute-done | bytes 262176 | tf_op jit(solution)/shard_map/ppermute | solution.py:337
  206.6 4.0 %collective-permute-done.3.refs_4_ = bf16[2,512,128]{2,1,0:T(8,128)(2,1)S(1)} collective-permute-done((bf16[2,512,128]{2,1,0:T(8,128)(2,1)S(1)}, bf16[2,512,128]{2,1,0:T(8,128)(2,1)S(1)}, u32[]{:S(2)}, u32[]{:S(2)}) %collective-permute-start.3) | collective-permute-done | bytes 262176 | tf_op jit(solution)/shard_map/ppermute | solution.py:337
  210.6 1.9 collective-permute-done.4.refs_5_
  212.5 6.1 %collective-permute-done.5.refs_6_ = bf16[2,512,128]{2,1,0:T(8,128)(2,1)S(1)} collective-permute-done((bf16[2,512,128]{2,1,0:T(8,128)(2,1)S(1)}, bf16[2,512,128]{2,1,0:T(8,128)(2,1)S(1)}, u32[]{:S(2)}, u32[]{:S(2)}) %collective-permute-start.5) | collective-permute-done | bytes 262176 | tf_op jit(solution)/shard_map/ppermute | solution.py:337
  218.6 0.6 copy-done.29
  219.4 7.3 %clean.7 = bf16[32,1,2,128,128]{4,3,2,1,0:T(8,128)(2,1)} custom-call(s32[1]{0:T(128)} %bitcast.at_ref, bf16[2,512,128]{2,1,0:T(8,128)(2,1)} %get-tuple-element.22.refs_0_, bf16[2,512,128]{2,1,0:T(8,128)(2,1)} %copy-done.24, bf16[2,512,128]{2,1,0:T(8,128)(2,1)} %copy-done.25, bf16[2,512,128]{2,1,0:T(8,128)(2,1)} %copy-done.26, ...), custom_call_target="tpu_custom_call" | custom-call | flops 3221225472 | bytes 4194304 | tf_op jit(solution)/shard_map/clean/pallas_call | solution.py:242
  226.6 14.3 %all-to-all-done.4 = bf16[32,2,2,128,128]{4,3,2,1,0:T(8,128)(2,1)} async-done(((bf16[32,2,2,128,128]{4,3,2,1,0:T(8,128)(2,1)}), bf16[32,2,2,128,128]{4,3,2,1,0:T(8,128)(2,1)}, u32[]{:S(2)}, u32[]{:S(2)}) %all-to-all-start.4) | async-done | bytes 4194336 | tf_op jit(solution)/shard_map/all_to_all | solution.py:331
  241.0 7.5 %all-to-all-start.3 = ((bf16[32,1,2,128,128]{4,3,2,1,0:T(8,128)(2,1)}), bf16[32,1,2,128,128]{4,3,2,1,0:T(8,128)(2,1)S(1)}, u32[]{:S(2)}, u32[]{:S(2)}) async-start(bf16[32,1,2,128,128]{4,3,2,1,0:T(8,128)(2,1)} %clean.7), calls=%async_computation.3 | async-start | bytes 4194304 | tf_op jit(solution)/shard_map/all_to_all | solution.py:331
  248.5 6.5 %image.4.refs_0_ = bf16[2,16,32,4096]{3,2,1,0:T(8,128)(2,1)} custom-call(bf16[4,8,1,2,128,128]{5,4,3,2,1,0:T(8,128)(2,1)} %bitcast.6, bf16[256,256]{1,0:T(8,128)(2,1)} %constant.20.clone.table_ref, bf16[1024,1024]{1,0:T(8,128)(2,1)} %constant.21.clone.order_ref), custom_call_target="tpu_custom_call" | custom-call | flops 2147483648 | bytes 4194304 | tf_op jit(solution)/shard_map/image/pallas_call | solution.py:288
  255.0 6.5 %image.5.refs_0_ = bf16[2,16,32,4096]{3,2,1,0:T(8,128)(2,1)} custom-call(bf16[4,8,2,2,128,128]{5,4,3,2,1,0:T(8,128)(2,1)} %bitcast.4.x_ref, bf16[256,256]{1,0:T(8,128)(2,1)} %constant.20.clone.table_ref, bf16[1024,1024]{1,0:T(8,128)(2,1)} %constant.21.clone.order_ref, bf16[2,16,32,4096]{3,2,1,0:T(8,128)(2,1)} %image.4.refs_0_), custom_call_target="tpu_custom_call", output_to_operand_aliasing={{}: (3, {})} | custom-call | flops 2147483648 | bytes 4194304 | tf_op jit(solution)/shard_map/image/pallas_call | solution.py:288
  261.5 6.5 %image.6.refs_0_ = bf16[2,16,32,4096]{3,2,1,0:T(8,128)(2,1)} custom-call(bf16[4,8,2,2,128,128]{5,4,3,2,1,0:T(8,128)(2,1)} %bitcast.4.x_ref, bf16[256,256]{1,0:T(8,128)(2,1)} %constant.20.clone.table_ref, bf16[1024,1024]{1,0:T(8,128)(2,1)} %constant.21.clone.order_ref, bf16[2,16,32,4096]{3,2,1,0:T(8,128)(2,1)} %image.5.refs_0_), custom_call_target="tpu_custom_call", output_to_operand_aliasing={{}: (3, {})} | custom-call | flops 2147483648 | bytes 4194304 | tf_op jit(solution)/shard_map/image/pallas_call | solution.py:288
  267.9 27.2 %all-to-all-done.3 = bf16[32,1,2,128,128]{4,3,2,1,0:T(8,128)(2,1)S(1)} async-done(((bf16[32,1,2,128,128]{4,3,2,1,0:T(8,128)(2,1)}), bf16[32,1,2,128,128]{4,3,2,1,0:T(8,128)(2,1)S(1)}, u32[]{:S(2)}, u32[]{:S(2)}) %all-to-all-start.3) | async-done | bytes 2097184 | tf_op jit(solution)/shard_map/all_to_all | solution.py:331
  295.2 1.3 copy-done.1
  296.5 6.4 %image.7 = bf16[2,16,32,4096]{3,2,1,0:T(8,128)(2,1)} custom-call(bf16[4,8,1,2,128,128]{5,4,3,2,1,0:T(8,128)(2,1)} %bitcast.7, bf16[256,256]{1,0:T(8,128)(2,1)} %constant.20.clone.table_ref, bf16[1024,1024]{1,0:T(8,128)(2,1)} %constant.21.clone.order_ref, bf16[2,16,32,4096]{3,2,1,0:T(8,128)(2,1)} %image.6.refs_0_), custom_call_target="tpu_custom_call", output_to_operand_aliasing={{}: (3, {})} | custom-call | flops 2147483648 | bytes 4194304 | tf_op jit(solution)/shard_map/image/pallas_call | solution.py:288
  (67 shorter events, 1.4 us)
Async XLA Ops:
  1.7 14.3 %all-to-all-start = ((bf16[8,64,512]{2,1,0:T(8,128)(2,1)}), bf16[8,64,512]{2,1,0:T(8,128)(2,1)S(1)}, u32[]{:S(2)}, u32[]{:S(2)}) async-start(bf16[8,64,512]{2,1,0:T(8,128)(2,1)} %broadcast_in_dim.2), calls=%async_computation | async-start | bytes 1048576 | tf_op jit(solution)/shard_map/all_to_all | solution.py:331
  16.0 0.8 copy-start.2
  16.8 30.8 %all-to-all-start.2 = ((bf16[8,2,512,128]{3,2,1,0:T(8,128)(2,1)}), bf16[8,2,512,128]{3,2,1,0:T(8,128)(2,1)S(1)}, u32[]{:S(2)}, u32[]{:S(2)}) async-start(bf16[8,2,512,128]{3,2,1,0:T(8,128)(2,1)} %column_transform.3), calls=%async_computation.2 | async-start | bytes 4194304 | tf_op jit(solution)/shard_map/all_to_all | solution.py:331
  47.6 1.4 copy-start.4
  47.6 5.0 %copy-start.12 = (f32[512]{0:T(512)S(1)}, f32[512]{0:T(512)}, u32[]{:S(2)}) copy-start(f32[512]{0:T(512)} %param.26) | copy-start | bytes 6148
  47.6 5.0 %copy-start.13 = (f32[8]{0:T(128)S(1)}, f32[8]{0:T(128)}, u32[]{:S(2)}) copy-start(f32[8]{0:T(128)} %param.27) | copy-start | bytes 100
  49.0 30.2 %all-to-all-start.1 = ((bf16[8,2,512,128]{3,2,1,0:T(8,128)(2,1)}), bf16[8,2,512,128]{3,2,1,0:T(8,128)(2,1)S(1)}, u32[]{:S(2)}, u32[]{:S(2)}) async-start(bf16[8,2,512,128]{3,2,1,0:T(8,128)(2,1)} %get-tuple-element.38.refs_6_), calls=%async_computation.1 | async-start | bytes 4194304 | tf_op jit(solution)/shard_map/all_to_all | solution.py:331
  62.6 24.9 %copy-start.23 = (bf16[2,512,128]{2,1,0:T(8,128)(2,1)S(1)}, bf16[2,512,128]{2,1,0:T(8,128)(2,1)}, u32[]{:S(2)}) copy-start(bf16[2,512,128]{2,1,0:T(8,128)(2,1)} %get-tuple-element.33) | copy-start | bytes 786436
  62.6 26.1 %copy-start.22 = (bf16[2,512,128]{2,1,0:T(8,128)(2,1)S(1)}, bf16[2,512,128]{2,1,0:T(8,128)(2,1)}, u32[]{:S(2)}) copy-start(bf16[2,512,128]{2,1,0:T(8,128)(2,1)} %get-tuple-element.34) | copy-start | bytes 786436
  62.6 26.6 %copy-start.21 = (bf16[2,512,128]{2,1,0:T(8,128)(2,1)S(1)}, bf16[2,512,128]{2,1,0:T(8,128)(2,1)}, u32[]{:S(2)}) copy-start(bf16[2,512,128]{2,1,0:T(8,128)(2,1)} %get-tuple-element.35) | copy-start | bytes 786436
  62.6 46.9 %copy-start.20 = (bf16[2,512,128]{2,1,0:T(8,128)(2,1)S(1)}, bf16[2,512,128]{2,1,0:T(8,128)(2,1)}, u32[]{:S(2)}) copy-start(bf16[2,512,128]{2,1,0:T(8,128)(2,1)} %get-tuple-element.36) | copy-start | bytes 786436
  62.6 59.5 %copy-start.19 = (bf16[2,512,128]{2,1,0:T(8,128)(2,1)S(1)}, bf16[2,512,128]{2,1,0:T(8,128)(2,1)}, u32[]{:S(2)}) copy-start(bf16[2,512,128]{2,1,0:T(8,128)(2,1)} %get-tuple-element.37) | copy-start | bytes 786436
  79.2 1.4 copy-start.3
  80.6 62.0 %all-to-all-start.5 = ((bf16[32,1,2,128,128]{4,3,2,1,0:T(8,128)(2,1)}), bf16[32,1,2,128,128]{4,3,2,1,0:T(8,128)(2,1)S(1)}, u32[]{:S(2)}, u32[]{:S(2)}) async-start(bf16[32,1,2,128,128]{4,3,2,1,0:T(8,128)(2,1)} %clean.4.refs_6_), calls=%async_computation.5 | async-start | bytes 4194304 | tf_op jit(solution)/shard_map/all_to_all | solution.py:331
  84.8 24.8 %collective-permute-start.7 = (bf16[2,512,128]{2,1,0:T(8,128)(2,1)}, bf16[2,512,128]{2,1,0:T(8,128)(2,1)S(1)}, u32[]{:S(2)}, u32[]{:S(2)}) collective-permute-start(bf16[2,512,128]{2,1,0:T(8,128)(2,1)} %get-tuple-element.31), channel_id=1, source_target_pairs={{0,7},{1,6},{2,5},{3,4},{4,3},{5,2},{6,1},{7,0},{8,15},{9,14},{10,... | collective-permute-start | bytes 786440 | tf_op jit(solution)/shard_map/ppermute | solution.py:337
  87.0 35.2 %collective-permute-start.8 = (bf16[2,512,128]{2,1,0:T(8,128)(2,1)}, bf16[2,512,128]{2,1,0:T(8,128)(2,1)S(1)}, u32[]{:S(2)}, u32[]{:S(2)}) collective-permute-start(bf16[2,512,128]{2,1,0:T(8,128)(2,1)} %get-tuple-element.32), channel_id=1, source_target_pairs={{0,6},{1,7},{2,4},{3,5},{4,2},{5,3},{6,0},{7,1},{8,14},{9,15},{10,... | collective-permute-start | bytes 786440 | tf_op jit(solution)/shard_map/ppermute | solution.py:337
  87.5 41.8 %collective-permute-start.9 = (bf16[2,512,128]{2,1,0:T(8,128)(2,1)S(1)}, bf16[2,512,128]{2,1,0:T(8,128)(2,1)S(1)}, u32[]{:S(2)}, u32[]{:S(2)}) collective-permute-start(bf16[2,512,128]{2,1,0:T(8,128)(2,1)S(1)} %copy-done.23), channel_id=1, source_target_pairs={{0,5},{1,4},{2,7},{3,6},{4,1},{5,0},{6,3},{7,2},{8,13},{9,12},{10,... | collective-permute-start | bytes 786440 | tf_op jit(solution)/shard_map/ppermute | solution.py:337
  88.7 43.6 %collective-permute-start.10 = (bf16[2,512,128]{2,1,0:T(8,128)(2,1)S(1)}, bf16[2,512,128]{2,1,0:T(8,128)(2,1)S(1)}, u32[]{:S(2)}, u32[]{:S(2)}) collective-permute-start(bf16[2,512,128]{2,1,0:T(8,128)(2,1)S(1)} %copy-done.22), channel_id=1, source_target_pairs={{0,4},{1,5},{2,6},{3,7},{4,0},{5,1},{6,2},{7,3},{8,12},{9,13},{10,... | collective-permute-start | bytes 786440 | tf_op jit(solution)/shard_map/ppermute | solution.py:337
  89.2 43.0 %collective-permute-start.11 = (bf16[2,512,128]{2,1,0:T(8,128)(2,1)S(1)}, bf16[2,512,128]{2,1,0:T(8,128)(2,1)S(1)}, u32[]{:S(2)}, u32[]{:S(2)}) collective-permute-start(bf16[2,512,128]{2,1,0:T(8,128)(2,1)S(1)} %copy-done.21), channel_id=1, source_target_pairs={{0,3},{1,2},{2,1},{3,0},{4,7},{5,6},{6,5},{7,4},{8,11},{9,10},{10,... | collective-permute-start | bytes 786440 | tf_op jit(solution)/shard_map/ppermute | solution.py:337
  109.5 19.8 %copy-start.5 = (bf16[2,512,128]{2,1,0:T(8,128)(2,1)}, bf16[2,512,128]{2,1,0:T(8,128)(2,1)S(1)}, u32[]{:S(2)}) copy-start(bf16[2,512,128]{2,1,0:T(8,128)(2,1)S(1)} %collective-permute-done.7.refs_1_) | copy-start | bytes 786436
  109.5 24.9 %collective-permute-start.12 = (bf16[2,512,128]{2,1,0:T(8,128)(2,1)S(1)}, bf16[2,512,128]{2,1,0:T(8,128)(2,1)S(1)}, u32[]{:S(2)}, u32[]{:S(2)}) collective-permute-start(bf16[2,512,128]{2,1,0:T(8,128)(2,1)S(1)} %copy-done.20), channel_id=1, source_target_pairs={{0,2},{1,3},{2,0},{3,1},{4,6},{5,7},{6,4},{7,5},{8,10},{9,11},{10,... | collective-permute-start | bytes 786440 | tf_op jit(solution)/shard_map/ppermute | solution.py:337
  122.1 7.2 %copy-start.6 = (bf16[2,512,128]{2,1,0:T(8,128)(2,1)}, bf16[2,512,128]{2,1,0:T(8,128)(2,1)S(1)}, u32[]{:S(2)}) copy-start(bf16[2,512,128]{2,1,0:T(8,128)(2,1)S(1)} %collective-permute-done.8.refs_2_) | copy-start | bytes 786436
  122.1 12.4 %collective-permute-start.13 = (bf16[2,512,128]{2,1,0:T(8,128)(2,1)S(1)}, bf16[2,512,128]{2,1,0:T(8,128)(2,1)S(1)}, u32[]{:S(2)}, u32[]{:S(2)}) collective-permute-start(bf16[2,512,128]{2,1,0:T(8,128)(2,1)S(1)} %copy-done.19), channel_id=1, source_target_pairs={{0,1},{1,0},{2,3},{3,2},{4,5},{5,4},{6,7},{7,6},{8,9},{9,8},{10,11... | collective-permute-start | bytes 786440 | tf_op jit(solution)/shard_map/ppermute | solution.py:337
  129.3 5.2 %copy-start.7 = (bf16[2,512,128]{2,1,0:T(8,128)(2,1)}, bf16[2,512,128]{2,1,0:T(8,128)(2,1)S(1)}, u32[]{:S(2)}) copy-start(bf16[2,512,128]{2,1,0:T(8,128)(2,1)S(1)} %collective-permute-done.9.refs_3_) | copy-start | bytes 786436
  132.2 2.3 copy-start.8
  132.2 2.3 copy-start.9
  134.5 0.8 copy-start.11
  142.5 9.8 %copy-start.18 = (bf16[2,512,128]{2,1,0:T(8,128)(2,1)S(1)}, bf16[2,512,128]{2,1,0:T(8,128)(2,1)}, u32[]{:S(2)}) copy-start(bf16[2,512,128]{2,1,0:T(8,128)(2,1)} %get-tuple-element.25) | copy-start | bytes 786436
  142.5 11.0 %copy-start.17 = (bf16[2,512,128]{2,1,0:T(8,128)(2,1)S(1)}, bf16[2,512,128]{2,1,0:T(8,128)(2,1)}, u32[]{:S(2)}) copy-start(bf16[2,512,128]{2,1,0:T(8,128)(2,1)} %get-tuple-element.26) | copy-start | bytes 786436
  142.5 11.5 %copy-start.16 = (bf16[2,512,128]{2,1,0:T(8,128)(2,1)S(1)}, bf16[2,512,128]{2,1,0:T(8,128)(2,1)}, u32[]{:S(2)}) copy-start(bf16[2,512,128]{2,1,0:T(8,128)(2,1)} %get-tuple-element.27) | copy-start | bytes 786436
  142.5 44.0 %copy-start.15 = (bf16[2,512,128]{2,1,0:T(8,128)(2,1)S(1)}, bf16[2,512,128]{2,1,0:T(8,128)(2,1)}, u32[]{:S(2)}) copy-start(bf16[2,512,128]{2,1,0:T(8,128)(2,1)} %get-tuple-element.28) | copy-start | bytes 786436
  142.5 64.0 %copy-start.14 = (bf16[2,512,128]{2,1,0:T(8,128)(2,1)S(1)}, bf16[2,512,128]{2,1,0:T(8,128)(2,1)}, u32[]{:S(2)}) copy-start(bf16[2,512,128]{2,1,0:T(8,128)(2,1)} %get-tuple-element.29) | copy-start | bytes 786436
  142.6 1.4 copy-start
  143.9 97.1 %all-to-all-start.4 = ((bf16[32,2,2,128,128]{4,3,2,1,0:T(8,128)(2,1)}), bf16[32,2,2,128,128]{4,3,2,1,0:T(8,128)(2,1)}, u32[]{:S(2)}, u32[]{:S(2)}) async-start(bf16[32,2,2,128,128]{4,3,2,1,0:T(8,128)(2,1)} %clean.6.refs_13_), calls=%async_computation.4 | async-start | bytes 8388608 | tf_op jit(solution)/shard_map/all_to_all | solution.py:331
  149.6 36.9 %collective-permute-start = (bf16[2,512,128]{2,1,0:T(8,128)(2,1)}, bf16[2,512,128]{2,1,0:T(8,128)(2,1)S(1)}, u32[]{:S(2)}, u32[]{:S(2)}) collective-permute-start(bf16[2,512,128]{2,1,0:T(8,128)(2,1)} %get-tuple-element.23), channel_id=1, source_target_pairs={{0,7},{1,6},{2,5},{3,4},{4,3},{5,2},{6,1},{7,0},{8,15},{9,14},{10,... | collective-permute-start | bytes 786440 | tf_op jit(solution)/shard_map/ppermute | solution.py:337
  151.8 54.8 %collective-permute-start.1 = (bf16[2,512,128]{2,1,0:T(8,128)(2,1)}, bf16[2,512,128]{2,1,0:T(8,128)(2,1)S(1)}, u32[]{:S(2)}, u32[]{:S(2)}) collective-permute-start(bf16[2,512,128]{2,1,0:T(8,128)(2,1)} %get-tuple-element.24), channel_id=1, source_target_pairs={{0,6},{1,7},{2,4},{3,5},{4,2},{5,3},{6,0},{7,1},{8,14},{9,15},{10,... | collective-permute-start | bytes 786440 | tf_op jit(solution)/shard_map/ppermute | solution.py:337
  152.4 54.2 %collective-permute-start.2 = (bf16[2,512,128]{2,1,0:T(8,128)(2,1)S(1)}, bf16[2,512,128]{2,1,0:T(8,128)(2,1)S(1)}, u32[]{:S(2)}, u32[]{:S(2)}) collective-permute-start(bf16[2,512,128]{2,1,0:T(8,128)(2,1)S(1)} %copy-done.18), channel_id=1, source_target_pairs={{0,5},{1,4},{2,7},{3,6},{4,1},{5,0},{6,3},{7,2},{8,13},{9,12},{10,... | collective-permute-start | bytes 786440 | tf_op jit(solution)/shard_map/ppermute | solution.py:337
  153.5 57.1 %collective-permute-start.3 = (bf16[2,512,128]{2,1,0:T(8,128)(2,1)S(1)}, bf16[2,512,128]{2,1,0:T(8,128)(2,1)S(1)}, u32[]{:S(2)}, u32[]{:S(2)}) collective-permute-start(bf16[2,512,128]{2,1,0:T(8,128)(2,1)S(1)} %copy-done.17), channel_id=1, source_target_pairs={{0,4},{1,5},{2,6},{3,7},{4,0},{5,1},{6,2},{7,3},{8,12},{9,13},{10,... | collective-permute-start | bytes 786440 | tf_op jit(solution)/shard_map/ppermute | solution.py:337
  154.1 58.4 %collective-permute-start.4 = (bf16[2,512,128]{2,1,0:T(8,128)(2,1)S(1)}, bf16[2,512,128]{2,1,0:T(8,128)(2,1)S(1)}, u32[]{:S(2)}, u32[]{:S(2)}) collective-permute-start(bf16[2,512,128]{2,1,0:T(8,128)(2,1)S(1)} %copy-done.16), channel_id=1, source_target_pairs={{0,3},{1,2},{2,1},{3,0},{4,7},{5,6},{6,5},{7,4},{8,11},{9,10},{10,... | collective-permute-start | bytes 786440 | tf_op jit(solution)/shard_map/ppermute | solution.py:337
  186.5 32.0 %copy-start.24 = (bf16[2,512,128]{2,1,0:T(8,128)(2,1)}, bf16[2,512,128]{2,1,0:T(8,128)(2,1)S(1)}, u32[]{:S(2)}) copy-start(bf16[2,512,128]{2,1,0:T(8,128)(2,1)S(1)} %collective-permute-done.refs_1_) | copy-start | bytes 786436
  186.5 32.0 %collective-permute-start.5 = (bf16[2,512,128]{2,1,0:T(8,128)(2,1)S(1)}, bf16[2,512,128]{2,1,0:T(8,128)(2,1)S(1)}, u32[]{:S(2)}, u32[]{:S(2)}) collective-permute-start(bf16[2,512,128]{2,1,0:T(8,128)(2,1)S(1)} %copy-done.15), channel_id=1, source_target_pairs={{0,2},{1,3},{2,0},{3,1},{4,6},{5,7},{6,4},{7,5},{8,10},{9,11},{10,... | collective-permute-start | bytes 786440 | tf_op jit(solution)/shard_map/ppermute | solution.py:337
  206.5 12.0 %copy-start.25 = (bf16[2,512,128]{2,1,0:T(8,128)(2,1)}, bf16[2,512,128]{2,1,0:T(8,128)(2,1)S(1)}, u32[]{:S(2)}) copy-start(bf16[2,512,128]{2,1,0:T(8,128)(2,1)S(1)} %collective-permute-done.1.refs_2_) | copy-start | bytes 786436
  206.5 12.0 %collective-permute-start.6 = (bf16[2,512,128]{2,1,0:T(8,128)(2,1)S(1)}, bf16[2,512,128]{2,1,0:T(8,128)(2,1)S(1)}, u32[]{:S(2)}, u32[]{:S(2)}) collective-permute-start(bf16[2,512,128]{2,1,0:T(8,128)(2,1)S(1)} %copy-done.14), channel_id=1, source_target_pairs={{0,1},{1,0},{2,3},{3,2},{4,5},{5,4},{6,7},{7,6},{8,9},{9,8},{10,11... | collective-permute-start | bytes 786440 | tf_op jit(solution)/shard_map/ppermute | solution.py:337
  206.6 12.0 %copy-start.26 = (bf16[2,512,128]{2,1,0:T(8,128)(2,1)}, bf16[2,512,128]{2,1,0:T(8,128)(2,1)S(1)}, u32[]{:S(2)}) copy-start(bf16[2,512,128]{2,1,0:T(8,128)(2,1)S(1)} %collective-permute-done.2.refs_3_) | copy-start | bytes 786436
  210.6 8.0 %copy-start.27 = (bf16[2,512,128]{2,1,0:T(8,128)(2,1)}, bf16[2,512,128]{2,1,0:T(8,128)(2,1)S(1)}, u32[]{:S(2)}) copy-start(bf16[2,512,128]{2,1,0:T(8,128)(2,1)S(1)} %collective-permute-done.3.refs_4_) | copy-start | bytes 786436
  212.5 6.1 %copy-start.28 = (bf16[2,512,128]{2,1,0:T(8,128)(2,1)}, bf16[2,512,128]{2,1,0:T(8,128)(2,1)S(1)}, u32[]{:S(2)}) copy-start(bf16[2,512,128]{2,1,0:T(8,128)(2,1)S(1)} %collective-permute-done.4.refs_5_) | copy-start | bytes 786436
  241.0 54.2 %all-to-all-start.3 = ((bf16[32,1,2,128,128]{4,3,2,1,0:T(8,128)(2,1)}), bf16[32,1,2,128,128]{4,3,2,1,0:T(8,128)(2,1)S(1)}, u32[]{:S(2)}, u32[]{:S(2)}) async-start(bf16[32,1,2,128,128]{4,3,2,1,0:T(8,128)(2,1)} %clean.7), calls=%async_computation.3 | async-start | bytes 4194304 | tf_op jit(solution)/shard_map/all_to_all | solution.py:331
  295.2 1.3 copy-start.1
  (3 other events, 2.2 us)

commit v14 on v13

--- a/solution.py
+++ b/solution.py
@@ -57,6 +57,23 @@
     size = 2 * group * total
     table = np.einsum("tsxzu,cd->tcxzsdu", parts, np.eye(group))
     return table.reshape(size, size).astype(jnp.bfloat16)
+
+
+def row_tables(rows_dev, uv_count, group):
+    total = rows_dev * uv_count
+    position = np.arange(total)
+    phase = 2.0 * np.pi * (np.outer(position, position) % total) / total
+    cosine, sine = np.cos(phase), np.sin(phase)
+    parts = np.array([[cosine, -sine], [sine, cosine]])
+    parts = parts.reshape(2, 2, total, uv_count, rows_dev)
+    eye = np.eye(group)
+    size = 2 * group * total
+    tables = []
+    for at in range(uv_count):
+        order = (at - np.arange(uv_count)) % uv_count
+        table = np.einsum("tsxzu,cd->tcxzsdu", parts[:, :, :, order], eye)
+        tables.append(table.reshape(size, size).astype(jnp.bfloat16))
+    return np.stack(tables)
 
 
 def butterfly8(re, im):
@@ -178,8 +195,8 @@
     )(at, x, jnp.asarray(twiddle_table(length)), jnp.asarray(inner_table(inner)))
 
 
-def clean_kernel(split, waits, at_ref, *refs):
-    *refs, out_ref, slab = refs
+def clean_kernel(split, waits, steps, at_ref, *refs):
+    refs, out_refs, slab = refs[: -1 - steps], refs[-1 - steps : -1], refs[-1]
     *x_refs, basis_ref, basis_t_ref, gain_ref, swap_ref, back_ref = refs[: len(refs) - waits]
     chans = slab.shape[0]
     pair = 2 * LANES
@@ -209,28 +226,31 @@
         front = (gain_ref[:, u : u + 1] * amps).astype(jnp.bfloat16)
         drop = jnp.dot(basis_ref[...], front, preferred_element_type=jnp.float32)
         slab[:, lanes] = (line.astype(jnp.float32) - drop).astype(jnp.bfloat16)
-    out_rows = out_ref.shape[3]
+    out_rows = out_refs[0].shape[3]
     tall = back_ref.shape[0]
     group = tall // rows_dev
-    for b in range(chans // group):
-        channels = slice(b * group, (b + 1) * group)
-        tile = jnp.concatenate(
-            [slab[channels, u * pair : (u + 1) * pair] for u in range(rows_dev)], axis=0
-        )
-        value = jnp.dot(back_ref[...], tile, preferred_element_type=jnp.float32)
-        for part in range(2):
-            half = value[:, part * LANES : (part + 1) * LANES]
-            if out_rows % tall == 0:
-                target, row = divmod(b * tall, out_rows)
-                out_ref[target, 0, part, row : row + tall, :] = half.astype(jnp.bfloat16)
-            else:
-                take = tall // out_rows
-                out_ref[b * take : (b + 1) * take, 0, part] = half.reshape(
-                    take, out_rows, LANES
-                ).astype(jnp.bfloat16)
-
-
-def clean(at, xs, basis, basis_t, gain, targets, rows_dev, slot, slots, before):
+    share = chans // steps
+    for step, out_ref in enumerate(out_refs):
+        start = lax.rem(at_ref[1] + step, steps) * share if steps > 1 else 0
+        for b in range(share // group):
+            channels = pl.ds(pl.multiple_of(start + b * group, group), group)
+            tile = jnp.concatenate(
+                [slab[channels, u * pair : (u + 1) * pair] for u in range(rows_dev)], axis=0
+            )
+            value = jnp.dot(back_ref[...], tile, preferred_element_type=jnp.float32)
+            for part in range(2):
+                half = value[:, part * LANES : (part + 1) * LANES]
+                if out_rows % tall == 0:
+                    target, row = divmod(b * tall, out_rows)
+                    out_ref[target, 0, part, row : row + tall, :] = half.astype(jnp.bfloat16)
+                else:
+                    take = tall // out_rows
+                    out_ref[b * take : (b + 1) * take, 0, part] = half.reshape(
+                        take, out_rows, LANES
+                    ).astype(jnp.bfloat16)
+
+
+def clean(at, xs, basis, basis_t, gain, targets, rows_dev, slot, slots, before, steps=1):
     split = len(xs) > 1
     chans = basis.shape[0]
     sources = len(xs) if split else xs[0].shape[0]
@@ -240,13 +260,19 @@
     vmem = pl.BlockSpec(memory_space=pltpu.VMEM)
     out_rows = chans * rows_dev // targets
     return pl.pallas_call(
-        functools.partial(clean_kernel, split, len(before)),
+        functools.partial(clean_kernel, split, len(before), steps),
         grid=(1,),
         in_specs=[pl.BlockSpec(memory_space=pltpu.SMEM)]
         + [vmem] * (len(xs) + 5)
         + [pl.BlockSpec(memory_space=pl.ANY)] * len(before),
-        out_specs=pl.BlockSpec((targets, 1, 2, out_rows, LANES), lambda i: (0, slot, 0, 0, 0)),
-        out_shape=jax.ShapeDtypeStruct((targets, slots, 2, out_rows, LANES), jnp.bfloat16),
+        out_specs=[
+            pl.BlockSpec((targets // steps, 1, 2, out_rows, LANES), lambda i: (0, slot, 0, 0, 0))
+        ]
+        * steps,
+        out_shape=[
+            jax.ShapeDtypeStruct((targets // steps, slots, 2, out_rows, LANES), jnp.bfloat16)
+        ]
+        * steps,
         input_output_aliases={6 + len(xs): 0} if slot else {},
         scratch_shapes=[pltpu.VMEM((chans, rows_dev * 2 * LANES), jnp.bfloat16)],
         compiler_params=params(),
@@ -311,6 +337,98 @@
     )(x, jnp.asarray(table), jnp.asarray(order), *held)
 
 
+def row_kernel(scale, group, steps, at_ref, *refs):
+    x_refs, table_ref, stage = refs[:steps], refs[steps], refs[-1]
+    out_refs = refs[steps + 1 : -1]
+    targets, _, chans, total, _ = stage.shape
+    tall = x_refs[0].shape[3] // chans * group
+    for target in range(targets):
+        for c in range(chans // group):
+            rows = slice(c * tall, (c + 1) * tall)
+            tile = jnp.concatenate(
+                [x_ref[target, 0, s, rows, :] for x_ref in x_refs for s in range(2)], axis=0
+            )
+            value = jnp.dot(table_ref[...], tile, preferred_element_type=jnp.float32) * scale
+            stage[target, :, c * group : (c + 1) * group] = value.reshape(
+                2, group, total, LANES
+            ).astype(jnp.bfloat16)
+    for step, out_ref in enumerate(out_refs):
+        out_ref[...] = stage[partner(at_ref[0], step, targets)]
+
+
+def row_transform(parts, at, chans, rows_dev, length):
+    steps = len(parts)
+    targets = parts[0].shape[0]
+    total = steps * rows_dev
+    group = min(chans, max(1, 256 // (2 * total)))
+    tables = jnp.asarray(row_tables(rows_dev, steps, group))
+    table = lax.dynamic_index_in_dim(tables, at[1], 0, keepdims=False)
+    vmem = pl.BlockSpec(memory_space=pltpu.VMEM)
+    return pl.pallas_call(
+        functools.partial(row_kernel, 1.0 / math.sqrt(total * length), group, steps),
+        in_specs=[pl.BlockSpec(memory_space=pltpu.SMEM)] + [vmem] * (steps + 1),
+        out_specs=[vmem] * targets,
+        out_shape=[jax.ShapeDtypeStruct((2, chans, total, LANES), jnp.bfloat16)] * targets,
+        scratch_shapes=[pltpu.VMEM((targets, 2, chans, total, LANES), jnp.bfloat16)],
+        compiler_params=params(),
+        name="row_transform",
+    )(at, *parts, table)
+
+
+def place_kernel(count, at_ref, *refs):
+    x_refs, order_ref, out_ref, stage = refs[:count], refs[count], refs[-2], refs[-1]
+    for step, x_ref in enumerate(x_refs):
+        stage[partner(at_ref[0], step, count)] = x_ref[...].reshape(stage.shape[1:])
+    tile = jnp.concatenate([stage[y_lo] for y_lo in range(count)], axis=1)
+    value = jnp.dot(tile, order_ref[...], preferred_element_type=jnp.float32)
+    out_ref[...] = value.astype(jnp.bfloat16).reshape(out_ref.shape)
+
+
+def place(xs, at, chunk, count, held):
+    _, chans, total, _ = xs[0].shape
+    order = order_table()
+    wide = RADIX * LANES
+    block = math.gcd(chans, 4)
+    return pl.pallas_call(
+        functools.partial(place_kernel, len(xs)),
+        grid=(chans // block,),
+        in_specs=[pl.BlockSpec(memory_space=pltpu.SMEM)]
+        + [pl.BlockSpec((2, block, total, LANES), lambda c: (0, c, 0, 0))] * len(xs)
+        + [pl.BlockSpec(order.shape, lambda c: (0, 0))]
+        + [pl.BlockSpec(memory_space=pl.ANY)] * len(held),
+        out_specs=pl.BlockSpec((2, block, total, wide), lambda c: (0, c, 0, chunk)),
+        out_shape=jax.ShapeDtypeStruct((2, chans, total, count * wide), jnp.bfloat16),
+        scratch_shapes=[pltpu.VMEM((len(xs), 2 * block * total, LANES), jnp.bfloat16)],
+        input_output_aliases={2 + len(xs): 0} if held else {},
+        compiler_params=params(),
+        name="place",
+    )(at, *xs, jnp.asarray(order), *held)
+
+
+def hold_kernel(*refs):
+    pass
+
+
+def hold(x, after):
+    untouched = pl.BlockSpec(memory_space=pl.ANY)
+    return pl.pallas_call(
+        hold_kernel,
+        in_specs=[untouched] * (1 + len(after)),
+        out_specs=untouched,
+        out_shape=jax.ShapeDtypeStruct(x.shape, x.dtype),
+        input_output_aliases={0: 0},
+        name="hold",
+    )(x, *after)
+
+
+def spread_rows(parts):
+    count = len(parts)
+    out = list(parts)
+    for step in sorted(range(1, count), key=lambda n: -min(n, count - n)):
+        out[step] = lax.ppermute(parts[step], "uv", [(z, (z + step) % count) for z in range(count)])
+    return out
+
+
 def turn_kernel(basis_ref, out_ref):
     out_ref[...] = basis_ref[...].T
 
@@ -347,29 +465,47 @@
     _, chans, rows_dev, length = visibility.shape
     count = length // chan_count // LANES
     targets = uv_count * chan_count
-    at = lax.axis_index("chan").astype(jnp.int32).reshape(1)
+    at = jnp.stack([lax.axis_index("chan"), lax.axis_index("uv")]).astype(jnp.int32)
     basis = exchange(jnp.broadcast_to(eigen_basis, (chan_count,) + eigen_basis.shape), "chan")
     basis = basis.reshape(chan_count * chans, -1)
     basis_t = turn(basis)
     gain = eigenvalues[:, None] / (eigenvalues[:, None] + noise_power[None, :])
     flat = visibility.reshape(2, chans * rows_dev, length)
+    rows_first = count > 3 and chan_count == RADIX
+    whole = 3 if rows_first else 2
     first = column_transform(flat, at, chan_count, [(0, False)])
     cells = [[exchange(first[0], "chan")]]
+    sends = []
     if count > 1:
-        second, *sends = column_transform(
-            flat, at, chan_count, [(k, k > 1) for k in range(1, count)]
+        sends = column_transform(flat, at, chan_count, [(k, k >= whole) for k in range(1, count)])
+        cells.append([exchange(sends[0], "chan")])
+
+    def cleaned_chunk(k, slot, slots, before, steps=1):
+        return clean(
+            at, cells[k], basis, basis_t, gain, targets, rows_dev, slot, slots, before, steps
         )
-        cells.append([exchange(second, "chan")])
-        cells += [
-            scatter(sends[k * chan_count : (k + 1) * chan_count]) for k in range(count - 2)
-        ]
+
+    before, lines = sends[:1], []
     groups = [[0]] + [g for g in (list(range(1, count - 1)), [count - 1]) if g and count > 1]
-    held, before = [], [second] if count > 1 else []
+    if rows_first:
+        groups = groups[1:]
+        parts = spread_rows(cleaned_chunk(0, 0, 1, before, uv_count))
+        before = []
+        cells.append([exchange(hold(sends[1], [parts[uv_count // 2]]), "chan")])
+        sends = sends[1:]
+        lines = scatter(row_transform(parts, at, chans // uv_count, rows_dev, length))
+    sends = sends[1:]
+    for k in range(len(cells), count):
+        cells.append(scatter(sends[:chan_count]))
+        sends = sends[chan_count:]
+    held = []
     for chunks in groups:
+        if lines and chunks[-1] == count - 1:
+            held = [place(lines, at, 0, count, held)]
         for slot, k in enumerate(chunks):
-            cleaned = clean(
-                at, cells[k], basis, basis_t, gain, targets, rows_dev, slot, len(chunks), before
-            )
+            if rows_first and k == 2:
+                before = before + parts[1:]
+            (cleaned,) = cleaned_chunk(k, slot, len(chunks), before)
             before = [cleaned]
         planes = exchange(cleaned, ("uv", "chan"))
         planes = planes.reshape((uv_count, chan_count) + planes.shape[1:])

time: 307 us -> 305 us (level)
  waiting for transfers between devices: 168 us -> 155 us
  Pallas kernels: 83.6 us -> 87.9 us
  starting transfers between devices: 41 us -> 45.1 us
  local copies, waits for them, and re-layouts: 9.5 us -> 13 us
    all_to_all x6, waiting for transfers between devices: 68.4 us -> 24.7 us  [exchange(): return lax.all_to_all(x, axes, split_axis=0, concat_axis=0, tiled=True)]
    ppermute x0 -> x3, waiting for transfers between devices: none -> 41.3 us  [spread_rows(): lax.ppermute(parts[step], 'uv', [(z, (z + step) % count) for z in range(c...]
    ppermute x14, waiting for transfers between devices: 99.4 us -> 88.6 us  [scatter(): lax.ppermute(pieces[step], 'chan', [(j, int(partner(np.int32(j), step, co...]
    pallas_call x4 -> x7, Pallas kernels: 28.8 us -> 38.7 us  [the longest x4 28.4 us: clean(): pl.pallas_call(functools.partial(clean_kernel, split, len(before), steps)...]
    pallas_call x4 -> x3, Pallas kernels: 25.9 us -> 19.5 us  [image(): pl.pallas_call(functools.partial(image_kernel, scale), grid=(chans // gro...]
    ppermute x0 -> x3, starting transfers between devices: none -> 4.64 us  [spread_rows(): lax.ppermute(parts[step], 'uv', [(z, (z + step) % count) for z in range(c...]
  transfers between devices with their start and end apart: 20 -> 23, of which waited for: 13 -> 12; matrix products, arithmetic and copies ran while one was open for 0% -> 1% of each run, Pallas kernels for 25% -> 25%
where the time goes in v14:
time: 305 us; the launch traced here: 302 us
  waiting for transfers between devices  155 us (51%)
  Pallas kernels  87.9 us (29%)
  starting transfers between devices  45.1 us (15%)
  local copies, waits for them, and re-layouts  13 us (4%)
    ppermute x14, waiting for transfers between devices, scatter(): lax.ppermute(pieces[step], 'chan', [(j, int(partner(np.int32(j), step, co...  88.6 us
    ppermute x3, waiting for transfers between devices, spread_rows(): lax.ppermute(parts[step], 'uv', [(z, (z + step) % count) for z in range(c...  41.3 us
    all_to_all x6, starting transfers between devices, exchange(): return lax.all_to_all(x, axes, split_axis=0, concat_axis=0, tiled=True)  28.5 us
    pallas_call x4, Pallas kernels, clean(): pl.pallas_call(functools.partial(clean_kernel, split, len(before), steps)...  28.4 us
    pallas_call x2, Pallas kernels, column_transform(): pl.pallas_call(functools.partial(column_kernel, chunks, pieces // RADIX),...  27.6 us
    all_to_all x6, waiting for transfers between devices, exchange(): return lax.all_to_all(x, axes, split_axis=0, concat_axis=0, tiled=True)  24.7 us
    pallas_call x3, Pallas kernels, image(): pl.pallas_call(functools.partial(image_kernel, scale), grid=(chans // gro...  19.5 us
    ppermute x14, starting transfers between devices, scatter(): lax.ppermute(pieces[step], 'chan', [(j, int(partner(np.int32(j), step, co...  12 us
  transfers between devices with their start and end apart: 23, of which 12 were waited for; matrix products, arithmetic and copies ran while one was open for 1% of the time, Pallas kernels for 25%

profile of v14, /device:TPU:8, one launch (start us, length us, event | category | flops | bytes accessed | tf_op | source)
XLA Modules:
  0.0 302.4 jit_solution(17642027825683369769)
XLA Ops:
  0.0 1.7 broadcast_in_dim.2
  1.7 3.7 %all-to-all-start = ((bf16[8,64,512]{2,1,0:T(8,128)(2,1)}), bf16[8,64,512]{2,1,0:T(8,128)(2,1)S(1)}, u32[]{:S(2)}, u32[]{:S(2)}) async-start(bf16[8,64,512]{2,1,0:T(8,128)(2,1)} %broadcast_in_dim.2), calls=%async_computation | async-start | bytes 1048576 | tf_op jit(solution)/shard_map/all_to_all | solution.py:449
  6.0 11.3 %column_transform.3 = bf16[8,2,512,128]{3,2,1,0:T(8,128)(2,1)} custom-call(s32[2]{0:T(128)} %pad_add_fusion.at_ref, bf16[2,512,4096]{2,1,0:T(8,128)(2,1)} %bitcast.14, f32[8,2,512]{2,1,0:T(2,128)} %constant.28.clone.twiddle_ref, bf16[1024,1024]{1,0:T(8,128)(2,1)} %constant.29.clone.table_ref), custom_call_target="tpu_custom_call" | custom-call | flops 8589934592 | bytes 16777216 | tf_op jit(solution)/shard_map/column_transform/pallas_call | solution.py:171
  17.3 0.9 copy-done.3
  18.2 4.2 %all-to-all-start.1 = ((bf16[8,2,512,128]{3,2,1,0:T(8,128)(2,1)}), bf16[8,2,512,128]{3,2,1,0:T(8,128)(2,1)S(1)}, u32[]{:S(2)}, u32[]{:S(2)}) async-start(bf16[8,2,512,128]{3,2,1,0:T(8,128)(2,1)} %column_transform.3), calls=%async_computation.1 | async-start | bytes 4194304 | tf_op jit(solution)/shard_map/all_to_all | solution.py:449
  22.4 16.3 %column_transform.2 = (bf16[8,2,512,128]{3,2,1,0:T(8,128)(2,1)}, bf16[8,2,512,128]{3,2,1,0:T(8,128)(2,1)}, bf16[2,512,128]{2,1,0:T(8,128)(2,1)}, bf16[2,512,128]...) custom-call(s32[2]{0:T(128)} %pad_add_fusion.at_ref, ...), custom_call_target="tpu_custom_call" | custom-call | flops 25769803776 | bytes 16777216 | tf_op jit(solution)/shard_map/column_transform/pallas_call | solution.py:171
  38.7 10.3 %all-to-all-done.1.refs_0_ = bf16[8,2,512,128]{3,2,1,0:T(8,128)(2,1)S(1)} async-done(((bf16[8,2,512,128]{3,2,1,0:T(8,128)(2,1)}), bf16[8,2,512,128]{3,2,1,0:T(8,128)(2,1)S(1)}, u32[]{:S(2)}, u32[]{:S(2)}) %all-to-all-start.1) | async-done | bytes 2097184 | tf_op jit(solution)/shard_map/all_to_all | solution.py:449
  49.1 1.4 copy-done.5
  50.4 3.6 %all-to-all-start.3 = ((bf16[8,2,512,128]{3,2,1,0:T(8,128)(2,1)}), bf16[8,2,512,128]{3,2,1,0:T(8,128)(2,1)S(1)}, u32[]{:S(2)}, u32[]{:S(2)}) async-start(bf16[8,2,512,128]{3,2,1,0:T(8,128)(2,1)} %get-tuple-element.36.refs_6_), calls=%async_computation.3 | async-start | bytes 4194304 | tf_op jit(solution)/shard_map/all_to_all | solution.py:449
  54.1 0.9 add_divide_fusion.refs_3_.refs_10_
  54.9 2.0 turn.1.refs_2_.refs_9_
  56.9 6.9 %clean.4 = (bf16[8,1,2,128,128]{4,3,2,1,0:T(8,128)(2,1)}, bf16[8,1,2,128,128]{4,3,2,1,0:T(8,128)(2,1)}, bf16[8,1,2,128,128]{4,3,2,1,0:T(8,128)(2,1)}, bf16[8,1,2,128,128]{4,3,2,1,0:T(8,128)(2,1)}) custom-call(s32[2]{0:T(128)} %pad_add_fusion.at_ref, bf16[8,2,512,128]{3,2,1,0:T(8,128)(2,1)} %copy-done.5, bf16[512,512]{1,0:T(8,128)(2,1)} %bitcast.10, ...), custom_call_target="tpu_custom_call" | custom-call | flops 3221225472 | bytes 4194304 | tf_op jit(solution)/shard_map/clean/pallas_call | solution.py:262
  63.8 2.6 collective-permute-start.7
  66.4 23.1 %collective-permute-done.7.refs_1_.refs_8_.refs_2_ = bf16[8,1,2,128,128]{4,3,2,1,0:T(8,128)(2,1)S(1)} collective-permute-done((bf16[8,1,2,128,128]{4,3,2,1,0:T(8,128)(2,1)}, bf16[8,1,2,128,128]{4,3,2,1,0:T(8,128)(2,1)S(1)}, u32[]{:S(2)}, u32[]{:S(2)}) %collective-permute-start.7) | collective-permute-done | bytes 524320 | tf_op jit(solution)/shard_map/ppermute | solution.py:428
  89.6 0.8 copy-done.2
  90.4 1.4 copy-done.4
  91.8 3.9 %all-to-all-start.2 = ((bf16[8,2,512,128]{3,2,1,0:T(8,128)(2,1)}), bf16[8,2,512,128]{3,2,1,0:T(8,128)(2,1)S(1)}, u32[]{:S(2)}, u32[]{:S(2)}) async-start(bf16[8,2,512,128]{3,2,1,0:T(8,128)(2,1)} %hold.1), calls=%async_computation.2 | async-start | bytes 4194304 | tf_op jit(solution)/shard_map/all_to_all | solution.py:449
  95.7 2.0 collective-permute-start.9
  97.7 7.1 %clean.5.refs_6_ = bf16[32,2,2,128,128]{4,3,2,1,0:T(8,128)(2,1)} custom-call(s32[2]{0:T(128)} %pad_add_fusion.at_ref, bf16[8,2,512,128]{3,2,1,0:T(8,128)(2,1)} %copy-done.4, bf16[512,512]{1,0:T(8,128)(2,1)} %bitcast.11, bf16[512,512]{1,0:T(8,128)(2,1)} %turn.1.refs_2_.refs_9_, f32[512,8]{1,0:T(8,128)} %add_divide_fusion.refs_3_.refs_10_, ...), custom_call_target="tpu_custom_call" | custom-call | flops 3221225472 | bytes 4194304 | tf_op jit(solution)/shard_map/clean/pallas_call | solution.py:262
  104.8 5.8 %collective-permute-done.8.refs_7_.refs_1_ = bf16[8,1,2,128,128]{4,3,2,1,0:T(8,128)(2,1)S(1)} collective-permute-done((bf16[8,1,2,128,128]{4,3,2,1,0:T(8,128)(2,1)}, bf16[8,1,2,128,128]{4,3,2,1,0:T(8,128)(2,1)S(1)}, u32[]{:S(2)}, u32[]{:S(2)}) %collective-permute-start.8) | collective-permute-done | bytes 524320 | tf_op jit(solution)/shard_map/ppermute | solution.py:428
  110.6 12.4 %collective-permute-done.9.refs_9_.refs_3_ = bf16[8,1,2,128,128]{4,3,2,1,0:T(8,128)(2,1)S(1)} collective-permute-done((bf16[8,1,2,128,128]{4,3,2,1,0:T(8,128)(2,1)}, bf16[8,1,2,128,128]{4,3,2,1,0:T(8,128)(2,1)S(1)}, u32[]{:S(2)}, u32[]{:S(2)}) %collective-permute-start.9) | collective-permute-done | bytes 524320 | tf_op jit(solution)/shard_map/ppermute | solution.py:428
  123.0 0.8 copy-done.7
  123.8 1.4 copy-done.1
  125.2 7.1 %clean.6.refs_13_ = bf16[32,2,2,128,128]{4,3,2,1,0:T(8,128)(2,1)} custom-call(s32[2]{0:T(128)} %pad_add_fusion.at_ref, bf16[8,2,512,128]{3,2,1,0:T(8,128)(2,1)} %copy-done.1, bf16[512,512]{1,0:T(8,128)(2,1)} %bitcast.12, bf16[512,512]{1,0:T(8,128)(2,1)} %turn.1.refs_2_.refs_9_, ...), custom_call_target="tpu_custom_call", output_to_operand_aliasing={{}: (7, {})} | custom-call | flops 3221225472 | bytes 4194304 | tf_op jit(solution)/shard_map/clean/pallas_call | solution.py:262
  132.3 5.6 %all-to-all-start.5 = ((bf16[32,2,2,128,128]{4,3,2,1,0:T(8,128)(2,1)}), bf16[32,2,2,128,128]{4,3,2,1,0:T(8,128)(2,1)}, u32[]{:S(2)}, u32[]{:S(2)}) async-start(bf16[32,2,2,128,128]{4,3,2,1,0:T(8,128)(2,1)} %clean.6.refs_13_), calls=%async_computation.5 | async-start | bytes 8388608 | tf_op jit(solution)/shard_map/all_to_all | solution.py:449
  137.9 2.2 collective-permute-start
  140.6 1.1 collective-permute-start.2
  142.3 1.2 collective-permute-start.4
  143.6 31.2 %collective-permute-done.refs_1_ = bf16[2,512,128]{2,1,0:T(8,128)(2,1)S(1)} collective-permute-done((bf16[2,512,128]{2,1,0:T(8,128)(2,1)S(1)}, bf16[2,512,128]{2,1,0:T(8,128)(2,1)S(1)}, u32[]{:S(2)}, u32[]{:S(2)}) %collective-permute-start) | collective-permute-done | bytes 262176 | tf_op jit(solution)/shard_map/ppermute | solution.py:455
  174.8 20.0 %collective-permute-done.1.refs_2_ = bf16[2,512,128]{2,1,0:T(8,128)(2,1)S(1)} collective-permute-done((bf16[2,512,128]{2,1,0:T(8,128)(2,1)S(1)}, bf16[2,512,128]{2,1,0:T(8,128)(2,1)S(1)}, u32[]{:S(2)}, u32[]{:S(2)}) %collective-permute-start.1) | collective-permute-done | bytes 262176 | tf_op jit(solution)/shard_map/ppermute | solution.py:455
  194.8 4.0 %collective-permute-done.3.refs_4_ = bf16[2,512,128]{2,1,0:T(8,128)(2,1)S(1)} collective-permute-done((bf16[2,512,128]{2,1,0:T(8,128)(2,1)S(1)}, bf16[2,512,128]{2,1,0:T(8,128)(2,1)S(1)}, u32[]{:S(2)}, u32[]{:S(2)}) %collective-permute-start.3) | collective-permute-done | bytes 262176 | tf_op jit(solution)/shard_map/ppermute | solution.py:455
  198.8 1.9 collective-permute-done.4.refs_5_
  200.7 6.1 %collective-permute-done.5.refs_6_ = bf16[2,512,128]{2,1,0:T(8,128)(2,1)S(1)} collective-permute-done((bf16[2,512,128]{2,1,0:T(8,128)(2,1)S(1)}, bf16[2,512,128]{2,1,0:T(8,128)(2,1)S(1)}, u32[]{:S(2)}, u32[]{:S(2)}) %collective-permute-start.5) | collective-permute-done | bytes 262176 | tf_op jit(solution)/shard_map/ppermute | solution.py:455
  207.6 7.3 %clean.7 = bf16[32,1,2,128,128]{4,3,2,1,0:T(8,128)(2,1)} custom-call(s32[2]{0:T(128)} %pad_add_fusion.at_ref, bf16[2,512,128]{2,1,0:T(8,128)(2,1)} %get-tuple-element.27.refs_0_, bf16[2,512,128]{2,1,0:T(8,128)(2,1)} %copy-done.24, bf16[2,512,128]{2,1,0:T(8,128)(2,1)} %copy-done.25, bf16[2,512,128]{2,1,0:T(8,128)(2,1)} %copy-done.26, ...), custom_call_target="tpu_custom_call" | custom-call | flops 3221225472 | bytes 4194304 | tf_op jit(solution)/shard_map/clean/pallas_call | solution.py:262
  214.9 14.3 %all-to-all-done.5 = bf16[32,2,2,128,128]{4,3,2,1,0:T(8,128)(2,1)} async-done(((bf16[32,2,2,128,128]{4,3,2,1,0:T(8,128)(2,1)}), bf16[32,2,2,128,128]{4,3,2,1,0:T(8,128)(2,1)}, u32[]{:S(2)}, u32[]{:S(2)}) %all-to-all-start.5) | async-done | bytes 4194336 | tf_op jit(solution)/shard_map/all_to_all | solution.py:449
  229.2 7.6 %all-to-all-start.4 = ((bf16[32,1,2,128,128]{4,3,2,1,0:T(8,128)(2,1)}), bf16[32,1,2,128,128]{4,3,2,1,0:T(8,128)(2,1)S(1)}, u32[]{:S(2)}, u32[]{:S(2)}) async-start(bf16[32,1,2,128,128]{4,3,2,1,0:T(8,128)(2,1)} %clean.7), calls=%async_computation.4 | async-start | bytes 4194304 | tf_op jit(solution)/shard_map/all_to_all | solution.py:449
  236.8 1.6 dynamic-slice_bitcast_fusion.refs_4_
  238.4 4.1 %row_transform.1 = (bf16[2,16,32,128]{3,2,1,0:T(8,128)(2,1)}, bf16[2,16,32,128]{3,2,1,0:T(8,128)(2,1)}, bf16[2,16,32,128]{3,2,1,0:T(8,128)(2,1)}, bf16[2,16,32,1...) custom-call(s32[2]{0:T(128)} %pad_add_fusion.at_ref, ...), custom_call_target="tpu_custom_call" | custom-call | tf_op jit(solution)/shard_map/row_transform/pallas_call | solution.py:367
  242.5 2.1 collective-permute-start.10
  245.2 1.1 collective-permute-start.12
  246.9 1.2 collective-permute-start.14
  248.1 13.4 %collective-permute-done.10.refs_1_ = bf16[2,16,32,128]{3,2,1,0:T(8,128)(2,1)S(1)} collective-permute-done((bf16[2,16,32,128]{3,2,1,0:T(8,128)(2,1)}, bf16[2,16,32,128]{3,2,1,0:T(8,128)(2,1)S(1)}, u32[]{:S(2)}, u32[]{:S(2)}) %collective-permute-start.10) | collective-permute-done | bytes 262176 | tf_op jit(solution)/shard_map/ppermute | solution.py:455
  262.2 11.9 %collective-permute-done.11.refs_2_ = bf16[2,16,32,128]{3,2,1,0:T(8,128)(2,1)S(1)} collective-permute-done((bf16[2,16,32,128]{3,2,1,0:T(8,128)(2,1)}, bf16[2,16,32,128]{3,2,1,0:T(8,128)(2,1)S(1)}, u32[]{:S(2)}, u32[]{:S(2)}) %collective-permute-start.11) | collective-permute-done | bytes 262176 | tf_op jit(solution)/shard_map/ppermute | solution.py:455
  274.2 6.6 %image.3.refs_0_ = bf16[2,16,32,4096]{3,2,1,0:T(8,128)(2,1)} custom-call(bf16[4,8,2,2,128,128]{5,4,3,2,1,0:T(8,128)(2,1)} %bitcast.6.x_ref, bf16[256,256]{1,0:T(8,128)(2,1)} %constant.33.clone.table_ref, bf16[1024,1024]{1,0:T(8,128)(2,1)} %constant.34.clone.order_ref.refs_8_), custom_call_target="tpu_custom_call" | custom-call | flops 2147483648 | bytes 4194304 | tf_op jit(solution)/shard_map/image/pallas_call | solution.py:314
  280.8 6.5 %image.4.refs_9_ = bf16[2,16,32,4096]{3,2,1,0:T(8,128)(2,1)} custom-call(bf16[4,8,2,2,128,128]{5,4,3,2,1,0:T(8,128)(2,1)} %bitcast.6.x_ref, bf16[256,256]{1,0:T(8,128)(2,1)} %constant.33.clone.table_ref, bf16[1024,1024]{1,0:T(8,128)(2,1)} %constant.34.clone.order_ref.refs_8_, bf16[2,16,32,4096]{3,2,1,0:T(8,128)(2,1)} %image.3.refs_0_), custom_call_target="tpu_custom_call", output_to_operand_aliasing={{}: (3, {})} | custom-call | flops 2147483648 | bytes 4194304 | tf_op jit(solution)/shard_map/image/pallas_call | solution.py:314
  288.4 6.2 %place.1.refs_0_ = bf16[2,16,32,4096]{3,2,1,0:T(8,128)(2,1)} custom-call(s32[2]{0:T(128)} %pad_add_fusion.at_ref, bf16[2,16,32,128]{3,2,1,0:T(8,128)(2,1)} %get-tuple-element.41.refs_0_, bf16[2,16,32,128]{3,2,1,0:T(8,128)(2,1)} %copy-done.8, bf16[2,16,32,128]{3,2,1,0:T(8,128)(2,1)} %copy-done.9, ...), custom_call_target="tpu_custom_call", output_to_operand_aliasing={{}: (10, {})} | custom-call | tf_op jit(solution)/shard_map/place/pallas_call | solution.py:392
  294.6 1.3 copy-done
  296.0 6.4 %image.5 = bf16[2,16,32,4096]{3,2,1,0:T(8,128)(2,1)} custom-call(bf16[4,8,1,2,128,128]{5,4,3,2,1,0:T(8,128)(2,1)} %bitcast.8, bf16[256,256]{1,0:T(8,128)(2,1)} %constant.33.clone.table_ref, bf16[1024,1024]{1,0:T(8,128)(2,1)} %constant.34.clone.order_ref.refs_8_, bf16[2,16,32,4096]{3,2,1,0:T(8,128)(2,1)} %place.1.refs_0_), custom_call_target="tpu_custom_call", output_to_operand_aliasing={{}: (3, {})} | custom-call | flops 2147483648 | bytes 4194304 | tf_op jit(solution)/shard_map/image/pallas_call | solution.py:314
  (77 shorter events, 5.4 us)
Async XLA Ops:
  1.7 15.7 %all-to-all-start = ((bf16[8,64,512]{2,1,0:T(8,128)(2,1)}), bf16[8,64,512]{2,1,0:T(8,128)(2,1)S(1)}, u32[]{:S(2)}, u32[]{:S(2)}) async-start(bf16[8,64,512]{2,1,0:T(8,128)(2,1)} %broadcast_in_dim.2), calls=%async_computation | async-start | bytes 1048576 | tf_op jit(solution)/shard_map/all_to_all | solution.py:449
  17.3 0.9 copy-start.3
  18.2 30.8 %all-to-all-start.1 = ((bf16[8,2,512,128]{3,2,1,0:T(8,128)(2,1)}), bf16[8,2,512,128]{3,2,1,0:T(8,128)(2,1)S(1)}, u32[]{:S(2)}, u32[]{:S(2)}) async-start(bf16[8,2,512,128]{3,2,1,0:T(8,128)(2,1)} %column_transform.3), calls=%async_computation.1 | async-start | bytes 4194304 | tf_op jit(solution)/shard_map/all_to_all | solution.py:449
  49.0 1.4 copy-start.5
  49.0 5.0 %copy-start.15 = (f32[512]{0:T(512)S(1)}, f32[512]{0:T(512)}, u32[]{:S(2)}) copy-start(f32[512]{0:T(512)} %param.26) | copy-start | bytes 6148
  49.1 5.0 %copy-start.16 = (f32[8]{0:T(128)S(1)}, f32[8]{0:T(128)}, u32[]{:S(2)}) copy-start(f32[8]{0:T(128)} %param.27) | copy-start | bytes 100
  50.4 40.0 %all-to-all-start.3 = ((bf16[8,2,512,128]{3,2,1,0:T(8,128)(2,1)}), bf16[8,2,512,128]{3,2,1,0:T(8,128)(2,1)S(1)}, u32[]{:S(2)}, u32[]{:S(2)}) async-start(bf16[8,2,512,128]{3,2,1,0:T(8,128)(2,1)} %get-tuple-element.36.refs_6_), calls=%async_computation.3 | async-start | bytes 4194304 | tf_op jit(solution)/shard_map/all_to_all | solution.py:449
  63.8 25.8 %collective-permute-start.7 = (bf16[8,1,2,128,128]{4,3,2,1,0:T(8,128)(2,1)}, bf16[8,1,2,128,128]{4,3,2,1,0:T(8,128)(2,1)S(1)}, u32[]{:S(2)}, u32[]{:S(2)}) collective-permute-start(bf16[8,1,2,128,128]{4,3,2,1,0:T(8,128)(2,1)} %get-tuple-element.37), channel_id=1, source_target_pairs={{0,16},{8,24},{16,0},{24,8},{1,17},{9,25},{17,1},{25,9},{2,18},{10... | collective-permute-start | bytes 1572872 | tf_op jit(solution)/shard_map/ppermute | solution.py:428
  90.4 1.4 copy-start.4
  91.8 31.2 %all-to-all-start.2 = ((bf16[8,2,512,128]{3,2,1,0:T(8,128)(2,1)}), bf16[8,2,512,128]{3,2,1,0:T(8,128)(2,1)S(1)}, u32[]{:S(2)}, u32[]{:S(2)}) async-start(bf16[8,2,512,128]{3,2,1,0:T(8,128)(2,1)} %hold.1), calls=%async_computation.2 | async-start | bytes 4194304 | tf_op jit(solution)/shard_map/all_to_all | solution.py:449
  95.6 14.9 %collective-permute-start.8 = (bf16[8,1,2,128,128]{4,3,2,1,0:T(8,128)(2,1)}, bf16[8,1,2,128,128]{4,3,2,1,0:T(8,128)(2,1)S(1)}, u32[]{:S(2)}, u32[]{:S(2)}) collective-permute-start(bf16[8,1,2,128,128]{4,3,2,1,0:T(8,128)(2,1)} %get-tuple-element.38), channel_id=1, source_target_pairs={{0,8},{8,16},{16,24},{24,0},{1,9},{9,17},{17,25},{25,1},{2,10},{10... | collective-permute-start | bytes 1572872 | tf_op jit(solution)/shard_map/ppermute | solution.py:428
  95.7 27.3 %collective-permute-start.9 = (bf16[8,1,2,128,128]{4,3,2,1,0:T(8,128)(2,1)}, bf16[8,1,2,128,128]{4,3,2,1,0:T(8,128)(2,1)S(1)}, u32[]{:S(2)}, u32[]{:S(2)}) collective-permute-start(bf16[8,1,2,128,128]{4,3,2,1,0:T(8,128)(2,1)} %get-tuple-element.39), channel_id=1, source_target_pairs={{0,24},{8,0},{16,8},{24,16},{1,25},{9,1},{17,9},{25,17},{2,26},{10... | collective-permute-start | bytes 1572872 | tf_op jit(solution)/shard_map/ppermute | solution.py:428
  110.6 12.4 %copy-start.6 = (bf16[8,1,2,128,128]{4,3,2,1,0:T(8,128)(2,1)}, bf16[8,1,2,128,128]{4,3,2,1,0:T(8,128)(2,1)S(1)}, u32[]{:S(2)}) copy-start(bf16[8,1,2,128,128]{4,3,2,1,0:T(8,128)(2,1)S(1)} %collective-permute-done.8.refs_7_.refs_1_) | copy-start | bytes 1572868
  123.8 1.4 copy-start.1
  132.2 5.6 %copy-start.23 = (bf16[2,512,128]{2,1,0:T(8,128)(2,1)S(1)}, bf16[2,512,128]{2,1,0:T(8,128)(2,1)}, u32[]{:S(2)}) copy-start(bf16[2,512,128]{2,1,0:T(8,128)(2,1)} %get-tuple-element.28) | copy-start | bytes 786436
  132.2 7.8 %copy-start.22 = (bf16[2,512,128]{2,1,0:T(8,128)(2,1)S(1)}, bf16[2,512,128]{2,1,0:T(8,128)(2,1)}, u32[]{:S(2)}) copy-start(bf16[2,512,128]{2,1,0:T(8,128)(2,1)} %get-tuple-element.29) | copy-start | bytes 786436
  132.2 8.4 %copy-start.21 = (bf16[2,512,128]{2,1,0:T(8,128)(2,1)S(1)}, bf16[2,512,128]{2,1,0:T(8,128)(2,1)}, u32[]{:S(2)}) copy-start(bf16[2,512,128]{2,1,0:T(8,128)(2,1)} %get-tuple-element.30) | copy-start | bytes 786436
  132.2 9.5 %copy-start.20 = (bf16[2,512,128]{2,1,0:T(8,128)(2,1)S(1)}, bf16[2,512,128]{2,1,0:T(8,128)(2,1)}, u32[]{:S(2)}) copy-start(bf16[2,512,128]{2,1,0:T(8,128)(2,1)} %get-tuple-element.31) | copy-start | bytes 786436
  132.3 10.1 %copy-start.19 = (bf16[2,512,128]{2,1,0:T(8,128)(2,1)S(1)}, bf16[2,512,128]{2,1,0:T(8,128)(2,1)}, u32[]{:S(2)}) copy-start(bf16[2,512,128]{2,1,0:T(8,128)(2,1)} %get-tuple-element.32) | copy-start | bytes 786436
  132.3 42.5 %copy-start.18 = (bf16[2,512,128]{2,1,0:T(8,128)(2,1)S(1)}, bf16[2,512,128]{2,1,0:T(8,128)(2,1)}, u32[]{:S(2)}) copy-start(bf16[2,512,128]{2,1,0:T(8,128)(2,1)} %get-tuple-element.33) | copy-start | bytes 786436
  132.3 62.5 %copy-start.17 = (bf16[2,512,128]{2,1,0:T(8,128)(2,1)S(1)}, bf16[2,512,128]{2,1,0:T(8,128)(2,1)}, u32[]{:S(2)}) copy-start(bf16[2,512,128]{2,1,0:T(8,128)(2,1)} %get-tuple-element.34) | copy-start | bytes 786436
  132.3 97.0 %all-to-all-start.5 = ((bf16[32,2,2,128,128]{4,3,2,1,0:T(8,128)(2,1)}), bf16[32,2,2,128,128]{4,3,2,1,0:T(8,128)(2,1)}, u32[]{:S(2)}, u32[]{:S(2)}) async-start(bf16[32,2,2,128,128]{4,3,2,1,0:T(8,128)(2,1)} %clean.6.refs_13_), calls=%async_computation.5 | async-start | bytes 8388608 | tf_op jit(solution)/shard_map/all_to_all | solution.py:449
  137.9 36.9 %collective-permute-start = (bf16[2,512,128]{2,1,0:T(8,128)(2,1)S(1)}, bf16[2,512,128]{2,1,0:T(8,128)(2,1)S(1)}, u32[]{:S(2)}, u32[]{:S(2)}) collective-permute-start(bf16[2,512,128]{2,1,0:T(8,128)(2,1)S(1)} %copy-done.23), channel_id=1, source_target_pairs={{0,7},{1,6},{2,5},{3,4},{4,3},{5,2},{6,1},{7,0},{8,15},{9,14},{10,... | collective-permute-start | bytes 786440 | tf_op jit(solution)/shard_map/ppermute | solution.py:455
  140.1 54.7 %collective-permute-start.1 = (bf16[2,512,128]{2,1,0:T(8,128)(2,1)S(1)}, bf16[2,512,128]{2,1,0:T(8,128)(2,1)S(1)}, u32[]{:S(2)}, u32[]{:S(2)}) collective-permute-start(bf16[2,512,128]{2,1,0:T(8,128)(2,1)S(1)} %copy-done.22), channel_id=1, source_target_pairs={{0,6},{1,7},{2,4},{3,5},{4,2},{5,3},{6,0},{7,1},{8,14},{9,15},{10,... | collective-permute-start | bytes 786440 | tf_op jit(solution)/shard_map/ppermute | solution.py:455
  140.6 54.2 %collective-permute-start.2 = (bf16[2,512,128]{2,1,0:T(8,128)(2,1)S(1)}, bf16[2,512,128]{2,1,0:T(8,128)(2,1)S(1)}, u32[]{:S(2)}, u32[]{:S(2)}) collective-permute-start(bf16[2,512,128]{2,1,0:T(8,128)(2,1)S(1)} %copy-done.21), channel_id=1, source_target_pairs={{0,5},{1,4},{2,7},{3,6},{4,1},{5,0},{6,3},{7,2},{8,13},{9,12},{10,... | collective-permute-start | bytes 786440 | tf_op jit(solution)/shard_map/ppermute | solution.py:455
  141.8 57.1 %collective-permute-start.3 = (bf16[2,512,128]{2,1,0:T(8,128)(2,1)S(1)}, bf16[2,512,128]{2,1,0:T(8,128)(2,1)S(1)}, u32[]{:S(2)}, u32[]{:S(2)}) collective-permute-start(bf16[2,512,128]{2,1,0:T(8,128)(2,1)S(1)} %copy-done.20), channel_id=1, source_target_pairs={{0,4},{1,5},{2,6},{3,7},{4,0},{5,1},{6,2},{7,3},{8,12},{9,13},{10,... | collective-permute-start | bytes 786440 | tf_op jit(solution)/shard_map/ppermute | solution.py:455
  142.3 58.4 %collective-permute-start.4 = (bf16[2,512,128]{2,1,0:T(8,128)(2,1)S(1)}, bf16[2,512,128]{2,1,0:T(8,128)(2,1)S(1)}, u32[]{:S(2)}, u32[]{:S(2)}) collective-permute-start(bf16[2,512,128]{2,1,0:T(8,128)(2,1)S(1)} %copy-done.19), channel_id=1, source_target_pairs={{0,3},{1,2},{2,1},{3,0},{4,7},{5,6},{6,5},{7,4},{8,11},{9,10},{10,... | collective-permute-start | bytes 786440 | tf_op jit(solution)/shard_map/ppermute | solution.py:455
  174.8 32.0 %copy-start.24 = (bf16[2,512,128]{2,1,0:T(8,128)(2,1)}, bf16[2,512,128]{2,1,0:T(8,128)(2,1)S(1)}, u32[]{:S(2)}) copy-start(bf16[2,512,128]{2,1,0:T(8,128)(2,1)S(1)} %collective-permute-done.refs_1_) | copy-start | bytes 786436
  174.8 32.0 %collective-permute-start.5 = (bf16[2,512,128]{2,1,0:T(8,128)(2,1)S(1)}, bf16[2,512,128]{2,1,0:T(8,128)(2,1)S(1)}, u32[]{:S(2)}, u32[]{:S(2)}) collective-permute-start(bf16[2,512,128]{2,1,0:T(8,128)(2,1)S(1)} %copy-done.18), channel_id=1, source_target_pairs={{0,2},{1,3},{2,0},{3,1},{4,6},{5,7},{6,4},{7,5},{8,10},{9,11},{10,... | collective-permute-start | bytes 786440 | tf_op jit(solution)/shard_map/ppermute | solution.py:455
  194.8 12.0 %copy-start.25 = (bf16[2,512,128]{2,1,0:T(8,128)(2,1)}, bf16[2,512,128]{2,1,0:T(8,128)(2,1)S(1)}, u32[]{:S(2)}) copy-start(bf16[2,512,128]{2,1,0:T(8,128)(2,1)S(1)} %collective-permute-done.1.refs_2_) | copy-start | bytes 786436
  194.8 12.0 %collective-permute-start.6 = (bf16[2,512,128]{2,1,0:T(8,128)(2,1)S(1)}, bf16[2,512,128]{2,1,0:T(8,128)(2,1)S(1)}, u32[]{:S(2)}, u32[]{:S(2)}) collective-permute-start(bf16[2,512,128]{2,1,0:T(8,128)(2,1)S(1)} %copy-done.17), channel_id=1, source_target_pairs={{0,1},{1,0},{2,3},{3,2},{4,5},{5,4},{6,7},{7,6},{8,9},{9,8},{10,11... | collective-permute-start | bytes 786440 | tf_op jit(solution)/shard_map/ppermute | solution.py:455
  194.8 12.0 %copy-start.26 = (bf16[2,512,128]{2,1,0:T(8,128)(2,1)}, bf16[2,512,128]{2,1,0:T(8,128)(2,1)S(1)}, u32[]{:S(2)}) copy-start(bf16[2,512,128]{2,1,0:T(8,128)(2,1)S(1)} %collective-permute-done.2.refs_3_) | copy-start | bytes 786436
  198.8 8.0 %copy-start.27 = (bf16[2,512,128]{2,1,0:T(8,128)(2,1)}, bf16[2,512,128]{2,1,0:T(8,128)(2,1)S(1)}, u32[]{:S(2)}) copy-start(bf16[2,512,128]{2,1,0:T(8,128)(2,1)S(1)} %collective-permute-done.3.refs_4_) | copy-start | bytes 786436
  200.7 6.1 %copy-start.28 = (bf16[2,512,128]{2,1,0:T(8,128)(2,1)}, bf16[2,512,128]{2,1,0:T(8,128)(2,1)S(1)}, u32[]{:S(2)}) copy-start(bf16[2,512,128]{2,1,0:T(8,128)(2,1)S(1)} %collective-permute-done.4.refs_5_) | copy-start | bytes 786436
  229.2 65.4 %all-to-all-start.4 = ((bf16[32,1,2,128,128]{4,3,2,1,0:T(8,128)(2,1)}), bf16[32,1,2,128,128]{4,3,2,1,0:T(8,128)(2,1)S(1)}, u32[]{:S(2)}, u32[]{:S(2)}) async-start(bf16[32,1,2,128,128]{4,3,2,1,0:T(8,128)(2,1)} %clean.7), calls=%async_computation.4 | async-start | bytes 4194304 | tf_op jit(solution)/shard_map/all_to_all | solution.py:449
  242.5 19.1 %collective-permute-start.10 = (bf16[2,16,32,128]{3,2,1,0:T(8,128)(2,1)}, bf16[2,16,32,128]{3,2,1,0:T(8,128)(2,1)S(1)}, u32[]{:S(2)}, u32[]{:S(2)}) collective-permute-start(bf16[2,16,32,128]{3,2,1,0:T(8,128)(2,1)} %get-tuple-element.42), channel_id=1, source_target_pairs={{0,7},{1,6},{2,5},{3,4},{4,3},{5,2},{6,1},{7,0},{8,15},{9,14},{10,... | collective-permute-start | bytes 786440 | tf_op jit(solution)/shard_map/ppermute | solution.py:455
  244.6 29.5 %collective-permute-start.11 = (bf16[2,16,32,128]{3,2,1,0:T(8,128)(2,1)}, bf16[2,16,32,128]{3,2,1,0:T(8,128)(2,1)S(1)}, u32[]{:S(2)}, u32[]{:S(2)}) collective-permute-start(bf16[2,16,32,128]{3,2,1,0:T(8,128)(2,1)} %get-tuple-element.43), channel_id=1, source_target_pairs={{0,6},{1,7},{2,4},{3,5},{4,2},{5,3},{6,0},{7,1},{8,14},{9,15},{10,... | collective-permute-start | bytes 786440 | tf_op jit(solution)/shard_map/ppermute | solution.py:455
  245.2 42.1 %collective-permute-start.12 = (bf16[2,16,32,128]{3,2,1,0:T(8,128)(2,1)}, bf16[2,16,32,128]{3,2,1,0:T(8,128)(2,1)S(1)}, u32[]{:S(2)}, u32[]{:S(2)}) collective-permute-start(bf16[2,16,32,128]{3,2,1,0:T(8,128)(2,1)} %get-tuple-element.44), channel_id=1, source_target_pairs={{0,5},{1,4},{2,7},{3,6},{4,1},{5,0},{6,3},{7,2},{8,13},{9,12},{10,... | collective-permute-start | bytes 786440 | tf_op jit(solution)/shard_map/ppermute | solution.py:455
  246.3 40.9 %collective-permute-start.13 = (bf16[2,16,32,128]{3,2,1,0:T(8,128)(2,1)}, bf16[2,16,32,128]{3,2,1,0:T(8,128)(2,1)S(1)}, u32[]{:S(2)}, u32[]{:S(2)}) collective-permute-start(bf16[2,16,32,128]{3,2,1,0:T(8,128)(2,1)} %get-tuple-element.45), channel_id=1, source_target_pairs={{0,4},{1,5},{2,6},{3,7},{4,0},{5,1},{6,2},{7,3},{8,12},{9,13},{10,... | collective-permute-start | bytes 786440 | tf_op jit(solution)/shard_map/ppermute | solution.py:455
  246.9 40.4 %collective-permute-start.14 = (bf16[2,16,32,128]{3,2,1,0:T(8,128)(2,1)}, bf16[2,16,32,128]{3,2,1,0:T(8,128)(2,1)S(1)}, u32[]{:S(2)}, u32[]{:S(2)}) collective-permute-start(bf16[2,16,32,128]{3,2,1,0:T(8,128)(2,1)} %get-tuple-element.46), channel_id=1, source_target_pairs={{0,3},{1,2},{2,1},{3,0},{4,7},{5,6},{6,5},{7,4},{8,11},{9,10},{10,... | collective-permute-start | bytes 786440 | tf_op jit(solution)/shard_map/ppermute | solution.py:455
  261.6 19.2 %copy-start.8 = (bf16[2,16,32,128]{3,2,1,0:T(8,128)(2,1)}, bf16[2,16,32,128]{3,2,1,0:T(8,128)(2,1)S(1)}, u32[]{:S(2)}) copy-start(bf16[2,16,32,128]{3,2,1,0:T(8,128)(2,1)S(1)} %collective-permute-done.10.refs_1_) | copy-start | bytes 786436
  261.6 25.7 %collective-permute-start.15 = (bf16[2,16,32,128]{3,2,1,0:T(8,128)(2,1)}, bf16[2,16,32,128]{3,2,1,0:T(8,128)(2,1)S(1)}, u32[]{:S(2)}, u32[]{:S(2)}) collective-permute-start(bf16[2,16,32,128]{3,2,1,0:T(8,128)(2,1)} %get-tuple-element.47), channel_id=1, source_target_pairs={{0,2},{1,3},{2,0},{3,1},{4,6},{5,7},{6,4},{7,5},{8,10},{9,11},{10,... | collective-permute-start | bytes 786440 | tf_op jit(solution)/shard_map/ppermute | solution.py:455
  274.2 6.6 %copy-start.9 = (bf16[2,16,32,128]{3,2,1,0:T(8,128)(2,1)}, bf16[2,16,32,128]{3,2,1,0:T(8,128)(2,1)S(1)}, u32[]{:S(2)}) copy-start(bf16[2,16,32,128]{3,2,1,0:T(8,128)(2,1)S(1)} %collective-permute-done.11.refs_2_) | copy-start | bytes 786436
  274.2 13.1 %collective-permute-start.16 = (bf16[2,16,32,128]{3,2,1,0:T(8,128)(2,1)}, bf16[2,16,32,128]{3,2,1,0:T(8,128)(2,1)S(1)}, u32[]{:S(2)}, u32[]{:S(2)}) collective-permute-start(bf16[2,16,32,128]{3,2,1,0:T(8,128)(2,1)} %get-tuple-element.48), channel_id=1, source_target_pairs={{0,1},{1,0},{2,3},{3,2},{4,5},{5,4},{6,7},{7,6},{8,9},{9,8},{10,11... | collective-permute-start | bytes 786440 | tf_op jit(solution)/shard_map/ppermute | solution.py:455
  287.3 0.9 copy-start.12
  287.3 1.0 copy-start.13
  287.3 1.0 copy-start.14
  294.6 1.4 copy-start
  (6 other events, 4.6 us)

commit v15 on v14

--- a/solution.py
+++ b/solution.py
@@ -477,7 +477,10 @@
     cells = [[exchange(first[0], "chan")]]
     sends = []
     if count > 1:
-        sends = column_transform(flat, at, chan_count, [(k, k >= whole) for k in range(1, count)])
+        sends = list(
+            column_transform(flat, at, chan_count, [(k, k >= whole) for k in range(1, count)])
+        )
+        sends[0] = hold(sends[0], [basis_t])
         cells.append([exchange(sends[0], "chan")])
 
     def cleaned_chunk(k, slot, slots, before, steps=1):
@@ -491,7 +494,7 @@
         groups = groups[1:]
         parts = spread_rows(cleaned_chunk(0, 0, 1, before, uv_count))
         before = []
-        cells.append([exchange(hold(sends[1], [parts[uv_count // 2]]), "chan")])
+        cells.append([exchange(hold(sends[1], [parts[1]]), "chan")])
         sends = sends[1:]
         lines = scatter(row_transform(parts, at, chans // uv_count, rows_dev, length))
     sends = sends[1:]
@@ -504,7 +507,9 @@
             held = [place(lines, at, 0, count, held)]
         for slot, k in enumerate(chunks):
             if rows_first and k == 2:
-                before = before + parts[1:]
+                before = before + [parts[uv_count // 2]]
+            if rows_first and k == count - 1:
+                before = before + lines[:1]
             (cleaned,) = cleaned_chunk(k, slot, len(chunks), before)
             before = [cleaned]
         planes = exchange(cleaned, ("uv", "chan"))

time: 305 us -> 317 us (1.039)
  waiting for transfers between devices: 155 us -> 173 us
  starting transfers between devices: 45.1 us -> 40.7 us
    ppermute x3, waiting for transfers between devices: 41.3 us -> 77.2 us  [spread_rows(): lax.ppermute(parts[step], 'uv', [(z, (z + step) % count) for z in range(c...]
    all_to_all x6, waiting for transfers between devices: 24.7 us -> 13 us  [exchange(): return lax.all_to_all(x, axes, split_axis=0, concat_axis=0, tiled=True)]
    ppermute x14, waiting for transfers between devices: 88.6 us -> 82.9 us  [scatter(): lax.ppermute(pieces[step], 'chan', [(j, int(partner(np.int32(j), step, co...]
    unnamed x62 -> x70, local copies, waits for them, and re-layouts: 9.75 us -> 8.15 us
  transfers between devices with their start and end apart: 23 -> 23, of which waited for: 12 -> 10; matrix products, arithmetic and copies ran while one was open for 1% -> 1% of each run, Pallas kernels for 25% -> 24%
where the time goes in v15:
time: 317 us; the launch traced here: 315 us
  waiting for transfers between devices  173 us (55%)
  Pallas kernels  87.8 us (28%)
  starting transfers between devices  40.7 us (13%)
  local copies, waits for them, and re-layouts  11.6 us (4%)
    ppermute x14, waiting for transfers between devices, scatter(): lax.ppermute(pieces[step], 'chan', [(j, int(partner(np.int32(j), step, co...  82.9 us
    ppermute x3, waiting for transfers between devices, spread_rows(): lax.ppermute(parts[step], 'uv', [(z, (z + step) % count) for z in range(c...  77.2 us
    pallas_call x4, Pallas kernels, clean(): pl.pallas_call(functools.partial(clean_kernel, split, len(before), steps)...  28.3 us
    pallas_call x2, Pallas kernels, column_transform(): pl.pallas_call(functools.partial(column_kernel, chunks, pieces // RADIX),...  27.6 us
    all_to_all x6, starting transfers between devices, exchange(): return lax.all_to_all(x, axes, split_axis=0, concat_axis=0, tiled=True)  25.4 us
    pallas_call x3, Pallas kernels, image(): pl.pallas_call(functools.partial(image_kernel, scale), grid=(chans // gro...  19.5 us
    all_to_all x6, waiting for transfers between devices, exchange(): return lax.all_to_all(x, axes, split_axis=0, concat_axis=0, tiled=True)  13 us
    ppermute x14, starting transfers between devices, scatter(): lax.ppermute(pieces[step], 'chan', [(j, int(partner(np.int32(j), step, co...  10.4 us
  transfers between devices with their start and end apart: 23, of which 10 were waited for; matrix products, arithmetic and copies ran while one was open for 1% of the time, Pallas kernels for 24%

profile of v15, /device:TPU:8, one launch (start us, length us, event | category | flops | bytes accessed | tf_op | source)
XLA Modules:
  0.0 315.1 jit_solution(16313106331634991375)
XLA Ops:
  0.0 1.7 broadcast_in_dim.2
  1.7 3.7 %all-to-all-start = ((bf16[8,64,512]{2,1,0:T(8,128)(2,1)}), bf16[8,64,512]{2,1,0:T(8,128)(2,1)S(1)}, u32[]{:S(2)}, u32[]{:S(2)}) async-start(bf16[8,64,512]{2,1,0:T(8,128)(2,1)} %broadcast_in_dim.2), calls=%async_computation | async-start | bytes 1048576 | tf_op jit(solution)/shard_map/all_to_all | solution.py:449
  5.4 0.6 pad_add_fusion.at_ref
  6.0 11.3 %column_transform.3 = bf16[8,2,512,128]{3,2,1,0:T(8,128)(2,1)} custom-call(s32[2]{0:T(128)} %pad_add_fusion.at_ref, bf16[2,512,4096]{2,1,0:T(8,128)(2,1)} %bitcast.14, f32[8,2,512]{2,1,0:T(2,128)} %constant.28.clone.twiddle_ref, bf16[1024,1024]{1,0:T(8,128)(2,1)} %constant.29.clone.table_ref), custom_call_target="tpu_custom_call" | custom-call | flops 8589934592 | bytes 16777216 | tf_op jit(solution)/shard_map/column_transform/pallas_call | solution.py:171
  17.4 0.8 copy-done.2
  18.1 4.2 %all-to-all-start.1 = ((bf16[8,2,512,128]{3,2,1,0:T(8,128)(2,1)}), bf16[8,2,512,128]{3,2,1,0:T(8,128)(2,1)S(1)}, u32[]{:S(2)}, u32[]{:S(2)}) async-start(bf16[8,2,512,128]{3,2,1,0:T(8,128)(2,1)} %column_transform.3), calls=%async_computation.1 | async-start | bytes 4194304 | tf_op jit(solution)/shard_map/all_to_all | solution.py:449
  22.3 16.3 %column_transform.2 = (bf16[8,2,512,128]{3,2,1,0:T(8,128)(2,1)}, bf16[8,2,512,128]{3,2,1,0:T(8,128)(2,1)}, bf16[2,512,128]{2,1,0:T(8,128)(2,1)}, bf16[2,512,128]...) custom-call(s32[2]{0:T(128)} %pad_add_fusion.at_ref, ...), custom_call_target="tpu_custom_call" | custom-call | flops 25769803776 | bytes 16777216 | tf_op jit(solution)/shard_map/column_transform/pallas_call | solution.py:171
  38.7 2.1 turn.1.refs_1_.refs_2_.refs_9_
  40.7 8.3 %all-to-all-done.1.refs_0_ = bf16[8,2,512,128]{3,2,1,0:T(8,128)(2,1)S(1)} async-done(((bf16[8,2,512,128]{3,2,1,0:T(8,128)(2,1)}), bf16[8,2,512,128]{3,2,1,0:T(8,128)(2,1)S(1)}, u32[]{:S(2)}, u32[]{:S(2)}) %all-to-all-start.1) | async-done | bytes 2097184 | tf_op jit(solution)/shard_map/all_to_all | solution.py:449
  49.0 1.4 copy-done.5
  50.3 4.3 %all-to-all-start.3 = ((bf16[8,2,512,128]{3,2,1,0:T(8,128)(2,1)}), bf16[8,2,512,128]{3,2,1,0:T(8,128)(2,1)}, u32[]{:S(2)}, u32[]{:S(2)}) async-start(bf16[8,2,512,128]{3,2,1,0:T(8,128)(2,1)} %hold.2.refs_6_), calls=%async_computation.3 | async-start | bytes 4194304 | tf_op jit(solution)/shard_map/all_to_all | solution.py:449
  54.7 0.9 add_divide_fusion.refs_3_.refs_10_
  55.6 6.8 %clean.4 = (bf16[8,1,2,128,128]{4,3,2,1,0:T(8,128)(2,1)}, bf16[8,1,2,128,128]{4,3,2,1,0:T(8,128)(2,1)}, bf16[8,1,2,128,128]{4,3,2,1,0:T(8,128)(2,1)}, bf16[8,1,2,128,128]{4,3,2,1,0:T(8,128)(2,1)}) custom-call(s32[2]{0:T(128)} %pad_add_fusion.at_ref, bf16[8,2,512,128]{3,2,1,0:T(8,128)(2,1)} %copy-done.5, bf16[512,512]{1,0:T(8,128)(2,1)} %bitcast.10, ...), custom_call_target="tpu_custom_call" | custom-call | flops 3221225472 | bytes 4194304 | tf_op jit(solution)/shard_map/clean/pallas_call | solution.py:262
  62.4 1.6 collective-permute-start.7
  64.0 12.8 %collective-permute-done.7.refs_1_ = bf16[8,1,2,128,128]{4,3,2,1,0:T(8,128)(2,1)S(1)} collective-permute-done((bf16[8,1,2,128,128]{4,3,2,1,0:T(8,128)(2,1)}, bf16[8,1,2,128,128]{4,3,2,1,0:T(8,128)(2,1)S(1)}, u32[]{:S(2)}, u32[]{:S(2)}) %collective-permute-start.7) | collective-permute-done | bytes 524320 | tf_op jit(solution)/shard_map/ppermute | solution.py:428
  76.8 0.8 copy-done.3
  77.7 3.7 %all-to-all-done.3.refs_0_ = bf16[8,2,512,128]{3,2,1,0:T(8,128)(2,1)} async-done(((bf16[8,2,512,128]{3,2,1,0:T(8,128)(2,1)}), bf16[8,2,512,128]{3,2,1,0:T(8,128)(2,1)}, u32[]{:S(2)}, u32[]{:S(2)}) %all-to-all-start.3) | async-done | bytes 2097184 | tf_op jit(solution)/shard_map/all_to_all | solution.py:449
  81.4 3.8 %all-to-all-start.2 = ((bf16[8,2,512,128]{3,2,1,0:T(8,128)(2,1)}), bf16[8,2,512,128]{3,2,1,0:T(8,128)(2,1)S(1)}, u32[]{:S(2)}, u32[]{:S(2)}) async-start(bf16[8,2,512,128]{3,2,1,0:T(8,128)(2,1)} %hold.3), calls=%async_computation.2 | async-start | bytes 4194304 | tf_op jit(solution)/shard_map/all_to_all | solution.py:449
  85.2 2.7 collective-permute-start.8
  87.8 7.1 %clean.5.refs_6_ = bf16[32,2,2,128,128]{4,3,2,1,0:T(8,128)(2,1)} custom-call(s32[2]{0:T(128)} %pad_add_fusion.at_ref, bf16[8,2,512,128]{3,2,1,0:T(8,128)(2,1)} %all-to-all-done.3.refs_0_, bf16[512,512]{1,0:T(8,128)(2,1)} %bitcast.11, bf16[512,512]{1,0:T(8,128)(2,1)} %turn.1.refs_1_.refs_2_.refs_9_, f32[512,8]{1,0:T(8,128)} %add_divide_fusion.refs_3_.refs_10_, ...), custom_call_target="tpu_custom_call" | custom-call | flops 3221225472 | bytes 4194304 | tf_op jit(solution)/shard_map/clean/pallas_call | solution.py:262
  94.9 15.6 %collective-permute-done.8.refs_7_.refs_2_ = bf16[8,1,2,128,128]{4,3,2,1,0:T(8,128)(2,1)S(1)} collective-permute-done((bf16[8,1,2,128,128]{4,3,2,1,0:T(8,128)(2,1)S(1)}, bf16[8,1,2,128,128]{4,3,2,1,0:T(8,128)(2,1)S(1)}, u32[]{:S(2)}, u32[]{:S(2)}) %collective-permute-start.8) | collective-permute-done | bytes 524320 | tf_op jit(solution)/shard_map/ppermute | solution.py:428
  110.4 1.1 all-to-all-done.2.refs_0_
  111.5 1.3 copy-done.1
  112.9 7.1 %clean.6.refs_13_ = bf16[32,2,2,128,128]{4,3,2,1,0:T(8,128)(2,1)} custom-call(s32[2]{0:T(128)} %pad_add_fusion.at_ref, bf16[8,2,512,128]{3,2,1,0:T(8,128)(2,1)} %copy-done.1, bf16[512,512]{1,0:T(8,128)(2,1)} %bitcast.12, bf16[512,512]{1,0:T(8,128)(2,1)} %turn.1.refs_1_.refs_2_.refs_9_, ...), custom_call_target="tpu_custom_call", output_to_operand_aliasing={{}: (7, {})} | custom-call | flops 3221225472 | bytes 4194304 | tf_op jit(solution)/shard_map/clean/pallas_call | solution.py:262
  120.0 6.7 %all-to-all-start.5 = ((bf16[32,2,2,128,128]{4,3,2,1,0:T(8,128)(2,1)}), bf16[32,2,2,128,128]{4,3,2,1,0:T(8,128)(2,1)}, u32[]{:S(2)}, u32[]{:S(2)}) async-start(bf16[32,2,2,128,128]{4,3,2,1,0:T(8,128)(2,1)} %clean.6.refs_13_), calls=%async_computation.5 | async-start | bytes 8388608 | tf_op jit(solution)/shard_map/all_to_all | solution.py:449
  127.4 2.1 collective-permute-start
  130.1 1.4 collective-permute-start.2
  131.8 31.9 %collective-permute-done.refs_1_ = bf16[2,512,128]{2,1,0:T(8,128)(2,1)S(1)} collective-permute-done((bf16[2,512,128]{2,1,0:T(8,128)(2,1)S(1)}, bf16[2,512,128]{2,1,0:T(8,128)(2,1)S(1)}, u32[]{:S(2)}, u32[]{:S(2)}) %collective-permute-start) | collective-permute-done | bytes 262176 | tf_op jit(solution)/shard_map/ppermute | solution.py:455
  163.7 20.0 %collective-permute-done.1.refs_2_ = bf16[2,512,128]{2,1,0:T(8,128)(2,1)S(1)} collective-permute-done((bf16[2,512,128]{2,1,0:T(8,128)(2,1)S(1)}, bf16[2,512,128]{2,1,0:T(8,128)(2,1)S(1)}, u32[]{:S(2)}, u32[]{:S(2)}) %collective-permute-start.1) | collective-permute-done | bytes 262176 | tf_op jit(solution)/shard_map/ppermute | solution.py:455
  183.7 48.9 %collective-permute-done.9.refs_3_ = bf16[8,1,2,128,128]{4,3,2,1,0:T(8,128)(2,1)S(1)} collective-permute-done((bf16[8,1,2,128,128]{4,3,2,1,0:T(8,128)(2,1)S(1)}, bf16[8,1,2,128,128]{4,3,2,1,0:T(8,128)(2,1)S(1)}, u32[]{:S(2)}, u32[]{:S(2)}) %collective-permute-start.9) | collective-permute-done | bytes 524320 | tf_op jit(solution)/shard_map/ppermute | solution.py:428
  232.6 1.7 dynamic-slice_bitcast_fusion.refs_4_
  234.3 4.1 %row_transform.1 = (bf16[2,16,32,128]{3,2,1,0:T(8,128)(2,1)}, bf16[2,16,32,128]{3,2,1,0:T(8,128)(2,1)}, bf16[2,16,32,128]{3,2,1,0:T(8,128)(2,1)}, bf16[2,16,32,1...) custom-call(s32[2]{0:T(128)} %pad_add_fusion.at_ref, ...), custom_call_target="tpu_custom_call" | custom-call | tf_op jit(solution)/shard_map/row_transform/pallas_call | solution.py:367
  238.5 0.7 copy-done.32
  239.3 7.3 %clean.7 = bf16[32,1,2,128,128]{4,3,2,1,0:T(8,128)(2,1)} custom-call(s32[2]{0:T(128)} %pad_add_fusion.at_ref, bf16[2,512,128]{2,1,0:T(8,128)(2,1)} %get-tuple-element.27.refs_0_, bf16[2,512,128]{2,1,0:T(8,128)(2,1)} %copy-done.30, bf16[2,512,128]{2,1,0:T(8,128)(2,1)} %copy-done.31, bf16[2,512,128]{2,1,0:T(8,128)(2,1)} %collective-permute-done.2.refs_3_, ...), custom_call_target="tpu_custom_call" | custom-call | flops 3221225472 | bytes 4194304 | tf_op jit(solution)/shard_map/clean/pallas_call | solution.py:262
  246.6 2.6 all-to-all-start.4
  249.3 1.8 collective-permute-start.10
  251.1 1.1 collective-permute-start.11
  252.8 0.9 collective-permute-start.13
  253.7 0.9 collective-permute-start.14
  254.6 19.1 %collective-permute-done.10.refs_1_ = bf16[2,16,32,128]{3,2,1,0:T(8,128)(2,1)S(1)} collective-permute-done((bf16[2,16,32,128]{3,2,1,0:T(8,128)(2,1)}, bf16[2,16,32,128]{3,2,1,0:T(8,128)(2,1)S(1)}, u32[]{:S(2)}, u32[]{:S(2)}) %collective-permute-start.10) | collective-permute-done | bytes 262176 | tf_op jit(solution)/shard_map/ppermute | solution.py:455
  273.7 0.6 collective-permute-start.15
  274.4 11.9 %collective-permute-done.11.refs_2_ = bf16[2,16,32,128]{3,2,1,0:T(8,128)(2,1)S(1)} collective-permute-done((bf16[2,16,32,128]{3,2,1,0:T(8,128)(2,1)}, bf16[2,16,32,128]{3,2,1,0:T(8,128)(2,1)S(1)}, u32[]{:S(2)}, u32[]{:S(2)}) %collective-permute-start.11) | collective-permute-done | bytes 262176 | tf_op jit(solution)/shard_map/ppermute | solution.py:455
  286.3 6.6 %image.3.refs_0_ = bf16[2,16,32,4096]{3,2,1,0:T(8,128)(2,1)} custom-call(bf16[4,8,2,2,128,128]{5,4,3,2,1,0:T(8,128)(2,1)} %bitcast.6.x_ref, bf16[256,256]{1,0:T(8,128)(2,1)} %constant.33.clone.table_ref, bf16[1024,1024]{1,0:T(8,128)(2,1)} %constant.34.clone.order_ref.refs_8_), custom_call_target="tpu_custom_call" | custom-call | flops 2147483648 | bytes 4194304 | tf_op jit(solution)/shard_map/image/pallas_call | solution.py:314
  292.9 6.5 %image.4.refs_9_ = bf16[2,16,32,4096]{3,2,1,0:T(8,128)(2,1)} custom-call(bf16[4,8,2,2,128,128]{5,4,3,2,1,0:T(8,128)(2,1)} %bitcast.6.x_ref, bf16[256,256]{1,0:T(8,128)(2,1)} %constant.33.clone.table_ref, bf16[1024,1024]{1,0:T(8,128)(2,1)} %constant.34.clone.order_ref.refs_8_, bf16[2,16,32,4096]{3,2,1,0:T(8,128)(2,1)} %image.3.refs_0_), custom_call_target="tpu_custom_call", output_to_operand_aliasing={{}: (3, {})} | custom-call | flops 2147483648 | bytes 4194304 | tf_op jit(solution)/shard_map/image/pallas_call | solution.py:314
  300.3 0.7 copy-done.13
  301.0 6.2 %place.1.refs_0_ = bf16[2,16,32,4096]{3,2,1,0:T(8,128)(2,1)} custom-call(s32[2]{0:T(128)} %pad_add_fusion.at_ref, bf16[2,16,32,128]{3,2,1,0:T(8,128)(2,1)} %get-tuple-element.41.refs_14_.refs_0_, bf16[2,16,32,128]{3,2,1,0:T(8,128)(2,1)} %copy-done.7, bf16[2,16,32,128]{3,2,1,0:T(8,128)(2,1)} %copy-done.8, ...), custom_call_target="tpu_custom_call", output_to_operand_aliasing={{}: (10, {})} | custom-call | tf_op jit(solution)/shard_map/place/pallas_call | solution.py:392
  307.3 1.3 copy-done
  308.6 6.4 %image.5 = bf16[2,16,32,4096]{3,2,1,0:T(8,128)(2,1)} custom-call(bf16[4,8,1,2,128,128]{5,4,3,2,1,0:T(8,128)(2,1)} %bitcast.8, bf16[256,256]{1,0:T(8,128)(2,1)} %constant.33.clone.table_ref, bf16[1024,1024]{1,0:T(8,128)(2,1)} %constant.34.clone.order_ref.refs_8_, bf16[2,16,32,4096]{3,2,1,0:T(8,128)(2,1)} %place.1.refs_0_), custom_call_target="tpu_custom_call", output_to_operand_aliasing={{}: (3, {})} | custom-call | flops 2147483648 | bytes 4194304 | tf_op jit(solution)/shard_map/image/pallas_call | solution.py:314
  (86 shorter events, 3.4 us)
Async XLA Ops:
  1.7 15.7 %all-to-all-start = ((bf16[8,64,512]{2,1,0:T(8,128)(2,1)}), bf16[8,64,512]{2,1,0:T(8,128)(2,1)S(1)}, u32[]{:S(2)}, u32[]{:S(2)}) async-start(bf16[8,64,512]{2,1,0:T(8,128)(2,1)} %broadcast_in_dim.2), calls=%async_computation | async-start | bytes 1048576 | tf_op jit(solution)/shard_map/all_to_all | solution.py:449
  18.1 30.8 %all-to-all-start.1 = ((bf16[8,2,512,128]{3,2,1,0:T(8,128)(2,1)}), bf16[8,2,512,128]{3,2,1,0:T(8,128)(2,1)S(1)}, u32[]{:S(2)}, u32[]{:S(2)}) async-start(bf16[8,2,512,128]{3,2,1,0:T(8,128)(2,1)} %column_transform.3), calls=%async_computation.1 | async-start | bytes 4194304 | tf_op jit(solution)/shard_map/all_to_all | solution.py:449
  40.7 14.0 %copy-start.14 = (f32[512]{0:T(512)S(1)}, f32[512]{0:T(512)}, u32[]{:S(2)}) copy-start(f32[512]{0:T(512)} %param.26) | copy-start | bytes 6148
  40.7 14.0 %copy-start.15 = (f32[8]{0:T(128)S(1)}, f32[8]{0:T(128)}, u32[]{:S(2)}) copy-start(f32[8]{0:T(128)} %param.27) | copy-start | bytes 100
  49.0 1.4 copy-start.5
  50.3 31.0 %all-to-all-start.3 = ((bf16[8,2,512,128]{3,2,1,0:T(8,128)(2,1)}), bf16[8,2,512,128]{3,2,1,0:T(8,128)(2,1)}, u32[]{:S(2)}, u32[]{:S(2)}) async-start(bf16[8,2,512,128]{3,2,1,0:T(8,128)(2,1)} %hold.2.refs_6_), calls=%async_computation.3 | async-start | bytes 4194304 | tf_op jit(solution)/shard_map/all_to_all | solution.py:449
  62.4 14.4 %collective-permute-start.7 = (bf16[8,1,2,128,128]{4,3,2,1,0:T(8,128)(2,1)}, bf16[8,1,2,128,128]{4,3,2,1,0:T(8,128)(2,1)S(1)}, u32[]{:S(2)}, u32[]{:S(2)}) collective-permute-start(bf16[8,1,2,128,128]{4,3,2,1,0:T(8,128)(2,1)} %get-tuple-element.37), channel_id=1, source_target_pairs={{0,8},{8,16},{16,24},{24,0},{1,9},{9,17},{17,25},{25,1},{2,10},{10... | collective-permute-start | bytes 1572872 | tf_op jit(solution)/shard_map/ppermute | solution.py:428
  77.7 7.5 %copy-start.17 = (bf16[8,1,2,128,128]{4,3,2,1,0:T(8,128)(2,1)S(1)}, bf16[8,1,2,128,128]{4,3,2,1,0:T(8,128)(2,1)}, u32[]{:S(2)}) copy-start(bf16[8,1,2,128,128]{4,3,2,1,0:T(8,128)(2,1)} %get-tuple-element.38) | copy-start | bytes 1572868
  81.4 30.2 %all-to-all-start.2 = ((bf16[8,2,512,128]{3,2,1,0:T(8,128)(2,1)}), bf16[8,2,512,128]{3,2,1,0:T(8,128)(2,1)S(1)}, u32[]{:S(2)}, u32[]{:S(2)}) async-start(bf16[8,2,512,128]{3,2,1,0:T(8,128)(2,1)} %hold.3), calls=%async_computation.2 | async-start | bytes 4194304 | tf_op jit(solution)/shard_map/all_to_all | solution.py:449
  85.2 25.3 %collective-permute-start.8 = (bf16[8,1,2,128,128]{4,3,2,1,0:T(8,128)(2,1)S(1)}, bf16[8,1,2,128,128]{4,3,2,1,0:T(8,128)(2,1)S(1)}, u32[]{:S(2)}, u32[]{:S(2)}) collective-permute-start(bf16[8,1,2,128,128]{4,3,2,1,0:T(8,128)(2,1)S(1)} %copy-done.17), channel_id=1, source_target_pairs={{0,16},{8,24},{16,0},{24,8},{1,17},{9,25},{17,1},{25,9},{2,18},{10... | collective-permute-start | bytes 1572872 | tf_op jit(solution)/shard_map/ppermute | solution.py:428
  110.4 1.1 copy-start.4
  111.5 1.3 copy-start.1
  120.0 6.8 %copy-start.16 = (bf16[8,1,2,128,128]{4,3,2,1,0:T(8,128)(2,1)S(1)}, bf16[8,1,2,128,128]{4,3,2,1,0:T(8,128)(2,1)}, u32[]{:S(2)}) copy-start(bf16[8,1,2,128,128]{4,3,2,1,0:T(8,128)(2,1)} %get-tuple-element.40) | copy-start | bytes 1572868
  120.0 7.4 %copy-start.29 = (bf16[2,512,128]{2,1,0:T(8,128)(2,1)S(1)}, bf16[2,512,128]{2,1,0:T(8,128)(2,1)}, u32[]{:S(2)}) copy-start(bf16[2,512,128]{2,1,0:T(8,128)(2,1)} %get-tuple-element.28) | copy-start | bytes 786436
  120.0 9.5 %copy-start.26 = (bf16[2,512,128]{2,1,0:T(8,128)(2,1)S(1)}, bf16[2,512,128]{2,1,0:T(8,128)(2,1)}, u32[]{:S(2)}) copy-start(bf16[2,512,128]{2,1,0:T(8,128)(2,1)} %get-tuple-element.29) | copy-start | bytes 786436
  120.0 10.1 %copy-start.22 = (bf16[2,512,128]{2,1,0:T(8,128)(2,1)S(1)}, bf16[2,512,128]{2,1,0:T(8,128)(2,1)}, u32[]{:S(2)}) copy-start(bf16[2,512,128]{2,1,0:T(8,128)(2,1)} %get-tuple-element.30) | copy-start | bytes 786436
  120.0 11.5 %copy-start.21 = (bf16[2,512,128]{2,1,0:T(8,128)(2,1)S(1)}, bf16[2,512,128]{2,1,0:T(8,128)(2,1)}, u32[]{:S(2)}) copy-start(bf16[2,512,128]{2,1,0:T(8,128)(2,1)} %get-tuple-element.31) | copy-start | bytes 786436
  120.0 43.7 %copy-start.20 = (bf16[2,512,128]{2,1,0:T(8,128)(2,1)S(1)}, bf16[2,512,128]{2,1,0:T(8,128)(2,1)}, u32[]{:S(2)}) copy-start(bf16[2,512,128]{2,1,0:T(8,128)(2,1)} %get-tuple-element.32) | copy-start | bytes 786436
  120.0 63.7 %copy-start.19 = (bf16[2,512,128]{2,1,0:T(8,128)(2,1)S(1)}, bf16[2,512,128]{2,1,0:T(8,128)(2,1)}, u32[]{:S(2)}) copy-start(bf16[2,512,128]{2,1,0:T(8,128)(2,1)} %get-tuple-element.33) | copy-start | bytes 786436
  120.0 112.6 %copy-start.18 = (bf16[2,512,128]{2,1,0:T(8,128)(2,1)S(1)}, bf16[2,512,128]{2,1,0:T(8,128)(2,1)}, u32[]{:S(2)}) copy-start(bf16[2,512,128]{2,1,0:T(8,128)(2,1)} %get-tuple-element.34) | copy-start | bytes 786436
  120.0 126.6 %all-to-all-start.5 = ((bf16[32,2,2,128,128]{4,3,2,1,0:T(8,128)(2,1)}), bf16[32,2,2,128,128]{4,3,2,1,0:T(8,128)(2,1)}, u32[]{:S(2)}, u32[]{:S(2)}) async-start(bf16[32,2,2,128,128]{4,3,2,1,0:T(8,128)(2,1)} %clean.6.refs_13_), calls=%async_computation.5 | async-start | bytes 8388608 | tf_op jit(solution)/shard_map/all_to_all | solution.py:449
  126.8 105.8 %collective-permute-start.9 = (bf16[8,1,2,128,128]{4,3,2,1,0:T(8,128)(2,1)S(1)}, bf16[8,1,2,128,128]{4,3,2,1,0:T(8,128)(2,1)S(1)}, u32[]{:S(2)}, u32[]{:S(2)}) collective-permute-start(bf16[8,1,2,128,128]{4,3,2,1,0:T(8,128)(2,1)S(1)} %copy-done.16), channel_id=1, source_target_pairs={{0,24},{8,0},{16,8},{24,16},{1,25},{9,1},{17,9},{25,17},{2,26},{10... | collective-permute-start | bytes 1572872 | tf_op jit(solution)/shard_map/ppermute | solution.py:428
  127.4 36.3 %collective-permute-start = (bf16[2,512,128]{2,1,0:T(8,128)(2,1)S(1)}, bf16[2,512,128]{2,1,0:T(8,128)(2,1)S(1)}, u32[]{:S(2)}, u32[]{:S(2)}) collective-permute-start(bf16[2,512,128]{2,1,0:T(8,128)(2,1)S(1)} %copy-done.29), channel_id=1, source_target_pairs={{0,7},{1,6},{2,5},{3,4},{4,3},{5,2},{6,1},{7,0},{8,15},{9,14},{10,... | collective-permute-start | bytes 786440 | tf_op jit(solution)/shard_map/ppermute | solution.py:455
  129.4 54.3 %collective-permute-start.1 = (bf16[2,512,128]{2,1,0:T(8,128)(2,1)S(1)}, bf16[2,512,128]{2,1,0:T(8,128)(2,1)S(1)}, u32[]{:S(2)}, u32[]{:S(2)}) collective-permute-start(bf16[2,512,128]{2,1,0:T(8,128)(2,1)S(1)} %copy-done.26), channel_id=1, source_target_pairs={{0,6},{1,7},{2,4},{3,5},{4,2},{5,3},{6,0},{7,1},{8,14},{9,15},{10,... | collective-permute-start | bytes 786440 | tf_op jit(solution)/shard_map/ppermute | solution.py:455
  130.1 108.3 %collective-permute-start.2 = (bf16[2,512,128]{2,1,0:T(8,128)(2,1)S(1)}, bf16[2,512,128]{2,1,0:T(8,128)(2,1)}, u32[]{:S(2)}, u32[]{:S(2)}) collective-permute-start(bf16[2,512,128]{2,1,0:T(8,128)(2,1)S(1)} %copy-done.22), channel_id=1, source_target_pairs={{0,5},{1,4},{2,7},{3,6},{4,1},{5,0},{6,3},{7,2},{8,13},{9,12},{10,... | collective-permute-start | bytes 786440 | tf_op jit(solution)/shard_map/ppermute | solution.py:455
  131.4 107.0 %collective-permute-start.3 = (bf16[2,512,128]{2,1,0:T(8,128)(2,1)S(1)}, bf16[2,512,128]{2,1,0:T(8,128)(2,1)}, u32[]{:S(2)}, u32[]{:S(2)}) collective-permute-start(bf16[2,512,128]{2,1,0:T(8,128)(2,1)S(1)} %copy-done.21), channel_id=1, source_target_pairs={{0,4},{1,5},{2,6},{3,7},{4,0},{5,1},{6,2},{7,3},{8,12},{9,13},{10,... | collective-permute-start | bytes 786440 | tf_op jit(solution)/shard_map/ppermute | solution.py:455
  163.7 74.8 %copy-start.30 = (bf16[2,512,128]{2,1,0:T(8,128)(2,1)}, bf16[2,512,128]{2,1,0:T(8,128)(2,1)S(1)}, u32[]{:S(2)}) copy-start(bf16[2,512,128]{2,1,0:T(8,128)(2,1)S(1)} %collective-permute-done.refs_1_) | copy-start | bytes 786436
  163.7 74.7 %collective-permute-start.4 = (bf16[2,512,128]{2,1,0:T(8,128)(2,1)S(1)}, bf16[2,512,128]{2,1,0:T(8,128)(2,1)S(1)}, u32[]{:S(2)}, u32[]{:S(2)}) collective-permute-start(bf16[2,512,128]{2,1,0:T(8,128)(2,1)S(1)} %copy-done.20), channel_id=1, source_target_pairs={{0,3},{1,2},{2,1},{3,0},{4,7},{5,6},{6,5},{7,4},{8,11},{9,10},{10,... | collective-permute-start | bytes 786440 | tf_op jit(solution)/shard_map/ppermute | solution.py:455
  183.7 54.8 %copy-start.31 = (bf16[2,512,128]{2,1,0:T(8,128)(2,1)}, bf16[2,512,128]{2,1,0:T(8,128)(2,1)S(1)}, u32[]{:S(2)}) copy-start(bf16[2,512,128]{2,1,0:T(8,128)(2,1)S(1)} %collective-permute-done.1.refs_2_) | copy-start | bytes 786436
  183.7 54.7 %collective-permute-start.5 = (bf16[2,512,128]{2,1,0:T(8,128)(2,1)S(1)}, bf16[2,512,128]{2,1,0:T(8,128)(2,1)S(1)}, u32[]{:S(2)}, u32[]{:S(2)}) collective-permute-start(bf16[2,512,128]{2,1,0:T(8,128)(2,1)S(1)} %copy-done.19), channel_id=1, source_target_pairs={{0,2},{1,3},{2,0},{3,1},{4,6},{5,7},{6,4},{7,5},{8,10},{9,11},{10,... | collective-permute-start | bytes 786440 | tf_op jit(solution)/shard_map/ppermute | solution.py:455
  232.6 1.8 copy-start.6
  232.6 5.9 %collective-permute-start.6 = (bf16[2,512,128]{2,1,0:T(8,128)(2,1)S(1)}, bf16[2,512,128]{2,1,0:T(8,128)(2,1)S(1)}, u32[]{:S(2)}, u32[]{:S(2)}) collective-permute-start(bf16[2,512,128]{2,1,0:T(8,128)(2,1)S(1)} %copy-done.18), channel_id=1, source_target_pairs={{0,1},{1,0},{2,3},{3,2},{4,5},{5,4},{6,7},{7,6},{8,9},{9,8},{10,11... | collective-permute-start | bytes 786440 | tf_op jit(solution)/shard_map/ppermute | solution.py:455
  246.6 5.6 %copy-start.28 = (bf16[2,16,32,128]{3,2,1,0:T(8,128)(2,1)S(1)}, bf16[2,16,32,128]{3,2,1,0:T(8,128)(2,1)}, u32[]{:S(2)}) copy-start(bf16[2,16,32,128]{3,2,1,0:T(8,128)(2,1)} %get-tuple-element.44) | copy-start | bytes 786436
  246.6 6.2 %copy-start.27 = (bf16[2,16,32,128]{3,2,1,0:T(8,128)(2,1)S(1)}, bf16[2,16,32,128]{3,2,1,0:T(8,128)(2,1)}, u32[]{:S(2)}) copy-start(bf16[2,16,32,128]{3,2,1,0:T(8,128)(2,1)} %get-tuple-element.45) | copy-start | bytes 786436
  246.6 7.1 %copy-start.25 = (bf16[2,16,32,128]{3,2,1,0:T(8,128)(2,1)S(1)}, bf16[2,16,32,128]{3,2,1,0:T(8,128)(2,1)}, u32[]{:S(2)}) copy-start(bf16[2,16,32,128]{3,2,1,0:T(8,128)(2,1)} %get-tuple-element.46) | copy-start | bytes 786436
  246.6 27.1 %copy-start.24 = (bf16[2,16,32,128]{3,2,1,0:T(8,128)(2,1)S(1)}, bf16[2,16,32,128]{3,2,1,0:T(8,128)(2,1)}, u32[]{:S(2)}) copy-start(bf16[2,16,32,128]{3,2,1,0:T(8,128)(2,1)} %get-tuple-element.47) | copy-start | bytes 786436
  246.6 39.7 %copy-start.23 = (bf16[2,16,32,128]{3,2,1,0:T(8,128)(2,1)S(1)}, bf16[2,16,32,128]{3,2,1,0:T(8,128)(2,1)}, u32[]{:S(2)}) copy-start(bf16[2,16,32,128]{3,2,1,0:T(8,128)(2,1)} %get-tuple-element.48) | copy-start | bytes 786436
  246.6 60.6 %all-to-all-start.4 = ((bf16[32,1,2,128,128]{4,3,2,1,0:T(8,128)(2,1)}), bf16[32,1,2,128,128]{4,3,2,1,0:T(8,128)(2,1)S(1)}, u32[]{:S(2)}, u32[]{:S(2)}) async-start(bf16[32,1,2,128,128]{4,3,2,1,0:T(8,128)(2,1)} %clean.7), calls=%async_computation.4 | async-start | bytes 4194304 | tf_op jit(solution)/shard_map/all_to_all | solution.py:449
  249.3 24.4 %collective-permute-start.10 = (bf16[2,16,32,128]{3,2,1,0:T(8,128)(2,1)}, bf16[2,16,32,128]{3,2,1,0:T(8,128)(2,1)S(1)}, u32[]{:S(2)}, u32[]{:S(2)}) collective-permute-start(bf16[2,16,32,128]{3,2,1,0:T(8,128)(2,1)} %get-tuple-element.42), channel_id=1, source_target_pairs={{0,7},{1,6},{2,5},{3,4},{4,3},{5,2},{6,1},{7,0},{8,15},{9,14},{10,... | collective-permute-start | bytes 786440 | tf_op jit(solution)/shard_map/ppermute | solution.py:455
  251.1 35.2 %collective-permute-start.11 = (bf16[2,16,32,128]{3,2,1,0:T(8,128)(2,1)}, bf16[2,16,32,128]{3,2,1,0:T(8,128)(2,1)S(1)}, u32[]{:S(2)}, u32[]{:S(2)}) collective-permute-start(bf16[2,16,32,128]{3,2,1,0:T(8,128)(2,1)} %get-tuple-element.43), channel_id=1, source_target_pairs={{0,6},{1,7},{2,4},{3,5},{4,2},{5,3},{6,0},{7,1},{8,14},{9,15},{10,... | collective-permute-start | bytes 786440 | tf_op jit(solution)/shard_map/ppermute | solution.py:455
  252.2 47.2 %collective-permute-start.12 = (bf16[2,16,32,128]{3,2,1,0:T(8,128)(2,1)S(1)}, bf16[2,16,32,128]{3,2,1,0:T(8,128)(2,1)S(1)}, u32[]{:S(2)}, u32[]{:S(2)}) collective-permute-start(bf16[2,16,32,128]{3,2,1,0:T(8,128)(2,1)S(1)} %copy-done.28), channel_id=1, source_target_pairs={{0,5},{1,4},{2,7},{3,6},{4,1},{5,0},{6,3},{7,2},{8,13},{9,12},{10,... | collective-permute-start | bytes 786440 | tf_op jit(solution)/shard_map/ppermute | solution.py:455
  252.8 46.6 %collective-permute-start.13 = (bf16[2,16,32,128]{3,2,1,0:T(8,128)(2,1)S(1)}, bf16[2,16,32,128]{3,2,1,0:T(8,128)(2,1)S(1)}, u32[]{:S(2)}, u32[]{:S(2)}) collective-permute-start(bf16[2,16,32,128]{3,2,1,0:T(8,128)(2,1)S(1)} %copy-done.27), channel_id=1, source_target_pairs={{0,4},{1,5},{2,6},{3,7},{4,0},{5,1},{6,2},{7,3},{8,12},{9,13},{10,... | collective-permute-start | bytes 786440 | tf_op jit(solution)/shard_map/ppermute | solution.py:455
  253.7 45.7 %collective-permute-start.14 = (bf16[2,16,32,128]{3,2,1,0:T(8,128)(2,1)S(1)}, bf16[2,16,32,128]{3,2,1,0:T(8,128)(2,1)S(1)}, u32[]{:S(2)}, u32[]{:S(2)}) collective-permute-start(bf16[2,16,32,128]{3,2,1,0:T(8,128)(2,1)S(1)} %copy-done.25), channel_id=1, source_target_pairs={{0,3},{1,2},{2,1},{3,0},{4,7},{5,6},{6,5},{7,4},{8,11},{9,10},{10,... | collective-permute-start | bytes 786440 | tf_op jit(solution)/shard_map/ppermute | solution.py:455
  273.7 19.2 %copy-start.7 = (bf16[2,16,32,128]{3,2,1,0:T(8,128)(2,1)}, bf16[2,16,32,128]{3,2,1,0:T(8,128)(2,1)S(1)}, u32[]{:S(2)}) copy-start(bf16[2,16,32,128]{3,2,1,0:T(8,128)(2,1)S(1)} %collective-permute-done.10.refs_1_) | copy-start | bytes 786436
  273.7 25.7 %collective-permute-start.15 = (bf16[2,16,32,128]{3,2,1,0:T(8,128)(2,1)S(1)}, bf16[2,16,32,128]{3,2,1,0:T(8,128)(2,1)S(1)}, u32[]{:S(2)}, u32[]{:S(2)}) collective-permute-start(bf16[2,16,32,128]{3,2,1,0:T(8,128)(2,1)S(1)} %copy-done.24), channel_id=1, source_target_pairs={{0,2},{1,3},{2,0},{3,1},{4,6},{5,7},{6,4},{7,5},{8,10},{9,11},{10,... | collective-permute-start | bytes 786440 | tf_op jit(solution)/shard_map/ppermute | solution.py:455
  286.3 6.6 %copy-start.8 = (bf16[2,16,32,128]{3,2,1,0:T(8,128)(2,1)}, bf16[2,16,32,128]{3,2,1,0:T(8,128)(2,1)S(1)}, u32[]{:S(2)}) copy-start(bf16[2,16,32,128]{3,2,1,0:T(8,128)(2,1)S(1)} %collective-permute-done.11.refs_2_) | copy-start | bytes 786436
  286.3 13.1 %collective-permute-start.16 = (bf16[2,16,32,128]{3,2,1,0:T(8,128)(2,1)S(1)}, bf16[2,16,32,128]{3,2,1,0:T(8,128)(2,1)S(1)}, u32[]{:S(2)}, u32[]{:S(2)}) collective-permute-start(bf16[2,16,32,128]{3,2,1,0:T(8,128)(2,1)S(1)} %copy-done.23), channel_id=1, source_target_pairs={{0,1},{1,0},{2,3},{3,2},{4,5},{5,4},{6,7},{7,6},{8,9},{9,8},{10,11... | collective-permute-start | bytes 786440 | tf_op jit(solution)/shard_map/ppermute | solution.py:455
  307.3 1.3 copy-start
  (10 other events, 8.0 us)

commit v16 on v15

--- a/solution.py
+++ b/solution.py
@@ -288,17 +288,29 @@
 def image_kernel(scale, x_ref, table_ref, order_ref, *refs):
     out_ref = refs[-1]
     z, _, _, parts, rows, _ = x_ref.shape
-    tiles = []
-    for y_lo in range(RADIX):
-        tile = x_ref[:, y_lo, 0]
-        if rows % 16:
-            tile = tile.astype(jnp.float32)
-        tile = tile.reshape(z * parts * rows, LANES).astype(jnp.bfloat16)
-        tiles.append(tile)
-    value = jnp.dot(table_ref[...], jnp.concatenate(tiles, axis=1), preferred_element_type=jnp.float32)
-    value = (value * scale).astype(jnp.bfloat16)
-    value = jnp.dot(value, order_ref[...], preferred_element_type=jnp.float32)
-    out_ref[...] = value.astype(jnp.bfloat16).reshape(out_ref.shape)
+    _, chans, total, _ = out_ref.shape
+    subs = 2 * chans * total // table_ref.shape[0]
+    own = rows // subs
+    values = []
+    for sub in range(subs):
+        tiles = []
+        for y_lo in range(RADIX):
+            tile = x_ref[:, y_lo, 0, :, sub * own : (sub + 1) * own, :]
+            if own % 16:
+                tile = tile.astype(jnp.float32)
+            tiles.append(tile.reshape(z * parts * own, LANES).astype(jnp.bfloat16))
+        tile = jnp.concatenate(tiles, axis=1)
+        value = jnp.dot(table_ref[...], tile, preferred_element_type=jnp.float32)
+        values.append((value * scale).astype(jnp.bfloat16))
+    value = jnp.dot(
+        jnp.concatenate(values, axis=0), order_ref[...], preferred_element_type=jnp.float32
+    ).astype(jnp.bfloat16)
+    size = table_ref.shape[0]
+    group = chans // subs
+    for sub in range(subs):
+        out_ref[:, sub * group : (sub + 1) * group] = value[sub * size : (sub + 1) * size].reshape(
+            2, group, total, RADIX * LANES
+        )
 
 
 def image(x, slot, chunk, count, rows_dev, held):
@@ -311,19 +323,20 @@
     table = row_table(rows_dev, z, group)
     order = order_table()
     scale = 1.0 / math.sqrt(total * count * spread * wide)
+    block = group * math.gcd(chans // group, 2)
     return pl.pallas_call(
         functools.partial(image_kernel, scale),
-        grid=(chans // group, spread),
+        grid=(chans // block, spread),
         in_specs=[
             pl.BlockSpec(
-                (z, RADIX, 1, 2, group * rows_dev, LANES), lambda c, g: (0, g, slot, 0, c, 0)
+                (z, RADIX, 1, 2, block * rows_dev, LANES), lambda c, g: (0, g, slot, 0, c, 0)
             ),
             pl.BlockSpec(table.shape, lambda c, g: (0, 0)),
             pl.BlockSpec(order.shape, lambda c, g: (0, 0)),
         ]
         + [pl.BlockSpec(memory_space=pl.ANY)] * len(held),
         out_specs=pl.BlockSpec(
-            (2, group, total, wide), lambda c, g: (0, c, 0, chunk * spread + g)
+            (2, block, total, wide), lambda c, g: (0, c, 0, chunk * spread + g)
         ),
         out_shape=jax.ShapeDtypeStruct((2, chans, total, count * spread * wide), jnp.bfloat16),
         input_output_aliases={3: 0} if held else {},
@@ -494,7 +507,7 @@
         groups = groups[1:]
         parts = spread_rows(cleaned_chunk(0, 0, 1, before, uv_count))
         before = []
-        cells.append([exchange(hold(sends[1], [parts[1]]), "chan")])
+        cells.append([exchange(hold(sends[1], [parts[uv_count // 2]]), "chan")])
         sends = sends[1:]
         lines = scatter(row_transform(parts, at, chans // uv_count, rows_dev, length))
     sends = sends[1:]
@@ -507,9 +520,9 @@
             held = [place(lines, at, 0, count, held)]
         for slot, k in enumerate(chunks):
             if rows_first and k == 2:
-                before = before + [parts[uv_count // 2]]
+                before = before + parts[1:]
             if rows_first and k == count - 1:
-                before = before + lines[:1]
+                before = before + lines[1:4]
             (cleaned,) = cleaned_chunk(k, slot, len(chunks), before)
             before = [cleaned]
         planes = exchange(cleaned, ("uv", "chan"))

time: 317 us -> 298 us (0.940)
  waiting for transfers between devices: 173 us -> 150 us
    ppermute x3, waiting for transfers between devices: 77.2 us -> 41.4 us  [spread_rows(): lax.ppermute(parts[step], 'uv', [(z, (z + step) % count) for z in range(c...]
    ppermute x14, waiting for transfers between devices: 82.9 us -> 94.5 us  [scatter(): lax.ppermute(pieces[step], 'chan', [(j, int(partner(np.int32(j), step, co...]
  transfers between devices with their start and end apart: 23 -> 23, of which waited for: 10 -> 14; matrix products, arithmetic and copies ran while one was open for 1% -> 1% of each run, Pallas kernels for 24% -> 25%
where the time goes in v16:
time: 298 us; the launch traced here: 294 us
  waiting for transfers between devices  150 us (50%)
  Pallas kernels  86.3 us (29%)
  starting transfers between devices  41.3 us (14%)
  local copies, waits for them, and re-layouts  13.9 us (5%)
    ppermute x14, waiting for transfers between devices, scatter(): lax.ppermute(pieces[step], 'chan', [(j, int(partner(np.int32(j), step, co...  94.5 us
    ppermute x3, waiting for transfers between devices, spread_rows(): lax.ppermute(parts[step], 'uv', [(z, (z + step) % count) for z in range(c...  41.4 us
    pallas_call x4, Pallas kernels, clean(): pl.pallas_call(functools.partial(clean_kernel, split, len(before), steps)...  28.3 us
    pallas_call x2, Pallas kernels, column_transform(): pl.pallas_call(functools.partial(column_kernel, chunks, pieces // RADIX),...  27.6 us
    all_to_all x6, starting transfers between devices, exchange(): return lax.all_to_all(x, axes, split_axis=0, concat_axis=0, tiled=True)  24.1 us
    pallas_call x3, Pallas kernels, image(): pl.pallas_call(functools.partial(image_kernel, scale), grid=(chans // blo...  18 us
    all_to_all x6, waiting for transfers between devices, exchange(): return lax.all_to_all(x, axes, split_axis=0, concat_axis=0, tiled=True)  14.4 us
    ppermute x14, starting transfers between devices, scatter(): lax.ppermute(pieces[step], 'chan', [(j, int(partner(np.int32(j), step, co...  12.5 us
  transfers between devices with their start and end apart: 23, of which 14 were waited for; matrix products, arithmetic and copies ran while one was open for 1% of the time, Pallas kernels for 25%

profile of v16, /device:TPU:8, one launch (start us, length us, event | category | flops | bytes accessed | tf_op | source)
XLA Modules:
  0.0 293.6 jit_solution(5153206774682888629)
XLA Ops:
  0.0 1.7 broadcast_in_dim.2
  1.7 3.7 %all-to-all-start = ((bf16[8,64,512]{2,1,0:T(8,128)(2,1)}), bf16[8,64,512]{2,1,0:T(8,128)(2,1)S(1)}, u32[]{:S(2)}, u32[]{:S(2)}) async-start(bf16[8,64,512]{2,1,0:T(8,128)(2,1)} %broadcast_in_dim.2), calls=%async_computation | async-start | bytes 1048576 | tf_op jit(solution)/shard_map/all_to_all | solution.py:462
  6.0 11.3 %column_transform.3 = bf16[8,2,512,128]{3,2,1,0:T(8,128)(2,1)} custom-call(s32[2]{0:T(128)} %pad_add_fusion.at_ref, bf16[2,512,4096]{2,1,0:T(8,128)(2,1)} %bitcast.14, f32[8,2,512]{2,1,0:T(2,128)} %constant.28.clone.twiddle_ref, bf16[1024,1024]{1,0:T(8,128)(2,1)} %constant.29.clone.table_ref), custom_call_target="tpu_custom_call" | custom-call | flops 8589934592 | bytes 16777216 | tf_op jit(solution)/shard_map/column_transform/pallas_call | solution.py:171
  18.1 4.2 %all-to-all-start.1 = ((bf16[8,2,512,128]{3,2,1,0:T(8,128)(2,1)}), bf16[8,2,512,128]{3,2,1,0:T(8,128)(2,1)S(1)}, u32[]{:S(2)}, u32[]{:S(2)}) async-start(bf16[8,2,512,128]{3,2,1,0:T(8,128)(2,1)} %column_transform.3), calls=%async_computation.1 | async-start | bytes 4194304 | tf_op jit(solution)/shard_map/all_to_all | solution.py:462
  22.3 16.3 %column_transform.2 = (bf16[8,2,512,128]{3,2,1,0:T(8,128)(2,1)}, bf16[8,2,512,128]{3,2,1,0:T(8,128)(2,1)}, bf16[2,512,128]{2,1,0:T(8,128)(2,1)}, bf16[2,512,128]...) custom-call(s32[2]{0:T(128)} %pad_add_fusion.at_ref, ...), custom_call_target="tpu_custom_call" | custom-call | flops 25769803776 | bytes 16777216 | tf_op jit(solution)/shard_map/column_transform/pallas_call | solution.py:171
  38.7 2.1 turn.1.refs_1_.refs_2_.refs_9_
  40.7 8.2 %all-to-all-done.1.refs_0_ = bf16[8,2,512,128]{3,2,1,0:T(8,128)(2,1)S(1)} async-done(((bf16[8,2,512,128]{3,2,1,0:T(8,128)(2,1)}), bf16[8,2,512,128]{3,2,1,0:T(8,128)(2,1)S(1)}, u32[]{:S(2)}, u32[]{:S(2)}) %all-to-all-start.1) | async-done | bytes 2097184 | tf_op jit(solution)/shard_map/all_to_all | solution.py:462
  49.0 1.4 copy-done.5
  50.3 3.6 %all-to-all-start.3 = ((bf16[8,2,512,128]{3,2,1,0:T(8,128)(2,1)}), bf16[8,2,512,128]{3,2,1,0:T(8,128)(2,1)S(1)}, u32[]{:S(2)}, u32[]{:S(2)}) async-start(bf16[8,2,512,128]{3,2,1,0:T(8,128)(2,1)} %hold.2.refs_6_), calls=%async_computation.3 | async-start | bytes 4194304 | tf_op jit(solution)/shard_map/all_to_all | solution.py:462
  54.0 0.9 add_divide_fusion.refs_3_.refs_10_
  54.8 6.8 %clean.4 = (bf16[8,1,2,128,128]{4,3,2,1,0:T(8,128)(2,1)}, bf16[8,1,2,128,128]{4,3,2,1,0:T(8,128)(2,1)}, bf16[8,1,2,128,128]{4,3,2,1,0:T(8,128)(2,1)}, bf16[8,1,2,128,128]{4,3,2,1,0:T(8,128)(2,1)}) custom-call(s32[2]{0:T(128)} %pad_add_fusion.at_ref, bf16[8,2,512,128]{3,2,1,0:T(8,128)(2,1)} %copy-done.5, bf16[512,512]{1,0:T(8,128)(2,1)} %bitcast.10, ...), custom_call_target="tpu_custom_call" | custom-call | flops 3221225472 | bytes 4194304 | tf_op jit(solution)/shard_map/clean/pallas_call | solution.py:262
  61.7 2.6 collective-permute-start.7
  64.3 23.1 %collective-permute-done.7.refs_1_.refs_8_.refs_2_ = bf16[8,1,2,128,128]{4,3,2,1,0:T(8,128)(2,1)S(1)} collective-permute-done((bf16[8,1,2,128,128]{4,3,2,1,0:T(8,128)(2,1)}, bf16[8,1,2,128,128]{4,3,2,1,0:T(8,128)(2,1)S(1)}, u32[]{:S(2)}, u32[]{:S(2)}) %collective-permute-start.7) | collective-permute-done | bytes 524320 | tf_op jit(solution)/shard_map/ppermute | solution.py:441
  87.4 0.8 copy-done.2
  88.2 1.4 copy-done.4
  89.6 3.9 %all-to-all-start.2 = ((bf16[8,2,512,128]{3,2,1,0:T(8,128)(2,1)}), bf16[8,2,512,128]{3,2,1,0:T(8,128)(2,1)S(1)}, u32[]{:S(2)}, u32[]{:S(2)}) async-start(bf16[8,2,512,128]{3,2,1,0:T(8,128)(2,1)} %hold.3), calls=%async_computation.2 | async-start | bytes 4194304 | tf_op jit(solution)/shard_map/all_to_all | solution.py:462
  93.5 2.0 collective-permute-start.9
  95.5 7.1 %clean.5.refs_6_ = bf16[32,2,2,128,128]{4,3,2,1,0:T(8,128)(2,1)} custom-call(s32[2]{0:T(128)} %pad_add_fusion.at_ref, bf16[8,2,512,128]{3,2,1,0:T(8,128)(2,1)} %copy-done.4, bf16[512,512]{1,0:T(8,128)(2,1)} %bitcast.11, bf16[512,512]{1,0:T(8,128)(2,1)} %turn.1.refs_1_.refs_2_.refs_9_, f32[512,8]{1,0:T(8,128)} %add_divide_fusion.refs_3_.refs_10_, ...), custom_call_target="tpu_custom_call" | custom-call | flops 3221225472 | bytes 4194304 | tf_op jit(solution)/shard_map/clean/pallas_call | solution.py:262
  102.6 5.8 %collective-permute-done.8.refs_7_.refs_1_ = bf16[8,1,2,128,128]{4,3,2,1,0:T(8,128)(2,1)S(1)} collective-permute-done((bf16[8,1,2,128,128]{4,3,2,1,0:T(8,128)(2,1)}, bf16[8,1,2,128,128]{4,3,2,1,0:T(8,128)(2,1)S(1)}, u32[]{:S(2)}, u32[]{:S(2)}) %collective-permute-start.8) | collective-permute-done | bytes 524320 | tf_op jit(solution)/shard_map/ppermute | solution.py:441
  108.4 12.4 %collective-permute-done.9.refs_9_.refs_3_ = bf16[8,1,2,128,128]{4,3,2,1,0:T(8,128)(2,1)S(1)} collective-permute-done((bf16[8,1,2,128,128]{4,3,2,1,0:T(8,128)(2,1)}, bf16[8,1,2,128,128]{4,3,2,1,0:T(8,128)(2,1)S(1)}, u32[]{:S(2)}, u32[]{:S(2)}) %collective-permute-start.9) | collective-permute-done | bytes 524320 | tf_op jit(solution)/shard_map/ppermute | solution.py:441
  121.6 1.3 copy-done.1
  123.0 7.1 %clean.6.refs_13_ = bf16[32,2,2,128,128]{4,3,2,1,0:T(8,128)(2,1)} custom-call(s32[2]{0:T(128)} %pad_add_fusion.at_ref, bf16[8,2,512,128]{3,2,1,0:T(8,128)(2,1)} %copy-done.1, bf16[512,512]{1,0:T(8,128)(2,1)} %bitcast.12, bf16[512,512]{1,0:T(8,128)(2,1)} %turn.1.refs_1_.refs_2_.refs_9_, ...), custom_call_target="tpu_custom_call", output_to_operand_aliasing={{}: (7, {})} | custom-call | flops 3221225472 | bytes 4194304 | tf_op jit(solution)/shard_map/clean/pallas_call | solution.py:262
  130.1 5.5 %all-to-all-start.5 = ((bf16[32,2,2,128,128]{4,3,2,1,0:T(8,128)(2,1)}), bf16[32,2,2,128,128]{4,3,2,1,0:T(8,128)(2,1)}, u32[]{:S(2)}, u32[]{:S(2)}) async-start(bf16[32,2,2,128,128]{4,3,2,1,0:T(8,128)(2,1)} %clean.6.refs_13_), calls=%async_computation.5 | async-start | bytes 8388608 | tf_op jit(solution)/shard_map/all_to_all | solution.py:462
  135.7 2.2 collective-permute-start
  138.4 1.1 collective-permute-start.2
  140.1 1.2 collective-permute-start.4
  141.4 1.6 dynamic-slice_bitcast_fusion.refs_4_
  142.9 4.1 %row_transform.1 = (bf16[2,16,32,128]{3,2,1,0:T(8,128)(2,1)}, bf16[2,16,32,128]{3,2,1,0:T(8,128)(2,1)}, bf16[2,16,32,128]{3,2,1,0:T(8,128)(2,1)}, bf16[2,16,32,1...) custom-call(s32[2]{0:T(128)} %pad_add_fusion.at_ref, ...), custom_call_target="tpu_custom_call" | custom-call | tf_op jit(solution)/shard_map/row_transform/pallas_call | solution.py:380
  147.1 25.5 %collective-permute-done.refs_1_ = bf16[2,512,128]{2,1,0:T(8,128)(2,1)S(1)} collective-permute-done((bf16[2,512,128]{2,1,0:T(8,128)(2,1)S(1)}, bf16[2,512,128]{2,1,0:T(8,128)(2,1)S(1)}, u32[]{:S(2)}, u32[]{:S(2)}) %collective-permute-start) | collective-permute-done | bytes 262176 | tf_op jit(solution)/shard_map/ppermute | solution.py:468
  172.6 20.0 %collective-permute-done.1.refs_2_ = bf16[2,512,128]{2,1,0:T(8,128)(2,1)S(1)} collective-permute-done((bf16[2,512,128]{2,1,0:T(8,128)(2,1)S(1)}, bf16[2,512,128]{2,1,0:T(8,128)(2,1)S(1)}, u32[]{:S(2)}, u32[]{:S(2)}) %collective-permute-start.1) | collective-permute-done | bytes 262176 | tf_op jit(solution)/shard_map/ppermute | solution.py:468
  192.7 3.9 %collective-permute-done.3.refs_4_ = bf16[2,512,128]{2,1,0:T(8,128)(2,1)S(1)} collective-permute-done((bf16[2,512,128]{2,1,0:T(8,128)(2,1)S(1)}, bf16[2,512,128]{2,1,0:T(8,128)(2,1)S(1)}, u32[]{:S(2)}, u32[]{:S(2)}) %collective-permute-start.3) | collective-permute-done | bytes 262176 | tf_op jit(solution)/shard_map/ppermute | solution.py:468
  197.3 3.4 %collective-permute-start.11 = (bf16[2,16,32,128]{3,2,1,0:T(8,128)(2,1)}, bf16[2,16,32,128]{3,2,1,0:T(8,128)(2,1)S(1)}, u32[]{:S(2)}, u32[]{:S(2)}) collective-permute-start(bf16[2,16,32,128]{3,2,1,0:T(8,128)(2,1)} %get-tuple-element.42), channel_id=1, source_target_pairs={{0,6},{1,7},{2,4},{3,5},{4,2},{5,3},{6,0},{7,1},{8,14},{9,15},{10,... | collective-permute-start | bytes 786440 | tf_op jit(solution)/shard_map/ppermute | solution.py:468
  201.4 3.8 %collective-permute-done.5.refs_6_ = bf16[2,512,128]{2,1,0:T(8,128)(2,1)S(1)} collective-permute-done((bf16[2,512,128]{2,1,0:T(8,128)(2,1)S(1)}, bf16[2,512,128]{2,1,0:T(8,128)(2,1)S(1)}, u32[]{:S(2)}, u32[]{:S(2)}) %collective-permute-start.5) | collective-permute-done | bytes 262176 | tf_op jit(solution)/shard_map/ppermute | solution.py:468
  205.2 7.3 %collective-permute-done.10.refs_14_.refs_1_ = bf16[2,16,32,128]{3,2,1,0:T(8,128)(2,1)S(1)} collective-permute-done((bf16[2,16,32,128]{3,2,1,0:T(8,128)(2,1)}, bf16[2,16,32,128]{3,2,1,0:T(8,128)(2,1)S(1)}, u32[]{:S(2)}, u32[]{:S(2)}) %collective-permute-start.10) | collective-permute-done | bytes 262176 | tf_op jit(solution)/shard_map/ppermute | solution.py:468
  212.6 10.3 %collective-permute-done.11.refs_15_.refs_2_ = bf16[2,16,32,128]{3,2,1,0:T(8,128)(2,1)S(1)} collective-permute-done((bf16[2,16,32,128]{3,2,1,0:T(8,128)(2,1)}, bf16[2,16,32,128]{3,2,1,0:T(8,128)(2,1)S(1)}, u32[]{:S(2)}, u32[]{:S(2)}) %collective-permute-start.11) | collective-permute-done | bytes 262176 | tf_op jit(solution)/shard_map/ppermute | solution.py:468
  222.9 5.5 %collective-permute-done.12.refs_16_.refs_3_ = bf16[2,16,32,128]{3,2,1,0:T(8,128)(2,1)S(1)} collective-permute-done((bf16[2,16,32,128]{3,2,1,0:T(8,128)(2,1)}, bf16[2,16,32,128]{3,2,1,0:T(8,128)(2,1)S(1)}, u32[]{:S(2)}, u32[]{:S(2)}) %collective-permute-start.12) | collective-permute-done | bytes 262176 | tf_op jit(solution)/shard_map/ppermute | solution.py:468
  229.1 7.3 %clean.7 = bf16[32,1,2,128,128]{4,3,2,1,0:T(8,128)(2,1)} custom-call(s32[2]{0:T(128)} %pad_add_fusion.at_ref, bf16[2,512,128]{2,1,0:T(8,128)(2,1)} %get-tuple-element.27.refs_0_, bf16[2,512,128]{2,1,0:T(8,128)(2,1)} %copy-done.28, bf16[2,512,128]{2,1,0:T(8,128)(2,1)} %copy-done.29, bf16[2,512,128]{2,1,0:T(8,128)(2,1)} %copy-done.30, ...), custom_call_target="tpu_custom_call" | custom-call | flops 3221225472 | bytes 4194304 | tf_op jit(solution)/shard_map/clean/pallas_call | solution.py:262
  236.4 3.2 %all-to-all-start.4 = ((bf16[32,1,2,128,128]{4,3,2,1,0:T(8,128)(2,1)}), bf16[32,1,2,128,128]{4,3,2,1,0:T(8,128)(2,1)S(1)}, u32[]{:S(2)}, u32[]{:S(2)}) async-start(bf16[32,1,2,128,128]{4,3,2,1,0:T(8,128)(2,1)} %clean.7), calls=%async_computation.4 | async-start | bytes 4194304 | tf_op jit(solution)/shard_map/all_to_all | solution.py:462
  239.6 1.5 collective-permute-start.13
  241.2 0.9 collective-permute-start.14
  243.0 6.0 %image.3.refs_0_ = bf16[2,16,32,4096]{3,2,1,0:T(8,128)(2,1)} custom-call(bf16[4,8,2,2,128,128]{5,4,3,2,1,0:T(8,128)(2,1)} %bitcast.6.x_ref, bf16[256,256]{1,0:T(8,128)(2,1)} %constant.33.clone.table_ref, bf16[1024,1024]{1,0:T(8,128)(2,1)} %constant.34.clone.order_ref.refs_8_), custom_call_target="tpu_custom_call" | custom-call | flops 2147483648 | bytes 4194304 | tf_op jit(solution)/shard_map/image/pallas_call | solution.py:327
  249.1 6.0 %image.4.refs_9_ = bf16[2,16,32,4096]{3,2,1,0:T(8,128)(2,1)} custom-call(bf16[4,8,2,2,128,128]{5,4,3,2,1,0:T(8,128)(2,1)} %bitcast.6.x_ref, bf16[256,256]{1,0:T(8,128)(2,1)} %constant.33.clone.table_ref, bf16[1024,1024]{1,0:T(8,128)(2,1)} %constant.34.clone.order_ref.refs_8_, bf16[2,16,32,4096]{3,2,1,0:T(8,128)(2,1)} %image.3.refs_0_), custom_call_target="tpu_custom_call", output_to_operand_aliasing={{}: (3, {})} | custom-call | flops 2147483648 | bytes 4194304 | tf_op jit(solution)/shard_map/image/pallas_call | solution.py:327
  255.1 5.4 %collective-permute-done.13.refs_4_ = bf16[2,16,32,128]{3,2,1,0:T(8,128)(2,1)S(1)} collective-permute-done((bf16[2,16,32,128]{3,2,1,0:T(8,128)(2,1)S(1)}, bf16[2,16,32,128]{3,2,1,0:T(8,128)(2,1)S(1)}, u32[]{:S(2)}, u32[]{:S(2)}) %collective-permute-start.13) | collective-permute-done | bytes 262176 | tf_op jit(solution)/shard_map/ppermute | solution.py:468
  260.5 12.6 %collective-permute-done.15.refs_6_ = bf16[2,16,32,128]{3,2,1,0:T(8,128)(2,1)S(1)} collective-permute-done((bf16[2,16,32,128]{3,2,1,0:T(8,128)(2,1)S(1)}, bf16[2,16,32,128]{3,2,1,0:T(8,128)(2,1)S(1)}, u32[]{:S(2)}, u32[]{:S(2)}) %collective-permute-start.15) | collective-permute-done | bytes 262176 | tf_op jit(solution)/shard_map/ppermute | solution.py:468
  273.9 6.2 %place.1.refs_0_ = bf16[2,16,32,4096]{3,2,1,0:T(8,128)(2,1)} custom-call(s32[2]{0:T(128)} %pad_add_fusion.at_ref, bf16[2,16,32,128]{3,2,1,0:T(8,128)(2,1)} %get-tuple-element.44.refs_0_, bf16[2,16,32,128]{3,2,1,0:T(8,128)(2,1)} %copy-done.8, bf16[2,16,32,128]{3,2,1,0:T(8,128)(2,1)} %copy-done.9, ...), custom_call_target="tpu_custom_call", output_to_operand_aliasing={{}: (10, {})} | custom-call | tf_op jit(solution)/shard_map/place/pallas_call | solution.py:405
  280.1 6.2 %all-to-all-done.4 = bf16[32,1,2,128,128]{4,3,2,1,0:T(8,128)(2,1)S(1)} async-done(((bf16[32,1,2,128,128]{4,3,2,1,0:T(8,128)(2,1)}), bf16[32,1,2,128,128]{4,3,2,1,0:T(8,128)(2,1)S(1)}, u32[]{:S(2)}, u32[]{:S(2)}) %all-to-all-start.4) | async-done | bytes 2097184 | tf_op jit(solution)/shard_map/all_to_all | solution.py:462
  286.3 1.3 copy-done
  287.6 6.0 %image.5 = bf16[2,16,32,4096]{3,2,1,0:T(8,128)(2,1)} custom-call(bf16[4,8,1,2,128,128]{5,4,3,2,1,0:T(8,128)(2,1)} %bitcast.8, bf16[256,256]{1,0:T(8,128)(2,1)} %constant.33.clone.table_ref, bf16[1024,1024]{1,0:T(8,128)(2,1)} %constant.34.clone.order_ref.refs_8_, bf16[2,16,32,4096]{3,2,1,0:T(8,128)(2,1)} %place.1.refs_0_), custom_call_target="tpu_custom_call", output_to_operand_aliasing={{}: (3, {})} | custom-call | flops 2147483648 | bytes 4194304 | tf_op jit(solution)/shard_map/image/pallas_call | solution.py:327
  (86 shorter events, 7.3 us)
Async XLA Ops:
  1.7 15.7 %all-to-all-start = ((bf16[8,64,512]{2,1,0:T(8,128)(2,1)}), bf16[8,64,512]{2,1,0:T(8,128)(2,1)S(1)}, u32[]{:S(2)}, u32[]{:S(2)}) async-start(bf16[8,64,512]{2,1,0:T(8,128)(2,1)} %broadcast_in_dim.2), calls=%async_computation | async-start | bytes 1048576 | tf_op jit(solution)/shard_map/all_to_all | solution.py:462
  18.1 30.8 %all-to-all-start.1 = ((bf16[8,2,512,128]{3,2,1,0:T(8,128)(2,1)}), bf16[8,2,512,128]{3,2,1,0:T(8,128)(2,1)S(1)}, u32[]{:S(2)}, u32[]{:S(2)}) async-start(bf16[8,2,512,128]{3,2,1,0:T(8,128)(2,1)} %column_transform.3), calls=%async_computation.1 | async-start | bytes 4194304 | tf_op jit(solution)/shard_map/all_to_all | solution.py:462
  40.7 13.2 %copy-start.15 = (f32[512]{0:T(512)S(1)}, f32[512]{0:T(512)}, u32[]{:S(2)}) copy-start(f32[512]{0:T(512)} %param.26) | copy-start | bytes 6148
  40.7 13.2 %copy-start.16 = (f32[8]{0:T(128)S(1)}, f32[8]{0:T(128)}, u32[]{:S(2)}) copy-start(f32[8]{0:T(128)} %param.27) | copy-start | bytes 100
  49.0 1.4 copy-start.5
  50.3 37.9 %all-to-all-start.3 = ((bf16[8,2,512,128]{3,2,1,0:T(8,128)(2,1)}), bf16[8,2,512,128]{3,2,1,0:T(8,128)(2,1)S(1)}, u32[]{:S(2)}, u32[]{:S(2)}) async-start(bf16[8,2,512,128]{3,2,1,0:T(8,128)(2,1)} %hold.2.refs_6_), calls=%async_computation.3 | async-start | bytes 4194304 | tf_op jit(solution)/shard_map/all_to_all | solution.py:462
  61.7 25.8 %collective-permute-start.7 = (bf16[8,1,2,128,128]{4,3,2,1,0:T(8,128)(2,1)}, bf16[8,1,2,128,128]{4,3,2,1,0:T(8,128)(2,1)S(1)}, u32[]{:S(2)}, u32[]{:S(2)}) collective-permute-start(bf16[8,1,2,128,128]{4,3,2,1,0:T(8,128)(2,1)} %get-tuple-element.37), channel_id=1, source_target_pairs={{0,16},{8,24},{16,0},{24,8},{1,17},{9,25},{17,1},{25,9},{2,18},{10... | collective-permute-start | bytes 1572872 | tf_op jit(solution)/shard_map/ppermute | solution.py:441
  88.2 1.4 copy-start.4
  89.6 31.2 %all-to-all-start.2 = ((bf16[8,2,512,128]{3,2,1,0:T(8,128)(2,1)}), bf16[8,2,512,128]{3,2,1,0:T(8,128)(2,1)S(1)}, u32[]{:S(2)}, u32[]{:S(2)}) async-start(bf16[8,2,512,128]{3,2,1,0:T(8,128)(2,1)} %hold.3), calls=%async_computation.2 | async-start | bytes 4194304 | tf_op jit(solution)/shard_map/all_to_all | solution.py:462
  93.5 14.9 %collective-permute-start.8 = (bf16[8,1,2,128,128]{4,3,2,1,0:T(8,128)(2,1)}, bf16[8,1,2,128,128]{4,3,2,1,0:T(8,128)(2,1)S(1)}, u32[]{:S(2)}, u32[]{:S(2)}) collective-permute-start(bf16[8,1,2,128,128]{4,3,2,1,0:T(8,128)(2,1)} %get-tuple-element.38), channel_id=1, source_target_pairs={{0,8},{8,16},{16,24},{24,0},{1,9},{9,17},{17,25},{25,1},{2,10},{10... | collective-permute-start | bytes 1572872 | tf_op jit(solution)/shard_map/ppermute | solution.py:441
  93.5 27.4 %collective-permute-start.9 = (bf16[8,1,2,128,128]{4,3,2,1,0:T(8,128)(2,1)}, bf16[8,1,2,128,128]{4,3,2,1,0:T(8,128)(2,1)S(1)}, u32[]{:S(2)}, u32[]{:S(2)}) collective-permute-start(bf16[8,1,2,128,128]{4,3,2,1,0:T(8,128)(2,1)} %get-tuple-element.39), channel_id=1, source_target_pairs={{0,24},{8,0},{16,8},{24,16},{1,25},{9,1},{17,9},{25,17},{2,26},{10... | collective-permute-start | bytes 1572872 | tf_op jit(solution)/shard_map/ppermute | solution.py:441
  108.4 12.4 %copy-start.6 = (bf16[8,1,2,128,128]{4,3,2,1,0:T(8,128)(2,1)}, bf16[8,1,2,128,128]{4,3,2,1,0:T(8,128)(2,1)S(1)}, u32[]{:S(2)}) copy-start(bf16[8,1,2,128,128]{4,3,2,1,0:T(8,128)(2,1)S(1)} %collective-permute-done.8.refs_7_.refs_1_) | copy-start | bytes 1572868
  130.1 5.6 %copy-start.23 = (bf16[2,512,128]{2,1,0:T(8,128)(2,1)S(1)}, bf16[2,512,128]{2,1,0:T(8,128)(2,1)}, u32[]{:S(2)}) copy-start(bf16[2,512,128]{2,1,0:T(8,128)(2,1)} %get-tuple-element.28) | copy-start | bytes 786436
  130.1 7.8 %copy-start.22 = (bf16[2,512,128]{2,1,0:T(8,128)(2,1)S(1)}, bf16[2,512,128]{2,1,0:T(8,128)(2,1)}, u32[]{:S(2)}) copy-start(bf16[2,512,128]{2,1,0:T(8,128)(2,1)} %get-tuple-element.29) | copy-start | bytes 786436
  130.1 8.4 %copy-start.21 = (bf16[2,512,128]{2,1,0:T(8,128)(2,1)S(1)}, bf16[2,512,128]{2,1,0:T(8,128)(2,1)}, u32[]{:S(2)}) copy-start(bf16[2,512,128]{2,1,0:T(8,128)(2,1)} %get-tuple-element.30) | copy-start | bytes 786436
  130.1 9.5 %copy-start.20 = (bf16[2,512,128]{2,1,0:T(8,128)(2,1)S(1)}, bf16[2,512,128]{2,1,0:T(8,128)(2,1)}, u32[]{:S(2)}) copy-start(bf16[2,512,128]{2,1,0:T(8,128)(2,1)} %get-tuple-element.31) | copy-start | bytes 786436
  130.1 10.1 %copy-start.19 = (bf16[2,512,128]{2,1,0:T(8,128)(2,1)S(1)}, bf16[2,512,128]{2,1,0:T(8,128)(2,1)}, u32[]{:S(2)}) copy-start(bf16[2,512,128]{2,1,0:T(8,128)(2,1)} %get-tuple-element.32) | copy-start | bytes 786436
  130.1 106.3 %all-to-all-start.5 = ((bf16[32,2,2,128,128]{4,3,2,1,0:T(8,128)(2,1)}), bf16[32,2,2,128,128]{4,3,2,1,0:T(8,128)(2,1)}, u32[]{:S(2)}, u32[]{:S(2)}) async-start(bf16[32,2,2,128,128]{4,3,2,1,0:T(8,128)(2,1)} %clean.6.refs_13_), calls=%async_computation.5 | async-start | bytes 8388608 | tf_op jit(solution)/shard_map/all_to_all | solution.py:462
  135.6 36.9 %copy-start.18 = (bf16[2,512,128]{2,1,0:T(8,128)(2,1)S(1)}, bf16[2,512,128]{2,1,0:T(8,128)(2,1)}, u32[]{:S(2)}) copy-start(bf16[2,512,128]{2,1,0:T(8,128)(2,1)} %get-tuple-element.33) | copy-start | bytes 786436
  135.6 56.9 %copy-start.17 = (bf16[2,512,128]{2,1,0:T(8,128)(2,1)S(1)}, bf16[2,512,128]{2,1,0:T(8,128)(2,1)}, u32[]{:S(2)}) copy-start(bf16[2,512,128]{2,1,0:T(8,128)(2,1)} %get-tuple-element.34) | copy-start | bytes 786436
  135.7 36.9 %collective-permute-start = (bf16[2,512,128]{2,1,0:T(8,128)(2,1)S(1)}, bf16[2,512,128]{2,1,0:T(8,128)(2,1)S(1)}, u32[]{:S(2)}, u32[]{:S(2)}) collective-permute-start(bf16[2,512,128]{2,1,0:T(8,128)(2,1)S(1)} %copy-done.23), channel_id=1, source_target_pairs={{0,7},{1,6},{2,5},{3,4},{4,3},{5,2},{6,1},{7,0},{8,15},{9,14},{10,... | collective-permute-start | bytes 786440 | tf_op jit(solution)/shard_map/ppermute | solution.py:468
  137.9 54.7 %collective-permute-start.1 = (bf16[2,512,128]{2,1,0:T(8,128)(2,1)S(1)}, bf16[2,512,128]{2,1,0:T(8,128)(2,1)S(1)}, u32[]{:S(2)}, u32[]{:S(2)}) collective-permute-start(bf16[2,512,128]{2,1,0:T(8,128)(2,1)S(1)} %copy-done.22), channel_id=1, source_target_pairs={{0,6},{1,7},{2,4},{3,5},{4,2},{5,3},{6,0},{7,1},{8,14},{9,15},{10,... | collective-permute-start | bytes 786440 | tf_op jit(solution)/shard_map/ppermute | solution.py:468
  138.4 54.2 %collective-permute-start.2 = (bf16[2,512,128]{2,1,0:T(8,128)(2,1)S(1)}, bf16[2,512,128]{2,1,0:T(8,128)(2,1)S(1)}, u32[]{:S(2)}, u32[]{:S(2)}) collective-permute-start(bf16[2,512,128]{2,1,0:T(8,128)(2,1)S(1)} %copy-done.21), channel_id=1, source_target_pairs={{0,5},{1,4},{2,7},{3,6},{4,1},{5,0},{6,3},{7,2},{8,13},{9,12},{10,... | collective-permute-start | bytes 786440 | tf_op jit(solution)/shard_map/ppermute | solution.py:468
  139.6 57.0 %collective-permute-start.3 = (bf16[2,512,128]{2,1,0:T(8,128)(2,1)S(1)}, bf16[2,512,128]{2,1,0:T(8,128)(2,1)S(1)}, u32[]{:S(2)}, u32[]{:S(2)}) collective-permute-start(bf16[2,512,128]{2,1,0:T(8,128)(2,1)S(1)} %copy-done.20), channel_id=1, source_target_pairs={{0,4},{1,5},{2,6},{3,7},{4,0},{5,1},{6,2},{7,3},{8,12},{9,13},{10,... | collective-permute-start | bytes 786440 | tf_op jit(solution)/shard_map/ppermute | solution.py:468
  140.1 60.5 %collective-permute-start.4 = (bf16[2,512,128]{2,1,0:T(8,128)(2,1)S(1)}, bf16[2,512,128]{2,1,0:T(8,128)(2,1)S(1)}, u32[]{:S(2)}, u32[]{:S(2)}) collective-permute-start(bf16[2,512,128]{2,1,0:T(8,128)(2,1)S(1)} %copy-done.19), channel_id=1, source_target_pairs={{0,3},{1,2},{2,1},{3,0},{4,7},{5,6},{6,5},{7,4},{8,11},{9,10},{10,... | collective-permute-start | bytes 786440 | tf_op jit(solution)/shard_map/ppermute | solution.py:468
  172.6 55.9 %copy-start.28 = (bf16[2,512,128]{2,1,0:T(8,128)(2,1)}, bf16[2,512,128]{2,1,0:T(8,128)(2,1)S(1)}, u32[]{:S(2)}) copy-start(bf16[2,512,128]{2,1,0:T(8,128)(2,1)S(1)} %collective-permute-done.refs_1_) | copy-start | bytes 786436
  172.6 32.7 %collective-permute-start.5 = (bf16[2,512,128]{2,1,0:T(8,128)(2,1)S(1)}, bf16[2,512,128]{2,1,0:T(8,128)(2,1)S(1)}, u32[]{:S(2)}, u32[]{:S(2)}) collective-permute-start(bf16[2,512,128]{2,1,0:T(8,128)(2,1)S(1)} %copy-done.18), channel_id=1, source_target_pairs={{0,2},{1,3},{2,0},{3,1},{4,6},{5,7},{6,4},{7,5},{8,10},{9,11},{10,... | collective-permute-start | bytes 786440 | tf_op jit(solution)/shard_map/ppermute | solution.py:468
  192.6 35.9 %copy-start.29 = (bf16[2,512,128]{2,1,0:T(8,128)(2,1)}, bf16[2,512,128]{2,1,0:T(8,128)(2,1)S(1)}, u32[]{:S(2)}) copy-start(bf16[2,512,128]{2,1,0:T(8,128)(2,1)S(1)} %collective-permute-done.1.refs_2_) | copy-start | bytes 786436
  192.6 12.7 %collective-permute-start.6 = (bf16[2,512,128]{2,1,0:T(8,128)(2,1)S(1)}, bf16[2,512,128]{2,1,0:T(8,128)(2,1)S(1)}, u32[]{:S(2)}, u32[]{:S(2)}) collective-permute-start(bf16[2,512,128]{2,1,0:T(8,128)(2,1)S(1)} %copy-done.17), channel_id=1, source_target_pairs={{0,1},{1,0},{2,3},{3,2},{4,5},{5,4},{6,7},{7,6},{8,9},{9,8},{10,11... | collective-permute-start | bytes 786440 | tf_op jit(solution)/shard_map/ppermute | solution.py:468
  192.6 35.8 %copy-start.30 = (bf16[2,512,128]{2,1,0:T(8,128)(2,1)}, bf16[2,512,128]{2,1,0:T(8,128)(2,1)S(1)}, u32[]{:S(2)}) copy-start(bf16[2,512,128]{2,1,0:T(8,128)(2,1)S(1)} %collective-permute-done.2.refs_3_) | copy-start | bytes 786436
  192.6 20.0 %collective-permute-start.10 = (bf16[2,16,32,128]{3,2,1,0:T(8,128)(2,1)}, bf16[2,16,32,128]{3,2,1,0:T(8,128)(2,1)S(1)}, u32[]{:S(2)}, u32[]{:S(2)}) collective-permute-start(bf16[2,16,32,128]{3,2,1,0:T(8,128)(2,1)} %get-tuple-element.41), channel_id=1, source_target_pairs={{0,7},{1,6},{2,5},{3,4},{4,3},{5,2},{6,1},{7,0},{8,15},{9,14},{10,... | collective-permute-start | bytes 786440 | tf_op jit(solution)/shard_map/ppermute | solution.py:468
  197.3 25.6 %collective-permute-start.11 = (bf16[2,16,32,128]{3,2,1,0:T(8,128)(2,1)}, bf16[2,16,32,128]{3,2,1,0:T(8,128)(2,1)S(1)}, u32[]{:S(2)}, u32[]{:S(2)}) collective-permute-start(bf16[2,16,32,128]{3,2,1,0:T(8,128)(2,1)} %get-tuple-element.42), channel_id=1, source_target_pairs={{0,6},{1,7},{2,4},{3,5},{4,2},{5,3},{6,0},{7,1},{8,14},{9,15},{10,... | collective-permute-start | bytes 786440 | tf_op jit(solution)/shard_map/ppermute | solution.py:468
  201.4 27.0 %collective-permute-start.12 = (bf16[2,16,32,128]{3,2,1,0:T(8,128)(2,1)}, bf16[2,16,32,128]{3,2,1,0:T(8,128)(2,1)S(1)}, u32[]{:S(2)}, u32[]{:S(2)}) collective-permute-start(bf16[2,16,32,128]{3,2,1,0:T(8,128)(2,1)} %get-tuple-element.43), channel_id=1, source_target_pairs={{0,5},{1,4},{2,7},{3,6},{4,1},{5,0},{6,3},{7,2},{8,13},{9,12},{10,... | collective-permute-start | bytes 786440 | tf_op jit(solution)/shard_map/ppermute | solution.py:468
  205.2 23.2 %copy-start.33 = (bf16[2,512,128]{2,1,0:T(8,128)(2,1)}, bf16[2,512,128]{2,1,0:T(8,128)(2,1)S(1)}, u32[]{:S(2)}) copy-start(bf16[2,512,128]{2,1,0:T(8,128)(2,1)S(1)} %collective-permute-done.5.refs_6_) | copy-start | bytes 786436
  205.2 23.2 %copy-start.34 = (bf16[2,512,128]{2,1,0:T(8,128)(2,1)}, bf16[2,512,128]{2,1,0:T(8,128)(2,1)S(1)}, u32[]{:S(2)}) copy-start(bf16[2,512,128]{2,1,0:T(8,128)(2,1)S(1)} %collective-permute-done.6.refs_7_) | copy-start | bytes 786436
  212.6 15.9 %copy-start.8 = (bf16[2,16,32,128]{3,2,1,0:T(8,128)(2,1)}, bf16[2,16,32,128]{3,2,1,0:T(8,128)(2,1)S(1)}, u32[]{:S(2)}) copy-start(bf16[2,16,32,128]{3,2,1,0:T(8,128)(2,1)S(1)} %collective-permute-done.10.refs_14_.refs_1_) | copy-start | bytes 786436
  222.9 5.6 %copy-start.9 = (bf16[2,16,32,128]{3,2,1,0:T(8,128)(2,1)}, bf16[2,16,32,128]{3,2,1,0:T(8,128)(2,1)S(1)}, u32[]{:S(2)}) copy-start(bf16[2,16,32,128]{3,2,1,0:T(8,128)(2,1)S(1)} %collective-permute-done.11.refs_15_.refs_2_) | copy-start | bytes 786436
  236.4 3.2 %copy-start.27 = (bf16[2,16,32,128]{3,2,1,0:T(8,128)(2,1)S(1)}, bf16[2,16,32,128]{3,2,1,0:T(8,128)(2,1)}, u32[]{:S(2)}) copy-start(bf16[2,16,32,128]{3,2,1,0:T(8,128)(2,1)} %get-tuple-element.45) | copy-start | bytes 786436
  236.4 4.8 %copy-start.26 = (bf16[2,16,32,128]{3,2,1,0:T(8,128)(2,1)S(1)}, bf16[2,16,32,128]{3,2,1,0:T(8,128)(2,1)}, u32[]{:S(2)}) copy-start(bf16[2,16,32,128]{3,2,1,0:T(8,128)(2,1)} %get-tuple-element.46) | copy-start | bytes 786436
  236.4 5.7 %copy-start.25 = (bf16[2,16,32,128]{3,2,1,0:T(8,128)(2,1)S(1)}, bf16[2,16,32,128]{3,2,1,0:T(8,128)(2,1)}, u32[]{:S(2)}) copy-start(bf16[2,16,32,128]{3,2,1,0:T(8,128)(2,1)} %get-tuple-element.47) | copy-start | bytes 786436
  236.4 6.3 %copy-start.24 = (bf16[2,16,32,128]{3,2,1,0:T(8,128)(2,1)S(1)}, bf16[2,16,32,128]{3,2,1,0:T(8,128)(2,1)}, u32[]{:S(2)}) copy-start(bf16[2,16,32,128]{3,2,1,0:T(8,128)(2,1)} %get-tuple-element.48) | copy-start | bytes 786436
  236.4 49.9 %all-to-all-start.4 = ((bf16[32,1,2,128,128]{4,3,2,1,0:T(8,128)(2,1)}), bf16[32,1,2,128,128]{4,3,2,1,0:T(8,128)(2,1)S(1)}, u32[]{:S(2)}, u32[]{:S(2)}) async-start(bf16[32,1,2,128,128]{4,3,2,1,0:T(8,128)(2,1)} %clean.7), calls=%async_computation.4 | async-start | bytes 4194304 | tf_op jit(solution)/shard_map/all_to_all | solution.py:462
  239.6 20.8 %collective-permute-start.13 = (bf16[2,16,32,128]{3,2,1,0:T(8,128)(2,1)S(1)}, bf16[2,16,32,128]{3,2,1,0:T(8,128)(2,1)S(1)}, u32[]{:S(2)}, u32[]{:S(2)}) collective-permute-start(bf16[2,16,32,128]{3,2,1,0:T(8,128)(2,1)S(1)} %copy-done.27), channel_id=1, source_target_pairs={{0,4},{1,5},{2,6},{3,7},{4,0},{5,1},{6,2},{7,3},{8,12},{9,13},{10,... | collective-permute-start | bytes 786440 | tf_op jit(solution)/shard_map/ppermute | solution.py:468
  241.2 19.3 %collective-permute-start.14 = (bf16[2,16,32,128]{3,2,1,0:T(8,128)(2,1)S(1)}, bf16[2,16,32,128]{3,2,1,0:T(8,128)(2,1)S(1)}, u32[]{:S(2)}, u32[]{:S(2)}) collective-permute-start(bf16[2,16,32,128]{3,2,1,0:T(8,128)(2,1)S(1)} %copy-done.26), channel_id=1, source_target_pairs={{0,3},{1,2},{2,1},{3,0},{4,7},{5,6},{6,5},{7,4},{8,11},{9,10},{10,... | collective-permute-start | bytes 786440 | tf_op jit(solution)/shard_map/ppermute | solution.py:468
  242.1 31.0 %collective-permute-start.15 = (bf16[2,16,32,128]{3,2,1,0:T(8,128)(2,1)S(1)}, bf16[2,16,32,128]{3,2,1,0:T(8,128)(2,1)S(1)}, u32[]{:S(2)}, u32[]{:S(2)}) collective-permute-start(bf16[2,16,32,128]{3,2,1,0:T(8,128)(2,1)S(1)} %copy-done.25), channel_id=1, source_target_pairs={{0,2},{1,3},{2,0},{3,1},{4,6},{5,7},{6,4},{7,5},{8,10},{9,11},{10,... | collective-permute-start | bytes 786440 | tf_op jit(solution)/shard_map/ppermute | solution.py:468
  242.7 30.4 %collective-permute-start.16 = (bf16[2,16,32,128]{3,2,1,0:T(8,128)(2,1)S(1)}, bf16[2,16,32,128]{3,2,1,0:T(8,128)(2,1)S(1)}, u32[]{:S(2)}, u32[]{:S(2)}) collective-permute-start(bf16[2,16,32,128]{3,2,1,0:T(8,128)(2,1)S(1)} %copy-done.24), channel_id=1, source_target_pairs={{0,1},{1,0},{2,3},{3,2},{4,5},{5,4},{6,7},{7,6},{8,9},{9,8},{10,11... | collective-permute-start | bytes 786440 | tf_op jit(solution)/shard_map/ppermute | solution.py:468
  260.5 12.6 %copy-start.11 = (bf16[2,16,32,128]{3,2,1,0:T(8,128)(2,1)}, bf16[2,16,32,128]{3,2,1,0:T(8,128)(2,1)S(1)}, u32[]{:S(2)}) copy-start(bf16[2,16,32,128]{3,2,1,0:T(8,128)(2,1)S(1)} %collective-permute-done.13.refs_4_) | copy-start | bytes 786436
  260.5 12.6 %copy-start.12 = (bf16[2,16,32,128]{3,2,1,0:T(8,128)(2,1)}, bf16[2,16,32,128]{3,2,1,0:T(8,128)(2,1)S(1)}, u32[]{:S(2)}) copy-start(bf16[2,16,32,128]{3,2,1,0:T(8,128)(2,1)S(1)} %collective-permute-done.14.refs_5_) | copy-start | bytes 786436
  (10 other events, 8.7 us)

commit v17 on v16

--- a/solution.py
+++ b/solution.py
@@ -11,7 +11,7 @@
 
 LANES = 128
 RADIX = 8
-VMEM_BYTES = 56 * 1024 * 1024
+VMEM_BYTES = 40 * 1024 * 1024
 
 
 def params():
@@ -522,7 +522,7 @@
             if rows_first and k == 2:
                 before = before + parts[1:]
             if rows_first and k == count - 1:
-                before = before + lines[1:4]
+                before = before + lines[1:3]
             (cleaned,) = cleaned_chunk(k, slot, len(chunks), before)
             before = [cleaned]
         planes = exchange(cleaned, ("uv", "chan"))

time: 298 us -> 302 us (1.013)
  local copies, waits for them, and re-layouts: 13.9 us -> 42 us
  Pallas kernels: 86.3 us -> 68.2 us
  waiting for transfers between devices: 150 us -> 141 us
  starting transfers between devices: 41.3 us -> 45.3 us
    unnamed x70 -> x130, local copies, waits for them, and re-layouts: 10.7 us -> 39.3 us
    pallas_call x4, Pallas kernels: 28.3 us -> 21.5 us  [clean(): pl.pallas_call(functools.partial(clean_kernel, split, len(before), steps)...]
    ppermute x14, waiting for transfers between devices: 94.5 us -> 89.7 us  [scatter(): lax.ppermute(pieces[step], 'chan', [(j, int(partner(np.int32(j), step, co...]
    all_to_all x6, starting transfers between devices: 24.1 us -> 27.8 us  [exchange(): return lax.all_to_all(x, axes, split_axis=0, concat_axis=0, tiled=True)]
    ppermute x3, waiting for transfers between devices: 41.4 us -> 37.9 us  [spread_rows(): lax.ppermute(parts[step], 'uv', [(z, (z + step) % count) for z in range(c...]
    pallas_call x2, Pallas kernels: 27.6 us -> 24.1 us  [column_transform(): pl.pallas_call(functools.partial(column_kernel, chunks, pieces // RADIX),...]
  transfers between devices with their start and end apart: 23 -> 23, of which waited for: 14 -> 14; matrix products, arithmetic and copies ran while one was open for 1% -> 0% of each run, Pallas kernels for 25% -> 20%
where the time goes in v17:
time: 302 us; the launch traced here: 297 us
  waiting for transfers between devices  141 us (47%)
  Pallas kernels  68.2 us (23%)
  starting transfers between devices  45.3 us (15%)
  local copies, waits for them, and re-layouts  42 us (14%)
    ppermute x14, waiting for transfers between devices, scatter(): lax.ppermute(pieces[step], 'chan', [(j, int(partner(np.int32(j), step, co...  89.7 us
    unnamed x130, local copies, waits for them, and re-layouts  39.3 us
    ppermute x3, waiting for transfers between devices, spread_rows(): lax.ppermute(parts[step], 'uv', [(z, (z + step) % count) for z in range(c...  37.9 us
    all_to_all x6, starting transfers between devices, exchange(): return lax.all_to_all(x, axes, split_axis=0, concat_axis=0, tiled=True)  27.8 us
    pallas_call x2, Pallas kernels, column_transform(): pl.pallas_call(functools.partial(column_kernel, chunks, pieces // RADIX),...  24.1 us
    pallas_call x4, Pallas kernels, clean(): pl.pallas_call(functools.partial(clean_kernel, split, len(before), steps)...  21.5 us
    pallas_call x3, Pallas kernels, image(): pl.pallas_call(functools.partial(image_kernel, scale), grid=(chans // blo...  15.9 us
    all_to_all x6, waiting for transfers between devices, exchange(): return lax.all_to_all(x, axes, split_axis=0, concat_axis=0, tiled=True)  13.3 us
  transfers between devices with their start and end apart: 23, of which 14 were waited for; matrix products, arithmetic and copies ran while one was open for 0% of the time, Pallas kernels for 20%

profile of v17, /device:TPU:8, one launch (start us, length us, event | category | flops | bytes accessed | tf_op | source)
XLA Modules:
  0.0 297.0 jit_solution(11331519127613258571)
XLA Ops:
  0.0 1.7 broadcast_in_dim.2
  1.7 3.7 %all-to-all-start = ((bf16[8,64,512]{2,1,0:T(8,128)(2,1)}), bf16[8,64,512]{2,1,0:T(8,128)(2,1)S(1)}, u32[]{:S(2)}, u32[]{:S(2)}) async-start(bf16[8,64,512]{2,1,0:T(8,128)(2,1)} %broadcast_in_dim.2), calls=%async_computation | async-start | bytes 1048576 | tf_op jit(solution)/shard_map/all_to_all | solution.py:462
  5.5 3.4 %copy-done.37 = bf16[2,64,8,4096]{3,2,1,0:T(8,128)(2,1)S(1)} copy-done((bf16[2,64,8,4096]{3,2,1,0:T(8,128)(2,1)S(1)}, bf16[2,64,8,4096]{3,2,1,0:T(8,128)(2,1)}, u32[]{:S(2)}) %copy-start.37) | copy-done | bytes 8388632
  8.9 1.6 copy-done.58
  11.2 9.4 %column_transform.3 = bf16[8,2,512,128]{3,2,1,0:T(8,128)(2,1)} custom-call(s32[2]{0:T(128)S(1)} %pad_add_fusion.at_ref, bf16[2,512,4096]{2,1,0:T(8,128)(2,1)S(1)} %bitcast.14, f32[8,2,512]{2,1,0:T(2,128)S(1)} %copy-done.60, bf16[1024,1024]{1,0:T(8,128)(2,1)S(1)} %copy-done.58), custom_call_target="tpu_custom_call" | custom-call | flops 8589934592 | bytes 16777216 | tf_op jit(solution)/shard_map/column_transform/pallas_call | solution.py:171
  20.7 4.6 %all-to-all-start.1 = ((bf16[8,2,512,128]{3,2,1,0:T(8,128)(2,1)}), bf16[8,2,512,128]{3,2,1,0:T(8,128)(2,1)}, u32[]{:S(2)}, u32[]{:S(2)}) async-start(bf16[8,2,512,128]{3,2,1,0:T(8,128)(2,1)} %column_transform.3), calls=%async_computation.1 | async-start | bytes 4194304 | tf_op jit(solution)/shard_map/all_to_all | solution.py:462
  25.3 14.7 %column_transform.2 = (bf16[8,2,512,128]{3,2,1,0:T(8,128)(2,1)S(1)}, bf16[8,2,512,128]{3,2,1,0:T(8,128)(2,1)S(1)}, bf16[2,512,128]{2,1,0:T(8,128)(2,1)S(1)}, bf1...) custom-call(s32[2]{0:T(128)S(1)} %pad_add_fusion.at_ref, ...), custom_call_target="tpu_custom_call" | custom-call | flops 25769803776 | bytes 16777216 | tf_op jit(solution)/shard_map/column_transform/pallas_call | solution.py:171
  40.0 1.3 copy-done.5
  41.4 1.3 copy-done.6
  47.4 4.6 %all-to-all-done.1.refs_0_ = bf16[8,2,512,128]{3,2,1,0:T(8,128)(2,1)} async-done(((bf16[8,2,512,128]{3,2,1,0:T(8,128)(2,1)}), bf16[8,2,512,128]{3,2,1,0:T(8,128)(2,1)}, u32[]{:S(2)}, u32[]{:S(2)}) %all-to-all-start.1) | async-done | bytes 2097184 | tf_op jit(solution)/shard_map/all_to_all | solution.py:462
  52.0 4.4 %all-to-all-start.3 = ((bf16[8,2,512,128]{3,2,1,0:T(8,128)(2,1)}), bf16[8,2,512,128]{3,2,1,0:T(8,128)(2,1)}, u32[]{:S(2)}, u32[]{:S(2)}) async-start(bf16[8,2,512,128]{3,2,1,0:T(8,128)(2,1)} %hold.2.refs_6_), calls=%async_computation.3 | async-start | bytes 4194304 | tf_op jit(solution)/shard_map/all_to_all | solution.py:462
  57.5 6.1 %clean.4 = (bf16[8,1,2,128,128]{4,3,2,1,0:T(8,128)(2,1)S(1)}, bf16[8,1,2,128,128]{4,3,2,1,0:T(8,128)(2,1)}, bf16[8,1,2,128,128]{4,3,2,1,0:T(8,128)(2,1)S(1)}, bf16[8,1,2,128,128]{4,3,2,1,0:T(8,128)(2,1)S(1)}) custom-call(s32[2]{0:T(128)S(1)} %pad_add_fusion.at_ref, bf16[8,2,512,128]{3,2,1,0:T(8,128)(2,1)} %all-to-all-done.1.refs_0_, ...), custom_call_target="tpu_custom_call" | custom-call | flops 3221225472 | bytes 4194304 | tf_op jit(solution)/shard_map/clean/pallas_call | solution.py:262
  65.2 2.6 collective-permute-start.7
  67.8 22.8 %collective-permute-done.7.refs_1_.refs_8_.refs_2_ = bf16[8,1,2,128,128]{4,3,2,1,0:T(8,128)(2,1)S(1)} collective-permute-done((bf16[8,1,2,128,128]{4,3,2,1,0:T(8,128)(2,1)S(1)}, bf16[8,1,2,128,128]{4,3,2,1,0:T(8,128)(2,1)S(1)}, u32[]{:S(2)}, u32[]{:S(2)}) %collective-permute-start.7) | collective-permute-done | bytes 524320 | tf_op jit(solution)/shard_map/ppermute | solution.py:441
  91.5 3.9 %all-to-all-start.2 = ((bf16[8,2,512,128]{3,2,1,0:T(8,128)(2,1)}), bf16[8,2,512,128]{3,2,1,0:T(8,128)(2,1)S(1)}, u32[]{:S(2)}, u32[]{:S(2)}) async-start(bf16[8,2,512,128]{3,2,1,0:T(8,128)(2,1)} %hold.3), calls=%async_computation.2 | async-start | bytes 4194304 | tf_op jit(solution)/shard_map/all_to_all | solution.py:462
  95.4 2.0 collective-permute-start.9
  99.4 5.6 %clean.5.refs_6_ = bf16[32,2,2,128,128]{4,3,2,1,0:T(8,128)(2,1)S(1)} custom-call(s32[2]{0:T(128)S(1)} %pad_add_fusion.at_ref, bf16[8,2,512,128]{3,2,1,0:T(8,128)(2,1)} %all-to-all-done.3.refs_0_, bf16[512,512]{1,0:T(8,128)(2,1)S(1)} %bitcast.10, bf16[512,512]{1,0:T(8,128)(2,1)S(1)} %copy-done.11, f32[512,8]{1,0:T(8,128)S(1)} %add_divide_fusion.refs_3_.refs_10_, ...), custom_call_target="tpu_custom_call" | custom-call | flops 3221225472 | bytes 4194304 | tf_op jit(solution)/shard_map/clean/pallas_call | solution.py:262
  105.0 2.0 copy-done.1
  107.0 3.3 %collective-permute-done.8.refs_7_.refs_1_ = bf16[8,1,2,128,128]{4,3,2,1,0:T(8,128)(2,1)S(1)} collective-permute-done((bf16[8,1,2,128,128]{4,3,2,1,0:T(8,128)(2,1)}, bf16[8,1,2,128,128]{4,3,2,1,0:T(8,128)(2,1)S(1)}, u32[]{:S(2)}, u32[]{:S(2)}) %collective-permute-start.8) | collective-permute-done | bytes 524320 | tf_op jit(solution)/shard_map/ppermute | solution.py:441
  111.1 11.7 %collective-permute-done.9.refs_9_.refs_3_ = bf16[8,1,2,128,128]{4,3,2,1,0:T(8,128)(2,1)S(1)} collective-permute-done((bf16[8,1,2,128,128]{4,3,2,1,0:T(8,128)(2,1)}, bf16[8,1,2,128,128]{4,3,2,1,0:T(8,128)(2,1)S(1)}, u32[]{:S(2)}, u32[]{:S(2)}) %collective-permute-start.9) | collective-permute-done | bytes 524320 | tf_op jit(solution)/shard_map/ppermute | solution.py:441
  123.7 2.2 copy-done.2
  129.9 4.5 %clean.6.refs_13_ = bf16[32,2,2,128,128]{4,3,2,1,0:T(8,128)(2,1)S(1)} custom-call(s32[2]{0:T(128)S(1)} %pad_add_fusion.at_ref, bf16[8,2,512,128]{3,2,1,0:T(8,128)(2,1)S(1)} %all-to-all-done.2.refs_0_, bf16[512,512]{1,0:T(8,128)(2,1)S(1)} %bitcast.11, bf16[512,512]{1,0:T(8,128)(2,1)S(1)} %copy-done.11, ...), custom_call_target="tpu_custom_call", output_to_operand_aliasing={{}: (7, {})} | custom-call | flops 3221225472 | bytes 4194304 | tf_op jit(solution)/shard_map/clean/pallas_call | solution.py:262
  134.4 2.0 copy-done.3
  136.4 6.1 %all-to-all-start.5 = ((bf16[32,2,2,128,128]{4,3,2,1,0:T(8,128)(2,1)}), bf16[32,2,2,128,128]{4,3,2,1,0:T(8,128)(2,1)}, u32[]{:S(2)}, u32[]{:S(2)}) async-start(bf16[32,2,2,128,128]{4,3,2,1,0:T(8,128)(2,1)} %copy-done.3), calls=%async_computation.5 | async-start | bytes 8388608 | tf_op jit(solution)/shard_map/all_to_all | solution.py:462
  142.6 2.2 collective-permute-start
  145.4 1.1 collective-permute-start.2
  147.1 1.2 collective-permute-start.4
  149.3 1.9 row_transform.1
  155.6 24.1 %collective-permute-done.refs_1_ = bf16[2,512,128]{2,1,0:T(8,128)(2,1)} collective-permute-done((bf16[2,512,128]{2,1,0:T(8,128)(2,1)}, bf16[2,512,128]{2,1,0:T(8,128)(2,1)}, u32[]{:S(2)}, u32[]{:S(2)}) %collective-permute-start) | collective-permute-done | bytes 262176 | tf_op jit(solution)/shard_map/ppermute | solution.py:468
  179.6 20.0 %collective-permute-done.1.refs_2_ = bf16[2,512,128]{2,1,0:T(8,128)(2,1)} collective-permute-done((bf16[2,512,128]{2,1,0:T(8,128)(2,1)}, bf16[2,512,128]{2,1,0:T(8,128)(2,1)}, u32[]{:S(2)}, u32[]{:S(2)}) %collective-permute-start.1) | collective-permute-done | bytes 262176 | tf_op jit(solution)/shard_map/ppermute | solution.py:468
  199.7 3.9 %collective-permute-done.3.refs_4_ = bf16[2,512,128]{2,1,0:T(8,128)(2,1)} collective-permute-done((bf16[2,512,128]{2,1,0:T(8,128)(2,1)}, bf16[2,512,128]{2,1,0:T(8,128)(2,1)}, u32[]{:S(2)}, u32[]{:S(2)}) %collective-permute-start.3) | collective-permute-done | bytes 262176 | tf_op jit(solution)/shard_map/ppermute | solution.py:468
  203.7 3.4 %collective-permute-start.11 = (bf16[2,16,32,128]{3,2,1,0:T(8,128)(2,1)S(1)}, bf16[2,16,32,128]{3,2,1,0:T(8,128)(2,1)S(1)}, u32[]{:S(2)}, u32[]{:S(2)}) collective-permute-start(bf16[2,16,32,128]{3,2,1,0:T(8,128)(2,1)S(1)} %get-tuple-element.42), channel_id=1, source_target_pairs={{0,6},{1,7},{2,4},{3,5},{4,2},{5,3},{6,0},{7,1},{8,14},{9,15},{10,... | collective-permute-start | bytes 786440 | tf_op jit(solution)/shard_map/ppermute | solution.py:468
  207.1 5.2 %collective-permute-done.5.refs_6_ = bf16[2,512,128]{2,1,0:T(8,128)(2,1)S(1)} collective-permute-done((bf16[2,512,128]{2,1,0:T(8,128)(2,1)S(1)}, bf16[2,512,128]{2,1,0:T(8,128)(2,1)S(1)}, u32[]{:S(2)}, u32[]{:S(2)}) %collective-permute-start.5) | collective-permute-done | bytes 262176 | tf_op jit(solution)/shard_map/ppermute | solution.py:468
  212.2 7.3 %collective-permute-done.10.refs_14_.refs_1_ = bf16[2,16,32,128]{3,2,1,0:T(8,128)(2,1)S(1)} collective-permute-done((bf16[2,16,32,128]{3,2,1,0:T(8,128)(2,1)S(1)}, bf16[2,16,32,128]{3,2,1,0:T(8,128)(2,1)S(1)}, u32[]{:S(2)}, u32[]{:S(2)}) %collective-permute-start.10) | collective-permute-done | bytes 262176 | tf_op jit(solution)/shard_map/ppermute | solution.py:468
  219.5 10.3 %collective-permute-done.11.refs_15_.refs_2_ = bf16[2,16,32,128]{3,2,1,0:T(8,128)(2,1)S(1)} collective-permute-done((bf16[2,16,32,128]{3,2,1,0:T(8,128)(2,1)S(1)}, bf16[2,16,32,128]{3,2,1,0:T(8,128)(2,1)S(1)}, u32[]{:S(2)}, u32[]{:S(2)}) %collective-permute-start.11) | collective-permute-done | bytes 262176 | tf_op jit(solution)/shard_map/ppermute | solution.py:468
  229.7 2.2 copy-done.4
  231.9 5.2 %clean.7 = bf16[32,1,2,128,128]{4,3,2,1,0:T(8,128)(2,1)S(1)} custom-call(s32[2]{0:T(128)S(1)} %pad_add_fusion.at_ref, bf16[2,512,128]{2,1,0:T(8,128)(2,1)S(1)} %copy-done.62, bf16[2,512,128]{2,1,0:T(8,128)(2,1)} %collective-permute-done.refs_1_, bf16[2,512,128]{2,1,0:T(8,128)(2,1)} %collective-permute-done.1.refs_2_, ...), custom_call_target="tpu_custom_call" | custom-call | flops 3221225472 | bytes 4194304 | tf_op jit(solution)/shard_map/clean/pallas_call | solution.py:262
  237.1 1.3 copy-done.16
  239.9 5.1 %all-to-all-start.4 = ((bf16[32,1,2,128,128]{4,3,2,1,0:T(8,128)(2,1)}), bf16[32,1,2,128,128]{4,3,2,1,0:T(8,128)(2,1)}, u32[]{:S(2)}, u32[]{:S(2)}) async-start(bf16[32,1,2,128,128]{4,3,2,1,0:T(8,128)(2,1)} %copy-done.16), calls=%async_computation.4 | async-start | bytes 4194304 | tf_op jit(solution)/shard_map/all_to_all | solution.py:462
  245.0 1.3 collective-permute-start.12
  248.7 5.3 %image.3.refs_0_ = bf16[2,16,32,4096]{3,2,1,0:T(8,128)(2,1)} custom-call(bf16[4,8,2,2,128,128]{5,4,3,2,1,0:T(8,128)(2,1)} %bitcast.6.x_ref, bf16[256,256]{1,0:T(8,128)(2,1)S(1)} %copy-done.23, bf16[1024,1024]{1,0:T(8,128)(2,1)S(1)} %copy-done), custom_call_target="tpu_custom_call" | custom-call | flops 2147483648 | bytes 4194304 | tf_op jit(solution)/shard_map/image/pallas_call | solution.py:327
  254.0 5.4 %image.4.refs_9_ = bf16[2,16,32,4096]{3,2,1,0:T(8,128)(2,1)} custom-call(bf16[4,8,2,2,128,128]{5,4,3,2,1,0:T(8,128)(2,1)} %bitcast.6.x_ref, bf16[256,256]{1,0:T(8,128)(2,1)S(1)} %copy-done.23, bf16[1024,1024]{1,0:T(8,128)(2,1)S(1)} %copy-done, bf16[2,16,32,4096]{3,2,1,0:T(8,128)(2,1)} %image.3.refs_0_), custom_call_target="tpu_custom_call", output_to_operand_aliasing={{}: (3, {})} | custom-call | flops 2147483648 | bytes 4194304 | tf_op jit(solution)/shard_map/image/pallas_call | solution.py:327
  259.4 5.6 %collective-permute-done.12.refs_3_ = bf16[2,16,32,128]{3,2,1,0:T(8,128)(2,1)S(1)} collective-permute-done((bf16[2,16,32,128]{3,2,1,0:T(8,128)(2,1)S(1)}, bf16[2,16,32,128]{3,2,1,0:T(8,128)(2,1)S(1)}, u32[]{:S(2)}, u32[]{:S(2)}) %collective-permute-start.12) | collective-permute-done | bytes 262176 | tf_op jit(solution)/shard_map/ppermute | solution.py:468
  265.0 10.7 %collective-permute-done.13.refs_4_ = bf16[2,16,32,128]{3,2,1,0:T(8,128)(2,1)S(1)} collective-permute-done((bf16[2,16,32,128]{3,2,1,0:T(8,128)(2,1)S(1)}, bf16[2,16,32,128]{3,2,1,0:T(8,128)(2,1)S(1)}, u32[]{:S(2)}, u32[]{:S(2)}) %collective-permute-start.13) | collective-permute-done | bytes 262176 | tf_op jit(solution)/shard_map/ppermute | solution.py:468
  275.7 2.7 collective-permute-done.15.refs_6_
  278.4 4.6 %place.1.refs_0_ = bf16[2,16,32,4096]{3,2,1,0:T(8,128)(2,1)} custom-call(s32[2]{0:T(128)S(1)} %pad_add_fusion.at_ref, bf16[2,16,32,128]{3,2,1,0:T(8,128)(2,1)S(1)} %copy-done.27, bf16[2,16,32,128]{3,2,1,0:T(8,128)(2,1)S(1)} %copy-done.29, bf16[2,16,32,128]{3,2,1,0:T(8,128)(2,1)S(1)} %copy-done.31, ...), custom_call_target="tpu_custom_call", output_to_operand_aliasing={{}: (10, {})} | custom-call | tf_op jit(solution)/shard_map/place/pallas_call | solution.py:405
  283.0 8.7 %all-to-all-done.4 = bf16[32,1,2,128,128]{4,3,2,1,0:T(8,128)(2,1)} async-done(((bf16[32,1,2,128,128]{4,3,2,1,0:T(8,128)(2,1)}), bf16[32,1,2,128,128]{4,3,2,1,0:T(8,128)(2,1)}, u32[]{:S(2)}, u32[]{:S(2)}) %all-to-all-start.4) | async-done | bytes 2097184 | tf_op jit(solution)/shard_map/all_to_all | solution.py:462
  291.7 5.3 %image.5 = bf16[2,16,32,4096]{3,2,1,0:T(8,128)(2,1)} custom-call(bf16[4,8,1,2,128,128]{5,4,3,2,1,0:T(8,128)(2,1)} %bitcast.5.x_ref, bf16[256,256]{1,0:T(8,128)(2,1)S(1)} %copy-done.23, bf16[1024,1024]{1,0:T(8,128)(2,1)S(1)} %copy-done, bf16[2,16,32,4096]{3,2,1,0:T(8,128)(2,1)} %place.1.refs_0_), custom_call_target="tpu_custom_call", output_to_operand_aliasing={{}: (3, {})} | custom-call | flops 2147483648 | bytes 4194304 | tf_op jit(solution)/shard_map/image/pallas_call | solution.py:327
  (146 shorter events, 27.1 us)
Async XLA Ops:
  1.7 19.0 %all-to-all-start = ((bf16[8,64,512]{2,1,0:T(8,128)(2,1)}), bf16[8,64,512]{2,1,0:T(8,128)(2,1)S(1)}, u32[]{:S(2)}, u32[]{:S(2)}) async-start(bf16[8,64,512]{2,1,0:T(8,128)(2,1)} %broadcast_in_dim.2), calls=%async_computation | async-start | bytes 1048576 | tf_op jit(solution)/shard_map/all_to_all | solution.py:462
  20.7 35.9 %copy-start.12 = (bf16[8,64,512]{2,1,0:T(8,128)(2,1)}, bf16[8,64,512]{2,1,0:T(8,128)(2,1)S(1)}, u32[]{:S(2)}) copy-start(bf16[8,64,512]{2,1,0:T(8,128)(2,1)S(1)} %all-to-all-done) | copy-start | bytes 1572868
  20.7 31.3 %all-to-all-start.1 = ((bf16[8,2,512,128]{3,2,1,0:T(8,128)(2,1)}), bf16[8,2,512,128]{3,2,1,0:T(8,128)(2,1)}, u32[]{:S(2)}, u32[]{:S(2)}) async-start(bf16[8,2,512,128]{3,2,1,0:T(8,128)(2,1)} %column_transform.3), calls=%async_computation.1 | async-start | bytes 4194304 | tf_op jit(solution)/shard_map/all_to_all | solution.py:462
  47.4 9.0 %copy-start.63 = (f32[512]{0:T(512)S(1)}, f32[512]{0:T(512)}, u32[]{:S(2)}) copy-start(f32[512]{0:T(512)} %param.26) | copy-start | bytes 6148
  47.4 9.0 %copy-start.64 = (f32[8]{0:T(128)S(1)}, f32[8]{0:T(128)}, u32[]{:S(2)}) copy-start(f32[8]{0:T(128)} %param.27) | copy-start | bytes 100
  47.4 9.2 %copy-start.7 = (bf16[8,2,512,128]{3,2,1,0:T(8,128)(2,1)S(1)}, bf16[8,2,512,128]{3,2,1,0:T(8,128)(2,1)}, u32[]{:S(2)}) copy-start(bf16[8,2,512,128]{3,2,1,0:T(8,128)(2,1)} %hold.2.refs_6_) | copy-start | bytes 6291460
  47.4 9.2 %copy-start.11 = (bf16[512,512]{1,0:T(8,128)(2,1)S(1)}, bf16[512,512]{1,0:T(8,128)(2,1)}, u32[]{:S(2)}) copy-start(bf16[512,512]{1,0:T(8,128)(2,1)} %copy-done.10) | copy-start | bytes 1572868
  47.4 9.2 %copy-start.32 = (bf16[256,256]{1,0:T(8,128)(2,1)S(1)}, bf16[256,256]{1,0:T(8,128)(2,1)}, u32[]{:S(2)}) copy-start(bf16[256,256]{1,0:T(8,128)(2,1)} %constant.31.clone.refs_5_.refs_12_) | copy-start | bytes 393220
  52.0 39.6 %all-to-all-start.3 = ((bf16[8,2,512,128]{3,2,1,0:T(8,128)(2,1)}), bf16[8,2,512,128]{3,2,1,0:T(8,128)(2,1)}, u32[]{:S(2)}, u32[]{:S(2)}) async-start(bf16[8,2,512,128]{3,2,1,0:T(8,128)(2,1)} %hold.2.refs_6_), calls=%async_computation.3 | async-start | bytes 4194304 | tf_op jit(solution)/shard_map/all_to_all | solution.py:462
  65.2 25.4 %collective-permute-start.7 = (bf16[8,1,2,128,128]{4,3,2,1,0:T(8,128)(2,1)S(1)}, bf16[8,1,2,128,128]{4,3,2,1,0:T(8,128)(2,1)S(1)}, u32[]{:S(2)}, u32[]{:S(2)}) collective-permute-start(bf16[8,1,2,128,128]{4,3,2,1,0:T(8,128)(2,1)S(1)} %get-tuple-element.37), channel_id=1, source_target_pairs={{0,16},{8,24},{16,0},{24,8},{1,17},{9,25},{17,1},{25,9},{2,18},{10... | collective-permute-start | bytes 1572872 | tf_op jit(solution)/shard_map/ppermute | solution.py:441
  91.5 32.1 %all-to-all-start.2 = ((bf16[8,2,512,128]{3,2,1,0:T(8,128)(2,1)}), bf16[8,2,512,128]{3,2,1,0:T(8,128)(2,1)S(1)}, u32[]{:S(2)}, u32[]{:S(2)}) async-start(bf16[8,2,512,128]{3,2,1,0:T(8,128)(2,1)} %hold.3), calls=%async_computation.2 | async-start | bytes 4194304 | tf_op jit(solution)/shard_map/all_to_all | solution.py:462
  95.4 14.9 %collective-permute-start.8 = (bf16[8,1,2,128,128]{4,3,2,1,0:T(8,128)(2,1)}, bf16[8,1,2,128,128]{4,3,2,1,0:T(8,128)(2,1)S(1)}, u32[]{:S(2)}, u32[]{:S(2)}) collective-permute-start(bf16[8,1,2,128,128]{4,3,2,1,0:T(8,128)(2,1)} %get-tuple-element.38), channel_id=1, source_target_pairs={{0,8},{8,16},{16,24},{24,0},{1,9},{9,17},{17,25},{25,1},{2,10},{10... | collective-permute-start | bytes 1572872 | tf_op jit(solution)/shard_map/ppermute | solution.py:441
  95.4 28.3 %copy-start.9 = (bf16[8,1,2,128,128]{4,3,2,1,0:T(8,128)(2,1)S(1)}, bf16[8,1,2,128,128]{4,3,2,1,0:T(8,128)(2,1)}, u32[]{:S(2)}) copy-start(bf16[8,1,2,128,128]{4,3,2,1,0:T(8,128)(2,1)} %copy-done.8) | copy-start | bytes 1572868
  95.4 27.4 %collective-permute-start.9 = (bf16[8,1,2,128,128]{4,3,2,1,0:T(8,128)(2,1)}, bf16[8,1,2,128,128]{4,3,2,1,0:T(8,128)(2,1)S(1)}, u32[]{:S(2)}, u32[]{:S(2)}) collective-permute-start(bf16[8,1,2,128,128]{4,3,2,1,0:T(8,128)(2,1)} %copy-done.38), channel_id=1, source_target_pairs={{0,24},{8,0},{16,8},{24,16},{1,25},{9,1},{17,9},{25,17},{2,26},{10... | collective-permute-start | bytes 1572872 | tf_op jit(solution)/shard_map/ppermute | solution.py:441
  136.4 12.9 %copy-start.19 = (bf16[8,1,2,128,128]{4,3,2,1,0:T(8,128)(2,1)S(1)}, bf16[8,1,2,128,128]{4,3,2,1,0:T(8,128)(2,1)}, u32[]{:S(2)}) copy-start(bf16[8,1,2,128,128]{4,3,2,1,0:T(8,128)(2,1)} %copy-done.17) | copy-start | bytes 1572868
  136.4 12.9 %copy-start.22 = (bf16[8,1,2,128,128]{4,3,2,1,0:T(8,128)(2,1)S(1)}, bf16[8,1,2,128,128]{4,3,2,1,0:T(8,128)(2,1)}, u32[]{:S(2)}) copy-start(bf16[8,1,2,128,128]{4,3,2,1,0:T(8,128)(2,1)} %copy-done.20) | copy-start | bytes 1572868
  136.4 12.9 %copy-start.25 = (bf16[8,1,2,128,128]{4,3,2,1,0:T(8,128)(2,1)S(1)}, bf16[8,1,2,128,128]{4,3,2,1,0:T(8,128)(2,1)}, u32[]{:S(2)}) copy-start(bf16[8,1,2,128,128]{4,3,2,1,0:T(8,128)(2,1)} %copy-done.24) | copy-start | bytes 1572868
  136.4 103.4 %all-to-all-start.5 = ((bf16[32,2,2,128,128]{4,3,2,1,0:T(8,128)(2,1)}), bf16[32,2,2,128,128]{4,3,2,1,0:T(8,128)(2,1)}, u32[]{:S(2)}, u32[]{:S(2)}) async-start(bf16[32,2,2,128,128]{4,3,2,1,0:T(8,128)(2,1)} %copy-done.3), calls=%async_computation.5 | async-start | bytes 8388608 | tf_op jit(solution)/shard_map/all_to_all | solution.py:462
  142.6 87.1 %copy-start.15 = (bf16[8,64,512]{2,1,0:T(8,128)(2,1)S(1)}, bf16[8,64,512]{2,1,0:T(8,128)(2,1)}, u32[]{:S(2)}) copy-start(bf16[8,64,512]{2,1,0:T(8,128)(2,1)} %copy-done.12) | copy-start | bytes 1572868
  142.6 37.0 %collective-permute-start = (bf16[2,512,128]{2,1,0:T(8,128)(2,1)}, bf16[2,512,128]{2,1,0:T(8,128)(2,1)}, u32[]{:S(2)}, u32[]{:S(2)}) collective-permute-start(bf16[2,512,128]{2,1,0:T(8,128)(2,1)} %copy-done.47), channel_id=1, source_target_pairs={{0,7},{1,6},{2,5},{3,4},{4,3},{5,2},{6,1},{7,0},{8,15},{9,14},{10,... | collective-permute-start | bytes 786440 | tf_op jit(solution)/shard_map/ppermute | solution.py:468
  144.8 54.8 %collective-permute-start.1 = (bf16[2,512,128]{2,1,0:T(8,128)(2,1)}, bf16[2,512,128]{2,1,0:T(8,128)(2,1)}, u32[]{:S(2)}, u32[]{:S(2)}) collective-permute-start(bf16[2,512,128]{2,1,0:T(8,128)(2,1)} %copy-done.46), channel_id=1, source_target_pairs={{0,6},{1,7},{2,4},{3,5},{4,2},{5,3},{6,0},{7,1},{8,14},{9,15},{10,... | collective-permute-start | bytes 786440 | tf_op jit(solution)/shard_map/ppermute | solution.py:468
  145.4 54.3 %collective-permute-start.2 = (bf16[2,512,128]{2,1,0:T(8,128)(2,1)}, bf16[2,512,128]{2,1,0:T(8,128)(2,1)}, u32[]{:S(2)}, u32[]{:S(2)}) collective-permute-start(bf16[2,512,128]{2,1,0:T(8,128)(2,1)} %copy-done.45), channel_id=1, source_target_pairs={{0,5},{1,4},{2,7},{3,6},{4,1},{5,0},{6,3},{7,2},{8,13},{9,12},{10,... | collective-permute-start | bytes 786440 | tf_op jit(solution)/shard_map/ppermute | solution.py:468
  146.5 57.2 %collective-permute-start.3 = (bf16[2,512,128]{2,1,0:T(8,128)(2,1)}, bf16[2,512,128]{2,1,0:T(8,128)(2,1)}, u32[]{:S(2)}, u32[]{:S(2)}) collective-permute-start(bf16[2,512,128]{2,1,0:T(8,128)(2,1)} %copy-done.44), channel_id=1, source_target_pairs={{0,4},{1,5},{2,6},{3,7},{4,0},{5,1},{6,2},{7,3},{8,12},{9,13},{10,... | collective-permute-start | bytes 786440 | tf_op jit(solution)/shard_map/ppermute | solution.py:468
  147.1 60.0 %collective-permute-start.4 = (bf16[2,512,128]{2,1,0:T(8,128)(2,1)}, bf16[2,512,128]{2,1,0:T(8,128)(2,1)}, u32[]{:S(2)}, u32[]{:S(2)}) collective-permute-start(bf16[2,512,128]{2,1,0:T(8,128)(2,1)} %copy-done.43), channel_id=1, source_target_pairs={{0,3},{1,2},{2,1},{3,0},{4,7},{5,6},{6,5},{7,4},{8,11},{9,10},{10,... | collective-permute-start | bytes 786440 | tf_op jit(solution)/shard_map/ppermute | solution.py:468
  148.3 31.3 %copy-start.42 = (bf16[2,512,128]{2,1,0:T(8,128)(2,1)S(1)}, bf16[2,512,128]{2,1,0:T(8,128)(2,1)}, u32[]{:S(2)}) copy-start(bf16[2,512,128]{2,1,0:T(8,128)(2,1)} %copy-done.41) | copy-start | bytes 786436
  148.3 51.3 %copy-start.40 = (bf16[2,512,128]{2,1,0:T(8,128)(2,1)S(1)}, bf16[2,512,128]{2,1,0:T(8,128)(2,1)}, u32[]{:S(2)}) copy-start(bf16[2,512,128]{2,1,0:T(8,128)(2,1)} %copy-done.39) | copy-start | bytes 786436
  148.3 81.4 %copy-start.36 = (bf16[256,256]{1,0:T(8,128)(2,1)S(1)}, bf16[256,256]{1,0:T(8,128)(2,1)}, u32[]{:S(2)}) copy-start(bf16[256,256]{1,0:T(8,128)(2,1)} %constant.30.clone.refs_4_.refs_11_) | copy-start | bytes 393220
  148.3 81.4 %copy-start.62 = (bf16[2,512,128]{2,1,0:T(8,128)(2,1)S(1)}, bf16[2,512,128]{2,1,0:T(8,128)(2,1)}, u32[]{:S(2)}) copy-start(bf16[2,512,128]{2,1,0:T(8,128)(2,1)} %copy-done.61) | copy-start | bytes 786436
  179.6 32.6 %collective-permute-start.5 = (bf16[2,512,128]{2,1,0:T(8,128)(2,1)S(1)}, bf16[2,512,128]{2,1,0:T(8,128)(2,1)S(1)}, u32[]{:S(2)}, u32[]{:S(2)}) collective-permute-start(bf16[2,512,128]{2,1,0:T(8,128)(2,1)S(1)} %copy-done.42), channel_id=1, source_target_pairs={{0,2},{1,3},{2,0},{3,1},{4,6},{5,7},{6,4},{7,5},{8,10},{9,11},{10,... | collective-permute-start | bytes 786440 | tf_op jit(solution)/shard_map/ppermute | solution.py:468
  199.6 12.6 %collective-permute-start.6 = (bf16[2,512,128]{2,1,0:T(8,128)(2,1)S(1)}, bf16[2,512,128]{2,1,0:T(8,128)(2,1)S(1)}, u32[]{:S(2)}, u32[]{:S(2)}) collective-permute-start(bf16[2,512,128]{2,1,0:T(8,128)(2,1)S(1)} %copy-done.40), channel_id=1, source_target_pairs={{0,1},{1,0},{2,3},{3,2},{4,5},{5,4},{6,7},{7,6},{8,9},{9,8},{10,11... | collective-permute-start | bytes 786440 | tf_op jit(solution)/shard_map/ppermute | solution.py:468
  199.7 19.8 %collective-permute-start.10 = (bf16[2,16,32,128]{3,2,1,0:T(8,128)(2,1)S(1)}, bf16[2,16,32,128]{3,2,1,0:T(8,128)(2,1)S(1)}, u32[]{:S(2)}, u32[]{:S(2)}) collective-permute-start(bf16[2,16,32,128]{3,2,1,0:T(8,128)(2,1)S(1)} %get-tuple-element.41), channel_id=1, source_target_pairs={{0,7},{1,6},{2,5},{3,4},{4,3},{5,2},{6,1},{7,0},{8,15},{9,14},{10,... | collective-permute-start | bytes 786440 | tf_op jit(solution)/shard_map/ppermute | solution.py:468
  203.7 26.0 %collective-permute-start.11 = (bf16[2,16,32,128]{3,2,1,0:T(8,128)(2,1)S(1)}, bf16[2,16,32,128]{3,2,1,0:T(8,128)(2,1)S(1)}, u32[]{:S(2)}, u32[]{:S(2)}) collective-permute-start(bf16[2,16,32,128]{3,2,1,0:T(8,128)(2,1)S(1)} %get-tuple-element.42), channel_id=1, source_target_pairs={{0,6},{1,7},{2,4},{3,5},{4,2},{5,3},{6,0},{7,1},{8,14},{9,15},{10,... | collective-permute-start | bytes 786440 | tf_op jit(solution)/shard_map/ppermute | solution.py:468
  239.8 5.2 %copy-start.57 = (bf16[2,16,32,128]{3,2,1,0:T(8,128)(2,1)S(1)}, bf16[2,16,32,128]{3,2,1,0:T(8,128)(2,1)}, u32[]{:S(2)}) copy-start(bf16[2,16,32,128]{3,2,1,0:T(8,128)(2,1)} %copy-done.56) | copy-start | bytes 786436
  239.8 6.4 %copy-start.55 = (bf16[2,16,32,128]{3,2,1,0:T(8,128)(2,1)S(1)}, bf16[2,16,32,128]{3,2,1,0:T(8,128)(2,1)}, u32[]{:S(2)}) copy-start(bf16[2,16,32,128]{3,2,1,0:T(8,128)(2,1)} %copy-done.54) | copy-start | bytes 786436
  239.8 7.0 %copy-start.53 = (bf16[2,16,32,128]{3,2,1,0:T(8,128)(2,1)S(1)}, bf16[2,16,32,128]{3,2,1,0:T(8,128)(2,1)}, u32[]{:S(2)}) copy-start(bf16[2,16,32,128]{3,2,1,0:T(8,128)(2,1)} %copy-done.52) | copy-start | bytes 786436
  239.8 8.2 %copy-start.51 = (bf16[2,16,32,128]{3,2,1,0:T(8,128)(2,1)S(1)}, bf16[2,16,32,128]{3,2,1,0:T(8,128)(2,1)}, u32[]{:S(2)}) copy-start(bf16[2,16,32,128]{3,2,1,0:T(8,128)(2,1)} %copy-done.50) | copy-start | bytes 786436
  239.8 8.7 %copy-start.49 = (bf16[2,16,32,128]{3,2,1,0:T(8,128)(2,1)S(1)}, bf16[2,16,32,128]{3,2,1,0:T(8,128)(2,1)}, u32[]{:S(2)}) copy-start(bf16[2,16,32,128]{3,2,1,0:T(8,128)(2,1)} %copy-done.48) | copy-start | bytes 786436
  239.9 8.9 %copy-start = (bf16[1024,1024]{1,0:T(8,128)(2,1)S(1)}, bf16[1024,1024]{1,0:T(8,128)(2,1)}, u32[]{:S(2)}) copy-start(bf16[1024,1024]{1,0:T(8,128)(2,1)} %constant.34.clone.order_ref.refs_8_) | copy-start | bytes 6291460
  239.9 8.9 %copy-start.23 = (bf16[256,256]{1,0:T(8,128)(2,1)S(1)}, bf16[256,256]{1,0:T(8,128)(2,1)}, u32[]{:S(2)}) copy-start(bf16[256,256]{1,0:T(8,128)(2,1)} %constant.33.clone.table_ref) | copy-start | bytes 393220
  239.9 51.8 %all-to-all-start.4 = ((bf16[32,1,2,128,128]{4,3,2,1,0:T(8,128)(2,1)}), bf16[32,1,2,128,128]{4,3,2,1,0:T(8,128)(2,1)}, u32[]{:S(2)}, u32[]{:S(2)}) async-start(bf16[32,1,2,128,128]{4,3,2,1,0:T(8,128)(2,1)} %copy-done.16), calls=%async_computation.4 | async-start | bytes 4194304 | tf_op jit(solution)/shard_map/all_to_all | solution.py:462
  245.0 20.0 %collective-permute-start.12 = (bf16[2,16,32,128]{3,2,1,0:T(8,128)(2,1)S(1)}, bf16[2,16,32,128]{3,2,1,0:T(8,128)(2,1)S(1)}, u32[]{:S(2)}, u32[]{:S(2)}) collective-permute-start(bf16[2,16,32,128]{3,2,1,0:T(8,128)(2,1)S(1)} %copy-done.57), channel_id=1, source_target_pairs={{0,5},{1,4},{2,7},{3,6},{4,1},{5,0},{6,3},{7,2},{8,13},{9,12},{10,... | collective-permute-start | bytes 786440 | tf_op jit(solution)/shard_map/ppermute | solution.py:468
  246.3 29.4 %collective-permute-start.13 = (bf16[2,16,32,128]{3,2,1,0:T(8,128)(2,1)S(1)}, bf16[2,16,32,128]{3,2,1,0:T(8,128)(2,1)S(1)}, u32[]{:S(2)}, u32[]{:S(2)}) collective-permute-start(bf16[2,16,32,128]{3,2,1,0:T(8,128)(2,1)S(1)} %copy-done.55), channel_id=1, source_target_pairs={{0,4},{1,5},{2,6},{3,7},{4,0},{5,1},{6,2},{7,3},{8,12},{9,13},{10,... | collective-permute-start | bytes 786440 | tf_op jit(solution)/shard_map/ppermute | solution.py:468
  246.9 28.8 %collective-permute-start.14 = (bf16[2,16,32,128]{3,2,1,0:T(8,128)(2,1)S(1)}, bf16[2,16,32,128]{3,2,1,0:T(8,128)(2,1)S(1)}, u32[]{:S(2)}, u32[]{:S(2)}) collective-permute-start(bf16[2,16,32,128]{3,2,1,0:T(8,128)(2,1)S(1)} %copy-done.53), channel_id=1, source_target_pairs={{0,3},{1,2},{2,1},{3,0},{4,7},{5,6},{6,5},{7,4},{8,11},{9,10},{10,... | collective-permute-start | bytes 786440 | tf_op jit(solution)/shard_map/ppermute | solution.py:468
  248.0 30.4 %collective-permute-start.15 = (bf16[2,16,32,128]{3,2,1,0:T(8,128)(2,1)S(1)}, bf16[2,16,32,128]{3,2,1,0:T(8,128)(2,1)S(1)}, u32[]{:S(2)}, u32[]{:S(2)}) collective-permute-start(bf16[2,16,32,128]{3,2,1,0:T(8,128)(2,1)S(1)} %copy-done.51), channel_id=1, source_target_pairs={{0,2},{1,3},{2,0},{3,1},{4,6},{5,7},{6,4},{7,5},{8,10},{9,11},{10,... | collective-permute-start | bytes 786440 | tf_op jit(solution)/shard_map/ppermute | solution.py:468
  248.6 29.8 %collective-permute-start.16 = (bf16[2,16,32,128]{3,2,1,0:T(8,128)(2,1)S(1)}, bf16[2,16,32,128]{3,2,1,0:T(8,128)(2,1)S(1)}, u32[]{:S(2)}, u32[]{:S(2)}) collective-permute-start(bf16[2,16,32,128]{3,2,1,0:T(8,128)(2,1)S(1)} %copy-done.49), channel_id=1, source_target_pairs={{0,1},{1,0},{2,3},{3,2},{4,5},{5,4},{6,7},{7,6},{8,9},{9,8},{10,11... | collective-permute-start | bytes 786440 | tf_op jit(solution)/shard_map/ppermute | solution.py:468
  254.0 24.4 %copy-start.27 = (bf16[2,16,32,128]{3,2,1,0:T(8,128)(2,1)S(1)}, bf16[2,16,32,128]{3,2,1,0:T(8,128)(2,1)}, u32[]{:S(2)}) copy-start(bf16[2,16,32,128]{3,2,1,0:T(8,128)(2,1)} %copy-done.26) | copy-start | bytes 786436
  254.0 24.4 %copy-start.29 = (bf16[2,16,32,128]{3,2,1,0:T(8,128)(2,1)S(1)}, bf16[2,16,32,128]{3,2,1,0:T(8,128)(2,1)}, u32[]{:S(2)}) copy-start(bf16[2,16,32,128]{3,2,1,0:T(8,128)(2,1)} %copy-done.28) | copy-start | bytes 786436
  254.0 24.4 %copy-start.31 = (bf16[2,16,32,128]{3,2,1,0:T(8,128)(2,1)S(1)}, bf16[2,16,32,128]{3,2,1,0:T(8,128)(2,1)}, u32[]{:S(2)}) copy-start(bf16[2,16,32,128]{3,2,1,0:T(8,128)(2,1)} %copy-done.30) | copy-start | bytes 786436
  (40 other events, 46.5 us)

commit v18 on v17

--- a/solution.py
+++ b/solution.py
@@ -11,7 +11,7 @@
 
 LANES = 128
 RADIX = 8
-VMEM_BYTES = 40 * 1024 * 1024
+VMEM_BYTES = 56 * 1024 * 1024
 
 
 def params():

time: 302 us -> 294 us (0.974)
  local copies, waits for them, and re-layouts: 42 us -> 12.6 us
  Pallas kernels: 68.2 us -> 86.4 us
  waiting for transfers between devices: 141 us -> 146 us
    unnamed x130 -> x70, local copies, waits for them, and re-layouts: 39.3 us -> 9.36 us
    pallas_call x4, Pallas kernels: 21.5 us -> 28.3 us  [clean(): pl.pallas_call(functools.partial(clean_kernel, split, len(before), steps)...]
    ppermute x3, waiting for transfers between devices: 37.9 us -> 41.4 us  [spread_rows(): lax.ppermute(parts[step], 'uv', [(z, (z + step) % count) for z in range(c...]
    pallas_call x2, Pallas kernels: 24.1 us -> 27.6 us  [column_transform(): pl.pallas_call(functools.partial(column_kernel, chunks, pieces // RADIX),...]
  transfers between devices with their start and end apart: 23 -> 23, of which waited for: 14 -> 14; matrix products, arithmetic and copies ran while one was open for 0% -> 1% of each run, Pallas kernels for 20% -> 25%
where the time goes in v18:
time: 294 us; the launch traced here: 290 us
  waiting for transfers between devices  146 us (50%)
  Pallas kernels  86.4 us (29%)
  starting transfers between devices  43.5 us (15%)
  local copies, waits for them, and re-layouts  12.6 us (4%)
    ppermute x14, waiting for transfers between devices, scatter(): lax.ppermute(pieces[step], 'chan', [(j, int(partner(np.int32(j), step, co...  89.8 us
    ppermute x3, waiting for transfers between devices, spread_rows(): lax.ppermute(parts[step], 'uv', [(z, (z + step) % count) for z in range(c...  41.4 us
    pallas_call x4, Pallas kernels, clean(): pl.pallas_call(functools.partial(clean_kernel, split, len(before), steps)...  28.3 us
    pallas_call x2, Pallas kernels, column_transform(): pl.pallas_call(functools.partial(column_kernel, chunks, pieces // RADIX),...  27.6 us
    all_to_all x6, starting transfers between devices, exchange(): return lax.all_to_all(x, axes, split_axis=0, concat_axis=0, tiled=True)  26 us
    pallas_call x3, Pallas kernels, image(): pl.pallas_call(functools.partial(image_kernel, scale), grid=(chans // blo...  18 us
    all_to_all x6, waiting for transfers between devices, exchange(): return lax.all_to_all(x, axes, split_axis=0, concat_axis=0, tiled=True)  14.4 us
    ppermute x14, starting transfers between devices, scatter(): lax.ppermute(pieces[step], 'chan', [(j, int(partner(np.int32(j), step, co...  12.9 us
  transfers between devices with their start and end apart: 23, of which 14 were waited for; matrix products, arithmetic and copies ran while one was open for 1% of the time, Pallas kernels for 25%

profile of v18, /device:TPU:8, one launch (start us, length us, event | category | flops | bytes accessed | tf_op | source)
XLA Modules:
  0.0 289.8 jit_solution(11143926231535206851)
XLA Ops:
  0.0 1.7 broadcast_in_dim.2
  1.7 3.7 %all-to-all-start = ((bf16[8,64,512]{2,1,0:T(8,128)(2,1)}), bf16[8,64,512]{2,1,0:T(8,128)(2,1)S(1)}, u32[]{:S(2)}, u32[]{:S(2)}) async-start(bf16[8,64,512]{2,1,0:T(8,128)(2,1)} %broadcast_in_dim.2), calls=%async_computation | async-start | bytes 1048576 | tf_op jit(solution)/shard_map/all_to_all | solution.py:462
  6.0 11.3 %column_transform.3 = bf16[8,2,512,128]{3,2,1,0:T(8,128)(2,1)} custom-call(s32[2]{0:T(128)} %pad_add_fusion.at_ref, bf16[2,512,4096]{2,1,0:T(8,128)(2,1)} %bitcast.14, f32[8,2,512]{2,1,0:T(2,128)} %constant.28.clone.twiddle_ref, bf16[1024,1024]{1,0:T(8,128)(2,1)} %constant.29.clone.table_ref), custom_call_target="tpu_custom_call" | custom-call | flops 8589934592 | bytes 16777216 | tf_op jit(solution)/shard_map/column_transform/pallas_call | solution.py:171
  18.1 4.2 %all-to-all-start.1 = ((bf16[8,2,512,128]{3,2,1,0:T(8,128)(2,1)}), bf16[8,2,512,128]{3,2,1,0:T(8,128)(2,1)S(1)}, u32[]{:S(2)}, u32[]{:S(2)}) async-start(bf16[8,2,512,128]{3,2,1,0:T(8,128)(2,1)} %column_transform.3), calls=%async_computation.1 | async-start | bytes 4194304 | tf_op jit(solution)/shard_map/all_to_all | solution.py:462
  22.3 16.3 %column_transform.2 = (bf16[8,2,512,128]{3,2,1,0:T(8,128)(2,1)}, bf16[8,2,512,128]{3,2,1,0:T(8,128)(2,1)}, bf16[2,512,128]{2,1,0:T(8,128)(2,1)}, bf16[2,512,128]...) custom-call(s32[2]{0:T(128)} %pad_add_fusion.at_ref, ...), custom_call_target="tpu_custom_call" | custom-call | flops 25769803776 | bytes 16777216 | tf_op jit(solution)/shard_map/column_transform/pallas_call | solution.py:171
  38.7 2.1 turn.1.refs_1_.refs_2_.refs_9_
  40.7 8.2 %all-to-all-done.1.refs_0_ = bf16[8,2,512,128]{3,2,1,0:T(8,128)(2,1)S(1)} async-done(((bf16[8,2,512,128]{3,2,1,0:T(8,128)(2,1)}), bf16[8,2,512,128]{3,2,1,0:T(8,128)(2,1)S(1)}, u32[]{:S(2)}, u32[]{:S(2)}) %all-to-all-start.1) | async-done | bytes 2097184 | tf_op jit(solution)/shard_map/all_to_all | solution.py:462
  49.0 1.4 copy-done.5
  50.3 3.6 %all-to-all-start.3 = ((bf16[8,2,512,128]{3,2,1,0:T(8,128)(2,1)}), bf16[8,2,512,128]{3,2,1,0:T(8,128)(2,1)S(1)}, u32[]{:S(2)}, u32[]{:S(2)}) async-start(bf16[8,2,512,128]{3,2,1,0:T(8,128)(2,1)} %hold.2.refs_6_), calls=%async_computation.3 | async-start | bytes 4194304 | tf_op jit(solution)/shard_map/all_to_all | solution.py:462
  54.0 0.9 add_divide_fusion.refs_3_.refs_10_
  54.8 6.8 %clean.4 = (bf16[8,1,2,128,128]{4,3,2,1,0:T(8,128)(2,1)}, bf16[8,1,2,128,128]{4,3,2,1,0:T(8,128)(2,1)}, bf16[8,1,2,128,128]{4,3,2,1,0:T(8,128)(2,1)}, bf16[8,1,2,128,128]{4,3,2,1,0:T(8,128)(2,1)}) custom-call(s32[2]{0:T(128)} %pad_add_fusion.at_ref, bf16[8,2,512,128]{3,2,1,0:T(8,128)(2,1)} %copy-done.5, bf16[512,512]{1,0:T(8,128)(2,1)} %bitcast.10, ...), custom_call_target="tpu_custom_call" | custom-call | flops 3221225472 | bytes 4194304 | tf_op jit(solution)/shard_map/clean/pallas_call | solution.py:262
  61.7 2.6 collective-permute-start.7
  64.3 23.1 %collective-permute-done.7.refs_1_.refs_8_.refs_2_ = bf16[8,1,2,128,128]{4,3,2,1,0:T(8,128)(2,1)S(1)} collective-permute-done((bf16[8,1,2,128,128]{4,3,2,1,0:T(8,128)(2,1)}, bf16[8,1,2,128,128]{4,3,2,1,0:T(8,128)(2,1)S(1)}, u32[]{:S(2)}, u32[]{:S(2)}) %collective-permute-start.7) | collective-permute-done | bytes 524320 | tf_op jit(solution)/shard_map/ppermute | solution.py:441
  87.4 0.8 copy-done.2
  88.2 1.4 copy-done.4
  89.6 3.9 %all-to-all-start.2 = ((bf16[8,2,512,128]{3,2,1,0:T(8,128)(2,1)}), bf16[8,2,512,128]{3,2,1,0:T(8,128)(2,1)S(1)}, u32[]{:S(2)}, u32[]{:S(2)}) async-start(bf16[8,2,512,128]{3,2,1,0:T(8,128)(2,1)} %hold.3), calls=%async_computation.2 | async-start | bytes 4194304 | tf_op jit(solution)/shard_map/all_to_all | solution.py:462
  93.5 2.0 collective-permute-start.9
  95.5 7.1 %clean.5.refs_6_ = bf16[32,2,2,128,128]{4,3,2,1,0:T(8,128)(2,1)} custom-call(s32[2]{0:T(128)} %pad_add_fusion.at_ref, bf16[8,2,512,128]{3,2,1,0:T(8,128)(2,1)} %copy-done.4, bf16[512,512]{1,0:T(8,128)(2,1)} %bitcast.11, bf16[512,512]{1,0:T(8,128)(2,1)} %turn.1.refs_1_.refs_2_.refs_9_, f32[512,8]{1,0:T(8,128)} %add_divide_fusion.refs_3_.refs_10_, ...), custom_call_target="tpu_custom_call" | custom-call | flops 3221225472 | bytes 4194304 | tf_op jit(solution)/shard_map/clean/pallas_call | solution.py:262
  102.6 5.8 %collective-permute-done.8.refs_7_.refs_1_ = bf16[8,1,2,128,128]{4,3,2,1,0:T(8,128)(2,1)S(1)} collective-permute-done((bf16[8,1,2,128,128]{4,3,2,1,0:T(8,128)(2,1)}, bf16[8,1,2,128,128]{4,3,2,1,0:T(8,128)(2,1)S(1)}, u32[]{:S(2)}, u32[]{:S(2)}) %collective-permute-start.8) | collective-permute-done | bytes 524320 | tf_op jit(solution)/shard_map/ppermute | solution.py:441
  108.4 12.4 %collective-permute-done.9.refs_9_.refs_3_ = bf16[8,1,2,128,128]{4,3,2,1,0:T(8,128)(2,1)S(1)} collective-permute-done((bf16[8,1,2,128,128]{4,3,2,1,0:T(8,128)(2,1)}, bf16[8,1,2,128,128]{4,3,2,1,0:T(8,128)(2,1)S(1)}, u32[]{:S(2)}, u32[]{:S(2)}) %collective-permute-start.9) | collective-permute-done | bytes 524320 | tf_op jit(solution)/shard_map/ppermute | solution.py:441
  121.6 1.3 copy-done.1
  123.0 7.1 %clean.6.refs_13_ = bf16[32,2,2,128,128]{4,3,2,1,0:T(8,128)(2,1)} custom-call(s32[2]{0:T(128)} %pad_add_fusion.at_ref, bf16[8,2,512,128]{3,2,1,0:T(8,128)(2,1)} %copy-done.1, bf16[512,512]{1,0:T(8,128)(2,1)} %bitcast.12, bf16[512,512]{1,0:T(8,128)(2,1)} %turn.1.refs_1_.refs_2_.refs_9_, ...), custom_call_target="tpu_custom_call", output_to_operand_aliasing={{}: (7, {})} | custom-call | flops 3221225472 | bytes 4194304 | tf_op jit(solution)/shard_map/clean/pallas_call | solution.py:262
  130.1 5.5 %all-to-all-start.5 = ((bf16[32,2,2,128,128]{4,3,2,1,0:T(8,128)(2,1)}), bf16[32,2,2,128,128]{4,3,2,1,0:T(8,128)(2,1)}, u32[]{:S(2)}, u32[]{:S(2)}) async-start(bf16[32,2,2,128,128]{4,3,2,1,0:T(8,128)(2,1)} %clean.6.refs_13_), calls=%async_computation.5 | async-start | bytes 8388608 | tf_op jit(solution)/shard_map/all_to_all | solution.py:462
  135.7 2.2 collective-permute-start
  138.4 1.1 collective-permute-start.2
  140.1 1.2 collective-permute-start.4
  141.4 1.6 dynamic-slice_bitcast_fusion.refs_4_
  142.9 4.2 %row_transform.1 = (bf16[2,16,32,128]{3,2,1,0:T(8,128)(2,1)}, bf16[2,16,32,128]{3,2,1,0:T(8,128)(2,1)}, bf16[2,16,32,128]{3,2,1,0:T(8,128)(2,1)}, bf16[2,16,32,1...) custom-call(s32[2]{0:T(128)} %pad_add_fusion.at_ref, ...), custom_call_target="tpu_custom_call" | custom-call | tf_op jit(solution)/shard_map/row_transform/pallas_call | solution.py:380
  147.1 25.4 %collective-permute-done.refs_1_ = bf16[2,512,128]{2,1,0:T(8,128)(2,1)S(1)} collective-permute-done((bf16[2,512,128]{2,1,0:T(8,128)(2,1)S(1)}, bf16[2,512,128]{2,1,0:T(8,128)(2,1)S(1)}, u32[]{:S(2)}, u32[]{:S(2)}) %collective-permute-start) | collective-permute-done | bytes 262176 | tf_op jit(solution)/shard_map/ppermute | solution.py:468
  172.6 20.0 %collective-permute-done.1.refs_2_ = bf16[2,512,128]{2,1,0:T(8,128)(2,1)S(1)} collective-permute-done((bf16[2,512,128]{2,1,0:T(8,128)(2,1)S(1)}, bf16[2,512,128]{2,1,0:T(8,128)(2,1)S(1)}, u32[]{:S(2)}, u32[]{:S(2)}) %collective-permute-start.1) | collective-permute-done | bytes 262176 | tf_op jit(solution)/shard_map/ppermute | solution.py:468
  192.7 3.9 %collective-permute-done.3.refs_4_ = bf16[2,512,128]{2,1,0:T(8,128)(2,1)S(1)} collective-permute-done((bf16[2,512,128]{2,1,0:T(8,128)(2,1)S(1)}, bf16[2,512,128]{2,1,0:T(8,128)(2,1)S(1)}, u32[]{:S(2)}, u32[]{:S(2)}) %collective-permute-start.3) | collective-permute-done | bytes 262176 | tf_op jit(solution)/shard_map/ppermute | solution.py:468
  196.6 3.4 %collective-permute-start.11 = (bf16[2,16,32,128]{3,2,1,0:T(8,128)(2,1)}, bf16[2,16,32,128]{3,2,1,0:T(8,128)(2,1)S(1)}, u32[]{:S(2)}, u32[]{:S(2)}) collective-permute-start(bf16[2,16,32,128]{3,2,1,0:T(8,128)(2,1)} %get-tuple-element.42), channel_id=1, source_target_pairs={{0,6},{1,7},{2,4},{3,5},{4,2},{5,3},{6,0},{7,1},{8,14},{9,15},{10,... | collective-permute-start | bytes 786440 | tf_op jit(solution)/shard_map/ppermute | solution.py:468
  200.0 5.3 %collective-permute-done.5.refs_6_ = bf16[2,512,128]{2,1,0:T(8,128)(2,1)S(1)} collective-permute-done((bf16[2,512,128]{2,1,0:T(8,128)(2,1)S(1)}, bf16[2,512,128]{2,1,0:T(8,128)(2,1)S(1)}, u32[]{:S(2)}, u32[]{:S(2)}) %collective-permute-start.5) | collective-permute-done | bytes 262176 | tf_op jit(solution)/shard_map/ppermute | solution.py:468
  205.2 7.3 %collective-permute-done.10.refs_14_.refs_1_ = bf16[2,16,32,128]{3,2,1,0:T(8,128)(2,1)S(1)} collective-permute-done((bf16[2,16,32,128]{3,2,1,0:T(8,128)(2,1)}, bf16[2,16,32,128]{3,2,1,0:T(8,128)(2,1)S(1)}, u32[]{:S(2)}, u32[]{:S(2)}) %collective-permute-start.10) | collective-permute-done | bytes 262176 | tf_op jit(solution)/shard_map/ppermute | solution.py:468
  212.5 10.3 %collective-permute-done.11.refs_15_.refs_2_ = bf16[2,16,32,128]{3,2,1,0:T(8,128)(2,1)S(1)} collective-permute-done((bf16[2,16,32,128]{3,2,1,0:T(8,128)(2,1)}, bf16[2,16,32,128]{3,2,1,0:T(8,128)(2,1)S(1)}, u32[]{:S(2)}, u32[]{:S(2)}) %collective-permute-start.11) | collective-permute-done | bytes 262176 | tf_op jit(solution)/shard_map/ppermute | solution.py:468
  223.5 7.3 %clean.7 = bf16[32,1,2,128,128]{4,3,2,1,0:T(8,128)(2,1)} custom-call(s32[2]{0:T(128)} %pad_add_fusion.at_ref, bf16[2,512,128]{2,1,0:T(8,128)(2,1)} %get-tuple-element.27.refs_0_, bf16[2,512,128]{2,1,0:T(8,128)(2,1)} %copy-done.29, bf16[2,512,128]{2,1,0:T(8,128)(2,1)} %copy-done.30, bf16[2,512,128]{2,1,0:T(8,128)(2,1)} %copy-done.31, ...), custom_call_target="tpu_custom_call" | custom-call | flops 3221225472 | bytes 4194304 | tf_op jit(solution)/shard_map/clean/pallas_call | solution.py:262
  230.8 5.0 %all-to-all-start.4 = ((bf16[32,1,2,128,128]{4,3,2,1,0:T(8,128)(2,1)}), bf16[32,1,2,128,128]{4,3,2,1,0:T(8,128)(2,1)S(1)}, u32[]{:S(2)}, u32[]{:S(2)}) async-start(bf16[32,1,2,128,128]{4,3,2,1,0:T(8,128)(2,1)} %clean.7), calls=%async_computation.4 | async-start | bytes 4194304 | tf_op jit(solution)/shard_map/all_to_all | solution.py:462
  235.9 1.3 collective-permute-start.12
  237.7 1.1 collective-permute-start.14
  239.6 6.0 %image.3.refs_0_ = bf16[2,16,32,4096]{3,2,1,0:T(8,128)(2,1)} custom-call(bf16[4,8,2,2,128,128]{5,4,3,2,1,0:T(8,128)(2,1)} %bitcast.6.x_ref, bf16[256,256]{1,0:T(8,128)(2,1)} %constant.33.clone.table_ref, bf16[1024,1024]{1,0:T(8,128)(2,1)} %constant.34.clone.order_ref.refs_8_), custom_call_target="tpu_custom_call" | custom-call | flops 2147483648 | bytes 4194304 | tf_op jit(solution)/shard_map/image/pallas_call | solution.py:327
  245.6 6.0 %image.4.refs_9_ = bf16[2,16,32,4096]{3,2,1,0:T(8,128)(2,1)} custom-call(bf16[4,8,2,2,128,128]{5,4,3,2,1,0:T(8,128)(2,1)} %bitcast.6.x_ref, bf16[256,256]{1,0:T(8,128)(2,1)} %constant.33.clone.table_ref, bf16[1024,1024]{1,0:T(8,128)(2,1)} %constant.34.clone.order_ref.refs_8_, bf16[2,16,32,4096]{3,2,1,0:T(8,128)(2,1)} %image.3.refs_0_), custom_call_target="tpu_custom_call", output_to_operand_aliasing={{}: (3, {})} | custom-call | flops 2147483648 | bytes 4194304 | tf_op jit(solution)/shard_map/image/pallas_call | solution.py:327
  251.6 4.3 %collective-permute-done.12.refs_3_ = bf16[2,16,32,128]{3,2,1,0:T(8,128)(2,1)S(1)} collective-permute-done((bf16[2,16,32,128]{3,2,1,0:T(8,128)(2,1)S(1)}, bf16[2,16,32,128]{3,2,1,0:T(8,128)(2,1)S(1)}, u32[]{:S(2)}, u32[]{:S(2)}) %collective-permute-start.12) | collective-permute-done | bytes 262176 | tf_op jit(solution)/shard_map/ppermute | solution.py:468
  255.9 10.7 %collective-permute-done.13.refs_4_ = bf16[2,16,32,128]{3,2,1,0:T(8,128)(2,1)S(1)} collective-permute-done((bf16[2,16,32,128]{3,2,1,0:T(8,128)(2,1)S(1)}, bf16[2,16,32,128]{3,2,1,0:T(8,128)(2,1)S(1)}, u32[]{:S(2)}, u32[]{:S(2)}) %collective-permute-start.13) | collective-permute-done | bytes 262176 | tf_op jit(solution)/shard_map/ppermute | solution.py:468
  266.6 2.7 collective-permute-done.15.refs_6_
  270.1 6.2 %place.1.refs_0_ = bf16[2,16,32,4096]{3,2,1,0:T(8,128)(2,1)} custom-call(s32[2]{0:T(128)} %pad_add_fusion.at_ref, bf16[2,16,32,128]{3,2,1,0:T(8,128)(2,1)} %get-tuple-element.43.refs_0_, bf16[2,16,32,128]{3,2,1,0:T(8,128)(2,1)} %copy-done.8, bf16[2,16,32,128]{3,2,1,0:T(8,128)(2,1)} %copy-done.9, ...), custom_call_target="tpu_custom_call", output_to_operand_aliasing={{}: (10, {})} | custom-call | tf_op jit(solution)/shard_map/place/pallas_call | solution.py:405
  276.4 6.1 %all-to-all-done.4 = bf16[32,1,2,128,128]{4,3,2,1,0:T(8,128)(2,1)S(1)} async-done(((bf16[32,1,2,128,128]{4,3,2,1,0:T(8,128)(2,1)}), bf16[32,1,2,128,128]{4,3,2,1,0:T(8,128)(2,1)S(1)}, u32[]{:S(2)}, u32[]{:S(2)}) %all-to-all-start.4) | async-done | bytes 2097184 | tf_op jit(solution)/shard_map/all_to_all | solution.py:462
  282.5 1.3 copy-done
  283.9 6.0 %image.5 = bf16[2,16,32,4096]{3,2,1,0:T(8,128)(2,1)} custom-call(bf16[4,8,1,2,128,128]{5,4,3,2,1,0:T(8,128)(2,1)} %bitcast.8, bf16[256,256]{1,0:T(8,128)(2,1)} %constant.33.clone.table_ref, bf16[1024,1024]{1,0:T(8,128)(2,1)} %constant.34.clone.order_ref.refs_8_, bf16[2,16,32,4096]{3,2,1,0:T(8,128)(2,1)} %place.1.refs_0_), custom_call_target="tpu_custom_call", output_to_operand_aliasing={{}: (3, {})} | custom-call | flops 2147483648 | bytes 4194304 | tf_op jit(solution)/shard_map/image/pallas_call | solution.py:327
  (86 shorter events, 6.4 us)
Async XLA Ops:
  1.7 15.7 %all-to-all-start = ((bf16[8,64,512]{2,1,0:T(8,128)(2,1)}), bf16[8,64,512]{2,1,0:T(8,128)(2,1)S(1)}, u32[]{:S(2)}, u32[]{:S(2)}) async-start(bf16[8,64,512]{2,1,0:T(8,128)(2,1)} %broadcast_in_dim.2), calls=%async_computation | async-start | bytes 1048576 | tf_op jit(solution)/shard_map/all_to_all | solution.py:462
  18.1 30.8 %all-to-all-start.1 = ((bf16[8,2,512,128]{3,2,1,0:T(8,128)(2,1)}), bf16[8,2,512,128]{3,2,1,0:T(8,128)(2,1)S(1)}, u32[]{:S(2)}, u32[]{:S(2)}) async-start(bf16[8,2,512,128]{3,2,1,0:T(8,128)(2,1)} %column_transform.3), calls=%async_computation.1 | async-start | bytes 4194304 | tf_op jit(solution)/shard_map/all_to_all | solution.py:462
  40.7 13.2 %copy-start.15 = (f32[512]{0:T(512)S(1)}, f32[512]{0:T(512)}, u32[]{:S(2)}) copy-start(f32[512]{0:T(512)} %param.26) | copy-start | bytes 6148
  40.7 13.2 %copy-start.16 = (f32[8]{0:T(128)S(1)}, f32[8]{0:T(128)}, u32[]{:S(2)}) copy-start(f32[8]{0:T(128)} %param.27) | copy-start | bytes 100
  50.3 37.9 %all-to-all-start.3 = ((bf16[8,2,512,128]{3,2,1,0:T(8,128)(2,1)}), bf16[8,2,512,128]{3,2,1,0:T(8,128)(2,1)S(1)}, u32[]{:S(2)}, u32[]{:S(2)}) async-start(bf16[8,2,512,128]{3,2,1,0:T(8,128)(2,1)} %hold.2.refs_6_), calls=%async_computation.3 | async-start | bytes 4194304 | tf_op jit(solution)/shard_map/all_to_all | solution.py:462
  61.7 25.8 %collective-permute-start.7 = (bf16[8,1,2,128,128]{4,3,2,1,0:T(8,128)(2,1)}, bf16[8,1,2,128,128]{4,3,2,1,0:T(8,128)(2,1)S(1)}, u32[]{:S(2)}, u32[]{:S(2)}) collective-permute-start(bf16[8,1,2,128,128]{4,3,2,1,0:T(8,128)(2,1)} %get-tuple-element.37), channel_id=1, source_target_pairs={{0,16},{8,24},{16,0},{24,8},{1,17},{9,25},{17,1},{25,9},{2,18},{10... | collective-permute-start | bytes 1572872 | tf_op jit(solution)/shard_map/ppermute | solution.py:441
  89.6 31.2 %all-to-all-start.2 = ((bf16[8,2,512,128]{3,2,1,0:T(8,128)(2,1)}), bf16[8,2,512,128]{3,2,1,0:T(8,128)(2,1)S(1)}, u32[]{:S(2)}, u32[]{:S(2)}) async-start(bf16[8,2,512,128]{3,2,1,0:T(8,128)(2,1)} %hold.3), calls=%async_computation.2 | async-start | bytes 4194304 | tf_op jit(solution)/shard_map/all_to_all | solution.py:462
  93.5 14.9 %collective-permute-start.8 = (bf16[8,1,2,128,128]{4,3,2,1,0:T(8,128)(2,1)}, bf16[8,1,2,128,128]{4,3,2,1,0:T(8,128)(2,1)S(1)}, u32[]{:S(2)}, u32[]{:S(2)}) collective-permute-start(bf16[8,1,2,128,128]{4,3,2,1,0:T(8,128)(2,1)} %get-tuple-element.38), channel_id=1, source_target_pairs={{0,8},{8,16},{16,24},{24,0},{1,9},{9,17},{17,25},{25,1},{2,10},{10... | collective-permute-start | bytes 1572872 | tf_op jit(solution)/shard_map/ppermute | solution.py:441
  93.5 27.4 %collective-permute-start.9 = (bf16[8,1,2,128,128]{4,3,2,1,0:T(8,128)(2,1)}, bf16[8,1,2,128,128]{4,3,2,1,0:T(8,128)(2,1)S(1)}, u32[]{:S(2)}, u32[]{:S(2)}) collective-permute-start(bf16[8,1,2,128,128]{4,3,2,1,0:T(8,128)(2,1)} %get-tuple-element.39), channel_id=1, source_target_pairs={{0,24},{8,0},{16,8},{24,16},{1,25},{9,1},{17,9},{25,17},{2,26},{10... | collective-permute-start | bytes 1572872 | tf_op jit(solution)/shard_map/ppermute | solution.py:441
  108.4 12.4 %copy-start.6 = (bf16[8,1,2,128,128]{4,3,2,1,0:T(8,128)(2,1)}, bf16[8,1,2,128,128]{4,3,2,1,0:T(8,128)(2,1)S(1)}, u32[]{:S(2)}) copy-start(bf16[8,1,2,128,128]{4,3,2,1,0:T(8,128)(2,1)S(1)} %collective-permute-done.8.refs_7_.refs_1_) | copy-start | bytes 1572868
  130.1 5.6 %copy-start.23 = (bf16[2,512,128]{2,1,0:T(8,128)(2,1)S(1)}, bf16[2,512,128]{2,1,0:T(8,128)(2,1)}, u32[]{:S(2)}) copy-start(bf16[2,512,128]{2,1,0:T(8,128)(2,1)} %get-tuple-element.28) | copy-start | bytes 786436
  130.1 7.8 %copy-start.22 = (bf16[2,512,128]{2,1,0:T(8,128)(2,1)S(1)}, bf16[2,512,128]{2,1,0:T(8,128)(2,1)}, u32[]{:S(2)}) copy-start(bf16[2,512,128]{2,1,0:T(8,128)(2,1)} %get-tuple-element.29) | copy-start | bytes 786436
  130.1 8.4 %copy-start.21 = (bf16[2,512,128]{2,1,0:T(8,128)(2,1)S(1)}, bf16[2,512,128]{2,1,0:T(8,128)(2,1)}, u32[]{:S(2)}) copy-start(bf16[2,512,128]{2,1,0:T(8,128)(2,1)} %get-tuple-element.30) | copy-start | bytes 786436
  130.1 9.5 %copy-start.20 = (bf16[2,512,128]{2,1,0:T(8,128)(2,1)S(1)}, bf16[2,512,128]{2,1,0:T(8,128)(2,1)}, u32[]{:S(2)}) copy-start(bf16[2,512,128]{2,1,0:T(8,128)(2,1)} %get-tuple-element.31) | copy-start | bytes 786436
  130.1 10.1 %copy-start.19 = (bf16[2,512,128]{2,1,0:T(8,128)(2,1)S(1)}, bf16[2,512,128]{2,1,0:T(8,128)(2,1)}, u32[]{:S(2)}) copy-start(bf16[2,512,128]{2,1,0:T(8,128)(2,1)} %get-tuple-element.32) | copy-start | bytes 786436
  130.1 100.7 %all-to-all-start.5 = ((bf16[32,2,2,128,128]{4,3,2,1,0:T(8,128)(2,1)}), bf16[32,2,2,128,128]{4,3,2,1,0:T(8,128)(2,1)}, u32[]{:S(2)}, u32[]{:S(2)}) async-start(bf16[32,2,2,128,128]{4,3,2,1,0:T(8,128)(2,1)} %clean.6.refs_13_), calls=%async_computation.5 | async-start | bytes 8388608 | tf_op jit(solution)/shard_map/all_to_all | solution.py:462
  135.6 36.9 %copy-start.18 = (bf16[2,512,128]{2,1,0:T(8,128)(2,1)S(1)}, bf16[2,512,128]{2,1,0:T(8,128)(2,1)}, u32[]{:S(2)}) copy-start(bf16[2,512,128]{2,1,0:T(8,128)(2,1)} %get-tuple-element.33) | copy-start | bytes 786436
  135.6 56.9 %copy-start.17 = (bf16[2,512,128]{2,1,0:T(8,128)(2,1)S(1)}, bf16[2,512,128]{2,1,0:T(8,128)(2,1)}, u32[]{:S(2)}) copy-start(bf16[2,512,128]{2,1,0:T(8,128)(2,1)} %get-tuple-element.34) | copy-start | bytes 786436
  135.7 36.9 %collective-permute-start = (bf16[2,512,128]{2,1,0:T(8,128)(2,1)S(1)}, bf16[2,512,128]{2,1,0:T(8,128)(2,1)S(1)}, u32[]{:S(2)}, u32[]{:S(2)}) collective-permute-start(bf16[2,512,128]{2,1,0:T(8,128)(2,1)S(1)} %copy-done.23), channel_id=1, source_target_pairs={{0,7},{1,6},{2,5},{3,4},{4,3},{5,2},{6,1},{7,0},{8,15},{9,14},{10,... | collective-permute-start | bytes 786440 | tf_op jit(solution)/shard_map/ppermute | solution.py:468
  137.9 54.7 %collective-permute-start.1 = (bf16[2,512,128]{2,1,0:T(8,128)(2,1)S(1)}, bf16[2,512,128]{2,1,0:T(8,128)(2,1)S(1)}, u32[]{:S(2)}, u32[]{:S(2)}) collective-permute-start(bf16[2,512,128]{2,1,0:T(8,128)(2,1)S(1)} %copy-done.22), channel_id=1, source_target_pairs={{0,6},{1,7},{2,4},{3,5},{4,2},{5,3},{6,0},{7,1},{8,14},{9,15},{10,... | collective-permute-start | bytes 786440 | tf_op jit(solution)/shard_map/ppermute | solution.py:468
  138.4 54.2 %collective-permute-start.2 = (bf16[2,512,128]{2,1,0:T(8,128)(2,1)S(1)}, bf16[2,512,128]{2,1,0:T(8,128)(2,1)S(1)}, u32[]{:S(2)}, u32[]{:S(2)}) collective-permute-start(bf16[2,512,128]{2,1,0:T(8,128)(2,1)S(1)} %copy-done.21), channel_id=1, source_target_pairs={{0,5},{1,4},{2,7},{3,6},{4,1},{5,0},{6,3},{7,2},{8,13},{9,12},{10,... | collective-permute-start | bytes 786440 | tf_op jit(solution)/shard_map/ppermute | solution.py:468
  139.6 57.0 %collective-permute-start.3 = (bf16[2,512,128]{2,1,0:T(8,128)(2,1)S(1)}, bf16[2,512,128]{2,1,0:T(8,128)(2,1)S(1)}, u32[]{:S(2)}, u32[]{:S(2)}) collective-permute-start(bf16[2,512,128]{2,1,0:T(8,128)(2,1)S(1)} %copy-done.20), channel_id=1, source_target_pairs={{0,4},{1,5},{2,6},{3,7},{4,0},{5,1},{6,2},{7,3},{8,12},{9,13},{10,... | collective-permute-start | bytes 786440 | tf_op jit(solution)/shard_map/ppermute | solution.py:468
  140.1 59.8 %collective-permute-start.4 = (bf16[2,512,128]{2,1,0:T(8,128)(2,1)S(1)}, bf16[2,512,128]{2,1,0:T(8,128)(2,1)}, u32[]{:S(2)}, u32[]{:S(2)}) collective-permute-start(bf16[2,512,128]{2,1,0:T(8,128)(2,1)S(1)} %copy-done.19), channel_id=1, source_target_pairs={{0,3},{1,2},{2,1},{3,0},{4,7},{5,6},{6,5},{7,4},{8,11},{9,10},{10,... | collective-permute-start | bytes 786440 | tf_op jit(solution)/shard_map/ppermute | solution.py:468
  172.6 50.2 %copy-start.29 = (bf16[2,512,128]{2,1,0:T(8,128)(2,1)}, bf16[2,512,128]{2,1,0:T(8,128)(2,1)S(1)}, u32[]{:S(2)}) copy-start(bf16[2,512,128]{2,1,0:T(8,128)(2,1)S(1)} %collective-permute-done.refs_1_) | copy-start | bytes 786436
  172.6 32.7 %collective-permute-start.5 = (bf16[2,512,128]{2,1,0:T(8,128)(2,1)S(1)}, bf16[2,512,128]{2,1,0:T(8,128)(2,1)S(1)}, u32[]{:S(2)}, u32[]{:S(2)}) collective-permute-start(bf16[2,512,128]{2,1,0:T(8,128)(2,1)S(1)} %copy-done.18), channel_id=1, source_target_pairs={{0,2},{1,3},{2,0},{3,1},{4,6},{5,7},{6,4},{7,5},{8,10},{9,11},{10,... | collective-permute-start | bytes 786440 | tf_op jit(solution)/shard_map/ppermute | solution.py:468
  192.6 30.2 %copy-start.30 = (bf16[2,512,128]{2,1,0:T(8,128)(2,1)}, bf16[2,512,128]{2,1,0:T(8,128)(2,1)S(1)}, u32[]{:S(2)}) copy-start(bf16[2,512,128]{2,1,0:T(8,128)(2,1)S(1)} %collective-permute-done.1.refs_2_) | copy-start | bytes 786436
  192.6 12.7 %collective-permute-start.6 = (bf16[2,512,128]{2,1,0:T(8,128)(2,1)S(1)}, bf16[2,512,128]{2,1,0:T(8,128)(2,1)S(1)}, u32[]{:S(2)}, u32[]{:S(2)}) collective-permute-start(bf16[2,512,128]{2,1,0:T(8,128)(2,1)S(1)} %copy-done.17), channel_id=1, source_target_pairs={{0,1},{1,0},{2,3},{3,2},{4,5},{5,4},{6,7},{7,6},{8,9},{9,8},{10,11... | collective-permute-start | bytes 786440 | tf_op jit(solution)/shard_map/ppermute | solution.py:468
  192.6 30.2 %copy-start.31 = (bf16[2,512,128]{2,1,0:T(8,128)(2,1)}, bf16[2,512,128]{2,1,0:T(8,128)(2,1)S(1)}, u32[]{:S(2)}) copy-start(bf16[2,512,128]{2,1,0:T(8,128)(2,1)S(1)} %collective-permute-done.2.refs_3_) | copy-start | bytes 786436
  192.6 19.9 %collective-permute-start.10 = (bf16[2,16,32,128]{3,2,1,0:T(8,128)(2,1)}, bf16[2,16,32,128]{3,2,1,0:T(8,128)(2,1)S(1)}, u32[]{:S(2)}, u32[]{:S(2)}) collective-permute-start(bf16[2,16,32,128]{3,2,1,0:T(8,128)(2,1)} %get-tuple-element.41), channel_id=1, source_target_pairs={{0,7},{1,6},{2,5},{3,4},{4,3},{5,2},{6,1},{7,0},{8,15},{9,14},{10,... | collective-permute-start | bytes 786440 | tf_op jit(solution)/shard_map/ppermute | solution.py:468
  196.6 26.2 %copy-start.32 = (bf16[2,512,128]{2,1,0:T(8,128)(2,1)}, bf16[2,512,128]{2,1,0:T(8,128)(2,1)S(1)}, u32[]{:S(2)}) copy-start(bf16[2,512,128]{2,1,0:T(8,128)(2,1)S(1)} %collective-permute-done.3.refs_4_) | copy-start | bytes 786436
  196.6 26.2 %collective-permute-start.11 = (bf16[2,16,32,128]{3,2,1,0:T(8,128)(2,1)}, bf16[2,16,32,128]{3,2,1,0:T(8,128)(2,1)S(1)}, u32[]{:S(2)}, u32[]{:S(2)}) collective-permute-start(bf16[2,16,32,128]{3,2,1,0:T(8,128)(2,1)} %get-tuple-element.42), channel_id=1, source_target_pairs={{0,6},{1,7},{2,4},{3,5},{4,2},{5,3},{6,0},{7,1},{8,14},{9,15},{10,... | collective-permute-start | bytes 786440 | tf_op jit(solution)/shard_map/ppermute | solution.py:468
  205.2 17.5 %copy-start.33 = (bf16[2,512,128]{2,1,0:T(8,128)(2,1)}, bf16[2,512,128]{2,1,0:T(8,128)(2,1)S(1)}, u32[]{:S(2)}) copy-start(bf16[2,512,128]{2,1,0:T(8,128)(2,1)S(1)} %collective-permute-done.5.refs_6_) | copy-start | bytes 786436
  205.2 17.6 %copy-start.34 = (bf16[2,512,128]{2,1,0:T(8,128)(2,1)}, bf16[2,512,128]{2,1,0:T(8,128)(2,1)S(1)}, u32[]{:S(2)}) copy-start(bf16[2,512,128]{2,1,0:T(8,128)(2,1)S(1)} %collective-permute-done.6.refs_7_) | copy-start | bytes 786436
  212.5 10.3 %copy-start.8 = (bf16[2,16,32,128]{3,2,1,0:T(8,128)(2,1)}, bf16[2,16,32,128]{3,2,1,0:T(8,128)(2,1)S(1)}, u32[]{:S(2)}) copy-start(bf16[2,16,32,128]{3,2,1,0:T(8,128)(2,1)S(1)} %collective-permute-done.10.refs_14_.refs_1_) | copy-start | bytes 786436
  230.8 5.1 %copy-start.28 = (bf16[2,16,32,128]{3,2,1,0:T(8,128)(2,1)S(1)}, bf16[2,16,32,128]{3,2,1,0:T(8,128)(2,1)}, u32[]{:S(2)}) copy-start(bf16[2,16,32,128]{3,2,1,0:T(8,128)(2,1)} %get-tuple-element.44) | copy-start | bytes 786436
  230.8 6.4 %copy-start.27 = (bf16[2,16,32,128]{3,2,1,0:T(8,128)(2,1)S(1)}, bf16[2,16,32,128]{3,2,1,0:T(8,128)(2,1)}, u32[]{:S(2)}) copy-start(bf16[2,16,32,128]{3,2,1,0:T(8,128)(2,1)} %get-tuple-element.45) | copy-start | bytes 786436
  230.8 7.0 %copy-start.26 = (bf16[2,16,32,128]{3,2,1,0:T(8,128)(2,1)S(1)}, bf16[2,16,32,128]{3,2,1,0:T(8,128)(2,1)}, u32[]{:S(2)}) copy-start(bf16[2,16,32,128]{3,2,1,0:T(8,128)(2,1)} %get-tuple-element.46) | copy-start | bytes 786436
  230.8 8.1 %copy-start.25 = (bf16[2,16,32,128]{3,2,1,0:T(8,128)(2,1)S(1)}, bf16[2,16,32,128]{3,2,1,0:T(8,128)(2,1)}, u32[]{:S(2)}) copy-start(bf16[2,16,32,128]{3,2,1,0:T(8,128)(2,1)} %get-tuple-element.47) | copy-start | bytes 786436
  230.8 8.6 %copy-start.24 = (bf16[2,16,32,128]{3,2,1,0:T(8,128)(2,1)S(1)}, bf16[2,16,32,128]{3,2,1,0:T(8,128)(2,1)}, u32[]{:S(2)}) copy-start(bf16[2,16,32,128]{3,2,1,0:T(8,128)(2,1)} %get-tuple-element.48) | copy-start | bytes 786436
  230.8 51.7 %all-to-all-start.4 = ((bf16[32,1,2,128,128]{4,3,2,1,0:T(8,128)(2,1)}), bf16[32,1,2,128,128]{4,3,2,1,0:T(8,128)(2,1)S(1)}, u32[]{:S(2)}, u32[]{:S(2)}) async-start(bf16[32,1,2,128,128]{4,3,2,1,0:T(8,128)(2,1)} %clean.7), calls=%async_computation.4 | async-start | bytes 4194304 | tf_op jit(solution)/shard_map/all_to_all | solution.py:462
  235.9 20.0 %collective-permute-start.12 = (bf16[2,16,32,128]{3,2,1,0:T(8,128)(2,1)S(1)}, bf16[2,16,32,128]{3,2,1,0:T(8,128)(2,1)S(1)}, u32[]{:S(2)}, u32[]{:S(2)}) collective-permute-start(bf16[2,16,32,128]{3,2,1,0:T(8,128)(2,1)S(1)} %copy-done.28), channel_id=1, source_target_pairs={{0,5},{1,4},{2,7},{3,6},{4,1},{5,0},{6,3},{7,2},{8,13},{9,12},{10,... | collective-permute-start | bytes 786440 | tf_op jit(solution)/shard_map/ppermute | solution.py:468
  237.1 29.4 %collective-permute-start.13 = (bf16[2,16,32,128]{3,2,1,0:T(8,128)(2,1)S(1)}, bf16[2,16,32,128]{3,2,1,0:T(8,128)(2,1)S(1)}, u32[]{:S(2)}, u32[]{:S(2)}) collective-permute-start(bf16[2,16,32,128]{3,2,1,0:T(8,128)(2,1)S(1)} %copy-done.27), channel_id=1, source_target_pairs={{0,4},{1,5},{2,6},{3,7},{4,0},{5,1},{6,2},{7,3},{8,12},{9,13},{10,... | collective-permute-start | bytes 786440 | tf_op jit(solution)/shard_map/ppermute | solution.py:468
  237.7 28.9 %collective-permute-start.14 = (bf16[2,16,32,128]{3,2,1,0:T(8,128)(2,1)S(1)}, bf16[2,16,32,128]{3,2,1,0:T(8,128)(2,1)S(1)}, u32[]{:S(2)}, u32[]{:S(2)}) collective-permute-start(bf16[2,16,32,128]{3,2,1,0:T(8,128)(2,1)S(1)} %copy-done.26), channel_id=1, source_target_pairs={{0,3},{1,2},{2,1},{3,0},{4,7},{5,6},{6,5},{7,4},{8,11},{9,10},{10,... | collective-permute-start | bytes 786440 | tf_op jit(solution)/shard_map/ppermute | solution.py:468
  238.9 30.4 %collective-permute-start.15 = (bf16[2,16,32,128]{3,2,1,0:T(8,128)(2,1)S(1)}, bf16[2,16,32,128]{3,2,1,0:T(8,128)(2,1)S(1)}, u32[]{:S(2)}, u32[]{:S(2)}) collective-permute-start(bf16[2,16,32,128]{3,2,1,0:T(8,128)(2,1)S(1)} %copy-done.25), channel_id=1, source_target_pairs={{0,2},{1,3},{2,0},{3,1},{4,6},{5,7},{6,4},{7,5},{8,10},{9,11},{10,... | collective-permute-start | bytes 786440 | tf_op jit(solution)/shard_map/ppermute | solution.py:468
  239.4 29.9 %collective-permute-start.16 = (bf16[2,16,32,128]{3,2,1,0:T(8,128)(2,1)S(1)}, bf16[2,16,32,128]{3,2,1,0:T(8,128)(2,1)S(1)}, u32[]{:S(2)}, u32[]{:S(2)}) collective-permute-start(bf16[2,16,32,128]{3,2,1,0:T(8,128)(2,1)S(1)} %copy-done.24), channel_id=1, source_target_pairs={{0,1},{1,0},{2,3},{3,2},{4,5},{5,4},{6,7},{7,6},{8,9},{9,8},{10,11... | collective-permute-start | bytes 786440 | tf_op jit(solution)/shard_map/ppermute | solution.py:468
  255.9 13.4 %copy-start.10 = (bf16[2,16,32,128]{3,2,1,0:T(8,128)(2,1)}, bf16[2,16,32,128]{3,2,1,0:T(8,128)(2,1)S(1)}, u32[]{:S(2)}) copy-start(bf16[2,16,32,128]{3,2,1,0:T(8,128)(2,1)S(1)} %collective-permute-done.12.refs_3_) | copy-start | bytes 786436
  266.6 2.7 copy-start.11
  266.6 2.7 copy-start.12
  (10 other events, 10.1 us)
